TPU v7x, 32 devices: a whole 2x2x4 slice. The times are simulated.
32 devices in a mesh: seq: 8 (over z, x), rep: 4 (over y, core).
Axes of the slice: x: 2, y: 2, z: 4, core: 2. Of those that a mesh axis runs over, the one named last changes fastest.
Arguments:
- tokens: bfloat16 [1024, 1440], P('seq'), may hold values from -36 to 36
- norm_gain: float32 [1440], replicated, may hold values from 0.1 to 1.9
- expert_ids: int32 [1024, 4], P('seq'), may hold values from 0 to 7, all different within a row; in each aligned block of 128 rows (0 to 127, 128 to 255, ...) at most 128 rows name the same one
- route_weights: float32 [1024, 4], P('seq'), may hold values from 0.1 to 0.6
- gate_weight: bfloat16 [8, 1440, 1440], P('seq', None, 'rep'), may hold values from -0.15625 to 0.15625
- gate_bias: float32 [8, 1440], P('seq', 'rep'), may hold values from -3 to 3
- up_weight: bfloat16 [8, 1440, 1440], P('seq', None, 'rep'), may hold values from -0.15625 to 0.15625
- up_bias: float32 [8, 1440], P('seq', 'rep'), may hold values from -3 to 3
- down_weight: bfloat16 [8, 1440, 1440], P('seq', 'rep'), may hold values from -0.15625 to 0.15625
- down_bias: float32 [8, 1440], P('seq', 'rep'), may hold values from -3 to 3
Outputs:
- mixed: bfloat16 [1024, 1440], P('seq', 'rep')
Inputs may be any that keep to these rules, and one draw needn't show every extreme that they name: `expert_ids`: each row names 4 different experts. Among the 128 rows of one index of seq no expert is named more than 128 times, and in every draw some expert is named exactly 128 times by the rows of one index.
All inputs are finite; a program needn't handle non-finite values.
Results may differ from a plain program's by a relative error of at most 0.014.
Values may be sent and summed in bfloat16 or wider, within the bound.
No kernel may reach another device: no remote copies, remote signals or barrier semaphores. Data moves between devices by JAX's collectives and lax.ppermute only.
A program may use at most 64 MiB of HBM per device.

v0:
```python
import jax
import jax.numpy as jnp
from jax import lax
from jax.sharding import PartitionSpec as P


def on_device(
    tokens,
    norm_gain,
    expert_ids,
    route_weights,
    gate_weight,
    gate_bias,
    up_weight,
    up_bias,
    down_weight,
    down_bias,
):
    tok_rows, features = tokens.shape
    per_token = expert_ids.shape[1]
    experts = lax.axis_size("seq")
    groups = lax.axis_size("rep")
    quarter = features // groups
    capacity = 2 * tok_rows * per_token // experts
    values = tokens.astype(jnp.float32)
    normed = (
        values * lax.rsqrt(jnp.mean(values * values, axis=-1, keepdims=True) + 1e-05) * norm_gain
    ).astype(jnp.bfloat16)
    flat_ids = expert_ids.reshape(-1)
    onehot = (flat_ids[:, None] == jnp.arange(experts, dtype=jnp.int32)[None, :]).astype(jnp.int32)
    before = jnp.cumsum(onehot, axis=0) - onehot
    slot_index = jnp.sum(before * onehot, axis=1)
    destination = flat_ids * capacity + slot_index
    owner_row = jnp.arange(tok_rows * per_token, dtype=jnp.int32) // per_token
    buffer = jnp.zeros((experts * capacity, normed.shape[1]), jnp.bfloat16)
    buffer = buffer.at[destination].set(normed[owner_row])
    received = lax.all_to_all(
        buffer.reshape(experts, capacity, normed.shape[1]),
        "seq",
        split_axis=0,
        concat_axis=0,
        tiled=True,
    )
    in_rows = received.reshape(-1, features)
    gate_pre = jnp.dot(in_rows, gate_weight[0], preferred_element_type=jnp.float32) + gate_bias[0]
    up_pre = jnp.dot(in_rows, up_weight[0], preferred_element_type=jnp.float32) + up_bias[0]
    activated = (gate_pre * jax.nn.sigmoid(1.702 * gate_pre) * (up_pre + 1.0)).astype(jnp.bfloat16)
    partial_value = jnp.dot(activated, down_weight[0], preferred_element_type=jnp.float32)
    rounded = lax.optimization_barrier(partial_value.astype(jnp.bfloat16))
    partial_value = rounded.reshape(received.shape[0], received.shape[1], features)
    summed = lax.psum_scatter(
        partial_value.astype(jnp.float32).astype(jnp.bfloat16),
        "rep",
        scatter_dimension=2,
        tiled=True,
    ).astype(jnp.float32)
    expert_out = (summed + down_bias[0][None, None, :]).astype(jnp.bfloat16)
    returned = lax.all_to_all(expert_out, "seq", split_axis=0, concat_axis=0, tiled=True)
    picked = returned.reshape(-1, quarter)[destination].reshape(tok_rows, per_token, quarter)
    mixed = jnp.sum(route_weights[:, :, None] * picked.astype(jnp.float32), axis=1)
    return mixed.astype(jnp.bfloat16)


def solution(mesh):
    placed = (
        P("seq", None),
        P(),
        P("seq", None),
        P("seq", None),
        P("seq", None, "rep"),
        P("seq", "rep"),
        P("seq", None, "rep"),
        P("seq", "rep"),
        P("seq", "rep", None),
        P("seq", "rep"),
    )
    return jax.shard_map(
        on_device, mesh=mesh, in_specs=placed, out_specs=P("seq", "rep"), check_vma=False
    )
```

profile of v0, /device:TPU:0, one launch (start us, length us, event | category | flops | bytes accessed | tf_op | source)
XLA Modules:
  0.0 190.6 jit_solution(17149998580576540810)
XLA Ops:
  6.5 0.0 copy-start
  6.5 0.0 copy-start.1
  6.5 0.9 copy.62
  7.4 0.1 eq.29
  7.5 0.1 eq.25
  7.6 0.7 broadcast_multiply_fusion
  8.4 1.1 reduce-window.6
  9.5 0.2 slice_reduce_fusion
  9.8 0.1 copy.61
  9.9 0.1 mul.57
  10.0 1.2 copy.64
  11.2 0.2 fusion.17
  11.3 0.1 fusion.25
  11.4 0.0 copy-done.1
  11.5 0.2 fusion.19
  11.6 10.2 %scatter_custom_fusion = bf16[1024,1440]{1,0:T(8,128)(2,1)} fusion(s32[512]{0:T(512)S(1)} %bitcast.61, bf16[128,1440]{1,0:T(8,128)(2,1)S(1)} %fusion.19, s32[1024]{0:T(1024)S(1)} %pad_clamp_fusion.1, bf16[]{:T(256)} %constant.28.clone.1), kind=kCustom, calls=%fused_computation.11 | custom fusion | bytes 2949122 | tf_op jit(solution)/shard_map/scatter | solution.py:36
  21.8 4.7 %copy.66 = bf16[8,128,1440]{1,2,0:T(8,128)(2,1)} copy(bf16[8,128,1440]{2,1,0:T(8,128)(2,1)} %bitcast.56) | data formatting | bytes 5898240 | tf_op jit(solution)/shard_map/reshape | solution.py:38
  26.5 0.0 copy-start.3
  26.5 0.0 copy-start.4
  26.5 0.0 copy-start.6
  26.5 7.4 %all-to-all-start = ((bf16[8,128,1440]{1,2,0:T(8,128)(2,1)}), bf16[8,128,1440]{1,2,0:T(8,128)(2,1)}, u32[]{:S(2)}, u32[]{:S(2)}) async-start(bf16[8,128,1440]{1,2,0:T(8,128)(2,1)} %copy.66), calls=%async_computation | async-start | bytes 5898240 | tf_op jit(solution)/shard_map/all_to_all | solution.py:37
  33.9 0.2 reduce-scatter.4.cloned.1.call-start
  34.1 0.0 copy-done.3
  34.1 0.0 copy-done.4
  34.2 0.0 copy-start.7
  34.2 66.3 %all-to-all-done = bf16[8,128,1440]{1,2,0:T(8,128)(2,1)} async-done(((bf16[8,128,1440]{1,2,0:T(8,128)(2,1)}), bf16[8,128,1440]{1,2,0:T(8,128)(2,1)}, u32[]{:S(2)}, u32[]{:S(2)}) %all-to-all-start) | async-done | bytes 2949152 | tf_op jit(solution)/shard_map/all_to_all | solution.py:37
  100.5 0.0 copy-done.6
  100.5 4.4 %fusion = f32[1024,360]{0,1:T(8,128)} fusion(bf16[1,1440,360]{2,1,0:T(8,128)(2,1)S(1)} %copy-done.6, bf16[8,128,1440]{1,2,0:T(8,128)(2,1)} %all-to-all-done), kind=kOutput, calls=%fused_computation.5 | convolution fusion | flops 1061683200 | bytes 5460480 | tf_op jit(solution)/shard_map/dot_general | solution.py:46
  104.8 0.0 copy-done
  104.8 0.0 copy-done.7
  104.9 7.1 %convolution_convert_fusion = bf16[1024,1440]{0,1:T(8,128)(2,1)} fusion(f32[1024,360]{0,1:T(8,128)} %fusion, bf16[1,360,1440]{2,1,0:T(8,128)(2,1)S(1)} %copy-done, bf16[1,1440,360]{2,1,0:T(8,128)(2,1)S(1)} %copy-done.7, f32[360]{0:T(512)S(1)} %reduce.2, f32[360]{0:T(512)S(1)} %reduce.1, bf16[8,128,1440]{1,2,0:T(8,128)(2,1)} %all-to-all-done), kind=kOutput, calls=%fused_computation.3 | convolution fusion | flops 2128527360 | bytes 9449280 | tf_op jit(solution)/shard_map/dot_general | solution.py:48
  112.0 2.6 %copy.76 = bf16[180,8,8,128]{3,2,1,0:T(8,128)(2,1)S(1)} copy(bf16[180,8,8,128]{3,1,2,0:T(8,128)(2,1)} %bitcast.58) | data formatting | bytes 5898240
  114.6 2.4 %copy.93 = bf16[180,8,8,128]{3,1,2,0:T(8,128)(2,1)} copy(bf16[180,8,8,128]{3,2,1,0:T(8,128)(2,1)S(1)} %copy.76) | data formatting | bytes 5898240
  117.0 0.0 reduce-scatter.4.cloned.1.call-update
  117.0 0.7 copy-done.5
  117.7 35.3 %reduce-scatter.4.cloned.1.call-done = bf16[360,1024]{1,0:T(8,128)(2,1)} async-done(((bf16[1440,1024]{1,0:T(8,128)(2,1)}), bf16[360,1024]{1,0:T(8,128)(2,1)}) %reduce-scatter.4.cloned.1.call-update) | async-done | bytes 737296
  153.0 1.3 copy.78
  154.2 0.0 copy-start.2
  154.3 1.1 add_convert_fusion
  155.3 5.5 %all-to-all-start.1 = ((bf16[8,128,360]{1,2,0:T(8,128)(2,1)}), bf16[8,128,360]{1,2,0:T(8,128)(2,1)S(1)}, u32[]{:S(2)}, u32[]{:S(2)}) async-start(bf16[8,128,360]{1,2,0:T(8,128)(2,1)} %add_convert_fusion), calls=%async_computation.1 | async-start | bytes 1474560 | tf_op jit(solution)/shard_map/all_to_all | solution.py:58
  160.8 0.0 copy-done.2
  160.8 0.1 copy.60
  161.0 19.0 %all-to-all-done.1 = bf16[8,128,360]{1,2,0:T(8,128)(2,1)S(1)} async-done(((bf16[8,128,360]{1,2,0:T(8,128)(2,1)}), bf16[8,128,360]{1,2,0:T(8,128)(2,1)S(1)}, u32[]{:S(2)}, u32[]{:S(2)}) %all-to-all-start.1) | async-done | bytes 737312 | tf_op jit(solution)/shard_map/all_to_all | solution.py:58
  179.9 0.4 copy.69
  180.3 1.9 %gather_fusion = bf16[512,360]{1,0:T(8,128)(2,1)S(1)} fusion(bf16[1024,360]{1,0:T(8,128)(2,1)S(1)} %bitcast.55, s32[1024]{0:T(1024)S(1)} %pad_clamp_fusion), kind=kCustom, calls=%fused_computation.1 | custom fusion | bytes 739328 | tf_op jit(solution)/shard_map/gather | solution.py:59
  182.2 0.2 reshape.120
  182.5 0.6 multiply_reduce_fusion
  183.0 0.8 copy.70
  (12 shorter events, 0.1 us)
Async XLA Ops:
  6.5 98.3 %copy-start = (bf16[1,360,1440]{2,1,0:T(8,128)(2,1)S(1)}, bf16[1,360,1440]{2,1,0:T(8,128)(2,1)}, u32[]{:S(2)}) copy-start(bf16[1,360,1440]{2,1,0:T(8,128)(2,1)} %param.18) | copy-start | bytes 3110404
  6.5 4.9 %copy-start.1 = (f32[1440]{0:T(1024)S(1)}, f32[1440]{0:T(1024)}, u32[]{:S(2)}) copy-start(f32[1440]{0:T(1024)} %param.11) | copy-start | bytes 17284
  26.5 7.6 %copy-start.3 = (f32[1,360]{1,0:T(1,128)S(1)}, f32[1,360]{1,0:T(1,128)}, u32[]{:S(2)}) copy-start(f32[1,360]{1,0:T(1,128)} %param.15) | copy-start | bytes 4324
  26.5 7.7 %copy-start.4 = (f32[1,360]{1,0:T(1,128)S(1)}, f32[1,360]{1,0:T(1,128)}, u32[]{:S(2)}) copy-start(f32[1,360]{1,0:T(1,128)} %param.17) | copy-start | bytes 4324
  26.5 74.0 %copy-start.6 = (bf16[1,1440,360]{2,1,0:T(8,128)(2,1)S(1)}, bf16[1,1440,360]{2,1,0:T(8,128)(2,1)}, u32[]{:S(2)}) copy-start(bf16[1,1440,360]{2,1,0:T(8,128)(2,1)} %param.16) | copy-start | bytes 3110404
  26.5 74.0 %all-to-all-start = ((bf16[8,128,1440]{1,2,0:T(8,128)(2,1)}), bf16[8,128,1440]{1,2,0:T(8,128)(2,1)}, u32[]{:S(2)}, u32[]{:S(2)}) async-start(bf16[8,128,1440]{1,2,0:T(8,128)(2,1)} %copy.66), calls=%async_computation | async-start | bytes 5898240 | tf_op jit(solution)/shard_map/all_to_all | solution.py:37
  33.9 119.1 %reduce-scatter.4.cloned.1.call-start = ((), (), s32[]{:S(2)}) async-start(), calls=%async_computation.3 | async-start | bytes 3686400
  34.2 70.7 %copy-start.7 = (bf16[1,1440,360]{2,1,0:T(8,128)(2,1)S(1)}, bf16[1,1440,360]{2,1,0:T(8,128)(2,1)}, u32[]{:S(2)}) copy-start(bf16[1,1440,360]{2,1,0:T(8,128)(2,1)} %param.14) | copy-start | bytes 3110404
  117.0 0.7 copy-start.5
  154.2 6.6 %copy-start.2 = (f32[128,4]{0,1:T(4,128)S(1)}, f32[128,4]{0,1:T(4,128)}, u32[]{:S(2)}) copy-start(f32[128,4]{0,1:T(4,128)} %param.13) | copy-start | bytes 6148
  155.3 24.6 %all-to-all-start.1 = ((bf16[8,128,360]{1,2,0:T(8,128)(2,1)}), bf16[8,128,360]{1,2,0:T(8,128)(2,1)S(1)}, u32[]{:S(2)}, u32[]{:S(2)}) async-start(bf16[8,128,360]{1,2,0:T(8,128)(2,1)} %add_convert_fusion), calls=%async_computation.1 | async-start | bytes 1474560 | tf_op jit(solution)/shard_map/all_to_all | solution.py:58
Sparse Core Ops, SparseCore 0:
  117.1 35.8 reduce-scatter.3
where the time goes:
time: 191 us
  waiting for transfers between devices  121 us (63%)
  local copies, waits for them, and re-layouts  27.9 us (15%)
  between operations  13.5 us (7%)
  starting transfers between devices  13.1 us (7%)
  matrix products  11.5 us (6%)
  other arithmetic  4 us (2%)
    all_to_all x1, waiting for transfers between devices, on_device(): lax.all_to_all(buffer.reshape(experts, capacity, normed.shape[1]), 'seq',...  66.3 us
    unnamed x2, waiting for transfers between devices  35.3 us
    all_to_all x1, waiting for transfers between devices, on_device(): lax.all_to_all(expert_out, 'seq', split_axis=0, concat_axis=0, tiled=True)  19 us
    scatter x1, local copies, waits for them, and re-layouts, on_device(): buffer = buffer.at[destination].set(normed[owner_row])  10.2 us
    unnamed x22, local copies, waits for them, and re-layouts  9.08 us
    all_to_all x1, starting transfers between devices, on_device(): lax.all_to_all(buffer.reshape(experts, capacity, normed.shape[1]), 'seq',...  7.39 us
    dot_general x1, matrix products, on_device(): jnp.dot(activated, down_weight[0], preferred_element_type=jnp.float32)  7.13 us
    all_to_all x1, starting transfers between devices, on_device(): lax.all_to_all(expert_out, 'seq', split_axis=0, concat_axis=0, tiled=True)  5.51 us
  transfers between devices with their start and end apart: 3, of which 3 were waited for; matrix products, arithmetic and copies ran while one was open for 0% of the time, Pallas kernels for 0%

commit v1 on v0

v1 whole, which is shorter than its diff:
```python
import jax
import jax.numpy as jnp
from jax import lax
from jax.sharding import PartitionSpec as P


def rms_normed(values, norm_gain, axis):
    values = values.astype(jnp.float32)
    scale = lax.rsqrt(jnp.mean(values * values, axis=axis, keepdims=True) + 1e-05)
    return (values * scale * norm_gain).astype(jnp.bfloat16)


def gated(gate_pre, up_pre):
    return (gate_pre * jax.nn.sigmoid(1.702 * gate_pre) * (up_pre + 1.0)).astype(jnp.bfloat16)


def routed(
    tokens,
    norm_gain,
    expert_ids,
    route_weights,
    gate_weight,
    gate_bias,
    up_weight,
    up_bias,
    down_weight,
    down_bias,
    capacity,
):
    tok_rows, features = tokens.shape
    per_token = expert_ids.shape[1]
    experts = lax.axis_size("seq")
    quarter = features // lax.axis_size("rep")
    normed = rms_normed(tokens, norm_gain, -1)
    flat_ids = expert_ids.reshape(-1)
    onehot = (flat_ids[:, None] == jnp.arange(experts, dtype=jnp.int32)[None, :]).astype(jnp.int32)
    before = jnp.cumsum(onehot, axis=0) - onehot
    slot_index = jnp.sum(before * onehot, axis=1)
    destination = flat_ids * capacity + slot_index
    owner_row = jnp.arange(tok_rows * per_token, dtype=jnp.int32) // per_token
    buffer = jnp.zeros((experts * capacity, features), jnp.bfloat16)
    buffer = buffer.at[destination].set(normed[owner_row])
    received = lax.all_to_all(
        buffer.reshape(experts, capacity, features), "seq", split_axis=0, concat_axis=0, tiled=True
    )
    in_rows = received.reshape(-1, features)
    gate_pre = jnp.dot(in_rows, gate_weight[0], preferred_element_type=jnp.float32) + gate_bias[0]
    up_pre = jnp.dot(in_rows, up_weight[0], preferred_element_type=jnp.float32) + up_bias[0]
    partial_value = jnp.dot(
        gated(gate_pre, up_pre), down_weight[0], preferred_element_type=jnp.float32
    ).astype(jnp.bfloat16)
    summed = lax.psum_scatter(
        partial_value.reshape(experts, capacity, features),
        "rep",
        scatter_dimension=2,
        tiled=True,
    ).astype(jnp.float32)
    expert_out = (summed + down_bias[0][None, None, :]).astype(jnp.bfloat16)
    returned = lax.all_to_all(expert_out, "seq", split_axis=0, concat_axis=0, tiled=True)
    picked = returned.reshape(-1, quarter)[destination].reshape(tok_rows, per_token, quarter)
    mixed = jnp.sum(route_weights[:, :, None] * picked.astype(jnp.float32), axis=1)
    return mixed.astype(jnp.bfloat16)


def dense(
    tokens,
    norm_gain,
    expert_ids,
    route_weights,
    gate_weight,
    gate_bias,
    up_weight,
    up_bias,
    down_weight,
    down_bias,
):
    tok_rows, features = tokens.shape
    experts = lax.axis_size("seq")
    groups = lax.axis_size("rep")
    quarter = features // groups
    rep = lax.axis_index("rep")
    own = lax.dynamic_slice_in_dim(tokens.T, rep * quarter, quarter, 0)
    every = lax.all_gather(own, ("seq", "rep"), axis=0, tiled=True)
    every = every.reshape(experts, features, tok_rows)
    chosen = expert_ids.T[None] == jnp.arange(experts, dtype=jnp.int32)[:, None, None]
    shares = jnp.sum(jnp.where(chosen, route_weights.T[None], 0.0), axis=1)
    shares = lax.all_to_all(shares, "seq", split_axis=0, concat_axis=0, tiled=True)
    normed = rms_normed(every, norm_gain[:, None], 1)
    gate_pre = jnp.einsum("dh,sdt->sht", gate_weight[0], normed, preferred_element_type=jnp.float32)
    up_pre = jnp.einsum("dh,sdt->sht", up_weight[0], normed, preferred_element_type=jnp.float32)
    activated = gated(gate_pre + gate_bias[0][:, None], up_pre + up_bias[0][:, None])
    part = jnp.einsum("hd,sht->sdt", down_weight[0], activated, preferred_element_type=jnp.float32)
    bias = lax.dynamic_update_slice_in_dim(
        jnp.zeros((features,), jnp.float32), down_bias[0], rep * quarter, 0
    )
    part = ((part + bias[:, None]) * shares[:, None, :]).astype(jnp.bfloat16)
    mixed = lax.psum_scatter(
        part.reshape(experts * features, tok_rows), ("seq", "rep"), scatter_dimension=0, tiled=True
    )
    return mixed.T


def on_device(*args):
    tokens, expert_ids = args[0], args[2]
    capacity = 2 * tokens.shape[0] * expert_ids.shape[1] // lax.axis_size("seq")
    if capacity >= tokens.shape[0]:
        return dense(*args)
    return routed(*args, capacity)


def solution(mesh):
    placed = (
        P("seq", None),
        P(),
        P("seq", None),
        P("seq", None),
        P("seq", None, "rep"),
        P("seq", "rep"),
        P("seq", None, "rep"),
        P("seq", "rep"),
        P("seq", "rep", None),
        P("seq", "rep"),
    )
    return jax.shard_map(
        on_device, mesh=mesh, in_specs=placed, out_specs=P("seq", "rep"), check_vma=False
    )
```

time: 191 us -> 240 us (1.26); the launches traced: 191 us -> 237 us
  other arithmetic: 4 us -> 57.6 us
  waiting for transfers between devices: 121 us -> 145 us
  local copies, waits for them, and re-layouts: 27.9 us -> 4.3 us
  starting transfers between devices: 13.1 us -> 7.29 us
    all_to_all x2 -> x1, waiting for transfers between devices: 85.3 us -> 0.01 us  [dense(): lax.all_to_all(shares, 'seq', split_axis=0, concat_axis=0, tiled=True)]
    unnamed x2 -> x3, waiting for transfers between devices: 35.3 us -> 92.9 us
    all_gather x0 -> x1, waiting for transfers between devices: none -> 51.8 us  [dense(): every = lax.all_gather(own, ('seq', 'rep'), axis=0, tiled=True)]
    convert_element_type x3 -> x1, other arithmetic: 1.23 us -> 47.2 us  [rms_normed(): return (values * scale * norm_gain).astype(jnp.bfloat16)]
    scatter x1 -> x0, local copies, waits for them, and re-layouts: 10.2 us -> none  [on_device(): buffer = buffer.at[destination].set(normed[owner_row])]
    unnamed x22 -> x8, local copies, waits for them, and re-layouts: 9.08 us -> 1.6 us
    all_to_all x2 -> x1, starting transfers between devices: 12.9 us -> 7.25 us  [dense(): lax.all_to_all(shares, 'seq', split_axis=0, concat_axis=0, tiled=True)]
    reshape x1 -> x0, local copies, waits for them, and re-layouts: 4.66 us -> none  [on_device(): buffer.reshape(experts, capacity, normed.shape[1])]
  transfers between devices with their start and end apart: 3 -> 3, of which waited for: 3 -> 2; matrix products, arithmetic and copies ran while one was open for 0% -> 26% of each run, Pallas kernels for 0% -> 0%
where the time goes in v1:
time: 240 us; the launch traced here: 237 us
  waiting for transfers between devices  145 us (60%)
  other arithmetic  57.6 us (24%)
  between operations  13.5 us (6%)
  matrix products  9.69 us (4%)
  starting transfers between devices  7.29 us (3%)
  local copies, waits for them, and re-layouts  4.3 us (2%)
    unnamed x3, waiting for transfers between devices  92.9 us
    all_gather x1, waiting for transfers between devices, dense(): every = lax.all_gather(own, ('seq', 'rep'), axis=0, tiled=True)  51.8 us
    convert_element_type x1, other arithmetic, rms_normed(): return (values * scale * norm_gain).astype(jnp.bfloat16)  47.2 us
    all_to_all x1, starting transfers between devices, dense(): lax.all_to_all(shares, 'seq', split_axis=0, concat_axis=0, tiled=True)  7.25 us
    dot_general x1, matrix products, dense(): jnp.einsum('hd,sht->sdt', down_weight[0], activated, preferred_element_ty...  7.17 us
  transfers between devices with their start and end apart: 3, of which 2 were waited for; matrix products, arithmetic and copies ran while one was open for 26% of the time, Pallas kernels for 0%

profile of v1, /device:TPU:0, one launch (start us, length us, event | category | flops | bytes accessed | tf_op | source)
XLA Modules:
  0.0 237.0 jit_solution(1361541869099658520)
XLA Ops:
  6.5 0.0 copy-start
  6.5 0.0 all-gather.2.cloned.1.call-start
  6.5 1.6 dynamic-slice_bitcast_fusion
  8.2 0.0 all-gather.2.cloned.1.call-update
  8.2 1.3 select_reduce_fusion
  9.5 7.3 %all-to-all-start = ((f32[8,1,128]{2,1,0:T(1,128)}), f32[8,1,128]{2,1,0:T(1,128)S(1)}, u32[]{:S(2)}, u32[]{:S(2)}) async-start(f32[8,1,128]{2,1,0:T(1,128)} %bitcast.15), calls=%async_computation | async-start | bytes 8192 | tf_op jit(solution)/shard_map/all_to_all | solution.py:87
  16.7 0.0 reduce-scatter.4.cloned.1.call-start
  16.8 0.7 mul.65
  17.5 0.1 mul.66
  17.6 0.7 reduce.2
  18.3 0.7 reduce
  19.0 0.7 reduce.1
  19.7 0.3 dynamic_update_slice.5
  20.0 51.8 %all-gather.2.cloned.1.call-done = bf16[11520,128]{1,0:T(8,128)(2,1)} async-done(((bf16[360,128]{1,0:T(8,128)(2,1)}), bf16[11520,128]{1,0:T(8,128)(2,1)}) %all-gather.2.cloned.1.call-update) | async-done | bytes 2949136 | tf_op jit(solution)/shard_map/all_gather | solution.py:83
  71.7 4.1 %convert_multiply_fusion.1 = f32[11520,128]{1,0:T(8,128)} fusion(bf16[11520,128]{1,0:T(8,128)(2,1)} %all-gather.2.cloned.1.call-done), kind=kLoop, calls=%fused_computation.1 | loop fusion | flops 2949120 | bytes 8847360 | tf_op jit(solution)/shard_map/mul | solution.py:9
  75.8 2.9 %reduce_sum.18 = f32[8,128]{1,0:T(8,128)S(1)} reduce(f32[8,1440,128]{2,1,0:T(8,128)} %bitcast.58, f32[]{:T(128)} %constant.6.clone.1), dimensions={1}, to_apply=%region_0.1 | reduce | flops 1473536 | bytes 5902340 | tf_op jit(solution)/shard_map/reduce_sum | solution.py:9
  78.8 0.0 copy-start.2
  78.8 47.2 %fusion.1 = bf16[11520,128]{1,0:T(8,128)(2,1)S(1)} fusion(bf16[11520,128]{1,0:T(8,128)(2,1)} %all-gather.2.cloned.1.call-done, f32[11520]{0:T(1024)S(1)} %mul.66, f32[8,128]{1,0:T(8,128)S(1)} %add_rsqrt_fusion), kind=kLoop, calls=%fused_computation.3 | loop fusion | flops 5898240 | bytes 5948416 | tf_op jit(solution)/shard_map/convert_element_type | solution.py:10
  126.0 0.0 copy-start.1
  126.0 1.6 copy-done.1
  127.6 0.0 copy-done.2
  127.6 0.0 copy-start.3
  127.6 2.5 %fusion.9 = f32[8,128,360]{1,2,0:T(8,128)} fusion(bf16[8,1440,128]{2,1,0:T(8,128)(2,1)S(1)} %bitcast.59, bf16[1,1440,360]{2,1,0:T(8,128)(2,1)S(1)} %copy-done.2), kind=kOutput, calls=%fused_computation.15 | convolution fusion | flops 1061683200 | bytes 5460480 | tf_op jit(solution)/shard_map/dh,sdt->sht/dot_general | solution.py:89
  130.1 0.0 all-to-all-done
  130.1 0.0 copy-done
  130.1 0.0 copy-done.3
  130.1 7.2 %multiply_convert_fusion = bf16[8,128,1440]{1,2,0:T(8,128)(2,1)} fusion(f32[8,128]{1,0:T(8,128)S(1)} %bitcast.62, f32[1440]{0:T(1024)S(1)} %dynamic_update_slice.5, bf16[1,360,1440]{2,1,0:T(8,128)(2,1)S(1)} %copy-done, f32[8,128,360]{1,2,0:T(8,128)} %fusion.9, bf16[8,1440,128]{2,1,0:T(8,128)(2,1)} %bitcast.60, bf16[1,1440,360]{2,1,0:T(8,128)(2,1)S(1)} %copy-done.3, ...), kind=kOutput, calls=%fused_computation.4 | convolution fusion | flops 2131476480 | bytes 9459136 | tf_op jit(solution)/shard_map/hd,sht->sdt/dot_general | solution.py:92
  137.3 0.0 reduce-scatter.4.cloned.1.call-update
  137.3 92.9 %reduce-scatter.4.cloned.1.call-done = bf16[360,128]{1,0:T(8,128)(2,1)} async-done(((bf16[11520,128]{1,0:T(8,128)(2,1)}), bf16[360,128]{1,0:T(8,128)(2,1)}) %reduce-scatter.4.cloned.1.call-update) | async-done | bytes 92176
  (2 shorter events, 0.0 us)
Async XLA Ops:
  6.5 123.6 %copy-start = (bf16[1,360,1440]{2,1,0:T(8,128)(2,1)S(1)}, bf16[1,360,1440]{2,1,0:T(8,128)(2,1)}, u32[]{:S(2)}) copy-start(bf16[1,360,1440]{2,1,0:T(8,128)(2,1)} %param.18) | copy-start | bytes 3110404
  6.5 65.2 %all-gather.2.cloned.1.call-start = ((), (), s32[]{:S(2)}) async-start(), calls=%async_computation.2 | async-start | bytes 3041280 | tf_op jit(solution)/shard_map/all_gather | solution.py:83
  9.5 120.6 %all-to-all-start = ((f32[8,1,128]{2,1,0:T(1,128)}), f32[8,1,128]{2,1,0:T(1,128)S(1)}, u32[]{:S(2)}, u32[]{:S(2)}) async-start(f32[8,1,128]{2,1,0:T(1,128)} %bitcast.15), calls=%async_computation | async-start | bytes 8192 | tf_op jit(solution)/shard_map/all_to_all | solution.py:87
  16.7 213.4 %reduce-scatter.4.cloned.1.call-start = ((), (), s32[]{:S(2)}) async-start(), calls=%async_computation.3 | async-start | bytes 3041280
  78.8 48.8 %copy-start.2 = (bf16[1,1440,360]{2,1,0:T(8,128)(2,1)S(1)}, bf16[1,1440,360]{2,1,0:T(8,128)(2,1)}, u32[]{:S(2)}) copy-start(bf16[1,1440,360]{2,1,0:T(8,128)(2,1)} %param.14) | copy-start | bytes 3110404
  126.0 1.6 copy-start.1
  127.6 2.5 %copy-start.3 = (bf16[1,1440,360]{2,1,0:T(8,128)(2,1)S(1)}, bf16[1,1440,360]{2,1,0:T(8,128)(2,1)}, u32[]{:S(2)}) copy-start(bf16[1,1440,360]{2,1,0:T(8,128)(2,1)} %param.16) | copy-start | bytes 3110404
Sparse Core Ops, SparseCore 0:
  10.2 61.5 all-gather.1
  137.4 92.7 reduce-scatter.3

commit v2 on v1

--- a/solution.py
+++ b/solution.py
@@ -1,6 +1,10 @@
+import functools
+
 import jax
 import jax.numpy as jnp
 from jax import lax
+from jax.experimental import pallas as pl
+from jax.experimental.pallas import tpu as pltpu
 from jax.sharding import PartitionSpec as P
 
 
@@ -62,6 +66,125 @@
     return mixed.astype(jnp.bfloat16)
 
 
+def round_up(number, step):
+    return -(-number // step) * step
+
+
+def add_up(*terms):
+    total = terms[0].astype(jnp.float32)
+    for term in terms[1:]:
+        total = total + term.astype(jnp.float32)
+    return total.astype(jnp.bfloat16)
+
+
+def expert_kernel(
+    quarter,
+    features,
+    p0,
+    p1,
+    p2,
+    p3,
+    gate_up_ref,
+    down_ref,
+    gain_ref,
+    bias_ref,
+    down_bias_ref,
+    pick_ref,
+    keep_ref,
+    send_ref,
+    rows_ref,
+):
+    pieces = (p0, p1, p2, p3)
+    count, piece_rows, lanes = p0.shape
+    block = gain_ref.shape[1]
+    hidden = gate_up_ref.shape[0] // 2
+
+    @pl.when(pl.program_id(0) == 0)
+    def _():
+        rows_ref[...] = jnp.zeros_like(rows_ref)
+
+    shares = []
+    for j in range(count):
+        squares = jnp.zeros((1, lanes), jnp.float32)
+        share = jnp.zeros((1, lanes), jnp.float32)
+        for k, piece in enumerate(pieces):
+            values = piece[j].astype(jnp.float32)
+            body = values[:quarter]
+            squares += jnp.sum(body * body, axis=0, keepdims=True)
+            share += jnp.sum(values[quarter:] * pick_ref[k], axis=0, keepdims=True)
+        scale = lax.rsqrt(squares * (1.0 / features) + 1e-05)
+        for k, piece in enumerate(pieces):
+            values = piece[j].astype(jnp.float32)
+            rows_ref[k * block : k * block + piece_rows, j * lanes : (j + 1) * lanes] = (
+                values * scale * gain_ref[k, :piece_rows]
+            ).astype(jnp.bfloat16)
+        shares.append(share)
+    wide = jnp.concatenate(shares, axis=1)
+    both = jnp.dot(gate_up_ref[...], rows_ref[...], preferred_element_type=jnp.float32)
+    bias = jnp.concatenate([bias_ref[...]] * count, axis=1)
+    both = both + bias
+    activated = gated(both[:hidden], both[hidden:])
+    part = jnp.dot(down_ref[...], activated, preferred_element_type=jnp.float32)
+    for k in range(len(pieces)):
+        rows = part[k * block : k * block + quarter]
+        if k == 0:
+            rows = rows + jnp.concatenate([down_bias_ref[...]] * count, axis=1)
+        rows = (rows * wide).astype(jnp.bfloat16)
+        target = send_ref if k % 2 else keep_ref
+        for j in range(count):
+            target[k // 2, j] = rows[:, j * lanes : (j + 1) * lanes]
+
+
+def run_expert(pieces, weights, quarter, features):
+    chunks, piece_rows, lanes = pieces[0].shape
+    count = 2
+    gate_up, down = weights[0], weights[1]
+    flops = 2 * chunks * lanes * (gate_up.size + down.size)
+    out = jax.ShapeDtypeStruct((2, chunks, quarter, lanes), jnp.bfloat16)
+    return pl.pallas_call(
+        functools.partial(expert_kernel, quarter, features),
+        grid=(chunks // count,),
+        in_specs=[pl.BlockSpec((count, piece_rows, lanes), lambda i: (i, 0, 0))] * 4
+        + [pl.BlockSpec(w.shape, lambda i, n=w.ndim: (0,) * n) for w in weights],
+        out_specs=[pl.BlockSpec((2, count, quarter, lanes), lambda i: (0, i, 0, 0))] * 2,
+        out_shape=[out, out],
+        scratch_shapes=[pltpu.VMEM((gate_up.shape[1], count * lanes), jnp.bfloat16)],
+        compiler_params=pltpu.CompilerParams(vmem_limit_bytes=40 * 2**20),
+        cost_estimate=pl.CostEstimate(
+            flops=flops, bytes_accessed=2 * (gate_up.size + down.size), transcendentals=0
+        ),
+    )(*pieces, *weights)
+
+
+def arrange(gate_weight, up_weight, down_weight, gate_bias, up_bias, norm_gain, down_bias, rep, groups, lanes):
+    features, hidden = gate_weight.shape
+    quarter = features // groups
+    hidden_pad, block = round_up(hidden, 128), round_up(quarter, 128)
+
+    def relative(array):
+        return jnp.stack(
+            [lax.dynamic_index_in_dim(array, rep ^ k, 0, keepdims=False) for k in range(groups)]
+        )
+
+    def inward(weight):
+        blocks = relative(weight.reshape(groups, quarter, hidden))
+        blocks = jnp.pad(blocks, ((0, 0), (0, block - quarter), (0, hidden_pad - hidden)))
+        return blocks.reshape(groups * block, hidden_pad).T
+
+    def column(vector, size):
+        return jnp.broadcast_to(jnp.pad(vector, (0, size - vector.shape[0]))[:, None], (size, lanes))
+
+    gate_up = jnp.concatenate([inward(gate_weight), inward(up_weight)], axis=0)
+    outward = relative(down_weight.T.reshape(groups, quarter, hidden))
+    outward = jnp.pad(outward, ((0, 0), (0, block - quarter), (0, hidden_pad - hidden)))
+    outward = outward.reshape(groups * block, hidden_pad)
+    gain = relative(norm_gain.reshape(groups, quarter))
+    gain = jnp.pad(gain, ((0, 0), (0, block - quarter)))
+    gain = jnp.broadcast_to(gain[:, :, None], (groups, block, lanes))
+    bias = jnp.concatenate([column(gate_bias, hidden_pad), column(up_bias, hidden_pad)], axis=0)
+    return gate_up, outward, gain, bias, column(down_bias, quarter)
+
+
 def dense(
     tokens,
     norm_gain,
@@ -74,36 +197,80 @@
     down_weight,
     down_bias,
 ):
-    tok_rows, features = tokens.shape
+    lanes, features = tokens.shape
     experts = lax.axis_size("seq")
     groups = lax.axis_size("rep")
     quarter = features // groups
-    rep = lax.axis_index("rep")
-    own = lax.dynamic_slice_in_dim(tokens.T, rep * quarter, quarter, 0)
-    every = lax.all_gather(own, ("seq", "rep"), axis=0, tiled=True)
-    every = every.reshape(experts, features, tok_rows)
+    rep, seq = lax.axis_index("rep"), lax.axis_index("seq")
+    devices = experts * groups
+    lines = experts // 2
+    half = lines // 2
+    core, along_y, along_x, along_z = 1, 2, groups, 2 * groups
+
+    def swap(array, step):
+        return lax.ppermute(array, ("seq", "rep"), [(i, i ^ step) for i in range(devices)])
+
+    per = -(-experts // groups)
+    piece_rows = round_up(quarter + 3 * per, 16)
+    tail = piece_rows - quarter
     chosen = expert_ids.T[None] == jnp.arange(experts, dtype=jnp.int32)[:, None, None]
     shares = jnp.sum(jnp.where(chosen, route_weights.T[None], 0.0), axis=1)
-    shares = lax.all_to_all(shares, "seq", split_axis=0, concat_axis=0, tiled=True)
-    normed = rms_normed(every, norm_gain[:, None], 1)
-    gate_pre = jnp.einsum("dh,sdt->sht", gate_weight[0], normed, preferred_element_type=jnp.float32)
-    up_pre = jnp.einsum("dh,sdt->sht", up_weight[0], normed, preferred_element_type=jnp.float32)
-    activated = gated(gate_pre + gate_bias[0][:, None], up_pre + up_bias[0][:, None])
-    part = jnp.einsum("hd,sht->sdt", down_weight[0], activated, preferred_element_type=jnp.float32)
-    bias = lax.dynamic_update_slice_in_dim(
-        jnp.zeros((features,), jnp.float32), down_bias[0], rep * quarter, 0
-    )
-    part = ((part + bias[:, None]) * shares[:, None, :]).astype(jnp.bfloat16)
-    mixed = lax.psum_scatter(
-        part.reshape(experts * features, tok_rows), ("seq", "rep"), scatter_dimension=0, tiled=True
-    )
+    high = lax.reduce_precision(shares, 8, 7)
+    middle = lax.reduce_precision(shares - high, 8, 7)
+    low = lax.reduce_precision(shares - high - middle, 8, 7)
+    terms = jnp.stack([high, middle, low], axis=1).reshape(3 * experts, lanes)
+    terms = jnp.pad(terms, ((0, 3 * per * groups - 3 * experts), (0, 0)))
+    terms = lax.dynamic_slice_in_dim(terms, rep * 3 * per, 3 * per, 0).astype(jnp.bfloat16)
+    own = lax.dynamic_slice_in_dim(tokens.T, rep * quarter, quarter, 0)
+    own = jnp.concatenate([own, jnp.pad(terms, ((0, tail - 3 * per), (0, 0)))], axis=0)
+    source = rep ^ jnp.arange(groups, dtype=jnp.int32)
+    row = jnp.arange(tail, dtype=jnp.int32)
+    pick = (source[:, None] * per + row[None, :] // 3 == seq) & (row[None, :] < 3 * per)
+    pick = jnp.broadcast_to(pick.astype(jnp.float32)[:, :, None], (groups, tail, lanes))
+
+    here = jnp.stack([own] + [swap(own, k * along_z) for k in range(1, lines)])
+    from_x, from_y = swap(here, along_x), swap(here, along_y)
+    here_core = swap(here, core)
+    corner = jnp.concatenate(
+        [swap(from_x[:half], along_y), swap(from_y[half:], along_x)], axis=0
+    )
+    from_y_core = swap(from_y, core)
+    from_x_core = swap(from_x, core)
+    corner_core = swap(corner, core)
+
+    weights = arrange(
+        gate_weight[0],
+        up_weight[0],
+        down_weight[0],
+        gate_bias[0],
+        up_bias[0],
+        norm_gain,
+        down_bias[0],
+        rep,
+        groups,
+        lanes,
+    ) + (pick,)
+    keep, send = run_expert((here, here_core, from_y, from_y_core), weights, quarter, features)
+    near = add_up(keep, swap(send, core))
+    near_y = swap(near[1, :half], along_y)
+    keep, send = run_expert((from_x, from_x_core, corner, corner_core), weights, quarter, features)
+    far = add_up(keep, swap(send, core))
+    far_y = swap(far[1, :half], along_y)
+    far_x = swap(far[:, half:], along_x)
+    last_x = swap(add_up(far[0, :half], far_y), along_x)
+    last_y = swap(add_up(near[1, half:], far_x[1]), along_y)
+    first = add_up(near[0, :half], near_y, last_x)
+    second = add_up(near[0, half:], far_x[0], last_y)
+    columns = [first[k] for k in range(half)] + [second[k] for k in range(lines - half)]
+    mixed = add_up(columns[0], *[swap(columns[k], k * along_z) for k in range(1, lines)])
     return mixed.T
 
 
 def on_device(*args):
     tokens, expert_ids = args[0], args[2]
-    capacity = 2 * tokens.shape[0] * expert_ids.shape[1] // lax.axis_size("seq")
-    if capacity >= tokens.shape[0]:
+    experts, groups = lax.axis_size("seq"), lax.axis_size("rep")
+    capacity = 2 * tokens.shape[0] * expert_ids.shape[1] // experts
+    if capacity >= tokens.shape[0] and experts & (experts - 1) == 0 and experts > 3 and groups == 4:
         return dense(*args)
     return routed(*args, capacity)
 

time: 240 us -> 108 us (0.45)
  waiting for transfers between devices: 145 us -> 27.7 us
  other arithmetic: 57.6 us -> 16.8 us
  local copies, waits for them, and re-layouts: 4.3 us -> 28.7 us
  starting transfers between devices: 7.29 us -> 22.5 us
  between operations: 13.5 us -> 0.43 us
  Pallas kernels: 0 us -> 10.8 us
  matrix products: 9.69 us -> 0 us
    unnamed x3 -> x0, waiting for transfers between devices: 92.9 us -> none
    all_gather x1 -> x0, waiting for transfers between devices: 51.8 us -> none  [dense(): every = lax.all_gather(own, ('seq', 'rep'), axis=0, tiled=True)]
    convert_element_type x1 -> x6, other arithmetic: 47.2 us -> 0.76 us  [the longest x5 0.68 us: add_up(): return total.astype(jnp.bfloat16)]
    ppermute x0 -> x21, waiting for transfers between devices: none -> 27.7 us  [swap(): lax.ppermute(array, ('seq', 'rep'), [(i, i ^ step) for i in range(devices)])]
    ppermute x0 -> x21, starting transfers between devices: none -> 22.5 us  [swap(): lax.ppermute(array, ('seq', 'rep'), [(i, i ^ step) for i in range(devices)])]
    unnamed x8 -> x39, local copies, waits for them, and re-layouts: 1.6 us -> 19.1 us
    another operation x0 -> x7, other arithmetic: none -> 12.7 us  [the longest x4 11 us: relative(): jnp.stack([lax.dynamic_index_in_dim(array, rep ^ k, 0, keepdims=False) fo...]
    pallas_call x0 -> x2, Pallas kernels: none -> 10.8 us  [run_expert(): pl.pallas_call(functools.partial(expert_kernel, quarter, features), grid=...]
  transfers between devices with their start and end apart: 3 -> 21, of which waited for: 2 -> 10; matrix products, arithmetic and copies ran while one was open for 26% -> 39% of each run, Pallas kernels for 0% -> 10%
where the time goes in v2:
time: 108 us; the launch traced here: 107 us
  local copies, waits for them, and re-layouts  28.7 us (27%)
  waiting for transfers between devices  27.7 us (26%)
  starting transfers between devices  22.5 us (21%)
  other arithmetic  16.8 us (16%)
  Pallas kernels  10.8 us (10%)
    ppermute x21, waiting for transfers between devices, swap(): lax.ppermute(array, ('seq', 'rep'), [(i, i ^ step) for i in range(devices)])  27.7 us
    ppermute x21, starting transfers between devices, swap(): lax.ppermute(array, ('seq', 'rep'), [(i, i ^ step) for i in range(devices)])  22.5 us
    unnamed x39, local copies, waits for them, and re-layouts  19.1 us
    another operation x4, other arithmetic, relative(): jnp.stack([lax.dynamic_index_in_dim(array, rep ^ k, 0, keepdims=False) fo...  11 us
    pallas_call x2, Pallas kernels, run_expert(): pl.pallas_call(functools.partial(expert_kernel, quarter, features), grid=...  10.8 us
    dynamic_slice x3, local copies, waits for them, and re-layouts, relative(): lax.dynamic_index_in_dim(array, rep ^ k, 0, keepdims=False)  3.34 us
    reshape x1, local copies, waits for them, and re-layouts, arrange(): outward = relative(down_weight.T.reshape(groups, quarter, hidden))  2.21 us
  transfers between devices with their start and end apart: 21, of which 10 were waited for; matrix products, arithmetic and copies ran while one was open for 39% of the time, Pallas kernels for 10%

profile of v2, /device:TPU:0, one launch (start us, length us, event | category | flops | bytes accessed | tf_op | source)
XLA Modules:
  0.0 107.0 jit_solution(13334861363107989609)
XLA Ops:
  0.0 0.8 select_reduce_fusion
  1.0 0.6 fusion.50
  1.7 3.0 %collective-permute-start = (bf16[368,128]{1,0:T(8,128)(2,1)}, bf16[368,128]{1,0:T(8,128)(2,1)}, u32[]{:S(2)}, u32[]{:S(2)}) collective-permute-start(bf16[368,128]{1,0:T(8,128)(2,1)} %get-tuple-element.30), channel_id=1, source_target_pairs={{0,8},{1,9},{2,10},{3,11},{4,12},{5,13},{6,14},{7,15},{8,0},{9,1},... | collective-permute-start | bytes 282632 | tf_op jit(solution)/shard_map/ppermute | solution.py:211
  4.7 2.6 %collective-permute-start.1 = (bf16[368,128]{1,0:T(8,128)(2,1)}, bf16[368,128]{1,0:T(8,128)(2,1)}, u32[]{:S(2)}, u32[]{:S(2)}) collective-permute-start(bf16[368,128]{1,0:T(8,128)(2,1)} %get-tuple-element.30), channel_id=1, source_target_pairs={{0,16},{1,17},{2,18},{3,19},{4,20},{5,21},{6,22},{7,23},{8,24},{9,... | collective-permute-start | bytes 282632 | tf_op jit(solution)/shard_map/ppermute | solution.py:211
  7.3 2.2 %copy.48 = bf16[1440,360]{1,0:T(8,128)(2,1)S(1)} copy(bf16[1440,360]{0,1:T(8,128)(2,1)} %bitcast.82) | data formatting | bytes 2073600 | tf_op jit(solution)/shard_map/reshape | solution.py:178
  9.6 1.2 %constant_dynamic-slice_fusion.7 = (bf16[1,360,360]{2,1,0:T(8,128)(2,1)}, bf16[1,360,360]{2,1,0:T(8,128)(2,1)}, bf16[1,360,360]{2,1,0:T(8,128)(2,1)}, bf16[1,360...) fusion(bf16[4,360,360]{2,1,0:T(8,128)(2,1)S(1)} %bitcast.80, ...), kind=kLoop, calls=%fused_computation.85 | loop fusion | bytes 4147216 | tf_op jit(solution)/shard_map/jit(dynamic_index_in_dim)/dynamic_slice | solution.py:166
  10.7 2.4 %copy.53 = bf16[1,360,360]{1,0,2:T(2,128)(2,1)S(1)} copy(bf16[1,360,360]{2,1,0:T(8,128)(2,1)} %get-tuple-element.41) | data formatting | bytes 518400
  13.2 1.0 copy.54
  14.2 1.0 copy.55
  15.3 1.0 copy.56
  16.3 2.1 %constant_dynamic-slice_fusion.15 = (bf16[1,360,360]{2,1,0:T(8,128)(2,1)}, bf16[1,360,360]{2,1,0:T(8,128)(2,1)}, bf16[1,360,360]{2,1,0:T(8,128)(2,1)}, bf16[1,360,360]{2,1,0:T(8,128)(2,1)S(1)}) fusion(bf16[4,360,360]{2,1,0:T(8,128)(2,1)} %bitcast.81, s32[]{:T(128)S(6)} %select_n.49, s32[]{:T(128)S(6)} %select_n.51, s32[]{:T(128)S(6)} %select_n.50, ...), kind=kLoop, calls=%fused_computation.93 | loop fusion | bytes 2073616 | tf_op jit(solution)/shard_map/jit(dynamic_index_in_dim)/dynamic_slice | solution.py:166
  18.5 2.4 %copy.49 = bf16[1,360,360]{1,0,2:T(2,128)(2,1)S(1)} copy(bf16[1,360,360]{2,1,0:T(8,128)(2,1)} %get-tuple-element.17) | data formatting | bytes 518400
  20.9 2.9 %copy.50 = bf16[1,360,360]{1,0,2:T(2,128)(2,1)} copy(bf16[1,360,360]{2,1,0:T(8,128)(2,1)} %get-tuple-element.19) | data formatting | bytes 518400
  23.8 2.9 %copy.51 = bf16[1,360,360]{1,0,2:T(2,128)(2,1)} copy(bf16[1,360,360]{2,1,0:T(8,128)(2,1)} %get-tuple-element.18) | data formatting | bytes 518400
  26.7 1.8 %copy.52 = bf16[1,360,360]{1,0,2:T(2,128)(2,1)} copy(bf16[1,360,360]{2,1,0:T(8,128)(2,1)S(1)} %get-tuple-element.20) | data formatting | bytes 518400
  28.5 4.9 %fusion.24 = bf16[4,384,384]{1,0,2:T(4,128)(2,1)S(1)} fusion(bf16[1,360,360]{1,0,2:T(2,128)(2,1)S(1)} %copy.56, bf16[1,360,360]{1,0,2:T(2,128)(2,1)S(1)} %copy.55, bf16[1,360,360]{1,0,2:T(2,128)(2,1)S(1)} %copy.54, bf16[1,360,360]{1,0,2:T(2,128)(2,1)S(1)} %copy.53), kind=kLoop, calls=%fused_computation.31 | loop fusion | flops 11206656 | bytes 2216448 | tf_op jit(solution)/shard_map/stack | solution.py:165
  33.4 4.9 %fusion.17 = bf16[4,384,384]{1,0,2:T(4,128)(2,1)S(1)} fusion(bf16[1,360,360]{1,0,2:T(2,128)(2,1)S(1)} %copy-done.4, bf16[1,360,360]{1,0,2:T(2,128)(2,1)S(1)} %copy-done.3, bf16[1,360,360]{1,0,2:T(2,128)(2,1)S(1)} %copy-done.2, bf16[1,360,360]{1,0,2:T(2,128)(2,1)S(1)} %copy.49), kind=kLoop, calls=%fused_computation.24 | loop fusion | flops 11206656 | bytes 2216448 | tf_op jit(solution)/shard_map/stack | solution.py:165
  38.4 1.2 %fusion.31 = bf16[4,384,384]{2,1,0:T(8,128)(2,1)} fusion(bf16[1,360,360]{2,1,0:T(8,128)(2,1)S(1)} %copy-done.7, bf16[1,360,360]{2,1,0:T(8,128)(2,1)S(1)} %copy-done.8, bf16[1,360,360]{2,1,0:T(8,128)(2,1)S(1)} %copy-done.9, bf16[1,360,360]{2,1,0:T(8,128)(2,1)S(1)} %copy-done.6), kind=kLoop, calls=%fused_computation.38 | loop fusion | flops 11206656 | bytes 2216448 | tf_op jit(solution)/shard_map/stack | solution.py:165
  39.6 1.0 pad_maximum_fusion.1.p0
  40.6 1.8 %collective-permute-start.8 = (bf16[4,368,128]{2,1,0:T(8,128)(2,1)S(1)}, bf16[4,368,128]{2,1,0:T(8,128)(2,1)S(1)}, u32[]{:S(2)}, u32[]{:S(2)}) collective-permute-start(bf16[4,368,128]{2,1,0:T(8,128)(2,1)S(1)} %pad_maximum_fusion.1.p0), channel_id=1, source_target_pairs={{0,4},{1,5},{2,6},{3,7},{4,0},{5,1},{6,2},{7,3},{8,12},{9,13},{10,... | collective-permute-start | bytes 1130504 | tf_op jit(solution)/shard_map/ppermute | solution.py:211
  42.5 1.2 %copy.58 = bf16[48,8,4,384]{3,1,2,0:T(8,128)(2,1)} copy(bf16[48,8,4,384]{3,2,1,0:T(4,128)(2,1)S(1)} %bitcast.76) | data formatting | bytes 2359296
  43.7 1.2 %copy.57 = bf16[48,8,4,384]{3,1,2,0:T(8,128)(2,1)} copy(bf16[48,8,4,384]{3,2,1,0:T(4,128)(2,1)S(1)} %bitcast.77) | data formatting | bytes 2359296
  45.0 1.5 %collective-permute-start.4 = (bf16[4,368,128]{2,1,0:T(8,128)(2,1)S(1)}, bf16[4,368,128]{2,1,0:T(8,128)(2,1)}, u32[]{:S(2)}, u32[]{:S(2)}) collective-permute-start(bf16[4,368,128]{2,1,0:T(8,128)(2,1)S(1)} %pad_maximum_fusion.1.p0), channel_id=1, source_target_pairs={{0,2},{1,3},{2,0},{3,1},{4,6},{5,7},{6,4},{7,5},{8,10},{9,11},{10,... | collective-permute-start | bytes 1130504 | tf_op jit(solution)/shard_map/ppermute | solution.py:211
  46.5 1.8 %pad_maximum_fusion.gate_up_ref = bf16[768,1536]{1,0:T(8,128)(2,1)S(1)} fusion(bf16[384,1536]{1,0:T(8,128)(2,1)} %bitcast.78, bf16[384,1536]{1,0:T(8,128)(2,1)} %bitcast.79), kind=kLoop, calls=%fused_computation.18 | loop fusion | flops 4718592 | bytes 4718592 | tf_op jit(solution)/shard_map/concatenate | solution.py:177
  48.4 2.3 %collective-permute-done.8.p0 = bf16[4,368,128]{2,1,0:T(8,128)(2,1)S(1)} collective-permute-done((bf16[4,368,128]{2,1,0:T(8,128)(2,1)S(1)}, bf16[4,368,128]{2,1,0:T(8,128)(2,1)S(1)}, u32[]{:S(2)}, u32[]{:S(2)}) %collective-permute-start.8) | collective-permute-done | bytes 376864 | tf_op jit(solution)/shard_map/ppermute | solution.py:211
  50.6 0.7 slice.62
  51.3 1.5 %collective-permute-start.10 = (bf16[2,368,128]{2,1,0:T(8,128)(2,1)}, bf16[2,368,128]{2,1,0:T(8,128)(2,1)}, u32[]{:S(2)}, u32[]{:S(2)}) collective-permute-start(bf16[2,368,128]{2,1,0:T(8,128)(2,1)} %slice.62), channel_id=1, source_target_pairs={{0,2},{1,3},{2,0},{3,1},{4,6},{5,7},{6,4},{7,5},{8,10},{9,11},{10,... | collective-permute-start | bytes 565256 | tf_op jit(solution)/shard_map/ppermute | solution.py:211
  52.9 3.4 %collective-permute-done.4.p2 = bf16[4,368,128]{2,1,0:T(8,128)(2,1)} collective-permute-done((bf16[4,368,128]{2,1,0:T(8,128)(2,1)S(1)}, bf16[4,368,128]{2,1,0:T(8,128)(2,1)}, u32[]{:S(2)}, u32[]{:S(2)}) %collective-permute-start.4) | collective-permute-done | bytes 376864 | tf_op jit(solution)/shard_map/ppermute | solution.py:211
  56.4 1.6 %slice.63 = bf16[2,368,128]{2,1,0:T(8,128)(2,1)} slice(bf16[4,368,128]{2,1,0:T(8,128)(2,1)} %collective-permute-done.4.p2), slice={[2:4], [0:368], [0:128]} | slice | bytes 376832 | tf_op jit(solution)/shard_map/slice | solution.py:235
  58.1 0.6 collective-permute-start.9
  58.7 0.9 constant_dynamic-update-slice_fusion.1
  59.6 4.3 %collective-permute-done.11 = bf16[2,368,128]{2,1,0:T(8,128)(2,1)} collective-permute-done((bf16[2,368,128]{2,1,0:T(8,128)(2,1)}, bf16[2,368,128]{2,1,0:T(8,128)(2,1)}, u32[]{:S(2)}, u32[]{:S(2)}) %collective-permute-start.11) | collective-permute-done | bytes 188448 | tf_op jit(solution)/shard_map/ppermute | solution.py:211
  63.9 0.9 constant_dynamic-update-slice_fusion.p2
  65.6 6.0 %shard_map.100 = (bf16[2,4,360,128]{3,2,1,0:T(8,128)(2,1)S(1)}, bf16[2,4,360,128]{3,2,1,0:T(8,128)(2,1)S(1)}) custom-call(bf16[4,368,128]{2,1,0:T(8,128)(2,1)S(1)} %pad_maximum_fusion.1.p0, bf16[4,368,128]{2,1,0:T(8,128)(2,1)} %collective-permute-done.3.p1, bf16[4,368,128]{2,1,0:T(8,128)(2,1)} %collective-permute-done.4.p2, ...), custom_call_target="tpu_custom_call" | custom-call | flops 1811939328 | bytes 3538944 | tf_op jit(solution)/shard_map/pallas_call | solution.py:144
  72.1 4.8 %shard_map.101 = (bf16[2,4,360,128]{3,2,1,0:T(8,128)(2,1)S(1)}, bf16[2,4,360,128]{3,2,1,0:T(8,128)(2,1)S(1)}) custom-call(bf16[4,368,128]{2,1,0:T(8,128)(2,1)S(1)} %collective-permute-done.8.p0, bf16[4,368,128]{2,1,0:T(8,128)(2,1)S(1)} %collective-permute-done.9.p1, bf16[4,368,128]{2,1,0:T(8,128)(2,1)S(1)} %constant_dynamic-update-slice_fusion.p2, ...), custom_call_target="tpu_custom_call" | custom-call | flops 1811939328 | bytes 3538944 | tf_op jit(solution)/shard_map/pallas_call | solution.py:144
  77.5 1.8 %collective-permute-done.13 = bf16[2,4,360,128]{3,2,1,0:T(8,128)(2,1)S(1)} collective-permute-done((bf16[2,4,360,128]{3,2,1,0:T(8,128)(2,1)S(1)}, bf16[2,4,360,128]{3,2,1,0:T(8,128)(2,1)S(1)}, u32[]{:S(2)}, u32[]{:S(2)}) %collective-permute-start.13) | collective-permute-done | bytes 737312 | tf_op jit(solution)/shard_map/ppermute | solution.py:211
  79.6 1.8 %collective-permute-start.14 = (bf16[2,360,128]{2,1,0:T(8,128)(2,1)S(1)}, bf16[2,360,128]{2,1,0:T(8,128)(2,1)S(1)}, u32[]{:S(2)}, u32[]{:S(2)}) collective-permute-start(bf16[2,360,128]{2,1,0:T(8,128)(2,1)S(1)} %slice_bitcast_fusion), channel_id=1, source_target_pairs={{0,2},{1,3},{2,0},{3,1},{4,6},{5,7},{6,4},{7,5},{8,10},{9,11},{10,... | collective-permute-start | bytes 552968 | tf_op jit(solution)/shard_map/ppermute | solution.py:211
  81.8 5.4 %collective-permute-done.14 = bf16[2,360,128]{2,1,0:T(8,128)(2,1)S(1)} collective-permute-done((bf16[2,360,128]{2,1,0:T(8,128)(2,1)S(1)}, bf16[2,360,128]{2,1,0:T(8,128)(2,1)S(1)}, u32[]{:S(2)}, u32[]{:S(2)}) %collective-permute-start.14) | collective-permute-done | bytes 184352 | tf_op jit(solution)/shard_map/ppermute | solution.py:211
  87.2 2.1 %collective-permute-start.15 = (bf16[2,360,128]{2,1,0:T(8,128)(2,1)S(1)}, bf16[2,360,128]{2,1,0:T(8,128)(2,1)S(1)}, u32[]{:S(2)}, u32[]{:S(2)}) collective-permute-start(bf16[2,360,128]{2,1,0:T(8,128)(2,1)S(1)} %fusion.35), channel_id=1, source_target_pairs={{0,4},{1,5},{2,6},{3,7},{4,0},{5,1},{6,2},{7,3},{8,12},{9,13},{10,... | collective-permute-start | bytes 552968 | tf_op jit(solution)/shard_map/ppermute | solution.py:211
  89.2 1.8 %collective-permute-done.17 = bf16[2,2,360,128]{3,2,1,0:T(8,128)(2,1)S(1)} collective-permute-done((bf16[2,2,360,128]{3,2,1,0:T(8,128)(2,1)S(1)}, bf16[2,2,360,128]{3,2,1,0:T(8,128)(2,1)S(1)}, u32[]{:S(2)}, u32[]{:S(2)}) %collective-permute-start.17) | collective-permute-done | bytes 368672 | tf_op jit(solution)/shard_map/ppermute | solution.py:211
  91.1 1.8 %collective-permute-start.18 = (bf16[2,360,128]{2,1,0:T(8,128)(2,1)S(1)}, bf16[2,360,128]{2,1,0:T(8,128)(2,1)S(1)}, u32[]{:S(2)}, u32[]{:S(2)}) collective-permute-start(bf16[2,360,128]{2,1,0:T(8,128)(2,1)S(1)} %fusion.40), channel_id=1, source_target_pairs={{0,2},{1,3},{2,0},{3,1},{4,6},{5,7},{6,4},{7,5},{8,10},{9,11},{10,... | collective-permute-start | bytes 552968 | tf_op jit(solution)/shard_map/ppermute | solution.py:211
  92.8 1.4 %collective-permute-done.15 = bf16[2,360,128]{2,1,0:T(8,128)(2,1)S(1)} collective-permute-done((bf16[2,360,128]{2,1,0:T(8,128)(2,1)S(1)}, bf16[2,360,128]{2,1,0:T(8,128)(2,1)S(1)}, u32[]{:S(2)}, u32[]{:S(2)}) %collective-permute-start.15) | collective-permute-done | bytes 184352 | tf_op jit(solution)/shard_map/ppermute | solution.py:211
  94.2 2.4 %collective-permute-done.18 = bf16[2,360,128]{2,1,0:T(8,128)(2,1)S(1)} collective-permute-done((bf16[2,360,128]{2,1,0:T(8,128)(2,1)S(1)}, bf16[2,360,128]{2,1,0:T(8,128)(2,1)S(1)}, u32[]{:S(2)}, u32[]{:S(2)}) %collective-permute-start.18) | collective-permute-done | bytes 184352 | tf_op jit(solution)/shard_map/ppermute | solution.py:211
  96.9 1.9 %collective-permute-start.19 = (bf16[360,128]{1,0:T(8,128)(2,1)S(1)}, bf16[360,128]{1,0:T(8,128)(2,1)S(1)}, u32[]{:S(2)}, u32[]{:S(2)}) collective-permute-start(bf16[360,128]{1,0:T(8,128)(2,1)S(1)} %get-tuple-element.27), channel_id=1, source_target_pairs={{0,16},{1,17},{2,18},{3,19},{4,20},{5,21},{6,22},{7,23},{8,24},{9,... | collective-permute-start | bytes 276488 | tf_op jit(solution)/shard_map/ppermute | solution.py:211
  98.8 2.0 %collective-permute-start.20 = (bf16[360,128]{1,0:T(8,128)(2,1)S(1)}, bf16[360,128]{1,0:T(8,128)(2,1)S(1)}, u32[]{:S(2)}, u32[]{:S(2)}) collective-permute-start(bf16[360,128]{1,0:T(8,128)(2,1)S(1)} %get-tuple-element.28), channel_id=1, source_target_pairs={{0,24},{1,25},{2,26},{3,27},{4,28},{5,29},{6,30},{7,31},{8,16},{9,... | collective-permute-start | bytes 276488 | tf_op jit(solution)/shard_map/ppermute | solution.py:211
  101.3 4.2 %collective-permute-done.19 = bf16[360,128]{1,0:T(8,128)(2,1)S(1)} collective-permute-done((bf16[360,128]{1,0:T(8,128)(2,1)S(1)}, bf16[360,128]{1,0:T(8,128)(2,1)S(1)}, u32[]{:S(2)}, u32[]{:S(2)}) %collective-permute-start.19) | collective-permute-done | bytes 92192 | tf_op jit(solution)/shard_map/ppermute | solution.py:211
  105.5 0.8 collective-permute-done.16
  106.3 0.7 fusion.45
  (80 shorter events, 3.9 us)
Async XLA Ops:
  0.0 1.0 copy-start
  1.7 7.9 %copy-start.5 = (bf16[1,1440,360]{2,1,0:T(8,128)(2,1)S(1)}, bf16[1,1440,360]{2,1,0:T(8,128)(2,1)}, u32[]{:S(2)}) copy-start(bf16[1,1440,360]{2,1,0:T(8,128)(2,1)} %param.16) | copy-start | bytes 3110404
  1.7 37.9 %collective-permute-start = (bf16[368,128]{1,0:T(8,128)(2,1)}, bf16[368,128]{1,0:T(8,128)(2,1)}, u32[]{:S(2)}, u32[]{:S(2)}) collective-permute-start(bf16[368,128]{1,0:T(8,128)(2,1)} %get-tuple-element.30), channel_id=1, source_target_pairs={{0,8},{1,9},{2,10},{3,11},{4,12},{5,13},{6,14},{7,15},{8,0},{9,1},... | collective-permute-start | bytes 282632 | tf_op jit(solution)/shard_map/ppermute | solution.py:211
  4.7 34.9 %collective-permute-start.1 = (bf16[368,128]{1,0:T(8,128)(2,1)}, bf16[368,128]{1,0:T(8,128)(2,1)}, u32[]{:S(2)}, u32[]{:S(2)}) collective-permute-start(bf16[368,128]{1,0:T(8,128)(2,1)} %get-tuple-element.30), channel_id=1, source_target_pairs={{0,16},{1,17},{2,18},{3,19},{4,20},{5,21},{6,22},{7,23},{8,24},{9,... | collective-permute-start | bytes 282632 | tf_op jit(solution)/shard_map/ppermute | solution.py:211
  7.3 32.3 %collective-permute-start.2 = (bf16[368,128]{1,0:T(8,128)(2,1)}, bf16[368,128]{1,0:T(8,128)(2,1)}, u32[]{:S(2)}, u32[]{:S(2)}) collective-permute-start(bf16[368,128]{1,0:T(8,128)(2,1)} %get-tuple-element.30), channel_id=1, source_target_pairs={{0,24},{1,25},{2,26},{3,27},{4,28},{5,29},{6,30},{7,31},{8,16},{9,... | collective-permute-start | bytes 282632 | tf_op jit(solution)/shard_map/ppermute | solution.py:211
  28.5 4.9 %copy-start.2 = (bf16[1,360,360]{1,0,2:T(2,128)(2,1)S(1)}, bf16[1,360,360]{1,0,2:T(2,128)(2,1)}, u32[]{:S(2)}) copy-start(bf16[1,360,360]{1,0,2:T(2,128)(2,1)} %copy.50) | copy-start | bytes 777604
  28.5 4.9 %copy-start.3 = (bf16[1,360,360]{1,0,2:T(2,128)(2,1)S(1)}, bf16[1,360,360]{1,0,2:T(2,128)(2,1)}, u32[]{:S(2)}) copy-start(bf16[1,360,360]{1,0,2:T(2,128)(2,1)} %copy.51) | copy-start | bytes 777604
  28.5 4.9 %copy-start.4 = (bf16[1,360,360]{1,0,2:T(2,128)(2,1)S(1)}, bf16[1,360,360]{1,0,2:T(2,128)(2,1)}, u32[]{:S(2)}) copy-start(bf16[1,360,360]{1,0,2:T(2,128)(2,1)} %copy.52) | copy-start | bytes 777604
  33.4 4.9 %copy-start.6 = (bf16[1,360,360]{2,1,0:T(8,128)(2,1)S(1)}, bf16[1,360,360]{2,1,0:T(8,128)(2,1)}, u32[]{:S(2)}) copy-start(bf16[1,360,360]{2,1,0:T(8,128)(2,1)} %get-tuple-element.13) | copy-start | bytes 777604
  33.4 4.9 %copy-start.7 = (bf16[1,360,360]{2,1,0:T(8,128)(2,1)S(1)}, bf16[1,360,360]{2,1,0:T(8,128)(2,1)}, u32[]{:S(2)}) copy-start(bf16[1,360,360]{2,1,0:T(8,128)(2,1)} %get-tuple-element.14) | copy-start | bytes 777604
  33.4 4.9 %copy-start.8 = (bf16[1,360,360]{2,1,0:T(8,128)(2,1)S(1)}, bf16[1,360,360]{2,1,0:T(8,128)(2,1)}, u32[]{:S(2)}) copy-start(bf16[1,360,360]{2,1,0:T(8,128)(2,1)} %get-tuple-element.15) | copy-start | bytes 777604
  33.4 4.9 %copy-start.9 = (bf16[1,360,360]{2,1,0:T(8,128)(2,1)S(1)}, bf16[1,360,360]{2,1,0:T(8,128)(2,1)}, u32[]{:S(2)}) copy-start(bf16[1,360,360]{2,1,0:T(8,128)(2,1)} %get-tuple-element.16) | copy-start | bytes 777604
  40.6 10.0 %collective-permute-start.8 = (bf16[4,368,128]{2,1,0:T(8,128)(2,1)S(1)}, bf16[4,368,128]{2,1,0:T(8,128)(2,1)S(1)}, u32[]{:S(2)}, u32[]{:S(2)}) collective-permute-start(bf16[4,368,128]{2,1,0:T(8,128)(2,1)S(1)} %pad_maximum_fusion.1.p0), channel_id=1, source_target_pairs={{0,4},{1,5},{2,6},{3,7},{4,0},{5,1},{6,2},{7,3},{8,12},{9,13},{10,... | collective-permute-start | bytes 1130504 | tf_op jit(solution)/shard_map/ppermute | solution.py:211
  43.7 1.2 %copy-start.10 = (f32[1440]{0:T(1024)S(1)}, f32[1440]{0:T(1024)}, u32[]{:S(2)}) copy-start(f32[1440]{0:T(1024)} %param.11) | copy-start | bytes 17284
  45.0 11.4 %collective-permute-start.4 = (bf16[4,368,128]{2,1,0:T(8,128)(2,1)S(1)}, bf16[4,368,128]{2,1,0:T(8,128)(2,1)}, u32[]{:S(2)}, u32[]{:S(2)}) collective-permute-start(bf16[4,368,128]{2,1,0:T(8,128)(2,1)S(1)} %pad_maximum_fusion.1.p0), channel_id=1, source_target_pairs={{0,2},{1,3},{2,0},{3,1},{4,6},{5,7},{6,4},{7,5},{8,10},{9,11},{10,... | collective-permute-start | bytes 1130504 | tf_op jit(solution)/shard_map/ppermute | solution.py:211
  46.5 11.5 %copy-start.11 = (f32[1,360]{1,0:T(1,128)S(1)}, f32[1,360]{1,0:T(1,128)}, u32[]{:S(2)}) copy-start(f32[1,360]{1,0:T(1,128)} %param.15) | copy-start | bytes 4324
  46.5 11.5 %copy-start.12 = (f32[1,360]{1,0:T(1,128)S(1)}, f32[1,360]{1,0:T(1,128)}, u32[]{:S(2)}) copy-start(f32[1,360]{1,0:T(1,128)} %param.17) | copy-start | bytes 4324
  46.5 11.5 %copy-start.13 = (f32[1,360]{1,0:T(1,128)S(1)}, f32[1,360]{1,0:T(1,128)}, u32[]{:S(2)}) copy-start(f32[1,360]{1,0:T(1,128)} %param.19) | copy-start | bytes 4324
  51.3 7.4 %collective-permute-start.10 = (bf16[2,368,128]{2,1,0:T(8,128)(2,1)}, bf16[2,368,128]{2,1,0:T(8,128)(2,1)}, u32[]{:S(2)}, u32[]{:S(2)}) collective-permute-start(bf16[2,368,128]{2,1,0:T(8,128)(2,1)} %slice.62), channel_id=1, source_target_pairs={{0,2},{1,3},{2,0},{3,1},{4,6},{5,7},{6,4},{7,5},{8,10},{9,11},{10,... | collective-permute-start | bytes 565256 | tf_op jit(solution)/shard_map/ppermute | solution.py:211
  52.8 12.1 %collective-permute-start.3 = (bf16[4,368,128]{2,1,0:T(8,128)(2,1)S(1)}, bf16[4,368,128]{2,1,0:T(8,128)(2,1)}, u32[]{:S(2)}, u32[]{:S(2)}) collective-permute-start(bf16[4,368,128]{2,1,0:T(8,128)(2,1)S(1)} %pad_maximum_fusion.1.p0), channel_id=1, source_target_pairs={{0,1},{1,0},{2,3},{3,2},{4,5},{5,4},{6,7},{7,6},{8,9},{9,8},{10,11... | collective-permute-start | bytes 1130504 | tf_op jit(solution)/shard_map/ppermute | solution.py:211
  58.0 5.9 %collective-permute-start.11 = (bf16[2,368,128]{2,1,0:T(8,128)(2,1)}, bf16[2,368,128]{2,1,0:T(8,128)(2,1)}, u32[]{:S(2)}, u32[]{:S(2)}) collective-permute-start(bf16[2,368,128]{2,1,0:T(8,128)(2,1)} %slice.63), channel_id=1, source_target_pairs={{0,4},{1,5},{2,6},{3,7},{4,0},{5,1},{6,2},{7,3},{8,12},{9,13},{10,... | collective-permute-start | bytes 565256 | tf_op jit(solution)/shard_map/ppermute | solution.py:211
  58.0 7.0 %collective-permute-start.5 = (bf16[4,368,128]{2,1,0:T(8,128)(2,1)}, bf16[4,368,128]{2,1,0:T(8,128)(2,1)}, u32[]{:S(2)}, u32[]{:S(2)}) collective-permute-start(bf16[4,368,128]{2,1,0:T(8,128)(2,1)} %collective-permute-done.4.p2), channel_id=1, source_target_pairs={{0,1},{1,0},{2,3},{3,2},{4,5},{5,4},{6,7},{7,6},{8,9},{9,8},{10,11... | collective-permute-start | bytes 1130504 | tf_op jit(solution)/shard_map/ppermute | solution.py:211
  58.1 7.5 %copy-start.1 = (bf16[4,384,384]{2,1,0:T(8,128)(2,1)S(1)}, bf16[4,384,384]{2,1,0:T(8,128)(2,1)}, u32[]{:S(2)}) copy-start(bf16[4,384,384]{2,1,0:T(8,128)(2,1)} %fusion.31) | copy-start | bytes 3538948
  58.1 14.0 %collective-permute-start.9 = (bf16[4,368,128]{2,1,0:T(8,128)(2,1)S(1)}, bf16[4,368,128]{2,1,0:T(8,128)(2,1)S(1)}, u32[]{:S(2)}, u32[]{:S(2)}) collective-permute-start(bf16[4,368,128]{2,1,0:T(8,128)(2,1)S(1)} %collective-permute-done.8.p0), channel_id=1, source_target_pairs={{0,1},{1,0},{2,3},{3,2},{4,5},{5,4},{6,7},{7,6},{8,9},{9,8},{10,11... | collective-permute-start | bytes 1130504 | tf_op jit(solution)/shard_map/ppermute | solution.py:211
  64.8 7.3 %collective-permute-start.12 = (bf16[4,368,128]{2,1,0:T(8,128)(2,1)S(1)}, bf16[4,368,128]{2,1,0:T(8,128)(2,1)S(1)}, u32[]{:S(2)}, u32[]{:S(2)}) collective-permute-start(bf16[4,368,128]{2,1,0:T(8,128)(2,1)S(1)} %constant_dynamic-update-slice_fusion.p2), channel_id=1, source_target_pairs={{0,1},{1,0},{2,3},{3,2},{4,5},{5,4},{6,7},{7,6},{8,9},{9,8},{10,11... | collective-permute-start | bytes 1130504 | tf_op jit(solution)/shard_map/ppermute | solution.py:211
  71.6 5.7 %collective-permute-start.6 = (bf16[2,4,360,128]{3,2,1,0:T(8,128)(2,1)S(1)}, bf16[2,4,360,128]{3,2,1,0:T(8,128)(2,1)S(1)}, u32[]{:S(2)}, u32[]{:S(2)}) collective-permute-start(bf16[2,4,360,128]{3,2,1,0:T(8,128)(2,1)S(1)} %get-tuple-element.10), channel_id=1, source_target_pairs={{0,1},{1,0},{2,3},{3,2},{4,5},{5,4},{6,7},{7,6},{8,9},{9,8},{10,11... | collective-permute-start | bytes 2211848 | tf_op jit(solution)/shard_map/ppermute | solution.py:211
  77.0 2.3 %collective-permute-start.13 = (bf16[2,4,360,128]{3,2,1,0:T(8,128)(2,1)S(1)}, bf16[2,4,360,128]{3,2,1,0:T(8,128)(2,1)S(1)}, u32[]{:S(2)}, u32[]{:S(2)}) collective-permute-start(bf16[2,4,360,128]{3,2,1,0:T(8,128)(2,1)S(1)} %get-tuple-element.12), channel_id=1, source_target_pairs={{0,1},{1,0},{2,3},{3,2},{4,5},{5,4},{6,7},{7,6},{8,9},{9,8},{10,11... | collective-permute-start | bytes 2211848 | tf_op jit(solution)/shard_map/ppermute | solution.py:211
  79.5 11.5 %collective-permute-start.17 = (bf16[2,2,360,128]{3,2,1,0:T(8,128)(2,1)S(1)}, bf16[2,2,360,128]{3,2,1,0:T(8,128)(2,1)S(1)}, u32[]{:S(2)}, u32[]{:S(2)}) collective-permute-start(bf16[2,2,360,128]{3,2,1,0:T(8,128)(2,1)S(1)} %slice.69), channel_id=1, source_target_pairs={{0,4},{1,5},{2,6},{3,7},{4,0},{5,1},{6,2},{7,3},{8,12},{9,13},{10,... | collective-permute-start | bytes 1105928 | tf_op jit(solution)/shard_map/ppermute | solution.py:211
  79.6 7.5 %collective-permute-start.14 = (bf16[2,360,128]{2,1,0:T(8,128)(2,1)S(1)}, bf16[2,360,128]{2,1,0:T(8,128)(2,1)S(1)}, u32[]{:S(2)}, u32[]{:S(2)}) collective-permute-start(bf16[2,360,128]{2,1,0:T(8,128)(2,1)S(1)} %slice_bitcast_fusion), channel_id=1, source_target_pairs={{0,2},{1,3},{2,0},{3,1},{4,6},{5,7},{6,4},{7,5},{8,10},{9,11},{10,... | collective-permute-start | bytes 552968 | tf_op jit(solution)/shard_map/ppermute | solution.py:211
  81.4 11.5 %collective-permute-start.7 = (bf16[2,360,128]{2,1,0:T(8,128)(2,1)S(1)}, bf16[2,360,128]{2,1,0:T(8,128)(2,1)S(1)}, u32[]{:S(2)}, u32[]{:S(2)}) collective-permute-start(bf16[2,360,128]{2,1,0:T(8,128)(2,1)S(1)} %slice_bitcast_fusion.2), channel_id=1, source_target_pairs={{0,2},{1,3},{2,0},{3,1},{4,6},{5,7},{6,4},{7,5},{8,10},{9,11},{10,... | collective-permute-start | bytes 552968 | tf_op jit(solution)/shard_map/ppermute | solution.py:211
  87.2 7.1 %collective-permute-start.15 = (bf16[2,360,128]{2,1,0:T(8,128)(2,1)S(1)}, bf16[2,360,128]{2,1,0:T(8,128)(2,1)S(1)}, u32[]{:S(2)}, u32[]{:S(2)}) collective-permute-start(bf16[2,360,128]{2,1,0:T(8,128)(2,1)S(1)} %fusion.35), channel_id=1, source_target_pairs={{0,4},{1,5},{2,6},{3,7},{4,0},{5,1},{6,2},{7,3},{8,12},{9,13},{10,... | collective-permute-start | bytes 552968 | tf_op jit(solution)/shard_map/ppermute | solution.py:211
  91.1 5.6 %collective-permute-start.18 = (bf16[2,360,128]{2,1,0:T(8,128)(2,1)S(1)}, bf16[2,360,128]{2,1,0:T(8,128)(2,1)S(1)}, u32[]{:S(2)}, u32[]{:S(2)}) collective-permute-start(bf16[2,360,128]{2,1,0:T(8,128)(2,1)S(1)} %fusion.40), channel_id=1, source_target_pairs={{0,2},{1,3},{2,0},{3,1},{4,6},{5,7},{6,4},{7,5},{8,10},{9,11},{10,... | collective-permute-start | bytes 552968 | tf_op jit(solution)/shard_map/ppermute | solution.py:211
  96.9 8.7 %collective-permute-start.19 = (bf16[360,128]{1,0:T(8,128)(2,1)S(1)}, bf16[360,128]{1,0:T(8,128)(2,1)S(1)}, u32[]{:S(2)}, u32[]{:S(2)}) collective-permute-start(bf16[360,128]{1,0:T(8,128)(2,1)S(1)} %get-tuple-element.27), channel_id=1, source_target_pairs={{0,16},{1,17},{2,18},{3,19},{4,20},{5,21},{6,22},{7,23},{8,24},{9,... | collective-permute-start | bytes 276488 | tf_op jit(solution)/shard_map/ppermute | solution.py:211
  98.8 6.8 %collective-permute-start.20 = (bf16[360,128]{1,0:T(8,128)(2,1)S(1)}, bf16[360,128]{1,0:T(8,128)(2,1)S(1)}, u32[]{:S(2)}, u32[]{:S(2)}) collective-permute-start(bf16[360,128]{1,0:T(8,128)(2,1)S(1)} %get-tuple-element.28), channel_id=1, source_target_pairs={{0,24},{1,25},{2,26},{3,27},{4,28},{5,29},{6,30},{7,31},{8,16},{9,... | collective-permute-start | bytes 276488 | tf_op jit(solution)/shard_map/ppermute | solution.py:211
  100.8 5.6 %collective-permute-start.16 = (bf16[360,128]{1,0:T(8,128)(2,1)S(1)}, bf16[360,128]{1,0:T(8,128)(2,1)S(1)}, u32[]{:S(2)}, u32[]{:S(2)}) collective-permute-start(bf16[360,128]{1,0:T(8,128)(2,1)S(1)} %slice_bitcast_fusion.6), channel_id=1, source_target_pairs={{0,8},{1,9},{2,10},{3,11},{4,12},{5,13},{6,14},{7,15},{8,0},{9,1},... | collective-permute-start | bytes 276488 | tf_op jit(solution)/shard_map/ppermute | solution.py:211

commit v3 on v1

--- a/solution.py
+++ b/solution.py
@@ -1,6 +1,10 @@
+import functools
+
 import jax
 import jax.numpy as jnp
 from jax import lax
+from jax.experimental import pallas as pl
+from jax.experimental.pallas import tpu as pltpu
 from jax.sharding import PartitionSpec as P
 
 
@@ -62,6 +66,196 @@
     return mixed.astype(jnp.bfloat16)
 
 
+def round_up(number, step):
+    return -(-number // step) * step
+
+
+def add_up(*terms):
+    total = terms[0].astype(jnp.float32)
+    for term in terms[1:]:
+        total = total + term.astype(jnp.float32)
+    return total.astype(jnp.bfloat16)
+
+
+def arrange_kernel(
+    groups,
+    gate_ref,
+    up_ref,
+    down_ref,
+    gate_bias_ref,
+    up_bias_ref,
+    down_bias_ref,
+    gate_up_out,
+    down_out,
+    bias_out,
+    down_bias_out,
+):
+    features, hidden = gate_ref.shape
+    quarter = features // groups
+    hidden_pad, block = round_up(hidden, 128), round_up(quarter, 128)
+    lanes = bias_out.shape[1]
+
+    def padded(array, rows, columns):
+        return jnp.pad(array, ((0, rows - array.shape[0]), (0, columns - array.shape[1])))
+
+    def column(row, size):
+        return jnp.broadcast_to(padded(row, 1, size), (lanes, size)).T
+
+    for n, (weight, bias) in enumerate(((gate_ref, gate_bias_ref), (up_ref, up_bias_ref))):
+        values = weight[...].astype(jnp.float32)
+        rows = slice(n * hidden_pad, (n + 1) * hidden_pad)
+        for q in range(groups):
+            part = padded(values[q * quarter : (q + 1) * quarter], block, hidden_pad)
+            gate_up_out[rows, q * block : (q + 1) * block] = part.T.astype(jnp.bfloat16)
+        bias_out[rows] = column(bias[...], hidden_pad)
+    values = padded(down_ref[...].astype(jnp.float32), hidden_pad, round_up(features, 128)).T
+    for q in range(groups):
+        part = padded(values[q * quarter : (q + 1) * quarter], block, hidden_pad)
+        down_out[q * block : (q + 1) * block] = part.astype(jnp.bfloat16)
+    down_bias_out[...] = column(down_bias_ref[...], block)
+
+
+def arrange(groups, lanes, gate, up, down, gate_bias, up_bias, down_bias):
+    features, hidden = gate.shape
+    hidden_pad, block = round_up(hidden, 128), round_up(features // groups, 128)
+    return pl.pallas_call(
+        functools.partial(arrange_kernel, groups),
+        out_shape=[
+            jax.ShapeDtypeStruct((2 * hidden_pad, groups * block), jnp.bfloat16),
+            jax.ShapeDtypeStruct((groups * block, hidden_pad), jnp.bfloat16),
+            jax.ShapeDtypeStruct((2 * hidden_pad, lanes), jnp.float32),
+            jax.ShapeDtypeStruct((block, lanes), jnp.float32),
+        ],
+        compiler_params=pltpu.CompilerParams(vmem_limit_bytes=40 * 2**20),
+        cost_estimate=pl.CostEstimate(
+            flops=0, bytes_accessed=8 * gate.size * 2, transcendentals=0
+        ),
+    )(gate, up, down, gate_bias, up_bias, down_bias)
+
+
+def pieces_kernel(groups, per, experts, place_ref, tokens_ref, gain_ref, ids_ref, weights_ref, one_ref, near_ref, far_ref):
+    features, lanes = tokens_ref.shape
+    quarter = features // groups
+    tail = one_ref.shape[0] - quarter
+    rep = place_ref[0]
+    values = tokens_ref[...].astype(jnp.float32)
+    scale = lax.rsqrt(jnp.mean(values * values, axis=0, keepdims=True) + 1e-05)
+    gain = jnp.broadcast_to(gain_ref[...], (lanes, features)).T
+    normed = values * scale * gain
+    row = lax.broadcasted_iota(jnp.int32, (tail, lanes), 0)
+    chosen = lax.broadcasted_iota(jnp.int32, (round_up(experts, 8), lanes), 0)
+    shares = jnp.zeros(chosen.shape, jnp.float32)
+    for k in range(ids_ref.shape[0]):
+        shares += jnp.where(ids_ref[k : k + 1] == chosen, weights_ref[k : k + 1], 0.0)
+    terms = []
+    for _ in range(3):
+        term = shares.astype(jnp.bfloat16).astype(jnp.float32)
+        terms.append(term)
+        shares = shares - term
+    for q in range(groups):
+        rows = jnp.zeros((tail, lanes), jnp.float32)
+        for n, term in enumerate(terms):
+            for i in range(per):
+                expert = q * per + i
+                if expert < experts:
+                    rows = jnp.where(row == n * per + i, term[expert : expert + 1], rows)
+        piece = jnp.concatenate([normed[q * quarter : (q + 1) * quarter], rows], axis=0)
+        piece = piece.astype(jnp.bfloat16)
+        k = rep ^ q
+        for side, target in enumerate((near_ref, far_ref)):
+
+            @pl.when(k % 2 == side)
+            def _(target=target, piece=piece, k=k):
+                target[k // 2] = piece
+
+        @pl.when(k == 0)
+        def _(piece=piece):
+            one_ref[...] = piece
+
+
+def make_pieces(place, tokens, norm_gain, expert_ids, route_weights, groups, per, experts):
+    features, lanes = tokens.shape
+    rows = round_up(features // groups + 3 * per, 16)
+    pair = jax.ShapeDtypeStruct((groups // 2, rows, lanes), jnp.bfloat16)
+    whole = pl.BlockSpec(memory_space=pltpu.VMEM)
+    return pl.pallas_call(
+        functools.partial(pieces_kernel, groups, per, experts),
+        in_specs=[pl.BlockSpec(memory_space=pltpu.SMEM)] + [whole] * 4,
+        out_specs=[whole] * 3,
+        out_shape=[jax.ShapeDtypeStruct((rows, lanes), jnp.bfloat16), pair, pair],
+        compiler_params=pltpu.CompilerParams(vmem_limit_bytes=40 * 2**20),
+    )(place, tokens, norm_gain, expert_ids, route_weights)
+
+
+def expert_kernel(quarter, per, blocks, slots, *refs):
+    groups = len(blocks[0])
+    counted = 1 + max(at for block in blocks for at, _ in block)
+    place_ref, arrays = refs[0], refs[1 : 1 + counted]
+    gate_up_ref, down_ref, bias_ref, down_bias_ref, keep_ref, send_ref = refs[1 + counted : 7 + counted]
+    scratch = refs[7 + counted :]
+    _, piece_rows, lanes = arrays[0].shape
+    size = gate_up_ref.shape[1] // groups
+    hidden = gate_up_ref.shape[0] // 2
+    rep, seq = place_ref[0], place_ref[1]
+    halves = len(scratch) // 2
+    count = len(blocks) // halves
+    row = lax.broadcasted_iota(jnp.int32, (piece_rows - quarter, lanes), 0)
+    for half in range(halves):
+        rows_ref, sums_ref = scratch[half], scratch[halves + half]
+        if size > piece_rows:
+            for k in range(groups):
+                rows_ref[k * size + piece_rows : (k + 1) * size, :] = jnp.zeros(
+                    (size - piece_rows, count * lanes), jnp.bfloat16
+                )
+        shares = [jnp.zeros((1, lanes), jnp.float32)] * count
+        for k in range(groups):
+            source = rep ^ k
+            at_row = pl.ds(pl.multiple_of(source * size, size), piece_rows)
+            mine = (lax.rem(row, per) == seq - source * per) & (row < 3 * per)
+            for j in range(count):
+                at, index = blocks[half * count + j][k]
+                values = arrays[at][index]
+                rows_ref[at_row, j * lanes : (j + 1) * lanes] = values
+                terms = values.astype(jnp.float32)[quarter:]
+                shares[j] += jnp.sum(jnp.where(mine, terms, 0.0), axis=0, keepdims=True)
+        wide = jnp.concatenate(shares, axis=1)
+        both = jnp.dot(gate_up_ref[...], rows_ref[...], preferred_element_type=jnp.float32)
+        both = both + jnp.concatenate([bias_ref[...]] * count, axis=1)
+        activated = gated(both[:hidden], both[hidden:])
+        sums_ref[...] = jnp.dot(down_ref[...], activated, preferred_element_type=jnp.float32)
+        for k in range(groups):
+            rows = sums_ref[pl.ds(pl.multiple_of((rep ^ k) * size, size), size), :]
+            if k == 0:
+                rows = rows + jnp.concatenate([down_bias_ref[...]] * count, axis=1)
+            rows = (rows * wide).astype(jnp.bfloat16)
+            target = send_ref if k % 2 else keep_ref
+            for j in range(count):
+                target[slots[half * count + j][k // 2]] = rows[:quarter, j * lanes : (j + 1) * lanes]
+
+
+def run_expert(place, arrays, blocks, slots, weights, quarter, per, halves):
+    lanes = arrays[0].shape[2]
+    gate_up, down = weights[0], weights[1]
+    tokens = len(blocks) * lanes
+    whole = pl.BlockSpec(memory_space=pltpu.VMEM)
+    out = jax.ShapeDtypeStruct((2 * len(blocks), quarter, lanes), jnp.bfloat16)
+    columns = tokens // halves
+    return pl.pallas_call(
+        functools.partial(expert_kernel, quarter, per, blocks, slots),
+        in_specs=[pl.BlockSpec(memory_space=pltpu.SMEM)] + [whole] * (len(arrays) + len(weights)),
+        out_specs=[whole, whole],
+        out_shape=[out, out],
+        scratch_shapes=[pltpu.VMEM((gate_up.shape[1], columns), jnp.bfloat16)] * halves
+        + [pltpu.VMEM((down.shape[0], columns), jnp.float32)] * halves,
+        compiler_params=pltpu.CompilerParams(vmem_limit_bytes=40 * 2**20),
+        cost_estimate=pl.CostEstimate(
+            flops=4 * tokens * (gate_up.size + down.size),
+            bytes_accessed=2 * (gate_up.size + down.size),
+            transcendentals=0,
+        ),
+    )(place, *arrays, *weights)
+
+
 def dense(
     tokens,
     norm_gain,
@@ -74,36 +268,68 @@
     down_weight,
     down_bias,
 ):
-    tok_rows, features = tokens.shape
+    lanes, features = tokens.shape
     experts = lax.axis_size("seq")
     groups = lax.axis_size("rep")
     quarter = features // groups
-    rep = lax.axis_index("rep")
-    own = lax.dynamic_slice_in_dim(tokens.T, rep * quarter, quarter, 0)
-    every = lax.all_gather(own, ("seq", "rep"), axis=0, tiled=True)
-    every = every.reshape(experts, features, tok_rows)
-    chosen = expert_ids.T[None] == jnp.arange(experts, dtype=jnp.int32)[:, None, None]
-    shares = jnp.sum(jnp.where(chosen, route_weights.T[None], 0.0), axis=1)
-    shares = lax.all_to_all(shares, "seq", split_axis=0, concat_axis=0, tiled=True)
-    normed = rms_normed(every, norm_gain[:, None], 1)
-    gate_pre = jnp.einsum("dh,sdt->sht", gate_weight[0], normed, preferred_element_type=jnp.float32)
-    up_pre = jnp.einsum("dh,sdt->sht", up_weight[0], normed, preferred_element_type=jnp.float32)
-    activated = gated(gate_pre + gate_bias[0][:, None], up_pre + up_bias[0][:, None])
-    part = jnp.einsum("hd,sht->sdt", down_weight[0], activated, preferred_element_type=jnp.float32)
-    bias = lax.dynamic_update_slice_in_dim(
-        jnp.zeros((features,), jnp.float32), down_bias[0], rep * quarter, 0
-    )
-    part = ((part + bias[:, None]) * shares[:, None, :]).astype(jnp.bfloat16)
-    mixed = lax.psum_scatter(
-        part.reshape(experts * features, tok_rows), ("seq", "rep"), scatter_dimension=0, tiled=True
+    rep, seq = lax.axis_index("rep"), lax.axis_index("seq")
+    devices = experts * groups
+    core, along_y, along_x, along_z = 1, 2, groups, 2 * groups
+
+    def swap(array, step):
+        return lax.ppermute(array, ("seq", "rep"), [(i, i ^ step) for i in range(devices)])
+
+    per = -(-experts // groups)
+    place = jnp.stack([rep, seq]).astype(jnp.int32)
+    one, near, far = make_pieces(
+        place, tokens.T, norm_gain[None], expert_ids.T, route_weights.T, groups, per, experts
+    )
+    z_2, z_3 = swap(one, 2 * along_z), swap(one, 3 * along_z)
+    x_0 = swap(near, along_x)
+    z_1 = swap(near, along_z)
+    weights = arrange(
+        groups, lanes, gate_weight[0], up_weight[0], down_weight[0], gate_bias, up_bias, down_bias
+    )
+    z_high = jnp.stack([z_2, z_3])
+    x_high, y_high = swap(z_high, along_x), swap(z_high, along_y)
+    x_1 = swap(z_1, along_x)
+    corner = swap(x_high, along_y)
+
+    low = (near, far, x_0, swap(x_0, core), z_1, swap(z_1, core), x_1, swap(x_1, core))
+    high = (z_high, swap(z_high, core), y_high, swap(y_high, core))
+    high = high + (x_high, swap(x_high, core), corner, swap(corner, core))
+    low_blocks = [[(2 * n + k % 2, k // 2) for k in range(groups)] for n in range(4)]
+    high_blocks = [
+        [(4 * x + k, line) for k in range(groups)] for line in range(2) for x in range(2)
+    ]
+    slots = ((4, 0), (5, 1), (6, 7), (2, 3))
+
+    def plane(keep, send):
+        got = swap(send, core)
+        first_y = swap(add_up(keep[0:2], got[0:2]), along_y)
+        first_x = swap(add_up(keep[2:4], got[2:4]), along_x)
+        last_x = swap(add_up(keep[5], got[5], first_y[1]), along_x)
+        last_y = swap(add_up(keep[7], got[7], first_x[1]), along_y)
+        return (
+            add_up(keep[4], got[4], first_y[0], last_x),
+            add_up(keep[6], got[6], first_x[0], last_y),
+        )
+
+    keep_low, send_low = run_expert(place, low, low_blocks, slots, weights, quarter, per, 2)
+    keep_high, send_high = run_expert(place, high, high_blocks, slots, weights, quarter, per, 2)
+    line_2, line_3 = plane(keep_high, send_high)
+    line_0, line_1 = plane(keep_low, send_low)
+    mixed = add_up(
+        line_0, swap(line_1, along_z), swap(line_2, 2 * along_z), swap(line_3, 3 * along_z)
     )
     return mixed.T
 
 
 def on_device(*args):
     tokens, expert_ids = args[0], args[2]
-    capacity = 2 * tokens.shape[0] * expert_ids.shape[1] // lax.axis_size("seq")
-    if capacity >= tokens.shape[0]:
+    experts, groups = lax.axis_size("seq"), lax.axis_size("rep")
+    capacity = 2 * tokens.shape[0] * expert_ids.shape[1] // experts
+    if capacity >= tokens.shape[0] and experts == 2 * groups and groups == 4:
         return dense(*args)
     return routed(*args, capacity)
 

time: 240 us -> 75.6 us (0.32); the launches traced: 237 us -> 75.2 us
  waiting for transfers between devices: 145 us -> 25.4 us
  other arithmetic: 57.6 us -> 1.33 us
  starting transfers between devices: 7.29 us -> 26.7 us
  between operations: 13.5 us -> 0.12 us
  Pallas kernels: 0 us -> 12.9 us
  matrix products: 9.69 us -> 0 us
  local copies, waits for them, and re-layouts: 4.3 us -> 8.82 us
    unnamed x3 -> x0, waiting for transfers between devices: 92.9 us -> none
    all_gather x1 -> x0, waiting for transfers between devices: 51.8 us -> none  [dense(): every = lax.all_gather(own, ('seq', 'rep'), axis=0, tiled=True)]
    convert_element_type x1 -> x6, other arithmetic: 47.2 us -> 0.51 us  [add_up(): return total.astype(jnp.bfloat16)]
    ppermute x0 -> x28, starting transfers between devices: none -> 26.7 us  [swap(): lax.ppermute(array, ('seq', 'rep'), [(i, i ^ step) for i in range(devices)])]
    ppermute x0 -> x28, waiting for transfers between devices: none -> 25.4 us  [swap(): lax.ppermute(array, ('seq', 'rep'), [(i, i ^ step) for i in range(devices)])]
    pallas_call x0 -> x4, Pallas kernels: none -> 12.9 us  [the longest x2 10.7 us: run_expert(): pl.pallas_call(functools.partial(expert_kernel, quarter, per, blocks, slo...]
    dot_general x2 -> x0, matrix products: 9.69 us -> none  [the longest x1 7.17 us: dense(): jnp.einsum('hd,sht->sdt', down_weight[0], activated, preferred_element_ty...]
    all_to_all x1 -> x0, starting transfers between devices: 7.25 us -> none  [dense(): lax.all_to_all(shares, 'seq', split_axis=0, concat_axis=0, tiled=True)]
  transfers between devices with their start and end apart: 3 -> 28, of which waited for: 2 -> 12; matrix products, arithmetic and copies ran while one was open for 26% -> 1% of each run, Pallas kernels for 0% -> 16%
where the time goes in v3:
time: 75.6 us; the launch traced here: 75.2 us
  starting transfers between devices  26.7 us (35%)
  waiting for transfers between devices  25.4 us (34%)
  Pallas kernels  12.9 us (17%)
  local copies, waits for them, and re-layouts  8.82 us (12%)
  other arithmetic  1.33 us (2%)
    ppermute x28, starting transfers between devices, swap(): lax.ppermute(array, ('seq', 'rep'), [(i, i ^ step) for i in range(devices)])  26.7 us
    ppermute x28, waiting for transfers between devices, swap(): lax.ppermute(array, ('seq', 'rep'), [(i, i ^ step) for i in range(devices)])  25.4 us
    pallas_call x2, Pallas kernels, run_expert(): pl.pallas_call(functools.partial(expert_kernel, quarter, per, blocks, slo...  10.7 us
    unnamed x18, local copies, waits for them, and re-layouts  8.12 us
  transfers between devices with their start and end apart: 28, of which 12 were waited for; matrix products, arithmetic and copies ran while one was open for 1% of the time, Pallas kernels for 16%

profile of v3, /device:TPU:0, one launch (start us, length us, event | category | flops | bytes accessed | tf_op | source)
XLA Modules:
  0.0 75.2 jit_solution(3407113326516807308)
XLA Ops:
  0.0 0.7 broadcast_in_dim.3.gain_ref
  0.8 1.0 %copy-done.3 = bf16[128,1440]{0,1:T(8,128)(2,1)S(1)} copy-done((bf16[128,1440]{0,1:T(8,128)(2,1)S(1)}, bf16[128,1440]{0,1:T(8,128)(2,1)}, u32[]{:S(2)}) %copy-start.3) | copy-done | bytes 368664
  1.8 0.7 copy-done.4
  2.4 0.7 copy-done.5
  3.1 1.0 %shard_map.100 = (bf16[368,128]{1,0:T(8,128)(2,1)S(1)}, bf16[2,368,128]{2,1,0:T(8,128)(2,1)S(1)}, bf16[2,368,128]{2,1,0:T(8,128)(2,1)S(1)}) custom-call(s32[2]{0:T(128)S(1)} %pad_add_fusion.place_ref.refs_0_, bf16[1440,128]{1,0:T(8,128)(2,1)S(1)} %bitcast.41, f32[1,1440]{1,0:T(1,128)S(1)} %broadcast_in_dim.3.gain_ref, s32[4,128]{1,0:T(4,128)S(1)} %bitcast.42, ...), custom_call_target="tpu_custom_call" | custom-call | tf_op jit(solution)/shard_map/pallas_call | solution.py:181
  4.1 5.1 %collective-permute-start.13 = (bf16[368,128]{1,0:T(8,128)(2,1)S(1)}, bf16[368,128]{1,0:T(8,128)(2,1)S(1)}, u32[]{:S(2)}, u32[]{:S(2)}) collective-permute-start(bf16[368,128]{1,0:T(8,128)(2,1)S(1)} %get-tuple-element.24), channel_id=1, source_target_pairs={{0,24},{1,25},{2,26},{3,27},{4,28},{5,29},{6,30},{7,31},{8,16},{9,... | collective-permute-start | bytes 282632 | tf_op jit(solution)/shard_map/ppermute | solution.py:280
  9.2 0.6 collective-permute-start.2
  9.9 1.6 %collective-permute-start = (bf16[2,368,128]{2,1,0:T(8,128)(2,1)S(1)}, bf16[2,368,128]{2,1,0:T(8,128)(2,1)S(1)}, u32[]{:S(2)}, u32[]{:S(2)}) collective-permute-start(bf16[2,368,128]{2,1,0:T(8,128)(2,1)S(1)} %get-tuple-element.16.refs_1_), channel_id=1, source_target_pairs={{0,4},{1,5},{2,6},{3,7},{4,0},{5,1},{6,2},{7,3},{8,12},{9,13},{10,... | collective-permute-start | bytes 565256 | tf_op jit(solution)/shard_map/ppermute | solution.py:280
  11.5 1.2 %collective-permute-done.13 = bf16[368,128]{1,0:T(8,128)(2,1)S(1)} collective-permute-done((bf16[368,128]{1,0:T(8,128)(2,1)S(1)}, bf16[368,128]{1,0:T(8,128)(2,1)S(1)}, u32[]{:S(2)}, u32[]{:S(2)}) %collective-permute-start.13) | collective-permute-done | bytes 94240 | tf_op jit(solution)/shard_map/ppermute | solution.py:280
  12.7 4.5 %collective-permute-done.12 = bf16[368,128]{1,0:T(8,128)(2,1)S(1)} collective-permute-done((bf16[368,128]{1,0:T(8,128)(2,1)S(1)}, bf16[368,128]{1,0:T(8,128)(2,1)S(1)}, u32[]{:S(2)}, u32[]{:S(2)}) %collective-permute-start.12) | collective-permute-done | bytes 94240 | tf_op jit(solution)/shard_map/ppermute | solution.py:280
  17.3 1.6 %collective-permute-start.17 = (bf16[2,368,128]{2,1,0:T(8,128)(2,1)S(1)}, bf16[2,368,128]{2,1,0:T(8,128)(2,1)S(1)}, u32[]{:S(2)}, u32[]{:S(2)}) collective-permute-start(bf16[2,368,128]{2,1,0:T(8,128)(2,1)S(1)} %pad_maximum_fusion.refs_1_), channel_id=1, source_target_pairs={{0,4},{1,5},{2,6},{3,7},{4,0},{5,1},{6,2},{7,3},{8,12},{9,13},{10,... | collective-permute-start | bytes 565256 | tf_op jit(solution)/shard_map/ppermute | solution.py:280
  18.8 0.8 %collective-permute-start.4 = (bf16[2,368,128]{2,1,0:T(8,128)(2,1)S(1)}, bf16[2,368,128]{2,1,0:T(8,128)(2,1)S(1)}, u32[]{:S(2)}, u32[]{:S(2)}) collective-permute-start(bf16[2,368,128]{2,1,0:T(8,128)(2,1)S(1)} %collective-permute-done.2.refs_5_), channel_id=1, source_target_pairs={{0,4},{1,5},{2,6},{3,7},{4,0},{5,1},{6,2},{7,3},{8,12},{9,13},{10,... | collective-permute-start | bytes 565256 | tf_op jit(solution)/shard_map/ppermute | solution.py:280
  19.6 1.5 %collective-permute-start.15 = (bf16[2,368,128]{2,1,0:T(8,128)(2,1)S(1)}, bf16[2,368,128]{2,1,0:T(8,128)(2,1)S(1)}, u32[]{:S(2)}, u32[]{:S(2)}) collective-permute-start(bf16[2,368,128]{2,1,0:T(8,128)(2,1)S(1)} %pad_maximum_fusion.refs_1_), channel_id=1, source_target_pairs={{0,2},{1,3},{2,0},{3,1},{4,6},{5,7},{6,4},{7,5},{8,10},{9,11},{10,... | collective-permute-start | bytes 565256 | tf_op jit(solution)/shard_map/ppermute | solution.py:280
  21.2 0.5 collective-permute-start.3
  21.7 3.3 %collective-permute-done.17.refs_5_ = bf16[2,368,128]{2,1,0:T(8,128)(2,1)S(1)} collective-permute-done((bf16[2,368,128]{2,1,0:T(8,128)(2,1)S(1)}, bf16[2,368,128]{2,1,0:T(8,128)(2,1)S(1)}, u32[]{:S(2)}, u32[]{:S(2)}) %collective-permute-start.17) | collective-permute-done | bytes 188448 | tf_op jit(solution)/shard_map/ppermute | solution.py:280
  25.0 1.5 %collective-permute-start.19 = (bf16[2,368,128]{2,1,0:T(8,128)(2,1)S(1)}, bf16[2,368,128]{2,1,0:T(8,128)(2,1)S(1)}, u32[]{:S(2)}, u32[]{:S(2)}) collective-permute-start(bf16[2,368,128]{2,1,0:T(8,128)(2,1)S(1)} %collective-permute-done.17.refs_5_), channel_id=1, source_target_pairs={{0,2},{1,3},{2,0},{3,1},{4,6},{5,7},{6,4},{7,5},{8,10},{9,11},{10,... | collective-permute-start | bytes 565256 | tf_op jit(solution)/shard_map/ppermute | solution.py:280
  26.5 0.5 collective-permute-done.4.refs_7_
  27.1 1.2 %copy-done = bf16[1,1440,360]{2,1,0:T(8,128)(2,1)S(1)} copy-done((bf16[1,1440,360]{2,1,0:T(8,128)(2,1)S(1)}, bf16[1,1440,360]{2,1,0:T(8,128)(2,1)}, u32[]{:S(2)}) %copy-start) | copy-done | bytes 1036824
  28.3 1.2 %copy-done.1 = bf16[1,1440,360]{2,1,0:T(8,128)(2,1)S(1)} copy-done((bf16[1,1440,360]{2,1,0:T(8,128)(2,1)S(1)}, bf16[1,1440,360]{2,1,0:T(8,128)(2,1)}, u32[]{:S(2)}) %copy-start.1) | copy-done | bytes 1036824
  29.5 1.2 %copy-done.2 = bf16[1,360,1440]{2,1,0:T(8,128)(2,1)S(1)} copy-done((bf16[1,360,1440]{2,1,0:T(8,128)(2,1)S(1)}, bf16[1,360,1440]{2,1,0:T(8,128)(2,1)}, u32[]{:S(2)}) %copy-start.2) | copy-done | bytes 1036824
  30.8 0.7 copy-done.6
  31.5 0.7 copy-done.7
  32.1 0.7 copy-done.8
  32.8 1.2 %shard_map.101 = (bf16[768,1536]{1,0:T(8,128)(2,1)S(1)}, bf16[1536,384]{1,0:T(8,128)(2,1)S(1)}, f32[768,128]{1,0:T(8,128)S(1)}, f32[384,128]{1,0:T(8,128)S(1)}) custom-call(bf16[1440,360]{1,0:T(8,128)(2,1)S(1)} %bitcast.38, bf16[1440,360]{1,0:T(8,128)(2,1)S(1)} %bitcast.39, bf16[360,1440]{1,0:T(8,128)(2,1)S(1)} %bitcast.40, f32[1,360]{1,0:T(1,128)S(1)} %copy-done.6, ...), custom_call_target="tpu_custom_call" | custom-call | bytes 8294400 | tf_op jit(solution)/shard_map/pallas_call | solution.py:121
  34.0 0.6 collective-permute-start.14
  34.7 0.4 collective-permute-start.16
  35.2 5.4 %shard_map.102 = (bf16[8,360,128]{2,1,0:T(8,128)(2,1)S(1)}, bf16[8,360,128]{2,1,0:T(8,128)(2,1)S(1)}) custom-call(s32[2]{0:T(128)S(1)} %pad_add_fusion.place_ref.refs_0_, bf16[2,368,128]{2,1,0:T(8,128)(2,1)S(1)} %get-tuple-element.16.refs_1_, bf16[2,368,128]{2,1,0:T(8,128)(2,1)S(1)} %get-tuple-element.17.refs_2_, ...), custom_call_target="tpu_custom_call" | custom-call | flops 3623878656 | bytes 3538944 | tf_op jit(solution)/shard_map/pallas_call | solution.py:243
  40.6 0.5 collective-permute-start.6
  41.1 5.4 %shard_map.103 = (bf16[8,360,128]{2,1,0:T(8,128)(2,1)S(1)}, bf16[8,360,128]{2,1,0:T(8,128)(2,1)S(1)}) custom-call(s32[2]{0:T(128)S(1)} %pad_add_fusion.place_ref.refs_0_, bf16[2,368,128]{2,1,0:T(8,128)(2,1)S(1)} %pad_maximum_fusion.refs_1_, bf16[2,368,128]{2,1,0:T(8,128)(2,1)S(1)} %collective-permute-done.14.refs_2_, ...), custom_call_target="tpu_custom_call" | custom-call | flops 3623878656 | bytes 3538944 | tf_op jit(solution)/shard_map/pallas_call | solution.py:243
  46.4 0.2 collective-permute-start.21
  46.7 1.6 %collective-permute-start.7 = (bf16[2,360,128]{2,1,0:T(8,128)(2,1)S(1)}, bf16[2,360,128]{2,1,0:T(8,128)(2,1)S(1)}, u32[]{:S(2)}, u32[]{:S(2)}) collective-permute-start(bf16[2,360,128]{2,1,0:T(8,128)(2,1)S(1)} %get-tuple-element.29), channel_id=1, source_target_pairs={{0,2},{1,3},{2,0},{3,1},{4,6},{5,7},{6,4},{7,5},{8,10},{9,11},{10,... | collective-permute-start | bytes 552968 | tf_op jit(solution)/shard_map/ppermute | solution.py:280
  48.3 1.5 %collective-permute-start.9 = (bf16[2,360,128]{2,1,0:T(8,128)(2,1)S(1)}, bf16[2,360,128]{2,1,0:T(8,128)(2,1)S(1)}, u32[]{:S(2)}, u32[]{:S(2)}) collective-permute-start(bf16[2,360,128]{2,1,0:T(8,128)(2,1)S(1)} %get-tuple-element.30), channel_id=1, source_target_pairs={{0,4},{1,5},{2,6},{3,7},{4,0},{5,1},{6,2},{7,3},{8,12},{9,13},{10,... | collective-permute-start | bytes 552968 | tf_op jit(solution)/shard_map/ppermute | solution.py:280
  49.9 0.6 collective-permute-start.22
  50.5 1.4 %collective-permute-start.25 = (bf16[2,360,128]{2,1,0:T(8,128)(2,1)S(1)}, bf16[2,360,128]{2,1,0:T(8,128)(2,1)S(1)}, u32[]{:S(2)}, u32[]{:S(2)}) collective-permute-start(bf16[2,360,128]{2,1,0:T(8,128)(2,1)S(1)} %get-tuple-element.36), channel_id=1, source_target_pairs={{0,4},{1,5},{2,6},{3,7},{4,0},{5,1},{6,2},{7,3},{8,12},{9,13},{10,... | collective-permute-start | bytes 552968 | tf_op jit(solution)/shard_map/ppermute | solution.py:280
  51.9 2.3 %collective-permute-done.7 = bf16[2,360,128]{2,1,0:T(8,128)(2,1)S(1)} collective-permute-done((bf16[2,360,128]{2,1,0:T(8,128)(2,1)S(1)}, bf16[2,360,128]{2,1,0:T(8,128)(2,1)S(1)}, u32[]{:S(2)}, u32[]{:S(2)}) %collective-permute-start.7) | collective-permute-done | bytes 184352 | tf_op jit(solution)/shard_map/ppermute | solution.py:280
  54.2 1.6 %collective-permute-done.9 = bf16[2,360,128]{2,1,0:T(8,128)(2,1)S(1)} collective-permute-done((bf16[2,360,128]{2,1,0:T(8,128)(2,1)S(1)}, bf16[2,360,128]{2,1,0:T(8,128)(2,1)S(1)}, u32[]{:S(2)}, u32[]{:S(2)}) %collective-permute-start.9) | collective-permute-done | bytes 184352 | tf_op jit(solution)/shard_map/ppermute | solution.py:280
  55.8 0.6 collective-permute-start.10
  56.4 1.5 %collective-permute-start.8 = (bf16[360,128]{1,0:T(8,128)(2,1)S(1)}, bf16[360,128]{1,0:T(8,128)(2,1)S(1)}, u32[]{:S(2)}, u32[]{:S(2)}) collective-permute-start(bf16[360,128]{1,0:T(8,128)(2,1)S(1)} %get-tuple-element.27), channel_id=1, source_target_pairs={{0,4},{1,5},{2,6},{3,7},{4,0},{5,1},{6,2},{7,3},{8,12},{9,13},{10,... | collective-permute-start | bytes 276488 | tf_op jit(solution)/shard_map/ppermute | solution.py:280
  57.9 0.2 collective-permute-done.22
  58.2 1.6 %collective-permute-done.25 = bf16[2,360,128]{2,1,0:T(8,128)(2,1)S(1)} collective-permute-done((bf16[2,360,128]{2,1,0:T(8,128)(2,1)S(1)}, bf16[2,360,128]{2,1,0:T(8,128)(2,1)S(1)}, u32[]{:S(2)}, u32[]{:S(2)}) %collective-permute-start.25) | collective-permute-done | bytes 184352 | tf_op jit(solution)/shard_map/ppermute | solution.py:280
  59.8 1.6 %collective-permute-start.23 = (bf16[360,128]{1,0:T(8,128)(2,1)S(1)}, bf16[360,128]{1,0:T(8,128)(2,1)S(1)}, u32[]{:S(2)}, u32[]{:S(2)}) collective-permute-start(bf16[360,128]{1,0:T(8,128)(2,1)S(1)} %get-tuple-element.33), channel_id=1, source_target_pairs={{0,4},{1,5},{2,6},{3,7},{4,0},{5,1},{6,2},{7,3},{8,12},{9,13},{10,... | collective-permute-start | bytes 276488 | tf_op jit(solution)/shard_map/ppermute | solution.py:280
  61.3 0.3 collective-permute-start.26
  61.8 2.6 %collective-permute-done.23 = bf16[360,128]{1,0:T(8,128)(2,1)S(1)} collective-permute-done((bf16[360,128]{1,0:T(8,128)(2,1)S(1)}, bf16[360,128]{1,0:T(8,128)(2,1)S(1)}, u32[]{:S(2)}, u32[]{:S(2)}) %collective-permute-start.23) | collective-permute-done | bytes 92192 | tf_op jit(solution)/shard_map/ppermute | solution.py:280
  64.4 1.5 %collective-permute-done.26 = bf16[360,128]{1,0:T(8,128)(2,1)S(1)} collective-permute-done((bf16[360,128]{1,0:T(8,128)(2,1)S(1)}, bf16[360,128]{1,0:T(8,128)(2,1)S(1)}, u32[]{:S(2)}, u32[]{:S(2)}) %collective-permute-start.26) | collective-permute-done | bytes 92192 | tf_op jit(solution)/shard_map/ppermute | solution.py:280
  66.0 2.5 %collective-permute-start.27 = (bf16[360,128]{1,0:T(8,128)(2,1)S(1)}, bf16[360,128]{1,0:T(8,128)(2,1)S(1)}, u32[]{:S(2)}, u32[]{:S(2)}) collective-permute-start(bf16[360,128]{1,0:T(8,128)(2,1)S(1)} %get-tuple-element.32), channel_id=1, source_target_pairs={{0,24},{1,25},{2,26},{3,27},{4,28},{5,29},{6,30},{7,31},{8,16},{9,... | collective-permute-start | bytes 276488 | tf_op jit(solution)/shard_map/ppermute | solution.py:280
  68.5 4.0 %collective-permute-done.27 = bf16[360,128]{1,0:T(8,128)(2,1)S(1)} collective-permute-done((bf16[360,128]{1,0:T(8,128)(2,1)S(1)}, bf16[360,128]{1,0:T(8,128)(2,1)S(1)}, u32[]{:S(2)}, u32[]{:S(2)}) %collective-permute-start.27) | collective-permute-done | bytes 92192 | tf_op jit(solution)/shard_map/ppermute | solution.py:280
  72.5 2.0 %collective-permute-done.24 = bf16[360,128]{1,0:T(8,128)(2,1)S(1)} collective-permute-done((bf16[360,128]{1,0:T(8,128)(2,1)S(1)}, bf16[360,128]{1,0:T(8,128)(2,1)S(1)}, u32[]{:S(2)}, u32[]{:S(2)}) %collective-permute-start.24) | collective-permute-done | bytes 92192 | tf_op jit(solution)/shard_map/ppermute | solution.py:280
  74.5 0.7 fusion.8
  (40 shorter events, 0.9 us)
Async XLA Ops:
  0.8 1.0 %copy-start.3 = (bf16[128,1440]{0,1:T(8,128)(2,1)S(1)}, bf16[128,1440]{0,1:T(8,128)(2,1)}, u32[]{:S(2)}) copy-start(bf16[128,1440]{0,1:T(8,128)(2,1)} %param.10) | copy-start | bytes 1105924
  1.8 0.7 copy-start.4
  2.4 0.7 copy-start.5
  4.1 8.6 %collective-permute-start.13 = (bf16[368,128]{1,0:T(8,128)(2,1)S(1)}, bf16[368,128]{1,0:T(8,128)(2,1)S(1)}, u32[]{:S(2)}, u32[]{:S(2)}) collective-permute-start(bf16[368,128]{1,0:T(8,128)(2,1)S(1)} %get-tuple-element.24), channel_id=1, source_target_pairs={{0,24},{1,25},{2,26},{3,27},{4,28},{5,29},{6,30},{7,31},{8,16},{9,... | collective-permute-start | bytes 282632 | tf_op jit(solution)/shard_map/ppermute | solution.py:280
  9.2 8.0 %collective-permute-start.12 = (bf16[368,128]{1,0:T(8,128)(2,1)S(1)}, bf16[368,128]{1,0:T(8,128)(2,1)S(1)}, u32[]{:S(2)}, u32[]{:S(2)}) collective-permute-start(bf16[368,128]{1,0:T(8,128)(2,1)S(1)} %get-tuple-element.24), channel_id=1, source_target_pairs={{0,16},{1,17},{2,18},{3,19},{4,20},{5,21},{6,22},{7,23},{8,24},{9,... | collective-permute-start | bytes 282632 | tf_op jit(solution)/shard_map/ppermute | solution.py:280
  9.2 9.6 %collective-permute-start.2 = (bf16[2,368,128]{2,1,0:T(8,128)(2,1)S(1)}, bf16[2,368,128]{2,1,0:T(8,128)(2,1)S(1)}, u32[]{:S(2)}, u32[]{:S(2)}) collective-permute-start(bf16[2,368,128]{2,1,0:T(8,128)(2,1)S(1)} %get-tuple-element.16.refs_1_), channel_id=1, source_target_pairs={{0,8},{1,9},{2,10},{3,11},{4,12},{5,13},{6,14},{7,15},{8,0},{9,1},... | collective-permute-start | bytes 565256 | tf_op jit(solution)/shard_map/ppermute | solution.py:280
  9.9 11.3 %collective-permute-start = (bf16[2,368,128]{2,1,0:T(8,128)(2,1)S(1)}, bf16[2,368,128]{2,1,0:T(8,128)(2,1)S(1)}, u32[]{:S(2)}, u32[]{:S(2)}) collective-permute-start(bf16[2,368,128]{2,1,0:T(8,128)(2,1)S(1)} %get-tuple-element.16.refs_1_), channel_id=1, source_target_pairs={{0,4},{1,5},{2,6},{3,7},{4,0},{5,1},{6,2},{7,3},{8,12},{9,13},{10,... | collective-permute-start | bytes 565256 | tf_op jit(solution)/shard_map/ppermute | solution.py:280
  17.3 7.7 %collective-permute-start.17 = (bf16[2,368,128]{2,1,0:T(8,128)(2,1)S(1)}, bf16[2,368,128]{2,1,0:T(8,128)(2,1)S(1)}, u32[]{:S(2)}, u32[]{:S(2)}) collective-permute-start(bf16[2,368,128]{2,1,0:T(8,128)(2,1)S(1)} %pad_maximum_fusion.refs_1_), channel_id=1, source_target_pairs={{0,4},{1,5},{2,6},{3,7},{4,0},{5,1},{6,2},{7,3},{8,12},{9,13},{10,... | collective-permute-start | bytes 565256 | tf_op jit(solution)/shard_map/ppermute | solution.py:280
  18.8 8.2 %collective-permute-start.4 = (bf16[2,368,128]{2,1,0:T(8,128)(2,1)S(1)}, bf16[2,368,128]{2,1,0:T(8,128)(2,1)S(1)}, u32[]{:S(2)}, u32[]{:S(2)}) collective-permute-start(bf16[2,368,128]{2,1,0:T(8,128)(2,1)S(1)} %collective-permute-done.2.refs_5_), channel_id=1, source_target_pairs={{0,4},{1,5},{2,6},{3,7},{4,0},{5,1},{6,2},{7,3},{8,12},{9,13},{10,... | collective-permute-start | bytes 565256 | tf_op jit(solution)/shard_map/ppermute | solution.py:280
  19.6 14.4 %collective-permute-start.15 = (bf16[2,368,128]{2,1,0:T(8,128)(2,1)S(1)}, bf16[2,368,128]{2,1,0:T(8,128)(2,1)S(1)}, u32[]{:S(2)}, u32[]{:S(2)}) collective-permute-start(bf16[2,368,128]{2,1,0:T(8,128)(2,1)S(1)} %pad_maximum_fusion.refs_1_), channel_id=1, source_target_pairs={{0,2},{1,3},{2,0},{3,1},{4,6},{5,7},{6,4},{7,5},{8,10},{9,11},{10,... | collective-permute-start | bytes 565256 | tf_op jit(solution)/shard_map/ppermute | solution.py:280
  21.1 13.4 %collective-permute-start.1 = (bf16[2,368,128]{2,1,0:T(8,128)(2,1)S(1)}, bf16[2,368,128]{2,1,0:T(8,128)(2,1)S(1)}, u32[]{:S(2)}, u32[]{:S(2)}) collective-permute-start(bf16[2,368,128]{2,1,0:T(8,128)(2,1)S(1)} %collective-permute-done.refs_3_), channel_id=1, source_target_pairs={{0,1},{1,0},{2,3},{3,2},{4,5},{5,4},{6,7},{7,6},{8,9},{9,8},{10,11... | collective-permute-start | bytes 565256 | tf_op jit(solution)/shard_map/ppermute | solution.py:280
  21.2 13.5 %collective-permute-start.3 = (bf16[2,368,128]{2,1,0:T(8,128)(2,1)S(1)}, bf16[2,368,128]{2,1,0:T(8,128)(2,1)S(1)}, u32[]{:S(2)}, u32[]{:S(2)}) collective-permute-start(bf16[2,368,128]{2,1,0:T(8,128)(2,1)S(1)} %collective-permute-done.2.refs_5_), channel_id=1, source_target_pairs={{0,1},{1,0},{2,3},{3,2},{4,5},{5,4},{6,7},{7,6},{8,9},{9,8},{10,11... | collective-permute-start | bytes 565256 | tf_op jit(solution)/shard_map/ppermute | solution.py:280
  25.0 10.1 %collective-permute-start.19 = (bf16[2,368,128]{2,1,0:T(8,128)(2,1)S(1)}, bf16[2,368,128]{2,1,0:T(8,128)(2,1)S(1)}, u32[]{:S(2)}, u32[]{:S(2)}) collective-permute-start(bf16[2,368,128]{2,1,0:T(8,128)(2,1)S(1)} %collective-permute-done.17.refs_5_), channel_id=1, source_target_pairs={{0,2},{1,3},{2,0},{3,1},{4,6},{5,7},{6,4},{7,5},{8,10},{9,11},{10,... | collective-permute-start | bytes 565256 | tf_op jit(solution)/shard_map/ppermute | solution.py:280
  27.0 8.1 %collective-permute-start.5 = (bf16[2,368,128]{2,1,0:T(8,128)(2,1)S(1)}, bf16[2,368,128]{2,1,0:T(8,128)(2,1)S(1)}, u32[]{:S(2)}, u32[]{:S(2)}) collective-permute-start(bf16[2,368,128]{2,1,0:T(8,128)(2,1)S(1)} %collective-permute-done.4.refs_7_), channel_id=1, source_target_pairs={{0,1},{1,0},{2,3},{3,2},{4,5},{5,4},{6,7},{7,6},{8,9},{9,8},{10,11... | collective-permute-start | bytes 565256 | tf_op jit(solution)/shard_map/ppermute | solution.py:280
  27.0 1.2 %copy-start = (bf16[1,1440,360]{2,1,0:T(8,128)(2,1)S(1)}, bf16[1,1440,360]{2,1,0:T(8,128)(2,1)}, u32[]{:S(2)}) copy-start(bf16[1,1440,360]{2,1,0:T(8,128)(2,1)} %param.14) | copy-start | bytes 3110404
  28.3 1.2 %copy-start.1 = (bf16[1,1440,360]{2,1,0:T(8,128)(2,1)S(1)}, bf16[1,1440,360]{2,1,0:T(8,128)(2,1)}, u32[]{:S(2)}) copy-start(bf16[1,1440,360]{2,1,0:T(8,128)(2,1)} %param.16) | copy-start | bytes 3110404
  29.5 1.2 %copy-start.2 = (bf16[1,360,1440]{2,1,0:T(8,128)(2,1)S(1)}, bf16[1,360,1440]{2,1,0:T(8,128)(2,1)}, u32[]{:S(2)}) copy-start(bf16[1,360,1440]{2,1,0:T(8,128)(2,1)} %param.18) | copy-start | bytes 3110404
  30.8 0.7 copy-start.6
  31.5 0.7 copy-start.7
  32.1 0.7 copy-start.8
  34.0 7.0 %collective-permute-start.14 = (bf16[2,368,128]{2,1,0:T(8,128)(2,1)S(1)}, bf16[2,368,128]{2,1,0:T(8,128)(2,1)S(1)}, u32[]{:S(2)}, u32[]{:S(2)}) collective-permute-start(bf16[2,368,128]{2,1,0:T(8,128)(2,1)S(1)} %pad_maximum_fusion.refs_1_), channel_id=1, source_target_pairs={{0,1},{1,0},{2,3},{3,2},{4,5},{5,4},{6,7},{7,6},{8,9},{9,8},{10,11... | collective-permute-start | bytes 565256 | tf_op jit(solution)/shard_map/ppermute | solution.py:280
  34.6 6.5 %collective-permute-start.18 = (bf16[2,368,128]{2,1,0:T(8,128)(2,1)S(1)}, bf16[2,368,128]{2,1,0:T(8,128)(2,1)S(1)}, u32[]{:S(2)}, u32[]{:S(2)}) collective-permute-start(bf16[2,368,128]{2,1,0:T(8,128)(2,1)S(1)} %collective-permute-done.17.refs_5_), channel_id=1, source_target_pairs={{0,1},{1,0},{2,3},{3,2},{4,5},{5,4},{6,7},{7,6},{8,9},{9,8},{10,11... | collective-permute-start | bytes 565256 | tf_op jit(solution)/shard_map/ppermute | solution.py:280
  34.7 6.4 %collective-permute-start.16 = (bf16[2,368,128]{2,1,0:T(8,128)(2,1)S(1)}, bf16[2,368,128]{2,1,0:T(8,128)(2,1)S(1)}, u32[]{:S(2)}, u32[]{:S(2)}) collective-permute-start(bf16[2,368,128]{2,1,0:T(8,128)(2,1)S(1)} %collective-permute-done.15.refs_3_), channel_id=1, source_target_pairs={{0,1},{1,0},{2,3},{3,2},{4,5},{5,4},{6,7},{7,6},{8,9},{9,8},{10,11... | collective-permute-start | bytes 565256 | tf_op jit(solution)/shard_map/ppermute | solution.py:280
  35.1 6.0 %collective-permute-start.20 = (bf16[2,368,128]{2,1,0:T(8,128)(2,1)S(1)}, bf16[2,368,128]{2,1,0:T(8,128)(2,1)S(1)}, u32[]{:S(2)}, u32[]{:S(2)}) collective-permute-start(bf16[2,368,128]{2,1,0:T(8,128)(2,1)S(1)} %collective-permute-done.19.refs_7_), channel_id=1, source_target_pairs={{0,1},{1,0},{2,3},{3,2},{4,5},{5,4},{6,7},{7,6},{8,9},{9,8},{10,11... | collective-permute-start | bytes 565256 | tf_op jit(solution)/shard_map/ppermute | solution.py:280
  40.6 6.0 %collective-permute-start.6 = (bf16[8,360,128]{2,1,0:T(8,128)(2,1)S(1)}, bf16[8,360,128]{2,1,0:T(8,128)(2,1)S(1)}, u32[]{:S(2)}, u32[]{:S(2)}) collective-permute-start(bf16[8,360,128]{2,1,0:T(8,128)(2,1)S(1)} %get-tuple-element.23), channel_id=1, source_target_pairs={{0,1},{1,0},{2,3},{3,2},{4,5},{5,4},{6,7},{7,6},{8,9},{9,8},{10,11... | collective-permute-start | bytes 2211848 | tf_op jit(solution)/shard_map/ppermute | solution.py:280
  46.4 3.3 %collective-permute-start.21 = (bf16[8,360,128]{2,1,0:T(8,128)(2,1)S(1)}, bf16[8,360,128]{2,1,0:T(8,128)(2,1)S(1)}, u32[]{:S(2)}, u32[]{:S(2)}) collective-permute-start(bf16[8,360,128]{2,1,0:T(8,128)(2,1)S(1)} %get-tuple-element.26), channel_id=1, source_target_pairs={{0,1},{1,0},{2,3},{3,2},{4,5},{5,4},{6,7},{7,6},{8,9},{9,8},{10,11... | collective-permute-start | bytes 2211848 | tf_op jit(solution)/shard_map/ppermute | solution.py:280
  46.7 7.5 %collective-permute-start.7 = (bf16[2,360,128]{2,1,0:T(8,128)(2,1)S(1)}, bf16[2,360,128]{2,1,0:T(8,128)(2,1)S(1)}, u32[]{:S(2)}, u32[]{:S(2)}) collective-permute-start(bf16[2,360,128]{2,1,0:T(8,128)(2,1)S(1)} %get-tuple-element.29), channel_id=1, source_target_pairs={{0,2},{1,3},{2,0},{3,1},{4,6},{5,7},{6,4},{7,5},{8,10},{9,11},{10,... | collective-permute-start | bytes 552968 | tf_op jit(solution)/shard_map/ppermute | solution.py:280
  48.3 7.5 %collective-permute-start.9 = (bf16[2,360,128]{2,1,0:T(8,128)(2,1)S(1)}, bf16[2,360,128]{2,1,0:T(8,128)(2,1)S(1)}, u32[]{:S(2)}, u32[]{:S(2)}) collective-permute-start(bf16[2,360,128]{2,1,0:T(8,128)(2,1)S(1)} %get-tuple-element.30), channel_id=1, source_target_pairs={{0,4},{1,5},{2,6},{3,7},{4,0},{5,1},{6,2},{7,3},{8,12},{9,13},{10,... | collective-permute-start | bytes 552968 | tf_op jit(solution)/shard_map/ppermute | solution.py:280
  49.9 8.3 %collective-permute-start.22 = (bf16[2,360,128]{2,1,0:T(8,128)(2,1)S(1)}, bf16[2,360,128]{2,1,0:T(8,128)(2,1)S(1)}, u32[]{:S(2)}, u32[]{:S(2)}) collective-permute-start(bf16[2,360,128]{2,1,0:T(8,128)(2,1)S(1)} %get-tuple-element.35), channel_id=1, source_target_pairs={{0,2},{1,3},{2,0},{3,1},{4,6},{5,7},{6,4},{7,5},{8,10},{9,11},{10,... | collective-permute-start | bytes 552968 | tf_op jit(solution)/shard_map/ppermute | solution.py:280
  50.5 9.3 %collective-permute-start.25 = (bf16[2,360,128]{2,1,0:T(8,128)(2,1)S(1)}, bf16[2,360,128]{2,1,0:T(8,128)(2,1)S(1)}, u32[]{:S(2)}, u32[]{:S(2)}) collective-permute-start(bf16[2,360,128]{2,1,0:T(8,128)(2,1)S(1)} %get-tuple-element.36), channel_id=1, source_target_pairs={{0,4},{1,5},{2,6},{3,7},{4,0},{5,1},{6,2},{7,3},{8,12},{9,13},{10,... | collective-permute-start | bytes 552968 | tf_op jit(solution)/shard_map/ppermute | solution.py:280
  55.8 5.8 %collective-permute-start.10 = (bf16[360,128]{1,0:T(8,128)(2,1)S(1)}, bf16[360,128]{1,0:T(8,128)(2,1)S(1)}, u32[]{:S(2)}, u32[]{:S(2)}) collective-permute-start(bf16[360,128]{1,0:T(8,128)(2,1)S(1)} %get-tuple-element.28), channel_id=1, source_target_pairs={{0,2},{1,3},{2,0},{3,1},{4,6},{5,7},{6,4},{7,5},{8,10},{9,11},{10,... | collective-permute-start | bytes 276488 | tf_op jit(solution)/shard_map/ppermute | solution.py:280
  56.4 12.1 %collective-permute-start.8 = (bf16[360,128]{1,0:T(8,128)(2,1)S(1)}, bf16[360,128]{1,0:T(8,128)(2,1)S(1)}, u32[]{:S(2)}, u32[]{:S(2)}) collective-permute-start(bf16[360,128]{1,0:T(8,128)(2,1)S(1)} %get-tuple-element.27), channel_id=1, source_target_pairs={{0,4},{1,5},{2,6},{3,7},{4,0},{5,1},{6,2},{7,3},{8,12},{9,13},{10,... | collective-permute-start | bytes 276488 | tf_op jit(solution)/shard_map/ppermute | solution.py:280
  59.8 4.6 %collective-permute-start.23 = (bf16[360,128]{1,0:T(8,128)(2,1)S(1)}, bf16[360,128]{1,0:T(8,128)(2,1)S(1)}, u32[]{:S(2)}, u32[]{:S(2)}) collective-permute-start(bf16[360,128]{1,0:T(8,128)(2,1)S(1)} %get-tuple-element.33), channel_id=1, source_target_pairs={{0,4},{1,5},{2,6},{3,7},{4,0},{5,1},{6,2},{7,3},{8,12},{9,13},{10,... | collective-permute-start | bytes 276488 | tf_op jit(solution)/shard_map/ppermute | solution.py:280
  61.3 4.6 %collective-permute-start.26 = (bf16[360,128]{1,0:T(8,128)(2,1)S(1)}, bf16[360,128]{1,0:T(8,128)(2,1)S(1)}, u32[]{:S(2)}, u32[]{:S(2)}) collective-permute-start(bf16[360,128]{1,0:T(8,128)(2,1)S(1)} %get-tuple-element.34), channel_id=1, source_target_pairs={{0,2},{1,3},{2,0},{3,1},{4,6},{5,7},{6,4},{7,5},{8,10},{9,11},{10,... | collective-permute-start | bytes 276488 | tf_op jit(solution)/shard_map/ppermute | solution.py:280
  61.7 6.8 %collective-permute-start.11 = (bf16[360,128]{1,0:T(8,128)(2,1)S(1)}, bf16[360,128]{1,0:T(8,128)(2,1)S(1)}, u32[]{:S(2)}, u32[]{:S(2)}) collective-permute-start(bf16[360,128]{1,0:T(8,128)(2,1)S(1)} %fusion.2), channel_id=1, source_target_pairs={{0,8},{1,9},{2,10},{3,11},{4,12},{5,13},{6,14},{7,15},{8,0},{9,1},... | collective-permute-start | bytes 276488 | tf_op jit(solution)/shard_map/ppermute | solution.py:280
  66.0 6.5 %collective-permute-start.27 = (bf16[360,128]{1,0:T(8,128)(2,1)S(1)}, bf16[360,128]{1,0:T(8,128)(2,1)S(1)}, u32[]{:S(2)}, u32[]{:S(2)}) collective-permute-start(bf16[360,128]{1,0:T(8,128)(2,1)S(1)} %get-tuple-element.32), channel_id=1, source_target_pairs={{0,24},{1,25},{2,26},{3,27},{4,28},{5,29},{6,30},{7,31},{8,16},{9,... | collective-permute-start | bytes 276488 | tf_op jit(solution)/shard_map/ppermute | solution.py:280
  68.5 6.0 %collective-permute-start.24 = (bf16[360,128]{1,0:T(8,128)(2,1)S(1)}, bf16[360,128]{1,0:T(8,128)(2,1)S(1)}, u32[]{:S(2)}, u32[]{:S(2)}) collective-permute-start(bf16[360,128]{1,0:T(8,128)(2,1)S(1)} %get-tuple-element.31), channel_id=1, source_target_pairs={{0,16},{1,17},{2,18},{3,19},{4,20},{5,21},{6,22},{7,23},{8,24},{9,... | collective-permute-start | bytes 276488 | tf_op jit(solution)/shard_map/ppermute | solution.py:280

commit v4 on v3

--- a/solution.py
+++ b/solution.py
@@ -66,6 +66,9 @@
     return mixed.astype(jnp.bfloat16)
 
 
+tied = lax.optimization_barrier
+
+
 def round_up(number, step):
     return -(-number // step) * step
 
@@ -77,19 +80,10 @@
     return total.astype(jnp.bfloat16)
 
 
-def arrange_kernel(
-    groups,
-    gate_ref,
-    up_ref,
-    down_ref,
-    gate_bias_ref,
-    up_bias_ref,
-    down_bias_ref,
-    gate_up_out,
-    down_out,
-    bias_out,
-    down_bias_out,
-):
+def arrange_kernel(groups, *refs):
+    gate_up_out, down_out, bias_out, down_bias_out = refs[6:10]
+    gate_ref, up_ref, down_ref, gate_bias_ref, up_bias_ref, down_bias_ref = refs[10:16]
+    fetch(refs[:6], refs[10:16], refs[16])
     features, hidden = gate_ref.shape
     quarter = features // groups
     hidden_pad, block = round_up(hidden, 128), round_up(quarter, 128)
@@ -118,8 +112,13 @@
 def arrange(groups, lanes, gate, up, down, gate_bias, up_bias, down_bias):
     features, hidden = gate.shape
     hidden_pad, block = round_up(hidden, 128), round_up(features // groups, 128)
+    arrays = (gate, up, down, gate_bias, up_bias, down_bias)
     return pl.pallas_call(
         functools.partial(arrange_kernel, groups),
+        in_specs=[pl.BlockSpec(memory_space=pltpu.HBM)] * len(arrays),
+        out_specs=[pl.BlockSpec(memory_space=pltpu.VMEM)] * 4,
+        scratch_shapes=[pltpu.VMEM(a.shape, a.dtype) for a in arrays]
+        + [pltpu.SemaphoreType.DMA((len(arrays),))],
         out_shape=[
             jax.ShapeDtypeStruct((2 * hidden_pad, groups * block), jnp.bfloat16),
             jax.ShapeDtypeStruct((groups * block, hidden_pad), jnp.bfloat16),
@@ -130,17 +129,31 @@
         cost_estimate=pl.CostEstimate(
             flops=0, bytes_accessed=8 * gate.size * 2, transcendentals=0
         ),
-    )(gate, up, down, gate_bias, up_bias, down_bias)
-
-
-def pieces_kernel(groups, per, experts, place_ref, tokens_ref, gain_ref, ids_ref, weights_ref, one_ref, near_ref, far_ref):
+    )(*arrays)
+
+
+def fetch(sources, targets, sems):
+    copies = [
+        pltpu.make_async_copy(source, target, sems.at[n])
+        for n, (source, target) in enumerate(zip(sources, targets))
+    ]
+    for copy in copies:
+        copy.start()
+    for copy in copies:
+        copy.wait()
+
+
+def pieces_kernel(groups, per, experts, place_ref, *refs):
+    sources, (one_ref, near_ref, far_ref) = refs[:4], refs[4:7]
+    tokens_ref, gain_ref, ids_ref, weights_ref = refs[7:11]
+    fetch(sources, refs[7:11], refs[11])
     features, lanes = tokens_ref.shape
     quarter = features // groups
     tail = one_ref.shape[0] - quarter
     rep = place_ref[0]
     values = tokens_ref[...].astype(jnp.float32)
     scale = lax.rsqrt(jnp.mean(values * values, axis=0, keepdims=True) + 1e-05)
-    gain = jnp.broadcast_to(gain_ref[...], (lanes, features)).T
+    gain = jnp.broadcast_to(gain_ref[...].reshape(1, features), (lanes, features)).T
     normed = values * scale * gain
     row = lax.broadcasted_iota(jnp.int32, (tail, lanes), 0)
     chosen = lax.broadcasted_iota(jnp.int32, (round_up(experts, 8), lanes), 0)
@@ -177,14 +190,16 @@
     features, lanes = tokens.shape
     rows = round_up(features // groups + 3 * per, 16)
     pair = jax.ShapeDtypeStruct((groups // 2, rows, lanes), jnp.bfloat16)
-    whole = pl.BlockSpec(memory_space=pltpu.VMEM)
+    arrays = (tokens, norm_gain, expert_ids, route_weights)
     return pl.pallas_call(
         functools.partial(pieces_kernel, groups, per, experts),
-        in_specs=[pl.BlockSpec(memory_space=pltpu.SMEM)] + [whole] * 4,
-        out_specs=[whole] * 3,
+        in_specs=[pl.BlockSpec(memory_space=pltpu.SMEM)] + [pl.BlockSpec(memory_space=pltpu.HBM)] * 4,
+        out_specs=[pl.BlockSpec(memory_space=pltpu.VMEM)] * 3,
         out_shape=[jax.ShapeDtypeStruct((rows, lanes), jnp.bfloat16), pair, pair],
+        scratch_shapes=[pltpu.VMEM(a.shape, a.dtype) for a in arrays]
+        + [pltpu.SemaphoreType.DMA((len(arrays),))],
         compiler_params=pltpu.CompilerParams(vmem_limit_bytes=40 * 2**20),
-    )(place, tokens, norm_gain, expert_ids, route_weights)
+    )(place, *arrays)
 
 
 def expert_kernel(quarter, per, blocks, slots, *refs):
@@ -197,11 +212,11 @@
     size = gate_up_ref.shape[1] // groups
     hidden = gate_up_ref.shape[0] // 2
     rep, seq = place_ref[0], place_ref[1]
-    halves = len(scratch) // 2
+    halves = len(scratch)
     count = len(blocks) // halves
     row = lax.broadcasted_iota(jnp.int32, (piece_rows - quarter, lanes), 0)
     for half in range(halves):
-        rows_ref, sums_ref = scratch[half], scratch[halves + half]
+        rows_ref = scratch[half]
         if size > piece_rows:
             for k in range(groups):
                 rows_ref[k * size + piece_rows : (k + 1) * size, :] = jnp.zeros(
@@ -222,9 +237,9 @@
         both = jnp.dot(gate_up_ref[...], rows_ref[...], preferred_element_type=jnp.float32)
         both = both + jnp.concatenate([bias_ref[...]] * count, axis=1)
         activated = gated(both[:hidden], both[hidden:])
-        sums_ref[...] = jnp.dot(down_ref[...], activated, preferred_element_type=jnp.float32)
         for k in range(groups):
-            rows = sums_ref[pl.ds(pl.multiple_of((rep ^ k) * size, size), size), :]
+            own_rows = down_ref[pl.ds(pl.multiple_of((rep ^ k) * size, size), size), :]
+            rows = jnp.dot(own_rows, activated, preferred_element_type=jnp.float32)
             if k == 0:
                 rows = rows + jnp.concatenate([down_bias_ref[...]] * count, axis=1)
             rows = (rows * wide).astype(jnp.bfloat16)
@@ -233,7 +248,8 @@
                 target[slots[half * count + j][k // 2]] = rows[:quarter, j * lanes : (j + 1) * lanes]
 
 
-def run_expert(place, arrays, blocks, slots, weights, quarter, per, halves):
+def run_expert(place, arrays, blocks, slots, weights, sizes, halves):
+    quarter, per = sizes
     lanes = arrays[0].shape[2]
     gate_up, down = weights[0], weights[1]
     tokens = len(blocks) * lanes
@@ -245,8 +261,7 @@
         in_specs=[pl.BlockSpec(memory_space=pltpu.SMEM)] + [whole] * (len(arrays) + len(weights)),
         out_specs=[whole, whole],
         out_shape=[out, out],
-        scratch_shapes=[pltpu.VMEM((gate_up.shape[1], columns), jnp.bfloat16)] * halves
-        + [pltpu.VMEM((down.shape[0], columns), jnp.float32)] * halves,
+        scratch_shapes=[pltpu.VMEM((gate_up.shape[1], columns), jnp.bfloat16)] * halves,
         compiler_params=pltpu.CompilerParams(vmem_limit_bytes=40 * 2**20),
         cost_estimate=pl.CostEstimate(
             flops=4 * tokens * (gate_up.size + down.size),
@@ -282,7 +297,7 @@
     per = -(-experts // groups)
     place = jnp.stack([rep, seq]).astype(jnp.int32)
     one, near, far = make_pieces(
-        place, tokens.T, norm_gain[None], expert_ids.T, route_weights.T, groups, per, experts
+        place, tokens.T, norm_gain, expert_ids.T, route_weights.T, groups, per, experts
     )
     z_2, z_3 = swap(one, 2 * along_z), swap(one, 3 * along_z)
     x_0 = swap(near, along_x)
@@ -290,35 +305,45 @@
     weights = arrange(
         groups, lanes, gate_weight[0], up_weight[0], down_weight[0], gate_bias, up_bias, down_bias
     )
+    z_2, z_3, weights = tied((z_2, z_3, weights))
     z_high = jnp.stack([z_2, z_3])
     x_high, y_high = swap(z_high, along_x), swap(z_high, along_y)
+    z_1, x_high, y_high = tied((z_1, x_high, y_high))
+    corner = swap(x_high, along_y)
     x_1 = swap(z_1, along_x)
-    corner = swap(x_high, along_y)
-
-    low = (near, far, x_0, swap(x_0, core), z_1, swap(z_1, core), x_1, swap(x_1, core))
+
+    def pairs(first):
+        return [[(first + 2 * x + k % 2, k // 2) for k in range(groups)] for x in range(2)]
+
+    slots_a, slots_b = ((2, 0), (3, 1)), ((2, 3), (0, 1))
     high = (z_high, swap(z_high, core), y_high, swap(y_high, core))
     high = high + (x_high, swap(x_high, core), corner, swap(corner, core))
-    low_blocks = [[(2 * n + k % 2, k // 2) for k in range(groups)] for n in range(4)]
-    high_blocks = [
-        [(4 * x + k, line) for k in range(groups)] for line in range(2) for x in range(2)
-    ]
-    slots = ((4, 0), (5, 1), (6, 7), (2, 3))
-
-    def plane(keep, send):
-        got = swap(send, core)
-        first_y = swap(add_up(keep[0:2], got[0:2]), along_y)
-        first_x = swap(add_up(keep[2:4], got[2:4]), along_x)
-        last_x = swap(add_up(keep[5], got[5], first_y[1]), along_x)
-        last_y = swap(add_up(keep[7], got[7], first_x[1]), along_y)
+    blocks = [[(4 * x + k, line) for k in range(groups)] for line in range(2) for x in range(2)]
+    slots = slots_a + tuple((4 + i, 4 + j) for i, j in slots_b)
+    sizes = (quarter, per)
+    keep_0, send_0 = run_expert(
+        place, (near, far, x_0, swap(x_0, core)), pairs(0), slots_a, weights, sizes, 1
+    )
+    keep_high, send_high = run_expert(place, high, blocks, slots, weights, sizes, 2)
+    got_0 = swap(send_0, core)
+    got = swap(send_high, core)
+    near_1 = (z_1, swap(z_1, core), x_1, swap(x_1, core))
+    got, near_1 = tied((got, near_1))
+    keep_1, send_1 = run_expert(place, near_1, pairs(0), slots_b, weights, sizes, 1)
+    keep_0, got_0, keep_1, send_1 = tied((keep_0, got_0, keep_1, send_1))
+
+    def plane(keep_a, got_a, keep_b, got_b):
+        first_y = swap(add_up(keep_a[0:2], got_a[0:2]), along_y)
+        first_x = swap(add_up(keep_b[0:2], got_b[0:2]), along_x)
+        last_x = swap(add_up(keep_a[3], got_a[3], first_y[1]), along_x)
+        last_y = swap(add_up(keep_b[3], got_b[3], first_x[1]), along_y)
         return (
-            add_up(keep[4], got[4], first_y[0], last_x),
-            add_up(keep[6], got[6], first_x[0], last_y),
+            add_up(keep_a[2], got_a[2], first_y[0], last_x),
+            add_up(keep_b[2], got_b[2], first_x[0], last_y),
         )
 
-    keep_low, send_low = run_expert(place, low, low_blocks, slots, weights, quarter, per, 2)
-    keep_high, send_high = run_expert(place, high, high_blocks, slots, weights, quarter, per, 2)
-    line_2, line_3 = plane(keep_high, send_high)
-    line_0, line_1 = plane(keep_low, send_low)
+    line_2, line_3 = plane(keep_high[:4], got[:4], keep_high[4:], got[4:])
+    line_0, line_1 = plane(keep_0, got_0, keep_1, swap(send_1, core))
     mixed = add_up(
         line_0, swap(line_1, along_z), swap(line_2, 2 * along_z), swap(line_3, 3 * along_z)
     )

time: 75.6 us -> 79.8 us (1.056)
  waiting for transfers between devices: 25.4 us -> 28.9 us
    ppermute x28 -> x29, waiting for transfers between devices: 25.4 us -> 28.9 us  [swap(): lax.ppermute(array, ('seq', 'rep'), [(i, i ^ step) for i in range(devices)])]
    unnamed x18 -> x20, local copies, waits for them, and re-layouts: 8.12 us -> 8.82 us
    pallas_call x2 -> x3, Pallas kernels: 10.7 us -> 10.6 us  [run_expert(): pl.pallas_call(functools.partial(expert_kernel, quarter, per, blocks, slo...]
    ppermute x28 -> x29, starting transfers between devices: 26.7 us -> 26.8 us  [swap(): lax.ppermute(array, ('seq', 'rep'), [(i, i ^ step) for i in range(devices)])]
  transfers between devices with their start and end apart: 28 -> 29, of which waited for: 12 -> 13; matrix products, arithmetic and copies ran while one was open for 1% -> 1% of each run, Pallas kernels for 16% -> 9%
where the time goes in v4:
time: 79.8 us; the launch traced here: 79.4 us
  waiting for transfers between devices  28.9 us (36%)
  starting transfers between devices  26.8 us (34%)
  Pallas kernels  13.4 us (17%)
  local copies, waits for them, and re-layouts  8.82 us (11%)
  other arithmetic  1.37 us (2%)
    ppermute x29, waiting for transfers between devices, swap(): lax.ppermute(array, ('seq', 'rep'), [(i, i ^ step) for i in range(devices)])  28.9 us
    ppermute x29, starting transfers between devices, swap(): lax.ppermute(array, ('seq', 'rep'), [(i, i ^ step) for i in range(devices)])  26.8 us
    pallas_call x3, Pallas kernels, run_expert(): pl.pallas_call(functools.partial(expert_kernel, quarter, per, blocks, slo...  10.6 us
    unnamed x20, local copies, waits for them, and re-layouts  8.82 us
    pallas_call x1, Pallas kernels, arrange(): pl.pallas_call(functools.partial(arrange_kernel, groups), in_specs=[pl.Bl...  1.66 us
  transfers between devices with their start and end apart: 29, of which 13 were waited for; matrix products, arithmetic and copies ran while one was open for 1% of the time, Pallas kernels for 9%

profile of v4, /device:TPU:0, one launch (start us, length us, event | category | flops | bytes accessed | tf_op | source)
XLA Modules:
  0.0 79.4 jit_solution(10508505527628557266)
XLA Ops:
  0.1 1.0 %copy-done.3 = bf16[128,1440]{0,1:T(8,128)(2,1)S(1)} copy-done((bf16[128,1440]{0,1:T(8,128)(2,1)S(1)}, bf16[128,1440]{0,1:T(8,128)(2,1)}, u32[]{:S(2)}) %copy-start.3) | copy-done | bytes 368664
  1.1 0.7 copy-done.4
  1.8 0.7 copy-done.5
  2.4 0.7 copy-done.6
  3.1 1.2 %shard_map.100 = (bf16[368,128]{1,0:T(8,128)(2,1)S(1)}, bf16[2,368,128]{2,1,0:T(8,128)(2,1)S(1)}, bf16[2,368,128]{2,1,0:T(8,128)(2,1)S(1)}) custom-call(s32[2]{0:T(128)S(1)} %pad_add_fusion.place_ref.refs_0_, bf16[1440,128]{1,0:T(8,128)(2,1)S(1)} %bitcast.41, f32[1440]{0:T(1024)S(1)} %copy-done.4, s32[4,128]{1,0:T(4,128)S(1)} %bitcast.42, f32[4,128]{1,0:T(4,128)S(1)} %bitcast.43), custom_call_target="tpu_custom_call" | custom-call | tf_op jit(solution)/shard_map/pallas_call | solution.py:194
  4.3 4.1 %collective-permute-start.2 = (bf16[368,128]{1,0:T(8,128)(2,1)S(1)}, bf16[368,128]{1,0:T(8,128)(2,1)S(1)}, u32[]{:S(2)}, u32[]{:S(2)}) collective-permute-start(bf16[368,128]{1,0:T(8,128)(2,1)S(1)} %get-tuple-element.38), channel_id=1, source_target_pairs={{0,16},{1,17},{2,18},{3,19},{4,20},{5,21},{6,22},{7,23},{8,24},{9,... | collective-permute-start | bytes 282632 | tf_op jit(solution)/shard_map/ppermute | solution.py:295
  8.4 1.3 %collective-permute-start.3 = (bf16[368,128]{1,0:T(8,128)(2,1)S(1)}, bf16[368,128]{1,0:T(8,128)(2,1)S(1)}, u32[]{:S(2)}, u32[]{:S(2)}) collective-permute-start(bf16[368,128]{1,0:T(8,128)(2,1)S(1)} %get-tuple-element.38), channel_id=1, source_target_pairs={{0,24},{1,25},{2,26},{3,27},{4,28},{5,29},{6,30},{7,31},{8,16},{9,... | collective-permute-start | bytes 282632 | tf_op jit(solution)/shard_map/ppermute | solution.py:295
  10.0 1.2 %copy-done = bf16[1,1440,360]{2,1,0:T(8,128)(2,1)S(1)} copy-done((bf16[1,1440,360]{2,1,0:T(8,128)(2,1)S(1)}, bf16[1,1440,360]{2,1,0:T(8,128)(2,1)}, u32[]{:S(2)}) %copy-start) | copy-done | bytes 1036824
  11.2 1.2 %copy-done.1 = bf16[1,1440,360]{2,1,0:T(8,128)(2,1)S(1)} copy-done((bf16[1,1440,360]{2,1,0:T(8,128)(2,1)S(1)}, bf16[1,1440,360]{2,1,0:T(8,128)(2,1)}, u32[]{:S(2)}) %copy-start.1) | copy-done | bytes 1036824
  12.5 1.2 %copy-done.2 = bf16[1,360,1440]{2,1,0:T(8,128)(2,1)S(1)} copy-done((bf16[1,360,1440]{2,1,0:T(8,128)(2,1)S(1)}, bf16[1,360,1440]{2,1,0:T(8,128)(2,1)}, u32[]{:S(2)}) %copy-start.2) | copy-done | bytes 1036824
  13.7 0.7 copy-done.7
  14.4 0.7 copy-done.8
  15.1 0.7 copy-done.9
  15.8 1.7 %shard_map.101 = (bf16[768,1536]{1,0:T(8,128)(2,1)S(1)}, bf16[1536,384]{1,0:T(8,128)(2,1)S(1)}, f32[768,128]{1,0:T(8,128)S(1)}, f32[384,128]{1,0:T(8,128)S(1)}) custom-call(bf16[1440,360]{1,0:T(8,128)(2,1)S(1)} %bitcast.38, bf16[1440,360]{1,0:T(8,128)(2,1)S(1)} %bitcast.39, bf16[360,1440]{1,0:T(8,128)(2,1)S(1)} %bitcast.40, f32[1,360]{1,0:T(1,128)S(1)} %copy-done.7, ...), custom_call_target="tpu_custom_call" | custom-call | bytes 8294400 | tf_op jit(solution)/shard_map/pallas_call | solution.py:116
  17.5 1.6 %collective-permute-start.7 = (bf16[2,368,128]{2,1,0:T(8,128)(2,1)S(1)}, bf16[2,368,128]{2,1,0:T(8,128)(2,1)S(1)}, u32[]{:S(2)}, u32[]{:S(2)}) collective-permute-start(bf16[2,368,128]{2,1,0:T(8,128)(2,1)S(1)} %pad_maximum_fusion.refs_1_), channel_id=1, source_target_pairs={{0,4},{1,5},{2,6},{3,7},{4,0},{5,1},{6,2},{7,3},{8,12},{9,13},{10,... | collective-permute-start | bytes 565256 | tf_op jit(solution)/shard_map/ppermute | solution.py:295
  19.0 1.5 %collective-permute-start.8 = (bf16[2,368,128]{2,1,0:T(8,128)(2,1)S(1)}, bf16[2,368,128]{2,1,0:T(8,128)(2,1)S(1)}, u32[]{:S(2)}, u32[]{:S(2)}) collective-permute-start(bf16[2,368,128]{2,1,0:T(8,128)(2,1)S(1)} %pad_maximum_fusion.refs_1_), channel_id=1, source_target_pairs={{0,2},{1,3},{2,0},{3,1},{4,6},{5,7},{6,4},{7,5},{8,10},{9,11},{10,... | collective-permute-start | bytes 565256 | tf_op jit(solution)/shard_map/ppermute | solution.py:295
  20.5 2.9 %collective-permute-done.7.refs_5_ = bf16[2,368,128]{2,1,0:T(8,128)(2,1)S(1)} collective-permute-done((bf16[2,368,128]{2,1,0:T(8,128)(2,1)S(1)}, bf16[2,368,128]{2,1,0:T(8,128)(2,1)S(1)}, u32[]{:S(2)}, u32[]{:S(2)}) %collective-permute-start.7) | collective-permute-done | bytes 188448 | tf_op jit(solution)/shard_map/ppermute | solution.py:295
  23.4 1.2 %collective-permute-done.8.refs_3_ = bf16[2,368,128]{2,1,0:T(8,128)(2,1)S(1)} collective-permute-done((bf16[2,368,128]{2,1,0:T(8,128)(2,1)S(1)}, bf16[2,368,128]{2,1,0:T(8,128)(2,1)S(1)}, u32[]{:S(2)}, u32[]{:S(2)}) %collective-permute-start.8) | collective-permute-done | bytes 188448 | tf_op jit(solution)/shard_map/ppermute | solution.py:295
  24.7 1.5 %collective-permute-start.11 = (bf16[2,368,128]{2,1,0:T(8,128)(2,1)S(1)}, bf16[2,368,128]{2,1,0:T(8,128)(2,1)S(1)}, u32[]{:S(2)}, u32[]{:S(2)}) collective-permute-start(bf16[2,368,128]{2,1,0:T(8,128)(2,1)S(1)} %collective-permute-done.7.refs_5_), channel_id=1, source_target_pairs={{0,2},{1,3},{2,0},{3,1},{4,6},{5,7},{6,4},{7,5},{8,10},{9,11},{10,... | collective-permute-start | bytes 565256 | tf_op jit(solution)/shard_map/ppermute | solution.py:295
  26.2 0.5 collective-permute-start.10
  26.7 3.5 %collective-permute-done.11.refs_7_ = bf16[2,368,128]{2,1,0:T(8,128)(2,1)S(1)} collective-permute-done((bf16[2,368,128]{2,1,0:T(8,128)(2,1)S(1)}, bf16[2,368,128]{2,1,0:T(8,128)(2,1)S(1)}, u32[]{:S(2)}, u32[]{:S(2)}) %collective-permute-start.11) | collective-permute-done | bytes 188448 | tf_op jit(solution)/shard_map/ppermute | solution.py:295
  30.3 1.4 %collective-permute-done.12.refs_8_ = bf16[2,368,128]{2,1,0:T(8,128)(2,1)S(1)} collective-permute-done((bf16[2,368,128]{2,1,0:T(8,128)(2,1)S(1)}, bf16[2,368,128]{2,1,0:T(8,128)(2,1)S(1)}, u32[]{:S(2)}, u32[]{:S(2)}) %collective-permute-start.12) | collective-permute-done | bytes 188448 | tf_op jit(solution)/shard_map/ppermute | solution.py:295
  31.7 5.1 %shard_map.103 = (bf16[8,360,128]{2,1,0:T(8,128)(2,1)S(1)}, bf16[8,360,128]{2,1,0:T(8,128)(2,1)S(1)}) custom-call(s32[2]{0:T(128)S(1)} %pad_add_fusion.place_ref.refs_0_, bf16[2,368,128]{2,1,0:T(8,128)(2,1)S(1)} %pad_maximum_fusion.refs_1_, bf16[2,368,128]{2,1,0:T(8,128)(2,1)S(1)} %collective-permute-done.5.refs_2_, ...), custom_call_target="tpu_custom_call" | custom-call | flops 3623878656 | bytes 3538944 | tf_op jit(solution)/shard_map/pallas_call | solution.py:259
  37.0 0.5 collective-permute-start
  37.5 1.5 %collective-permute-start.15 = (bf16[2,368,128]{2,1,0:T(8,128)(2,1)S(1)}, bf16[2,368,128]{2,1,0:T(8,128)(2,1)S(1)}, u32[]{:S(2)}, u32[]{:S(2)}) collective-permute-start(bf16[2,368,128]{2,1,0:T(8,128)(2,1)S(1)} %collective-permute-done.6.refs_1_), channel_id=1, source_target_pairs={{0,4},{1,5},{2,6},{3,7},{4,0},{5,1},{6,2},{7,3},{8,12},{9,13},{10,... | collective-permute-start | bytes 565256 | tf_op jit(solution)/shard_map/ppermute | solution.py:295
  39.0 5.5 %collective-permute-done.refs_3_ = bf16[2,368,128]{2,1,0:T(8,128)(2,1)S(1)} collective-permute-done((bf16[2,368,128]{2,1,0:T(8,128)(2,1)S(1)}, bf16[2,368,128]{2,1,0:T(8,128)(2,1)S(1)}, u32[]{:S(2)}, u32[]{:S(2)}) %collective-permute-start) | collective-permute-done | bytes 188448 | tf_op jit(solution)/shard_map/ppermute | solution.py:295
  44.5 0.5 collective-permute-start.14
  45.1 3.0 %collective-permute-done.15.refs_3_ = bf16[2,368,128]{2,1,0:T(8,128)(2,1)S(1)} collective-permute-done((bf16[2,368,128]{2,1,0:T(8,128)(2,1)S(1)}, bf16[2,368,128]{2,1,0:T(8,128)(2,1)S(1)}, u32[]{:S(2)}, u32[]{:S(2)}) %collective-permute-start.15) | collective-permute-done | bytes 188448 | tf_op jit(solution)/shard_map/ppermute | solution.py:295
  48.0 2.7 %shard_map.102 = (bf16[4,360,128]{2,1,0:T(8,128)(2,1)S(1)}, bf16[4,360,128]{2,1,0:T(8,128)(2,1)S(1)}) custom-call(s32[2]{0:T(128)S(1)} %pad_add_fusion.place_ref.refs_0_, bf16[2,368,128]{2,1,0:T(8,128)(2,1)S(1)} %get-tuple-element.36.refs_1_, bf16[2,368,128]{2,1,0:T(8,128)(2,1)S(1)} %get-tuple-element.37.refs_2_, ...), custom_call_target="tpu_custom_call" | custom-call | flops 1811939328 | bytes 3538944 | tf_op jit(solution)/shard_map/pallas_call | solution.py:259
  50.8 0.6 collective-permute-start.4
  51.5 1.6 %collective-permute-start.23 = (bf16[2,360,128]{2,1,0:T(8,128)(2,1)S(1)}, bf16[2,360,128]{2,1,0:T(8,128)(2,1)S(1)}, u32[]{:S(2)}, u32[]{:S(2)}) collective-permute-start(bf16[2,360,128]{2,1,0:T(8,128)(2,1)S(1)} %get-tuple-element.71), channel_id=1, source_target_pairs={{0,2},{1,3},{2,0},{3,1},{4,6},{5,7},{6,4},{7,5},{8,10},{9,11},{10,... | collective-permute-start | bytes 552968 | tf_op jit(solution)/shard_map/ppermute | solution.py:295
  53.1 0.5 collective-permute-start.26
  53.6 2.7 %shard_map.104 = (bf16[4,360,128]{2,1,0:T(8,128)(2,1)S(1)}, bf16[4,360,128]{2,1,0:T(8,128)(2,1)S(1)}) custom-call(s32[2]{0:T(128)S(1)} %pad_add_fusion.place_ref.refs_0_, bf16[2,368,128]{2,1,0:T(8,128)(2,1)S(1)} %collective-permute-done.6.refs_1_, bf16[2,368,128]{2,1,0:T(8,128)(2,1)S(1)} %collective-permute-done.14.refs_2_, ...), custom_call_target="tpu_custom_call" | custom-call | flops 1811939328 | bytes 3538944 | tf_op jit(solution)/shard_map/pallas_call | solution.py:259
  56.5 0.6 collective-permute-start.17
  57.1 1.0 %collective-permute-done.23 = bf16[2,360,128]{2,1,0:T(8,128)(2,1)S(1)} collective-permute-done((bf16[2,360,128]{2,1,0:T(8,128)(2,1)S(1)}, bf16[2,360,128]{2,1,0:T(8,128)(2,1)S(1)}, u32[]{:S(2)}, u32[]{:S(2)}) %collective-permute-start.23) | collective-permute-done | bytes 184352 | tf_op jit(solution)/shard_map/ppermute | solution.py:295
  58.1 1.2 %collective-permute-done.26 = bf16[2,360,128]{2,1,0:T(8,128)(2,1)S(1)} collective-permute-done((bf16[2,360,128]{2,1,0:T(8,128)(2,1)S(1)}, bf16[2,360,128]{2,1,0:T(8,128)(2,1)S(1)}, u32[]{:S(2)}, u32[]{:S(2)}) %collective-permute-start.26) | collective-permute-done | bytes 184352 | tf_op jit(solution)/shard_map/ppermute | solution.py:295
  59.4 0.6 collective-permute-start.24
  60.6 1.6 %collective-permute-start.20 = (bf16[2,360,128]{2,1,0:T(8,128)(2,1)S(1)}, bf16[2,360,128]{2,1,0:T(8,128)(2,1)S(1)}, u32[]{:S(2)}, u32[]{:S(2)}) collective-permute-start(bf16[2,360,128]{2,1,0:T(8,128)(2,1)S(1)} %add_convert_fusion.2), channel_id=1, source_target_pairs={{0,4},{1,5},{2,6},{3,7},{4,0},{5,1},{6,2},{7,3},{8,12},{9,13},{10,... | collective-permute-start | bytes 552968 | tf_op jit(solution)/shard_map/ppermute | solution.py:295
  62.2 1.8 %collective-permute-done.17 = bf16[2,360,128]{2,1,0:T(8,128)(2,1)S(1)} collective-permute-done((bf16[2,360,128]{2,1,0:T(8,128)(2,1)S(1)}, bf16[2,360,128]{2,1,0:T(8,128)(2,1)S(1)}, u32[]{:S(2)}, u32[]{:S(2)}) %collective-permute-start.17) | collective-permute-done | bytes 184352 | tf_op jit(solution)/shard_map/ppermute | solution.py:295
  64.0 1.6 %collective-permute-start.18 = (bf16[360,128]{1,0:T(8,128)(2,1)S(1)}, bf16[360,128]{1,0:T(8,128)(2,1)S(1)}, u32[]{:S(2)}, u32[]{:S(2)}) collective-permute-start(bf16[360,128]{1,0:T(8,128)(2,1)S(1)} %fusion.4), channel_id=1, source_target_pairs={{0,4},{1,5},{2,6},{3,7},{4,0},{5,1},{6,2},{7,3},{8,12},{9,13},{10,... | collective-permute-start | bytes 276488 | tf_op jit(solution)/shard_map/ppermute | solution.py:295
  65.6 2.9 %collective-permute-done.20 = bf16[2,360,128]{2,1,0:T(8,128)(2,1)S(1)} collective-permute-done((bf16[2,360,128]{2,1,0:T(8,128)(2,1)S(1)}, bf16[2,360,128]{2,1,0:T(8,128)(2,1)S(1)}, u32[]{:S(2)}, u32[]{:S(2)}) %collective-permute-start.20) | collective-permute-done | bytes 184352 | tf_op jit(solution)/shard_map/ppermute | solution.py:295
  68.6 0.6 collective-permute-start.21
  69.3 2.9 %collective-permute-start.28 = (bf16[360,128]{1,0:T(8,128)(2,1)S(1)}, bf16[360,128]{1,0:T(8,128)(2,1)S(1)}, u32[]{:S(2)}, u32[]{:S(2)}) collective-permute-start(bf16[360,128]{1,0:T(8,128)(2,1)S(1)} %get-tuple-element.68), channel_id=1, source_target_pairs={{0,24},{1,25},{2,26},{3,27},{4,28},{5,29},{6,30},{7,31},{8,16},{9,... | collective-permute-start | bytes 276488 | tf_op jit(solution)/shard_map/ppermute | solution.py:295
  72.6 0.6 collective-permute-done.21
  73.3 1.8 %collective-permute-start.22 = (bf16[360,128]{1,0:T(8,128)(2,1)S(1)}, bf16[360,128]{1,0:T(8,128)(2,1)S(1)}, u32[]{:S(2)}, u32[]{:S(2)}) collective-permute-start(bf16[360,128]{1,0:T(8,128)(2,1)S(1)} %fusion.2), channel_id=1, source_target_pairs={{0,8},{1,9},{2,10},{3,11},{4,12},{5,13},{6,14},{7,15},{8,0},{9,1},... | collective-permute-start | bytes 276488 | tf_op jit(solution)/shard_map/ppermute | solution.py:295
  75.1 1.3 %collective-permute-done.28 = bf16[360,128]{1,0:T(8,128)(2,1)S(1)} collective-permute-done((bf16[360,128]{1,0:T(8,128)(2,1)S(1)}, bf16[360,128]{1,0:T(8,128)(2,1)S(1)}, u32[]{:S(2)}, u32[]{:S(2)}) %collective-permute-start.28) | collective-permute-done | bytes 92192 | tf_op jit(solution)/shard_map/ppermute | solution.py:295
  76.4 2.3 %collective-permute-done.25 = bf16[360,128]{1,0:T(8,128)(2,1)S(1)} collective-permute-done((bf16[360,128]{1,0:T(8,128)(2,1)S(1)}, bf16[360,128]{1,0:T(8,128)(2,1)S(1)}, u32[]{:S(2)}, u32[]{:S(2)}) %collective-permute-start.25) | collective-permute-done | bytes 92192 | tf_op jit(solution)/shard_map/ppermute | solution.py:295
  78.7 0.7 fusion.8
  (46 shorter events, 2.1 us)
Async XLA Ops:
  0.1 1.0 %copy-start.3 = (bf16[128,1440]{0,1:T(8,128)(2,1)S(1)}, bf16[128,1440]{0,1:T(8,128)(2,1)}, u32[]{:S(2)}) copy-start(bf16[128,1440]{0,1:T(8,128)(2,1)} %param.10) | copy-start | bytes 1105924
  1.1 0.7 copy-start.4
  1.8 0.7 copy-start.5
  2.4 0.7 copy-start.6
  4.3 13.1 %collective-permute-start.2 = (bf16[368,128]{1,0:T(8,128)(2,1)S(1)}, bf16[368,128]{1,0:T(8,128)(2,1)S(1)}, u32[]{:S(2)}, u32[]{:S(2)}) collective-permute-start(bf16[368,128]{1,0:T(8,128)(2,1)S(1)} %get-tuple-element.38), channel_id=1, source_target_pairs={{0,16},{1,17},{2,18},{3,19},{4,20},{5,21},{6,22},{7,23},{8,24},{9,... | collective-permute-start | bytes 282632 | tf_op jit(solution)/shard_map/ppermute | solution.py:295
  8.4 9.0 %collective-permute-start.3 = (bf16[368,128]{1,0:T(8,128)(2,1)S(1)}, bf16[368,128]{1,0:T(8,128)(2,1)S(1)}, u32[]{:S(2)}, u32[]{:S(2)}) collective-permute-start(bf16[368,128]{1,0:T(8,128)(2,1)S(1)} %get-tuple-element.38), channel_id=1, source_target_pairs={{0,24},{1,25},{2,26},{3,27},{4,28},{5,29},{6,30},{7,31},{8,16},{9,... | collective-permute-start | bytes 282632 | tf_op jit(solution)/shard_map/ppermute | solution.py:295
  9.7 10.8 %collective-permute-start.6 = (bf16[2,368,128]{2,1,0:T(8,128)(2,1)S(1)}, bf16[2,368,128]{2,1,0:T(8,128)(2,1)S(1)}, u32[]{:S(2)}, u32[]{:S(2)}) collective-permute-start(bf16[2,368,128]{2,1,0:T(8,128)(2,1)S(1)} %get-tuple-element.36.refs_1_), channel_id=1, source_target_pairs={{0,8},{1,9},{2,10},{3,11},{4,12},{5,13},{6,14},{7,15},{8,0},{9,1},... | collective-permute-start | bytes 565256 | tf_op jit(solution)/shard_map/ppermute | solution.py:295
  10.0 1.2 %copy-start = (bf16[1,1440,360]{2,1,0:T(8,128)(2,1)S(1)}, bf16[1,1440,360]{2,1,0:T(8,128)(2,1)}, u32[]{:S(2)}) copy-start(bf16[1,1440,360]{2,1,0:T(8,128)(2,1)} %param.14) | copy-start | bytes 3110404
  11.2 1.2 %copy-start.1 = (bf16[1,1440,360]{2,1,0:T(8,128)(2,1)S(1)}, bf16[1,1440,360]{2,1,0:T(8,128)(2,1)}, u32[]{:S(2)}) copy-start(bf16[1,1440,360]{2,1,0:T(8,128)(2,1)} %param.16) | copy-start | bytes 3110404
  12.5 1.2 %copy-start.2 = (bf16[1,360,1440]{2,1,0:T(8,128)(2,1)S(1)}, bf16[1,360,1440]{2,1,0:T(8,128)(2,1)}, u32[]{:S(2)}) copy-start(bf16[1,360,1440]{2,1,0:T(8,128)(2,1)} %param.18) | copy-start | bytes 3110404
  13.7 0.7 copy-start.7
  14.4 0.7 copy-start.8
  15.1 0.7 copy-start.9
  17.5 6.0 %collective-permute-start.7 = (bf16[2,368,128]{2,1,0:T(8,128)(2,1)S(1)}, bf16[2,368,128]{2,1,0:T(8,128)(2,1)S(1)}, u32[]{:S(2)}, u32[]{:S(2)}) collective-permute-start(bf16[2,368,128]{2,1,0:T(8,128)(2,1)S(1)} %pad_maximum_fusion.refs_1_), channel_id=1, source_target_pairs={{0,4},{1,5},{2,6},{3,7},{4,0},{5,1},{6,2},{7,3},{8,12},{9,13},{10,... | collective-permute-start | bytes 565256 | tf_op jit(solution)/shard_map/ppermute | solution.py:295
  19.0 5.6 %collective-permute-start.8 = (bf16[2,368,128]{2,1,0:T(8,128)(2,1)S(1)}, bf16[2,368,128]{2,1,0:T(8,128)(2,1)S(1)}, u32[]{:S(2)}, u32[]{:S(2)}) collective-permute-start(bf16[2,368,128]{2,1,0:T(8,128)(2,1)S(1)} %pad_maximum_fusion.refs_1_), channel_id=1, source_target_pairs={{0,2},{1,3},{2,0},{3,1},{4,6},{5,7},{6,4},{7,5},{8,10},{9,11},{10,... | collective-permute-start | bytes 565256 | tf_op jit(solution)/shard_map/ppermute | solution.py:295
  24.7 5.6 %collective-permute-start.11 = (bf16[2,368,128]{2,1,0:T(8,128)(2,1)S(1)}, bf16[2,368,128]{2,1,0:T(8,128)(2,1)S(1)}, u32[]{:S(2)}, u32[]{:S(2)}) collective-permute-start(bf16[2,368,128]{2,1,0:T(8,128)(2,1)S(1)} %collective-permute-done.7.refs_5_), channel_id=1, source_target_pairs={{0,2},{1,3},{2,0},{3,1},{4,6},{5,7},{6,4},{7,5},{8,10},{9,11},{10,... | collective-permute-start | bytes 565256 | tf_op jit(solution)/shard_map/ppermute | solution.py:295
  26.2 4.1 %collective-permute-start.5 = (bf16[2,368,128]{2,1,0:T(8,128)(2,1)S(1)}, bf16[2,368,128]{2,1,0:T(8,128)(2,1)S(1)}, u32[]{:S(2)}, u32[]{:S(2)}) collective-permute-start(bf16[2,368,128]{2,1,0:T(8,128)(2,1)S(1)} %pad_maximum_fusion.refs_1_), channel_id=1, source_target_pairs={{0,1},{1,0},{2,3},{3,2},{4,5},{5,4},{6,7},{7,6},{8,9},{9,8},{10,11... | collective-permute-start | bytes 565256 | tf_op jit(solution)/shard_map/ppermute | solution.py:295
  26.2 4.1 %collective-permute-start.10 = (bf16[2,368,128]{2,1,0:T(8,128)(2,1)S(1)}, bf16[2,368,128]{2,1,0:T(8,128)(2,1)S(1)}, u32[]{:S(2)}, u32[]{:S(2)}) collective-permute-start(bf16[2,368,128]{2,1,0:T(8,128)(2,1)S(1)} %collective-permute-done.7.refs_5_), channel_id=1, source_target_pairs={{0,1},{1,0},{2,3},{3,2},{4,5},{5,4},{6,7},{7,6},{8,9},{9,8},{10,11... | collective-permute-start | bytes 565256 | tf_op jit(solution)/shard_map/ppermute | solution.py:295
  26.7 3.6 %collective-permute-start.9 = (bf16[2,368,128]{2,1,0:T(8,128)(2,1)S(1)}, bf16[2,368,128]{2,1,0:T(8,128)(2,1)S(1)}, u32[]{:S(2)}, u32[]{:S(2)}) collective-permute-start(bf16[2,368,128]{2,1,0:T(8,128)(2,1)S(1)} %collective-permute-done.8.refs_3_), channel_id=1, source_target_pairs={{0,1},{1,0},{2,3},{3,2},{4,5},{5,4},{6,7},{7,6},{8,9},{9,8},{10,11... | collective-permute-start | bytes 565256 | tf_op jit(solution)/shard_map/ppermute | solution.py:295
  30.2 1.4 %collective-permute-start.12 = (bf16[2,368,128]{2,1,0:T(8,128)(2,1)S(1)}, bf16[2,368,128]{2,1,0:T(8,128)(2,1)S(1)}, u32[]{:S(2)}, u32[]{:S(2)}) collective-permute-start(bf16[2,368,128]{2,1,0:T(8,128)(2,1)S(1)} %collective-permute-done.11.refs_7_), channel_id=1, source_target_pairs={{0,1},{1,0},{2,3},{3,2},{4,5},{5,4},{6,7},{7,6},{8,9},{9,8},{10,11... | collective-permute-start | bytes 565256 | tf_op jit(solution)/shard_map/ppermute | solution.py:295
  36.8 14.6 %collective-permute-start.13 = (bf16[8,360,128]{2,1,0:T(8,128)(2,1)S(1)}, bf16[8,360,128]{2,1,0:T(8,128)(2,1)S(1)}, u32[]{:S(2)}, u32[]{:S(2)}) collective-permute-start(bf16[8,360,128]{2,1,0:T(8,128)(2,1)S(1)} %get-tuple-element.53), channel_id=1, source_target_pairs={{0,1},{1,0},{2,3},{3,2},{4,5},{5,4},{6,7},{7,6},{8,9},{9,8},{10,11... | collective-permute-start | bytes 2211848 | tf_op jit(solution)/shard_map/ppermute | solution.py:295
  37.0 7.6 %collective-permute-start = (bf16[2,368,128]{2,1,0:T(8,128)(2,1)S(1)}, bf16[2,368,128]{2,1,0:T(8,128)(2,1)S(1)}, u32[]{:S(2)}, u32[]{:S(2)}) collective-permute-start(bf16[2,368,128]{2,1,0:T(8,128)(2,1)S(1)} %get-tuple-element.36.refs_1_), channel_id=1, source_target_pairs={{0,4},{1,5},{2,6},{3,7},{4,0},{5,1},{6,2},{7,3},{8,12},{9,13},{10,... | collective-permute-start | bytes 565256 | tf_op jit(solution)/shard_map/ppermute | solution.py:295
  37.5 10.5 %collective-permute-start.15 = (bf16[2,368,128]{2,1,0:T(8,128)(2,1)S(1)}, bf16[2,368,128]{2,1,0:T(8,128)(2,1)S(1)}, u32[]{:S(2)}, u32[]{:S(2)}) collective-permute-start(bf16[2,368,128]{2,1,0:T(8,128)(2,1)S(1)} %collective-permute-done.6.refs_1_), channel_id=1, source_target_pairs={{0,4},{1,5},{2,6},{3,7},{4,0},{5,1},{6,2},{7,3},{8,12},{9,13},{10,... | collective-permute-start | bytes 565256 | tf_op jit(solution)/shard_map/ppermute | solution.py:295
  44.5 3.5 %collective-permute-start.1 = (bf16[2,368,128]{2,1,0:T(8,128)(2,1)S(1)}, bf16[2,368,128]{2,1,0:T(8,128)(2,1)S(1)}, u32[]{:S(2)}, u32[]{:S(2)}) collective-permute-start(bf16[2,368,128]{2,1,0:T(8,128)(2,1)S(1)} %collective-permute-done.refs_3_), channel_id=1, source_target_pairs={{0,1},{1,0},{2,3},{3,2},{4,5},{5,4},{6,7},{7,6},{8,9},{9,8},{10,11... | collective-permute-start | bytes 565256 | tf_op jit(solution)/shard_map/ppermute | solution.py:295
  44.5 6.8 %collective-permute-start.14 = (bf16[2,368,128]{2,1,0:T(8,128)(2,1)S(1)}, bf16[2,368,128]{2,1,0:T(8,128)(2,1)S(1)}, u32[]{:S(2)}, u32[]{:S(2)}) collective-permute-start(bf16[2,368,128]{2,1,0:T(8,128)(2,1)S(1)} %collective-permute-done.6.refs_1_), channel_id=1, source_target_pairs={{0,1},{1,0},{2,3},{3,2},{4,5},{5,4},{6,7},{7,6},{8,9},{9,8},{10,11... | collective-permute-start | bytes 565256 | tf_op jit(solution)/shard_map/ppermute | solution.py:295
  48.0 3.3 %collective-permute-start.16 = (bf16[2,368,128]{2,1,0:T(8,128)(2,1)S(1)}, bf16[2,368,128]{2,1,0:T(8,128)(2,1)S(1)}, u32[]{:S(2)}, u32[]{:S(2)}) collective-permute-start(bf16[2,368,128]{2,1,0:T(8,128)(2,1)S(1)} %collective-permute-done.15.refs_3_), channel_id=1, source_target_pairs={{0,1},{1,0},{2,3},{3,2},{4,5},{5,4},{6,7},{7,6},{8,9},{9,8},{10,11... | collective-permute-start | bytes 565256 | tf_op jit(solution)/shard_map/ppermute | solution.py:295
  50.8 5.6 %collective-permute-start.4 = (bf16[4,360,128]{2,1,0:T(8,128)(2,1)S(1)}, bf16[4,360,128]{2,1,0:T(8,128)(2,1)S(1)}, u32[]{:S(2)}, u32[]{:S(2)}) collective-permute-start(bf16[4,360,128]{2,1,0:T(8,128)(2,1)S(1)} %get-tuple-element.48), channel_id=1, source_target_pairs={{0,1},{1,0},{2,3},{3,2},{4,5},{5,4},{6,7},{7,6},{8,9},{9,8},{10,11... | collective-permute-start | bytes 1105928 | tf_op jit(solution)/shard_map/ppermute | solution.py:295
  51.5 6.6 %collective-permute-start.23 = (bf16[2,360,128]{2,1,0:T(8,128)(2,1)S(1)}, bf16[2,360,128]{2,1,0:T(8,128)(2,1)S(1)}, u32[]{:S(2)}, u32[]{:S(2)}) collective-permute-start(bf16[2,360,128]{2,1,0:T(8,128)(2,1)S(1)} %get-tuple-element.71), channel_id=1, source_target_pairs={{0,2},{1,3},{2,0},{3,1},{4,6},{5,7},{6,4},{7,5},{8,10},{9,11},{10,... | collective-permute-start | bytes 552968 | tf_op jit(solution)/shard_map/ppermute | solution.py:295
  53.1 6.3 %collective-permute-start.26 = (bf16[2,360,128]{2,1,0:T(8,128)(2,1)S(1)}, bf16[2,360,128]{2,1,0:T(8,128)(2,1)S(1)}, u32[]{:S(2)}, u32[]{:S(2)}) collective-permute-start(bf16[2,360,128]{2,1,0:T(8,128)(2,1)S(1)} %get-tuple-element.72), channel_id=1, source_target_pairs={{0,4},{1,5},{2,6},{3,7},{4,0},{5,1},{6,2},{7,3},{8,12},{9,13},{10,... | collective-permute-start | bytes 552968 | tf_op jit(solution)/shard_map/ppermute | solution.py:295
  56.4 4.2 %collective-permute-start.19 = (bf16[4,360,128]{2,1,0:T(8,128)(2,1)S(1)}, bf16[4,360,128]{2,1,0:T(8,128)(2,1)S(1)}, u32[]{:S(2)}, u32[]{:S(2)}) collective-permute-start(bf16[4,360,128]{2,1,0:T(8,128)(2,1)S(1)} %get-tuple-element.64), channel_id=1, source_target_pairs={{0,1},{1,0},{2,3},{3,2},{4,5},{5,4},{6,7},{7,6},{8,9},{9,8},{10,11... | collective-permute-start | bytes 1105928 | tf_op jit(solution)/shard_map/ppermute | solution.py:295
  56.5 7.5 %collective-permute-start.17 = (bf16[2,360,128]{2,1,0:T(8,128)(2,1)S(1)}, bf16[2,360,128]{2,1,0:T(8,128)(2,1)S(1)}, u32[]{:S(2)}, u32[]{:S(2)}) collective-permute-start(bf16[2,360,128]{2,1,0:T(8,128)(2,1)S(1)} %add_convert_fusion.3), channel_id=1, source_target_pairs={{0,2},{1,3},{2,0},{3,1},{4,6},{5,7},{6,4},{7,5},{8,10},{9,11},{10,... | collective-permute-start | bytes 552968 | tf_op jit(solution)/shard_map/ppermute | solution.py:295
  59.4 9.7 %collective-permute-start.24 = (bf16[360,128]{1,0:T(8,128)(2,1)S(1)}, bf16[360,128]{1,0:T(8,128)(2,1)S(1)}, u32[]{:S(2)}, u32[]{:S(2)}) collective-permute-start(bf16[360,128]{1,0:T(8,128)(2,1)S(1)} %get-tuple-element.69), channel_id=1, source_target_pairs={{0,4},{1,5},{2,6},{3,7},{4,0},{5,1},{6,2},{7,3},{8,12},{9,13},{10,... | collective-permute-start | bytes 276488 | tf_op jit(solution)/shard_map/ppermute | solution.py:295
  60.0 9.1 %collective-permute-start.27 = (bf16[360,128]{1,0:T(8,128)(2,1)S(1)}, bf16[360,128]{1,0:T(8,128)(2,1)S(1)}, u32[]{:S(2)}, u32[]{:S(2)}) collective-permute-start(bf16[360,128]{1,0:T(8,128)(2,1)S(1)} %get-tuple-element.70), channel_id=1, source_target_pairs={{0,2},{1,3},{2,0},{3,1},{4,6},{5,7},{6,4},{7,5},{8,10},{9,11},{10,... | collective-permute-start | bytes 276488 | tf_op jit(solution)/shard_map/ppermute | solution.py:295
  60.6 7.9 %collective-permute-start.20 = (bf16[2,360,128]{2,1,0:T(8,128)(2,1)S(1)}, bf16[2,360,128]{2,1,0:T(8,128)(2,1)S(1)}, u32[]{:S(2)}, u32[]{:S(2)}) collective-permute-start(bf16[2,360,128]{2,1,0:T(8,128)(2,1)S(1)} %add_convert_fusion.2), channel_id=1, source_target_pairs={{0,4},{1,5},{2,6},{3,7},{4,0},{5,1},{6,2},{7,3},{8,12},{9,13},{10,... | collective-permute-start | bytes 552968 | tf_op jit(solution)/shard_map/ppermute | solution.py:295
  64.0 11.0 %collective-permute-start.18 = (bf16[360,128]{1,0:T(8,128)(2,1)S(1)}, bf16[360,128]{1,0:T(8,128)(2,1)S(1)}, u32[]{:S(2)}, u32[]{:S(2)}) collective-permute-start(bf16[360,128]{1,0:T(8,128)(2,1)S(1)} %fusion.4), channel_id=1, source_target_pairs={{0,4},{1,5},{2,6},{3,7},{4,0},{5,1},{6,2},{7,3},{8,12},{9,13},{10,... | collective-permute-start | bytes 276488 | tf_op jit(solution)/shard_map/ppermute | solution.py:295
  68.6 4.6 %collective-permute-start.21 = (bf16[360,128]{1,0:T(8,128)(2,1)S(1)}, bf16[360,128]{1,0:T(8,128)(2,1)S(1)}, u32[]{:S(2)}, u32[]{:S(2)}) collective-permute-start(bf16[360,128]{1,0:T(8,128)(2,1)S(1)} %fusion.5), channel_id=1, source_target_pairs={{0,2},{1,3},{2,0},{3,1},{4,6},{5,7},{6,4},{7,5},{8,10},{9,11},{10,... | collective-permute-start | bytes 276488 | tf_op jit(solution)/shard_map/ppermute | solution.py:295
  69.3 7.1 %collective-permute-start.28 = (bf16[360,128]{1,0:T(8,128)(2,1)S(1)}, bf16[360,128]{1,0:T(8,128)(2,1)S(1)}, u32[]{:S(2)}, u32[]{:S(2)}) collective-permute-start(bf16[360,128]{1,0:T(8,128)(2,1)S(1)} %get-tuple-element.68), channel_id=1, source_target_pairs={{0,24},{1,25},{2,26},{3,27},{4,28},{5,29},{6,30},{7,31},{8,16},{9,... | collective-permute-start | bytes 276488 | tf_op jit(solution)/shard_map/ppermute | solution.py:295
  72.2 6.4 %collective-permute-start.25 = (bf16[360,128]{1,0:T(8,128)(2,1)S(1)}, bf16[360,128]{1,0:T(8,128)(2,1)S(1)}, u32[]{:S(2)}, u32[]{:S(2)}) collective-permute-start(bf16[360,128]{1,0:T(8,128)(2,1)S(1)} %get-tuple-element.67), channel_id=1, source_target_pairs={{0,16},{1,17},{2,18},{3,19},{4,20},{5,21},{6,22},{7,23},{8,24},{9,... | collective-permute-start | bytes 276488 | tf_op jit(solution)/shard_map/ppermute | solution.py:295
  73.3 5.4 %collective-permute-start.22 = (bf16[360,128]{1,0:T(8,128)(2,1)S(1)}, bf16[360,128]{1,0:T(8,128)(2,1)S(1)}, u32[]{:S(2)}, u32[]{:S(2)}) collective-permute-start(bf16[360,128]{1,0:T(8,128)(2,1)S(1)} %fusion.2), channel_id=1, source_target_pairs={{0,8},{1,9},{2,10},{3,11},{4,12},{5,13},{6,14},{7,15},{8,0},{9,1},... | collective-permute-start | bytes 276488 | tf_op jit(solution)/shard_map/ppermute | solution.py:295

commit v5 on v4

--- a/solution.py
+++ b/solution.py
@@ -80,54 +80,48 @@
     return total.astype(jnp.bfloat16)
 
 
-def arrange_kernel(groups, *refs):
-    gate_up_out, down_out, bias_out, down_bias_out = refs[6:10]
-    gate_ref, up_ref, down_ref, gate_bias_ref, up_bias_ref, down_bias_ref = refs[10:16]
-    fetch(refs[:6], refs[10:16], refs[16])
+def padded(array, rows, columns):
+    return jnp.pad(array, ((0, rows - array.shape[0]), (0, columns - array.shape[1])))
+
+
+def column(row, size, lanes):
+    return jnp.broadcast_to(padded(row, 1, size), (lanes, size)).T
+
+
+def inward_kernel(groups, gate_ref, up_ref, biases_ref, weight_out, bias_out):
     features, hidden = gate_ref.shape
     quarter = features // groups
-    hidden_pad, block = round_up(hidden, 128), round_up(quarter, 128)
-    lanes = bias_out.shape[1]
-
-    def padded(array, rows, columns):
-        return jnp.pad(array, ((0, rows - array.shape[0]), (0, columns - array.shape[1])))
-
-    def column(row, size):
-        return jnp.broadcast_to(padded(row, 1, size), (lanes, size)).T
-
-    for n, (weight, bias) in enumerate(((gate_ref, gate_bias_ref), (up_ref, up_bias_ref))):
+    hidden_pad, size = round_up(hidden, 128), round_up(quarter, 128)
+    for n, weight in enumerate((gate_ref, up_ref)):
         values = weight[...].astype(jnp.float32)
         rows = slice(n * hidden_pad, (n + 1) * hidden_pad)
         for q in range(groups):
-            part = padded(values[q * quarter : (q + 1) * quarter], block, hidden_pad)
-            gate_up_out[rows, q * block : (q + 1) * block] = part.T.astype(jnp.bfloat16)
-        bias_out[rows] = column(bias[...], hidden_pad)
+            part = padded(values[q * quarter : (q + 1) * quarter], size, hidden_pad)
+            weight_out[rows, q * size : (q + 1) * size] = part.T.astype(jnp.bfloat16)
+        bias_out[rows] = column(biases_ref[n : n + 1], hidden_pad, bias_out.shape[1])
+
+
+def outward_kernel(groups, down_ref, biases_ref, weight_out, bias_out):
+    hidden, features = down_ref.shape
+    quarter = features // groups
+    hidden_pad, size = round_up(hidden, 128), round_up(quarter, 128)
     values = padded(down_ref[...].astype(jnp.float32), hidden_pad, round_up(features, 128)).T
     for q in range(groups):
-        part = padded(values[q * quarter : (q + 1) * quarter], block, hidden_pad)
-        down_out[q * block : (q + 1) * block] = part.astype(jnp.bfloat16)
-    down_bias_out[...] = column(down_bias_ref[...], block)
-
-
-def arrange(groups, lanes, gate, up, down, gate_bias, up_bias, down_bias):
-    features, hidden = gate.shape
-    hidden_pad, block = round_up(hidden, 128), round_up(features // groups, 128)
-    arrays = (gate, up, down, gate_bias, up_bias, down_bias)
+        part = padded(values[q * quarter : (q + 1) * quarter], size, hidden_pad)
+        weight_out[q * size : (q + 1) * size] = part.astype(jnp.bfloat16)
+    bias_out[...] = column(biases_ref[2:3], size, bias_out.shape[1])
+
+
+def arrange(kernel, groups, lanes, arrays, shape, bias_rows):
     return pl.pallas_call(
-        functools.partial(arrange_kernel, groups),
-        in_specs=[pl.BlockSpec(memory_space=pltpu.HBM)] * len(arrays),
-        out_specs=[pl.BlockSpec(memory_space=pltpu.VMEM)] * 4,
-        scratch_shapes=[pltpu.VMEM(a.shape, a.dtype) for a in arrays]
-        + [pltpu.SemaphoreType.DMA((len(arrays),))],
+        functools.partial(kernel, groups),
         out_shape=[
-            jax.ShapeDtypeStruct((2 * hidden_pad, groups * block), jnp.bfloat16),
-            jax.ShapeDtypeStruct((groups * block, hidden_pad), jnp.bfloat16),
-            jax.ShapeDtypeStruct((2 * hidden_pad, lanes), jnp.float32),
-            jax.ShapeDtypeStruct((block, lanes), jnp.float32),
+            jax.ShapeDtypeStruct(shape, jnp.bfloat16),
+            jax.ShapeDtypeStruct((bias_rows, lanes), jnp.float32),
         ],
         compiler_params=pltpu.CompilerParams(vmem_limit_bytes=40 * 2**20),
         cost_estimate=pl.CostEstimate(
-            flops=0, bytes_accessed=8 * gate.size * 2, transcendentals=0
+            flops=0, bytes_accessed=16 * arrays[0].size, transcendentals=0
         ),
     )(*arrays)
 
@@ -198,7 +192,7 @@
         out_shape=[jax.ShapeDtypeStruct((rows, lanes), jnp.bfloat16), pair, pair],
         scratch_shapes=[pltpu.VMEM(a.shape, a.dtype) for a in arrays]
         + [pltpu.SemaphoreType.DMA((len(arrays),))],
-        compiler_params=pltpu.CompilerParams(vmem_limit_bytes=40 * 2**20),
+        compiler_params=pltpu.CompilerParams(vmem_limit_bytes=60 * 2**20),
     )(place, *arrays)
 
 
@@ -206,7 +200,7 @@
     groups = len(blocks[0])
     counted = 1 + max(at for block in blocks for at, _ in block)
     place_ref, arrays = refs[0], refs[1 : 1 + counted]
-    gate_up_ref, down_ref, bias_ref, down_bias_ref, keep_ref, send_ref = refs[1 + counted : 7 + counted]
+    gate_up_ref, bias_ref, down_ref, down_bias_ref, keep_ref, send_ref = refs[1 + counted : 7 + counted]
     scratch = refs[7 + counted :]
     _, piece_rows, lanes = arrays[0].shape
     size = gate_up_ref.shape[1] // groups
@@ -251,7 +245,7 @@
 def run_expert(place, arrays, blocks, slots, weights, sizes, halves):
     quarter, per = sizes
     lanes = arrays[0].shape[2]
-    gate_up, down = weights[0], weights[1]
+    gate_up, down = weights[0], weights[2]
     tokens = len(blocks) * lanes
     whole = pl.BlockSpec(memory_space=pltpu.VMEM)
     out = jax.ShapeDtypeStruct((2 * len(blocks), quarter, lanes), jnp.bfloat16)
@@ -302,51 +296,75 @@
     z_2, z_3 = swap(one, 2 * along_z), swap(one, 3 * along_z)
     x_0 = swap(near, along_x)
     z_1 = swap(near, along_z)
-    weights = arrange(
-        groups, lanes, gate_weight[0], up_weight[0], down_weight[0], gate_bias, up_bias, down_bias
-    )
-    z_2, z_3, weights = tied((z_2, z_3, weights))
+    hidden_pad = round_up(gate_weight.shape[2], 128)
+    wide = groups * round_up(quarter, 128)
+    biases = jnp.concatenate([gate_bias, up_bias, down_bias], axis=0)
+    inward = arrange(
+        inward_kernel,
+        groups,
+        lanes,
+        (gate_weight[0], up_weight[0], biases),
+        (2 * hidden_pad, wide),
+        2 * hidden_pad,
+    )
+    z_2, z_3, inward = tied((z_2, z_3, inward))
     z_high = jnp.stack([z_2, z_3])
     x_high, y_high = swap(z_high, along_x), swap(z_high, along_y)
-    z_1, x_high, y_high = tied((z_1, x_high, y_high))
+    outward = arrange(
+        outward_kernel,
+        groups,
+        lanes,
+        (down_weight[0], biases),
+        (wide, hidden_pad),
+        wide // groups,
+    )
+    z_1, x_high, y_high, x_0, outward = tied((z_1, x_high, y_high, x_0, outward))
+    weights = (*inward, *outward)
     corner = swap(x_high, along_y)
     x_1 = swap(z_1, along_x)
 
-    def pairs(first):
-        return [[(first + 2 * x + k % 2, k // 2) for k in range(groups)] for x in range(2)]
+    def pairs(first, step):
+        return [[(first + step * x + k % 2, k // 2) for k in range(groups)] for x in range(2)]
 
     slots_a, slots_b = ((2, 0), (3, 1)), ((2, 3), (0, 1))
+    sizes = (quarter, per)
+    keep_0, send_0 = run_expert(
+        place, (near, far, x_0, swap(x_0, core)), pairs(0, 2), slots_a, weights, sizes, 1
+    )
+    got_0 = swap(send_0, core)
+    corner, keep_0, send_0 = tied((corner, keep_0, send_0))
     high = (z_high, swap(z_high, core), y_high, swap(y_high, core))
     high = high + (x_high, swap(x_high, core), corner, swap(corner, core))
-    blocks = [[(4 * x + k, line) for k in range(groups)] for line in range(2) for x in range(2)]
-    slots = slots_a + tuple((4 + i, 4 + j) for i, j in slots_b)
-    sizes = (quarter, per)
-    keep_0, send_0 = run_expert(
-        place, (near, far, x_0, swap(x_0, core)), pairs(0), slots_a, weights, sizes, 1
-    )
-    keep_high, send_high = run_expert(place, high, blocks, slots, weights, sizes, 2)
-    got_0 = swap(send_0, core)
-    got = swap(send_high, core)
-    near_1 = (z_1, swap(z_1, core), x_1, swap(x_1, core))
-    got, near_1 = tied((got, near_1))
-    keep_1, send_1 = run_expert(place, near_1, pairs(0), slots_b, weights, sizes, 1)
-    keep_0, got_0, keep_1, send_1 = tied((keep_0, got_0, keep_1, send_1))
-
-    def plane(keep_a, got_a, keep_b, got_b):
-        first_y = swap(add_up(keep_a[0:2], got_a[0:2]), along_y)
-        first_x = swap(add_up(keep_b[0:2], got_b[0:2]), along_x)
-        last_x = swap(add_up(keep_a[3], got_a[3], first_y[1]), along_x)
-        last_y = swap(add_up(keep_b[3], got_b[3], first_x[1]), along_y)
-        return (
-            add_up(keep_a[2], got_a[2], first_y[0], last_x),
-            add_up(keep_b[2], got_b[2], first_x[0], last_y),
-        )
-
-    line_2, line_3 = plane(keep_high[:4], got[:4], keep_high[4:], got[4:])
-    line_0, line_1 = plane(keep_0, got_0, keep_1, swap(send_1, core))
-    mixed = add_up(
-        line_0, swap(line_1, along_z), swap(line_2, 2 * along_z), swap(line_3, 3 * along_z)
-    )
+    z_1_core = swap(z_1, core)
+    keep_0, got_0, z_1_core, high = tied((keep_0, got_0, z_1_core, high))
+    line = [[[(4 * x + k, n) for k in range(groups)] for x in range(2)] for n in range(2)]
+    keep_2, send_2 = run_expert(place, high, line[0], slots_a, weights, sizes, 1)
+    got_2 = swap(send_2, core)
+    keep_2, x_1, high = tied((keep_2, x_1, high))
+    near_1 = (z_1, z_1_core, x_1, swap(x_1, core))
+    keep_3, send_3 = run_expert(place, high, line[1], slots_b, weights, sizes, 1)
+    got_2, keep_3, send_3, near_1 = tied((got_2, keep_3, send_3, near_1))
+    got_3 = swap(send_3, core)
+    first_y = swap(add_up(keep_2[0:2], got_2[0:2]), along_y)
+    first_x = swap(add_up(keep_3[0:2], got_3[0:2]), along_x)
+    got_2, got_3, near_1 = tied((got_2, got_3, near_1))
+    keep_1, send_1 = run_expert(place, near_1, pairs(0, 2), slots_b, weights, sizes, 1)
+    got_1 = swap(send_1, core)
+
+    first_y, first_x, keep_0, got_0, keep_1 = tied((first_y, first_x, keep_0, got_0, keep_1))
+    last_x = swap(add_up(keep_2[3], got_2[3], first_y[1]), along_x)
+    last_y = swap(add_up(keep_3[3], got_3[3], first_x[1]), along_y)
+    early_y = swap(add_up(keep_0[0:2], got_0[0:2]), along_y)
+    early_x = swap(add_up(keep_1[0:2], got_1[0:2]), along_x)
+    line_2 = add_up(keep_2[2], got_2[2], first_y[0], last_x)
+    line_3 = add_up(keep_3[2], got_3[2], first_x[0], last_y)
+    back_2, back_3 = swap(line_2, 2 * along_z), swap(line_3, 3 * along_z)
+    _, _, early_y, early_x = tied((line_2, line_3, early_y, early_x))
+    end_x = swap(add_up(keep_0[3], got_0[3], early_y[1]), along_x)
+    end_y = swap(add_up(keep_1[3], got_1[3], early_x[1]), along_y)
+    line_1 = add_up(keep_1[2], got_1[2], early_x[0], end_y)
+    back_1 = swap(line_1, along_z)
+    mixed = add_up(keep_0[2], got_0[2], early_y[0], end_x, back_1, back_2, back_3)
     return mixed.T
 
 

time: 79.8 us -> 75.3 us (0.944)
  local copies, waits for them, and re-layouts: 8.82 us -> 2.5 us
  Pallas kernels: 13.4 us -> 15.1 us
  waiting for transfers between devices: 28.9 us -> 27.6 us
  other arithmetic: 1.37 us -> 2.66 us
    unnamed x20 -> x12, local copies, waits for them, and re-layouts: 8.82 us -> 2.5 us
    pallas_call x1, Pallas kernels: 1.16 us -> 2.88 us  [make_pieces(): pl.pallas_call(functools.partial(pieces_kernel, groups, per, experts), in...]
    ppermute x29 -> x30, waiting for transfers between devices: 28.9 us -> 27.6 us  [swap(): lax.ppermute(array, ('seq', 'rep'), [(i, i ^ step) for i in range(devices)])]
    pallas_call x1 -> x2, Pallas kernels: 1.66 us -> 1.23 us  [arrange(): pl.pallas_call(functools.partial(kernel, groups), out_shape=[jax.ShapeDty...]
    pallas_call x3 -> x4, Pallas kernels: 10.6 us -> 11 us  [run_expert(): pl.pallas_call(functools.partial(expert_kernel, quarter, per, blocks, slo...]
    ppermute x29 -> x30, starting transfers between devices: 26.8 us -> 27 us  [swap(): lax.ppermute(array, ('seq', 'rep'), [(i, i ^ step) for i in range(devices)])]
  transfers between devices with their start and end apart: 29 -> 30, of which waited for: 13 -> 13; matrix products, arithmetic and copies ran while one was open for 1% -> 2% of each run, Pallas kernels for 9% -> 16%
where the time goes in v5:
time: 75.3 us; the launch traced here: 75.1 us
  waiting for transfers between devices  27.6 us (37%)
  starting transfers between devices  27 us (36%)
  Pallas kernels  15.1 us (20%)
  other arithmetic  2.66 us (4%)
  local copies, waits for them, and re-layouts  2.5 us (3%)
    ppermute x30, waiting for transfers between devices, swap(): lax.ppermute(array, ('seq', 'rep'), [(i, i ^ step) for i in range(devices)])  27.6 us
    ppermute x30, starting transfers between devices, swap(): lax.ppermute(array, ('seq', 'rep'), [(i, i ^ step) for i in range(devices)])  27 us
    pallas_call x4, Pallas kernels, run_expert(): pl.pallas_call(functools.partial(expert_kernel, quarter, per, blocks, slo...  11 us
    pallas_call x1, Pallas kernels, make_pieces(): pl.pallas_call(functools.partial(pieces_kernel, groups, per, experts), in...  2.88 us
    unnamed x12, local copies, waits for them, and re-layouts  2.5 us
  transfers between devices with their start and end apart: 30, of which 13 were waited for; matrix products, arithmetic and copies ran while one was open for 2% of the time, Pallas kernels for 16%

profile of v5, /device:TPU:0, one launch (start us, length us, event | category | flops | bytes accessed | tf_op | source)
XLA Modules:
  0.0 75.1 jit_solution(10613538644783470639)
XLA Ops:
  0.0 0.6 pad_add_fusion.place_ref.refs_0_
  0.6 2.9 %shard_map.100 = (bf16[368,128]{1,0:T(8,128)(2,1)}, bf16[2,368,128]{2,1,0:T(8,128)(2,1)}, bf16[2,368,128]{2,1,0:T(8,128)(2,1)}) custom-call(s32[2]{0:T(128)} %pad_add_fusion.place_ref.refs_0_, bf16[1440,128]{1,0:T(8,128)(2,1)} %bitcast.47, f32[1440]{0:T(1024)} %refs_1_.1, s32[4,128]{1,0:T(4,128)} %bitcast.50, f32[4,128]{1,0:T(4,128)} %bitcast.51), custom_call_target="tpu_custom_call" | custom-call | tf_op jit(solution)/shard_map/pallas_call | solution.py:188
  3.5 5.1 %collective-permute-start.2 = (bf16[368,128]{1,0:T(8,128)(2,1)}, bf16[368,128]{1,0:T(8,128)(2,1)S(1)}, u32[]{:S(2)}, u32[]{:S(2)}) collective-permute-start(bf16[368,128]{1,0:T(8,128)(2,1)} %get-tuple-element.74), channel_id=1, source_target_pairs={{0,24},{1,25},{2,26},{3,27},{4,28},{5,29},{6,30},{7,31},{8,16},{9,... | collective-permute-start | bytes 282632 | tf_op jit(solution)/shard_map/ppermute | solution.py:289
  8.6 1.5 %collective-permute-start.5 = (bf16[2,368,128]{2,1,0:T(8,128)(2,1)}, bf16[2,368,128]{2,1,0:T(8,128)(2,1)S(1)}, u32[]{:S(2)}, u32[]{:S(2)}) collective-permute-start(bf16[2,368,128]{2,1,0:T(8,128)(2,1)} %get-tuple-element.73.refs_1_), channel_id=1, source_target_pairs={{0,4},{1,5},{2,6},{3,7},{4,0},{5,1},{6,2},{7,3},{8,12},{9,13},{10,... | collective-permute-start | bytes 565256 | tf_op jit(solution)/shard_map/ppermute | solution.py:289
  10.1 0.8 %collective-permute-start = (bf16[2,368,128]{2,1,0:T(8,128)(2,1)}, bf16[2,368,128]{2,1,0:T(8,128)(2,1)S(1)}, u32[]{:S(2)}, u32[]{:S(2)}) collective-permute-start(bf16[2,368,128]{2,1,0:T(8,128)(2,1)} %get-tuple-element.73.refs_1_), channel_id=1, source_target_pairs={{0,8},{1,9},{2,10},{3,11},{4,12},{5,13},{6,14},{7,15},{8,0},{9,1},... | collective-permute-start | bytes 565256 | tf_op jit(solution)/shard_map/ppermute | solution.py:289
  10.9 0.7 pad_maximum_fusion.1.biases_ref
  11.6 1.2 %copy-done = bf16[1,1440,360]{2,1,0:T(8,128)(2,1)S(1)} copy-done((bf16[1,1440,360]{2,1,0:T(8,128)(2,1)S(1)}, bf16[1,1440,360]{2,1,0:T(8,128)(2,1)}, u32[]{:S(2)}) %copy-start) | copy-done | bytes 1036824
  12.9 1.2 %copy-done.1 = bf16[1,1440,360]{2,1,0:T(8,128)(2,1)S(1)} copy-done((bf16[1,1440,360]{2,1,0:T(8,128)(2,1)S(1)}, bf16[1,1440,360]{2,1,0:T(8,128)(2,1)}, u32[]{:S(2)}) %copy-start.1) | copy-done | bytes 1036824
  14.1 0.8 %shard_map.101 = (bf16[768,1536]{1,0:T(8,128)(2,1)S(1)}, f32[768,128]{1,0:T(8,128)S(1)}) custom-call(bf16[1440,360]{1,0:T(8,128)(2,1)S(1)} %bitcast.44, bf16[1440,360]{1,0:T(8,128)(2,1)S(1)} %bitcast.45, f32[3,360]{1,0:T(4,128)S(1)} %pad_maximum_fusion.1.biases_ref), custom_call_target="tpu_custom_call" | custom-call | bytes 8294400 | tf_op jit(solution)/shard_map/pallas_call | solution.py:116
  14.9 1.9 %collective-permute-done.1 = bf16[368,128]{1,0:T(8,128)(2,1)S(1)} collective-permute-done((bf16[368,128]{1,0:T(8,128)(2,1)}, bf16[368,128]{1,0:T(8,128)(2,1)S(1)}, u32[]{:S(2)}, u32[]{:S(2)}) %collective-permute-start.1) | collective-permute-done | bytes 94240 | tf_op jit(solution)/shard_map/ppermute | solution.py:289
  16.9 1.6 %collective-permute-start.4 = (bf16[2,368,128]{2,1,0:T(8,128)(2,1)S(1)}, bf16[2,368,128]{2,1,0:T(8,128)(2,1)S(1)}, u32[]{:S(2)}, u32[]{:S(2)}) collective-permute-start(bf16[2,368,128]{2,1,0:T(8,128)(2,1)S(1)} %pad_maximum_fusion.refs_1_), channel_id=1, source_target_pairs={{0,2},{1,3},{2,0},{3,1},{4,6},{5,7},{6,4},{7,5},{8,10},{9,11},{10,... | collective-permute-start | bytes 565256 | tf_op jit(solution)/shard_map/ppermute | solution.py:289
  18.4 1.5 %collective-permute-start.3 = (bf16[2,368,128]{2,1,0:T(8,128)(2,1)S(1)}, bf16[2,368,128]{2,1,0:T(8,128)(2,1)S(1)}, u32[]{:S(2)}, u32[]{:S(2)}) collective-permute-start(bf16[2,368,128]{2,1,0:T(8,128)(2,1)S(1)} %pad_maximum_fusion.refs_1_), channel_id=1, source_target_pairs={{0,4},{1,5},{2,6},{3,7},{4,0},{5,1},{6,2},{7,3},{8,12},{9,13},{10,... | collective-permute-start | bytes 565256 | tf_op jit(solution)/shard_map/ppermute | solution.py:289
  19.9 0.4 shard_map.102
  20.4 2.2 %collective-permute-done.4.refs_3_ = bf16[2,368,128]{2,1,0:T(8,128)(2,1)S(1)} collective-permute-done((bf16[2,368,128]{2,1,0:T(8,128)(2,1)S(1)}, bf16[2,368,128]{2,1,0:T(8,128)(2,1)S(1)}, u32[]{:S(2)}, u32[]{:S(2)}) %collective-permute-start.4) | collective-permute-done | bytes 188448 | tf_op jit(solution)/shard_map/ppermute | solution.py:289
  22.6 1.4 %collective-permute-done.3.refs_5_ = bf16[2,368,128]{2,1,0:T(8,128)(2,1)S(1)} collective-permute-done((bf16[2,368,128]{2,1,0:T(8,128)(2,1)S(1)}, bf16[2,368,128]{2,1,0:T(8,128)(2,1)S(1)}, u32[]{:S(2)}, u32[]{:S(2)}) %collective-permute-start.3) | collective-permute-done | bytes 188448 | tf_op jit(solution)/shard_map/ppermute | solution.py:289
  24.0 0.5 collective-permute-start.10
  24.5 0.5 collective-permute-start.6
  25.0 0.4 collective-permute-done.7.refs_4_
  25.5 2.7 %shard_map.103 = (bf16[4,360,128]{2,1,0:T(8,128)(2,1)S(1)}, bf16[4,360,128]{2,1,0:T(8,128)(2,1)S(1)}) custom-call(s32[2]{0:T(128)S(1)} %copy-done.3, bf16[2,368,128]{2,1,0:T(8,128)(2,1)S(1)} %copy-done.4, bf16[2,368,128]{2,1,0:T(8,128)(2,1)S(1)} %copy-done.5, bf16[2,368,128]{2,1,0:T(8,128)(2,1)S(1)} %collective-permute-done.5.refs_3_, ...), custom_call_target="tpu_custom_call" | custom-call | flops 1811939328 | bytes 3538944 | tf_op jit(solution)/shard_map/pallas_call | solution.py:253
  28.2 0.2 collective-permute-start.8
  28.4 0.4 collective-permute-start.12
  28.8 0.1 collective-permute-start.11
  28.9 2.2 %collective-permute-done.6.refs_7_ = bf16[2,368,128]{2,1,0:T(8,128)(2,1)S(1)} collective-permute-done((bf16[2,368,128]{2,1,0:T(8,128)(2,1)S(1)}, bf16[2,368,128]{2,1,0:T(8,128)(2,1)S(1)}, u32[]{:S(2)}, u32[]{:S(2)}) %collective-permute-start.6) | collective-permute-done | bytes 188448 | tf_op jit(solution)/shard_map/ppermute | solution.py:289
  31.2 0.5 collective-permute-start.13
  31.7 1.5 %collective-permute-start.14 = (bf16[2,368,128]{2,1,0:T(8,128)(2,1)S(1)}, bf16[2,368,128]{2,1,0:T(8,128)(2,1)S(1)}, u32[]{:S(2)}, u32[]{:S(2)}) collective-permute-start(bf16[2,368,128]{2,1,0:T(8,128)(2,1)S(1)} %collective-permute-done.refs_1_), channel_id=1, source_target_pairs={{0,4},{1,5},{2,6},{3,7},{4,0},{5,1},{6,2},{7,3},{8,12},{9,13},{10,... | collective-permute-start | bytes 565256 | tf_op jit(solution)/shard_map/ppermute | solution.py:289
  33.2 2.8 %shard_map.104 = (bf16[4,360,128]{2,1,0:T(8,128)(2,1)S(1)}, bf16[4,360,128]{2,1,0:T(8,128)(2,1)S(1)}) custom-call(s32[2]{0:T(128)S(1)} %copy-done.3, bf16[2,368,128]{2,1,0:T(8,128)(2,1)S(1)} %pad_maximum_fusion.refs_1_, bf16[2,368,128]{2,1,0:T(8,128)(2,1)S(1)} %collective-permute-done.10.refs_2_, bf16[2,368,128]{2,1,0:T(8,128)(2,1)S(1)} %collective-permute-done.4.refs_3_, ...), custom_call_target="tpu_custom_call" | custom-call | flops 1811939328 | bytes 3538944 | tf_op jit(solution)/shard_map/pallas_call | solution.py:253
  36.0 2.3 %collective-permute-done.14.refs_3_ = bf16[2,368,128]{2,1,0:T(8,128)(2,1)S(1)} collective-permute-done((bf16[2,368,128]{2,1,0:T(8,128)(2,1)S(1)}, bf16[2,368,128]{2,1,0:T(8,128)(2,1)S(1)}, u32[]{:S(2)}, u32[]{:S(2)}) %collective-permute-start.14) | collective-permute-done | bytes 188448 | tf_op jit(solution)/shard_map/ppermute | solution.py:289
  38.4 2.7 %shard_map.105 = (bf16[4,360,128]{2,1,0:T(8,128)(2,1)S(1)}, bf16[4,360,128]{2,1,0:T(8,128)(2,1)S(1)}) custom-call(s32[2]{0:T(128)S(1)} %copy-done.3, bf16[2,368,128]{2,1,0:T(8,128)(2,1)S(1)} %pad_maximum_fusion.refs_1_, bf16[2,368,128]{2,1,0:T(8,128)(2,1)S(1)} %collective-permute-done.10.refs_2_, bf16[2,368,128]{2,1,0:T(8,128)(2,1)S(1)} %collective-permute-done.4.refs_3_, ...), custom_call_target="tpu_custom_call" | custom-call | flops 1811939328 | bytes 3538944 | tf_op jit(solution)/shard_map/pallas_call | solution.py:253
  41.2 0.6 collective-permute-start.18
  41.8 0.6 collective-permute-start.17
  42.4 0.7 collective-permute-done.18
  43.1 1.6 %collective-permute-start.19 = (bf16[2,360,128]{2,1,0:T(8,128)(2,1)S(1)}, bf16[2,360,128]{2,1,0:T(8,128)(2,1)S(1)}, u32[]{:S(2)}, u32[]{:S(2)}) collective-permute-start(bf16[2,360,128]{2,1,0:T(8,128)(2,1)S(1)} %add_convert_fusion.2), channel_id=1, source_target_pairs={{0,4},{1,5},{2,6},{3,7},{4,0},{5,1},{6,2},{7,3},{8,12},{9,13},{10,... | collective-permute-start | bytes 552968 | tf_op jit(solution)/shard_map/ppermute | solution.py:289
  44.7 2.7 %shard_map.106 = (bf16[4,360,128]{2,1,0:T(8,128)(2,1)S(1)}, bf16[4,360,128]{2,1,0:T(8,128)(2,1)S(1)}) custom-call(s32[2]{0:T(128)S(1)} %copy-done.3, bf16[2,368,128]{2,1,0:T(8,128)(2,1)S(1)} %collective-permute-done.refs_1_, bf16[2,368,128]{2,1,0:T(8,128)(2,1)S(1)} %collective-permute-done.9.refs_2_, ...), custom_call_target="tpu_custom_call" | custom-call | flops 1811939328 | bytes 3538944 | tf_op jit(solution)/shard_map/pallas_call | solution.py:253
  47.4 0.1 collective-permute-start.23
  47.6 0.8 %collective-permute-done.17 = bf16[2,360,128]{2,1,0:T(8,128)(2,1)S(1)} collective-permute-done((bf16[2,360,128]{2,1,0:T(8,128)(2,1)S(1)}, bf16[2,360,128]{2,1,0:T(8,128)(2,1)S(1)}, u32[]{:S(2)}, u32[]{:S(2)}) %collective-permute-start.17) | collective-permute-done | bytes 184352 | tf_op jit(solution)/shard_map/ppermute | solution.py:289
  48.4 1.7 %collective-permute-done.19 = bf16[2,360,128]{2,1,0:T(8,128)(2,1)S(1)} collective-permute-done((bf16[2,360,128]{2,1,0:T(8,128)(2,1)S(1)}, bf16[2,360,128]{2,1,0:T(8,128)(2,1)S(1)}, u32[]{:S(2)}, u32[]{:S(2)}) %collective-permute-start.19) | collective-permute-done | bytes 184352 | tf_op jit(solution)/shard_map/ppermute | solution.py:289
  50.1 0.6 collective-permute-start.21
  50.8 1.6 %collective-permute-start.20 = (bf16[360,128]{1,0:T(8,128)(2,1)S(1)}, bf16[360,128]{1,0:T(8,128)(2,1)S(1)}, u32[]{:S(2)}, u32[]{:S(2)}) collective-permute-start(bf16[360,128]{1,0:T(8,128)(2,1)S(1)} %fusion.7), channel_id=1, source_target_pairs={{0,4},{1,5},{2,6},{3,7},{4,0},{5,1},{6,2},{7,3},{8,12},{9,13},{10,... | collective-permute-start | bytes 276488 | tf_op jit(solution)/shard_map/ppermute | solution.py:289
  52.4 1.6 %collective-permute-start.22 = (bf16[2,360,128]{2,1,0:T(8,128)(2,1)S(1)}, bf16[2,360,128]{2,1,0:T(8,128)(2,1)S(1)}, u32[]{:S(2)}, u32[]{:S(2)}) collective-permute-start(bf16[2,360,128]{2,1,0:T(8,128)(2,1)S(1)} %add_convert_fusion.1), channel_id=1, source_target_pairs={{0,2},{1,3},{2,0},{3,1},{4,6},{5,7},{6,4},{7,5},{8,10},{9,11},{10,... | collective-permute-start | bytes 552968 | tf_op jit(solution)/shard_map/ppermute | solution.py:289
  54.0 1.7 %collective-permute-done.21 = bf16[360,128]{1,0:T(8,128)(2,1)S(1)} collective-permute-done((bf16[360,128]{1,0:T(8,128)(2,1)S(1)}, bf16[360,128]{1,0:T(8,128)(2,1)S(1)}, u32[]{:S(2)}, u32[]{:S(2)}) %collective-permute-start.21) | collective-permute-done | bytes 92192 | tf_op jit(solution)/shard_map/ppermute | solution.py:289
  55.8 2.6 %collective-permute-start.29 = (bf16[360,128]{1,0:T(8,128)(2,1)S(1)}, bf16[360,128]{1,0:T(8,128)(2,1)S(1)}, u32[]{:S(2)}, u32[]{:S(2)}) collective-permute-start(bf16[360,128]{1,0:T(8,128)(2,1)S(1)} %fusion.5), channel_id=1, source_target_pairs={{0,24},{1,25},{2,26},{3,27},{4,28},{5,29},{6,30},{7,31},{8,16},{9,... | collective-permute-start | bytes 276488 | tf_op jit(solution)/shard_map/ppermute | solution.py:289
  58.4 1.7 %collective-permute-start.24 = (bf16[2,360,128]{2,1,0:T(8,128)(2,1)S(1)}, bf16[2,360,128]{2,1,0:T(8,128)(2,1)S(1)}, u32[]{:S(2)}, u32[]{:S(2)}) collective-permute-start(bf16[2,360,128]{2,1,0:T(8,128)(2,1)S(1)} %add_convert_fusion), channel_id=1, source_target_pairs={{0,4},{1,5},{2,6},{3,7},{4,0},{5,1},{6,2},{7,3},{8,12},{9,13},{10,... | collective-permute-start | bytes 552968 | tf_op jit(solution)/shard_map/ppermute | solution.py:289
  60.1 0.1 collective-permute-start.28
  60.2 4.8 %collective-permute-done.24 = bf16[2,360,128]{2,1,0:T(8,128)(2,1)S(1)} collective-permute-done((bf16[2,360,128]{2,1,0:T(8,128)(2,1)S(1)}, bf16[2,360,128]{2,1,0:T(8,128)(2,1)S(1)}, u32[]{:S(2)}, u32[]{:S(2)}) %collective-permute-start.24) | collective-permute-done | bytes 184352 | tf_op jit(solution)/shard_map/ppermute | solution.py:289
  65.2 1.7 %collective-permute-start.25 = (bf16[360,128]{1,0:T(8,128)(2,1)S(1)}, bf16[360,128]{1,0:T(8,128)(2,1)S(1)}, u32[]{:S(2)}, u32[]{:S(2)}) collective-permute-start(bf16[360,128]{1,0:T(8,128)(2,1)S(1)} %fusion.9), channel_id=1, source_target_pairs={{0,4},{1,5},{2,6},{3,7},{4,0},{5,1},{6,2},{7,3},{8,12},{9,13},{10,... | collective-permute-start | bytes 276488 | tf_op jit(solution)/shard_map/ppermute | solution.py:289
  66.8 2.8 %collective-permute-done.26 = bf16[360,128]{1,0:T(8,128)(2,1)S(1)} collective-permute-done((bf16[360,128]{1,0:T(8,128)(2,1)S(1)}, bf16[360,128]{1,0:T(8,128)(2,1)S(1)}, u32[]{:S(2)}, u32[]{:S(2)}) %collective-permute-start.26) | collective-permute-done | bytes 92192 | tf_op jit(solution)/shard_map/ppermute | solution.py:289
  69.8 4.5 %collective-permute-done.27 = bf16[360,128]{1,0:T(8,128)(2,1)S(1)} collective-permute-done((bf16[360,128]{1,0:T(8,128)(2,1)S(1)}, bf16[360,128]{1,0:T(8,128)(2,1)S(1)}, u32[]{:S(2)}, u32[]{:S(2)}) %collective-permute-start.27) | collective-permute-done | bytes 92192 | tf_op jit(solution)/shard_map/ppermute | solution.py:289
  74.3 0.7 fusion.11
  (46 shorter events, 0.9 us)
Async XLA Ops:
  3.5 11.4 %collective-permute-start.2 = (bf16[368,128]{1,0:T(8,128)(2,1)}, bf16[368,128]{1,0:T(8,128)(2,1)S(1)}, u32[]{:S(2)}, u32[]{:S(2)}) collective-permute-start(bf16[368,128]{1,0:T(8,128)(2,1)} %get-tuple-element.74), channel_id=1, source_target_pairs={{0,24},{1,25},{2,26},{3,27},{4,28},{5,29},{6,30},{7,31},{8,16},{9,... | collective-permute-start | bytes 282632 | tf_op jit(solution)/shard_map/ppermute | solution.py:289
  8.6 8.2 %collective-permute-start.1 = (bf16[368,128]{1,0:T(8,128)(2,1)}, bf16[368,128]{1,0:T(8,128)(2,1)S(1)}, u32[]{:S(2)}, u32[]{:S(2)}) collective-permute-start(bf16[368,128]{1,0:T(8,128)(2,1)} %get-tuple-element.74), channel_id=1, source_target_pairs={{0,16},{1,17},{2,18},{3,19},{4,20},{5,21},{6,22},{7,23},{8,24},{9,... | collective-permute-start | bytes 282632 | tf_op jit(solution)/shard_map/ppermute | solution.py:289
  8.6 11.8 %collective-permute-start.5 = (bf16[2,368,128]{2,1,0:T(8,128)(2,1)}, bf16[2,368,128]{2,1,0:T(8,128)(2,1)S(1)}, u32[]{:S(2)}, u32[]{:S(2)}) collective-permute-start(bf16[2,368,128]{2,1,0:T(8,128)(2,1)} %get-tuple-element.73.refs_1_), channel_id=1, source_target_pairs={{0,4},{1,5},{2,6},{3,7},{4,0},{5,1},{6,2},{7,3},{8,12},{9,13},{10,... | collective-permute-start | bytes 565256 | tf_op jit(solution)/shard_map/ppermute | solution.py:289
  10.1 10.3 %collective-permute-start = (bf16[2,368,128]{2,1,0:T(8,128)(2,1)}, bf16[2,368,128]{2,1,0:T(8,128)(2,1)S(1)}, u32[]{:S(2)}, u32[]{:S(2)}) collective-permute-start(bf16[2,368,128]{2,1,0:T(8,128)(2,1)} %get-tuple-element.73.refs_1_), channel_id=1, source_target_pairs={{0,8},{1,9},{2,10},{3,11},{4,12},{5,13},{6,14},{7,15},{8,0},{9,1},... | collective-permute-start | bytes 565256 | tf_op jit(solution)/shard_map/ppermute | solution.py:289
  11.6 1.2 %copy-start = (bf16[1,1440,360]{2,1,0:T(8,128)(2,1)S(1)}, bf16[1,1440,360]{2,1,0:T(8,128)(2,1)}, u32[]{:S(2)}) copy-start(bf16[1,1440,360]{2,1,0:T(8,128)(2,1)} %param.14) | copy-start | bytes 3110404
  12.9 1.2 %copy-start.1 = (bf16[1,1440,360]{2,1,0:T(8,128)(2,1)S(1)}, bf16[1,1440,360]{2,1,0:T(8,128)(2,1)}, u32[]{:S(2)}) copy-start(bf16[1,1440,360]{2,1,0:T(8,128)(2,1)} %param.16) | copy-start | bytes 3110404
  14.1 5.8 %copy-start.2 = (bf16[1,360,1440]{2,1,0:T(8,128)(2,1)S(1)}, bf16[1,360,1440]{2,1,0:T(8,128)(2,1)}, u32[]{:S(2)}) copy-start(bf16[1,360,1440]{2,1,0:T(8,128)(2,1)} %param.18) | copy-start | bytes 3110404
  14.9 10.6 %copy-start.3 = (s32[2]{0:T(128)S(1)}, s32[2]{0:T(128)}, u32[]{:S(2)}) copy-start(s32[2]{0:T(128)} %pad_add_fusion.place_ref.refs_0_) | copy-start | bytes 28
  14.9 10.6 %copy-start.4 = (bf16[2,368,128]{2,1,0:T(8,128)(2,1)S(1)}, bf16[2,368,128]{2,1,0:T(8,128)(2,1)}, u32[]{:S(2)}) copy-start(bf16[2,368,128]{2,1,0:T(8,128)(2,1)} %get-tuple-element.73.refs_1_) | copy-start | bytes 565252
  14.9 10.6 %copy-start.5 = (bf16[2,368,128]{2,1,0:T(8,128)(2,1)S(1)}, bf16[2,368,128]{2,1,0:T(8,128)(2,1)}, u32[]{:S(2)}) copy-start(bf16[2,368,128]{2,1,0:T(8,128)(2,1)} %get-tuple-element.82.refs_2_) | copy-start | bytes 565252
  16.9 5.7 %collective-permute-start.4 = (bf16[2,368,128]{2,1,0:T(8,128)(2,1)S(1)}, bf16[2,368,128]{2,1,0:T(8,128)(2,1)S(1)}, u32[]{:S(2)}, u32[]{:S(2)}) collective-permute-start(bf16[2,368,128]{2,1,0:T(8,128)(2,1)S(1)} %pad_maximum_fusion.refs_1_), channel_id=1, source_target_pairs={{0,2},{1,3},{2,0},{3,1},{4,6},{5,7},{6,4},{7,5},{8,10},{9,11},{10,... | collective-permute-start | bytes 565256 | tf_op jit(solution)/shard_map/ppermute | solution.py:289
  18.4 5.6 %collective-permute-start.3 = (bf16[2,368,128]{2,1,0:T(8,128)(2,1)S(1)}, bf16[2,368,128]{2,1,0:T(8,128)(2,1)S(1)}, u32[]{:S(2)}, u32[]{:S(2)}) collective-permute-start(bf16[2,368,128]{2,1,0:T(8,128)(2,1)S(1)} %pad_maximum_fusion.refs_1_), channel_id=1, source_target_pairs={{0,4},{1,5},{2,6},{3,7},{4,0},{5,1},{6,2},{7,3},{8,12},{9,13},{10,... | collective-permute-start | bytes 565256 | tf_op jit(solution)/shard_map/ppermute | solution.py:289
  24.0 1.4 %collective-permute-start.7 = (bf16[2,368,128]{2,1,0:T(8,128)(2,1)S(1)}, bf16[2,368,128]{2,1,0:T(8,128)(2,1)S(1)}, u32[]{:S(2)}, u32[]{:S(2)}) collective-permute-start(bf16[2,368,128]{2,1,0:T(8,128)(2,1)S(1)} %collective-permute-done.5.refs_3_), channel_id=1, source_target_pairs={{0,1},{1,0},{2,3},{3,2},{4,5},{5,4},{6,7},{7,6},{8,9},{9,8},{10,11... | collective-permute-start | bytes 565256 | tf_op jit(solution)/shard_map/ppermute | solution.py:289
  24.0 7.1 %collective-permute-start.10 = (bf16[2,368,128]{2,1,0:T(8,128)(2,1)S(1)}, bf16[2,368,128]{2,1,0:T(8,128)(2,1)S(1)}, u32[]{:S(2)}, u32[]{:S(2)}) collective-permute-start(bf16[2,368,128]{2,1,0:T(8,128)(2,1)S(1)} %pad_maximum_fusion.refs_1_), channel_id=1, source_target_pairs={{0,1},{1,0},{2,3},{3,2},{4,5},{5,4},{6,7},{7,6},{8,9},{9,8},{10,11... | collective-permute-start | bytes 565256 | tf_op jit(solution)/shard_map/ppermute | solution.py:289
  24.5 6.6 %collective-permute-start.6 = (bf16[2,368,128]{2,1,0:T(8,128)(2,1)S(1)}, bf16[2,368,128]{2,1,0:T(8,128)(2,1)S(1)}, u32[]{:S(2)}, u32[]{:S(2)}) collective-permute-start(bf16[2,368,128]{2,1,0:T(8,128)(2,1)S(1)} %collective-permute-done.3.refs_5_), channel_id=1, source_target_pairs={{0,2},{1,3},{2,0},{3,1},{4,6},{5,7},{6,4},{7,5},{8,10},{9,11},{10,... | collective-permute-start | bytes 565256 | tf_op jit(solution)/shard_map/ppermute | solution.py:289
  28.2 5.0 %collective-permute-start.8 = (bf16[4,360,128]{2,1,0:T(8,128)(2,1)S(1)}, bf16[4,360,128]{2,1,0:T(8,128)(2,1)S(1)}, u32[]{:S(2)}, u32[]{:S(2)}) collective-permute-start(bf16[4,360,128]{2,1,0:T(8,128)(2,1)S(1)} %get-tuple-element.89), channel_id=1, source_target_pairs={{0,1},{1,0},{2,3},{3,2},{4,5},{5,4},{6,7},{7,6},{8,9},{9,8},{10,11... | collective-permute-start | bytes 1105928 | tf_op jit(solution)/shard_map/ppermute | solution.py:289
  28.4 4.8 %collective-permute-start.12 = (bf16[2,368,128]{2,1,0:T(8,128)(2,1)S(1)}, bf16[2,368,128]{2,1,0:T(8,128)(2,1)S(1)}, u32[]{:S(2)}, u32[]{:S(2)}) collective-permute-start(bf16[2,368,128]{2,1,0:T(8,128)(2,1)S(1)} %collective-permute-done.3.refs_5_), channel_id=1, source_target_pairs={{0,1},{1,0},{2,3},{3,2},{4,5},{5,4},{6,7},{7,6},{8,9},{9,8},{10,11... | collective-permute-start | bytes 565256 | tf_op jit(solution)/shard_map/ppermute | solution.py:289
  28.8 2.9 %collective-permute-start.11 = (bf16[2,368,128]{2,1,0:T(8,128)(2,1)S(1)}, bf16[2,368,128]{2,1,0:T(8,128)(2,1)S(1)}, u32[]{:S(2)}, u32[]{:S(2)}) collective-permute-start(bf16[2,368,128]{2,1,0:T(8,128)(2,1)S(1)} %collective-permute-done.4.refs_3_), channel_id=1, source_target_pairs={{0,1},{1,0},{2,3},{3,2},{4,5},{5,4},{6,7},{7,6},{8,9},{9,8},{10,11... | collective-permute-start | bytes 565256 | tf_op jit(solution)/shard_map/ppermute | solution.py:289
  31.2 2.0 %collective-permute-start.9 = (bf16[2,368,128]{2,1,0:T(8,128)(2,1)S(1)}, bf16[2,368,128]{2,1,0:T(8,128)(2,1)S(1)}, u32[]{:S(2)}, u32[]{:S(2)}) collective-permute-start(bf16[2,368,128]{2,1,0:T(8,128)(2,1)S(1)} %collective-permute-done.refs_1_), channel_id=1, source_target_pairs={{0,1},{1,0},{2,3},{3,2},{4,5},{5,4},{6,7},{7,6},{8,9},{9,8},{10,11... | collective-permute-start | bytes 565256 | tf_op jit(solution)/shard_map/ppermute | solution.py:289
  31.2 2.0 %collective-permute-start.13 = (bf16[2,368,128]{2,1,0:T(8,128)(2,1)S(1)}, bf16[2,368,128]{2,1,0:T(8,128)(2,1)S(1)}, u32[]{:S(2)}, u32[]{:S(2)}) collective-permute-start(bf16[2,368,128]{2,1,0:T(8,128)(2,1)S(1)} %collective-permute-done.6.refs_7_), channel_id=1, source_target_pairs={{0,1},{1,0},{2,3},{3,2},{4,5},{5,4},{6,7},{7,6},{8,9},{9,8},{10,11... | collective-permute-start | bytes 565256 | tf_op jit(solution)/shard_map/ppermute | solution.py:289
  31.7 6.7 %collective-permute-start.14 = (bf16[2,368,128]{2,1,0:T(8,128)(2,1)S(1)}, bf16[2,368,128]{2,1,0:T(8,128)(2,1)S(1)}, u32[]{:S(2)}, u32[]{:S(2)}) collective-permute-start(bf16[2,368,128]{2,1,0:T(8,128)(2,1)S(1)} %collective-permute-done.refs_1_), channel_id=1, source_target_pairs={{0,4},{1,5},{2,6},{3,7},{4,0},{5,1},{6,2},{7,3},{8,12},{9,13},{10,... | collective-permute-start | bytes 565256 | tf_op jit(solution)/shard_map/ppermute | solution.py:289
  36.0 5.2 %collective-permute-start.15 = (bf16[4,360,128]{2,1,0:T(8,128)(2,1)S(1)}, bf16[4,360,128]{2,1,0:T(8,128)(2,1)S(1)}, u32[]{:S(2)}, u32[]{:S(2)}) collective-permute-start(bf16[4,360,128]{2,1,0:T(8,128)(2,1)S(1)} %get-tuple-element.104), channel_id=1, source_target_pairs={{0,1},{1,0},{2,3},{3,2},{4,5},{5,4},{6,7},{7,6},{8,9},{9,8},{10,11... | collective-permute-start | bytes 1105928 | tf_op jit(solution)/shard_map/ppermute | solution.py:289
  38.4 2.8 %collective-permute-start.16 = (bf16[2,368,128]{2,1,0:T(8,128)(2,1)S(1)}, bf16[2,368,128]{2,1,0:T(8,128)(2,1)S(1)}, u32[]{:S(2)}, u32[]{:S(2)}) collective-permute-start(bf16[2,368,128]{2,1,0:T(8,128)(2,1)S(1)} %collective-permute-done.14.refs_3_), channel_id=1, source_target_pairs={{0,1},{1,0},{2,3},{3,2},{4,5},{5,4},{6,7},{7,6},{8,9},{9,8},{10,11... | collective-permute-start | bytes 565256 | tf_op jit(solution)/shard_map/ppermute | solution.py:289
  41.2 1.9 %collective-permute-start.18 = (bf16[4,360,128]{2,1,0:T(8,128)(2,1)S(1)}, bf16[4,360,128]{2,1,0:T(8,128)(2,1)S(1)}, u32[]{:S(2)}, u32[]{:S(2)}) collective-permute-start(bf16[4,360,128]{2,1,0:T(8,128)(2,1)S(1)} %get-tuple-element.119), channel_id=1, source_target_pairs={{0,1},{1,0},{2,3},{3,2},{4,5},{5,4},{6,7},{7,6},{8,9},{9,8},{10,11... | collective-permute-start | bytes 1105928 | tf_op jit(solution)/shard_map/ppermute | solution.py:289
  41.8 6.6 %collective-permute-start.17 = (bf16[2,360,128]{2,1,0:T(8,128)(2,1)S(1)}, bf16[2,360,128]{2,1,0:T(8,128)(2,1)S(1)}, u32[]{:S(2)}, u32[]{:S(2)}) collective-permute-start(bf16[2,360,128]{2,1,0:T(8,128)(2,1)S(1)} %add_convert_fusion.3), channel_id=1, source_target_pairs={{0,2},{1,3},{2,0},{3,1},{4,6},{5,7},{6,4},{7,5},{8,10},{9,11},{10,... | collective-permute-start | bytes 552968 | tf_op jit(solution)/shard_map/ppermute | solution.py:289
  43.1 7.0 %collective-permute-start.19 = (bf16[2,360,128]{2,1,0:T(8,128)(2,1)S(1)}, bf16[2,360,128]{2,1,0:T(8,128)(2,1)S(1)}, u32[]{:S(2)}, u32[]{:S(2)}) collective-permute-start(bf16[2,360,128]{2,1,0:T(8,128)(2,1)S(1)} %add_convert_fusion.2), channel_id=1, source_target_pairs={{0,4},{1,5},{2,6},{3,7},{4,0},{5,1},{6,2},{7,3},{8,12},{9,13},{10,... | collective-permute-start | bytes 552968 | tf_op jit(solution)/shard_map/ppermute | solution.py:289
  47.4 10.9 %collective-permute-start.23 = (bf16[4,360,128]{2,1,0:T(8,128)(2,1)S(1)}, bf16[4,360,128]{2,1,0:T(8,128)(2,1)S(1)}, u32[]{:S(2)}, u32[]{:S(2)}) collective-permute-start(bf16[4,360,128]{2,1,0:T(8,128)(2,1)S(1)} %get-tuple-element.138), channel_id=1, source_target_pairs={{0,1},{1,0},{2,3},{3,2},{4,5},{5,4},{6,7},{7,6},{8,9},{9,8},{10,11... | collective-permute-start | bytes 1105928 | tf_op jit(solution)/shard_map/ppermute | solution.py:289
  50.1 5.5 %collective-permute-start.21 = (bf16[360,128]{1,0:T(8,128)(2,1)S(1)}, bf16[360,128]{1,0:T(8,128)(2,1)S(1)}, u32[]{:S(2)}, u32[]{:S(2)}) collective-permute-start(bf16[360,128]{1,0:T(8,128)(2,1)S(1)} %fusion.8), channel_id=1, source_target_pairs={{0,2},{1,3},{2,0},{3,1},{4,6},{5,7},{6,4},{7,5},{8,10},{9,11},{10,... | collective-permute-start | bytes 276488 | tf_op jit(solution)/shard_map/ppermute | solution.py:289
  50.8 9.3 %collective-permute-start.20 = (bf16[360,128]{1,0:T(8,128)(2,1)S(1)}, bf16[360,128]{1,0:T(8,128)(2,1)S(1)}, u32[]{:S(2)}, u32[]{:S(2)}) collective-permute-start(bf16[360,128]{1,0:T(8,128)(2,1)S(1)} %fusion.7), channel_id=1, source_target_pairs={{0,4},{1,5},{2,6},{3,7},{4,0},{5,1},{6,2},{7,3},{8,12},{9,13},{10,... | collective-permute-start | bytes 276488 | tf_op jit(solution)/shard_map/ppermute | solution.py:289
  52.4 7.8 %collective-permute-start.22 = (bf16[2,360,128]{2,1,0:T(8,128)(2,1)S(1)}, bf16[2,360,128]{2,1,0:T(8,128)(2,1)S(1)}, u32[]{:S(2)}, u32[]{:S(2)}) collective-permute-start(bf16[2,360,128]{2,1,0:T(8,128)(2,1)S(1)} %add_convert_fusion.1), channel_id=1, source_target_pairs={{0,2},{1,3},{2,0},{3,1},{4,6},{5,7},{6,4},{7,5},{8,10},{9,11},{10,... | collective-permute-start | bytes 552968 | tf_op jit(solution)/shard_map/ppermute | solution.py:289
  55.8 14.0 %collective-permute-start.29 = (bf16[360,128]{1,0:T(8,128)(2,1)S(1)}, bf16[360,128]{1,0:T(8,128)(2,1)S(1)}, u32[]{:S(2)}, u32[]{:S(2)}) collective-permute-start(bf16[360,128]{1,0:T(8,128)(2,1)S(1)} %fusion.5), channel_id=1, source_target_pairs={{0,24},{1,25},{2,26},{3,27},{4,28},{5,29},{6,30},{7,31},{8,16},{9,... | collective-permute-start | bytes 276488 | tf_op jit(solution)/shard_map/ppermute | solution.py:289
  58.4 6.6 %collective-permute-start.24 = (bf16[2,360,128]{2,1,0:T(8,128)(2,1)S(1)}, bf16[2,360,128]{2,1,0:T(8,128)(2,1)S(1)}, u32[]{:S(2)}, u32[]{:S(2)}) collective-permute-start(bf16[2,360,128]{2,1,0:T(8,128)(2,1)S(1)} %add_convert_fusion), channel_id=1, source_target_pairs={{0,4},{1,5},{2,6},{3,7},{4,0},{5,1},{6,2},{7,3},{8,12},{9,13},{10,... | collective-permute-start | bytes 552968 | tf_op jit(solution)/shard_map/ppermute | solution.py:289
  60.1 9.7 %collective-permute-start.28 = (bf16[360,128]{1,0:T(8,128)(2,1)S(1)}, bf16[360,128]{1,0:T(8,128)(2,1)S(1)}, u32[]{:S(2)}, u32[]{:S(2)}) collective-permute-start(bf16[360,128]{1,0:T(8,128)(2,1)S(1)} %fusion.6), channel_id=1, source_target_pairs={{0,16},{1,17},{2,18},{3,19},{4,20},{5,21},{6,22},{7,23},{8,24},{9,... | collective-permute-start | bytes 276488 | tf_op jit(solution)/shard_map/ppermute | solution.py:289
  65.0 4.6 %collective-permute-start.26 = (bf16[360,128]{1,0:T(8,128)(2,1)S(1)}, bf16[360,128]{1,0:T(8,128)(2,1)S(1)}, u32[]{:S(2)}, u32[]{:S(2)}) collective-permute-start(bf16[360,128]{1,0:T(8,128)(2,1)S(1)} %fusion.10), channel_id=1, source_target_pairs={{0,2},{1,3},{2,0},{3,1},{4,6},{5,7},{6,4},{7,5},{8,10},{9,11},{10,... | collective-permute-start | bytes 276488 | tf_op jit(solution)/shard_map/ppermute | solution.py:289
  65.2 4.6 %collective-permute-start.25 = (bf16[360,128]{1,0:T(8,128)(2,1)S(1)}, bf16[360,128]{1,0:T(8,128)(2,1)S(1)}, u32[]{:S(2)}, u32[]{:S(2)}) collective-permute-start(bf16[360,128]{1,0:T(8,128)(2,1)S(1)} %fusion.9), channel_id=1, source_target_pairs={{0,4},{1,5},{2,6},{3,7},{4,0},{5,1},{6,2},{7,3},{8,12},{9,13},{10,... | collective-permute-start | bytes 276488 | tf_op jit(solution)/shard_map/ppermute | solution.py:289
  69.7 4.6 %collective-permute-start.27 = (bf16[360,128]{1,0:T(8,128)(2,1)S(1)}, bf16[360,128]{1,0:T(8,128)(2,1)S(1)}, u32[]{:S(2)}, u32[]{:S(2)}) collective-permute-start(bf16[360,128]{1,0:T(8,128)(2,1)S(1)} %fusion), channel_id=1, source_target_pairs={{0,8},{1,9},{2,10},{3,11},{4,12},{5,13},{6,14},{7,15},{8,0},{9,1},... | collective-permute-start | bytes 276488 | tf_op jit(solution)/shard_map/ppermute | solution.py:289

commit v6 on v5

--- a/solution.py
+++ b/solution.py
@@ -137,14 +137,14 @@
         copy.wait()
 
 
-def pieces_kernel(groups, per, experts, place_ref, *refs):
+def pieces_kernel(groups, per, experts, *refs):
     sources, (one_ref, near_ref, far_ref) = refs[:4], refs[4:7]
     tokens_ref, gain_ref, ids_ref, weights_ref = refs[7:11]
     fetch(sources, refs[7:11], refs[11])
     features, lanes = tokens_ref.shape
     quarter = features // groups
     tail = one_ref.shape[0] - quarter
-    rep = place_ref[0]
+    rep = lax.axis_index("rep")
     values = tokens_ref[...].astype(jnp.float32)
     scale = lax.rsqrt(jnp.mean(values * values, axis=0, keepdims=True) + 1e-05)
     gain = jnp.broadcast_to(gain_ref[...].reshape(1, features), (lanes, features)).T
@@ -180,32 +180,32 @@
             one_ref[...] = piece
 
 
-def make_pieces(place, tokens, norm_gain, expert_ids, route_weights, groups, per, experts):
+def make_pieces(tokens, norm_gain, expert_ids, route_weights, groups, per, experts):
     features, lanes = tokens.shape
     rows = round_up(features // groups + 3 * per, 16)
     pair = jax.ShapeDtypeStruct((groups // 2, rows, lanes), jnp.bfloat16)
     arrays = (tokens, norm_gain, expert_ids, route_weights)
     return pl.pallas_call(
         functools.partial(pieces_kernel, groups, per, experts),
-        in_specs=[pl.BlockSpec(memory_space=pltpu.SMEM)] + [pl.BlockSpec(memory_space=pltpu.HBM)] * 4,
+        in_specs=[pl.BlockSpec(memory_space=pltpu.HBM)] * 4,
         out_specs=[pl.BlockSpec(memory_space=pltpu.VMEM)] * 3,
         out_shape=[jax.ShapeDtypeStruct((rows, lanes), jnp.bfloat16), pair, pair],
         scratch_shapes=[pltpu.VMEM(a.shape, a.dtype) for a in arrays]
         + [pltpu.SemaphoreType.DMA((len(arrays),))],
         compiler_params=pltpu.CompilerParams(vmem_limit_bytes=60 * 2**20),
-    )(place, *arrays)
+    )(*arrays)
 
 
 def expert_kernel(quarter, per, blocks, slots, *refs):
     groups = len(blocks[0])
     counted = 1 + max(at for block in blocks for at, _ in block)
-    place_ref, arrays = refs[0], refs[1 : 1 + counted]
-    gate_up_ref, bias_ref, down_ref, down_bias_ref, keep_ref, send_ref = refs[1 + counted : 7 + counted]
-    scratch = refs[7 + counted :]
+    arrays = refs[:counted]
+    gate_up_ref, bias_ref, down_ref, down_bias_ref, keep_ref, send_ref = refs[counted : 6 + counted]
+    scratch = refs[6 + counted :]
     _, piece_rows, lanes = arrays[0].shape
     size = gate_up_ref.shape[1] // groups
     hidden = gate_up_ref.shape[0] // 2
-    rep, seq = place_ref[0], place_ref[1]
+    rep, seq = lax.axis_index("rep"), lax.axis_index("seq")
     halves = len(scratch)
     count = len(blocks) // halves
     row = lax.broadcasted_iota(jnp.int32, (piece_rows - quarter, lanes), 0)
@@ -242,7 +242,7 @@
                 target[slots[half * count + j][k // 2]] = rows[:quarter, j * lanes : (j + 1) * lanes]
 
 
-def run_expert(place, arrays, blocks, slots, weights, sizes, halves):
+def run_expert(arrays, blocks, slots, weights, sizes, halves):
     quarter, per = sizes
     lanes = arrays[0].shape[2]
     gate_up, down = weights[0], weights[2]
@@ -252,7 +252,7 @@
     columns = tokens // halves
     return pl.pallas_call(
         functools.partial(expert_kernel, quarter, per, blocks, slots),
-        in_specs=[pl.BlockSpec(memory_space=pltpu.SMEM)] + [whole] * (len(arrays) + len(weights)),
+        in_specs=[whole] * (len(arrays) + len(weights)),
         out_specs=[whole, whole],
         out_shape=[out, out],
         scratch_shapes=[pltpu.VMEM((gate_up.shape[1], columns), jnp.bfloat16)] * halves,
@@ -262,7 +262,7 @@
             bytes_accessed=2 * (gate_up.size + down.size),
             transcendentals=0,
         ),
-    )(place, *arrays, *weights)
+    )(*arrays, *weights)
 
 
 def dense(
@@ -281,7 +281,6 @@
     experts = lax.axis_size("seq")
     groups = lax.axis_size("rep")
     quarter = features // groups
-    rep, seq = lax.axis_index("rep"), lax.axis_index("seq")
     devices = experts * groups
     core, along_y, along_x, along_z = 1, 2, groups, 2 * groups
 
@@ -289,9 +288,8 @@
         return lax.ppermute(array, ("seq", "rep"), [(i, i ^ step) for i in range(devices)])
 
     per = -(-experts // groups)
-    place = jnp.stack([rep, seq]).astype(jnp.int32)
     one, near, far = make_pieces(
-        place, tokens.T, norm_gain, expert_ids.T, route_weights.T, groups, per, experts
+        tokens.T, norm_gain, expert_ids.T, route_weights.T, groups, per, experts
     )
     z_2, z_3 = swap(one, 2 * along_z), swap(one, 3 * along_z)
     x_0 = swap(near, along_x)
@@ -309,7 +307,9 @@
     )
     z_2, z_3, inward = tied((z_2, z_3, inward))
     z_high = jnp.stack([z_2, z_3])
+    diagonal = along_x + along_y
     x_high, y_high = swap(z_high, along_x), swap(z_high, along_y)
+    d_high = swap(z_high, diagonal)
     outward = arrange(
         outward_kernel,
         groups,
@@ -318,53 +318,58 @@
         (wide, hidden_pad),
         wide // groups,
     )
-    z_1, x_high, y_high, x_0, outward = tied((z_1, x_high, y_high, x_0, outward))
+    x_0, outward = tied((x_0, outward))
     weights = (*inward, *outward)
-    corner = swap(x_high, along_y)
-    x_1 = swap(z_1, along_x)
 
     def pairs(first, step):
         return [[(first + step * x + k % 2, k // 2) for k in range(groups)] for x in range(2)]
 
-    slots_a, slots_b = ((2, 0), (3, 1)), ((2, 3), (0, 1))
+    slots = ((0, 1), (2, 3))
     sizes = (quarter, per)
     keep_0, send_0 = run_expert(
-        place, (near, far, x_0, swap(x_0, core)), pairs(0, 2), slots_a, weights, sizes, 1
-    )
+        (near, far, x_0, swap(x_0, core)), pairs(0, 2), slots, weights, sizes, 1
+    )
+    z_1, x_high, y_high, d_high, keep_0, send_0 = tied(
+        (z_1, x_high, y_high, d_high, keep_0, send_0)
+    )
+    x_1 = swap(z_1, along_x)
     got_0 = swap(send_0, core)
-    corner, keep_0, send_0 = tied((corner, keep_0, send_0))
     high = (z_high, swap(z_high, core), y_high, swap(y_high, core))
-    high = high + (x_high, swap(x_high, core), corner, swap(corner, core))
+    high = high + (x_high, swap(x_high, core), d_high, swap(d_high, core))
     z_1_core = swap(z_1, core)
-    keep_0, got_0, z_1_core, high = tied((keep_0, got_0, z_1_core, high))
+    got_0, z_1_core, high = tied((got_0, z_1_core, high))
     line = [[[(4 * x + k, n) for k in range(groups)] for x in range(2)] for n in range(2)]
-    keep_2, send_2 = run_expert(place, high, line[0], slots_a, weights, sizes, 1)
+    keep_2, send_2 = run_expert(high, line[0], slots, weights, sizes, 1)
     got_2 = swap(send_2, core)
-    keep_2, x_1, high = tied((keep_2, x_1, high))
+    keep_2, high = tied((keep_2, high))
+    keep_3, send_3 = run_expert(high, line[1], slots, weights, sizes, 1)
+    got_2, keep_3, x_1 = tied((got_2, keep_3, x_1))
+    got_3 = swap(send_3, core)
+
     near_1 = (z_1, z_1_core, x_1, swap(x_1, core))
-    keep_3, send_3 = run_expert(place, high, line[1], slots_b, weights, sizes, 1)
-    got_2, keep_3, send_3, near_1 = tied((got_2, keep_3, send_3, near_1))
-    got_3 = swap(send_3, core)
-    first_y = swap(add_up(keep_2[0:2], got_2[0:2]), along_y)
-    first_x = swap(add_up(keep_3[0:2], got_3[0:2]), along_x)
-    got_2, got_3, near_1 = tied((got_2, got_3, near_1))
-    keep_1, send_1 = run_expert(place, near_1, pairs(0, 2), slots_b, weights, sizes, 1)
+    keep_1, send_1 = run_expert(near_1, pairs(0, 2), slots, weights, sizes, 1)
     got_1 = swap(send_1, core)
-
-    first_y, first_x, keep_0, got_0, keep_1 = tied((first_y, first_x, keep_0, got_0, keep_1))
-    last_x = swap(add_up(keep_2[3], got_2[3], first_y[1]), along_x)
-    last_y = swap(add_up(keep_3[3], got_3[3], first_x[1]), along_y)
-    early_y = swap(add_up(keep_0[0:2], got_0[0:2]), along_y)
-    early_x = swap(add_up(keep_1[0:2], got_1[0:2]), along_x)
-    line_2 = add_up(keep_2[2], got_2[2], first_y[0], last_x)
-    line_3 = add_up(keep_3[2], got_3[2], first_x[0], last_y)
+    keep_1, got_3 = tied((keep_1, got_3))
+    def outer(first, second, at):
+        return jnp.stack([add_up(keep[at], got[at]) for keep, got in (first, second)])
+
+    far_lines = ((keep_2, got_2), (keep_3, got_3))
+    y_sum = swap(outer(*far_lines, 1), along_y)
+    x_sum = swap(outer(*far_lines, 2), along_x)
+    d_sum = swap(outer(*far_lines, 3), diagonal)
+    line_2 = add_up(keep_2[0], got_2[0], x_sum[0], y_sum[0], d_sum[0])
+    line_3 = add_up(keep_3[0], got_3[0], x_sum[1], y_sum[1], d_sum[1])
     back_2, back_3 = swap(line_2, 2 * along_z), swap(line_3, 3 * along_z)
-    _, _, early_y, early_x = tied((line_2, line_3, early_y, early_x))
-    end_x = swap(add_up(keep_0[3], got_0[3], early_y[1]), along_x)
-    end_y = swap(add_up(keep_1[3], got_1[3], early_x[1]), along_y)
-    line_1 = add_up(keep_1[2], got_1[2], early_x[0], end_y)
+    near_lines = ((keep_0, got_0), (keep_1, got_1))
+    x_near = swap(outer(*near_lines, 2), along_x)
+    y_near = swap(outer(*near_lines, 1), along_y)
+    d_near = swap(outer(*near_lines, 3), diagonal)
+    _, _, x_near, y_near, d_near = tied((line_2, line_3, x_near, y_near, d_near))
+    line_1 = add_up(keep_1[0], got_1[0], x_near[1], y_near[1], d_near[1])
     back_1 = swap(line_1, along_z)
-    mixed = add_up(keep_0[2], got_0[2], early_y[0], end_x, back_1, back_2, back_3)
+    mixed = add_up(
+        keep_0[0], got_0[0], x_near[0], y_near[0], d_near[0], back_1, back_2, back_3
+    )
     return mixed.T
 
 

time: 75.3 us -> 66.5 us (0.88)
  waiting for transfers between devices: 27.6 us -> 19.9 us
  Pallas kernels: 15.1 us -> 12.3 us
  starting transfers between devices: 27 us -> 28.7 us
    ppermute x30 -> x28, waiting for transfers between devices: 27.6 us -> 19.9 us  [swap(): lax.ppermute(array, ('seq', 'rep'), [(i, i ^ step) for i in range(devices)])]
    pallas_call x4, Pallas kernels: 11 us -> 8.8 us  [run_expert(): pl.pallas_call(functools.partial(expert_kernel, quarter, per, blocks, slo...]
    ppermute x30 -> x28, starting transfers between devices: 27 us -> 28.7 us  [swap(): lax.ppermute(array, ('seq', 'rep'), [(i, i ^ step) for i in range(devices)])]
    unnamed x12 -> x10, local copies, waits for them, and re-layouts: 2.5 us -> 2.88 us
  transfers between devices with their start and end apart: 30 -> 28, of which waited for: 13 -> 12; matrix products, arithmetic and copies ran while one was open for 2% -> 2% of each run, Pallas kernels for 16% -> 15%
where the time goes in v6:
time: 66.5 us; the launch traced here: 66.2 us
  starting transfers between devices  28.7 us (43%)
  waiting for transfers between devices  19.9 us (30%)
  Pallas kernels  12.3 us (18%)
  local copies, waits for them, and re-layouts  2.88 us (4%)
  other arithmetic  2.12 us (3%)
    ppermute x28, starting transfers between devices, swap(): lax.ppermute(array, ('seq', 'rep'), [(i, i ^ step) for i in range(devices)])  28.7 us
    ppermute x28, waiting for transfers between devices, swap(): lax.ppermute(array, ('seq', 'rep'), [(i, i ^ step) for i in range(devices)])  19.9 us
    pallas_call x4, Pallas kernels, run_expert(): pl.pallas_call(functools.partial(expert_kernel, quarter, per, blocks, slo...  8.8 us
    unnamed x10, local copies, waits for them, and re-layouts  2.88 us
    pallas_call x1, Pallas kernels, make_pieces(): pl.pallas_call(functools.partial(pieces_kernel, groups, per, experts), in...  2.3 us
  transfers between devices with their start and end apart: 28, of which 12 were waited for; matrix products, arithmetic and copies ran while one was open for 2% of the time, Pallas kernels for 15%

profile of v6, /device:TPU:0, one launch (start us, length us, event | category | flops | bytes accessed | tf_op | source)
XLA Modules:
  0.0 66.2 jit_solution(16385814497753985257)
XLA Ops:
  0.0 2.3 %shard_map.100 = (bf16[368,128]{1,0:T(8,128)(2,1)}, bf16[2,368,128]{2,1,0:T(8,128)(2,1)}, bf16[2,368,128]{2,1,0:T(8,128)(2,1)}) custom-call(bf16[1440,128]{1,0:T(8,128)(2,1)} %bitcast.29, f32[1440]{0:T(1024)} %refs_1_.1, s32[4,128]{1,0:T(4,128)} %bitcast.32, f32[4,128]{1,0:T(4,128)} %bitcast.33), custom_call_target="tpu_custom_call" | custom-call | tf_op jit(solution)/shard_map/pallas_call | solution.py:188
  2.3 3.0 %collective-permute-start.6 = (bf16[2,368,128]{2,1,0:T(8,128)(2,1)}, bf16[2,368,128]{2,1,0:T(8,128)(2,1)S(1)}, u32[]{:S(2)}, u32[]{:S(2)}) collective-permute-start(bf16[2,368,128]{2,1,0:T(8,128)(2,1)} %get-tuple-element.60.refs_0_), channel_id=1, source_target_pairs={{0,4},{1,5},{2,6},{3,7},{4,0},{5,1},{6,2},{7,3},{8,12},{9,13},{10,... | collective-permute-start | bytes 565256 | tf_op jit(solution)/shard_map/ppermute | solution.py:288
  5.3 2.6 %collective-permute-start.1 = (bf16[368,128]{1,0:T(8,128)(2,1)}, bf16[368,128]{1,0:T(8,128)(2,1)S(1)}, u32[]{:S(2)}, u32[]{:S(2)}) collective-permute-start(bf16[368,128]{1,0:T(8,128)(2,1)} %get-tuple-element.61), channel_id=1, source_target_pairs={{0,16},{1,17},{2,18},{3,19},{4,20},{5,21},{6,22},{7,23},{8,24},{9,... | collective-permute-start | bytes 282632 | tf_op jit(solution)/shard_map/ppermute | solution.py:288
  7.9 1.3 %collective-permute-start.2 = (bf16[368,128]{1,0:T(8,128)(2,1)}, bf16[368,128]{1,0:T(8,128)(2,1)S(1)}, u32[]{:S(2)}, u32[]{:S(2)}) collective-permute-start(bf16[368,128]{1,0:T(8,128)(2,1)} %get-tuple-element.61), channel_id=1, source_target_pairs={{0,24},{1,25},{2,26},{3,27},{4,28},{5,29},{6,30},{7,31},{8,16},{9,... | collective-permute-start | bytes 282632 | tf_op jit(solution)/shard_map/ppermute | solution.py:288
  9.3 0.7 %pad_maximum_fusion.7.biases_ref = f32[3,360]{1,0:T(4,128)S(1)} fusion(f32[1,360]{1,0:T(1,128)} %param.19, f32[1,360]{1,0:T(1,128)} %param.17, f32[1,360]{1,0:T(1,128)} %param.15), kind=kLoop, calls=%fused_computation.30 | loop fusion | flops 2160 | bytes 8640 | tf_op jit(solution)/shard_map/concatenate | solution.py:299
  10.0 1.2 %copy-done.2 = bf16[1,360,1440]{2,1,0:T(8,128)(2,1)S(1)} copy-done((bf16[1,360,1440]{2,1,0:T(8,128)(2,1)S(1)}, bf16[1,360,1440]{2,1,0:T(8,128)(2,1)}, u32[]{:S(2)}) %copy-start.2) | copy-done | bytes 1036824
  11.2 0.4 shard_map.102
  11.8 0.4 copy-done.3
  12.1 0.2 collective-permute-start
  12.4 1.2 %copy-done.1 = bf16[1,1440,360]{2,1,0:T(8,128)(2,1)S(1)} copy-done((bf16[1,1440,360]{2,1,0:T(8,128)(2,1)S(1)}, bf16[1,1440,360]{2,1,0:T(8,128)(2,1)}, u32[]{:S(2)}) %copy-start.1) | copy-done | bytes 1036824
  13.6 0.8 %shard_map.101 = (bf16[768,1536]{1,0:T(8,128)(2,1)S(1)}, f32[768,128]{1,0:T(8,128)S(1)}) custom-call(bf16[1440,360]{1,0:T(8,128)(2,1)S(1)} %bitcast.26, bf16[1440,360]{1,0:T(8,128)(2,1)S(1)} %bitcast.27, f32[3,360]{1,0:T(4,128)S(1)} %pad_maximum_fusion.7.biases_ref), custom_call_target="tpu_custom_call" | custom-call | bytes 8294400 | tf_op jit(solution)/shard_map/pallas_call | solution.py:116
  14.4 0.8 %collective-permute-done.1 = bf16[368,128]{1,0:T(8,128)(2,1)S(1)} collective-permute-done((bf16[368,128]{1,0:T(8,128)(2,1)}, bf16[368,128]{1,0:T(8,128)(2,1)S(1)}, u32[]{:S(2)}, u32[]{:S(2)}) %collective-permute-start.1) | collective-permute-done | bytes 94240 | tf_op jit(solution)/shard_map/ppermute | solution.py:288
  15.3 0.6 collective-permute-start.3
  15.8 1.6 %collective-permute-start.4 = (bf16[2,368,128]{2,1,0:T(8,128)(2,1)S(1)}, bf16[2,368,128]{2,1,0:T(8,128)(2,1)S(1)}, u32[]{:S(2)}, u32[]{:S(2)}) collective-permute-start(bf16[2,368,128]{2,1,0:T(8,128)(2,1)S(1)} %pad_maximum_fusion.refs_0_), channel_id=1, source_target_pairs={{0,2},{1,3},{2,0},{3,1},{4,6},{5,7},{6,4},{7,5},{8,10},{9,11},{10,... | collective-permute-start | bytes 565256 | tf_op jit(solution)/shard_map/ppermute | solution.py:288
  17.4 1.4 %collective-permute-start.5 = (bf16[2,368,128]{2,1,0:T(8,128)(2,1)S(1)}, bf16[2,368,128]{2,1,0:T(8,128)(2,1)S(1)}, u32[]{:S(2)}, u32[]{:S(2)}) collective-permute-start(bf16[2,368,128]{2,1,0:T(8,128)(2,1)S(1)} %pad_maximum_fusion.refs_0_), channel_id=1, source_target_pairs={{0,6},{1,7},{2,4},{3,5},{4,2},{5,3},{6,0},{7,1},{8,14},{9,15},{10,... | collective-permute-start | bytes 565256 | tf_op jit(solution)/shard_map/ppermute | solution.py:288
  18.8 2.2 %shard_map.103 = (bf16[4,360,128]{2,1,0:T(8,128)(2,1)S(1)}, bf16[4,360,128]{2,1,0:T(8,128)(2,1)S(1)}) custom-call(bf16[2,368,128]{2,1,0:T(8,128)(2,1)S(1)} %copy-done.3, bf16[2,368,128]{2,1,0:T(8,128)(2,1)S(1)} %copy-done.4, bf16[2,368,128]{2,1,0:T(8,128)(2,1)S(1)} %collective-permute-done.6.refs_2_, ...), custom_call_target="tpu_custom_call" | custom-call | flops 1811939328 | bytes 3538944 | tf_op jit(solution)/shard_map/pallas_call | solution.py:253
  21.1 1.7 %collective-permute-done.3.refs_4_ = bf16[2,368,128]{2,1,0:T(8,128)(2,1)S(1)} collective-permute-done((bf16[2,368,128]{2,1,0:T(8,128)(2,1)S(1)}, bf16[2,368,128]{2,1,0:T(8,128)(2,1)S(1)}, u32[]{:S(2)}, u32[]{:S(2)}) %collective-permute-start.3) | collective-permute-done | bytes 188448 | tf_op jit(solution)/shard_map/ppermute | solution.py:288
  22.8 3.5 %collective-permute-done.4.refs_2_ = bf16[2,368,128]{2,1,0:T(8,128)(2,1)S(1)} collective-permute-done((bf16[2,368,128]{2,1,0:T(8,128)(2,1)S(1)}, bf16[2,368,128]{2,1,0:T(8,128)(2,1)S(1)}, u32[]{:S(2)}, u32[]{:S(2)}) %collective-permute-start.4) | collective-permute-done | bytes 188448 | tf_op jit(solution)/shard_map/ppermute | solution.py:288
  26.3 0.5 collective-permute-start.9
  26.9 0.5 collective-permute-start.12
  27.4 0.9 %collective-permute-done.9.refs_1_ = bf16[2,368,128]{2,1,0:T(8,128)(2,1)S(1)} collective-permute-done((bf16[2,368,128]{2,1,0:T(8,128)(2,1)S(1)}, bf16[2,368,128]{2,1,0:T(8,128)(2,1)S(1)}, u32[]{:S(2)}, u32[]{:S(2)}) %collective-permute-start.9) | collective-permute-done | bytes 188448 | tf_op jit(solution)/shard_map/ppermute | solution.py:288
  28.3 1.2 %collective-permute-start.15 = (bf16[2,368,128]{2,1,0:T(8,128)(2,1)S(1)}, bf16[2,368,128]{2,1,0:T(8,128)(2,1)S(1)}, u32[]{:S(2)}, u32[]{:S(2)}) collective-permute-start(bf16[2,368,128]{2,1,0:T(8,128)(2,1)S(1)} %collective-permute-done.refs_0_), channel_id=1, source_target_pairs={{0,4},{1,5},{2,6},{3,7},{4,0},{5,1},{6,2},{7,3},{8,12},{9,13},{10,... | collective-permute-start | bytes 565256 | tf_op jit(solution)/shard_map/ppermute | solution.py:288
  29.6 2.2 %shard_map.104 = (bf16[4,360,128]{2,1,0:T(8,128)(2,1)S(1)}, bf16[4,360,128]{2,1,0:T(8,128)(2,1)S(1)}) custom-call(bf16[2,368,128]{2,1,0:T(8,128)(2,1)S(1)} %pad_maximum_fusion.refs_0_, bf16[2,368,128]{2,1,0:T(8,128)(2,1)S(1)} %collective-permute-done.10.refs_1_, bf16[2,368,128]{2,1,0:T(8,128)(2,1)S(1)} %collective-permute-done.4.refs_2_, ...), custom_call_target="tpu_custom_call" | custom-call | flops 1811939328 | bytes 3538944 | tf_op jit(solution)/shard_map/pallas_call | solution.py:253
  31.8 2.2 %shard_map.105 = (bf16[4,360,128]{2,1,0:T(8,128)(2,1)S(1)}, bf16[4,360,128]{2,1,0:T(8,128)(2,1)S(1)}) custom-call(bf16[2,368,128]{2,1,0:T(8,128)(2,1)S(1)} %pad_maximum_fusion.refs_0_, bf16[2,368,128]{2,1,0:T(8,128)(2,1)S(1)} %collective-permute-done.10.refs_1_, bf16[2,368,128]{2,1,0:T(8,128)(2,1)S(1)} %collective-permute-done.4.refs_2_, ...), custom_call_target="tpu_custom_call" | custom-call | flops 1811939328 | bytes 3538944 | tf_op jit(solution)/shard_map/pallas_call | solution.py:253
  34.1 0.6 collective-permute-start.17
  34.6 0.1 add_convert_fusion.4
  34.7 0.4 collective-permute-done.15.refs_2_
  35.1 0.1 add_convert_fusion.14
  35.2 1.3 %collective-permute-done.16.refs_3_ = bf16[2,368,128]{2,1,0:T(8,128)(2,1)S(1)} collective-permute-done((bf16[2,368,128]{2,1,0:T(8,128)(2,1)S(1)}, bf16[2,368,128]{2,1,0:T(8,128)(2,1)S(1)}, u32[]{:S(2)}, u32[]{:S(2)}) %collective-permute-start.16) | collective-permute-done | bytes 188448 | tf_op jit(solution)/shard_map/ppermute | solution.py:288
  36.5 2.2 %shard_map.106 = (bf16[4,360,128]{2,1,0:T(8,128)(2,1)S(1)}, bf16[4,360,128]{2,1,0:T(8,128)(2,1)S(1)}) custom-call(bf16[2,368,128]{2,1,0:T(8,128)(2,1)S(1)} %collective-permute-done.refs_0_, bf16[2,368,128]{2,1,0:T(8,128)(2,1)S(1)} %collective-permute-done.9.refs_1_, bf16[2,368,128]{2,1,0:T(8,128)(2,1)S(1)} %collective-permute-done.15.refs_2_, ...), custom_call_target="tpu_custom_call" | custom-call | flops 1811939328 | bytes 3538944 | tf_op jit(solution)/shard_map/pallas_call | solution.py:253
  38.7 0.2 collective-permute-start.21
  39.0 1.7 %collective-permute-start.20 = (bf16[2,360,128]{2,1,0:T(8,128)(2,1)S(1)}, bf16[2,360,128]{2,1,0:T(8,128)(2,1)S(1)}, u32[]{:S(2)}, u32[]{:S(2)}) collective-permute-start(bf16[2,360,128]{2,1,0:T(8,128)(2,1)S(1)} %pad_maximum_fusion.3), channel_id=1, source_target_pairs={{0,6},{1,7},{2,4},{3,5},{4,2},{5,3},{6,0},{7,1},{8,14},{9,15},{10,... | collective-permute-start | bytes 552968 | tf_op jit(solution)/shard_map/ppermute | solution.py:288
  40.8 1.1 %collective-permute-start.19 = (bf16[2,360,128]{2,1,0:T(8,128)(2,1)S(1)}, bf16[2,360,128]{2,1,0:T(8,128)(2,1)S(1)}, u32[]{:S(2)}, u32[]{:S(2)}) collective-permute-start(bf16[2,360,128]{2,1,0:T(8,128)(2,1)S(1)} %pad_maximum_fusion.2), channel_id=1, source_target_pairs={{0,2},{1,3},{2,0},{3,1},{4,6},{5,7},{6,4},{7,5},{8,10},{9,11},{10,... | collective-permute-start | bytes 552968 | tf_op jit(solution)/shard_map/ppermute | solution.py:288
  41.9 0.9 %collective-permute-start.18 = (bf16[2,360,128]{2,1,0:T(8,128)(2,1)S(1)}, bf16[2,360,128]{2,1,0:T(8,128)(2,1)S(1)}, u32[]{:S(2)}, u32[]{:S(2)}) collective-permute-start(bf16[2,360,128]{2,1,0:T(8,128)(2,1)S(1)} %pad_maximum_fusion.1), channel_id=1, source_target_pairs={{0,4},{1,5},{2,6},{3,7},{4,0},{5,1},{6,2},{7,3},{8,12},{9,13},{10,... | collective-permute-start | bytes 552968 | tf_op jit(solution)/shard_map/ppermute | solution.py:288
  42.9 1.3 %collective-permute-start.22 = (bf16[2,360,128]{2,1,0:T(8,128)(2,1)S(1)}, bf16[2,360,128]{2,1,0:T(8,128)(2,1)S(1)}, u32[]{:S(2)}, u32[]{:S(2)}) collective-permute-start(bf16[2,360,128]{2,1,0:T(8,128)(2,1)S(1)} %pad_maximum_fusion.4), channel_id=1, source_target_pairs={{0,4},{1,5},{2,6},{3,7},{4,0},{5,1},{6,2},{7,3},{8,12},{9,13},{10,... | collective-permute-start | bytes 552968 | tf_op jit(solution)/shard_map/ppermute | solution.py:288
  44.2 1.1 %collective-permute-start.23 = (bf16[2,360,128]{2,1,0:T(8,128)(2,1)S(1)}, bf16[2,360,128]{2,1,0:T(8,128)(2,1)S(1)}, u32[]{:S(2)}, u32[]{:S(2)}) collective-permute-start(bf16[2,360,128]{2,1,0:T(8,128)(2,1)S(1)} %pad_maximum_fusion.5), channel_id=1, source_target_pairs={{0,2},{1,3},{2,0},{3,1},{4,6},{5,7},{6,4},{7,5},{8,10},{9,11},{10,... | collective-permute-start | bytes 552968 | tf_op jit(solution)/shard_map/ppermute | solution.py:288
  45.3 2.2 %collective-permute-done.20 = bf16[2,360,128]{2,1,0:T(8,128)(2,1)S(1)} collective-permute-done((bf16[2,360,128]{2,1,0:T(8,128)(2,1)S(1)}, bf16[2,360,128]{2,1,0:T(8,128)(2,1)S(1)}, u32[]{:S(2)}, u32[]{:S(2)}) %collective-permute-start.20) | collective-permute-done | bytes 184352 | tf_op jit(solution)/shard_map/ppermute | solution.py:288
  47.5 1.7 %collective-permute-start.24 = (bf16[2,360,128]{2,1,0:T(8,128)(2,1)S(1)}, bf16[2,360,128]{2,1,0:T(8,128)(2,1)S(1)}, u32[]{:S(2)}, u32[]{:S(2)}) collective-permute-start(bf16[2,360,128]{2,1,0:T(8,128)(2,1)S(1)} %pad_maximum_fusion.6), channel_id=1, source_target_pairs={{0,6},{1,7},{2,4},{3,5},{4,2},{5,3},{6,0},{7,1},{8,14},{9,15},{10,... | collective-permute-start | bytes 552968 | tf_op jit(solution)/shard_map/ppermute | solution.py:288
  49.2 1.8 %collective-permute-done.19 = bf16[2,360,128]{2,1,0:T(8,128)(2,1)S(1)} collective-permute-done((bf16[2,360,128]{2,1,0:T(8,128)(2,1)S(1)}, bf16[2,360,128]{2,1,0:T(8,128)(2,1)S(1)}, u32[]{:S(2)}, u32[]{:S(2)}) %collective-permute-start.19) | collective-permute-done | bytes 184352 | tf_op jit(solution)/shard_map/ppermute | solution.py:288
  51.0 0.6 collective-permute-done.18
  51.5 0.1 fusion.3
  51.7 3.1 %collective-permute-start.27 = (bf16[360,128]{1,0:T(8,128)(2,1)S(1)}, bf16[360,128]{1,0:T(8,128)(2,1)S(1)}, u32[]{:S(2)}, u32[]{:S(2)}) collective-permute-start(bf16[360,128]{1,0:T(8,128)(2,1)S(1)} %get-tuple-element.128), channel_id=1, source_target_pairs={{0,24},{1,25},{2,26},{3,27},{4,28},{5,29},{6,30},{7,31},{8,16},{9,... | collective-permute-start | bytes 276488 | tf_op jit(solution)/shard_map/ppermute | solution.py:288
  54.7 1.2 %collective-permute-start.26 = (bf16[360,128]{1,0:T(8,128)(2,1)S(1)}, bf16[360,128]{1,0:T(8,128)(2,1)S(1)}, u32[]{:S(2)}, u32[]{:S(2)}) collective-permute-start(bf16[360,128]{1,0:T(8,128)(2,1)S(1)} %get-tuple-element.127), channel_id=1, source_target_pairs={{0,16},{1,17},{2,18},{3,19},{4,20},{5,21},{6,22},{7,23},{8,24},{9,... | collective-permute-start | bytes 276488 | tf_op jit(solution)/shard_map/ppermute | solution.py:288
  55.9 2.9 %collective-permute-done.24 = bf16[2,360,128]{2,1,0:T(8,128)(2,1)S(1)} collective-permute-done((bf16[2,360,128]{2,1,0:T(8,128)(2,1)S(1)}, bf16[2,360,128]{2,1,0:T(8,128)(2,1)S(1)}, u32[]{:S(2)}, u32[]{:S(2)}) %collective-permute-start.24) | collective-permute-done | bytes 184352 | tf_op jit(solution)/shard_map/ppermute | solution.py:288
  58.9 2.9 %collective-permute-start.25 = (bf16[360,128]{1,0:T(8,128)(2,1)S(1)}, bf16[360,128]{1,0:T(8,128)(2,1)S(1)}, u32[]{:S(2)}, u32[]{:S(2)}) collective-permute-start(bf16[360,128]{1,0:T(8,128)(2,1)S(1)} %fusion.5), channel_id=1, source_target_pairs={{0,8},{1,9},{2,10},{3,11},{4,12},{5,13},{6,14},{7,15},{8,0},{9,1},... | collective-permute-start | bytes 276488 | tf_op jit(solution)/shard_map/ppermute | solution.py:288
  61.8 1.8 %collective-permute-done.26 = bf16[360,128]{1,0:T(8,128)(2,1)S(1)} collective-permute-done((bf16[360,128]{1,0:T(8,128)(2,1)S(1)}, bf16[360,128]{1,0:T(8,128)(2,1)S(1)}, u32[]{:S(2)}, u32[]{:S(2)}) %collective-permute-start.26) | collective-permute-done | bytes 92192 | tf_op jit(solution)/shard_map/ppermute | solution.py:288
  63.6 1.9 %collective-permute-done.25 = bf16[360,128]{1,0:T(8,128)(2,1)S(1)} collective-permute-done((bf16[360,128]{1,0:T(8,128)(2,1)S(1)}, bf16[360,128]{1,0:T(8,128)(2,1)S(1)}, u32[]{:S(2)}, u32[]{:S(2)}) %collective-permute-start.25) | collective-permute-done | bytes 92192 | tf_op jit(solution)/shard_map/ppermute | solution.py:288
  65.5 0.7 %fusion.6 = bf16[128,360]{0,1:T(8,128)(2,1)} fusion(bf16[360,128]{1,0:T(8,128)(2,1)S(1)} %collective-permute-done.27, bf16[360,128]{1,0:T(8,128)(2,1)S(1)} %collective-permute-done.26, bf16[360,128]{1,0:T(8,128)(2,1)S(1)} %collective-permute-done.25, bf16[2,360,128]{2,1,0:T(8,128)(2,1)S(1)} %collective-permute-done.24, ...), kind=kLoop, calls=%fused_computation.29 | loop fusion | flops 737280 | bytes 829440 | tf_op jit(solution)/shard_map/transpose | solution.py:373
  (40 shorter events, 0.6 us)
Async XLA Ops:
  0.0 12.4 %copy-start = (bf16[1,1440,360]{2,1,0:T(8,128)(2,1)S(1)}, bf16[1,1440,360]{2,1,0:T(8,128)(2,1)}, u32[]{:S(2)}) copy-start(bf16[1,1440,360]{2,1,0:T(8,128)(2,1)} %param.14) | copy-start | bytes 3110404
  2.3 9.4 %collective-permute-start.6 = (bf16[2,368,128]{2,1,0:T(8,128)(2,1)}, bf16[2,368,128]{2,1,0:T(8,128)(2,1)S(1)}, u32[]{:S(2)}, u32[]{:S(2)}) collective-permute-start(bf16[2,368,128]{2,1,0:T(8,128)(2,1)} %get-tuple-element.60.refs_0_), channel_id=1, source_target_pairs={{0,4},{1,5},{2,6},{3,7},{4,0},{5,1},{6,2},{7,3},{8,12},{9,13},{10,... | collective-permute-start | bytes 565256 | tf_op jit(solution)/shard_map/ppermute | solution.py:288
  5.3 9.9 %collective-permute-start.1 = (bf16[368,128]{1,0:T(8,128)(2,1)}, bf16[368,128]{1,0:T(8,128)(2,1)S(1)}, u32[]{:S(2)}, u32[]{:S(2)}) collective-permute-start(bf16[368,128]{1,0:T(8,128)(2,1)} %get-tuple-element.61), channel_id=1, source_target_pairs={{0,16},{1,17},{2,18},{3,19},{4,20},{5,21},{6,22},{7,23},{8,24},{9,... | collective-permute-start | bytes 282632 | tf_op jit(solution)/shard_map/ppermute | solution.py:288
  7.9 7.3 %collective-permute-start.2 = (bf16[368,128]{1,0:T(8,128)(2,1)}, bf16[368,128]{1,0:T(8,128)(2,1)S(1)}, u32[]{:S(2)}, u32[]{:S(2)}) collective-permute-start(bf16[368,128]{1,0:T(8,128)(2,1)} %get-tuple-element.61), channel_id=1, source_target_pairs={{0,24},{1,25},{2,26},{3,27},{4,28},{5,29},{6,30},{7,31},{8,16},{9,... | collective-permute-start | bytes 282632 | tf_op jit(solution)/shard_map/ppermute | solution.py:288
  10.0 1.2 %copy-start.2 = (bf16[1,360,1440]{2,1,0:T(8,128)(2,1)S(1)}, bf16[1,360,1440]{2,1,0:T(8,128)(2,1)}, u32[]{:S(2)}) copy-start(bf16[1,360,1440]{2,1,0:T(8,128)(2,1)} %param.18) | copy-start | bytes 3110404
  11.2 0.9 %copy-start.3 = (bf16[2,368,128]{2,1,0:T(8,128)(2,1)S(1)}, bf16[2,368,128]{2,1,0:T(8,128)(2,1)}, u32[]{:S(2)}) copy-start(bf16[2,368,128]{2,1,0:T(8,128)(2,1)} %get-tuple-element.60.refs_0_) | copy-start | bytes 565252
  11.7 7.1 %collective-permute-start.7 = (bf16[2,368,128]{2,1,0:T(8,128)(2,1)S(1)}, bf16[2,368,128]{2,1,0:T(8,128)(2,1)S(1)}, u32[]{:S(2)}, u32[]{:S(2)}) collective-permute-start(bf16[2,368,128]{2,1,0:T(8,128)(2,1)S(1)} %collective-permute-done.6.refs_2_), channel_id=1, source_target_pairs={{0,1},{1,0},{2,3},{3,2},{4,5},{5,4},{6,7},{7,6},{8,9},{9,8},{10,11... | collective-permute-start | bytes 565256 | tf_op jit(solution)/shard_map/ppermute | solution.py:288
  12.1 8.9 %collective-permute-start = (bf16[2,368,128]{2,1,0:T(8,128)(2,1)S(1)}, bf16[2,368,128]{2,1,0:T(8,128)(2,1)S(1)}, u32[]{:S(2)}, u32[]{:S(2)}) collective-permute-start(bf16[2,368,128]{2,1,0:T(8,128)(2,1)S(1)} %copy-done.3), channel_id=1, source_target_pairs={{0,8},{1,9},{2,10},{3,11},{4,12},{5,13},{6,14},{7,15},{8,0},{9,1},... | collective-permute-start | bytes 565256 | tf_op jit(solution)/shard_map/ppermute | solution.py:288
  12.4 1.2 %copy-start.1 = (bf16[1,1440,360]{2,1,0:T(8,128)(2,1)S(1)}, bf16[1,1440,360]{2,1,0:T(8,128)(2,1)}, u32[]{:S(2)}) copy-start(bf16[1,1440,360]{2,1,0:T(8,128)(2,1)} %param.16) | copy-start | bytes 3110404
  13.6 5.2 %copy-start.4 = (bf16[2,368,128]{2,1,0:T(8,128)(2,1)S(1)}, bf16[2,368,128]{2,1,0:T(8,128)(2,1)}, u32[]{:S(2)}) copy-start(bf16[2,368,128]{2,1,0:T(8,128)(2,1)} %get-tuple-element.66.refs_1_) | copy-start | bytes 565252
  15.3 7.5 %collective-permute-start.3 = (bf16[2,368,128]{2,1,0:T(8,128)(2,1)S(1)}, bf16[2,368,128]{2,1,0:T(8,128)(2,1)S(1)}, u32[]{:S(2)}, u32[]{:S(2)}) collective-permute-start(bf16[2,368,128]{2,1,0:T(8,128)(2,1)S(1)} %pad_maximum_fusion.refs_0_), channel_id=1, source_target_pairs={{0,4},{1,5},{2,6},{3,7},{4,0},{5,1},{6,2},{7,3},{8,12},{9,13},{10,... | collective-permute-start | bytes 565256 | tf_op jit(solution)/shard_map/ppermute | solution.py:288
  15.8 10.5 %collective-permute-start.4 = (bf16[2,368,128]{2,1,0:T(8,128)(2,1)S(1)}, bf16[2,368,128]{2,1,0:T(8,128)(2,1)S(1)}, u32[]{:S(2)}, u32[]{:S(2)}) collective-permute-start(bf16[2,368,128]{2,1,0:T(8,128)(2,1)S(1)} %pad_maximum_fusion.refs_0_), channel_id=1, source_target_pairs={{0,2},{1,3},{2,0},{3,1},{4,6},{5,7},{6,4},{7,5},{8,10},{9,11},{10,... | collective-permute-start | bytes 565256 | tf_op jit(solution)/shard_map/ppermute | solution.py:288
  17.4 9.0 %collective-permute-start.5 = (bf16[2,368,128]{2,1,0:T(8,128)(2,1)S(1)}, bf16[2,368,128]{2,1,0:T(8,128)(2,1)S(1)}, u32[]{:S(2)}, u32[]{:S(2)}) collective-permute-start(bf16[2,368,128]{2,1,0:T(8,128)(2,1)S(1)} %pad_maximum_fusion.refs_0_), channel_id=1, source_target_pairs={{0,6},{1,7},{2,4},{3,5},{4,2},{5,3},{6,0},{7,1},{8,14},{9,15},{10,... | collective-permute-start | bytes 565256 | tf_op jit(solution)/shard_map/ppermute | solution.py:288
  18.8 8.5 %collective-permute-start.10 = (bf16[2,368,128]{2,1,0:T(8,128)(2,1)S(1)}, bf16[2,368,128]{2,1,0:T(8,128)(2,1)S(1)}, u32[]{:S(2)}, u32[]{:S(2)}) collective-permute-start(bf16[2,368,128]{2,1,0:T(8,128)(2,1)S(1)} %pad_maximum_fusion.refs_0_), channel_id=1, source_target_pairs={{0,1},{1,0},{2,3},{3,2},{4,5},{5,4},{6,7},{7,6},{8,9},{9,8},{10,11... | collective-permute-start | bytes 565256 | tf_op jit(solution)/shard_map/ppermute | solution.py:288
  26.3 3.2 %collective-permute-start.8 = (bf16[4,360,128]{2,1,0:T(8,128)(2,1)S(1)}, bf16[4,360,128]{2,1,0:T(8,128)(2,1)S(1)}, u32[]{:S(2)}, u32[]{:S(2)}) collective-permute-start(bf16[4,360,128]{2,1,0:T(8,128)(2,1)S(1)} %get-tuple-element.77), channel_id=1, source_target_pairs={{0,1},{1,0},{2,3},{3,2},{4,5},{5,4},{6,7},{7,6},{8,9},{9,8},{10,11... | collective-permute-start | bytes 1105928 | tf_op jit(solution)/shard_map/ppermute | solution.py:288
  26.3 2.0 %collective-permute-start.9 = (bf16[2,368,128]{2,1,0:T(8,128)(2,1)S(1)}, bf16[2,368,128]{2,1,0:T(8,128)(2,1)S(1)}, u32[]{:S(2)}, u32[]{:S(2)}) collective-permute-start(bf16[2,368,128]{2,1,0:T(8,128)(2,1)S(1)} %collective-permute-done.refs_0_), channel_id=1, source_target_pairs={{0,1},{1,0},{2,3},{3,2},{4,5},{5,4},{6,7},{7,6},{8,9},{9,8},{10,11... | collective-permute-start | bytes 565256 | tf_op jit(solution)/shard_map/ppermute | solution.py:288
  26.9 2.7 %collective-permute-start.11 = (bf16[2,368,128]{2,1,0:T(8,128)(2,1)S(1)}, bf16[2,368,128]{2,1,0:T(8,128)(2,1)S(1)}, u32[]{:S(2)}, u32[]{:S(2)}) collective-permute-start(bf16[2,368,128]{2,1,0:T(8,128)(2,1)S(1)} %collective-permute-done.4.refs_2_), channel_id=1, source_target_pairs={{0,1},{1,0},{2,3},{3,2},{4,5},{5,4},{6,7},{7,6},{8,9},{9,8},{10,11... | collective-permute-start | bytes 565256 | tf_op jit(solution)/shard_map/ppermute | solution.py:288
  26.9 2.7 %collective-permute-start.12 = (bf16[2,368,128]{2,1,0:T(8,128)(2,1)S(1)}, bf16[2,368,128]{2,1,0:T(8,128)(2,1)S(1)}, u32[]{:S(2)}, u32[]{:S(2)}) collective-permute-start(bf16[2,368,128]{2,1,0:T(8,128)(2,1)S(1)} %collective-permute-done.3.refs_4_), channel_id=1, source_target_pairs={{0,1},{1,0},{2,3},{3,2},{4,5},{5,4},{6,7},{7,6},{8,9},{9,8},{10,11... | collective-permute-start | bytes 565256 | tf_op jit(solution)/shard_map/ppermute | solution.py:288
  27.4 2.2 %collective-permute-start.13 = (bf16[2,368,128]{2,1,0:T(8,128)(2,1)S(1)}, bf16[2,368,128]{2,1,0:T(8,128)(2,1)S(1)}, u32[]{:S(2)}, u32[]{:S(2)}) collective-permute-start(bf16[2,368,128]{2,1,0:T(8,128)(2,1)S(1)} %collective-permute-done.5.refs_6_), channel_id=1, source_target_pairs={{0,1},{1,0},{2,3},{3,2},{4,5},{5,4},{6,7},{7,6},{8,9},{9,8},{10,11... | collective-permute-start | bytes 565256 | tf_op jit(solution)/shard_map/ppermute | solution.py:288
  28.3 6.8 %collective-permute-start.15 = (bf16[2,368,128]{2,1,0:T(8,128)(2,1)S(1)}, bf16[2,368,128]{2,1,0:T(8,128)(2,1)S(1)}, u32[]{:S(2)}, u32[]{:S(2)}) collective-permute-start(bf16[2,368,128]{2,1,0:T(8,128)(2,1)S(1)} %collective-permute-done.refs_0_), channel_id=1, source_target_pairs={{0,4},{1,5},{2,6},{3,7},{4,0},{5,1},{6,2},{7,3},{8,12},{9,13},{10,... | collective-permute-start | bytes 565256 | tf_op jit(solution)/shard_map/ppermute | solution.py:288
  31.8 3.3 %collective-permute-start.14 = (bf16[4,360,128]{2,1,0:T(8,128)(2,1)S(1)}, bf16[4,360,128]{2,1,0:T(8,128)(2,1)S(1)}, u32[]{:S(2)}, u32[]{:S(2)}) collective-permute-start(bf16[4,360,128]{2,1,0:T(8,128)(2,1)S(1)} %get-tuple-element.93), channel_id=1, source_target_pairs={{0,1},{1,0},{2,3},{3,2},{4,5},{5,4},{6,7},{7,6},{8,9},{9,8},{10,11... | collective-permute-start | bytes 1105928 | tf_op jit(solution)/shard_map/ppermute | solution.py:288
  34.1 4.7 %collective-permute-start.17 = (bf16[4,360,128]{2,1,0:T(8,128)(2,1)S(1)}, bf16[4,360,128]{2,1,0:T(8,128)(2,1)S(1)}, u32[]{:S(2)}, u32[]{:S(2)}) collective-permute-start(bf16[4,360,128]{2,1,0:T(8,128)(2,1)S(1)} %get-tuple-element.108), channel_id=1, source_target_pairs={{0,1},{1,0},{2,3},{3,2},{4,5},{5,4},{6,7},{7,6},{8,9},{9,8},{10,11... | collective-permute-start | bytes 1105928 | tf_op jit(solution)/shard_map/ppermute | solution.py:288
  35.1 1.4 %collective-permute-start.16 = (bf16[2,368,128]{2,1,0:T(8,128)(2,1)S(1)}, bf16[2,368,128]{2,1,0:T(8,128)(2,1)S(1)}, u32[]{:S(2)}, u32[]{:S(2)}) collective-permute-start(bf16[2,368,128]{2,1,0:T(8,128)(2,1)S(1)} %collective-permute-done.15.refs_2_), channel_id=1, source_target_pairs={{0,1},{1,0},{2,3},{3,2},{4,5},{5,4},{6,7},{7,6},{8,9},{9,8},{10,11... | collective-permute-start | bytes 565256 | tf_op jit(solution)/shard_map/ppermute | solution.py:288
  38.7 4.1 %collective-permute-start.21 = (bf16[4,360,128]{2,1,0:T(8,128)(2,1)S(1)}, bf16[4,360,128]{2,1,0:T(8,128)(2,1)S(1)}, u32[]{:S(2)}, u32[]{:S(2)}) collective-permute-start(bf16[4,360,128]{2,1,0:T(8,128)(2,1)S(1)} %get-tuple-element.111), channel_id=1, source_target_pairs={{0,1},{1,0},{2,3},{3,2},{4,5},{5,4},{6,7},{7,6},{8,9},{9,8},{10,11... | collective-permute-start | bytes 1105928 | tf_op jit(solution)/shard_map/ppermute | solution.py:288
  39.0 8.5 %collective-permute-start.20 = (bf16[2,360,128]{2,1,0:T(8,128)(2,1)S(1)}, bf16[2,360,128]{2,1,0:T(8,128)(2,1)S(1)}, u32[]{:S(2)}, u32[]{:S(2)}) collective-permute-start(bf16[2,360,128]{2,1,0:T(8,128)(2,1)S(1)} %pad_maximum_fusion.3), channel_id=1, source_target_pairs={{0,6},{1,7},{2,4},{3,5},{4,2},{5,3},{6,0},{7,1},{8,14},{9,15},{10,... | collective-permute-start | bytes 552968 | tf_op jit(solution)/shard_map/ppermute | solution.py:288
  40.8 10.2 %collective-permute-start.19 = (bf16[2,360,128]{2,1,0:T(8,128)(2,1)S(1)}, bf16[2,360,128]{2,1,0:T(8,128)(2,1)S(1)}, u32[]{:S(2)}, u32[]{:S(2)}) collective-permute-start(bf16[2,360,128]{2,1,0:T(8,128)(2,1)S(1)} %pad_maximum_fusion.2), channel_id=1, source_target_pairs={{0,2},{1,3},{2,0},{3,1},{4,6},{5,7},{6,4},{7,5},{8,10},{9,11},{10,... | collective-permute-start | bytes 552968 | tf_op jit(solution)/shard_map/ppermute | solution.py:288
  41.9 9.6 %collective-permute-start.18 = (bf16[2,360,128]{2,1,0:T(8,128)(2,1)S(1)}, bf16[2,360,128]{2,1,0:T(8,128)(2,1)S(1)}, u32[]{:S(2)}, u32[]{:S(2)}) collective-permute-start(bf16[2,360,128]{2,1,0:T(8,128)(2,1)S(1)} %pad_maximum_fusion.1), channel_id=1, source_target_pairs={{0,4},{1,5},{2,6},{3,7},{4,0},{5,1},{6,2},{7,3},{8,12},{9,13},{10,... | collective-permute-start | bytes 552968 | tf_op jit(solution)/shard_map/ppermute | solution.py:288
  42.9 13.0 %collective-permute-start.22 = (bf16[2,360,128]{2,1,0:T(8,128)(2,1)S(1)}, bf16[2,360,128]{2,1,0:T(8,128)(2,1)S(1)}, u32[]{:S(2)}, u32[]{:S(2)}) collective-permute-start(bf16[2,360,128]{2,1,0:T(8,128)(2,1)S(1)} %pad_maximum_fusion.4), channel_id=1, source_target_pairs={{0,4},{1,5},{2,6},{3,7},{4,0},{5,1},{6,2},{7,3},{8,12},{9,13},{10,... | collective-permute-start | bytes 552968 | tf_op jit(solution)/shard_map/ppermute | solution.py:288
  44.2 11.7 %collective-permute-start.23 = (bf16[2,360,128]{2,1,0:T(8,128)(2,1)S(1)}, bf16[2,360,128]{2,1,0:T(8,128)(2,1)S(1)}, u32[]{:S(2)}, u32[]{:S(2)}) collective-permute-start(bf16[2,360,128]{2,1,0:T(8,128)(2,1)S(1)} %pad_maximum_fusion.5), channel_id=1, source_target_pairs={{0,2},{1,3},{2,0},{3,1},{4,6},{5,7},{6,4},{7,5},{8,10},{9,11},{10,... | collective-permute-start | bytes 552968 | tf_op jit(solution)/shard_map/ppermute | solution.py:288
  47.5 11.3 %collective-permute-start.24 = (bf16[2,360,128]{2,1,0:T(8,128)(2,1)S(1)}, bf16[2,360,128]{2,1,0:T(8,128)(2,1)S(1)}, u32[]{:S(2)}, u32[]{:S(2)}) collective-permute-start(bf16[2,360,128]{2,1,0:T(8,128)(2,1)S(1)} %pad_maximum_fusion.6), channel_id=1, source_target_pairs={{0,6},{1,7},{2,4},{3,5},{4,2},{5,3},{6,0},{7,1},{8,14},{9,15},{10,... | collective-permute-start | bytes 552968 | tf_op jit(solution)/shard_map/ppermute | solution.py:288
  51.7 10.1 %collective-permute-start.27 = (bf16[360,128]{1,0:T(8,128)(2,1)S(1)}, bf16[360,128]{1,0:T(8,128)(2,1)S(1)}, u32[]{:S(2)}, u32[]{:S(2)}) collective-permute-start(bf16[360,128]{1,0:T(8,128)(2,1)S(1)} %get-tuple-element.128), channel_id=1, source_target_pairs={{0,24},{1,25},{2,26},{3,27},{4,28},{5,29},{6,30},{7,31},{8,16},{9,... | collective-permute-start | bytes 276488 | tf_op jit(solution)/shard_map/ppermute | solution.py:288
  54.7 8.9 %collective-permute-start.26 = (bf16[360,128]{1,0:T(8,128)(2,1)S(1)}, bf16[360,128]{1,0:T(8,128)(2,1)S(1)}, u32[]{:S(2)}, u32[]{:S(2)}) collective-permute-start(bf16[360,128]{1,0:T(8,128)(2,1)S(1)} %get-tuple-element.127), channel_id=1, source_target_pairs={{0,16},{1,17},{2,18},{3,19},{4,20},{5,21},{6,22},{7,23},{8,24},{9,... | collective-permute-start | bytes 276488 | tf_op jit(solution)/shard_map/ppermute | solution.py:288
  58.9 6.6 %collective-permute-start.25 = (bf16[360,128]{1,0:T(8,128)(2,1)S(1)}, bf16[360,128]{1,0:T(8,128)(2,1)S(1)}, u32[]{:S(2)}, u32[]{:S(2)}) collective-permute-start(bf16[360,128]{1,0:T(8,128)(2,1)S(1)} %fusion.5), channel_id=1, source_target_pairs={{0,8},{1,9},{2,10},{3,11},{4,12},{5,13},{6,14},{7,15},{8,0},{9,1},... | collective-permute-start | bytes 276488 | tf_op jit(solution)/shard_map/ppermute | solution.py:288

commit v7 on v6

--- a/solution.py
+++ b/solution.py
@@ -292,7 +292,6 @@
         tokens.T, norm_gain, expert_ids.T, route_weights.T, groups, per, experts
     )
     z_2, z_3 = swap(one, 2 * along_z), swap(one, 3 * along_z)
-    x_0 = swap(near, along_x)
     z_1 = swap(near, along_z)
     hidden_pad = round_up(gate_weight.shape[2], 128)
     wide = groups * round_up(quarter, 128)
@@ -305,11 +304,12 @@
         (2 * hidden_pad, wide),
         2 * hidden_pad,
     )
-    z_2, z_3, inward = tied((z_2, z_3, inward))
+    x_0 = swap(tied((near, inward))[0], along_x)
+    z_1, z_2, z_3, inward = tied((z_1, z_2, z_3, inward))
     z_high = jnp.stack([z_2, z_3])
     diagonal = along_x + along_y
-    x_high, y_high = swap(z_high, along_x), swap(z_high, along_y)
-    d_high = swap(z_high, diagonal)
+    x_all = swap(jnp.concatenate([z_1, z_high], axis=0), along_x)
+    d_high, y_high = swap(z_high, diagonal), swap(z_high, along_y)
     outward = arrange(
         outward_kernel,
         groups,
@@ -318,7 +318,6 @@
         (wide, hidden_pad),
         wide // groups,
     )
-    x_0, outward = tied((x_0, outward))
     weights = (*inward, *outward)
 
     def pairs(first, step):
@@ -329,27 +328,27 @@
     keep_0, send_0 = run_expert(
         (near, far, x_0, swap(x_0, core)), pairs(0, 2), slots, weights, sizes, 1
     )
-    z_1, x_high, y_high, d_high, keep_0, send_0 = tied(
-        (z_1, x_high, y_high, d_high, keep_0, send_0)
-    )
-    x_1 = swap(z_1, along_x)
+    x_all, y_high, d_high, keep_0, send_0 = tied((x_all, y_high, d_high, keep_0, send_0))
     got_0 = swap(send_0, core)
+    x_core = swap(x_all, core)
     high = (z_high, swap(z_high, core), y_high, swap(y_high, core))
-    high = high + (x_high, swap(x_high, core), d_high, swap(d_high, core))
-    z_1_core = swap(z_1, core)
-    got_0, z_1_core, high = tied((got_0, z_1_core, high))
-    line = [[[(4 * x + k, n) for k in range(groups)] for x in range(2)] for n in range(2)]
+    high = high + (x_all, x_core, d_high, swap(d_high, core))
+    near_1 = (z_1, swap(z_1, core), x_all, x_core)
+    line = [
+        [[(4 * x + k, n + 2 * (x > k // 2)) for k in range(groups)] for x in range(2)]
+        for n in range(2)
+    ]
     keep_2, send_2 = run_expert(high, line[0], slots, weights, sizes, 1)
     got_2 = swap(send_2, core)
     keep_2, high = tied((keep_2, high))
     keep_3, send_3 = run_expert(high, line[1], slots, weights, sizes, 1)
-    got_2, keep_3, x_1 = tied((got_2, keep_3, x_1))
+    got_2, keep_3, got_0 = tied((got_2, keep_3, got_0))
     got_3 = swap(send_3, core)
-
-    near_1 = (z_1, z_1_core, x_1, swap(x_1, core))
+    near_1, got_2 = tied((near_1, got_2))
     keep_1, send_1 = run_expert(near_1, pairs(0, 2), slots, weights, sizes, 1)
     got_1 = swap(send_1, core)
-    keep_1, got_3 = tied((keep_1, got_3))
+    got_3, keep_1, got_0 = tied((got_3, keep_1, got_0))
+
     def outer(first, second, at):
         return jnp.stack([add_up(keep[at], got[at]) for keep, got in (first, second)])
 

time: 66.5 us -> 69.8 us (1.050)
  waiting for transfers between devices: 19.9 us -> 26.3 us
  starting transfers between devices: 28.7 us -> 26 us
    ppermute x28 -> x26, waiting for transfers between devices: 19.9 us -> 26.3 us  [swap(): lax.ppermute(array, ('seq', 'rep'), [(i, i ^ step) for i in range(devices)])]
    ppermute x28 -> x26, starting transfers between devices: 28.7 us -> 26 us  [swap(): lax.ppermute(array, ('seq', 'rep'), [(i, i ^ step) for i in range(devices)])]
  transfers between devices with their start and end apart: 28 -> 26, of which waited for: 12 -> 12; matrix products, arithmetic and copies ran while one was open for 2% -> 2% of each run, Pallas kernels for 15% -> 14%
where the time goes in v7:
time: 69.8 us; the launch traced here: 69.5 us
  waiting for transfers between devices  26.3 us (38%)
  starting transfers between devices  26 us (37%)
  Pallas kernels  12.2 us (17%)
  local copies, waits for them, and re-layouts  2.62 us (4%)
  other arithmetic  2.19 us (3%)
    ppermute x26, waiting for transfers between devices, swap(): lax.ppermute(array, ('seq', 'rep'), [(i, i ^ step) for i in range(devices)])  26.3 us
    ppermute x26, starting transfers between devices, swap(): lax.ppermute(array, ('seq', 'rep'), [(i, i ^ step) for i in range(devices)])  26 us
    pallas_call x4, Pallas kernels, run_expert(): pl.pallas_call(functools.partial(expert_kernel, quarter, per, blocks, slo...  8.79 us
    unnamed x10, local copies, waits for them, and re-layouts  2.62 us
    pallas_call x1, Pallas kernels, make_pieces(): pl.pallas_call(functools.partial(pieces_kernel, groups, per, experts), in...  2.22 us
  transfers between devices with their start and end apart: 26, of which 12 were waited for; matrix products, arithmetic and copies ran while one was open for 2% of the time, Pallas kernels for 14%

profile of v7, /device:TPU:0, one launch (start us, length us, event | category | flops | bytes accessed | tf_op | source)
XLA Modules:
  0.0 69.5 jit_solution(7684060428615780732)
XLA Ops:
  0.0 2.2 %shard_map.100 = (bf16[368,128]{1,0:T(8,128)(2,1)}, bf16[2,368,128]{2,1,0:T(8,128)(2,1)}, bf16[2,368,128]{2,1,0:T(8,128)(2,1)}) custom-call(bf16[1440,128]{1,0:T(8,128)(2,1)} %bitcast.33, f32[1440]{0:T(1024)} %refs_1_.1, s32[4,128]{1,0:T(4,128)} %bitcast.34, f32[4,128]{1,0:T(4,128)} %bitcast.35), custom_call_target="tpu_custom_call" | custom-call | tf_op jit(solution)/shard_map/pallas_call | solution.py:188
  2.2 3.1 %collective-permute-start = (bf16[2,368,128]{2,1,0:T(8,128)(2,1)}, bf16[2,368,128]{2,1,0:T(8,128)(2,1)S(1)}, u32[]{:S(2)}, u32[]{:S(2)}) collective-permute-start(bf16[2,368,128]{2,1,0:T(8,128)(2,1)} %get-tuple-element.62.refs_0_), channel_id=1, source_target_pairs={{0,8},{1,9},{2,10},{3,11},{4,12},{5,13},{6,14},{7,15},{8,0},{9,1},... | collective-permute-start | bytes 565256 | tf_op jit(solution)/shard_map/ppermute | solution.py:288
  5.3 2.6 %collective-permute-start.1 = (bf16[368,128]{1,0:T(8,128)(2,1)}, bf16[368,128]{1,0:T(8,128)(2,1)S(1)}, u32[]{:S(2)}, u32[]{:S(2)}) collective-permute-start(bf16[368,128]{1,0:T(8,128)(2,1)} %get-tuple-element.55), channel_id=1, source_target_pairs={{0,16},{1,17},{2,18},{3,19},{4,20},{5,21},{6,22},{7,23},{8,24},{9,... | collective-permute-start | bytes 282632 | tf_op jit(solution)/shard_map/ppermute | solution.py:288
  7.9 0.7 %pad_maximum_fusion.8.biases_ref = f32[3,360]{1,0:T(4,128)S(1)} fusion(f32[1,360]{1,0:T(1,128)} %param.19, f32[1,360]{1,0:T(1,128)} %param.17, f32[1,360]{1,0:T(1,128)} %param.15), kind=kLoop, calls=%fused_computation.31 | loop fusion | flops 2160 | bytes 8640 | tf_op jit(solution)/shard_map/concatenate | solution.py:298
  8.6 1.2 %copy-done = bf16[1,1440,360]{2,1,0:T(8,128)(2,1)S(1)} copy-done((bf16[1,1440,360]{2,1,0:T(8,128)(2,1)S(1)}, bf16[1,1440,360]{2,1,0:T(8,128)(2,1)}, u32[]{:S(2)}) %copy-start) | copy-done | bytes 1036824
  9.9 1.2 %copy-done.1 = bf16[1,1440,360]{2,1,0:T(8,128)(2,1)S(1)} copy-done((bf16[1,1440,360]{2,1,0:T(8,128)(2,1)S(1)}, bf16[1,1440,360]{2,1,0:T(8,128)(2,1)}, u32[]{:S(2)}) %copy-start.1) | copy-done | bytes 1036824
  11.1 0.8 %shard_map.101 = (bf16[768,1536]{1,0:T(8,128)(2,1)S(1)}, f32[768,128]{1,0:T(8,128)S(1)}) custom-call(bf16[1440,360]{1,0:T(8,128)(2,1)S(1)} %bitcast.26, bf16[1440,360]{1,0:T(8,128)(2,1)S(1)} %bitcast.27, f32[3,360]{1,0:T(4,128)S(1)} %pad_maximum_fusion.8.biases_ref), custom_call_target="tpu_custom_call" | custom-call | bytes 8294400 | tf_op jit(solution)/shard_map/pallas_call | solution.py:116
  11.9 0.1 copy-done.3
  12.1 1.7 %collective-permute-start.6 = (bf16[2,368,128]{2,1,0:T(8,128)(2,1)S(1)}, bf16[2,368,128]{2,1,0:T(8,128)(2,1)S(1)}, u32[]{:S(2)}, u32[]{:S(2)}) collective-permute-start(bf16[2,368,128]{2,1,0:T(8,128)(2,1)S(1)} %copy-done.3), channel_id=1, source_target_pairs={{0,4},{1,5},{2,6},{3,7},{4,0},{5,1},{6,2},{7,3},{8,12},{9,13},{10,... | collective-permute-start | bytes 565256 | tf_op jit(solution)/shard_map/ppermute | solution.py:288
  13.8 2.8 %collective-permute-done.2 = bf16[368,128]{1,0:T(8,128)(2,1)S(1)} collective-permute-done((bf16[368,128]{1,0:T(8,128)(2,1)}, bf16[368,128]{1,0:T(8,128)(2,1)S(1)}, u32[]{:S(2)}, u32[]{:S(2)}) %collective-permute-start.2) | collective-permute-done | bytes 94240 | tf_op jit(solution)/shard_map/ppermute | solution.py:288
  16.6 1.6 %collective-permute-start.3 = (bf16[4,368,128]{2,1,0:T(8,128)(2,1)S(1)}, bf16[4,368,128]{2,1,0:T(8,128)(2,1)S(1)}, u32[]{:S(2)}, u32[]{:S(2)}) collective-permute-start(bf16[4,368,128]{2,1,0:T(8,128)(2,1)S(1)} %pad_maximum_fusion), channel_id=1, source_target_pairs={{0,4},{1,5},{2,6},{3,7},{4,0},{5,1},{6,2},{7,3},{8,12},{9,13},{10,... | collective-permute-start | bytes 1130504 | tf_op jit(solution)/shard_map/ppermute | solution.py:288
  18.2 1.6 %collective-permute-start.4 = (bf16[2,368,128]{2,1,0:T(8,128)(2,1)S(1)}, bf16[2,368,128]{2,1,0:T(8,128)(2,1)S(1)}, u32[]{:S(2)}, u32[]{:S(2)}) collective-permute-start(bf16[2,368,128]{2,1,0:T(8,128)(2,1)S(1)} %pad_maximum_fusion.1.refs_0_), channel_id=1, source_target_pairs={{0,2},{1,3},{2,0},{3,1},{4,6},{5,7},{6,4},{7,5},{8,10},{9,11},{10,... | collective-permute-start | bytes 565256 | tf_op jit(solution)/shard_map/ppermute | solution.py:288
  19.8 1.2 %collective-permute-start.5 = (bf16[2,368,128]{2,1,0:T(8,128)(2,1)S(1)}, bf16[2,368,128]{2,1,0:T(8,128)(2,1)S(1)}, u32[]{:S(2)}, u32[]{:S(2)}) collective-permute-start(bf16[2,368,128]{2,1,0:T(8,128)(2,1)S(1)} %pad_maximum_fusion.1.refs_0_), channel_id=1, source_target_pairs={{0,6},{1,7},{2,4},{3,5},{4,2},{5,3},{6,0},{7,1},{8,14},{9,15},{10,... | collective-permute-start | bytes 565256 | tf_op jit(solution)/shard_map/ppermute | solution.py:288
  21.0 0.4 shard_map.102
  21.5 2.2 %shard_map.103 = (bf16[4,360,128]{2,1,0:T(8,128)(2,1)S(1)}, bf16[4,360,128]{2,1,0:T(8,128)(2,1)S(1)}) custom-call(bf16[2,368,128]{2,1,0:T(8,128)(2,1)S(1)} %copy-done.3, bf16[2,368,128]{2,1,0:T(8,128)(2,1)S(1)} %copy-done.4, bf16[2,368,128]{2,1,0:T(8,128)(2,1)S(1)} %collective-permute-done.6.refs_2_, ...), custom_call_target="tpu_custom_call" | custom-call | flops 1811939328 | bytes 3538944 | tf_op jit(solution)/shard_map/pallas_call | solution.py:253
  23.7 2.6 %collective-permute-done.4.refs_2_ = bf16[2,368,128]{2,1,0:T(8,128)(2,1)S(1)} collective-permute-done((bf16[2,368,128]{2,1,0:T(8,128)(2,1)S(1)}, bf16[2,368,128]{2,1,0:T(8,128)(2,1)S(1)}, u32[]{:S(2)}, u32[]{:S(2)}) %collective-permute-start.4) | collective-permute-done | bytes 188448 | tf_op jit(solution)/shard_map/ppermute | solution.py:288
  26.2 4.8 %collective-permute-done.5.refs_6_ = bf16[2,368,128]{2,1,0:T(8,128)(2,1)S(1)} collective-permute-done((bf16[2,368,128]{2,1,0:T(8,128)(2,1)S(1)}, bf16[2,368,128]{2,1,0:T(8,128)(2,1)S(1)}, u32[]{:S(2)}, u32[]{:S(2)}) %collective-permute-start.5) | collective-permute-done | bytes 188448 | tf_op jit(solution)/shard_map/ppermute | solution.py:288
  31.0 0.5 collective-permute-start.8
  31.5 0.5 collective-permute-start.9
  32.1 0.9 %collective-permute-done.8.refs_1_ = bf16[2,368,128]{2,1,0:T(8,128)(2,1)S(1)} collective-permute-done((bf16[2,368,128]{2,1,0:T(8,128)(2,1)S(1)}, bf16[2,368,128]{2,1,0:T(8,128)(2,1)S(1)}, u32[]{:S(2)}, u32[]{:S(2)}) %collective-permute-start.8) | collective-permute-done | bytes 188448 | tf_op jit(solution)/shard_map/ppermute | solution.py:288
  33.0 0.3 collective-permute-done.11.refs_7_
  33.3 0.3 collective-permute-done.9.refs_3_
  33.5 2.2 %shard_map.104 = (bf16[4,360,128]{2,1,0:T(8,128)(2,1)S(1)}, bf16[4,360,128]{2,1,0:T(8,128)(2,1)S(1)}) custom-call(bf16[2,368,128]{2,1,0:T(8,128)(2,1)S(1)} %pad_maximum_fusion.1.refs_0_, bf16[2,368,128]{2,1,0:T(8,128)(2,1)S(1)} %collective-permute-done.8.refs_1_, bf16[2,368,128]{2,1,0:T(8,128)(2,1)S(1)} %collective-permute-done.4.refs_2_, ...), custom_call_target="tpu_custom_call" | custom-call | flops 1811939328 | bytes 3538944 | tf_op jit(solution)/shard_map/pallas_call | solution.py:253
  35.7 0.2 collective-permute-start.14
  36.0 2.2 %shard_map.105 = (bf16[4,360,128]{2,1,0:T(8,128)(2,1)S(1)}, bf16[4,360,128]{2,1,0:T(8,128)(2,1)S(1)}) custom-call(bf16[2,368,128]{2,1,0:T(8,128)(2,1)S(1)} %pad_maximum_fusion.1.refs_0_, bf16[2,368,128]{2,1,0:T(8,128)(2,1)S(1)} %collective-permute-done.8.refs_1_, bf16[2,368,128]{2,1,0:T(8,128)(2,1)S(1)} %collective-permute-done.4.refs_2_, ...), custom_call_target="tpu_custom_call" | custom-call | flops 1811939328 | bytes 3538944 | tf_op jit(solution)/shard_map/pallas_call | solution.py:253
  38.2 0.4 collective-permute-start.12
  38.6 0.1 collective-permute-start.13
  38.7 1.4 %collective-permute-done.13.refs_1_ = bf16[2,368,128]{2,1,0:T(8,128)(2,1)S(1)} collective-permute-done((bf16[2,368,128]{2,1,0:T(8,128)(2,1)S(1)}, bf16[2,368,128]{2,1,0:T(8,128)(2,1)S(1)}, u32[]{:S(2)}, u32[]{:S(2)}) %collective-permute-start.13) | collective-permute-done | bytes 188448 | tf_op jit(solution)/shard_map/ppermute | solution.py:288
  40.2 2.2 %shard_map.106 = (bf16[4,360,128]{2,1,0:T(8,128)(2,1)S(1)}, bf16[4,360,128]{2,1,0:T(8,128)(2,1)S(1)}) custom-call(bf16[2,368,128]{2,1,0:T(8,128)(2,1)S(1)} %collective-permute-done.refs_0_, bf16[2,368,128]{2,1,0:T(8,128)(2,1)S(1)} %collective-permute-done.13.refs_1_, bf16[4,368,128]{2,1,0:T(8,128)(2,1)S(1)} %collective-permute-done.3.refs_4_.refs_2_, ...), custom_call_target="tpu_custom_call" | custom-call | flops 1811939328 | bytes 3538944 | tf_op jit(solution)/shard_map/pallas_call | solution.py:253
  42.4 0.4 collective-permute-start.19
  43.0 1.6 %collective-permute-start.16 = (bf16[2,360,128]{2,1,0:T(8,128)(2,1)S(1)}, bf16[2,360,128]{2,1,0:T(8,128)(2,1)S(1)}, u32[]{:S(2)}, u32[]{:S(2)}) collective-permute-start(bf16[2,360,128]{2,1,0:T(8,128)(2,1)S(1)} %pad_maximum_fusion.2), channel_id=1, source_target_pairs={{0,4},{1,5},{2,6},{3,7},{4,0},{5,1},{6,2},{7,3},{8,12},{9,13},{10,... | collective-permute-start | bytes 552968 | tf_op jit(solution)/shard_map/ppermute | solution.py:288
  44.6 0.6 collective-permute-start.17
  45.2 1.5 %collective-permute-start.18 = (bf16[2,360,128]{2,1,0:T(8,128)(2,1)S(1)}, bf16[2,360,128]{2,1,0:T(8,128)(2,1)S(1)}, u32[]{:S(2)}, u32[]{:S(2)}) collective-permute-start(bf16[2,360,128]{2,1,0:T(8,128)(2,1)S(1)} %pad_maximum_fusion.4), channel_id=1, source_target_pairs={{0,6},{1,7},{2,4},{3,5},{4,2},{5,3},{6,0},{7,1},{8,14},{9,15},{10,... | collective-permute-start | bytes 552968 | tf_op jit(solution)/shard_map/ppermute | solution.py:288
  46.8 0.1 add_convert_fusion.4
  46.9 0.1 add_convert_fusion.3
  47.0 1.5 %collective-permute-start.22 = (bf16[2,360,128]{2,1,0:T(8,128)(2,1)S(1)}, bf16[2,360,128]{2,1,0:T(8,128)(2,1)S(1)}, u32[]{:S(2)}, u32[]{:S(2)}) collective-permute-start(bf16[2,360,128]{2,1,0:T(8,128)(2,1)S(1)} %pad_maximum_fusion.7), channel_id=1, source_target_pairs={{0,6},{1,7},{2,4},{3,5},{4,2},{5,3},{6,0},{7,1},{8,14},{9,15},{10,... | collective-permute-start | bytes 552968 | tf_op jit(solution)/shard_map/ppermute | solution.py:288
  48.5 1.6 %collective-permute-start.21 = (bf16[2,360,128]{2,1,0:T(8,128)(2,1)S(1)}, bf16[2,360,128]{2,1,0:T(8,128)(2,1)S(1)}, u32[]{:S(2)}, u32[]{:S(2)}) collective-permute-start(bf16[2,360,128]{2,1,0:T(8,128)(2,1)S(1)} %pad_maximum_fusion.6), channel_id=1, source_target_pairs={{0,2},{1,3},{2,0},{3,1},{4,6},{5,7},{6,4},{7,5},{8,10},{9,11},{10,... | collective-permute-start | bytes 552968 | tf_op jit(solution)/shard_map/ppermute | solution.py:288
  50.1 0.5 collective-permute-done.16
  50.6 1.5 %collective-permute-start.20 = (bf16[2,360,128]{2,1,0:T(8,128)(2,1)S(1)}, bf16[2,360,128]{2,1,0:T(8,128)(2,1)S(1)}, u32[]{:S(2)}, u32[]{:S(2)}) collective-permute-start(bf16[2,360,128]{2,1,0:T(8,128)(2,1)S(1)} %pad_maximum_fusion.5), channel_id=1, source_target_pairs={{0,4},{1,5},{2,6},{3,7},{4,0},{5,1},{6,2},{7,3},{8,12},{9,13},{10,... | collective-permute-start | bytes 552968 | tf_op jit(solution)/shard_map/ppermute | solution.py:288
  52.1 8.0 %collective-permute-done.17 = bf16[2,360,128]{2,1,0:T(8,128)(2,1)S(1)} collective-permute-done((bf16[2,360,128]{2,1,0:T(8,128)(2,1)S(1)}, bf16[2,360,128]{2,1,0:T(8,128)(2,1)S(1)}, u32[]{:S(2)}, u32[]{:S(2)}) %collective-permute-start.17) | collective-permute-done | bytes 184352 | tf_op jit(solution)/shard_map/ppermute | solution.py:288
  60.1 0.1 fusion.3
  60.2 1.2 %collective-permute-start.24 = (bf16[360,128]{1,0:T(8,128)(2,1)S(1)}, bf16[360,128]{1,0:T(8,128)(2,1)S(1)}, u32[]{:S(2)}, u32[]{:S(2)}) collective-permute-start(bf16[360,128]{1,0:T(8,128)(2,1)S(1)} %get-tuple-element.115), channel_id=1, source_target_pairs={{0,16},{1,17},{2,18},{3,19},{4,20},{5,21},{6,22},{7,23},{8,24},{9,... | collective-permute-start | bytes 276488 | tf_op jit(solution)/shard_map/ppermute | solution.py:288
  61.4 2.0 %collective-permute-start.25 = (bf16[360,128]{1,0:T(8,128)(2,1)S(1)}, bf16[360,128]{1,0:T(8,128)(2,1)S(1)}, u32[]{:S(2)}, u32[]{:S(2)}) collective-permute-start(bf16[360,128]{1,0:T(8,128)(2,1)S(1)} %get-tuple-element.116), channel_id=1, source_target_pairs={{0,24},{1,25},{2,26},{3,27},{4,28},{5,29},{6,30},{7,31},{8,16},{9,... | collective-permute-start | bytes 276488 | tf_op jit(solution)/shard_map/ppermute | solution.py:288
  63.5 0.6 collective-permute-start.23
  64.1 2.7 %collective-permute-done.24 = bf16[360,128]{1,0:T(8,128)(2,1)S(1)} collective-permute-done((bf16[360,128]{1,0:T(8,128)(2,1)S(1)}, bf16[360,128]{1,0:T(8,128)(2,1)S(1)}, u32[]{:S(2)}, u32[]{:S(2)}) %collective-permute-start.24) | collective-permute-done | bytes 92192 | tf_op jit(solution)/shard_map/ppermute | solution.py:288
  66.7 1.5 %collective-permute-done.25 = bf16[360,128]{1,0:T(8,128)(2,1)S(1)} collective-permute-done((bf16[360,128]{1,0:T(8,128)(2,1)S(1)}, bf16[360,128]{1,0:T(8,128)(2,1)S(1)}, u32[]{:S(2)}, u32[]{:S(2)}) %collective-permute-start.25) | collective-permute-done | bytes 92192 | tf_op jit(solution)/shard_map/ppermute | solution.py:288
  68.3 0.5 collective-permute-done.23
  68.8 0.7 %fusion.6 = bf16[128,360]{0,1:T(8,128)(2,1)} fusion(bf16[360,128]{1,0:T(8,128)(2,1)S(1)} %collective-permute-done.25, bf16[360,128]{1,0:T(8,128)(2,1)S(1)} %collective-permute-done.24, bf16[360,128]{1,0:T(8,128)(2,1)S(1)} %collective-permute-done.23, bf16[2,360,128]{2,1,0:T(8,128)(2,1)S(1)} %collective-permute-done.22, ...), kind=kLoop, calls=%fused_computation.30 | loop fusion | flops 737280 | bytes 829440 | tf_op jit(solution)/shard_map/transpose | solution.py:372
  (37 shorter events, 0.5 us)
Async XLA Ops:
  2.2 14.4 %collective-permute-start = (bf16[2,368,128]{2,1,0:T(8,128)(2,1)}, bf16[2,368,128]{2,1,0:T(8,128)(2,1)S(1)}, u32[]{:S(2)}, u32[]{:S(2)}) collective-permute-start(bf16[2,368,128]{2,1,0:T(8,128)(2,1)} %get-tuple-element.62.refs_0_), channel_id=1, source_target_pairs={{0,8},{1,9},{2,10},{3,11},{4,12},{5,13},{6,14},{7,15},{8,0},{9,1},... | collective-permute-start | bytes 565256 | tf_op jit(solution)/shard_map/ppermute | solution.py:288
  5.3 8.4 %collective-permute-start.1 = (bf16[368,128]{1,0:T(8,128)(2,1)}, bf16[368,128]{1,0:T(8,128)(2,1)S(1)}, u32[]{:S(2)}, u32[]{:S(2)}) collective-permute-start(bf16[368,128]{1,0:T(8,128)(2,1)} %get-tuple-element.55), channel_id=1, source_target_pairs={{0,16},{1,17},{2,18},{3,19},{4,20},{5,21},{6,22},{7,23},{8,24},{9,... | collective-permute-start | bytes 282632 | tf_op jit(solution)/shard_map/ppermute | solution.py:288
  7.9 8.7 %collective-permute-start.2 = (bf16[368,128]{1,0:T(8,128)(2,1)}, bf16[368,128]{1,0:T(8,128)(2,1)S(1)}, u32[]{:S(2)}, u32[]{:S(2)}) collective-permute-start(bf16[368,128]{1,0:T(8,128)(2,1)} %get-tuple-element.55), channel_id=1, source_target_pairs={{0,24},{1,25},{2,26},{3,27},{4,28},{5,29},{6,30},{7,31},{8,16},{9,... | collective-permute-start | bytes 282632 | tf_op jit(solution)/shard_map/ppermute | solution.py:288
  8.6 1.2 %copy-start = (bf16[1,1440,360]{2,1,0:T(8,128)(2,1)S(1)}, bf16[1,1440,360]{2,1,0:T(8,128)(2,1)}, u32[]{:S(2)}) copy-start(bf16[1,1440,360]{2,1,0:T(8,128)(2,1)} %param.14) | copy-start | bytes 3110404
  9.9 1.2 %copy-start.1 = (bf16[1,1440,360]{2,1,0:T(8,128)(2,1)S(1)}, bf16[1,1440,360]{2,1,0:T(8,128)(2,1)}, u32[]{:S(2)}) copy-start(bf16[1,1440,360]{2,1,0:T(8,128)(2,1)} %param.16) | copy-start | bytes 3110404
  11.1 0.9 %copy-start.3 = (bf16[2,368,128]{2,1,0:T(8,128)(2,1)S(1)}, bf16[2,368,128]{2,1,0:T(8,128)(2,1)}, u32[]{:S(2)}) copy-start(bf16[2,368,128]{2,1,0:T(8,128)(2,1)} %get-tuple-element.62.refs_0_) | copy-start | bytes 565252
  11.9 9.1 %copy-start.2 = (bf16[1,360,1440]{2,1,0:T(8,128)(2,1)S(1)}, bf16[1,360,1440]{2,1,0:T(8,128)(2,1)}, u32[]{:S(2)}) copy-start(bf16[1,360,1440]{2,1,0:T(8,128)(2,1)} %param.18) | copy-start | bytes 3110404
  12.1 6.2 %collective-permute-start.6 = (bf16[2,368,128]{2,1,0:T(8,128)(2,1)S(1)}, bf16[2,368,128]{2,1,0:T(8,128)(2,1)S(1)}, u32[]{:S(2)}, u32[]{:S(2)}) collective-permute-start(bf16[2,368,128]{2,1,0:T(8,128)(2,1)S(1)} %copy-done.3), channel_id=1, source_target_pairs={{0,4},{1,5},{2,6},{3,7},{4,0},{5,1},{6,2},{7,3},{8,12},{9,13},{10,... | collective-permute-start | bytes 565256 | tf_op jit(solution)/shard_map/ppermute | solution.py:288
  16.6 4.9 %copy-start.4 = (bf16[2,368,128]{2,1,0:T(8,128)(2,1)S(1)}, bf16[2,368,128]{2,1,0:T(8,128)(2,1)}, u32[]{:S(2)}) copy-start(bf16[2,368,128]{2,1,0:T(8,128)(2,1)} %get-tuple-element.61.refs_1_) | copy-start | bytes 565252
  16.6 14.4 %collective-permute-start.3 = (bf16[4,368,128]{2,1,0:T(8,128)(2,1)S(1)}, bf16[4,368,128]{2,1,0:T(8,128)(2,1)S(1)}, u32[]{:S(2)}, u32[]{:S(2)}) collective-permute-start(bf16[4,368,128]{2,1,0:T(8,128)(2,1)S(1)} %pad_maximum_fusion), channel_id=1, source_target_pairs={{0,4},{1,5},{2,6},{3,7},{4,0},{5,1},{6,2},{7,3},{8,12},{9,13},{10,... | collective-permute-start | bytes 1130504 | tf_op jit(solution)/shard_map/ppermute | solution.py:288
  18.2 3.3 %collective-permute-start.7 = (bf16[2,368,128]{2,1,0:T(8,128)(2,1)S(1)}, bf16[2,368,128]{2,1,0:T(8,128)(2,1)S(1)}, u32[]{:S(2)}, u32[]{:S(2)}) collective-permute-start(bf16[2,368,128]{2,1,0:T(8,128)(2,1)S(1)} %collective-permute-done.6.refs_2_), channel_id=1, source_target_pairs={{0,1},{1,0},{2,3},{3,2},{4,5},{5,4},{6,7},{7,6},{8,9},{9,8},{10,11... | collective-permute-start | bytes 565256 | tf_op jit(solution)/shard_map/ppermute | solution.py:288
  18.2 8.0 %collective-permute-start.4 = (bf16[2,368,128]{2,1,0:T(8,128)(2,1)S(1)}, bf16[2,368,128]{2,1,0:T(8,128)(2,1)S(1)}, u32[]{:S(2)}, u32[]{:S(2)}) collective-permute-start(bf16[2,368,128]{2,1,0:T(8,128)(2,1)S(1)} %pad_maximum_fusion.1.refs_0_), channel_id=1, source_target_pairs={{0,2},{1,3},{2,0},{3,1},{4,6},{5,7},{6,4},{7,5},{8,10},{9,11},{10,... | collective-permute-start | bytes 565256 | tf_op jit(solution)/shard_map/ppermute | solution.py:288
  19.8 11.2 %collective-permute-start.5 = (bf16[2,368,128]{2,1,0:T(8,128)(2,1)S(1)}, bf16[2,368,128]{2,1,0:T(8,128)(2,1)S(1)}, u32[]{:S(2)}, u32[]{:S(2)}) collective-permute-start(bf16[2,368,128]{2,1,0:T(8,128)(2,1)S(1)} %pad_maximum_fusion.1.refs_0_), channel_id=1, source_target_pairs={{0,6},{1,7},{2,4},{3,5},{4,2},{5,3},{6,0},{7,1},{8,14},{9,15},{10,... | collective-permute-start | bytes 565256 | tf_op jit(solution)/shard_map/ppermute | solution.py:288
  31.0 2.5 %collective-permute-start.10 = (bf16[4,368,128]{2,1,0:T(8,128)(2,1)S(1)}, bf16[4,368,128]{2,1,0:T(8,128)(2,1)S(1)}, u32[]{:S(2)}, u32[]{:S(2)}) collective-permute-start(bf16[4,368,128]{2,1,0:T(8,128)(2,1)S(1)} %collective-permute-done.3.refs_4_.refs_2_), channel_id=1, source_target_pairs={{0,1},{1,0},{2,3},{3,2},{4,5},{5,4},{6,7},{7,6},{8,9},{9,8},{10,11... | collective-permute-start | bytes 1130504 | tf_op jit(solution)/shard_map/ppermute | solution.py:288
  31.0 2.0 %collective-permute-start.8 = (bf16[2,368,128]{2,1,0:T(8,128)(2,1)S(1)}, bf16[2,368,128]{2,1,0:T(8,128)(2,1)S(1)}, u32[]{:S(2)}, u32[]{:S(2)}) collective-permute-start(bf16[2,368,128]{2,1,0:T(8,128)(2,1)S(1)} %pad_maximum_fusion.1.refs_0_), channel_id=1, source_target_pairs={{0,1},{1,0},{2,3},{3,2},{4,5},{5,4},{6,7},{7,6},{8,9},{9,8},{10,11... | collective-permute-start | bytes 565256 | tf_op jit(solution)/shard_map/ppermute | solution.py:288
  31.5 1.7 %collective-permute-start.11 = (bf16[2,368,128]{2,1,0:T(8,128)(2,1)S(1)}, bf16[2,368,128]{2,1,0:T(8,128)(2,1)S(1)}, u32[]{:S(2)}, u32[]{:S(2)}) collective-permute-start(bf16[2,368,128]{2,1,0:T(8,128)(2,1)S(1)} %collective-permute-done.5.refs_6_), channel_id=1, source_target_pairs={{0,1},{1,0},{2,3},{3,2},{4,5},{5,4},{6,7},{7,6},{8,9},{9,8},{10,11... | collective-permute-start | bytes 565256 | tf_op jit(solution)/shard_map/ppermute | solution.py:288
  31.5 2.0 %collective-permute-start.9 = (bf16[2,368,128]{2,1,0:T(8,128)(2,1)S(1)}, bf16[2,368,128]{2,1,0:T(8,128)(2,1)S(1)}, u32[]{:S(2)}, u32[]{:S(2)}) collective-permute-start(bf16[2,368,128]{2,1,0:T(8,128)(2,1)S(1)} %collective-permute-done.4.refs_2_), channel_id=1, source_target_pairs={{0,1},{1,0},{2,3},{3,2},{4,5},{5,4},{6,7},{7,6},{8,9},{9,8},{10,11... | collective-permute-start | bytes 565256 | tf_op jit(solution)/shard_map/ppermute | solution.py:288
  32.1 6.7 %collective-permute-start.15 = (bf16[4,360,128]{2,1,0:T(8,128)(2,1)S(1)}, bf16[4,360,128]{2,1,0:T(8,128)(2,1)S(1)}, u32[]{:S(2)}, u32[]{:S(2)}) collective-permute-start(bf16[4,360,128]{2,1,0:T(8,128)(2,1)S(1)} %get-tuple-element.85), channel_id=1, source_target_pairs={{0,1},{1,0},{2,3},{3,2},{4,5},{5,4},{6,7},{7,6},{8,9},{9,8},{10,11... | collective-permute-start | bytes 1105928 | tf_op jit(solution)/shard_map/ppermute | solution.py:288
  35.7 3.0 %collective-permute-start.14 = (bf16[4,360,128]{2,1,0:T(8,128)(2,1)S(1)}, bf16[4,360,128]{2,1,0:T(8,128)(2,1)S(1)}, u32[]{:S(2)}, u32[]{:S(2)}) collective-permute-start(bf16[4,360,128]{2,1,0:T(8,128)(2,1)S(1)} %get-tuple-element.83), channel_id=1, source_target_pairs={{0,1},{1,0},{2,3},{3,2},{4,5},{5,4},{6,7},{7,6},{8,9},{9,8},{10,11... | collective-permute-start | bytes 1105928 | tf_op jit(solution)/shard_map/ppermute | solution.py:288
  38.2 4.2 %collective-permute-start.12 = (bf16[4,360,128]{2,1,0:T(8,128)(2,1)S(1)}, bf16[4,360,128]{2,1,0:T(8,128)(2,1)S(1)}, u32[]{:S(2)}, u32[]{:S(2)}) collective-permute-start(bf16[4,360,128]{2,1,0:T(8,128)(2,1)S(1)} %get-tuple-element.82), channel_id=1, source_target_pairs={{0,1},{1,0},{2,3},{3,2},{4,5},{5,4},{6,7},{7,6},{8,9},{9,8},{10,11... | collective-permute-start | bytes 1105928 | tf_op jit(solution)/shard_map/ppermute | solution.py:288
  38.6 1.6 %collective-permute-start.13 = (bf16[2,368,128]{2,1,0:T(8,128)(2,1)S(1)}, bf16[2,368,128]{2,1,0:T(8,128)(2,1)S(1)}, u32[]{:S(2)}, u32[]{:S(2)}) collective-permute-start(bf16[2,368,128]{2,1,0:T(8,128)(2,1)S(1)} %collective-permute-done.refs_0_), channel_id=1, source_target_pairs={{0,1},{1,0},{2,3},{3,2},{4,5},{5,4},{6,7},{7,6},{8,9},{9,8},{10,11... | collective-permute-start | bytes 565256 | tf_op jit(solution)/shard_map/ppermute | solution.py:288
  42.4 4.5 %collective-permute-start.19 = (bf16[4,360,128]{2,1,0:T(8,128)(2,1)S(1)}, bf16[4,360,128]{2,1,0:T(8,128)(2,1)S(1)}, u32[]{:S(2)}, u32[]{:S(2)}) collective-permute-start(bf16[4,360,128]{2,1,0:T(8,128)(2,1)S(1)} %get-tuple-element.99), channel_id=1, source_target_pairs={{0,1},{1,0},{2,3},{3,2},{4,5},{5,4},{6,7},{7,6},{8,9},{9,8},{10,11... | collective-permute-start | bytes 1105928 | tf_op jit(solution)/shard_map/ppermute | solution.py:288
  43.0 7.5 %collective-permute-start.16 = (bf16[2,360,128]{2,1,0:T(8,128)(2,1)S(1)}, bf16[2,360,128]{2,1,0:T(8,128)(2,1)S(1)}, u32[]{:S(2)}, u32[]{:S(2)}) collective-permute-start(bf16[2,360,128]{2,1,0:T(8,128)(2,1)S(1)} %pad_maximum_fusion.2), channel_id=1, source_target_pairs={{0,4},{1,5},{2,6},{3,7},{4,0},{5,1},{6,2},{7,3},{8,12},{9,13},{10,... | collective-permute-start | bytes 552968 | tf_op jit(solution)/shard_map/ppermute | solution.py:288
  44.6 15.5 %collective-permute-start.17 = (bf16[2,360,128]{2,1,0:T(8,128)(2,1)S(1)}, bf16[2,360,128]{2,1,0:T(8,128)(2,1)S(1)}, u32[]{:S(2)}, u32[]{:S(2)}) collective-permute-start(bf16[2,360,128]{2,1,0:T(8,128)(2,1)S(1)} %pad_maximum_fusion.3), channel_id=1, source_target_pairs={{0,2},{1,3},{2,0},{3,1},{4,6},{5,7},{6,4},{7,5},{8,10},{9,11},{10,... | collective-permute-start | bytes 552968 | tf_op jit(solution)/shard_map/ppermute | solution.py:288
  45.2 14.9 %collective-permute-start.18 = (bf16[2,360,128]{2,1,0:T(8,128)(2,1)S(1)}, bf16[2,360,128]{2,1,0:T(8,128)(2,1)S(1)}, u32[]{:S(2)}, u32[]{:S(2)}) collective-permute-start(bf16[2,360,128]{2,1,0:T(8,128)(2,1)S(1)} %pad_maximum_fusion.4), channel_id=1, source_target_pairs={{0,6},{1,7},{2,4},{3,5},{4,2},{5,3},{6,0},{7,1},{8,14},{9,15},{10,... | collective-permute-start | bytes 552968 | tf_op jit(solution)/shard_map/ppermute | solution.py:288
  47.0 16.5 %collective-permute-start.22 = (bf16[2,360,128]{2,1,0:T(8,128)(2,1)S(1)}, bf16[2,360,128]{2,1,0:T(8,128)(2,1)S(1)}, u32[]{:S(2)}, u32[]{:S(2)}) collective-permute-start(bf16[2,360,128]{2,1,0:T(8,128)(2,1)S(1)} %pad_maximum_fusion.7), channel_id=1, source_target_pairs={{0,6},{1,7},{2,4},{3,5},{4,2},{5,3},{6,0},{7,1},{8,14},{9,15},{10,... | collective-permute-start | bytes 552968 | tf_op jit(solution)/shard_map/ppermute | solution.py:288
  48.5 14.9 %collective-permute-start.21 = (bf16[2,360,128]{2,1,0:T(8,128)(2,1)S(1)}, bf16[2,360,128]{2,1,0:T(8,128)(2,1)S(1)}, u32[]{:S(2)}, u32[]{:S(2)}) collective-permute-start(bf16[2,360,128]{2,1,0:T(8,128)(2,1)S(1)} %pad_maximum_fusion.6), channel_id=1, source_target_pairs={{0,2},{1,3},{2,0},{3,1},{4,6},{5,7},{6,4},{7,5},{8,10},{9,11},{10,... | collective-permute-start | bytes 552968 | tf_op jit(solution)/shard_map/ppermute | solution.py:288
  50.6 12.9 %collective-permute-start.20 = (bf16[2,360,128]{2,1,0:T(8,128)(2,1)S(1)}, bf16[2,360,128]{2,1,0:T(8,128)(2,1)S(1)}, u32[]{:S(2)}, u32[]{:S(2)}) collective-permute-start(bf16[2,360,128]{2,1,0:T(8,128)(2,1)S(1)} %pad_maximum_fusion.5), channel_id=1, source_target_pairs={{0,4},{1,5},{2,6},{3,7},{4,0},{5,1},{6,2},{7,3},{8,12},{9,13},{10,... | collective-permute-start | bytes 552968 | tf_op jit(solution)/shard_map/ppermute | solution.py:288
  60.2 6.5 %collective-permute-start.24 = (bf16[360,128]{1,0:T(8,128)(2,1)S(1)}, bf16[360,128]{1,0:T(8,128)(2,1)S(1)}, u32[]{:S(2)}, u32[]{:S(2)}) collective-permute-start(bf16[360,128]{1,0:T(8,128)(2,1)S(1)} %get-tuple-element.115), channel_id=1, source_target_pairs={{0,16},{1,17},{2,18},{3,19},{4,20},{5,21},{6,22},{7,23},{8,24},{9,... | collective-permute-start | bytes 276488 | tf_op jit(solution)/shard_map/ppermute | solution.py:288
  61.4 6.8 %collective-permute-start.25 = (bf16[360,128]{1,0:T(8,128)(2,1)S(1)}, bf16[360,128]{1,0:T(8,128)(2,1)S(1)}, u32[]{:S(2)}, u32[]{:S(2)}) collective-permute-start(bf16[360,128]{1,0:T(8,128)(2,1)S(1)} %get-tuple-element.116), channel_id=1, source_target_pairs={{0,24},{1,25},{2,26},{3,27},{4,28},{5,29},{6,30},{7,31},{8,16},{9,... | collective-permute-start | bytes 276488 | tf_op jit(solution)/shard_map/ppermute | solution.py:288
  63.5 5.3 %collective-permute-start.23 = (bf16[360,128]{1,0:T(8,128)(2,1)S(1)}, bf16[360,128]{1,0:T(8,128)(2,1)S(1)}, u32[]{:S(2)}, u32[]{:S(2)}) collective-permute-start(bf16[360,128]{1,0:T(8,128)(2,1)S(1)} %fusion.5), channel_id=1, source_target_pairs={{0,8},{1,9},{2,10},{3,11},{4,12},{5,13},{6,14},{7,15},{8,0},{9,1},... | collective-permute-start | bytes 276488 | tf_op jit(solution)/shard_map/ppermute | solution.py:288

commit v8 on v7

--- a/solution.py
+++ b/solution.py
@@ -307,9 +307,7 @@
     x_0 = swap(tied((near, inward))[0], along_x)
     z_1, z_2, z_3, inward = tied((z_1, z_2, z_3, inward))
     z_high = jnp.stack([z_2, z_3])
-    diagonal = along_x + along_y
-    x_all = swap(jnp.concatenate([z_1, z_high], axis=0), along_x)
-    d_high, y_high = swap(z_high, diagonal), swap(z_high, along_y)
+    x_high, y_high = swap(z_high, along_x), swap(z_high, along_y)
     outward = arrange(
         outward_kernel,
         groups,
@@ -320,55 +318,40 @@
     )
     weights = (*inward, *outward)
 
-    def pairs(first, step):
-        return [[(first + step * x + k % 2, k // 2) for k in range(groups)] for x in range(2)]
-
-    slots = ((0, 1), (2, 3))
-    sizes = (quarter, per)
-    keep_0, send_0 = run_expert(
-        (near, far, x_0, swap(x_0, core)), pairs(0, 2), slots, weights, sizes, 1
-    )
-    x_all, y_high, d_high, keep_0, send_0 = tied((x_all, y_high, d_high, keep_0, send_0))
-    got_0 = swap(send_0, core)
-    x_core = swap(x_all, core)
-    high = (z_high, swap(z_high, core), y_high, swap(y_high, core))
-    high = high + (x_all, x_core, d_high, swap(d_high, core))
-    near_1 = (z_1, swap(z_1, core), x_all, x_core)
-    line = [
-        [[(4 * x + k, n + 2 * (x > k // 2)) for k in range(groups)] for x in range(2)]
-        for n in range(2)
-    ]
-    keep_2, send_2 = run_expert(high, line[0], slots, weights, sizes, 1)
-    got_2 = swap(send_2, core)
-    keep_2, high = tied((keep_2, high))
-    keep_3, send_3 = run_expert(high, line[1], slots, weights, sizes, 1)
-    got_2, keep_3, got_0 = tied((got_2, keep_3, got_0))
-    got_3 = swap(send_3, core)
-    near_1, got_2 = tied((near_1, got_2))
-    keep_1, send_1 = run_expert(near_1, pairs(0, 2), slots, weights, sizes, 1)
-    got_1 = swap(send_1, core)
-    got_3, keep_1, got_0 = tied((got_3, keep_1, got_0))
-
-    def outer(first, second, at):
-        return jnp.stack([add_up(keep[at], got[at]) for keep, got in (first, second)])
-
-    far_lines = ((keep_2, got_2), (keep_3, got_3))
-    y_sum = swap(outer(*far_lines, 1), along_y)
-    x_sum = swap(outer(*far_lines, 2), along_x)
-    d_sum = swap(outer(*far_lines, 3), diagonal)
-    line_2 = add_up(keep_2[0], got_2[0], x_sum[0], y_sum[0], d_sum[0])
-    line_3 = add_up(keep_3[0], got_3[0], x_sum[1], y_sum[1], d_sum[1])
+    def expert(arrays, blocks):
+        return run_expert(arrays, blocks, ((0, 2), (1, 3)), weights, (quarter, per), 1)
+
+    def line(arrays, index):
+        return [(at, n) for at, n in zip(arrays, index)]
+
+    twice = [0, 0, 1, 1]
+    near_blocks = [line([0, 1, 0, 1], twice), line([2, 3, 2, 3], twice)]
+    far_blocks = [line([0, 1, 2, 3], [n] * groups) for n in range(2)]
+
+    keep_p, send_p = expert((near, far, z_1, swap(z_1, core)), near_blocks)
+    x_high, z_1, x_0, keep_p, send_p = tied((x_high, z_1, x_0, keep_p, send_p))
+    corner, x_1 = swap(x_high, along_y), swap(z_1, along_x)
+    got_p = swap(send_p, core)
+    keep_q, send_q = expert((z_high, swap(z_high, core), y_high, swap(y_high, core)), far_blocks)
+    corner, x_1, keep_q, send_q = tied((corner, x_1, keep_q, send_q))
+    got_q = swap(send_q, core)
+    y_p = swap(add_up(keep_p[2:4], got_p[2:4]), along_y)
+    y_q = swap(add_up(keep_q[2:4], got_q[2:4]), along_y)
+    keep_s, send_s = expert((x_high, swap(x_high, core), corner, swap(corner, core)), far_blocks)
+    keep_s, send_s, y_p, x_1 = tied((keep_s, send_s, y_p, x_1))
+    got_s = swap(send_s, core)
+    keep_r, send_r = expert((x_0, swap(x_0, core), x_1, swap(x_1, core)), near_blocks)
+    keep_r, send_r, y_q = tied((keep_r, send_r, y_q))
+    got_r = swap(send_r, core)
+
+    y_s = swap(add_up(keep_s[2:4], got_s[2:4]), along_y)
+    y_r = swap(add_up(keep_r[2:4], got_r[2:4]), along_y)
+    x_s = swap(add_up(keep_s[0:2], got_s[0:2], y_s), along_x)
+    x_r = swap(add_up(keep_r[0:2], got_r[0:2], y_r), along_x)
+    line_2, line_3 = [add_up(keep_q[n], got_q[n], y_q[n], x_s[n]) for n in range(2)]
     back_2, back_3 = swap(line_2, 2 * along_z), swap(line_3, 3 * along_z)
-    near_lines = ((keep_0, got_0), (keep_1, got_1))
-    x_near = swap(outer(*near_lines, 2), along_x)
-    y_near = swap(outer(*near_lines, 1), along_y)
-    d_near = swap(outer(*near_lines, 3), diagonal)
-    _, _, x_near, y_near, d_near = tied((line_2, line_3, x_near, y_near, d_near))
-    line_1 = add_up(keep_1[0], got_1[0], x_near[1], y_near[1], d_near[1])
-    back_1 = swap(line_1, along_z)
-    mixed = add_up(
-        keep_0[0], got_0[0], x_near[0], y_near[0], d_near[0], back_1, back_2, back_3
-    )
+    back_1 = swap(add_up(keep_p[1], got_p[1], y_p[1], x_r[1]), along_z)
+    mixed = add_up(keep_p[0], got_p[0], y_p[0], x_r[0], back_1, back_2, back_3)
     return mixed.T
 
 

time: 69.8 us -> 75.9 us (1.087)
  waiting for transfers between devices: 26.3 us -> 36 us
  starting transfers between devices: 26 us -> 22.7 us
    ppermute x26 -> x28, waiting for transfers between devices: 26.3 us -> 36 us  [swap(): lax.ppermute(array, ('seq', 'rep'), [(i, i ^ step) for i in range(devices)])]
    ppermute x26 -> x28, starting transfers between devices: 26 us -> 22.7 us  [swap(): lax.ppermute(array, ('seq', 'rep'), [(i, i ^ step) for i in range(devices)])]
  transfers between devices with their start and end apart: 26 -> 28, of which waited for: 12 -> 17; matrix products, arithmetic and copies ran while one was open for 2% -> 2% of each run, Pallas kernels for 14% -> 13%
where the time goes in v8:
time: 75.9 us; the launch traced here: 75.7 us
  waiting for transfers between devices  36 us (47%)
  starting transfers between devices  22.7 us (30%)
  Pallas kernels  12.3 us (16%)
  local copies, waits for them, and re-layouts  2.5 us (3%)
  other arithmetic  2.03 us (3%)
    ppermute x28, waiting for transfers between devices, swap(): lax.ppermute(array, ('seq', 'rep'), [(i, i ^ step) for i in range(devices)])  36 us
    ppermute x28, starting transfers between devices, swap(): lax.ppermute(array, ('seq', 'rep'), [(i, i ^ step) for i in range(devices)])  22.7 us
    pallas_call x4, Pallas kernels, run_expert(): pl.pallas_call(functools.partial(expert_kernel, quarter, per, blocks, slo...  8.8 us
    unnamed x10, local copies, waits for them, and re-layouts  2.5 us
    pallas_call x1, Pallas kernels, make_pieces(): pl.pallas_call(functools.partial(pieces_kernel, groups, per, experts), in...  2.23 us
  transfers between devices with their start and end apart: 28, of which 17 were waited for; matrix products, arithmetic and copies ran while one was open for 2% of the time, Pallas kernels for 13%

profile of v8, /device:TPU:0, one launch (start us, length us, event | category | flops | bytes accessed | tf_op | source)
XLA Modules:
  0.0 75.7 jit_solution(14252448854815344607)
XLA Ops:
  0.0 2.2 %shard_map.100 = (bf16[368,128]{1,0:T(8,128)(2,1)}, bf16[2,368,128]{2,1,0:T(8,128)(2,1)}, bf16[2,368,128]{2,1,0:T(8,128)(2,1)}) custom-call(bf16[1440,128]{1,0:T(8,128)(2,1)} %bitcast.29, f32[1440]{0:T(1024)} %refs_1_.1, s32[4,128]{1,0:T(4,128)} %bitcast.32, f32[4,128]{1,0:T(4,128)} %bitcast.33), custom_call_target="tpu_custom_call" | custom-call | tf_op jit(solution)/shard_map/pallas_call | solution.py:188
  2.2 3.1 %collective-permute-start = (bf16[2,368,128]{2,1,0:T(8,128)(2,1)}, bf16[2,368,128]{2,1,0:T(8,128)(2,1)S(1)}, u32[]{:S(2)}, u32[]{:S(2)}) collective-permute-start(bf16[2,368,128]{2,1,0:T(8,128)(2,1)} %get-tuple-element.49.refs_0_), channel_id=1, source_target_pairs={{0,8},{1,9},{2,10},{3,11},{4,12},{5,13},{6,14},{7,15},{8,0},{9,1},... | collective-permute-start | bytes 565256 | tf_op jit(solution)/shard_map/ppermute | solution.py:288
  5.3 2.6 %collective-permute-start.1 = (bf16[368,128]{1,0:T(8,128)(2,1)}, bf16[368,128]{1,0:T(8,128)(2,1)S(1)}, u32[]{:S(2)}, u32[]{:S(2)}) collective-permute-start(bf16[368,128]{1,0:T(8,128)(2,1)} %get-tuple-element.43), channel_id=1, source_target_pairs={{0,16},{1,17},{2,18},{3,19},{4,20},{5,21},{6,22},{7,23},{8,24},{9,... | collective-permute-start | bytes 282632 | tf_op jit(solution)/shard_map/ppermute | solution.py:288
  7.9 0.7 pad_maximum_fusion.1.biases_ref
  8.7 1.2 %copy-done = bf16[1,1440,360]{2,1,0:T(8,128)(2,1)S(1)} copy-done((bf16[1,1440,360]{2,1,0:T(8,128)(2,1)S(1)}, bf16[1,1440,360]{2,1,0:T(8,128)(2,1)}, u32[]{:S(2)}) %copy-start) | copy-done | bytes 1036824
  9.9 1.2 %copy-done.1 = bf16[1,1440,360]{2,1,0:T(8,128)(2,1)S(1)} copy-done((bf16[1,1440,360]{2,1,0:T(8,128)(2,1)S(1)}, bf16[1,1440,360]{2,1,0:T(8,128)(2,1)}, u32[]{:S(2)}) %copy-start.1) | copy-done | bytes 1036824
  11.1 0.8 %shard_map.101 = (bf16[768,1536]{1,0:T(8,128)(2,1)S(1)}, f32[768,128]{1,0:T(8,128)S(1)}) custom-call(bf16[1440,360]{1,0:T(8,128)(2,1)S(1)} %bitcast.26, bf16[1440,360]{1,0:T(8,128)(2,1)S(1)} %bitcast.27, f32[3,360]{1,0:T(4,128)S(1)} %pad_maximum_fusion.1.biases_ref), custom_call_target="tpu_custom_call" | custom-call | bytes 8294400 | tf_op jit(solution)/shard_map/pallas_call | solution.py:116
  11.9 0.8 %collective-permute-done.1 = bf16[368,128]{1,0:T(8,128)(2,1)S(1)} collective-permute-done((bf16[368,128]{1,0:T(8,128)(2,1)}, bf16[368,128]{1,0:T(8,128)(2,1)S(1)}, u32[]{:S(2)}, u32[]{:S(2)}) %collective-permute-start.1) | collective-permute-done | bytes 94240 | tf_op jit(solution)/shard_map/ppermute | solution.py:288
  12.7 3.9 %collective-permute-done.2 = bf16[368,128]{1,0:T(8,128)(2,1)S(1)} collective-permute-done((bf16[368,128]{1,0:T(8,128)(2,1)}, bf16[368,128]{1,0:T(8,128)(2,1)S(1)}, u32[]{:S(2)}, u32[]{:S(2)}) %collective-permute-start.2) | collective-permute-done | bytes 94240 | tf_op jit(solution)/shard_map/ppermute | solution.py:288
  16.6 1.6 %collective-permute-start.4 = (bf16[2,368,128]{2,1,0:T(8,128)(2,1)S(1)}, bf16[2,368,128]{2,1,0:T(8,128)(2,1)S(1)}, u32[]{:S(2)}, u32[]{:S(2)}) collective-permute-start(bf16[2,368,128]{2,1,0:T(8,128)(2,1)S(1)} %copy-done.3), channel_id=1, source_target_pairs={{0,4},{1,5},{2,6},{3,7},{4,0},{5,1},{6,2},{7,3},{8,12},{9,13},{10,... | collective-permute-start | bytes 565256 | tf_op jit(solution)/shard_map/ppermute | solution.py:288
  18.2 0.6 collective-permute-start.3
  18.8 1.5 %collective-permute-start.11 = (bf16[2,368,128]{2,1,0:T(8,128)(2,1)S(1)}, bf16[2,368,128]{2,1,0:T(8,128)(2,1)S(1)}, u32[]{:S(2)}, u32[]{:S(2)}) collective-permute-start(bf16[2,368,128]{2,1,0:T(8,128)(2,1)S(1)} %pad_maximum_fusion.refs_0_), channel_id=1, source_target_pairs={{0,2},{1,3},{2,0},{3,1},{4,6},{5,7},{6,4},{7,5},{8,10},{9,11},{10,... | collective-permute-start | bytes 565256 | tf_op jit(solution)/shard_map/ppermute | solution.py:288
  20.3 0.4 shard_map.102
  20.8 2.2 %shard_map.103 = (bf16[4,360,128]{2,1,0:T(8,128)(2,1)S(1)}, bf16[4,360,128]{2,1,0:T(8,128)(2,1)S(1)}) custom-call(bf16[2,368,128]{2,1,0:T(8,128)(2,1)S(1)} %copy-done.3, bf16[2,368,128]{2,1,0:T(8,128)(2,1)S(1)} %copy-done.4, bf16[2,368,128]{2,1,0:T(8,128)(2,1)S(1)} %collective-permute-done.refs_2_, bf16[2,368,128]{2,1,0:T(8,128)(2,1)S(1)} %collective-permute-done.5.refs_3_, ...), custom_call_target="tpu_custom_call" | custom-call | flops 1811939328 | bytes 3538944 | tf_op jit(solution)/shard_map/pallas_call | solution.py:253
  23.0 1.2 %collective-permute-done.4.refs_0_ = bf16[2,368,128]{2,1,0:T(8,128)(2,1)S(1)} collective-permute-done((bf16[2,368,128]{2,1,0:T(8,128)(2,1)S(1)}, bf16[2,368,128]{2,1,0:T(8,128)(2,1)S(1)}, u32[]{:S(2)}, u32[]{:S(2)}) %collective-permute-start.4) | collective-permute-done | bytes 188448 | tf_op jit(solution)/shard_map/ppermute | solution.py:288
  24.2 3.6 %collective-permute-done.3.refs_0_ = bf16[2,368,128]{2,1,0:T(8,128)(2,1)S(1)} collective-permute-done((bf16[2,368,128]{2,1,0:T(8,128)(2,1)S(1)}, bf16[2,368,128]{2,1,0:T(8,128)(2,1)S(1)}, u32[]{:S(2)}, u32[]{:S(2)}) %collective-permute-start.3) | collective-permute-done | bytes 188448 | tf_op jit(solution)/shard_map/ppermute | solution.py:288
  27.8 0.5 collective-permute-start.10
  28.3 1.5 %collective-permute-start.8 = (bf16[2,368,128]{2,1,0:T(8,128)(2,1)S(1)}, bf16[2,368,128]{2,1,0:T(8,128)(2,1)S(1)}, u32[]{:S(2)}, u32[]{:S(2)}) collective-permute-start(bf16[2,368,128]{2,1,0:T(8,128)(2,1)S(1)} %collective-permute-done.3.refs_0_), channel_id=1, source_target_pairs={{0,2},{1,3},{2,0},{3,1},{4,6},{5,7},{6,4},{7,5},{8,10},{9,11},{10,... | collective-permute-start | bytes 565256 | tf_op jit(solution)/shard_map/ppermute | solution.py:288
  29.8 1.5 %collective-permute-start.9 = (bf16[2,368,128]{2,1,0:T(8,128)(2,1)S(1)}, bf16[2,368,128]{2,1,0:T(8,128)(2,1)S(1)}, u32[]{:S(2)}, u32[]{:S(2)}) collective-permute-start(bf16[2,368,128]{2,1,0:T(8,128)(2,1)S(1)} %collective-permute-done.refs_2_), channel_id=1, source_target_pairs={{0,4},{1,5},{2,6},{3,7},{4,0},{5,1},{6,2},{7,3},{8,12},{9,13},{10,... | collective-permute-start | bytes 565256 | tf_op jit(solution)/shard_map/ppermute | solution.py:288
  31.3 2.2 %shard_map.104 = (bf16[4,360,128]{2,1,0:T(8,128)(2,1)S(1)}, bf16[4,360,128]{2,1,0:T(8,128)(2,1)S(1)}) custom-call(bf16[2,368,128]{2,1,0:T(8,128)(2,1)S(1)} %pad_maximum_fusion.refs_0_, bf16[2,368,128]{2,1,0:T(8,128)(2,1)S(1)} %collective-permute-done.10.refs_1_, bf16[2,368,128]{2,1,0:T(8,128)(2,1)S(1)} %collective-permute-done.11.refs_2_, ...), custom_call_target="tpu_custom_call" | custom-call | flops 1811939328 | bytes 3538944 | tf_op jit(solution)/shard_map/pallas_call | solution.py:253
  33.5 1.9 %collective-permute-done.8.refs_2_ = bf16[2,368,128]{2,1,0:T(8,128)(2,1)S(1)} collective-permute-done((bf16[2,368,128]{2,1,0:T(8,128)(2,1)S(1)}, bf16[2,368,128]{2,1,0:T(8,128)(2,1)S(1)}, u32[]{:S(2)}, u32[]{:S(2)}) %collective-permute-start.8) | collective-permute-done | bytes 188448 | tf_op jit(solution)/shard_map/ppermute | solution.py:288
  35.4 1.2 %collective-permute-done.9.refs_2_ = bf16[2,368,128]{2,1,0:T(8,128)(2,1)S(1)} collective-permute-done((bf16[2,368,128]{2,1,0:T(8,128)(2,1)S(1)}, bf16[2,368,128]{2,1,0:T(8,128)(2,1)S(1)}, u32[]{:S(2)}, u32[]{:S(2)}) %collective-permute-start.9) | collective-permute-done | bytes 188448 | tf_op jit(solution)/shard_map/ppermute | solution.py:288
  36.7 0.5 collective-permute-start.17
  37.3 0.6 collective-permute-start.14
  37.8 0.3 collective-permute-done.13.refs_3_
  38.1 2.2 %shard_map.105 = (bf16[4,360,128]{2,1,0:T(8,128)(2,1)S(1)}, bf16[4,360,128]{2,1,0:T(8,128)(2,1)S(1)}) custom-call(bf16[2,368,128]{2,1,0:T(8,128)(2,1)S(1)} %collective-permute-done.3.refs_0_, bf16[2,368,128]{2,1,0:T(8,128)(2,1)S(1)} %collective-permute-done.7.refs_1_, bf16[2,368,128]{2,1,0:T(8,128)(2,1)S(1)} %collective-permute-done.8.refs_2_, ...), custom_call_target="tpu_custom_call" | custom-call | flops 1811939328 | bytes 3538944 | tf_op jit(solution)/shard_map/pallas_call | solution.py:253
  40.3 3.6 %collective-permute-done.14 = bf16[2,360,128]{2,1,0:T(8,128)(2,1)S(1)} collective-permute-done((bf16[2,360,128]{2,1,0:T(8,128)(2,1)S(1)}, bf16[2,360,128]{2,1,0:T(8,128)(2,1)S(1)}, u32[]{:S(2)}, u32[]{:S(2)}) %collective-permute-start.14) | collective-permute-done | bytes 184352 | tf_op jit(solution)/shard_map/ppermute | solution.py:288
  43.9 0.5 collective-permute-start.16
  44.4 0.6 collective-permute-start.18
  45.0 0.8 %collective-permute-done.16.refs_3_ = bf16[2,368,128]{2,1,0:T(8,128)(2,1)S(1)} collective-permute-done((bf16[2,368,128]{2,1,0:T(8,128)(2,1)S(1)}, bf16[2,368,128]{2,1,0:T(8,128)(2,1)S(1)}, u32[]{:S(2)}, u32[]{:S(2)}) %collective-permute-start.16) | collective-permute-done | bytes 188448 | tf_op jit(solution)/shard_map/ppermute | solution.py:288
  45.8 2.2 %shard_map.106 = (bf16[4,360,128]{2,1,0:T(8,128)(2,1)S(1)}, bf16[4,360,128]{2,1,0:T(8,128)(2,1)S(1)}) custom-call(bf16[2,368,128]{2,1,0:T(8,128)(2,1)S(1)} %collective-permute-done.4.refs_0_, bf16[2,368,128]{2,1,0:T(8,128)(2,1)S(1)} %collective-permute-done.15.refs_1_, bf16[2,368,128]{2,1,0:T(8,128)(2,1)S(1)} %collective-permute-done.9.refs_2_, ...), custom_call_target="tpu_custom_call" | custom-call | flops 1811939328 | bytes 3538944 | tf_op jit(solution)/shard_map/pallas_call | solution.py:253
  48.0 3.0 %collective-permute-done.18 = bf16[2,360,128]{2,1,0:T(8,128)(2,1)S(1)} collective-permute-done((bf16[2,360,128]{2,1,0:T(8,128)(2,1)S(1)}, bf16[2,360,128]{2,1,0:T(8,128)(2,1)S(1)}, u32[]{:S(2)}, u32[]{:S(2)}) %collective-permute-start.18) | collective-permute-done | bytes 184352 | tf_op jit(solution)/shard_map/ppermute | solution.py:288
  51.1 0.6 collective-permute-start.24
  51.7 1.1 %collective-permute-done.19 = bf16[4,360,128]{2,1,0:T(8,128)(2,1)S(1)} collective-permute-done((bf16[4,360,128]{2,1,0:T(8,128)(2,1)S(1)}, bf16[4,360,128]{2,1,0:T(8,128)(2,1)S(1)}, u32[]{:S(2)}, u32[]{:S(2)}) %collective-permute-start.19) | collective-permute-done | bytes 368672 | tf_op jit(solution)/shard_map/ppermute | solution.py:288
  52.8 0.6 collective-permute-start.20
  53.4 5.2 %collective-permute-done.24 = bf16[2,360,128]{2,1,0:T(8,128)(2,1)S(1)} collective-permute-done((bf16[2,360,128]{2,1,0:T(8,128)(2,1)S(1)}, bf16[2,360,128]{2,1,0:T(8,128)(2,1)S(1)}, u32[]{:S(2)}, u32[]{:S(2)}) %collective-permute-start.24) | collective-permute-done | bytes 184352 | tf_op jit(solution)/shard_map/ppermute | solution.py:288
  58.7 1.6 %collective-permute-start.25 = (bf16[2,360,128]{2,1,0:T(8,128)(2,1)S(1)}, bf16[2,360,128]{2,1,0:T(8,128)(2,1)S(1)}, u32[]{:S(2)}, u32[]{:S(2)}) collective-permute-start(bf16[2,360,128]{2,1,0:T(8,128)(2,1)S(1)} %add_convert_fusion), channel_id=1, source_target_pairs={{0,4},{1,5},{2,6},{3,7},{4,0},{5,1},{6,2},{7,3},{8,12},{9,13},{10,... | collective-permute-start | bytes 552968 | tf_op jit(solution)/shard_map/ppermute | solution.py:288
  60.3 1.9 %collective-permute-done.20 = bf16[2,360,128]{2,1,0:T(8,128)(2,1)S(1)} collective-permute-done((bf16[2,360,128]{2,1,0:T(8,128)(2,1)S(1)}, bf16[2,360,128]{2,1,0:T(8,128)(2,1)S(1)}, u32[]{:S(2)}, u32[]{:S(2)}) %collective-permute-start.20) | collective-permute-done | bytes 184352 | tf_op jit(solution)/shard_map/ppermute | solution.py:288
  62.3 1.6 %collective-permute-start.21 = (bf16[2,360,128]{2,1,0:T(8,128)(2,1)S(1)}, bf16[2,360,128]{2,1,0:T(8,128)(2,1)S(1)}, u32[]{:S(2)}, u32[]{:S(2)}) collective-permute-start(bf16[2,360,128]{2,1,0:T(8,128)(2,1)S(1)} %add_convert_fusion.2), channel_id=1, source_target_pairs={{0,4},{1,5},{2,6},{3,7},{4,0},{5,1},{6,2},{7,3},{8,12},{9,13},{10,... | collective-permute-start | bytes 552968 | tf_op jit(solution)/shard_map/ppermute | solution.py:288
  63.8 0.8 %collective-permute-done.25 = bf16[2,360,128]{2,1,0:T(8,128)(2,1)S(1)} collective-permute-done((bf16[2,360,128]{2,1,0:T(8,128)(2,1)S(1)}, bf16[2,360,128]{2,1,0:T(8,128)(2,1)S(1)}, u32[]{:S(2)}, u32[]{:S(2)}) %collective-permute-start.25) | collective-permute-done | bytes 184352 | tf_op jit(solution)/shard_map/ppermute | solution.py:288
  64.7 0.1 fusion.4
  64.8 1.7 %collective-permute-start.27 = (bf16[360,128]{1,0:T(8,128)(2,1)S(1)}, bf16[360,128]{1,0:T(8,128)(2,1)S(1)}, u32[]{:S(2)}, u32[]{:S(2)}) collective-permute-start(bf16[360,128]{1,0:T(8,128)(2,1)S(1)} %get-tuple-element.80), channel_id=1, source_target_pairs={{0,24},{1,25},{2,26},{3,27},{4,28},{5,29},{6,30},{7,31},{8,16},{9,... | collective-permute-start | bytes 276488 | tf_op jit(solution)/shard_map/ppermute | solution.py:288
  66.4 0.8 %collective-permute-start.26 = (bf16[360,128]{1,0:T(8,128)(2,1)S(1)}, bf16[360,128]{1,0:T(8,128)(2,1)S(1)}, u32[]{:S(2)}, u32[]{:S(2)}) collective-permute-start(bf16[360,128]{1,0:T(8,128)(2,1)S(1)} %get-tuple-element.79), channel_id=1, source_target_pairs={{0,16},{1,17},{2,18},{3,19},{4,20},{5,21},{6,22},{7,23},{8,24},{9,... | collective-permute-start | bytes 276488 | tf_op jit(solution)/shard_map/ppermute | solution.py:288
  67.2 1.4 %collective-permute-done.21 = bf16[2,360,128]{2,1,0:T(8,128)(2,1)S(1)} collective-permute-done((bf16[2,360,128]{2,1,0:T(8,128)(2,1)S(1)}, bf16[2,360,128]{2,1,0:T(8,128)(2,1)S(1)}, u32[]{:S(2)}, u32[]{:S(2)}) %collective-permute-start.21) | collective-permute-done | bytes 184352 | tf_op jit(solution)/shard_map/ppermute | solution.py:288
  68.7 1.0 %collective-permute-start.22 = (bf16[360,128]{1,0:T(8,128)(2,1)S(1)}, bf16[360,128]{1,0:T(8,128)(2,1)S(1)}, u32[]{:S(2)}, u32[]{:S(2)}) collective-permute-start(bf16[360,128]{1,0:T(8,128)(2,1)S(1)} %fusion.3), channel_id=1, source_target_pairs={{0,8},{1,9},{2,10},{3,11},{4,12},{5,13},{6,14},{7,15},{8,0},{9,1},... | collective-permute-start | bytes 276488 | tf_op jit(solution)/shard_map/ppermute | solution.py:288
  69.7 1.6 %collective-permute-done.27 = bf16[360,128]{1,0:T(8,128)(2,1)S(1)} collective-permute-done((bf16[360,128]{1,0:T(8,128)(2,1)S(1)}, bf16[360,128]{1,0:T(8,128)(2,1)S(1)}, u32[]{:S(2)}, u32[]{:S(2)}) %collective-permute-start.27) | collective-permute-done | bytes 92192 | tf_op jit(solution)/shard_map/ppermute | solution.py:288
  71.3 3.6 %collective-permute-done.26 = bf16[360,128]{1,0:T(8,128)(2,1)S(1)} collective-permute-done((bf16[360,128]{1,0:T(8,128)(2,1)S(1)}, bf16[360,128]{1,0:T(8,128)(2,1)S(1)}, u32[]{:S(2)}, u32[]{:S(2)}) %collective-permute-start.26) | collective-permute-done | bytes 92192 | tf_op jit(solution)/shard_map/ppermute | solution.py:288
  74.9 0.7 fusion.6
  (36 shorter events, 0.6 us)
Async XLA Ops:
  2.2 14.4 %collective-permute-start = (bf16[2,368,128]{2,1,0:T(8,128)(2,1)}, bf16[2,368,128]{2,1,0:T(8,128)(2,1)S(1)}, u32[]{:S(2)}, u32[]{:S(2)}) collective-permute-start(bf16[2,368,128]{2,1,0:T(8,128)(2,1)} %get-tuple-element.49.refs_0_), channel_id=1, source_target_pairs={{0,8},{1,9},{2,10},{3,11},{4,12},{5,13},{6,14},{7,15},{8,0},{9,1},... | collective-permute-start | bytes 565256 | tf_op jit(solution)/shard_map/ppermute | solution.py:288
  5.3 7.4 %collective-permute-start.1 = (bf16[368,128]{1,0:T(8,128)(2,1)}, bf16[368,128]{1,0:T(8,128)(2,1)S(1)}, u32[]{:S(2)}, u32[]{:S(2)}) collective-permute-start(bf16[368,128]{1,0:T(8,128)(2,1)} %get-tuple-element.43), channel_id=1, source_target_pairs={{0,16},{1,17},{2,18},{3,19},{4,20},{5,21},{6,22},{7,23},{8,24},{9,... | collective-permute-start | bytes 282632 | tf_op jit(solution)/shard_map/ppermute | solution.py:288
  7.9 8.7 %collective-permute-start.2 = (bf16[368,128]{1,0:T(8,128)(2,1)}, bf16[368,128]{1,0:T(8,128)(2,1)S(1)}, u32[]{:S(2)}, u32[]{:S(2)}) collective-permute-start(bf16[368,128]{1,0:T(8,128)(2,1)} %get-tuple-element.43), channel_id=1, source_target_pairs={{0,24},{1,25},{2,26},{3,27},{4,28},{5,29},{6,30},{7,31},{8,16},{9,... | collective-permute-start | bytes 282632 | tf_op jit(solution)/shard_map/ppermute | solution.py:288
  8.6 1.2 %copy-start = (bf16[1,1440,360]{2,1,0:T(8,128)(2,1)S(1)}, bf16[1,1440,360]{2,1,0:T(8,128)(2,1)}, u32[]{:S(2)}) copy-start(bf16[1,1440,360]{2,1,0:T(8,128)(2,1)} %param.14) | copy-start | bytes 3110404
  9.9 1.2 %copy-start.1 = (bf16[1,1440,360]{2,1,0:T(8,128)(2,1)S(1)}, bf16[1,1440,360]{2,1,0:T(8,128)(2,1)}, u32[]{:S(2)}) copy-start(bf16[1,1440,360]{2,1,0:T(8,128)(2,1)} %param.16) | copy-start | bytes 3110404
  11.1 5.5 %copy-start.3 = (bf16[2,368,128]{2,1,0:T(8,128)(2,1)S(1)}, bf16[2,368,128]{2,1,0:T(8,128)(2,1)}, u32[]{:S(2)}) copy-start(bf16[2,368,128]{2,1,0:T(8,128)(2,1)} %get-tuple-element.49.refs_0_) | copy-start | bytes 565252
  11.1 9.2 %copy-start.2 = (bf16[1,360,1440]{2,1,0:T(8,128)(2,1)S(1)}, bf16[1,360,1440]{2,1,0:T(8,128)(2,1)}, u32[]{:S(2)}) copy-start(bf16[1,360,1440]{2,1,0:T(8,128)(2,1)} %param.18) | copy-start | bytes 3110404
  11.9 8.8 %copy-start.4 = (bf16[2,368,128]{2,1,0:T(8,128)(2,1)S(1)}, bf16[2,368,128]{2,1,0:T(8,128)(2,1)}, u32[]{:S(2)}) copy-start(bf16[2,368,128]{2,1,0:T(8,128)(2,1)} %get-tuple-element.50.refs_1_) | copy-start | bytes 565252
  16.6 4.2 %collective-permute-start.5 = (bf16[2,368,128]{2,1,0:T(8,128)(2,1)S(1)}, bf16[2,368,128]{2,1,0:T(8,128)(2,1)S(1)}, u32[]{:S(2)}, u32[]{:S(2)}) collective-permute-start(bf16[2,368,128]{2,1,0:T(8,128)(2,1)S(1)} %collective-permute-done.refs_2_), channel_id=1, source_target_pairs={{0,1},{1,0},{2,3},{3,2},{4,5},{5,4},{6,7},{7,6},{8,9},{9,8},{10,11... | collective-permute-start | bytes 565256 | tf_op jit(solution)/shard_map/ppermute | solution.py:288
  16.6 7.6 %collective-permute-start.4 = (bf16[2,368,128]{2,1,0:T(8,128)(2,1)S(1)}, bf16[2,368,128]{2,1,0:T(8,128)(2,1)S(1)}, u32[]{:S(2)}, u32[]{:S(2)}) collective-permute-start(bf16[2,368,128]{2,1,0:T(8,128)(2,1)S(1)} %copy-done.3), channel_id=1, source_target_pairs={{0,4},{1,5},{2,6},{3,7},{4,0},{5,1},{6,2},{7,3},{8,12},{9,13},{10,... | collective-permute-start | bytes 565256 | tf_op jit(solution)/shard_map/ppermute | solution.py:288
  18.2 9.6 %collective-permute-start.3 = (bf16[2,368,128]{2,1,0:T(8,128)(2,1)S(1)}, bf16[2,368,128]{2,1,0:T(8,128)(2,1)S(1)}, u32[]{:S(2)}, u32[]{:S(2)}) collective-permute-start(bf16[2,368,128]{2,1,0:T(8,128)(2,1)S(1)} %pad_maximum_fusion.refs_0_), channel_id=1, source_target_pairs={{0,4},{1,5},{2,6},{3,7},{4,0},{5,1},{6,2},{7,3},{8,12},{9,13},{10,... | collective-permute-start | bytes 565256 | tf_op jit(solution)/shard_map/ppermute | solution.py:288
  18.8 9.5 %collective-permute-start.11 = (bf16[2,368,128]{2,1,0:T(8,128)(2,1)S(1)}, bf16[2,368,128]{2,1,0:T(8,128)(2,1)S(1)}, u32[]{:S(2)}, u32[]{:S(2)}) collective-permute-start(bf16[2,368,128]{2,1,0:T(8,128)(2,1)S(1)} %pad_maximum_fusion.refs_0_), channel_id=1, source_target_pairs={{0,2},{1,3},{2,0},{3,1},{4,6},{5,7},{6,4},{7,5},{8,10},{9,11},{10,... | collective-permute-start | bytes 565256 | tf_op jit(solution)/shard_map/ppermute | solution.py:288
  27.8 9.4 %collective-permute-start.6 = (bf16[4,360,128]{2,1,0:T(8,128)(2,1)S(1)}, bf16[4,360,128]{2,1,0:T(8,128)(2,1)S(1)}, u32[]{:S(2)}, u32[]{:S(2)}) collective-permute-start(bf16[4,360,128]{2,1,0:T(8,128)(2,1)S(1)} %get-tuple-element.58), channel_id=1, source_target_pairs={{0,1},{1,0},{2,3},{3,2},{4,5},{5,4},{6,7},{7,6},{8,9},{9,8},{10,11... | collective-permute-start | bytes 1105928 | tf_op jit(solution)/shard_map/ppermute | solution.py:288
  27.8 3.5 %collective-permute-start.10 = (bf16[2,368,128]{2,1,0:T(8,128)(2,1)S(1)}, bf16[2,368,128]{2,1,0:T(8,128)(2,1)S(1)}, u32[]{:S(2)}, u32[]{:S(2)}) collective-permute-start(bf16[2,368,128]{2,1,0:T(8,128)(2,1)S(1)} %pad_maximum_fusion.refs_0_), channel_id=1, source_target_pairs={{0,1},{1,0},{2,3},{3,2},{4,5},{5,4},{6,7},{7,6},{8,9},{9,8},{10,11... | collective-permute-start | bytes 565256 | tf_op jit(solution)/shard_map/ppermute | solution.py:288
  28.3 3.0 %collective-permute-start.12 = (bf16[2,368,128]{2,1,0:T(8,128)(2,1)S(1)}, bf16[2,368,128]{2,1,0:T(8,128)(2,1)S(1)}, u32[]{:S(2)}, u32[]{:S(2)}) collective-permute-start(bf16[2,368,128]{2,1,0:T(8,128)(2,1)S(1)} %collective-permute-done.11.refs_2_), channel_id=1, source_target_pairs={{0,1},{1,0},{2,3},{3,2},{4,5},{5,4},{6,7},{7,6},{8,9},{9,8},{10,11... | collective-permute-start | bytes 565256 | tf_op jit(solution)/shard_map/ppermute | solution.py:288
  28.3 7.1 %collective-permute-start.8 = (bf16[2,368,128]{2,1,0:T(8,128)(2,1)S(1)}, bf16[2,368,128]{2,1,0:T(8,128)(2,1)S(1)}, u32[]{:S(2)}, u32[]{:S(2)}) collective-permute-start(bf16[2,368,128]{2,1,0:T(8,128)(2,1)S(1)} %collective-permute-done.3.refs_0_), channel_id=1, source_target_pairs={{0,2},{1,3},{2,0},{3,1},{4,6},{5,7},{6,4},{7,5},{8,10},{9,11},{10,... | collective-permute-start | bytes 565256 | tf_op jit(solution)/shard_map/ppermute | solution.py:288
  29.8 6.9 %collective-permute-start.9 = (bf16[2,368,128]{2,1,0:T(8,128)(2,1)S(1)}, bf16[2,368,128]{2,1,0:T(8,128)(2,1)S(1)}, u32[]{:S(2)}, u32[]{:S(2)}) collective-permute-start(bf16[2,368,128]{2,1,0:T(8,128)(2,1)S(1)} %collective-permute-done.refs_2_), channel_id=1, source_target_pairs={{0,4},{1,5},{2,6},{3,7},{4,0},{5,1},{6,2},{7,3},{8,12},{9,13},{10,... | collective-permute-start | bytes 565256 | tf_op jit(solution)/shard_map/ppermute | solution.py:288
  31.3 6.5 %collective-permute-start.7 = (bf16[2,368,128]{2,1,0:T(8,128)(2,1)S(1)}, bf16[2,368,128]{2,1,0:T(8,128)(2,1)S(1)}, u32[]{:S(2)}, u32[]{:S(2)}) collective-permute-start(bf16[2,368,128]{2,1,0:T(8,128)(2,1)S(1)} %collective-permute-done.3.refs_0_), channel_id=1, source_target_pairs={{0,1},{1,0},{2,3},{3,2},{4,5},{5,4},{6,7},{7,6},{8,9},{9,8},{10,11... | collective-permute-start | bytes 565256 | tf_op jit(solution)/shard_map/ppermute | solution.py:288
  36.7 1.4 %collective-permute-start.13 = (bf16[2,368,128]{2,1,0:T(8,128)(2,1)S(1)}, bf16[2,368,128]{2,1,0:T(8,128)(2,1)S(1)}, u32[]{:S(2)}, u32[]{:S(2)}) collective-permute-start(bf16[2,368,128]{2,1,0:T(8,128)(2,1)S(1)} %collective-permute-done.8.refs_2_), channel_id=1, source_target_pairs={{0,1},{1,0},{2,3},{3,2},{4,5},{5,4},{6,7},{7,6},{8,9},{9,8},{10,11... | collective-permute-start | bytes 565256 | tf_op jit(solution)/shard_map/ppermute | solution.py:288
  36.7 7.7 %collective-permute-start.17 = (bf16[4,360,128]{2,1,0:T(8,128)(2,1)S(1)}, bf16[4,360,128]{2,1,0:T(8,128)(2,1)S(1)}, u32[]{:S(2)}, u32[]{:S(2)}) collective-permute-start(bf16[4,360,128]{2,1,0:T(8,128)(2,1)S(1)} %get-tuple-element.73), channel_id=1, source_target_pairs={{0,1},{1,0},{2,3},{3,2},{4,5},{5,4},{6,7},{7,6},{8,9},{9,8},{10,11... | collective-permute-start | bytes 1105928 | tf_op jit(solution)/shard_map/ppermute | solution.py:288
  37.3 6.6 %collective-permute-start.14 = (bf16[2,360,128]{2,1,0:T(8,128)(2,1)S(1)}, bf16[2,360,128]{2,1,0:T(8,128)(2,1)S(1)}, u32[]{:S(2)}, u32[]{:S(2)}) collective-permute-start(bf16[2,360,128]{2,1,0:T(8,128)(2,1)S(1)} %add_convert_fusion.5), channel_id=1, source_target_pairs={{0,2},{1,3},{2,0},{3,1},{4,6},{5,7},{6,4},{7,5},{8,10},{9,11},{10,... | collective-permute-start | bytes 552968 | tf_op jit(solution)/shard_map/ppermute | solution.py:288
  37.8 7.2 %collective-permute-start.15 = (bf16[2,368,128]{2,1,0:T(8,128)(2,1)S(1)}, bf16[2,368,128]{2,1,0:T(8,128)(2,1)S(1)}, u32[]{:S(2)}, u32[]{:S(2)}) collective-permute-start(bf16[2,368,128]{2,1,0:T(8,128)(2,1)S(1)} %collective-permute-done.4.refs_0_), channel_id=1, source_target_pairs={{0,1},{1,0},{2,3},{3,2},{4,5},{5,4},{6,7},{7,6},{8,9},{9,8},{10,11... | collective-permute-start | bytes 565256 | tf_op jit(solution)/shard_map/ppermute | solution.py:288
  43.9 7.2 %collective-permute-start.23 = (bf16[4,360,128]{2,1,0:T(8,128)(2,1)S(1)}, bf16[4,360,128]{2,1,0:T(8,128)(2,1)S(1)}, u32[]{:S(2)}, u32[]{:S(2)}) collective-permute-start(bf16[4,360,128]{2,1,0:T(8,128)(2,1)S(1)} %get-tuple-element.78), channel_id=1, source_target_pairs={{0,1},{1,0},{2,3},{3,2},{4,5},{5,4},{6,7},{7,6},{8,9},{9,8},{10,11... | collective-permute-start | bytes 1105928 | tf_op jit(solution)/shard_map/ppermute | solution.py:288
  43.9 2.0 %collective-permute-start.16 = (bf16[2,368,128]{2,1,0:T(8,128)(2,1)S(1)}, bf16[2,368,128]{2,1,0:T(8,128)(2,1)S(1)}, u32[]{:S(2)}, u32[]{:S(2)}) collective-permute-start(bf16[2,368,128]{2,1,0:T(8,128)(2,1)S(1)} %collective-permute-done.9.refs_2_), channel_id=1, source_target_pairs={{0,1},{1,0},{2,3},{3,2},{4,5},{5,4},{6,7},{7,6},{8,9},{9,8},{10,11... | collective-permute-start | bytes 565256 | tf_op jit(solution)/shard_map/ppermute | solution.py:288
  44.4 6.6 %collective-permute-start.18 = (bf16[2,360,128]{2,1,0:T(8,128)(2,1)S(1)}, bf16[2,360,128]{2,1,0:T(8,128)(2,1)S(1)}, u32[]{:S(2)}, u32[]{:S(2)}) collective-permute-start(bf16[2,360,128]{2,1,0:T(8,128)(2,1)S(1)} %add_convert_fusion.4), channel_id=1, source_target_pairs={{0,2},{1,3},{2,0},{3,1},{4,6},{5,7},{6,4},{7,5},{8,10},{9,11},{10,... | collective-permute-start | bytes 552968 | tf_op jit(solution)/shard_map/ppermute | solution.py:288
  51.1 1.7 %collective-permute-start.19 = (bf16[4,360,128]{2,1,0:T(8,128)(2,1)S(1)}, bf16[4,360,128]{2,1,0:T(8,128)(2,1)S(1)}, u32[]{:S(2)}, u32[]{:S(2)}) collective-permute-start(bf16[4,360,128]{2,1,0:T(8,128)(2,1)S(1)} %get-tuple-element.75), channel_id=1, source_target_pairs={{0,1},{1,0},{2,3},{3,2},{4,5},{5,4},{6,7},{7,6},{8,9},{9,8},{10,11... | collective-permute-start | bytes 1105928 | tf_op jit(solution)/shard_map/ppermute | solution.py:288
  51.1 7.5 %collective-permute-start.24 = (bf16[2,360,128]{2,1,0:T(8,128)(2,1)S(1)}, bf16[2,360,128]{2,1,0:T(8,128)(2,1)S(1)}, u32[]{:S(2)}, u32[]{:S(2)}) collective-permute-start(bf16[2,360,128]{2,1,0:T(8,128)(2,1)S(1)} %add_convert_fusion.1), channel_id=1, source_target_pairs={{0,2},{1,3},{2,0},{3,1},{4,6},{5,7},{6,4},{7,5},{8,10},{9,11},{10,... | collective-permute-start | bytes 552968 | tf_op jit(solution)/shard_map/ppermute | solution.py:288
  52.8 9.4 %collective-permute-start.20 = (bf16[2,360,128]{2,1,0:T(8,128)(2,1)S(1)}, bf16[2,360,128]{2,1,0:T(8,128)(2,1)S(1)}, u32[]{:S(2)}, u32[]{:S(2)}) collective-permute-start(bf16[2,360,128]{2,1,0:T(8,128)(2,1)S(1)} %add_convert_fusion.3), channel_id=1, source_target_pairs={{0,2},{1,3},{2,0},{3,1},{4,6},{5,7},{6,4},{7,5},{8,10},{9,11},{10,... | collective-permute-start | bytes 552968 | tf_op jit(solution)/shard_map/ppermute | solution.py:288
  58.7 6.0 %collective-permute-start.25 = (bf16[2,360,128]{2,1,0:T(8,128)(2,1)S(1)}, bf16[2,360,128]{2,1,0:T(8,128)(2,1)S(1)}, u32[]{:S(2)}, u32[]{:S(2)}) collective-permute-start(bf16[2,360,128]{2,1,0:T(8,128)(2,1)S(1)} %add_convert_fusion), channel_id=1, source_target_pairs={{0,4},{1,5},{2,6},{3,7},{4,0},{5,1},{6,2},{7,3},{8,12},{9,13},{10,... | collective-permute-start | bytes 552968 | tf_op jit(solution)/shard_map/ppermute | solution.py:288
  62.3 6.3 %collective-permute-start.21 = (bf16[2,360,128]{2,1,0:T(8,128)(2,1)S(1)}, bf16[2,360,128]{2,1,0:T(8,128)(2,1)S(1)}, u32[]{:S(2)}, u32[]{:S(2)}) collective-permute-start(bf16[2,360,128]{2,1,0:T(8,128)(2,1)S(1)} %add_convert_fusion.2), channel_id=1, source_target_pairs={{0,4},{1,5},{2,6},{3,7},{4,0},{5,1},{6,2},{7,3},{8,12},{9,13},{10,... | collective-permute-start | bytes 552968 | tf_op jit(solution)/shard_map/ppermute | solution.py:288
  64.8 6.5 %collective-permute-start.27 = (bf16[360,128]{1,0:T(8,128)(2,1)S(1)}, bf16[360,128]{1,0:T(8,128)(2,1)S(1)}, u32[]{:S(2)}, u32[]{:S(2)}) collective-permute-start(bf16[360,128]{1,0:T(8,128)(2,1)S(1)} %get-tuple-element.80), channel_id=1, source_target_pairs={{0,24},{1,25},{2,26},{3,27},{4,28},{5,29},{6,30},{7,31},{8,16},{9,... | collective-permute-start | bytes 276488 | tf_op jit(solution)/shard_map/ppermute | solution.py:288
  66.4 8.4 %collective-permute-start.26 = (bf16[360,128]{1,0:T(8,128)(2,1)S(1)}, bf16[360,128]{1,0:T(8,128)(2,1)S(1)}, u32[]{:S(2)}, u32[]{:S(2)}) collective-permute-start(bf16[360,128]{1,0:T(8,128)(2,1)S(1)} %get-tuple-element.79), channel_id=1, source_target_pairs={{0,16},{1,17},{2,18},{3,19},{4,20},{5,21},{6,22},{7,23},{8,24},{9,... | collective-permute-start | bytes 276488 | tf_op jit(solution)/shard_map/ppermute | solution.py:288
  68.7 6.2 %collective-permute-start.22 = (bf16[360,128]{1,0:T(8,128)(2,1)S(1)}, bf16[360,128]{1,0:T(8,128)(2,1)S(1)}, u32[]{:S(2)}, u32[]{:S(2)}) collective-permute-start(bf16[360,128]{1,0:T(8,128)(2,1)S(1)} %fusion.3), channel_id=1, source_target_pairs={{0,8},{1,9},{2,10},{3,11},{4,12},{5,13},{6,14},{7,15},{8,0},{9,1},... | collective-permute-start | bytes 276488 | tf_op jit(solution)/shard_map/ppermute | solution.py:288

commit v9 on v6

--- a/solution.py
+++ b/solution.py
@@ -293,7 +293,7 @@
     )
     z_2, z_3 = swap(one, 2 * along_z), swap(one, 3 * along_z)
     x_0 = swap(near, along_x)
-    z_1 = swap(near, along_z)
+    z_1, x_1 = swap(near, along_z), swap(near, along_z + along_x)
     hidden_pad = round_up(gate_weight.shape[2], 128)
     wide = groups * round_up(quarter, 128)
     biases = jnp.concatenate([gate_bias, up_bias, down_bias], axis=0)
@@ -329,34 +329,33 @@
     keep_0, send_0 = run_expert(
         (near, far, x_0, swap(x_0, core)), pairs(0, 2), slots, weights, sizes, 1
     )
-    z_1, x_high, y_high, d_high, keep_0, send_0 = tied(
-        (z_1, x_high, y_high, d_high, keep_0, send_0)
-    )
-    x_1 = swap(z_1, along_x)
+    y_high, d_high, keep_0, send_0, z_1, x_1 = tied(
+        (y_high, d_high, keep_0, send_0, z_1, x_1)
+    )
     got_0 = swap(send_0, core)
     high = (z_high, swap(z_high, core), y_high, swap(y_high, core))
     high = high + (x_high, swap(x_high, core), d_high, swap(d_high, core))
-    z_1_core = swap(z_1, core)
-    got_0, z_1_core, high = tied((got_0, z_1_core, high))
+    got_0, high = tied((got_0, high))
     line = [[[(4 * x + k, n) for k in range(groups)] for x in range(2)] for n in range(2)]
     keep_2, send_2 = run_expert(high, line[0], slots, weights, sizes, 1)
     got_2 = swap(send_2, core)
     keep_2, high = tied((keep_2, high))
     keep_3, send_3 = run_expert(high, line[1], slots, weights, sizes, 1)
-    got_2, keep_3, x_1 = tied((got_2, keep_3, x_1))
+    got_2, keep_3, send_3 = tied((got_2, keep_3, send_3))
     got_3 = swap(send_3, core)
 
-    near_1 = (z_1, z_1_core, x_1, swap(x_1, core))
+    def outer(first, second, at):
+        return jnp.stack([add_up(keep[at], got[at]) for keep, got in (first, second)])
+
+    far_lines = ((keep_2, got_2), (keep_3, got_3))
+    y_sum, x_sum, d_sum = [outer(*far_lines, n) for n in (1, 2, 3)]
+    near_1 = (z_1, swap(z_1, core), x_1, swap(x_1, core))
+    y_sum, x_sum, d_sum, near_1, got_0 = tied((y_sum, x_sum, d_sum, near_1, got_0))
+    y_sum = swap(y_sum, along_y)
+    x_sum = swap(x_sum, along_x)
+    d_sum = swap(d_sum, diagonal)
     keep_1, send_1 = run_expert(near_1, pairs(0, 2), slots, weights, sizes, 1)
     got_1 = swap(send_1, core)
-    keep_1, got_3 = tied((keep_1, got_3))
-    def outer(first, second, at):
-        return jnp.stack([add_up(keep[at], got[at]) for keep, got in (first, second)])
-
-    far_lines = ((keep_2, got_2), (keep_3, got_3))
-    y_sum = swap(outer(*far_lines, 1), along_y)
-    x_sum = swap(outer(*far_lines, 2), along_x)
-    d_sum = swap(outer(*far_lines, 3), diagonal)
     line_2 = add_up(keep_2[0], got_2[0], x_sum[0], y_sum[0], d_sum[0])
     line_3 = add_up(keep_3[0], got_3[0], x_sum[1], y_sum[1], d_sum[1])
     back_2, back_3 = swap(line_2, 2 * along_z), swap(line_3, 3 * along_z)

time: 66.5 us -> 68.6 us (1.032)
  waiting for transfers between devices: 19.9 us -> 22.2 us
    ppermute x28, waiting for transfers between devices: 19.9 us -> 22.2 us  [swap(): lax.ppermute(array, ('seq', 'rep'), [(i, i ^ step) for i in range(devices)])]
  transfers between devices with their start and end apart: 28 -> 28, of which waited for: 12 -> 16; matrix products, arithmetic and copies ran while one was open for 2% -> 2% of each run, Pallas kernels for 15% -> 8%
where the time goes in v9:
time: 68.6 us; the launch traced here: 68.3 us
  starting transfers between devices  28.7 us (42%)
  waiting for transfers between devices  22.2 us (32%)
  Pallas kernels  12.3 us (18%)
  local copies, waits for them, and re-layouts  2.88 us (4%)
  other arithmetic  2.15 us (3%)
    ppermute x28, starting transfers between devices, swap(): lax.ppermute(array, ('seq', 'rep'), [(i, i ^ step) for i in range(devices)])  28.7 us
    ppermute x28, waiting for transfers between devices, swap(): lax.ppermute(array, ('seq', 'rep'), [(i, i ^ step) for i in range(devices)])  22.2 us
    pallas_call x4, Pallas kernels, run_expert(): pl.pallas_call(functools.partial(expert_kernel, quarter, per, blocks, slo...  8.79 us
    unnamed x10, local copies, waits for them, and re-layouts  2.88 us
    pallas_call x1, Pallas kernels, make_pieces(): pl.pallas_call(functools.partial(pieces_kernel, groups, per, experts), in...  2.3 us
  transfers between devices with their start and end apart: 28, of which 16 were waited for; matrix products, arithmetic and copies ran while one was open for 2% of the time, Pallas kernels for 8%

profile of v9, /device:TPU:0, one launch (start us, length us, event | category | flops | bytes accessed | tf_op | source)
XLA Modules:
  0.0 68.3 jit_solution(5964525180569993216)
XLA Ops:
  0.0 2.3 %shard_map.100 = (bf16[368,128]{1,0:T(8,128)(2,1)}, bf16[2,368,128]{2,1,0:T(8,128)(2,1)}, bf16[2,368,128]{2,1,0:T(8,128)(2,1)}) custom-call(bf16[1440,128]{1,0:T(8,128)(2,1)} %bitcast.29, f32[1440]{0:T(1024)} %refs_1_.1, s32[4,128]{1,0:T(4,128)} %bitcast.32, f32[4,128]{1,0:T(4,128)} %bitcast.33), custom_call_target="tpu_custom_call" | custom-call | tf_op jit(solution)/shard_map/pallas_call | solution.py:188
  2.3 3.0 %collective-permute-start.4 = (bf16[2,368,128]{2,1,0:T(8,128)(2,1)}, bf16[2,368,128]{2,1,0:T(8,128)(2,1)S(1)}, u32[]{:S(2)}, u32[]{:S(2)}) collective-permute-start(bf16[2,368,128]{2,1,0:T(8,128)(2,1)} %get-tuple-element.70.refs_0_), channel_id=1, source_target_pairs={{0,4},{1,5},{2,6},{3,7},{4,0},{5,1},{6,2},{7,3},{8,12},{9,13},{10,... | collective-permute-start | bytes 565256 | tf_op jit(solution)/shard_map/ppermute | solution.py:288
  5.3 2.6 %collective-permute-start = (bf16[368,128]{1,0:T(8,128)(2,1)}, bf16[368,128]{1,0:T(8,128)(2,1)S(1)}, u32[]{:S(2)}, u32[]{:S(2)}) collective-permute-start(bf16[368,128]{1,0:T(8,128)(2,1)} %get-tuple-element.65), channel_id=1, source_target_pairs={{0,16},{1,17},{2,18},{3,19},{4,20},{5,21},{6,22},{7,23},{8,24},{9,... | collective-permute-start | bytes 282632 | tf_op jit(solution)/shard_map/ppermute | solution.py:288
  7.9 1.3 %collective-permute-start.1 = (bf16[368,128]{1,0:T(8,128)(2,1)}, bf16[368,128]{1,0:T(8,128)(2,1)S(1)}, u32[]{:S(2)}, u32[]{:S(2)}) collective-permute-start(bf16[368,128]{1,0:T(8,128)(2,1)} %get-tuple-element.65), channel_id=1, source_target_pairs={{0,24},{1,25},{2,26},{3,27},{4,28},{5,29},{6,30},{7,31},{8,16},{9,... | collective-permute-start | bytes 282632 | tf_op jit(solution)/shard_map/ppermute | solution.py:288
  9.3 0.7 %pad_maximum_fusion.7.biases_ref = f32[3,360]{1,0:T(4,128)S(1)} fusion(f32[1,360]{1,0:T(1,128)} %param.19, f32[1,360]{1,0:T(1,128)} %param.17, f32[1,360]{1,0:T(1,128)} %param.15), kind=kLoop, calls=%fused_computation.30 | loop fusion | flops 2160 | bytes 8640 | tf_op jit(solution)/shard_map/concatenate | solution.py:299
  10.0 1.2 %copy-done.2 = bf16[1,360,1440]{2,1,0:T(8,128)(2,1)S(1)} copy-done((bf16[1,360,1440]{2,1,0:T(8,128)(2,1)S(1)}, bf16[1,360,1440]{2,1,0:T(8,128)(2,1)}, u32[]{:S(2)}) %copy-start.2) | copy-done | bytes 1036824
  11.2 0.4 shard_map.102
  11.8 0.4 copy-done.3
  12.4 1.8 %collective-permute-start.7 = (bf16[2,368,128]{2,1,0:T(8,128)(2,1)S(1)}, bf16[2,368,128]{2,1,0:T(8,128)(2,1)S(1)}, u32[]{:S(2)}, u32[]{:S(2)}) collective-permute-start(bf16[2,368,128]{2,1,0:T(8,128)(2,1)S(1)} %copy-done.3), channel_id=1, source_target_pairs={{0,12},{1,13},{2,14},{3,15},{4,8},{5,9},{6,10},{7,11},{8,4},{9,5},... | collective-permute-start | bytes 565256 | tf_op jit(solution)/shard_map/ppermute | solution.py:288
  14.2 1.2 %copy-done.1 = bf16[1,1440,360]{2,1,0:T(8,128)(2,1)S(1)} copy-done((bf16[1,1440,360]{2,1,0:T(8,128)(2,1)S(1)}, bf16[1,1440,360]{2,1,0:T(8,128)(2,1)}, u32[]{:S(2)}) %copy-start.1) | copy-done | bytes 1036824
  15.4 0.8 %shard_map.101 = (bf16[768,1536]{1,0:T(8,128)(2,1)S(1)}, f32[768,128]{1,0:T(8,128)S(1)}) custom-call(bf16[1440,360]{1,0:T(8,128)(2,1)S(1)} %bitcast.26, bf16[1440,360]{1,0:T(8,128)(2,1)S(1)} %bitcast.27, f32[3,360]{1,0:T(4,128)S(1)} %pad_maximum_fusion.7.biases_ref), custom_call_target="tpu_custom_call" | custom-call | bytes 8294400 | tf_op jit(solution)/shard_map/pallas_call | solution.py:116
  16.2 1.6 %collective-permute-start.2 = (bf16[2,368,128]{2,1,0:T(8,128)(2,1)S(1)}, bf16[2,368,128]{2,1,0:T(8,128)(2,1)S(1)}, u32[]{:S(2)}, u32[]{:S(2)}) collective-permute-start(bf16[2,368,128]{2,1,0:T(8,128)(2,1)S(1)} %pad_maximum_fusion.refs_0_), channel_id=1, source_target_pairs={{0,2},{1,3},{2,0},{3,1},{4,6},{5,7},{6,4},{7,5},{8,10},{9,11},{10,... | collective-permute-start | bytes 565256 | tf_op jit(solution)/shard_map/ppermute | solution.py:288
  17.8 1.4 %collective-permute-start.3 = (bf16[2,368,128]{2,1,0:T(8,128)(2,1)S(1)}, bf16[2,368,128]{2,1,0:T(8,128)(2,1)S(1)}, u32[]{:S(2)}, u32[]{:S(2)}) collective-permute-start(bf16[2,368,128]{2,1,0:T(8,128)(2,1)S(1)} %pad_maximum_fusion.refs_0_), channel_id=1, source_target_pairs={{0,6},{1,7},{2,4},{3,5},{4,2},{5,3},{6,0},{7,1},{8,14},{9,15},{10,... | collective-permute-start | bytes 565256 | tf_op jit(solution)/shard_map/ppermute | solution.py:288
  19.3 0.5 collective-permute-start.11
  19.8 2.2 %shard_map.103 = (bf16[4,360,128]{2,1,0:T(8,128)(2,1)S(1)}, bf16[4,360,128]{2,1,0:T(8,128)(2,1)S(1)}) custom-call(bf16[2,368,128]{2,1,0:T(8,128)(2,1)S(1)} %copy-done.3, bf16[2,368,128]{2,1,0:T(8,128)(2,1)S(1)} %copy-done.4, bf16[2,368,128]{2,1,0:T(8,128)(2,1)S(1)} %collective-permute-done.4.refs_2_, ...), custom_call_target="tpu_custom_call" | custom-call | flops 1811939328 | bytes 3538944 | tf_op jit(solution)/shard_map/pallas_call | solution.py:253
  22.0 1.2 %collective-permute-done.7.refs_2_ = bf16[2,368,128]{2,1,0:T(8,128)(2,1)S(1)} collective-permute-done((bf16[2,368,128]{2,1,0:T(8,128)(2,1)S(1)}, bf16[2,368,128]{2,1,0:T(8,128)(2,1)S(1)}, u32[]{:S(2)}, u32[]{:S(2)}) %collective-permute-start.7) | collective-permute-done | bytes 188448 | tf_op jit(solution)/shard_map/ppermute | solution.py:288
  23.2 5.0 %collective-permute-done.3.refs_6_ = bf16[2,368,128]{2,1,0:T(8,128)(2,1)S(1)} collective-permute-done((bf16[2,368,128]{2,1,0:T(8,128)(2,1)S(1)}, bf16[2,368,128]{2,1,0:T(8,128)(2,1)S(1)}, u32[]{:S(2)}, u32[]{:S(2)}) %collective-permute-start.3) | collective-permute-done | bytes 188448 | tf_op jit(solution)/shard_map/ppermute | solution.py:288
  28.2 0.5 collective-permute-start.9
  28.7 2.4 %collective-permute-done.11.refs_4_ = bf16[2,368,128]{2,1,0:T(8,128)(2,1)S(1)} collective-permute-done((bf16[2,368,128]{2,1,0:T(8,128)(2,1)S(1)}, bf16[2,368,128]{2,1,0:T(8,128)(2,1)S(1)}, u32[]{:S(2)}, u32[]{:S(2)}) %collective-permute-start.11) | collective-permute-done | bytes 188448 | tf_op jit(solution)/shard_map/ppermute | solution.py:288
  31.1 0.5 collective-permute-start.10
  31.6 0.9 %collective-permute-done.12.refs_5_ = bf16[2,368,128]{2,1,0:T(8,128)(2,1)S(1)} collective-permute-done((bf16[2,368,128]{2,1,0:T(8,128)(2,1)S(1)}, bf16[2,368,128]{2,1,0:T(8,128)(2,1)S(1)}, u32[]{:S(2)}, u32[]{:S(2)}) %collective-permute-start.12) | collective-permute-done | bytes 188448 | tf_op jit(solution)/shard_map/ppermute | solution.py:288
  32.5 0.3 collective-permute-done.10.refs_3_
  32.8 0.3 collective-permute-done.13.refs_7_
  33.1 2.2 %shard_map.104 = (bf16[4,360,128]{2,1,0:T(8,128)(2,1)S(1)}, bf16[4,360,128]{2,1,0:T(8,128)(2,1)S(1)}) custom-call(bf16[2,368,128]{2,1,0:T(8,128)(2,1)S(1)} %pad_maximum_fusion.refs_0_, bf16[2,368,128]{2,1,0:T(8,128)(2,1)S(1)} %collective-permute-done.9.refs_1_, bf16[2,368,128]{2,1,0:T(8,128)(2,1)S(1)} %collective-permute-done.2.refs_2_, ...), custom_call_target="tpu_custom_call" | custom-call | flops 1811939328 | bytes 3538944 | tf_op jit(solution)/shard_map/pallas_call | solution.py:253
  35.3 0.3 collective-permute-start.14
  35.6 2.2 %shard_map.105 = (bf16[4,360,128]{2,1,0:T(8,128)(2,1)S(1)}, bf16[4,360,128]{2,1,0:T(8,128)(2,1)S(1)}) custom-call(bf16[2,368,128]{2,1,0:T(8,128)(2,1)S(1)} %pad_maximum_fusion.refs_0_, bf16[2,368,128]{2,1,0:T(8,128)(2,1)S(1)} %collective-permute-done.9.refs_1_, bf16[2,368,128]{2,1,0:T(8,128)(2,1)S(1)} %collective-permute-done.2.refs_2_, ...), custom_call_target="tpu_custom_call" | custom-call | flops 1811939328 | bytes 3538944 | tf_op jit(solution)/shard_map/pallas_call | solution.py:253
  37.8 0.3 collective-permute-start.15
  38.4 0.3 collective-permute-start.17
  38.8 0.8 %collective-permute-done.15 = bf16[4,360,128]{2,1,0:T(8,128)(2,1)S(1)} collective-permute-done((bf16[4,360,128]{2,1,0:T(8,128)(2,1)S(1)}, bf16[4,360,128]{2,1,0:T(8,128)(2,1)S(1)}, u32[]{:S(2)}, u32[]{:S(2)}) %collective-permute-start.15) | collective-permute-done | bytes 368672 | tf_op jit(solution)/shard_map/ppermute | solution.py:288
  39.8 0.3 collective-permute-done.17.refs_3_
  40.1 2.2 %shard_map.106 = (bf16[4,360,128]{2,1,0:T(8,128)(2,1)S(1)}, bf16[4,360,128]{2,1,0:T(8,128)(2,1)S(1)}) custom-call(bf16[2,368,128]{2,1,0:T(8,128)(2,1)S(1)} %collective-permute-done.6.refs_0_, bf16[2,368,128]{2,1,0:T(8,128)(2,1)S(1)} %collective-permute-done.16.refs_1_, bf16[2,368,128]{2,1,0:T(8,128)(2,1)S(1)} %collective-permute-done.7.refs_2_, ...), custom_call_target="tpu_custom_call" | custom-call | flops 1811939328 | bytes 3538944 | tf_op jit(solution)/shard_map/pallas_call | solution.py:253
  42.3 0.3 collective-permute-start.21
  42.6 2.5 %collective-permute-start.20 = (bf16[2,360,128]{2,1,0:T(8,128)(2,1)S(1)}, bf16[2,360,128]{2,1,0:T(8,128)(2,1)S(1)}, u32[]{:S(2)}, u32[]{:S(2)}) collective-permute-start(bf16[2,360,128]{2,1,0:T(8,128)(2,1)S(1)} %pad_maximum_fusion.3), channel_id=1, source_target_pairs={{0,6},{1,7},{2,4},{3,5},{4,2},{5,3},{6,0},{7,1},{8,14},{9,15},{10,... | collective-permute-start | bytes 552968 | tf_op jit(solution)/shard_map/ppermute | solution.py:288
  45.1 0.5 collective-permute-start.19
  45.6 0.5 collective-permute-start.18
  46.3 1.6 %collective-permute-start.22 = (bf16[2,360,128]{2,1,0:T(8,128)(2,1)S(1)}, bf16[2,360,128]{2,1,0:T(8,128)(2,1)S(1)}, u32[]{:S(2)}, u32[]{:S(2)}) collective-permute-start(bf16[2,360,128]{2,1,0:T(8,128)(2,1)S(1)} %pad_maximum_fusion.4), channel_id=1, source_target_pairs={{0,4},{1,5},{2,6},{3,7},{4,0},{5,1},{6,2},{7,3},{8,12},{9,13},{10,... | collective-permute-start | bytes 552968 | tf_op jit(solution)/shard_map/ppermute | solution.py:288
  47.9 1.6 %collective-permute-start.23 = (bf16[2,360,128]{2,1,0:T(8,128)(2,1)S(1)}, bf16[2,360,128]{2,1,0:T(8,128)(2,1)S(1)}, u32[]{:S(2)}, u32[]{:S(2)}) collective-permute-start(bf16[2,360,128]{2,1,0:T(8,128)(2,1)S(1)} %pad_maximum_fusion.5), channel_id=1, source_target_pairs={{0,2},{1,3},{2,0},{3,1},{4,6},{5,7},{6,4},{7,5},{8,10},{9,11},{10,... | collective-permute-start | bytes 552968 | tf_op jit(solution)/shard_map/ppermute | solution.py:288
  49.6 1.5 %collective-permute-done.20 = bf16[2,360,128]{2,1,0:T(8,128)(2,1)S(1)} collective-permute-done((bf16[2,360,128]{2,1,0:T(8,128)(2,1)S(1)}, bf16[2,360,128]{2,1,0:T(8,128)(2,1)S(1)}, u32[]{:S(2)}, u32[]{:S(2)}) %collective-permute-start.20) | collective-permute-done | bytes 184352 | tf_op jit(solution)/shard_map/ppermute | solution.py:288
  51.1 2.5 %collective-permute-start.24 = (bf16[2,360,128]{2,1,0:T(8,128)(2,1)S(1)}, bf16[2,360,128]{2,1,0:T(8,128)(2,1)S(1)}, u32[]{:S(2)}, u32[]{:S(2)}) collective-permute-start(bf16[2,360,128]{2,1,0:T(8,128)(2,1)S(1)} %pad_maximum_fusion.6), channel_id=1, source_target_pairs={{0,6},{1,7},{2,4},{3,5},{4,2},{5,3},{6,0},{7,1},{8,14},{9,15},{10,... | collective-permute-start | bytes 552968 | tf_op jit(solution)/shard_map/ppermute | solution.py:288
  53.5 0.8 %collective-permute-done.19 = bf16[2,360,128]{2,1,0:T(8,128)(2,1)S(1)} collective-permute-done((bf16[2,360,128]{2,1,0:T(8,128)(2,1)S(1)}, bf16[2,360,128]{2,1,0:T(8,128)(2,1)S(1)}, u32[]{:S(2)}, u32[]{:S(2)}) %collective-permute-start.19) | collective-permute-done | bytes 184352 | tf_op jit(solution)/shard_map/ppermute | solution.py:288
  54.4 0.7 %collective-permute-done.18 = bf16[2,360,128]{2,1,0:T(8,128)(2,1)S(1)} collective-permute-done((bf16[2,360,128]{2,1,0:T(8,128)(2,1)S(1)}, bf16[2,360,128]{2,1,0:T(8,128)(2,1)S(1)}, u32[]{:S(2)}, u32[]{:S(2)}) %collective-permute-start.18) | collective-permute-done | bytes 184352 | tf_op jit(solution)/shard_map/ppermute | solution.py:288
  55.2 3.2 %collective-permute-start.27 = (bf16[360,128]{1,0:T(8,128)(2,1)S(1)}, bf16[360,128]{1,0:T(8,128)(2,1)S(1)}, u32[]{:S(2)}, u32[]{:S(2)}) collective-permute-start(bf16[360,128]{1,0:T(8,128)(2,1)S(1)} %get-tuple-element.138), channel_id=1, source_target_pairs={{0,24},{1,25},{2,26},{3,27},{4,28},{5,29},{6,30},{7,31},{8,16},{9,... | collective-permute-start | bytes 276488 | tf_op jit(solution)/shard_map/ppermute | solution.py:288
  58.5 0.6 collective-permute-done.22
  59.0 3.2 %collective-permute-done.24 = bf16[2,360,128]{2,1,0:T(8,128)(2,1)S(1)} collective-permute-done((bf16[2,360,128]{2,1,0:T(8,128)(2,1)S(1)}, bf16[2,360,128]{2,1,0:T(8,128)(2,1)S(1)}, u32[]{:S(2)}, u32[]{:S(2)}) %collective-permute-start.24) | collective-permute-done | bytes 184352 | tf_op jit(solution)/shard_map/ppermute | solution.py:288
  62.3 1.2 %collective-permute-start.25 = (bf16[360,128]{1,0:T(8,128)(2,1)S(1)}, bf16[360,128]{1,0:T(8,128)(2,1)S(1)}, u32[]{:S(2)}, u32[]{:S(2)}) collective-permute-start(bf16[360,128]{1,0:T(8,128)(2,1)S(1)} %fusion.5), channel_id=1, source_target_pairs={{0,8},{1,9},{2,10},{3,11},{4,12},{5,13},{6,14},{7,15},{8,0},{9,1},... | collective-permute-start | bytes 276488 | tf_op jit(solution)/shard_map/ppermute | solution.py:288
  63.5 2.4 %collective-permute-done.26 = bf16[360,128]{1,0:T(8,128)(2,1)S(1)} collective-permute-done((bf16[360,128]{1,0:T(8,128)(2,1)S(1)}, bf16[360,128]{1,0:T(8,128)(2,1)S(1)}, u32[]{:S(2)}, u32[]{:S(2)}) %collective-permute-start.26) | collective-permute-done | bytes 92192 | tf_op jit(solution)/shard_map/ppermute | solution.py:288
  65.9 1.7 %collective-permute-done.25 = bf16[360,128]{1,0:T(8,128)(2,1)S(1)} collective-permute-done((bf16[360,128]{1,0:T(8,128)(2,1)S(1)}, bf16[360,128]{1,0:T(8,128)(2,1)S(1)}, u32[]{:S(2)}, u32[]{:S(2)}) %collective-permute-start.25) | collective-permute-done | bytes 92192 | tf_op jit(solution)/shard_map/ppermute | solution.py:288
  67.6 0.7 %fusion.6 = bf16[128,360]{0,1:T(8,128)(2,1)} fusion(bf16[360,128]{1,0:T(8,128)(2,1)S(1)} %collective-permute-done.27, bf16[360,128]{1,0:T(8,128)(2,1)S(1)} %collective-permute-done.26, bf16[360,128]{1,0:T(8,128)(2,1)S(1)} %collective-permute-done.25, bf16[2,360,128]{2,1,0:T(8,128)(2,1)S(1)} %collective-permute-done.24, ...), kind=kLoop, calls=%fused_computation.29 | loop fusion | flops 737280 | bytes 829440 | tf_op jit(solution)/shard_map/transpose | solution.py:372
  (39 shorter events, 1.4 us)
Async XLA Ops:
  0.0 14.2 %copy-start = (bf16[1,1440,360]{2,1,0:T(8,128)(2,1)S(1)}, bf16[1,1440,360]{2,1,0:T(8,128)(2,1)}, u32[]{:S(2)}) copy-start(bf16[1,1440,360]{2,1,0:T(8,128)(2,1)} %param.14) | copy-start | bytes 3110404
  2.3 9.4 %collective-permute-start.4 = (bf16[2,368,128]{2,1,0:T(8,128)(2,1)}, bf16[2,368,128]{2,1,0:T(8,128)(2,1)S(1)}, u32[]{:S(2)}, u32[]{:S(2)}) collective-permute-start(bf16[2,368,128]{2,1,0:T(8,128)(2,1)} %get-tuple-element.70.refs_0_), channel_id=1, source_target_pairs={{0,4},{1,5},{2,6},{3,7},{4,0},{5,1},{6,2},{7,3},{8,12},{9,13},{10,... | collective-permute-start | bytes 565256 | tf_op jit(solution)/shard_map/ppermute | solution.py:288
  5.3 10.9 %collective-permute-start = (bf16[368,128]{1,0:T(8,128)(2,1)}, bf16[368,128]{1,0:T(8,128)(2,1)S(1)}, u32[]{:S(2)}, u32[]{:S(2)}) collective-permute-start(bf16[368,128]{1,0:T(8,128)(2,1)} %get-tuple-element.65), channel_id=1, source_target_pairs={{0,16},{1,17},{2,18},{3,19},{4,20},{5,21},{6,22},{7,23},{8,24},{9,... | collective-permute-start | bytes 282632 | tf_op jit(solution)/shard_map/ppermute | solution.py:288
  7.9 8.3 %collective-permute-start.1 = (bf16[368,128]{1,0:T(8,128)(2,1)}, bf16[368,128]{1,0:T(8,128)(2,1)S(1)}, u32[]{:S(2)}, u32[]{:S(2)}) collective-permute-start(bf16[368,128]{1,0:T(8,128)(2,1)} %get-tuple-element.65), channel_id=1, source_target_pairs={{0,24},{1,25},{2,26},{3,27},{4,28},{5,29},{6,30},{7,31},{8,16},{9,... | collective-permute-start | bytes 282632 | tf_op jit(solution)/shard_map/ppermute | solution.py:288
  10.0 1.2 %copy-start.2 = (bf16[1,360,1440]{2,1,0:T(8,128)(2,1)S(1)}, bf16[1,360,1440]{2,1,0:T(8,128)(2,1)}, u32[]{:S(2)}) copy-start(bf16[1,360,1440]{2,1,0:T(8,128)(2,1)} %param.18) | copy-start | bytes 3110404
  11.2 0.9 %copy-start.3 = (bf16[2,368,128]{2,1,0:T(8,128)(2,1)S(1)}, bf16[2,368,128]{2,1,0:T(8,128)(2,1)}, u32[]{:S(2)}) copy-start(bf16[2,368,128]{2,1,0:T(8,128)(2,1)} %get-tuple-element.70.refs_0_) | copy-start | bytes 565252
  11.7 7.6 %collective-permute-start.5 = (bf16[2,368,128]{2,1,0:T(8,128)(2,1)S(1)}, bf16[2,368,128]{2,1,0:T(8,128)(2,1)S(1)}, u32[]{:S(2)}, u32[]{:S(2)}) collective-permute-start(bf16[2,368,128]{2,1,0:T(8,128)(2,1)S(1)} %collective-permute-done.4.refs_2_), channel_id=1, source_target_pairs={{0,1},{1,0},{2,3},{3,2},{4,5},{5,4},{6,7},{7,6},{8,9},{9,8},{10,11... | collective-permute-start | bytes 565256 | tf_op jit(solution)/shard_map/ppermute | solution.py:288
  12.2 9.9 %collective-permute-start.6 = (bf16[2,368,128]{2,1,0:T(8,128)(2,1)S(1)}, bf16[2,368,128]{2,1,0:T(8,128)(2,1)S(1)}, u32[]{:S(2)}, u32[]{:S(2)}) collective-permute-start(bf16[2,368,128]{2,1,0:T(8,128)(2,1)S(1)} %copy-done.3), channel_id=1, source_target_pairs={{0,8},{1,9},{2,10},{3,11},{4,12},{5,13},{6,14},{7,15},{8,0},{9,1},... | collective-permute-start | bytes 565256 | tf_op jit(solution)/shard_map/ppermute | solution.py:288
  12.4 10.8 %collective-permute-start.7 = (bf16[2,368,128]{2,1,0:T(8,128)(2,1)S(1)}, bf16[2,368,128]{2,1,0:T(8,128)(2,1)S(1)}, u32[]{:S(2)}, u32[]{:S(2)}) collective-permute-start(bf16[2,368,128]{2,1,0:T(8,128)(2,1)S(1)} %copy-done.3), channel_id=1, source_target_pairs={{0,12},{1,13},{2,14},{3,15},{4,8},{5,9},{6,10},{7,11},{8,4},{9,5},... | collective-permute-start | bytes 565256 | tf_op jit(solution)/shard_map/ppermute | solution.py:288
  14.2 1.2 %copy-start.1 = (bf16[1,1440,360]{2,1,0:T(8,128)(2,1)S(1)}, bf16[1,1440,360]{2,1,0:T(8,128)(2,1)}, u32[]{:S(2)}) copy-start(bf16[1,1440,360]{2,1,0:T(8,128)(2,1)} %param.16) | copy-start | bytes 3110404
  15.4 4.4 %copy-start.4 = (bf16[2,368,128]{2,1,0:T(8,128)(2,1)S(1)}, bf16[2,368,128]{2,1,0:T(8,128)(2,1)}, u32[]{:S(2)}) copy-start(bf16[2,368,128]{2,1,0:T(8,128)(2,1)} %get-tuple-element.71.refs_1_) | copy-start | bytes 565252
  16.2 6.9 %collective-permute-start.2 = (bf16[2,368,128]{2,1,0:T(8,128)(2,1)S(1)}, bf16[2,368,128]{2,1,0:T(8,128)(2,1)S(1)}, u32[]{:S(2)}, u32[]{:S(2)}) collective-permute-start(bf16[2,368,128]{2,1,0:T(8,128)(2,1)S(1)} %pad_maximum_fusion.refs_0_), channel_id=1, source_target_pairs={{0,2},{1,3},{2,0},{3,1},{4,6},{5,7},{6,4},{7,5},{8,10},{9,11},{10,... | collective-permute-start | bytes 565256 | tf_op jit(solution)/shard_map/ppermute | solution.py:288
  17.8 10.4 %collective-permute-start.3 = (bf16[2,368,128]{2,1,0:T(8,128)(2,1)S(1)}, bf16[2,368,128]{2,1,0:T(8,128)(2,1)S(1)}, u32[]{:S(2)}, u32[]{:S(2)}) collective-permute-start(bf16[2,368,128]{2,1,0:T(8,128)(2,1)S(1)} %pad_maximum_fusion.refs_0_), channel_id=1, source_target_pairs={{0,6},{1,7},{2,4},{3,5},{4,2},{5,3},{6,0},{7,1},{8,14},{9,15},{10,... | collective-permute-start | bytes 565256 | tf_op jit(solution)/shard_map/ppermute | solution.py:288
  19.3 11.9 %collective-permute-start.11 = (bf16[2,368,128]{2,1,0:T(8,128)(2,1)S(1)}, bf16[2,368,128]{2,1,0:T(8,128)(2,1)S(1)}, u32[]{:S(2)}, u32[]{:S(2)}) collective-permute-start(bf16[2,368,128]{2,1,0:T(8,128)(2,1)S(1)} %pad_maximum_fusion.refs_0_), channel_id=1, source_target_pairs={{0,4},{1,5},{2,6},{3,7},{4,0},{5,1},{6,2},{7,3},{8,12},{9,13},{10,... | collective-permute-start | bytes 565256 | tf_op jit(solution)/shard_map/ppermute | solution.py:288
  28.2 4.9 %collective-permute-start.8 = (bf16[4,360,128]{2,1,0:T(8,128)(2,1)S(1)}, bf16[4,360,128]{2,1,0:T(8,128)(2,1)S(1)}, u32[]{:S(2)}, u32[]{:S(2)}) collective-permute-start(bf16[4,360,128]{2,1,0:T(8,128)(2,1)S(1)} %get-tuple-element.82), channel_id=1, source_target_pairs={{0,1},{1,0},{2,3},{3,2},{4,5},{5,4},{6,7},{7,6},{8,9},{9,8},{10,11... | collective-permute-start | bytes 1105928 | tf_op jit(solution)/shard_map/ppermute | solution.py:288
  28.2 3.4 %collective-permute-start.9 = (bf16[2,368,128]{2,1,0:T(8,128)(2,1)S(1)}, bf16[2,368,128]{2,1,0:T(8,128)(2,1)S(1)}, u32[]{:S(2)}, u32[]{:S(2)}) collective-permute-start(bf16[2,368,128]{2,1,0:T(8,128)(2,1)S(1)} %pad_maximum_fusion.refs_0_), channel_id=1, source_target_pairs={{0,1},{1,0},{2,3},{3,2},{4,5},{5,4},{6,7},{7,6},{8,9},{9,8},{10,11... | collective-permute-start | bytes 565256 | tf_op jit(solution)/shard_map/ppermute | solution.py:288
  31.1 1.4 %collective-permute-start.12 = (bf16[2,368,128]{2,1,0:T(8,128)(2,1)S(1)}, bf16[2,368,128]{2,1,0:T(8,128)(2,1)S(1)}, u32[]{:S(2)}, u32[]{:S(2)}) collective-permute-start(bf16[2,368,128]{2,1,0:T(8,128)(2,1)S(1)} %collective-permute-done.11.refs_4_), channel_id=1, source_target_pairs={{0,1},{1,0},{2,3},{3,2},{4,5},{5,4},{6,7},{7,6},{8,9},{9,8},{10,11... | collective-permute-start | bytes 565256 | tf_op jit(solution)/shard_map/ppermute | solution.py:288
  31.1 1.7 %collective-permute-start.10 = (bf16[2,368,128]{2,1,0:T(8,128)(2,1)S(1)}, bf16[2,368,128]{2,1,0:T(8,128)(2,1)S(1)}, u32[]{:S(2)}, u32[]{:S(2)}) collective-permute-start(bf16[2,368,128]{2,1,0:T(8,128)(2,1)S(1)} %collective-permute-done.2.refs_2_), channel_id=1, source_target_pairs={{0,1},{1,0},{2,3},{3,2},{4,5},{5,4},{6,7},{7,6},{8,9},{9,8},{10,11... | collective-permute-start | bytes 565256 | tf_op jit(solution)/shard_map/ppermute | solution.py:288
  31.6 1.5 %collective-permute-start.13 = (bf16[2,368,128]{2,1,0:T(8,128)(2,1)S(1)}, bf16[2,368,128]{2,1,0:T(8,128)(2,1)S(1)}, u32[]{:S(2)}, u32[]{:S(2)}) collective-permute-start(bf16[2,368,128]{2,1,0:T(8,128)(2,1)S(1)} %collective-permute-done.3.refs_6_), channel_id=1, source_target_pairs={{0,1},{1,0},{2,3},{3,2},{4,5},{5,4},{6,7},{7,6},{8,9},{9,8},{10,11... | collective-permute-start | bytes 565256 | tf_op jit(solution)/shard_map/ppermute | solution.py:288
  35.3 2.5 %collective-permute-start.14 = (bf16[4,360,128]{2,1,0:T(8,128)(2,1)S(1)}, bf16[4,360,128]{2,1,0:T(8,128)(2,1)S(1)}, u32[]{:S(2)}, u32[]{:S(2)}) collective-permute-start(bf16[4,360,128]{2,1,0:T(8,128)(2,1)S(1)} %get-tuple-element.95), channel_id=1, source_target_pairs={{0,1},{1,0},{2,3},{3,2},{4,5},{5,4},{6,7},{7,6},{8,9},{9,8},{10,11... | collective-permute-start | bytes 1105928 | tf_op jit(solution)/shard_map/ppermute | solution.py:288
  37.8 1.8 %collective-permute-start.15 = (bf16[4,360,128]{2,1,0:T(8,128)(2,1)S(1)}, bf16[4,360,128]{2,1,0:T(8,128)(2,1)S(1)}, u32[]{:S(2)}, u32[]{:S(2)}) collective-permute-start(bf16[4,360,128]{2,1,0:T(8,128)(2,1)S(1)} %get-tuple-element.108), channel_id=1, source_target_pairs={{0,1},{1,0},{2,3},{3,2},{4,5},{5,4},{6,7},{7,6},{8,9},{9,8},{10,11... | collective-permute-start | bytes 1105928 | tf_op jit(solution)/shard_map/ppermute | solution.py:288
  38.1 1.7 %collective-permute-start.16 = (bf16[2,368,128]{2,1,0:T(8,128)(2,1)S(1)}, bf16[2,368,128]{2,1,0:T(8,128)(2,1)S(1)}, u32[]{:S(2)}, u32[]{:S(2)}) collective-permute-start(bf16[2,368,128]{2,1,0:T(8,128)(2,1)S(1)} %collective-permute-done.6.refs_0_), channel_id=1, source_target_pairs={{0,1},{1,0},{2,3},{3,2},{4,5},{5,4},{6,7},{7,6},{8,9},{9,8},{10,11... | collective-permute-start | bytes 565256 | tf_op jit(solution)/shard_map/ppermute | solution.py:288
  38.4 1.7 %collective-permute-start.17 = (bf16[2,368,128]{2,1,0:T(8,128)(2,1)S(1)}, bf16[2,368,128]{2,1,0:T(8,128)(2,1)S(1)}, u32[]{:S(2)}, u32[]{:S(2)}) collective-permute-start(bf16[2,368,128]{2,1,0:T(8,128)(2,1)S(1)} %collective-permute-done.7.refs_2_), channel_id=1, source_target_pairs={{0,1},{1,0},{2,3},{3,2},{4,5},{5,4},{6,7},{7,6},{8,9},{9,8},{10,11... | collective-permute-start | bytes 565256 | tf_op jit(solution)/shard_map/ppermute | solution.py:288
  42.3 3.9 %collective-permute-start.21 = (bf16[4,360,128]{2,1,0:T(8,128)(2,1)S(1)}, bf16[4,360,128]{2,1,0:T(8,128)(2,1)S(1)}, u32[]{:S(2)}, u32[]{:S(2)}) collective-permute-start(bf16[4,360,128]{2,1,0:T(8,128)(2,1)S(1)} %get-tuple-element.121), channel_id=1, source_target_pairs={{0,1},{1,0},{2,3},{3,2},{4,5},{5,4},{6,7},{7,6},{8,9},{9,8},{10,11... | collective-permute-start | bytes 1105928 | tf_op jit(solution)/shard_map/ppermute | solution.py:288
  42.6 8.4 %collective-permute-start.20 = (bf16[2,360,128]{2,1,0:T(8,128)(2,1)S(1)}, bf16[2,360,128]{2,1,0:T(8,128)(2,1)S(1)}, u32[]{:S(2)}, u32[]{:S(2)}) collective-permute-start(bf16[2,360,128]{2,1,0:T(8,128)(2,1)S(1)} %pad_maximum_fusion.3), channel_id=1, source_target_pairs={{0,6},{1,7},{2,4},{3,5},{4,2},{5,3},{6,0},{7,1},{8,14},{9,15},{10,... | collective-permute-start | bytes 552968 | tf_op jit(solution)/shard_map/ppermute | solution.py:288
  45.1 9.3 %collective-permute-start.19 = (bf16[2,360,128]{2,1,0:T(8,128)(2,1)S(1)}, bf16[2,360,128]{2,1,0:T(8,128)(2,1)S(1)}, u32[]{:S(2)}, u32[]{:S(2)}) collective-permute-start(bf16[2,360,128]{2,1,0:T(8,128)(2,1)S(1)} %get-tuple-element.114), channel_id=1, source_target_pairs={{0,2},{1,3},{2,0},{3,1},{4,6},{5,7},{6,4},{7,5},{8,10},{9,11},{10,... | collective-permute-start | bytes 552968 | tf_op jit(solution)/shard_map/ppermute | solution.py:288
  45.6 9.5 %collective-permute-start.18 = (bf16[2,360,128]{2,1,0:T(8,128)(2,1)S(1)}, bf16[2,360,128]{2,1,0:T(8,128)(2,1)S(1)}, u32[]{:S(2)}, u32[]{:S(2)}) collective-permute-start(bf16[2,360,128]{2,1,0:T(8,128)(2,1)S(1)} %get-tuple-element.113), channel_id=1, source_target_pairs={{0,4},{1,5},{2,6},{3,7},{4,0},{5,1},{6,2},{7,3},{8,12},{9,13},{10,... | collective-permute-start | bytes 552968 | tf_op jit(solution)/shard_map/ppermute | solution.py:288
  46.3 12.7 %collective-permute-start.22 = (bf16[2,360,128]{2,1,0:T(8,128)(2,1)S(1)}, bf16[2,360,128]{2,1,0:T(8,128)(2,1)S(1)}, u32[]{:S(2)}, u32[]{:S(2)}) collective-permute-start(bf16[2,360,128]{2,1,0:T(8,128)(2,1)S(1)} %pad_maximum_fusion.4), channel_id=1, source_target_pairs={{0,4},{1,5},{2,6},{3,7},{4,0},{5,1},{6,2},{7,3},{8,12},{9,13},{10,... | collective-permute-start | bytes 552968 | tf_op jit(solution)/shard_map/ppermute | solution.py:288
  47.9 11.1 %collective-permute-start.23 = (bf16[2,360,128]{2,1,0:T(8,128)(2,1)S(1)}, bf16[2,360,128]{2,1,0:T(8,128)(2,1)S(1)}, u32[]{:S(2)}, u32[]{:S(2)}) collective-permute-start(bf16[2,360,128]{2,1,0:T(8,128)(2,1)S(1)} %pad_maximum_fusion.5), channel_id=1, source_target_pairs={{0,2},{1,3},{2,0},{3,1},{4,6},{5,7},{6,4},{7,5},{8,10},{9,11},{10,... | collective-permute-start | bytes 552968 | tf_op jit(solution)/shard_map/ppermute | solution.py:288
  51.1 11.2 %collective-permute-start.24 = (bf16[2,360,128]{2,1,0:T(8,128)(2,1)S(1)}, bf16[2,360,128]{2,1,0:T(8,128)(2,1)S(1)}, u32[]{:S(2)}, u32[]{:S(2)}) collective-permute-start(bf16[2,360,128]{2,1,0:T(8,128)(2,1)S(1)} %pad_maximum_fusion.6), channel_id=1, source_target_pairs={{0,6},{1,7},{2,4},{3,5},{4,2},{5,3},{6,0},{7,1},{8,14},{9,15},{10,... | collective-permute-start | bytes 552968 | tf_op jit(solution)/shard_map/ppermute | solution.py:288
  55.2 8.3 %collective-permute-start.27 = (bf16[360,128]{1,0:T(8,128)(2,1)S(1)}, bf16[360,128]{1,0:T(8,128)(2,1)S(1)}, u32[]{:S(2)}, u32[]{:S(2)}) collective-permute-start(bf16[360,128]{1,0:T(8,128)(2,1)S(1)} %get-tuple-element.138), channel_id=1, source_target_pairs={{0,24},{1,25},{2,26},{3,27},{4,28},{5,29},{6,30},{7,31},{8,16},{9,... | collective-permute-start | bytes 276488 | tf_op jit(solution)/shard_map/ppermute | solution.py:288
  58.5 7.4 %collective-permute-start.26 = (bf16[360,128]{1,0:T(8,128)(2,1)S(1)}, bf16[360,128]{1,0:T(8,128)(2,1)S(1)}, u32[]{:S(2)}, u32[]{:S(2)}) collective-permute-start(bf16[360,128]{1,0:T(8,128)(2,1)S(1)} %get-tuple-element.137), channel_id=1, source_target_pairs={{0,16},{1,17},{2,18},{3,19},{4,20},{5,21},{6,22},{7,23},{8,24},{9,... | collective-permute-start | bytes 276488 | tf_op jit(solution)/shard_map/ppermute | solution.py:288
  62.3 5.3 %collective-permute-start.25 = (bf16[360,128]{1,0:T(8,128)(2,1)S(1)}, bf16[360,128]{1,0:T(8,128)(2,1)S(1)}, u32[]{:S(2)}, u32[]{:S(2)}) collective-permute-start(bf16[360,128]{1,0:T(8,128)(2,1)S(1)} %fusion.5), channel_id=1, source_target_pairs={{0,8},{1,9},{2,10},{3,11},{4,12},{5,13},{6,14},{7,15},{8,0},{9,1},... | collective-permute-start | bytes 276488 | tf_op jit(solution)/shard_map/ppermute | solution.py:288

commit v10 on v9

--- a/solution.py
+++ b/solution.py
@@ -293,7 +293,6 @@
     )
     z_2, z_3 = swap(one, 2 * along_z), swap(one, 3 * along_z)
     x_0 = swap(near, along_x)
-    z_1, x_1 = swap(near, along_z), swap(near, along_z + along_x)
     hidden_pad = round_up(gate_weight.shape[2], 128)
     wide = groups * round_up(quarter, 128)
     biases = jnp.concatenate([gate_bias, up_bias, down_bias], axis=0)
@@ -329,13 +328,18 @@
     keep_0, send_0 = run_expert(
         (near, far, x_0, swap(x_0, core)), pairs(0, 2), slots, weights, sizes, 1
     )
-    y_high, d_high, keep_0, send_0, z_1, x_1 = tied(
-        (y_high, d_high, keep_0, send_0, z_1, x_1)
+    z_near = swap(jnp.concatenate([near, x_0], axis=0), along_z)
+    x_high, y_high, d_high, keep_0, send_0, z_near = tied(
+        (x_high, y_high, d_high, keep_0, send_0, z_near)
     )
     got_0 = swap(send_0, core)
     high = (z_high, swap(z_high, core), y_high, swap(y_high, core))
     high = high + (x_high, swap(x_high, core), d_high, swap(d_high, core))
-    got_0, high = tied((got_0, high))
+    near_1 = (z_near, swap(z_near, core))
+    blocks = [[(k % 2, 2 * x + k // 2) for k in range(groups)] for x in range(2)]
+    keep_1, send_1 = run_expert(near_1, blocks, slots, weights, sizes, 1)
+    got_0, high, keep_1, send_1 = tied((got_0, high, keep_1, send_1))
+    got_1 = swap(send_1, core)
     line = [[[(4 * x + k, n) for k in range(groups)] for x in range(2)] for n in range(2)]
     keep_2, send_2 = run_expert(high, line[0], slots, weights, sizes, 1)
     got_2 = swap(send_2, core)
@@ -343,32 +347,23 @@
     keep_3, send_3 = run_expert(high, line[1], slots, weights, sizes, 1)
     got_2, keep_3, send_3 = tied((got_2, keep_3, send_3))
     got_3 = swap(send_3, core)
-
-    def outer(first, second, at):
-        return jnp.stack([add_up(keep[at], got[at]) for keep, got in (first, second)])
-
-    far_lines = ((keep_2, got_2), (keep_3, got_3))
-    y_sum, x_sum, d_sum = [outer(*far_lines, n) for n in (1, 2, 3)]
-    near_1 = (z_1, swap(z_1, core), x_1, swap(x_1, core))
-    y_sum, x_sum, d_sum, near_1, got_0 = tied((y_sum, x_sum, d_sum, near_1, got_0))
-    y_sum = swap(y_sum, along_y)
-    x_sum = swap(x_sum, along_x)
-    d_sum = swap(d_sum, diagonal)
-    keep_1, send_1 = run_expert(near_1, pairs(0, 2), slots, weights, sizes, 1)
-    got_1 = swap(send_1, core)
-    line_2 = add_up(keep_2[0], got_2[0], x_sum[0], y_sum[0], d_sum[0])
-    line_3 = add_up(keep_3[0], got_3[0], x_sum[1], y_sum[1], d_sum[1])
+    got_1, got_3 = tied((got_1, got_3))
+    z_back = swap(add_up(keep_1, got_1), along_z)
+
+    def spread(*terms):
+        return [add_up(*[term[n] for term in terms]) for n in (1, 2, 3)]
+
+    def gather(parts):
+        return [swap(part, step) for part, step in zip(parts, (along_y, along_x, diagonal))]
+
+    far_sums = [jnp.stack(pair) for pair in zip(spread(keep_2, got_2), spread(keep_3, got_3))]
+    far_sums = gather(far_sums)
+    line_2 = add_up(keep_2[0], got_2[0], *[part[0] for part in far_sums])
+    line_3 = add_up(keep_3[0], got_3[0], *[part[1] for part in far_sums])
     back_2, back_3 = swap(line_2, 2 * along_z), swap(line_3, 3 * along_z)
-    near_lines = ((keep_0, got_0), (keep_1, got_1))
-    x_near = swap(outer(*near_lines, 2), along_x)
-    y_near = swap(outer(*near_lines, 1), along_y)
-    d_near = swap(outer(*near_lines, 3), diagonal)
-    _, _, x_near, y_near, d_near = tied((line_2, line_3, x_near, y_near, d_near))
-    line_1 = add_up(keep_1[0], got_1[0], x_near[1], y_near[1], d_near[1])
-    back_1 = swap(line_1, along_z)
-    mixed = add_up(
-        keep_0[0], got_0[0], x_near[0], y_near[0], d_near[0], back_1, back_2, back_3
-    )
+    z_back, _, _ = tied((z_back, line_2, line_3))
+    near_sums = gather(spread(keep_0, got_0, z_back))
+    mixed = add_up(keep_0[0], got_0[0], z_back[0], *near_sums, back_2, back_3)
     return mixed.T
 
 

time: 68.6 us -> 62.3 us (0.908)
  starting transfers between devices: 28.7 us -> 22.8 us
  local copies, waits for them, and re-layouts: 2.88 us -> 1.26 us
  other arithmetic: 2.15 us -> 3 us
    ppermute x28 -> x26, starting transfers between devices: 28.7 us -> 22.8 us  [swap(): lax.ppermute(array, ('seq', 'rep'), [(i, i ^ step) for i in range(devices)])]
    unnamed x10, local copies, waits for them, and re-layouts: 2.88 us -> 1.26 us
    concatenate x0 -> x1, other arithmetic: none -> 0.96 us  [dense(): z_near = swap(jnp.concatenate([near, x_0], axis=0), along_z)]
    ppermute x28 -> x26, waiting for transfers between devices: 22.2 us -> 22.4 us  [swap(): lax.ppermute(array, ('seq', 'rep'), [(i, i ^ step) for i in range(devices)])]
  transfers between devices with their start and end apart: 28 -> 26, of which waited for: 16 -> 12; matrix products, arithmetic and copies ran while one was open for 2% -> 3% of each run, Pallas kernels for 8% -> 13%
where the time goes in v10:
time: 62.3 us; the launch traced here: 62.1 us
  starting transfers between devices  22.8 us (37%)
  waiting for transfers between devices  22.4 us (36%)
  Pallas kernels  12.4 us (20%)
  other arithmetic  3 us (5%)
  local copies, waits for them, and re-layouts  1.26 us (2%)
    ppermute x26, starting transfers between devices, swap(): lax.ppermute(array, ('seq', 'rep'), [(i, i ^ step) for i in range(devices)])  22.8 us
    ppermute x26, waiting for transfers between devices, swap(): lax.ppermute(array, ('seq', 'rep'), [(i, i ^ step) for i in range(devices)])  22.4 us
    pallas_call x4, Pallas kernels, run_expert(): pl.pallas_call(functools.partial(expert_kernel, quarter, per, blocks, slo...  8.8 us
    pallas_call x1, Pallas kernels, make_pieces(): pl.pallas_call(functools.partial(pieces_kernel, groups, per, experts), in...  2.35 us
    unnamed x10, local copies, waits for them, and re-layouts  1.26 us
  transfers between devices with their start and end apart: 26, of which 12 were waited for; matrix products, arithmetic and copies ran while one was open for 3% of the time, Pallas kernels for 13%

profile of v10, /device:TPU:0, one launch (start us, length us, event | category | flops | bytes accessed | tf_op | source)
XLA Modules:
  0.0 62.1 jit_solution(18345512223201652016)
XLA Ops:
  0.0 2.4 %shard_map.100 = (bf16[368,128]{1,0:T(8,128)(2,1)}, bf16[2,368,128]{2,1,0:T(8,128)(2,1)}, bf16[2,368,128]{2,1,0:T(8,128)(2,1)}) custom-call(bf16[1440,128]{1,0:T(8,128)(2,1)} %bitcast.37, f32[1440]{0:T(1024)} %refs_1_.1, s32[4,128]{1,0:T(4,128)} %bitcast.40, f32[4,128]{1,0:T(4,128)} %bitcast.41), custom_call_target="tpu_custom_call" | custom-call | tf_op jit(solution)/shard_map/pallas_call | solution.py:188
  2.4 3.0 %collective-permute-start.5 = (bf16[2,368,128]{2,1,0:T(8,128)(2,1)}, bf16[2,368,128]{2,1,0:T(8,128)(2,1)S(1)}, u32[]{:S(2)}, u32[]{:S(2)}) collective-permute-start(bf16[2,368,128]{2,1,0:T(8,128)(2,1)} %get-tuple-element.64.refs_0_), channel_id=1, source_target_pairs={{0,4},{1,5},{2,6},{3,7},{4,0},{5,1},{6,2},{7,3},{8,12},{9,13},{10,... | collective-permute-start | bytes 565256 | tf_op jit(solution)/shard_map/ppermute | solution.py:288
  5.4 3.6 %collective-permute-start.1 = (bf16[368,128]{1,0:T(8,128)(2,1)}, bf16[368,128]{1,0:T(8,128)(2,1)S(1)}, u32[]{:S(2)}, u32[]{:S(2)}) collective-permute-start(bf16[368,128]{1,0:T(8,128)(2,1)} %get-tuple-element.59), channel_id=1, source_target_pairs={{0,24},{1,25},{2,26},{3,27},{4,28},{5,29},{6,30},{7,31},{8,16},{9,... | collective-permute-start | bytes 282632 | tf_op jit(solution)/shard_map/ppermute | solution.py:288
  9.0 0.7 %pad_maximum_fusion.5.biases_ref = f32[3,360]{1,0:T(4,128)S(1)} fusion(f32[1,360]{1,0:T(1,128)} %param.19, f32[1,360]{1,0:T(1,128)} %param.17, f32[1,360]{1,0:T(1,128)} %param.15), kind=kLoop, calls=%fused_computation.29 | loop fusion | flops 2160 | bytes 8640 | tf_op jit(solution)/shard_map/concatenate | solution.py:298
  9.7 1.2 %copy-done.2 = bf16[1,360,1440]{2,1,0:T(8,128)(2,1)S(1)} copy-done((bf16[1,360,1440]{2,1,0:T(8,128)(2,1)S(1)}, bf16[1,360,1440]{2,1,0:T(8,128)(2,1)}, u32[]{:S(2)}) %copy-start.2) | copy-done | bytes 1036824
  11.0 0.4 shard_map.102
  11.4 1.0 %pad_maximum_fusion = bf16[4,368,128]{2,1,0:T(8,128)(2,1)S(1)} fusion(bf16[2,368,128]{2,1,0:T(8,128)(2,1)S(1)} %collective-permute-done.5.refs_2_, bf16[2,368,128]{2,1,0:T(8,128)(2,1)} %get-tuple-element.64.refs_0_), kind=kLoop, calls=%fused_computation.1 | loop fusion | flops 188416 | bytes 753664 | tf_op jit(solution)/shard_map/concatenate | solution.py:331
  12.4 0.8 %collective-permute-start.7 = (bf16[4,368,128]{2,1,0:T(8,128)(2,1)S(1)}, bf16[4,368,128]{2,1,0:T(8,128)(2,1)S(1)}, u32[]{:S(2)}, u32[]{:S(2)}) collective-permute-start(bf16[4,368,128]{2,1,0:T(8,128)(2,1)S(1)} %pad_maximum_fusion), channel_id=1, source_target_pairs={{0,8},{1,9},{2,10},{3,11},{4,12},{5,13},{6,14},{7,15},{8,0},{9,1},... | collective-permute-start | bytes 1130504 | tf_op jit(solution)/shard_map/ppermute | solution.py:288
  13.3 0.8 %shard_map.101 = (bf16[768,1536]{1,0:T(8,128)(2,1)S(1)}, f32[768,128]{1,0:T(8,128)S(1)}) custom-call(bf16[1440,360]{1,0:T(8,128)(2,1)S(1)} %bitcast.34, bf16[1440,360]{1,0:T(8,128)(2,1)S(1)} %bitcast.35, f32[3,360]{1,0:T(4,128)S(1)} %pad_maximum_fusion.5.biases_ref), custom_call_target="tpu_custom_call" | custom-call | bytes 8294400 | tf_op jit(solution)/shard_map/pallas_call | solution.py:116
  14.1 2.9 %collective-permute-done = bf16[368,128]{1,0:T(8,128)(2,1)S(1)} collective-permute-done((bf16[368,128]{1,0:T(8,128)(2,1)}, bf16[368,128]{1,0:T(8,128)(2,1)S(1)}, u32[]{:S(2)}, u32[]{:S(2)}) %collective-permute-start) | collective-permute-done | bytes 94240 | tf_op jit(solution)/shard_map/ppermute | solution.py:288
  17.0 1.6 %collective-permute-start.4 = (bf16[2,368,128]{2,1,0:T(8,128)(2,1)S(1)}, bf16[2,368,128]{2,1,0:T(8,128)(2,1)S(1)}, u32[]{:S(2)}, u32[]{:S(2)}) collective-permute-start(bf16[2,368,128]{2,1,0:T(8,128)(2,1)S(1)} %pad_maximum_fusion.1.refs_0_), channel_id=1, source_target_pairs={{0,6},{1,7},{2,4},{3,5},{4,2},{5,3},{6,0},{7,1},{8,14},{9,15},{10,... | collective-permute-start | bytes 565256 | tf_op jit(solution)/shard_map/ppermute | solution.py:288
  18.5 0.5 collective-permute-start.3
  19.0 1.5 %collective-permute-start.2 = (bf16[2,368,128]{2,1,0:T(8,128)(2,1)S(1)}, bf16[2,368,128]{2,1,0:T(8,128)(2,1)S(1)}, u32[]{:S(2)}, u32[]{:S(2)}) collective-permute-start(bf16[2,368,128]{2,1,0:T(8,128)(2,1)S(1)} %pad_maximum_fusion.1.refs_0_), channel_id=1, source_target_pairs={{0,4},{1,5},{2,6},{3,7},{4,0},{5,1},{6,2},{7,3},{8,12},{9,13},{10,... | collective-permute-start | bytes 565256 | tf_op jit(solution)/shard_map/ppermute | solution.py:288
  20.5 2.2 %shard_map.103 = (bf16[4,360,128]{2,1,0:T(8,128)(2,1)S(1)}, bf16[4,360,128]{2,1,0:T(8,128)(2,1)S(1)}) custom-call(bf16[2,368,128]{2,1,0:T(8,128)(2,1)S(1)} %copy-done.3, bf16[2,368,128]{2,1,0:T(8,128)(2,1)S(1)} %copy-done.4, bf16[2,368,128]{2,1,0:T(8,128)(2,1)S(1)} %collective-permute-done.5.refs_2_, ...), custom_call_target="tpu_custom_call" | custom-call | flops 1811939328 | bytes 3538944 | tf_op jit(solution)/shard_map/pallas_call | solution.py:253
  22.7 2.9 %collective-permute-done.4.refs_6_ = bf16[2,368,128]{2,1,0:T(8,128)(2,1)S(1)} collective-permute-done((bf16[2,368,128]{2,1,0:T(8,128)(2,1)S(1)}, bf16[2,368,128]{2,1,0:T(8,128)(2,1)S(1)}, u32[]{:S(2)}, u32[]{:S(2)}) %collective-permute-start.4) | collective-permute-done | bytes 188448 | tf_op jit(solution)/shard_map/ppermute | solution.py:288
  25.6 2.2 %collective-permute-done.3.refs_2_ = bf16[2,368,128]{2,1,0:T(8,128)(2,1)S(1)} collective-permute-done((bf16[2,368,128]{2,1,0:T(8,128)(2,1)S(1)}, bf16[2,368,128]{2,1,0:T(8,128)(2,1)S(1)}, u32[]{:S(2)}, u32[]{:S(2)}) %collective-permute-start.3) | collective-permute-done | bytes 188448 | tf_op jit(solution)/shard_map/ppermute | solution.py:288
  27.8 0.1 collective-permute-done.2.refs_4_
  27.9 0.5 collective-permute-start.8
  28.4 0.5 collective-permute-start.10
  29.0 0.7 %collective-permute-done.13.refs_1_ = bf16[4,368,128]{2,1,0:T(8,128)(2,1)S(1)} collective-permute-done((bf16[4,368,128]{2,1,0:T(8,128)(2,1)S(1)}, bf16[4,368,128]{2,1,0:T(8,128)(2,1)S(1)}, u32[]{:S(2)}, u32[]{:S(2)}) %collective-permute-start.13) | collective-permute-done | bytes 376864 | tf_op jit(solution)/shard_map/ppermute | solution.py:288
  29.6 0.1 collective-permute-start.12
  29.7 2.2 %shard_map.104 = (bf16[4,360,128]{2,1,0:T(8,128)(2,1)S(1)}, bf16[4,360,128]{2,1,0:T(8,128)(2,1)S(1)}) custom-call(bf16[4,368,128]{2,1,0:T(8,128)(2,1)S(1)} %collective-permute-done.7.refs_0_, bf16[4,368,128]{2,1,0:T(8,128)(2,1)S(1)} %collective-permute-done.13.refs_1_, bf16[768,1536]{1,0:T(8,128)(2,1)S(1)} %get-tuple-element.69.refs_4_.refs_2_.refs_8_, ...), custom_call_target="tpu_custom_call" | custom-call | flops 1811939328 | bytes 3538944 | tf_op jit(solution)/shard_map/pallas_call | solution.py:253
  32.0 2.2 %shard_map.105 = (bf16[4,360,128]{2,1,0:T(8,128)(2,1)S(1)}, bf16[4,360,128]{2,1,0:T(8,128)(2,1)S(1)}) custom-call(bf16[2,368,128]{2,1,0:T(8,128)(2,1)S(1)} %pad_maximum_fusion.1.refs_0_, bf16[2,368,128]{2,1,0:T(8,128)(2,1)S(1)} %collective-permute-done.9.refs_1_, bf16[2,368,128]{2,1,0:T(8,128)(2,1)S(1)} %collective-permute-done.3.refs_2_, ...), custom_call_target="tpu_custom_call" | custom-call | flops 1811939328 | bytes 3538944 | tf_op jit(solution)/shard_map/pallas_call | solution.py:253
  34.2 0.4 collective-permute-start.15
  34.7 0.1 collective-permute-start.14
  34.8 2.2 %shard_map.106 = (bf16[4,360,128]{2,1,0:T(8,128)(2,1)S(1)}, bf16[4,360,128]{2,1,0:T(8,128)(2,1)S(1)}) custom-call(bf16[2,368,128]{2,1,0:T(8,128)(2,1)S(1)} %pad_maximum_fusion.1.refs_0_, bf16[2,368,128]{2,1,0:T(8,128)(2,1)S(1)} %collective-permute-done.9.refs_1_, bf16[2,368,128]{2,1,0:T(8,128)(2,1)S(1)} %collective-permute-done.3.refs_2_, ...), custom_call_target="tpu_custom_call" | custom-call | flops 1811939328 | bytes 3538944 | tf_op jit(solution)/shard_map/pallas_call | solution.py:253
  37.0 0.4 collective-permute-start.16
  37.4 0.1 add_convert_fusion.11
  37.5 1.2 %collective-permute-done.16 = bf16[4,360,128]{2,1,0:T(8,128)(2,1)S(1)} collective-permute-done((bf16[4,360,128]{2,1,0:T(8,128)(2,1)S(1)}, bf16[4,360,128]{2,1,0:T(8,128)(2,1)S(1)}, u32[]{:S(2)}, u32[]{:S(2)}) %collective-permute-start.16) | collective-permute-done | bytes 368672 | tf_op jit(solution)/shard_map/ppermute | solution.py:288
  38.8 0.1 add_convert_fusion.10
  38.9 0.6 collective-permute-start.19
  39.5 1.6 %collective-permute-start.20 = (bf16[2,360,128]{2,1,0:T(8,128)(2,1)S(1)}, bf16[2,360,128]{2,1,0:T(8,128)(2,1)S(1)}, u32[]{:S(2)}, u32[]{:S(2)}) collective-permute-start(bf16[2,360,128]{2,1,0:T(8,128)(2,1)S(1)} %pad_maximum_fusion.4), channel_id=1, source_target_pairs={{0,6},{1,7},{2,4},{3,5},{4,2},{5,3},{6,0},{7,1},{8,14},{9,15},{10,... | collective-permute-start | bytes 552968 | tf_op jit(solution)/shard_map/ppermute | solution.py:288
  41.1 1.5 %collective-permute-start.18 = (bf16[2,360,128]{2,1,0:T(8,128)(2,1)S(1)}, bf16[2,360,128]{2,1,0:T(8,128)(2,1)S(1)}, u32[]{:S(2)}, u32[]{:S(2)}) collective-permute-start(bf16[2,360,128]{2,1,0:T(8,128)(2,1)S(1)} %pad_maximum_fusion.2), channel_id=1, source_target_pairs={{0,2},{1,3},{2,0},{3,1},{4,6},{5,7},{6,4},{7,5},{8,10},{9,11},{10,... | collective-permute-start | bytes 552968 | tf_op jit(solution)/shard_map/ppermute | solution.py:288
  42.6 0.1 add_convert_fusion
  42.8 3.6 %collective-permute-done.19 = bf16[2,360,128]{2,1,0:T(8,128)(2,1)S(1)} collective-permute-done((bf16[2,360,128]{2,1,0:T(8,128)(2,1)S(1)}, bf16[2,360,128]{2,1,0:T(8,128)(2,1)S(1)}, u32[]{:S(2)}, u32[]{:S(2)}) %collective-permute-start.19) | collective-permute-done | bytes 184352 | tf_op jit(solution)/shard_map/ppermute | solution.py:288
  46.4 3.5 %collective-permute-done.20 = bf16[2,360,128]{2,1,0:T(8,128)(2,1)S(1)} collective-permute-done((bf16[2,360,128]{2,1,0:T(8,128)(2,1)S(1)}, bf16[2,360,128]{2,1,0:T(8,128)(2,1)S(1)}, u32[]{:S(2)}, u32[]{:S(2)}) %collective-permute-start.20) | collective-permute-done | bytes 184352 | tf_op jit(solution)/shard_map/ppermute | solution.py:288
  49.9 1.5 %collective-permute-done.18 = bf16[2,360,128]{2,1,0:T(8,128)(2,1)S(1)} collective-permute-done((bf16[2,360,128]{2,1,0:T(8,128)(2,1)S(1)}, bf16[2,360,128]{2,1,0:T(8,128)(2,1)S(1)}, u32[]{:S(2)}, u32[]{:S(2)}) %collective-permute-start.18) | collective-permute-done | bytes 184352 | tf_op jit(solution)/shard_map/ppermute | solution.py:288
  51.5 0.1 fusion.8
  51.6 1.8 %collective-permute-start.24 = (bf16[360,128]{1,0:T(8,128)(2,1)S(1)}, bf16[360,128]{1,0:T(8,128)(2,1)S(1)}, u32[]{:S(2)}, u32[]{:S(2)}) collective-permute-start(bf16[360,128]{1,0:T(8,128)(2,1)S(1)} %get-tuple-element.122), channel_id=1, source_target_pairs={{0,16},{1,17},{2,18},{3,19},{4,20},{5,21},{6,22},{7,23},{8,24},{9,... | collective-permute-start | bytes 276488 | tf_op jit(solution)/shard_map/ppermute | solution.py:288
  53.4 0.5 collective-permute-start.25
  53.9 0.1 fusion.5
  54.1 1.3 %collective-permute-start.21 = (bf16[360,128]{1,0:T(8,128)(2,1)S(1)}, bf16[360,128]{1,0:T(8,128)(2,1)S(1)}, u32[]{:S(2)}, u32[]{:S(2)}) collective-permute-start(bf16[360,128]{1,0:T(8,128)(2,1)S(1)} %get-tuple-element.113), channel_id=1, source_target_pairs={{0,2},{1,3},{2,0},{3,1},{4,6},{5,7},{6,4},{7,5},{8,10},{9,11},{10,... | collective-permute-start | bytes 276488 | tf_op jit(solution)/shard_map/ppermute | solution.py:288
  55.4 1.4 %collective-permute-start.23 = (bf16[360,128]{1,0:T(8,128)(2,1)S(1)}, bf16[360,128]{1,0:T(8,128)(2,1)S(1)}, u32[]{:S(2)}, u32[]{:S(2)}) collective-permute-start(bf16[360,128]{1,0:T(8,128)(2,1)S(1)} %get-tuple-element.114), channel_id=1, source_target_pairs={{0,6},{1,7},{2,4},{3,5},{4,2},{5,3},{6,0},{7,1},{8,14},{9,15},{10,... | collective-permute-start | bytes 276488 | tf_op jit(solution)/shard_map/ppermute | solution.py:288
  56.8 0.8 %collective-permute-start.22 = (bf16[360,128]{1,0:T(8,128)(2,1)S(1)}, bf16[360,128]{1,0:T(8,128)(2,1)S(1)}, u32[]{:S(2)}, u32[]{:S(2)}) collective-permute-start(bf16[360,128]{1,0:T(8,128)(2,1)S(1)} %get-tuple-element.115), channel_id=1, source_target_pairs={{0,4},{1,5},{2,6},{3,7},{4,0},{5,1},{6,2},{7,3},{8,12},{9,13},{10,... | collective-permute-start | bytes 276488 | tf_op jit(solution)/shard_map/ppermute | solution.py:288
  57.6 2.9 %collective-permute-done.24 = bf16[360,128]{1,0:T(8,128)(2,1)S(1)} collective-permute-done((bf16[360,128]{1,0:T(8,128)(2,1)S(1)}, bf16[360,128]{1,0:T(8,128)(2,1)S(1)}, u32[]{:S(2)}, u32[]{:S(2)}) %collective-permute-start.24) | collective-permute-done | bytes 92192 | tf_op jit(solution)/shard_map/ppermute | solution.py:288
  60.5 0.3 collective-permute-done.23
  60.8 0.5 collective-permute-done.22
  61.4 0.7 %fusion.10 = bf16[128,360]{0,1:T(8,128)(2,1)} fusion(bf16[360,128]{1,0:T(8,128)(2,1)S(1)} %collective-permute-done.25, bf16[360,128]{1,0:T(8,128)(2,1)S(1)} %collective-permute-done.24, bf16[360,128]{1,0:T(8,128)(2,1)S(1)} %collective-permute-done.23, bf16[360,128]{1,0:T(8,128)(2,1)S(1)} %collective-permute-done.22, ...), kind=kLoop, calls=%fused_computation.28 | loop fusion | flops 737280 | bytes 829440 | tf_op jit(solution)/shard_map/transpose | solution.py:367
  (33 shorter events, 0.2 us)
Async XLA Ops:
  0.0 13.2 %copy-start = (bf16[1,1440,360]{2,1,0:T(8,128)(2,1)S(1)}, bf16[1,1440,360]{2,1,0:T(8,128)(2,1)}, u32[]{:S(2)}) copy-start(bf16[1,1440,360]{2,1,0:T(8,128)(2,1)} %param.14) | copy-start | bytes 3110404
  0.0 13.2 %copy-start.1 = (bf16[1,1440,360]{2,1,0:T(8,128)(2,1)S(1)}, bf16[1,1440,360]{2,1,0:T(8,128)(2,1)}, u32[]{:S(2)}) copy-start(bf16[1,1440,360]{2,1,0:T(8,128)(2,1)} %param.16) | copy-start | bytes 3110404
  2.4 9.0 %collective-permute-start.5 = (bf16[2,368,128]{2,1,0:T(8,128)(2,1)}, bf16[2,368,128]{2,1,0:T(8,128)(2,1)S(1)}, u32[]{:S(2)}, u32[]{:S(2)}) collective-permute-start(bf16[2,368,128]{2,1,0:T(8,128)(2,1)} %get-tuple-element.64.refs_0_), channel_id=1, source_target_pairs={{0,4},{1,5},{2,6},{3,7},{4,0},{5,1},{6,2},{7,3},{8,12},{9,13},{10,... | collective-permute-start | bytes 565256 | tf_op jit(solution)/shard_map/ppermute | solution.py:288
  5.4 8.7 %collective-permute-start.1 = (bf16[368,128]{1,0:T(8,128)(2,1)}, bf16[368,128]{1,0:T(8,128)(2,1)S(1)}, u32[]{:S(2)}, u32[]{:S(2)}) collective-permute-start(bf16[368,128]{1,0:T(8,128)(2,1)} %get-tuple-element.59), channel_id=1, source_target_pairs={{0,24},{1,25},{2,26},{3,27},{4,28},{5,29},{6,30},{7,31},{8,16},{9,... | collective-permute-start | bytes 282632 | tf_op jit(solution)/shard_map/ppermute | solution.py:288
  9.0 8.0 %collective-permute-start = (bf16[368,128]{1,0:T(8,128)(2,1)}, bf16[368,128]{1,0:T(8,128)(2,1)S(1)}, u32[]{:S(2)}, u32[]{:S(2)}) collective-permute-start(bf16[368,128]{1,0:T(8,128)(2,1)} %get-tuple-element.59), channel_id=1, source_target_pairs={{0,16},{1,17},{2,18},{3,19},{4,20},{5,21},{6,22},{7,23},{8,24},{9,... | collective-permute-start | bytes 282632 | tf_op jit(solution)/shard_map/ppermute | solution.py:288
  9.7 1.2 %copy-start.2 = (bf16[1,360,1440]{2,1,0:T(8,128)(2,1)S(1)}, bf16[1,360,1440]{2,1,0:T(8,128)(2,1)}, u32[]{:S(2)}) copy-start(bf16[1,360,1440]{2,1,0:T(8,128)(2,1)} %param.18) | copy-start | bytes 3110404
  12.4 15.5 %collective-permute-start.7 = (bf16[4,368,128]{2,1,0:T(8,128)(2,1)S(1)}, bf16[4,368,128]{2,1,0:T(8,128)(2,1)S(1)}, u32[]{:S(2)}, u32[]{:S(2)}) collective-permute-start(bf16[4,368,128]{2,1,0:T(8,128)(2,1)S(1)} %pad_maximum_fusion), channel_id=1, source_target_pairs={{0,8},{1,9},{2,10},{3,11},{4,12},{5,13},{6,14},{7,15},{8,0},{9,1},... | collective-permute-start | bytes 1130504 | tf_op jit(solution)/shard_map/ppermute | solution.py:288
  13.2 7.3 %collective-permute-start.6 = (bf16[2,368,128]{2,1,0:T(8,128)(2,1)S(1)}, bf16[2,368,128]{2,1,0:T(8,128)(2,1)S(1)}, u32[]{:S(2)}, u32[]{:S(2)}) collective-permute-start(bf16[2,368,128]{2,1,0:T(8,128)(2,1)S(1)} %collective-permute-done.5.refs_2_), channel_id=1, source_target_pairs={{0,1},{1,0},{2,3},{3,2},{4,5},{5,4},{6,7},{7,6},{8,9},{9,8},{10,11... | collective-permute-start | bytes 565256 | tf_op jit(solution)/shard_map/ppermute | solution.py:288
  13.2 7.3 %copy-start.3 = (bf16[2,368,128]{2,1,0:T(8,128)(2,1)S(1)}, bf16[2,368,128]{2,1,0:T(8,128)(2,1)}, u32[]{:S(2)}) copy-start(bf16[2,368,128]{2,1,0:T(8,128)(2,1)} %get-tuple-element.64.refs_0_) | copy-start | bytes 565252
  13.2 7.3 %copy-start.4 = (bf16[2,368,128]{2,1,0:T(8,128)(2,1)S(1)}, bf16[2,368,128]{2,1,0:T(8,128)(2,1)}, u32[]{:S(2)}) copy-start(bf16[2,368,128]{2,1,0:T(8,128)(2,1)} %get-tuple-element.65.refs_1_) | copy-start | bytes 565252
  17.0 8.7 %collective-permute-start.4 = (bf16[2,368,128]{2,1,0:T(8,128)(2,1)S(1)}, bf16[2,368,128]{2,1,0:T(8,128)(2,1)S(1)}, u32[]{:S(2)}, u32[]{:S(2)}) collective-permute-start(bf16[2,368,128]{2,1,0:T(8,128)(2,1)S(1)} %pad_maximum_fusion.1.refs_0_), channel_id=1, source_target_pairs={{0,6},{1,7},{2,4},{3,5},{4,2},{5,3},{6,0},{7,1},{8,14},{9,15},{10,... | collective-permute-start | bytes 565256 | tf_op jit(solution)/shard_map/ppermute | solution.py:288
  18.5 9.3 %collective-permute-start.3 = (bf16[2,368,128]{2,1,0:T(8,128)(2,1)S(1)}, bf16[2,368,128]{2,1,0:T(8,128)(2,1)S(1)}, u32[]{:S(2)}, u32[]{:S(2)}) collective-permute-start(bf16[2,368,128]{2,1,0:T(8,128)(2,1)S(1)} %pad_maximum_fusion.1.refs_0_), channel_id=1, source_target_pairs={{0,2},{1,3},{2,0},{3,1},{4,6},{5,7},{6,4},{7,5},{8,10},{9,11},{10,... | collective-permute-start | bytes 565256 | tf_op jit(solution)/shard_map/ppermute | solution.py:288
  19.0 8.9 %collective-permute-start.2 = (bf16[2,368,128]{2,1,0:T(8,128)(2,1)S(1)}, bf16[2,368,128]{2,1,0:T(8,128)(2,1)S(1)}, u32[]{:S(2)}, u32[]{:S(2)}) collective-permute-start(bf16[2,368,128]{2,1,0:T(8,128)(2,1)S(1)} %pad_maximum_fusion.1.refs_0_), channel_id=1, source_target_pairs={{0,4},{1,5},{2,6},{3,7},{4,0},{5,1},{6,2},{7,3},{8,12},{9,13},{10,... | collective-permute-start | bytes 565256 | tf_op jit(solution)/shard_map/ppermute | solution.py:288
  27.9 1.7 %collective-permute-start.13 = (bf16[4,368,128]{2,1,0:T(8,128)(2,1)S(1)}, bf16[4,368,128]{2,1,0:T(8,128)(2,1)S(1)}, u32[]{:S(2)}, u32[]{:S(2)}) collective-permute-start(bf16[4,368,128]{2,1,0:T(8,128)(2,1)S(1)} %collective-permute-done.7.refs_0_), channel_id=1, source_target_pairs={{0,1},{1,0},{2,3},{3,2},{4,5},{5,4},{6,7},{7,6},{8,9},{9,8},{10,11... | collective-permute-start | bytes 1130504 | tf_op jit(solution)/shard_map/ppermute | solution.py:288
  27.9 4.1 %collective-permute-start.8 = (bf16[4,360,128]{2,1,0:T(8,128)(2,1)S(1)}, bf16[4,360,128]{2,1,0:T(8,128)(2,1)S(1)}, u32[]{:S(2)}, u32[]{:S(2)}) collective-permute-start(bf16[4,360,128]{2,1,0:T(8,128)(2,1)S(1)} %get-tuple-element.76), channel_id=1, source_target_pairs={{0,1},{1,0},{2,3},{3,2},{4,5},{5,4},{6,7},{7,6},{8,9},{9,8},{10,11... | collective-permute-start | bytes 1105928 | tf_op jit(solution)/shard_map/ppermute | solution.py:288
  28.4 3.5 %collective-permute-start.9 = (bf16[2,368,128]{2,1,0:T(8,128)(2,1)S(1)}, bf16[2,368,128]{2,1,0:T(8,128)(2,1)S(1)}, u32[]{:S(2)}, u32[]{:S(2)}) collective-permute-start(bf16[2,368,128]{2,1,0:T(8,128)(2,1)S(1)} %pad_maximum_fusion.1.refs_0_), channel_id=1, source_target_pairs={{0,1},{1,0},{2,3},{3,2},{4,5},{5,4},{6,7},{7,6},{8,9},{9,8},{10,11... | collective-permute-start | bytes 565256 | tf_op jit(solution)/shard_map/ppermute | solution.py:288
  28.4 3.5 %collective-permute-start.10 = (bf16[2,368,128]{2,1,0:T(8,128)(2,1)S(1)}, bf16[2,368,128]{2,1,0:T(8,128)(2,1)S(1)}, u32[]{:S(2)}, u32[]{:S(2)}) collective-permute-start(bf16[2,368,128]{2,1,0:T(8,128)(2,1)S(1)} %collective-permute-done.3.refs_2_), channel_id=1, source_target_pairs={{0,1},{1,0},{2,3},{3,2},{4,5},{5,4},{6,7},{7,6},{8,9},{9,8},{10,11... | collective-permute-start | bytes 565256 | tf_op jit(solution)/shard_map/ppermute | solution.py:288
  28.9 3.0 %collective-permute-start.11 = (bf16[2,368,128]{2,1,0:T(8,128)(2,1)S(1)}, bf16[2,368,128]{2,1,0:T(8,128)(2,1)S(1)}, u32[]{:S(2)}, u32[]{:S(2)}) collective-permute-start(bf16[2,368,128]{2,1,0:T(8,128)(2,1)S(1)} %collective-permute-done.2.refs_4_), channel_id=1, source_target_pairs={{0,1},{1,0},{2,3},{3,2},{4,5},{5,4},{6,7},{7,6},{8,9},{9,8},{10,11... | collective-permute-start | bytes 565256 | tf_op jit(solution)/shard_map/ppermute | solution.py:288
  29.6 2.4 %collective-permute-start.12 = (bf16[2,368,128]{2,1,0:T(8,128)(2,1)S(1)}, bf16[2,368,128]{2,1,0:T(8,128)(2,1)S(1)}, u32[]{:S(2)}, u32[]{:S(2)}) collective-permute-start(bf16[2,368,128]{2,1,0:T(8,128)(2,1)S(1)} %collective-permute-done.4.refs_6_), channel_id=1, source_target_pairs={{0,1},{1,0},{2,3},{3,2},{4,5},{5,4},{6,7},{7,6},{8,9},{9,8},{10,11... | collective-permute-start | bytes 565256 | tf_op jit(solution)/shard_map/ppermute | solution.py:288
  34.2 2.8 %collective-permute-start.15 = (bf16[4,360,128]{2,1,0:T(8,128)(2,1)S(1)}, bf16[4,360,128]{2,1,0:T(8,128)(2,1)S(1)}, u32[]{:S(2)}, u32[]{:S(2)}) collective-permute-start(bf16[4,360,128]{2,1,0:T(8,128)(2,1)S(1)} %get-tuple-element.94), channel_id=1, source_target_pairs={{0,1},{1,0},{2,3},{3,2},{4,5},{5,4},{6,7},{7,6},{8,9},{9,8},{10,11... | collective-permute-start | bytes 1105928 | tf_op jit(solution)/shard_map/ppermute | solution.py:288
  34.7 2.9 %collective-permute-start.14 = (bf16[4,360,128]{2,1,0:T(8,128)(2,1)S(1)}, bf16[4,360,128]{2,1,0:T(8,128)(2,1)S(1)}, u32[]{:S(2)}, u32[]{:S(2)}) collective-permute-start(bf16[4,360,128]{2,1,0:T(8,128)(2,1)S(1)} %get-tuple-element.85), channel_id=1, source_target_pairs={{0,1},{1,0},{2,3},{3,2},{4,5},{5,4},{6,7},{7,6},{8,9},{9,8},{10,11... | collective-permute-start | bytes 1105928 | tf_op jit(solution)/shard_map/ppermute | solution.py:288
  37.0 1.8 %collective-permute-start.16 = (bf16[4,360,128]{2,1,0:T(8,128)(2,1)S(1)}, bf16[4,360,128]{2,1,0:T(8,128)(2,1)S(1)}, u32[]{:S(2)}, u32[]{:S(2)}) collective-permute-start(bf16[4,360,128]{2,1,0:T(8,128)(2,1)S(1)} %get-tuple-element.106), channel_id=1, source_target_pairs={{0,1},{1,0},{2,3},{3,2},{4,5},{5,4},{6,7},{7,6},{8,9},{9,8},{10,11... | collective-permute-start | bytes 1105928 | tf_op jit(solution)/shard_map/ppermute | solution.py:288
  38.9 7.5 %collective-permute-start.19 = (bf16[2,360,128]{2,1,0:T(8,128)(2,1)S(1)}, bf16[2,360,128]{2,1,0:T(8,128)(2,1)S(1)}, u32[]{:S(2)}, u32[]{:S(2)}) collective-permute-start(bf16[2,360,128]{2,1,0:T(8,128)(2,1)S(1)} %pad_maximum_fusion.3), channel_id=1, source_target_pairs={{0,4},{1,5},{2,6},{3,7},{4,0},{5,1},{6,2},{7,3},{8,12},{9,13},{10,... | collective-permute-start | bytes 552968 | tf_op jit(solution)/shard_map/ppermute | solution.py:288
  39.5 10.4 %collective-permute-start.20 = (bf16[2,360,128]{2,1,0:T(8,128)(2,1)S(1)}, bf16[2,360,128]{2,1,0:T(8,128)(2,1)S(1)}, u32[]{:S(2)}, u32[]{:S(2)}) collective-permute-start(bf16[2,360,128]{2,1,0:T(8,128)(2,1)S(1)} %pad_maximum_fusion.4), channel_id=1, source_target_pairs={{0,6},{1,7},{2,4},{3,5},{4,2},{5,3},{6,0},{7,1},{8,14},{9,15},{10,... | collective-permute-start | bytes 552968 | tf_op jit(solution)/shard_map/ppermute | solution.py:288
  41.1 10.4 %collective-permute-start.18 = (bf16[2,360,128]{2,1,0:T(8,128)(2,1)S(1)}, bf16[2,360,128]{2,1,0:T(8,128)(2,1)S(1)}, u32[]{:S(2)}, u32[]{:S(2)}) collective-permute-start(bf16[2,360,128]{2,1,0:T(8,128)(2,1)S(1)} %pad_maximum_fusion.2), channel_id=1, source_target_pairs={{0,2},{1,3},{2,0},{3,1},{4,6},{5,7},{6,4},{7,5},{8,10},{9,11},{10,... | collective-permute-start | bytes 552968 | tf_op jit(solution)/shard_map/ppermute | solution.py:288
  42.7 11.2 %collective-permute-start.17 = (bf16[4,360,128]{2,1,0:T(8,128)(2,1)S(1)}, bf16[4,360,128]{2,1,0:T(8,128)(2,1)S(1)}, u32[]{:S(2)}, u32[]{:S(2)}) collective-permute-start(bf16[4,360,128]{2,1,0:T(8,128)(2,1)S(1)} %add_convert_fusion), channel_id=1, source_target_pairs={{0,8},{1,9},{2,10},{3,11},{4,12},{5,13},{6,14},{7,15},{8,0},{9,1},... | collective-permute-start | bytes 1105928 | tf_op jit(solution)/shard_map/ppermute | solution.py:288
  51.6 8.9 %collective-permute-start.24 = (bf16[360,128]{1,0:T(8,128)(2,1)S(1)}, bf16[360,128]{1,0:T(8,128)(2,1)S(1)}, u32[]{:S(2)}, u32[]{:S(2)}) collective-permute-start(bf16[360,128]{1,0:T(8,128)(2,1)S(1)} %get-tuple-element.122), channel_id=1, source_target_pairs={{0,16},{1,17},{2,18},{3,19},{4,20},{5,21},{6,22},{7,23},{8,24},{9,... | collective-permute-start | bytes 276488 | tf_op jit(solution)/shard_map/ppermute | solution.py:288
  53.4 7.1 %collective-permute-start.25 = (bf16[360,128]{1,0:T(8,128)(2,1)S(1)}, bf16[360,128]{1,0:T(8,128)(2,1)S(1)}, u32[]{:S(2)}, u32[]{:S(2)}) collective-permute-start(bf16[360,128]{1,0:T(8,128)(2,1)S(1)} %get-tuple-element.123), channel_id=1, source_target_pairs={{0,24},{1,25},{2,26},{3,27},{4,28},{5,29},{6,30},{7,31},{8,16},{9,... | collective-permute-start | bytes 276488 | tf_op jit(solution)/shard_map/ppermute | solution.py:288
  54.1 6.5 %collective-permute-start.21 = (bf16[360,128]{1,0:T(8,128)(2,1)S(1)}, bf16[360,128]{1,0:T(8,128)(2,1)S(1)}, u32[]{:S(2)}, u32[]{:S(2)}) collective-permute-start(bf16[360,128]{1,0:T(8,128)(2,1)S(1)} %get-tuple-element.113), channel_id=1, source_target_pairs={{0,2},{1,3},{2,0},{3,1},{4,6},{5,7},{6,4},{7,5},{8,10},{9,11},{10,... | collective-permute-start | bytes 276488 | tf_op jit(solution)/shard_map/ppermute | solution.py:288
  55.4 5.5 %collective-permute-start.23 = (bf16[360,128]{1,0:T(8,128)(2,1)S(1)}, bf16[360,128]{1,0:T(8,128)(2,1)S(1)}, u32[]{:S(2)}, u32[]{:S(2)}) collective-permute-start(bf16[360,128]{1,0:T(8,128)(2,1)S(1)} %get-tuple-element.114), channel_id=1, source_target_pairs={{0,6},{1,7},{2,4},{3,5},{4,2},{5,3},{6,0},{7,1},{8,14},{9,15},{10,... | collective-permute-start | bytes 276488 | tf_op jit(solution)/shard_map/ppermute | solution.py:288
  56.8 4.6 %collective-permute-start.22 = (bf16[360,128]{1,0:T(8,128)(2,1)S(1)}, bf16[360,128]{1,0:T(8,128)(2,1)S(1)}, u32[]{:S(2)}, u32[]{:S(2)}) collective-permute-start(bf16[360,128]{1,0:T(8,128)(2,1)S(1)} %get-tuple-element.115), channel_id=1, source_target_pairs={{0,4},{1,5},{2,6},{3,7},{4,0},{5,1},{6,2},{7,3},{8,12},{9,13},{10,... | collective-permute-start | bytes 276488 | tf_op jit(solution)/shard_map/ppermute | solution.py:288

commit v11 on v10

--- a/solution.py
+++ b/solution.py
@@ -335,26 +335,26 @@
     got_0 = swap(send_0, core)
     high = (z_high, swap(z_high, core), y_high, swap(y_high, core))
     high = high + (x_high, swap(x_high, core), d_high, swap(d_high, core))
-    near_1 = (z_near, swap(z_near, core))
-    blocks = [[(k % 2, 2 * x + k // 2) for k in range(groups)] for x in range(2)]
-    keep_1, send_1 = run_expert(near_1, blocks, slots, weights, sizes, 1)
-    got_0, high, keep_1, send_1 = tied((got_0, high, keep_1, send_1))
-    got_1 = swap(send_1, core)
+    got_0, high = tied((got_0, high))
     line = [[[(4 * x + k, n) for k in range(groups)] for x in range(2)] for n in range(2)]
     keep_2, send_2 = run_expert(high, line[0], slots, weights, sizes, 1)
     got_2 = swap(send_2, core)
-    keep_2, high = tied((keep_2, high))
+    keep_2, high, z_near = tied((keep_2, high, z_near))
+    near_1 = (z_near, swap(z_near, core))
     keep_3, send_3 = run_expert(high, line[1], slots, weights, sizes, 1)
-    got_2, keep_3, send_3 = tied((got_2, keep_3, send_3))
+    got_2, keep_3, send_3, near_1 = tied((got_2, keep_3, send_3, near_1))
     got_3 = swap(send_3, core)
-    got_1, got_3 = tied((got_1, got_3))
+    blocks = [[(k % 2, 2 * x + k // 2) for k in range(groups)] for x in range(2)]
+    keep_1, send_1 = run_expert(near_1, blocks, slots, weights, sizes, 1)
+    got_1 = swap(send_1, core)
+    keep_1, got_3 = tied((keep_1, got_3))
     z_back = swap(add_up(keep_1, got_1), along_z)
 
     def spread(*terms):
-        return [add_up(*[term[n] for term in terms]) for n in (1, 2, 3)]
+        return [add_up(*[term[n] for term in terms]) for n in (2, 3, 1)]
 
     def gather(parts):
-        return [swap(part, step) for part, step in zip(parts, (along_y, along_x, diagonal))]
+        return [swap(part, step) for part, step in zip(parts, (along_x, diagonal, along_y))]
 
     far_sums = [jnp.stack(pair) for pair in zip(spread(keep_2, got_2), spread(keep_3, got_3))]
     far_sums = gather(far_sums)

time: 62.3 us -> 61.2 us (0.982)
  waiting for transfers between devices: 22.4 us -> 21.4 us
    ppermute x26, waiting for transfers between devices: 22.4 us -> 21.4 us  [swap(): lax.ppermute(array, ('seq', 'rep'), [(i, i ^ step) for i in range(devices)])]
  transfers between devices with their start and end apart: 26 -> 26, of which waited for: 12 -> 12; matrix products, arithmetic and copies ran while one was open for 3% -> 4% of each run, Pallas kernels for 13% -> 13%
where the time goes in v11:
time: 61.2 us; the launch traced here: 61 us
  starting transfers between devices  22.7 us (37%)
  waiting for transfers between devices  21.4 us (35%)
  Pallas kernels  12.4 us (20%)
  other arithmetic  3.03 us (5%)
  local copies, waits for them, and re-layouts  1.26 us (2%)
    ppermute x26, starting transfers between devices, swap(): lax.ppermute(array, ('seq', 'rep'), [(i, i ^ step) for i in range(devices)])  22.7 us
    ppermute x26, waiting for transfers between devices, swap(): lax.ppermute(array, ('seq', 'rep'), [(i, i ^ step) for i in range(devices)])  21.4 us
    pallas_call x4, Pallas kernels, run_expert(): pl.pallas_call(functools.partial(expert_kernel, quarter, per, blocks, slo...  8.8 us
    pallas_call x1, Pallas kernels, make_pieces(): pl.pallas_call(functools.partial(pieces_kernel, groups, per, experts), in...  2.35 us
    unnamed x10, local copies, waits for them, and re-layouts  1.26 us
    pallas_call x2, Pallas kernels, arrange(): pl.pallas_call(functools.partial(kernel, groups), out_shape=[jax.ShapeDty...  1.23 us
  transfers between devices with their start and end apart: 26, of which 12 were waited for; matrix products, arithmetic and copies ran while one was open for 4% of the time, Pallas kernels for 13%

profile of v11, /device:TPU:0, one launch (start us, length us, event | category | flops | bytes accessed | tf_op | source)
XLA Modules:
  0.0 61.0 jit_solution(7919498715638944617)
XLA Ops:
  0.0 2.4 %shard_map.100 = (bf16[368,128]{1,0:T(8,128)(2,1)}, bf16[2,368,128]{2,1,0:T(8,128)(2,1)}, bf16[2,368,128]{2,1,0:T(8,128)(2,1)}) custom-call(bf16[1440,128]{1,0:T(8,128)(2,1)} %bitcast.37, f32[1440]{0:T(1024)} %refs_1_.1, s32[4,128]{1,0:T(4,128)} %bitcast.40, f32[4,128]{1,0:T(4,128)} %bitcast.41), custom_call_target="tpu_custom_call" | custom-call | tf_op jit(solution)/shard_map/pallas_call | solution.py:188
  2.4 3.0 %collective-permute-start.5 = (bf16[2,368,128]{2,1,0:T(8,128)(2,1)}, bf16[2,368,128]{2,1,0:T(8,128)(2,1)S(1)}, u32[]{:S(2)}, u32[]{:S(2)}) collective-permute-start(bf16[2,368,128]{2,1,0:T(8,128)(2,1)} %get-tuple-element.65.refs_0_), channel_id=1, source_target_pairs={{0,4},{1,5},{2,6},{3,7},{4,0},{5,1},{6,2},{7,3},{8,12},{9,13},{10,... | collective-permute-start | bytes 565256 | tf_op jit(solution)/shard_map/ppermute | solution.py:288
  5.4 3.6 %collective-permute-start.1 = (bf16[368,128]{1,0:T(8,128)(2,1)}, bf16[368,128]{1,0:T(8,128)(2,1)S(1)}, u32[]{:S(2)}, u32[]{:S(2)}) collective-permute-start(bf16[368,128]{1,0:T(8,128)(2,1)} %get-tuple-element.60), channel_id=1, source_target_pairs={{0,24},{1,25},{2,26},{3,27},{4,28},{5,29},{6,30},{7,31},{8,16},{9,... | collective-permute-start | bytes 282632 | tf_op jit(solution)/shard_map/ppermute | solution.py:288
  9.0 0.7 %pad_maximum_fusion.5.biases_ref = f32[3,360]{1,0:T(4,128)S(1)} fusion(f32[1,360]{1,0:T(1,128)} %param.19, f32[1,360]{1,0:T(1,128)} %param.17, f32[1,360]{1,0:T(1,128)} %param.15), kind=kLoop, calls=%fused_computation.29 | loop fusion | flops 2160 | bytes 8640 | tf_op jit(solution)/shard_map/concatenate | solution.py:298
  9.7 1.2 %copy-done.2 = bf16[1,360,1440]{2,1,0:T(8,128)(2,1)S(1)} copy-done((bf16[1,360,1440]{2,1,0:T(8,128)(2,1)S(1)}, bf16[1,360,1440]{2,1,0:T(8,128)(2,1)}, u32[]{:S(2)}) %copy-start.2) | copy-done | bytes 1036824
  11.0 0.4 shard_map.102
  11.4 1.0 %pad_maximum_fusion = bf16[4,368,128]{2,1,0:T(8,128)(2,1)S(1)} fusion(bf16[2,368,128]{2,1,0:T(8,128)(2,1)S(1)} %collective-permute-done.5.refs_2_, bf16[2,368,128]{2,1,0:T(8,128)(2,1)} %get-tuple-element.65.refs_0_), kind=kLoop, calls=%fused_computation.1 | loop fusion | flops 188416 | bytes 753664 | tf_op jit(solution)/shard_map/concatenate | solution.py:331
  12.4 0.8 %collective-permute-start.7 = (bf16[4,368,128]{2,1,0:T(8,128)(2,1)S(1)}, bf16[4,368,128]{2,1,0:T(8,128)(2,1)S(1)}, u32[]{:S(2)}, u32[]{:S(2)}) collective-permute-start(bf16[4,368,128]{2,1,0:T(8,128)(2,1)S(1)} %pad_maximum_fusion), channel_id=1, source_target_pairs={{0,8},{1,9},{2,10},{3,11},{4,12},{5,13},{6,14},{7,15},{8,0},{9,1},... | collective-permute-start | bytes 1130504 | tf_op jit(solution)/shard_map/ppermute | solution.py:288
  13.3 0.8 %shard_map.101 = (bf16[768,1536]{1,0:T(8,128)(2,1)S(1)}, f32[768,128]{1,0:T(8,128)S(1)}) custom-call(bf16[1440,360]{1,0:T(8,128)(2,1)S(1)} %bitcast.34, bf16[1440,360]{1,0:T(8,128)(2,1)S(1)} %bitcast.35, f32[3,360]{1,0:T(4,128)S(1)} %pad_maximum_fusion.5.biases_ref), custom_call_target="tpu_custom_call" | custom-call | bytes 8294400 | tf_op jit(solution)/shard_map/pallas_call | solution.py:116
  14.1 2.9 %collective-permute-done = bf16[368,128]{1,0:T(8,128)(2,1)S(1)} collective-permute-done((bf16[368,128]{1,0:T(8,128)(2,1)}, bf16[368,128]{1,0:T(8,128)(2,1)S(1)}, u32[]{:S(2)}, u32[]{:S(2)}) %collective-permute-start) | collective-permute-done | bytes 94240 | tf_op jit(solution)/shard_map/ppermute | solution.py:288
  17.0 1.6 %collective-permute-start.4 = (bf16[2,368,128]{2,1,0:T(8,128)(2,1)S(1)}, bf16[2,368,128]{2,1,0:T(8,128)(2,1)S(1)}, u32[]{:S(2)}, u32[]{:S(2)}) collective-permute-start(bf16[2,368,128]{2,1,0:T(8,128)(2,1)S(1)} %pad_maximum_fusion.1.refs_0_), channel_id=1, source_target_pairs={{0,6},{1,7},{2,4},{3,5},{4,2},{5,3},{6,0},{7,1},{8,14},{9,15},{10,... | collective-permute-start | bytes 565256 | tf_op jit(solution)/shard_map/ppermute | solution.py:288
  18.5 0.5 collective-permute-start.3
  19.0 1.5 %collective-permute-start.2 = (bf16[2,368,128]{2,1,0:T(8,128)(2,1)S(1)}, bf16[2,368,128]{2,1,0:T(8,128)(2,1)S(1)}, u32[]{:S(2)}, u32[]{:S(2)}) collective-permute-start(bf16[2,368,128]{2,1,0:T(8,128)(2,1)S(1)} %pad_maximum_fusion.1.refs_0_), channel_id=1, source_target_pairs={{0,4},{1,5},{2,6},{3,7},{4,0},{5,1},{6,2},{7,3},{8,12},{9,13},{10,... | collective-permute-start | bytes 565256 | tf_op jit(solution)/shard_map/ppermute | solution.py:288
  20.5 2.2 %shard_map.103 = (bf16[4,360,128]{2,1,0:T(8,128)(2,1)S(1)}, bf16[4,360,128]{2,1,0:T(8,128)(2,1)S(1)}) custom-call(bf16[2,368,128]{2,1,0:T(8,128)(2,1)S(1)} %copy-done.3, bf16[2,368,128]{2,1,0:T(8,128)(2,1)S(1)} %copy-done.4, bf16[2,368,128]{2,1,0:T(8,128)(2,1)S(1)} %collective-permute-done.5.refs_2_, ...), custom_call_target="tpu_custom_call" | custom-call | flops 1811939328 | bytes 3538944 | tf_op jit(solution)/shard_map/pallas_call | solution.py:253
  22.7 2.9 %collective-permute-done.4.refs_6_ = bf16[2,368,128]{2,1,0:T(8,128)(2,1)S(1)} collective-permute-done((bf16[2,368,128]{2,1,0:T(8,128)(2,1)S(1)}, bf16[2,368,128]{2,1,0:T(8,128)(2,1)S(1)}, u32[]{:S(2)}, u32[]{:S(2)}) %collective-permute-start.4) | collective-permute-done | bytes 188448 | tf_op jit(solution)/shard_map/ppermute | solution.py:288
  25.6 2.2 %collective-permute-done.3.refs_2_ = bf16[2,368,128]{2,1,0:T(8,128)(2,1)S(1)} collective-permute-done((bf16[2,368,128]{2,1,0:T(8,128)(2,1)S(1)}, bf16[2,368,128]{2,1,0:T(8,128)(2,1)S(1)}, u32[]{:S(2)}, u32[]{:S(2)}) %collective-permute-start.3) | collective-permute-done | bytes 188448 | tf_op jit(solution)/shard_map/ppermute | solution.py:288
  27.8 0.1 collective-permute-done.2.refs_4_
  27.9 0.5 collective-permute-start.9
  28.4 0.5 collective-permute-start.11
  29.0 0.9 %collective-permute-done.9.refs_1_ = bf16[2,368,128]{2,1,0:T(8,128)(2,1)S(1)} collective-permute-done((bf16[2,368,128]{2,1,0:T(8,128)(2,1)S(1)}, bf16[2,368,128]{2,1,0:T(8,128)(2,1)S(1)}, u32[]{:S(2)}, u32[]{:S(2)}) %collective-permute-start.9) | collective-permute-done | bytes 188448 | tf_op jit(solution)/shard_map/ppermute | solution.py:288
  29.9 0.3 collective-permute-done.10.refs_3_
  30.1 0.3 collective-permute-done.11.refs_5_
  30.4 0.3 collective-permute-done.12.refs_7_
  30.7 2.2 %shard_map.104 = (bf16[4,360,128]{2,1,0:T(8,128)(2,1)S(1)}, bf16[4,360,128]{2,1,0:T(8,128)(2,1)S(1)}) custom-call(bf16[2,368,128]{2,1,0:T(8,128)(2,1)S(1)} %pad_maximum_fusion.1.refs_0_, bf16[2,368,128]{2,1,0:T(8,128)(2,1)S(1)} %collective-permute-done.9.refs_1_, bf16[2,368,128]{2,1,0:T(8,128)(2,1)S(1)} %collective-permute-done.3.refs_2_, ...), custom_call_target="tpu_custom_call" | custom-call | flops 1811939328 | bytes 3538944 | tf_op jit(solution)/shard_map/pallas_call | solution.py:253
  32.9 0.2 collective-permute-start.14
  33.1 0.4 collective-permute-start.13
  33.5 2.2 %shard_map.105 = (bf16[4,360,128]{2,1,0:T(8,128)(2,1)S(1)}, bf16[4,360,128]{2,1,0:T(8,128)(2,1)S(1)}) custom-call(bf16[2,368,128]{2,1,0:T(8,128)(2,1)S(1)} %pad_maximum_fusion.1.refs_0_, bf16[2,368,128]{2,1,0:T(8,128)(2,1)S(1)} %collective-permute-done.9.refs_1_, bf16[2,368,128]{2,1,0:T(8,128)(2,1)S(1)} %collective-permute-done.3.refs_2_, ...), custom_call_target="tpu_custom_call" | custom-call | flops 1811939328 | bytes 3538944 | tf_op jit(solution)/shard_map/pallas_call | solution.py:253
  35.7 0.2 collective-permute-start.15
  35.9 2.2 %shard_map.106 = (bf16[4,360,128]{2,1,0:T(8,128)(2,1)S(1)}, bf16[4,360,128]{2,1,0:T(8,128)(2,1)S(1)}) custom-call(bf16[4,368,128]{2,1,0:T(8,128)(2,1)S(1)} %collective-permute-done.7.refs_0_, bf16[4,368,128]{2,1,0:T(8,128)(2,1)S(1)} %collective-permute-done.14.refs_1_, bf16[768,1536]{1,0:T(8,128)(2,1)S(1)} %get-tuple-element.70.refs_4_.refs_8_.refs_2_, ...), custom_call_target="tpu_custom_call" | custom-call | flops 1811939328 | bytes 3538944 | tf_op jit(solution)/shard_map/pallas_call | solution.py:253
  38.1 0.4 collective-permute-start.16
  38.5 0.1 add_convert_fusion.11
  38.6 0.1 add_convert_fusion.10
  38.7 1.5 %collective-permute-start.19 = (bf16[2,360,128]{2,1,0:T(8,128)(2,1)S(1)}, bf16[2,360,128]{2,1,0:T(8,128)(2,1)S(1)}, u32[]{:S(2)}, u32[]{:S(2)}) collective-permute-start(bf16[2,360,128]{2,1,0:T(8,128)(2,1)S(1)} %pad_maximum_fusion.3), channel_id=1, source_target_pairs={{0,6},{1,7},{2,4},{3,5},{4,2},{5,3},{6,0},{7,1},{8,14},{9,15},{10,... | collective-permute-start | bytes 552968 | tf_op jit(solution)/shard_map/ppermute | solution.py:288
  40.2 0.7 %collective-permute-start.20 = (bf16[2,360,128]{2,1,0:T(8,128)(2,1)S(1)}, bf16[2,360,128]{2,1,0:T(8,128)(2,1)S(1)}, u32[]{:S(2)}, u32[]{:S(2)}) collective-permute-start(bf16[2,360,128]{2,1,0:T(8,128)(2,1)S(1)} %pad_maximum_fusion.4), channel_id=1, source_target_pairs={{0,2},{1,3},{2,0},{3,1},{4,6},{5,7},{6,4},{7,5},{8,10},{9,11},{10,... | collective-permute-start | bytes 552968 | tf_op jit(solution)/shard_map/ppermute | solution.py:288
  40.9 1.6 %collective-permute-start.18 = (bf16[2,360,128]{2,1,0:T(8,128)(2,1)S(1)}, bf16[2,360,128]{2,1,0:T(8,128)(2,1)S(1)}, u32[]{:S(2)}, u32[]{:S(2)}) collective-permute-start(bf16[2,360,128]{2,1,0:T(8,128)(2,1)S(1)} %pad_maximum_fusion.2), channel_id=1, source_target_pairs={{0,4},{1,5},{2,6},{3,7},{4,0},{5,1},{6,2},{7,3},{8,12},{9,13},{10,... | collective-permute-start | bytes 552968 | tf_op jit(solution)/shard_map/ppermute | solution.py:288
  42.5 0.1 add_convert_fusion
  42.7 4.6 %collective-permute-done.19 = bf16[2,360,128]{2,1,0:T(8,128)(2,1)S(1)} collective-permute-done((bf16[2,360,128]{2,1,0:T(8,128)(2,1)S(1)}, bf16[2,360,128]{2,1,0:T(8,128)(2,1)S(1)}, u32[]{:S(2)}, u32[]{:S(2)}) %collective-permute-start.19) | collective-permute-done | bytes 184352 | tf_op jit(solution)/shard_map/ppermute | solution.py:288
  47.2 3.1 %collective-permute-done.20 = bf16[2,360,128]{2,1,0:T(8,128)(2,1)S(1)} collective-permute-done((bf16[2,360,128]{2,1,0:T(8,128)(2,1)S(1)}, bf16[2,360,128]{2,1,0:T(8,128)(2,1)S(1)}, u32[]{:S(2)}, u32[]{:S(2)}) %collective-permute-start.20) | collective-permute-done | bytes 184352 | tf_op jit(solution)/shard_map/ppermute | solution.py:288
  50.3 0.1 fusion.8
  50.5 1.0 %collective-permute-start.24 = (bf16[360,128]{1,0:T(8,128)(2,1)S(1)}, bf16[360,128]{1,0:T(8,128)(2,1)S(1)}, u32[]{:S(2)}, u32[]{:S(2)}) collective-permute-start(bf16[360,128]{1,0:T(8,128)(2,1)S(1)} %get-tuple-element.124), channel_id=1, source_target_pairs={{0,16},{1,17},{2,18},{3,19},{4,20},{5,21},{6,22},{7,23},{8,24},{9,... | collective-permute-start | bytes 276488 | tf_op jit(solution)/shard_map/ppermute | solution.py:288
  51.5 1.1 %collective-permute-start.25 = (bf16[360,128]{1,0:T(8,128)(2,1)S(1)}, bf16[360,128]{1,0:T(8,128)(2,1)S(1)}, u32[]{:S(2)}, u32[]{:S(2)}) collective-permute-start(bf16[360,128]{1,0:T(8,128)(2,1)S(1)} %get-tuple-element.125), channel_id=1, source_target_pairs={{0,24},{1,25},{2,26},{3,27},{4,28},{5,29},{6,30},{7,31},{8,16},{9,... | collective-permute-start | bytes 276488 | tf_op jit(solution)/shard_map/ppermute | solution.py:288
  52.6 0.1 fusion.5
  52.7 0.6 %collective-permute-start.21 = (bf16[360,128]{1,0:T(8,128)(2,1)S(1)}, bf16[360,128]{1,0:T(8,128)(2,1)S(1)}, u32[]{:S(2)}, u32[]{:S(2)}) collective-permute-start(bf16[360,128]{1,0:T(8,128)(2,1)S(1)} %get-tuple-element.115), channel_id=1, source_target_pairs={{0,4},{1,5},{2,6},{3,7},{4,0},{5,1},{6,2},{7,3},{8,12},{9,13},{10,... | collective-permute-start | bytes 276488 | tf_op jit(solution)/shard_map/ppermute | solution.py:288
  53.4 1.4 %collective-permute-start.23 = (bf16[360,128]{1,0:T(8,128)(2,1)S(1)}, bf16[360,128]{1,0:T(8,128)(2,1)S(1)}, u32[]{:S(2)}, u32[]{:S(2)}) collective-permute-start(bf16[360,128]{1,0:T(8,128)(2,1)S(1)} %get-tuple-element.116), channel_id=1, source_target_pairs={{0,2},{1,3},{2,0},{3,1},{4,6},{5,7},{6,4},{7,5},{8,10},{9,11},{10,... | collective-permute-start | bytes 276488 | tf_op jit(solution)/shard_map/ppermute | solution.py:288
  54.8 1.5 %collective-permute-start.22 = (bf16[360,128]{1,0:T(8,128)(2,1)S(1)}, bf16[360,128]{1,0:T(8,128)(2,1)S(1)}, u32[]{:S(2)}, u32[]{:S(2)}) collective-permute-start(bf16[360,128]{1,0:T(8,128)(2,1)S(1)} %get-tuple-element.117), channel_id=1, source_target_pairs={{0,6},{1,7},{2,4},{3,5},{4,2},{5,3},{6,0},{7,1},{8,14},{9,15},{10,... | collective-permute-start | bytes 276488 | tf_op jit(solution)/shard_map/ppermute | solution.py:288
  56.3 3.1 %collective-permute-done.24 = bf16[360,128]{1,0:T(8,128)(2,1)S(1)} collective-permute-done((bf16[360,128]{1,0:T(8,128)(2,1)S(1)}, bf16[360,128]{1,0:T(8,128)(2,1)S(1)}, u32[]{:S(2)}, u32[]{:S(2)}) %collective-permute-start.24) | collective-permute-done | bytes 92192 | tf_op jit(solution)/shard_map/ppermute | solution.py:288
  59.4 0.8 %collective-permute-done.22 = bf16[360,128]{1,0:T(8,128)(2,1)S(1)} collective-permute-done((bf16[360,128]{1,0:T(8,128)(2,1)S(1)}, bf16[360,128]{1,0:T(8,128)(2,1)S(1)}, u32[]{:S(2)}, u32[]{:S(2)}) %collective-permute-start.22) | collective-permute-done | bytes 92192 | tf_op jit(solution)/shard_map/ppermute | solution.py:288
  60.3 0.8 %fusion.10 = bf16[128,360]{0,1:T(8,128)(2,1)} fusion(bf16[360,128]{1,0:T(8,128)(2,1)S(1)} %collective-permute-done.25, bf16[360,128]{1,0:T(8,128)(2,1)S(1)} %collective-permute-done.24, bf16[360,128]{1,0:T(8,128)(2,1)S(1)} %collective-permute-done.23, bf16[360,128]{1,0:T(8,128)(2,1)S(1)} %collective-permute-done.22, ...), kind=kLoop, calls=%fused_computation.28 | loop fusion | flops 737280 | bytes 829440 | tf_op jit(solution)/shard_map/transpose | solution.py:367
  (33 shorter events, 0.2 us)
Async XLA Ops:
  0.0 13.2 %copy-start = (bf16[1,1440,360]{2,1,0:T(8,128)(2,1)S(1)}, bf16[1,1440,360]{2,1,0:T(8,128)(2,1)}, u32[]{:S(2)}) copy-start(bf16[1,1440,360]{2,1,0:T(8,128)(2,1)} %param.14) | copy-start | bytes 3110404
  0.0 13.2 %copy-start.1 = (bf16[1,1440,360]{2,1,0:T(8,128)(2,1)S(1)}, bf16[1,1440,360]{2,1,0:T(8,128)(2,1)}, u32[]{:S(2)}) copy-start(bf16[1,1440,360]{2,1,0:T(8,128)(2,1)} %param.16) | copy-start | bytes 3110404
  2.4 9.0 %collective-permute-start.5 = (bf16[2,368,128]{2,1,0:T(8,128)(2,1)}, bf16[2,368,128]{2,1,0:T(8,128)(2,1)S(1)}, u32[]{:S(2)}, u32[]{:S(2)}) collective-permute-start(bf16[2,368,128]{2,1,0:T(8,128)(2,1)} %get-tuple-element.65.refs_0_), channel_id=1, source_target_pairs={{0,4},{1,5},{2,6},{3,7},{4,0},{5,1},{6,2},{7,3},{8,12},{9,13},{10,... | collective-permute-start | bytes 565256 | tf_op jit(solution)/shard_map/ppermute | solution.py:288
  5.4 8.7 %collective-permute-start.1 = (bf16[368,128]{1,0:T(8,128)(2,1)}, bf16[368,128]{1,0:T(8,128)(2,1)S(1)}, u32[]{:S(2)}, u32[]{:S(2)}) collective-permute-start(bf16[368,128]{1,0:T(8,128)(2,1)} %get-tuple-element.60), channel_id=1, source_target_pairs={{0,24},{1,25},{2,26},{3,27},{4,28},{5,29},{6,30},{7,31},{8,16},{9,... | collective-permute-start | bytes 282632 | tf_op jit(solution)/shard_map/ppermute | solution.py:288
  9.0 8.0 %collective-permute-start = (bf16[368,128]{1,0:T(8,128)(2,1)}, bf16[368,128]{1,0:T(8,128)(2,1)S(1)}, u32[]{:S(2)}, u32[]{:S(2)}) collective-permute-start(bf16[368,128]{1,0:T(8,128)(2,1)} %get-tuple-element.60), channel_id=1, source_target_pairs={{0,16},{1,17},{2,18},{3,19},{4,20},{5,21},{6,22},{7,23},{8,24},{9,... | collective-permute-start | bytes 282632 | tf_op jit(solution)/shard_map/ppermute | solution.py:288
  9.7 1.2 %copy-start.2 = (bf16[1,360,1440]{2,1,0:T(8,128)(2,1)S(1)}, bf16[1,360,1440]{2,1,0:T(8,128)(2,1)}, u32[]{:S(2)}) copy-start(bf16[1,360,1440]{2,1,0:T(8,128)(2,1)} %param.18) | copy-start | bytes 3110404
  12.4 15.5 %collective-permute-start.7 = (bf16[4,368,128]{2,1,0:T(8,128)(2,1)S(1)}, bf16[4,368,128]{2,1,0:T(8,128)(2,1)S(1)}, u32[]{:S(2)}, u32[]{:S(2)}) collective-permute-start(bf16[4,368,128]{2,1,0:T(8,128)(2,1)S(1)} %pad_maximum_fusion), channel_id=1, source_target_pairs={{0,8},{1,9},{2,10},{3,11},{4,12},{5,13},{6,14},{7,15},{8,0},{9,1},... | collective-permute-start | bytes 1130504 | tf_op jit(solution)/shard_map/ppermute | solution.py:288
  13.2 7.3 %collective-permute-start.6 = (bf16[2,368,128]{2,1,0:T(8,128)(2,1)S(1)}, bf16[2,368,128]{2,1,0:T(8,128)(2,1)S(1)}, u32[]{:S(2)}, u32[]{:S(2)}) collective-permute-start(bf16[2,368,128]{2,1,0:T(8,128)(2,1)S(1)} %collective-permute-done.5.refs_2_), channel_id=1, source_target_pairs={{0,1},{1,0},{2,3},{3,2},{4,5},{5,4},{6,7},{7,6},{8,9},{9,8},{10,11... | collective-permute-start | bytes 565256 | tf_op jit(solution)/shard_map/ppermute | solution.py:288
  13.2 7.3 %copy-start.3 = (bf16[2,368,128]{2,1,0:T(8,128)(2,1)S(1)}, bf16[2,368,128]{2,1,0:T(8,128)(2,1)}, u32[]{:S(2)}) copy-start(bf16[2,368,128]{2,1,0:T(8,128)(2,1)} %get-tuple-element.65.refs_0_) | copy-start | bytes 565252
  13.2 7.3 %copy-start.4 = (bf16[2,368,128]{2,1,0:T(8,128)(2,1)S(1)}, bf16[2,368,128]{2,1,0:T(8,128)(2,1)}, u32[]{:S(2)}) copy-start(bf16[2,368,128]{2,1,0:T(8,128)(2,1)} %get-tuple-element.66.refs_1_) | copy-start | bytes 565252
  17.0 8.7 %collective-permute-start.4 = (bf16[2,368,128]{2,1,0:T(8,128)(2,1)S(1)}, bf16[2,368,128]{2,1,0:T(8,128)(2,1)S(1)}, u32[]{:S(2)}, u32[]{:S(2)}) collective-permute-start(bf16[2,368,128]{2,1,0:T(8,128)(2,1)S(1)} %pad_maximum_fusion.1.refs_0_), channel_id=1, source_target_pairs={{0,6},{1,7},{2,4},{3,5},{4,2},{5,3},{6,0},{7,1},{8,14},{9,15},{10,... | collective-permute-start | bytes 565256 | tf_op jit(solution)/shard_map/ppermute | solution.py:288
  18.5 9.3 %collective-permute-start.3 = (bf16[2,368,128]{2,1,0:T(8,128)(2,1)S(1)}, bf16[2,368,128]{2,1,0:T(8,128)(2,1)S(1)}, u32[]{:S(2)}, u32[]{:S(2)}) collective-permute-start(bf16[2,368,128]{2,1,0:T(8,128)(2,1)S(1)} %pad_maximum_fusion.1.refs_0_), channel_id=1, source_target_pairs={{0,2},{1,3},{2,0},{3,1},{4,6},{5,7},{6,4},{7,5},{8,10},{9,11},{10,... | collective-permute-start | bytes 565256 | tf_op jit(solution)/shard_map/ppermute | solution.py:288
  19.0 8.9 %collective-permute-start.2 = (bf16[2,368,128]{2,1,0:T(8,128)(2,1)S(1)}, bf16[2,368,128]{2,1,0:T(8,128)(2,1)S(1)}, u32[]{:S(2)}, u32[]{:S(2)}) collective-permute-start(bf16[2,368,128]{2,1,0:T(8,128)(2,1)S(1)} %pad_maximum_fusion.1.refs_0_), channel_id=1, source_target_pairs={{0,4},{1,5},{2,6},{3,7},{4,0},{5,1},{6,2},{7,3},{8,12},{9,13},{10,... | collective-permute-start | bytes 565256 | tf_op jit(solution)/shard_map/ppermute | solution.py:288
  27.9 2.8 %collective-permute-start.8 = (bf16[4,360,128]{2,1,0:T(8,128)(2,1)S(1)}, bf16[4,360,128]{2,1,0:T(8,128)(2,1)S(1)}, u32[]{:S(2)}, u32[]{:S(2)}) collective-permute-start(bf16[4,360,128]{2,1,0:T(8,128)(2,1)S(1)} %get-tuple-element.77), channel_id=1, source_target_pairs={{0,1},{1,0},{2,3},{3,2},{4,5},{5,4},{6,7},{7,6},{8,9},{9,8},{10,11... | collective-permute-start | bytes 1105928 | tf_op jit(solution)/shard_map/ppermute | solution.py:288
  27.9 2.0 %collective-permute-start.9 = (bf16[2,368,128]{2,1,0:T(8,128)(2,1)S(1)}, bf16[2,368,128]{2,1,0:T(8,128)(2,1)S(1)}, u32[]{:S(2)}, u32[]{:S(2)}) collective-permute-start(bf16[2,368,128]{2,1,0:T(8,128)(2,1)S(1)} %pad_maximum_fusion.1.refs_0_), channel_id=1, source_target_pairs={{0,1},{1,0},{2,3},{3,2},{4,5},{5,4},{6,7},{7,6},{8,9},{9,8},{10,11... | collective-permute-start | bytes 565256 | tf_op jit(solution)/shard_map/ppermute | solution.py:288
  28.4 1.7 %collective-permute-start.10 = (bf16[2,368,128]{2,1,0:T(8,128)(2,1)S(1)}, bf16[2,368,128]{2,1,0:T(8,128)(2,1)S(1)}, u32[]{:S(2)}, u32[]{:S(2)}) collective-permute-start(bf16[2,368,128]{2,1,0:T(8,128)(2,1)S(1)} %collective-permute-done.3.refs_2_), channel_id=1, source_target_pairs={{0,1},{1,0},{2,3},{3,2},{4,5},{5,4},{6,7},{7,6},{8,9},{9,8},{10,11... | collective-permute-start | bytes 565256 | tf_op jit(solution)/shard_map/ppermute | solution.py:288
  28.4 2.0 %collective-permute-start.11 = (bf16[2,368,128]{2,1,0:T(8,128)(2,1)S(1)}, bf16[2,368,128]{2,1,0:T(8,128)(2,1)S(1)}, u32[]{:S(2)}, u32[]{:S(2)}) collective-permute-start(bf16[2,368,128]{2,1,0:T(8,128)(2,1)S(1)} %collective-permute-done.2.refs_4_), channel_id=1, source_target_pairs={{0,1},{1,0},{2,3},{3,2},{4,5},{5,4},{6,7},{7,6},{8,9},{9,8},{10,11... | collective-permute-start | bytes 565256 | tf_op jit(solution)/shard_map/ppermute | solution.py:288
  28.9 1.7 %collective-permute-start.12 = (bf16[2,368,128]{2,1,0:T(8,128)(2,1)S(1)}, bf16[2,368,128]{2,1,0:T(8,128)(2,1)S(1)}, u32[]{:S(2)}, u32[]{:S(2)}) collective-permute-start(bf16[2,368,128]{2,1,0:T(8,128)(2,1)S(1)} %collective-permute-done.4.refs_6_), channel_id=1, source_target_pairs={{0,1},{1,0},{2,3},{3,2},{4,5},{5,4},{6,7},{7,6},{8,9},{9,8},{10,11... | collective-permute-start | bytes 565256 | tf_op jit(solution)/shard_map/ppermute | solution.py:288
  32.9 2.8 %collective-permute-start.14 = (bf16[4,368,128]{2,1,0:T(8,128)(2,1)S(1)}, bf16[4,368,128]{2,1,0:T(8,128)(2,1)S(1)}, u32[]{:S(2)}, u32[]{:S(2)}) collective-permute-start(bf16[4,368,128]{2,1,0:T(8,128)(2,1)S(1)} %collective-permute-done.7.refs_0_), channel_id=1, source_target_pairs={{0,1},{1,0},{2,3},{3,2},{4,5},{5,4},{6,7},{7,6},{8,9},{9,8},{10,11... | collective-permute-start | bytes 1130504 | tf_op jit(solution)/shard_map/ppermute | solution.py:288
  33.1 2.6 %collective-permute-start.13 = (bf16[4,360,128]{2,1,0:T(8,128)(2,1)S(1)}, bf16[4,360,128]{2,1,0:T(8,128)(2,1)S(1)}, u32[]{:S(2)}, u32[]{:S(2)}) collective-permute-start(bf16[4,360,128]{2,1,0:T(8,128)(2,1)S(1)} %get-tuple-element.90), channel_id=1, source_target_pairs={{0,1},{1,0},{2,3},{3,2},{4,5},{5,4},{6,7},{7,6},{8,9},{9,8},{10,11... | collective-permute-start | bytes 1105928 | tf_op jit(solution)/shard_map/ppermute | solution.py:288
  35.7 2.9 %collective-permute-start.15 = (bf16[4,360,128]{2,1,0:T(8,128)(2,1)S(1)}, bf16[4,360,128]{2,1,0:T(8,128)(2,1)S(1)}, u32[]{:S(2)}, u32[]{:S(2)}) collective-permute-start(bf16[4,360,128]{2,1,0:T(8,128)(2,1)S(1)} %get-tuple-element.107), channel_id=1, source_target_pairs={{0,1},{1,0},{2,3},{3,2},{4,5},{5,4},{6,7},{7,6},{8,9},{9,8},{10,11... | collective-permute-start | bytes 1105928 | tf_op jit(solution)/shard_map/ppermute | solution.py:288
  38.1 4.4 %collective-permute-start.16 = (bf16[4,360,128]{2,1,0:T(8,128)(2,1)S(1)}, bf16[4,360,128]{2,1,0:T(8,128)(2,1)S(1)}, u32[]{:S(2)}, u32[]{:S(2)}) collective-permute-start(bf16[4,360,128]{2,1,0:T(8,128)(2,1)S(1)} %get-tuple-element.109), channel_id=1, source_target_pairs={{0,1},{1,0},{2,3},{3,2},{4,5},{5,4},{6,7},{7,6},{8,9},{9,8},{10,11... | collective-permute-start | bytes 1105928 | tf_op jit(solution)/shard_map/ppermute | solution.py:288
  38.7 8.5 %collective-permute-start.19 = (bf16[2,360,128]{2,1,0:T(8,128)(2,1)S(1)}, bf16[2,360,128]{2,1,0:T(8,128)(2,1)S(1)}, u32[]{:S(2)}, u32[]{:S(2)}) collective-permute-start(bf16[2,360,128]{2,1,0:T(8,128)(2,1)S(1)} %pad_maximum_fusion.3), channel_id=1, source_target_pairs={{0,6},{1,7},{2,4},{3,5},{4,2},{5,3},{6,0},{7,1},{8,14},{9,15},{10,... | collective-permute-start | bytes 552968 | tf_op jit(solution)/shard_map/ppermute | solution.py:288
  40.2 10.1 %collective-permute-start.20 = (bf16[2,360,128]{2,1,0:T(8,128)(2,1)S(1)}, bf16[2,360,128]{2,1,0:T(8,128)(2,1)S(1)}, u32[]{:S(2)}, u32[]{:S(2)}) collective-permute-start(bf16[2,360,128]{2,1,0:T(8,128)(2,1)S(1)} %pad_maximum_fusion.4), channel_id=1, source_target_pairs={{0,2},{1,3},{2,0},{3,1},{4,6},{5,7},{6,4},{7,5},{8,10},{9,11},{10,... | collective-permute-start | bytes 552968 | tf_op jit(solution)/shard_map/ppermute | solution.py:288
  40.9 9.4 %collective-permute-start.18 = (bf16[2,360,128]{2,1,0:T(8,128)(2,1)S(1)}, bf16[2,360,128]{2,1,0:T(8,128)(2,1)S(1)}, u32[]{:S(2)}, u32[]{:S(2)}) collective-permute-start(bf16[2,360,128]{2,1,0:T(8,128)(2,1)S(1)} %pad_maximum_fusion.2), channel_id=1, source_target_pairs={{0,4},{1,5},{2,6},{3,7},{4,0},{5,1},{6,2},{7,3},{8,12},{9,13},{10,... | collective-permute-start | bytes 552968 | tf_op jit(solution)/shard_map/ppermute | solution.py:288
  42.6 10.1 %collective-permute-start.17 = (bf16[4,360,128]{2,1,0:T(8,128)(2,1)S(1)}, bf16[4,360,128]{2,1,0:T(8,128)(2,1)S(1)}, u32[]{:S(2)}, u32[]{:S(2)}) collective-permute-start(bf16[4,360,128]{2,1,0:T(8,128)(2,1)S(1)} %add_convert_fusion), channel_id=1, source_target_pairs={{0,8},{1,9},{2,10},{3,11},{4,12},{5,13},{6,14},{7,15},{8,0},{9,1},... | collective-permute-start | bytes 1105928 | tf_op jit(solution)/shard_map/ppermute | solution.py:288
  50.5 9.0 %collective-permute-start.24 = (bf16[360,128]{1,0:T(8,128)(2,1)S(1)}, bf16[360,128]{1,0:T(8,128)(2,1)S(1)}, u32[]{:S(2)}, u32[]{:S(2)}) collective-permute-start(bf16[360,128]{1,0:T(8,128)(2,1)S(1)} %get-tuple-element.124), channel_id=1, source_target_pairs={{0,16},{1,17},{2,18},{3,19},{4,20},{5,21},{6,22},{7,23},{8,24},{9,... | collective-permute-start | bytes 276488 | tf_op jit(solution)/shard_map/ppermute | solution.py:288
  51.5 8.0 %collective-permute-start.25 = (bf16[360,128]{1,0:T(8,128)(2,1)S(1)}, bf16[360,128]{1,0:T(8,128)(2,1)S(1)}, u32[]{:S(2)}, u32[]{:S(2)}) collective-permute-start(bf16[360,128]{1,0:T(8,128)(2,1)S(1)} %get-tuple-element.125), channel_id=1, source_target_pairs={{0,24},{1,25},{2,26},{3,27},{4,28},{5,29},{6,30},{7,31},{8,16},{9,... | collective-permute-start | bytes 276488 | tf_op jit(solution)/shard_map/ppermute | solution.py:288
  52.7 6.7 %collective-permute-start.21 = (bf16[360,128]{1,0:T(8,128)(2,1)S(1)}, bf16[360,128]{1,0:T(8,128)(2,1)S(1)}, u32[]{:S(2)}, u32[]{:S(2)}) collective-permute-start(bf16[360,128]{1,0:T(8,128)(2,1)S(1)} %get-tuple-element.115), channel_id=1, source_target_pairs={{0,4},{1,5},{2,6},{3,7},{4,0},{5,1},{6,2},{7,3},{8,12},{9,13},{10,... | collective-permute-start | bytes 276488 | tf_op jit(solution)/shard_map/ppermute | solution.py:288
  53.4 6.1 %collective-permute-start.23 = (bf16[360,128]{1,0:T(8,128)(2,1)S(1)}, bf16[360,128]{1,0:T(8,128)(2,1)S(1)}, u32[]{:S(2)}, u32[]{:S(2)}) collective-permute-start(bf16[360,128]{1,0:T(8,128)(2,1)S(1)} %get-tuple-element.116), channel_id=1, source_target_pairs={{0,2},{1,3},{2,0},{3,1},{4,6},{5,7},{6,4},{7,5},{8,10},{9,11},{10,... | collective-permute-start | bytes 276488 | tf_op jit(solution)/shard_map/ppermute | solution.py:288
  54.8 5.5 %collective-permute-start.22 = (bf16[360,128]{1,0:T(8,128)(2,1)S(1)}, bf16[360,128]{1,0:T(8,128)(2,1)S(1)}, u32[]{:S(2)}, u32[]{:S(2)}) collective-permute-start(bf16[360,128]{1,0:T(8,128)(2,1)S(1)} %get-tuple-element.117), channel_id=1, source_target_pairs={{0,6},{1,7},{2,4},{3,5},{4,2},{5,3},{6,0},{7,1},{8,14},{9,15},{10,... | collective-permute-start | bytes 276488 | tf_op jit(solution)/shard_map/ppermute | solution.py:288

commit v12 on v8

--- a/solution.py
+++ b/solution.py
@@ -292,7 +292,7 @@
         tokens.T, norm_gain, expert_ids.T, route_weights.T, groups, per, experts
     )
     z_2, z_3 = swap(one, 2 * along_z), swap(one, 3 * along_z)
-    z_1 = swap(near, along_z)
+    x_0 = swap(near, along_x)
     hidden_pad = round_up(gate_weight.shape[2], 128)
     wide = groups * round_up(quarter, 128)
     biases = jnp.concatenate([gate_bias, up_bias, down_bias], axis=0)
@@ -304,10 +304,11 @@
         (2 * hidden_pad, wide),
         2 * hidden_pad,
     )
-    x_0 = swap(tied((near, inward))[0], along_x)
-    z_1, z_2, z_3, inward = tied((z_1, z_2, z_3, inward))
+    z_2, z_3, inward = tied((z_2, z_3, inward))
     z_high = jnp.stack([z_2, z_3])
-    x_high, y_high = swap(z_high, along_x), swap(z_high, along_y)
+    diagonal = along_x + along_y
+    y_high, d_high = swap(z_high, along_y), swap(z_high, diagonal)
+    x_high = swap(z_high, along_x)
     outward = arrange(
         outward_kernel,
         groups,
@@ -316,42 +317,55 @@
         (wide, hidden_pad),
         wide // groups,
     )
+    x_0, outward = tied((x_0, outward))
     weights = (*inward, *outward)
 
     def expert(arrays, blocks):
         return run_expert(arrays, blocks, ((0, 2), (1, 3)), weights, (quarter, per), 1)
 
-    def line(arrays, index):
-        return [(at, n) for at, n in zip(arrays, index)]
-
-    twice = [0, 0, 1, 1]
-    near_blocks = [line([0, 1, 0, 1], twice), line([2, 3, 2, 3], twice)]
-    far_blocks = [line([0, 1, 2, 3], [n] * groups) for n in range(2)]
-
-    keep_p, send_p = expert((near, far, z_1, swap(z_1, core)), near_blocks)
-    x_high, z_1, x_0, keep_p, send_p = tied((x_high, z_1, x_0, keep_p, send_p))
-    corner, x_1 = swap(x_high, along_y), swap(z_1, along_x)
-    got_p = swap(send_p, core)
-    keep_q, send_q = expert((z_high, swap(z_high, core), y_high, swap(y_high, core)), far_blocks)
-    corner, x_1, keep_q, send_q = tied((corner, x_1, keep_q, send_q))
+    def pieces(arrays, first):
+        return [(arrays[k % 2], first + k // 2) for k in range(groups)]
+
+    z_near = swap(jnp.concatenate([near, x_0], axis=0), along_z)
+    own, other = pieces((0, 1), 0), pieces((2, 3), 0)
+    lines = [[(k, n) for k in range(groups)] for n in range(2)]
+
+    keep_0, send_0 = expert((near, far, x_0, swap(x_0, core)), [own, other])
+    z_core, y_core, d_core = [swap(array, core) for array in (z_high, y_high, d_high)]
+    x_high, y_core, d_core, z_core, keep_0, z_near = tied(
+        (x_high, y_core, d_core, z_core, keep_0, z_near)
+    )
+    far_own = (z_high, z_core, y_high, y_core)
+    far_other = (x_high, swap(x_high, core), d_high, d_core)
+    keep_q, send_q = expert(far_own, lines)
+    keep_q, far_other, z_near = tied((keep_q, far_other, z_near))
+    near_1 = (z_near, swap(z_near, core))
+    keep_s, send_s = expert(far_other, lines)
     got_q = swap(send_q, core)
-    y_p = swap(add_up(keep_p[2:4], got_p[2:4]), along_y)
-    y_q = swap(add_up(keep_q[2:4], got_q[2:4]), along_y)
-    keep_s, send_s = expert((x_high, swap(x_high, core), corner, swap(corner, core)), far_blocks)
-    keep_s, send_s, y_p, x_1 = tied((keep_s, send_s, y_p, x_1))
+    got_q, keep_s = tied((got_q, keep_s))
+    keep_s, send_s, near_1 = tied((keep_s, send_s, near_1))
+    keep_1, send_1 = expert(near_1, [pieces((0, 1), 0), pieces((0, 1), 2)])
     got_s = swap(send_s, core)
-    keep_r, send_r = expert((x_0, swap(x_0, core), x_1, swap(x_1, core)), near_blocks)
-    keep_r, send_r, y_q = tied((keep_r, send_r, y_q))
-    got_r = swap(send_r, core)
-
-    y_s = swap(add_up(keep_s[2:4], got_s[2:4]), along_y)
-    y_r = swap(add_up(keep_r[2:4], got_r[2:4]), along_y)
-    x_s = swap(add_up(keep_s[0:2], got_s[0:2], y_s), along_x)
-    x_r = swap(add_up(keep_r[0:2], got_r[0:2], y_r), along_x)
-    line_2, line_3 = [add_up(keep_q[n], got_q[n], y_q[n], x_s[n]) for n in range(2)]
+    keep_1, send_0, got_s = tied((keep_1, send_0, got_s))
+    got_1, got_0 = swap(send_1, core), swap(send_0, core)
+    far_y, far_x, far_d = [
+        add_up(keep[at : at + 2], got[at : at + 2])
+        for keep, got, at in ((keep_q, got_q, 2), (keep_s, got_s, 0), (keep_s, got_s, 2))
+    ]
+    far_x, far_d, far_y = tied((far_x, far_d, far_y))
+    z_back = swap(add_up(keep_1, got_1), along_z)
+    far_sums = [swap(far_x, along_x), swap(far_d, diagonal), swap(far_y, along_y)]
+    line_2, line_3 = [
+        add_up(keep_q[n], got_q[n], *[part[n] for part in far_sums]) for n in range(2)
+    ]
     back_2, back_3 = swap(line_2, 2 * along_z), swap(line_3, 3 * along_z)
-    back_1 = swap(add_up(keep_p[1], got_p[1], y_p[1], x_r[1]), along_z)
-    mixed = add_up(keep_p[0], got_p[0], y_p[0], x_r[0], back_1, back_2, back_3)
+    z_back, _, _ = tied((z_back, line_2, line_3))
+    terms = (keep_0, got_0, z_back)
+    near_sums = [
+        swap(add_up(*[term[at] for term in terms]), step)
+        for at, step in ((1, along_x), (3, diagonal), (2, along_y))
+    ]
+    mixed = add_up(*[term[0] for term in terms], *near_sums, back_2, back_3)
     return mixed.T
 
 

time: 75.9 us -> 63.1 us (0.83)
  waiting for transfers between devices: 36 us -> 18.3 us
  starting transfers between devices: 22.7 us -> 27.5 us
    ppermute x28 -> x26, waiting for transfers between devices: 36 us -> 18.3 us  [swap(): lax.ppermute(array, ('seq', 'rep'), [(i, i ^ step) for i in range(devices)])]
    ppermute x28 -> x26, starting transfers between devices: 22.7 us -> 27.5 us  [swap(): lax.ppermute(array, ('seq', 'rep'), [(i, i ^ step) for i in range(devices)])]
  transfers between devices with their start and end apart: 28 -> 26, of which waited for: 17 -> 9; matrix products, arithmetic and copies ran while one was open for 2% -> 2% of each run, Pallas kernels for 13% -> 16%
where the time goes in v12:
time: 63.1 us; the launch traced here: 62.9 us
  starting transfers between devices  27.5 us (44%)
  waiting for transfers between devices  18.3 us (29%)
  Pallas kernels  12.3 us (19%)
  local copies, waits for them, and re-layouts  2.49 us (4%)
  other arithmetic  2.04 us (3%)
    ppermute x26, starting transfers between devices, swap(): lax.ppermute(array, ('seq', 'rep'), [(i, i ^ step) for i in range(devices)])  27.5 us
    ppermute x26, waiting for transfers between devices, swap(): lax.ppermute(array, ('seq', 'rep'), [(i, i ^ step) for i in range(devices)])  18.3 us
    pallas_call x4, Pallas kernels, run_expert(): pl.pallas_call(functools.partial(expert_kernel, quarter, per, blocks, slo...  8.79 us
    unnamed x10, local copies, waits for them, and re-layouts  2.49 us
    pallas_call x1, Pallas kernels, make_pieces(): pl.pallas_call(functools.partial(pieces_kernel, groups, per, experts), in...  2.32 us
  transfers between devices with their start and end apart: 26, of which 9 were waited for; matrix products, arithmetic and copies ran while one was open for 2% of the time, Pallas kernels for 16%

profile of v12, /device:TPU:0, one launch (start us, length us, event | category | flops | bytes accessed | tf_op | source)
XLA Modules:
  0.0 62.9 jit_solution(7008359778464714538)
XLA Ops:
  0.0 2.3 %shard_map.100 = (bf16[368,128]{1,0:T(8,128)(2,1)}, bf16[2,368,128]{2,1,0:T(8,128)(2,1)}, bf16[2,368,128]{2,1,0:T(8,128)(2,1)}) custom-call(bf16[1440,128]{1,0:T(8,128)(2,1)} %bitcast.37, f32[1440]{0:T(1024)} %refs_1_.1, s32[4,128]{1,0:T(4,128)} %bitcast.40, f32[4,128]{1,0:T(4,128)} %bitcast.41), custom_call_target="tpu_custom_call" | custom-call | tf_op jit(solution)/shard_map/pallas_call | solution.py:188
  2.3 4.1 %collective-permute-start = (bf16[368,128]{1,0:T(8,128)(2,1)}, bf16[368,128]{1,0:T(8,128)(2,1)S(1)}, u32[]{:S(2)}, u32[]{:S(2)}) collective-permute-start(bf16[368,128]{1,0:T(8,128)(2,1)} %get-tuple-element.52), channel_id=1, source_target_pairs={{0,16},{1,17},{2,18},{3,19},{4,20},{5,21},{6,22},{7,23},{8,24},{9,... | collective-permute-start | bytes 282632 | tf_op jit(solution)/shard_map/ppermute | solution.py:288
  6.4 1.3 %collective-permute-start.1 = (bf16[368,128]{1,0:T(8,128)(2,1)}, bf16[368,128]{1,0:T(8,128)(2,1)S(1)}, u32[]{:S(2)}, u32[]{:S(2)}) collective-permute-start(bf16[368,128]{1,0:T(8,128)(2,1)} %get-tuple-element.52), channel_id=1, source_target_pairs={{0,24},{1,25},{2,26},{3,27},{4,28},{5,29},{6,30},{7,31},{8,16},{9,... | collective-permute-start | bytes 282632 | tf_op jit(solution)/shard_map/ppermute | solution.py:288
  7.8 1.5 %collective-permute-start.8 = (bf16[2,368,128]{2,1,0:T(8,128)(2,1)}, bf16[2,368,128]{2,1,0:T(8,128)(2,1)S(1)}, u32[]{:S(2)}, u32[]{:S(2)}) collective-permute-start(bf16[2,368,128]{2,1,0:T(8,128)(2,1)} %get-tuple-element.57.refs_0_), channel_id=1, source_target_pairs={{0,4},{1,5},{2,6},{3,7},{4,0},{5,1},{6,2},{7,3},{8,12},{9,13},{10,... | collective-permute-start | bytes 565256 | tf_op jit(solution)/shard_map/ppermute | solution.py:288
  9.3 0.7 %pad_maximum_fusion.2.biases_ref = f32[3,360]{1,0:T(4,128)S(1)} fusion(f32[1,360]{1,0:T(1,128)} %param.19, f32[1,360]{1,0:T(1,128)} %param.17, f32[1,360]{1,0:T(1,128)} %param.15), kind=kLoop, calls=%fused_computation.23 | loop fusion | flops 2160 | bytes 8640 | tf_op jit(solution)/shard_map/concatenate | solution.py:298
  10.0 0.0 copy-start.2
  10.0 1.2 %copy-done.2 = bf16[1,360,1440]{2,1,0:T(8,128)(2,1)S(1)} copy-done((bf16[1,360,1440]{2,1,0:T(8,128)(2,1)S(1)}, bf16[1,360,1440]{2,1,0:T(8,128)(2,1)}, u32[]{:S(2)}) %copy-start.2) | copy-done | bytes 1036824
  11.2 0.4 shard_map.102
  11.7 1.2 %copy-done.1 = bf16[1,1440,360]{2,1,0:T(8,128)(2,1)S(1)} copy-done((bf16[1,1440,360]{2,1,0:T(8,128)(2,1)S(1)}, bf16[1,1440,360]{2,1,0:T(8,128)(2,1)}, u32[]{:S(2)}) %copy-start.1) | copy-done | bytes 1036824
  13.0 0.8 %shard_map.101 = (bf16[768,1536]{1,0:T(8,128)(2,1)S(1)}, f32[768,128]{1,0:T(8,128)S(1)}) custom-call(bf16[1440,360]{1,0:T(8,128)(2,1)S(1)} %bitcast.34, bf16[1440,360]{1,0:T(8,128)(2,1)S(1)} %bitcast.35, f32[3,360]{1,0:T(4,128)S(1)} %pad_maximum_fusion.2.biases_ref), custom_call_target="tpu_custom_call" | custom-call | bytes 8294400 | tf_op jit(solution)/shard_map/pallas_call | solution.py:116
  13.8 0.5 collective-permute-done
  14.2 1.7 %collective-permute-start.3 = (bf16[2,368,128]{2,1,0:T(8,128)(2,1)S(1)}, bf16[2,368,128]{2,1,0:T(8,128)(2,1)S(1)}, u32[]{:S(2)}, u32[]{:S(2)}) collective-permute-start(bf16[2,368,128]{2,1,0:T(8,128)(2,1)S(1)} %pad_maximum_fusion.1.refs_0_), channel_id=1, source_target_pairs={{0,2},{1,3},{2,0},{3,1},{4,6},{5,7},{6,4},{7,5},{8,10},{9,11},{10,... | collective-permute-start | bytes 565256 | tf_op jit(solution)/shard_map/ppermute | solution.py:288
  15.9 1.4 %collective-permute-start.5 = (bf16[2,368,128]{2,1,0:T(8,128)(2,1)S(1)}, bf16[2,368,128]{2,1,0:T(8,128)(2,1)S(1)}, u32[]{:S(2)}, u32[]{:S(2)}) collective-permute-start(bf16[2,368,128]{2,1,0:T(8,128)(2,1)S(1)} %pad_maximum_fusion.1.refs_0_), channel_id=1, source_target_pairs={{0,6},{1,7},{2,4},{3,5},{4,2},{5,3},{6,0},{7,1},{8,14},{9,15},{10,... | collective-permute-start | bytes 565256 | tf_op jit(solution)/shard_map/ppermute | solution.py:288
  17.4 2.0 %collective-permute-start.10 = (bf16[4,368,128]{2,1,0:T(8,128)(2,1)S(1)}, bf16[4,368,128]{2,1,0:T(8,128)(2,1)S(1)}, u32[]{:S(2)}, u32[]{:S(2)}) collective-permute-start(bf16[4,368,128]{2,1,0:T(8,128)(2,1)S(1)} %pad_maximum_fusion), channel_id=1, source_target_pairs={{0,8},{1,9},{2,10},{3,11},{4,12},{5,13},{6,14},{7,15},{8,0},{9,1},... | collective-permute-start | bytes 1130504 | tf_op jit(solution)/shard_map/ppermute | solution.py:288
  19.4 0.5 collective-permute-start.2
  19.9 3.7 %collective-permute-done.3.refs_2_ = bf16[2,368,128]{2,1,0:T(8,128)(2,1)S(1)} collective-permute-done((bf16[2,368,128]{2,1,0:T(8,128)(2,1)S(1)}, bf16[2,368,128]{2,1,0:T(8,128)(2,1)S(1)}, u32[]{:S(2)}, u32[]{:S(2)}) %collective-permute-start.3) | collective-permute-done | bytes 188448 | tf_op jit(solution)/shard_map/ppermute | solution.py:288
  23.7 0.5 collective-permute-start.4
  24.2 0.1 collective-permute-start.6
  24.3 2.2 %shard_map.103 = (bf16[4,360,128]{2,1,0:T(8,128)(2,1)S(1)}, bf16[4,360,128]{2,1,0:T(8,128)(2,1)S(1)}) custom-call(bf16[2,368,128]{2,1,0:T(8,128)(2,1)S(1)} %copy-done.3, bf16[2,368,128]{2,1,0:T(8,128)(2,1)S(1)} %copy-done.4, bf16[2,368,128]{2,1,0:T(8,128)(2,1)S(1)} %collective-permute-done.8.refs_2_, ...), custom_call_target="tpu_custom_call" | custom-call | flops 1811939328 | bytes 3538944 | tf_op jit(solution)/shard_map/pallas_call | solution.py:253
  26.5 2.3 %collective-permute-done.10.refs_0_ = bf16[4,368,128]{2,1,0:T(8,128)(2,1)S(1)} collective-permute-done((bf16[4,368,128]{2,1,0:T(8,128)(2,1)S(1)}, bf16[4,368,128]{2,1,0:T(8,128)(2,1)S(1)}, u32[]{:S(2)}, u32[]{:S(2)}) %collective-permute-start.10) | collective-permute-done | bytes 376864 | tf_op jit(solution)/shard_map/ppermute | solution.py:288
  28.8 2.2 %shard_map.104 = (bf16[4,360,128]{2,1,0:T(8,128)(2,1)S(1)}, bf16[4,360,128]{2,1,0:T(8,128)(2,1)S(1)}) custom-call(bf16[2,368,128]{2,1,0:T(8,128)(2,1)S(1)} %pad_maximum_fusion.1.refs_0_, bf16[2,368,128]{2,1,0:T(8,128)(2,1)S(1)} %collective-permute-done.7.refs_1_, bf16[2,368,128]{2,1,0:T(8,128)(2,1)S(1)} %collective-permute-done.3.refs_2_, ...), custom_call_target="tpu_custom_call" | custom-call | flops 1811939328 | bytes 3538944 | tf_op jit(solution)/shard_map/pallas_call | solution.py:253
  31.0 0.6 collective-permute-start.13
  31.6 0.1 collective-permute-start.11
  31.7 2.2 %shard_map.105 = (bf16[4,360,128]{2,1,0:T(8,128)(2,1)S(1)}, bf16[4,360,128]{2,1,0:T(8,128)(2,1)S(1)}) custom-call(bf16[2,368,128]{2,1,0:T(8,128)(2,1)S(1)} %collective-permute-done.2.refs_0_, bf16[2,368,128]{2,1,0:T(8,128)(2,1)S(1)} %collective-permute-done.12.refs_1_, bf16[2,368,128]{2,1,0:T(8,128)(2,1)S(1)} %collective-permute-done.5.refs_2_, ...), custom_call_target="tpu_custom_call" | custom-call | flops 1811939328 | bytes 3538944 | tf_op jit(solution)/shard_map/pallas_call | solution.py:253
  33.9 0.5 collective-permute-start.14
  34.4 2.2 %shard_map.106 = (bf16[4,360,128]{2,1,0:T(8,128)(2,1)S(1)}, bf16[4,360,128]{2,1,0:T(8,128)(2,1)S(1)}) custom-call(bf16[4,368,128]{2,1,0:T(8,128)(2,1)S(1)} %collective-permute-done.10.refs_0_, bf16[4,368,128]{2,1,0:T(8,128)(2,1)S(1)} %collective-permute-done.13.refs_1_, bf16[768,1536]{1,0:T(8,128)(2,1)S(1)} %get-tuple-element.62.refs_4_.refs_2_, ...), custom_call_target="tpu_custom_call" | custom-call | flops 1811939328 | bytes 3538944 | tf_op jit(solution)/shard_map/pallas_call | solution.py:253
  36.6 0.1 collective-permute-start.16
  36.8 0.1 add_convert_fusion.1
  36.8 0.1 add_convert_fusion.2
  36.9 0.6 collective-permute-start.18
  37.5 2.4 %collective-permute-start.19 = (bf16[2,360,128]{2,1,0:T(8,128)(2,1)S(1)}, bf16[2,360,128]{2,1,0:T(8,128)(2,1)S(1)}, u32[]{:S(2)}, u32[]{:S(2)}) collective-permute-start(bf16[2,360,128]{2,1,0:T(8,128)(2,1)S(1)} %get-tuple-element.96), channel_id=1, source_target_pairs={{0,6},{1,7},{2,4},{3,5},{4,2},{5,3},{6,0},{7,1},{8,14},{9,15},{10,... | collective-permute-start | bytes 552968 | tf_op jit(solution)/shard_map/ppermute | solution.py:288
  40.0 0.5 collective-permute-start.20
  40.5 0.1 add_convert_fusion
  40.6 1.8 %collective-permute-start.17 = (bf16[4,360,128]{2,1,0:T(8,128)(2,1)S(1)}, bf16[4,360,128]{2,1,0:T(8,128)(2,1)S(1)}, u32[]{:S(2)}, u32[]{:S(2)}) collective-permute-start(bf16[4,360,128]{2,1,0:T(8,128)(2,1)S(1)} %add_convert_fusion), channel_id=1, source_target_pairs={{0,8},{1,9},{2,10},{3,11},{4,12},{5,13},{6,14},{7,15},{8,0},{9,1},... | collective-permute-start | bytes 1105928 | tf_op jit(solution)/shard_map/ppermute | solution.py:288
  42.4 2.0 %collective-permute-done.18 = bf16[2,360,128]{2,1,0:T(8,128)(2,1)S(1)} collective-permute-done((bf16[2,360,128]{2,1,0:T(8,128)(2,1)S(1)}, bf16[2,360,128]{2,1,0:T(8,128)(2,1)S(1)}, u32[]{:S(2)}, u32[]{:S(2)}) %collective-permute-start.18) | collective-permute-done | bytes 184352 | tf_op jit(solution)/shard_map/ppermute | solution.py:288
  44.5 4.5 %collective-permute-done.19 = bf16[2,360,128]{2,1,0:T(8,128)(2,1)S(1)} collective-permute-done((bf16[2,360,128]{2,1,0:T(8,128)(2,1)S(1)}, bf16[2,360,128]{2,1,0:T(8,128)(2,1)S(1)}, u32[]{:S(2)}, u32[]{:S(2)}) %collective-permute-start.19) | collective-permute-done | bytes 184352 | tf_op jit(solution)/shard_map/ppermute | solution.py:288
  49.0 1.4 %collective-permute-done.20 = bf16[2,360,128]{2,1,0:T(8,128)(2,1)S(1)} collective-permute-done((bf16[2,360,128]{2,1,0:T(8,128)(2,1)S(1)}, bf16[2,360,128]{2,1,0:T(8,128)(2,1)S(1)}, u32[]{:S(2)}, u32[]{:S(2)}) %collective-permute-start.20) | collective-permute-done | bytes 184352 | tf_op jit(solution)/shard_map/ppermute | solution.py:288
  50.4 0.1 fusion.8
  50.5 3.6 %collective-permute-start.24 = (bf16[360,128]{1,0:T(8,128)(2,1)S(1)}, bf16[360,128]{1,0:T(8,128)(2,1)S(1)}, u32[]{:S(2)}, u32[]{:S(2)}) collective-permute-start(bf16[360,128]{1,0:T(8,128)(2,1)S(1)} %get-tuple-element.99), channel_id=1, source_target_pairs={{0,16},{1,17},{2,18},{3,19},{4,20},{5,21},{6,22},{7,23},{8,24},{9,... | collective-permute-start | bytes 276488 | tf_op jit(solution)/shard_map/ppermute | solution.py:288
  54.1 0.5 collective-permute-start.25
  54.7 0.1 fusion.5
  54.8 0.9 %collective-permute-start.21 = (bf16[360,128]{1,0:T(8,128)(2,1)S(1)}, bf16[360,128]{1,0:T(8,128)(2,1)S(1)}, u32[]{:S(2)}, u32[]{:S(2)}) collective-permute-start(bf16[360,128]{1,0:T(8,128)(2,1)S(1)} %get-tuple-element.101), channel_id=1, source_target_pairs={{0,4},{1,5},{2,6},{3,7},{4,0},{5,1},{6,2},{7,3},{8,12},{9,13},{10,... | collective-permute-start | bytes 276488 | tf_op jit(solution)/shard_map/ppermute | solution.py:288
  55.7 1.1 %collective-permute-start.22 = (bf16[360,128]{1,0:T(8,128)(2,1)S(1)}, bf16[360,128]{1,0:T(8,128)(2,1)S(1)}, u32[]{:S(2)}, u32[]{:S(2)}) collective-permute-start(bf16[360,128]{1,0:T(8,128)(2,1)S(1)} %get-tuple-element.103), channel_id=1, source_target_pairs={{0,6},{1,7},{2,4},{3,5},{4,2},{5,3},{6,0},{7,1},{8,14},{9,15},{10,... | collective-permute-start | bytes 276488 | tf_op jit(solution)/shard_map/ppermute | solution.py:288
  56.9 1.5 %collective-permute-start.23 = (bf16[360,128]{1,0:T(8,128)(2,1)S(1)}, bf16[360,128]{1,0:T(8,128)(2,1)S(1)}, u32[]{:S(2)}, u32[]{:S(2)}) collective-permute-start(bf16[360,128]{1,0:T(8,128)(2,1)S(1)} %get-tuple-element.102), channel_id=1, source_target_pairs={{0,2},{1,3},{2,0},{3,1},{4,6},{5,7},{6,4},{7,5},{8,10},{9,11},{10,... | collective-permute-start | bytes 276488 | tf_op jit(solution)/shard_map/ppermute | solution.py:288
  58.4 2.3 %collective-permute-done.24 = bf16[360,128]{1,0:T(8,128)(2,1)S(1)} collective-permute-done((bf16[360,128]{1,0:T(8,128)(2,1)S(1)}, bf16[360,128]{1,0:T(8,128)(2,1)S(1)}, u32[]{:S(2)}, u32[]{:S(2)}) %collective-permute-start.24) | collective-permute-done | bytes 92192 | tf_op jit(solution)/shard_map/ppermute | solution.py:288
  60.7 0.6 collective-permute-done.22
  61.3 0.9 %collective-permute-done.23 = bf16[360,128]{1,0:T(8,128)(2,1)S(1)} collective-permute-done((bf16[360,128]{1,0:T(8,128)(2,1)S(1)}, bf16[360,128]{1,0:T(8,128)(2,1)S(1)}, u32[]{:S(2)}, u32[]{:S(2)}) %collective-permute-start.23) | collective-permute-done | bytes 92192 | tf_op jit(solution)/shard_map/ppermute | solution.py:288
  62.2 0.7 %fusion.10 = bf16[128,360]{0,1:T(8,128)(2,1)} fusion(bf16[360,128]{1,0:T(8,128)(2,1)S(1)} %collective-permute-done.25, bf16[360,128]{1,0:T(8,128)(2,1)S(1)} %collective-permute-done.24, bf16[360,128]{1,0:T(8,128)(2,1)S(1)} %collective-permute-done.23, bf16[360,128]{1,0:T(8,128)(2,1)S(1)} %collective-permute-done.22, ...), kind=kLoop, calls=%fused_computation.22 | loop fusion | flops 737280 | bytes 829440 | tf_op jit(solution)/shard_map/transpose | solution.py:369
  (30 shorter events, 0.1 us)
Async XLA Ops:
  0.0 11.7 %copy-start = (bf16[1,1440,360]{2,1,0:T(8,128)(2,1)S(1)}, bf16[1,1440,360]{2,1,0:T(8,128)(2,1)}, u32[]{:S(2)}) copy-start(bf16[1,1440,360]{2,1,0:T(8,128)(2,1)} %param.14) | copy-start | bytes 3110404
  2.3 11.9 %collective-permute-start = (bf16[368,128]{1,0:T(8,128)(2,1)}, bf16[368,128]{1,0:T(8,128)(2,1)S(1)}, u32[]{:S(2)}, u32[]{:S(2)}) collective-permute-start(bf16[368,128]{1,0:T(8,128)(2,1)} %get-tuple-element.52), channel_id=1, source_target_pairs={{0,16},{1,17},{2,18},{3,19},{4,20},{5,21},{6,22},{7,23},{8,24},{9,... | collective-permute-start | bytes 282632 | tf_op jit(solution)/shard_map/ppermute | solution.py:288
  6.4 7.8 %collective-permute-start.1 = (bf16[368,128]{1,0:T(8,128)(2,1)}, bf16[368,128]{1,0:T(8,128)(2,1)S(1)}, u32[]{:S(2)}, u32[]{:S(2)}) collective-permute-start(bf16[368,128]{1,0:T(8,128)(2,1)} %get-tuple-element.52), channel_id=1, source_target_pairs={{0,24},{1,25},{2,26},{3,27},{4,28},{5,29},{6,30},{7,31},{8,16},{9,... | collective-permute-start | bytes 282632 | tf_op jit(solution)/shard_map/ppermute | solution.py:288
  7.8 9.6 %collective-permute-start.8 = (bf16[2,368,128]{2,1,0:T(8,128)(2,1)}, bf16[2,368,128]{2,1,0:T(8,128)(2,1)S(1)}, u32[]{:S(2)}, u32[]{:S(2)}) collective-permute-start(bf16[2,368,128]{2,1,0:T(8,128)(2,1)} %get-tuple-element.57.refs_0_), channel_id=1, source_target_pairs={{0,4},{1,5},{2,6},{3,7},{4,0},{5,1},{6,2},{7,3},{8,12},{9,13},{10,... | collective-permute-start | bytes 565256 | tf_op jit(solution)/shard_map/ppermute | solution.py:288
  10.0 1.2 %copy-start.2 = (bf16[1,360,1440]{2,1,0:T(8,128)(2,1)S(1)}, bf16[1,360,1440]{2,1,0:T(8,128)(2,1)}, u32[]{:S(2)}) copy-start(bf16[1,360,1440]{2,1,0:T(8,128)(2,1)} %param.18) | copy-start | bytes 3110404
  11.7 1.2 %copy-start.1 = (bf16[1,1440,360]{2,1,0:T(8,128)(2,1)S(1)}, bf16[1,1440,360]{2,1,0:T(8,128)(2,1)}, u32[]{:S(2)}) copy-start(bf16[1,1440,360]{2,1,0:T(8,128)(2,1)} %param.16) | copy-start | bytes 3110404
  13.0 4.4 %copy-start.3 = (bf16[2,368,128]{2,1,0:T(8,128)(2,1)S(1)}, bf16[2,368,128]{2,1,0:T(8,128)(2,1)}, u32[]{:S(2)}) copy-start(bf16[2,368,128]{2,1,0:T(8,128)(2,1)} %get-tuple-element.57.refs_0_) | copy-start | bytes 565252
  13.7 10.5 %copy-start.4 = (bf16[2,368,128]{2,1,0:T(8,128)(2,1)S(1)}, bf16[2,368,128]{2,1,0:T(8,128)(2,1)}, u32[]{:S(2)}) copy-start(bf16[2,368,128]{2,1,0:T(8,128)(2,1)} %get-tuple-element.58.refs_1_) | copy-start | bytes 565252
  14.2 9.4 %collective-permute-start.3 = (bf16[2,368,128]{2,1,0:T(8,128)(2,1)S(1)}, bf16[2,368,128]{2,1,0:T(8,128)(2,1)S(1)}, u32[]{:S(2)}, u32[]{:S(2)}) collective-permute-start(bf16[2,368,128]{2,1,0:T(8,128)(2,1)S(1)} %pad_maximum_fusion.1.refs_0_), channel_id=1, source_target_pairs={{0,2},{1,3},{2,0},{3,1},{4,6},{5,7},{6,4},{7,5},{8,10},{9,11},{10,... | collective-permute-start | bytes 565256 | tf_op jit(solution)/shard_map/ppermute | solution.py:288
  15.9 7.7 %collective-permute-start.5 = (bf16[2,368,128]{2,1,0:T(8,128)(2,1)S(1)}, bf16[2,368,128]{2,1,0:T(8,128)(2,1)S(1)}, u32[]{:S(2)}, u32[]{:S(2)}) collective-permute-start(bf16[2,368,128]{2,1,0:T(8,128)(2,1)S(1)} %pad_maximum_fusion.1.refs_0_), channel_id=1, source_target_pairs={{0,6},{1,7},{2,4},{3,5},{4,2},{5,3},{6,0},{7,1},{8,14},{9,15},{10,... | collective-permute-start | bytes 565256 | tf_op jit(solution)/shard_map/ppermute | solution.py:288
  17.4 6.8 %collective-permute-start.9 = (bf16[2,368,128]{2,1,0:T(8,128)(2,1)S(1)}, bf16[2,368,128]{2,1,0:T(8,128)(2,1)S(1)}, u32[]{:S(2)}, u32[]{:S(2)}) collective-permute-start(bf16[2,368,128]{2,1,0:T(8,128)(2,1)S(1)} %collective-permute-done.8.refs_2_), channel_id=1, source_target_pairs={{0,1},{1,0},{2,3},{3,2},{4,5},{5,4},{6,7},{7,6},{8,9},{9,8},{10,11... | collective-permute-start | bytes 565256 | tf_op jit(solution)/shard_map/ppermute | solution.py:288
  17.4 11.4 %collective-permute-start.10 = (bf16[4,368,128]{2,1,0:T(8,128)(2,1)S(1)}, bf16[4,368,128]{2,1,0:T(8,128)(2,1)S(1)}, u32[]{:S(2)}, u32[]{:S(2)}) collective-permute-start(bf16[4,368,128]{2,1,0:T(8,128)(2,1)S(1)} %pad_maximum_fusion), channel_id=1, source_target_pairs={{0,8},{1,9},{2,10},{3,11},{4,12},{5,13},{6,14},{7,15},{8,0},{9,1},... | collective-permute-start | bytes 1130504 | tf_op jit(solution)/shard_map/ppermute | solution.py:288
  19.4 7.1 %collective-permute-start.2 = (bf16[2,368,128]{2,1,0:T(8,128)(2,1)S(1)}, bf16[2,368,128]{2,1,0:T(8,128)(2,1)S(1)}, u32[]{:S(2)}, u32[]{:S(2)}) collective-permute-start(bf16[2,368,128]{2,1,0:T(8,128)(2,1)S(1)} %pad_maximum_fusion.1.refs_0_), channel_id=1, source_target_pairs={{0,4},{1,5},{2,6},{3,7},{4,0},{5,1},{6,2},{7,3},{8,12},{9,13},{10,... | collective-permute-start | bytes 565256 | tf_op jit(solution)/shard_map/ppermute | solution.py:288
  23.7 2.8 %collective-permute-start.7 = (bf16[2,368,128]{2,1,0:T(8,128)(2,1)S(1)}, bf16[2,368,128]{2,1,0:T(8,128)(2,1)S(1)}, u32[]{:S(2)}, u32[]{:S(2)}) collective-permute-start(bf16[2,368,128]{2,1,0:T(8,128)(2,1)S(1)} %pad_maximum_fusion.1.refs_0_), channel_id=1, source_target_pairs={{0,1},{1,0},{2,3},{3,2},{4,5},{5,4},{6,7},{7,6},{8,9},{9,8},{10,11... | collective-permute-start | bytes 565256 | tf_op jit(solution)/shard_map/ppermute | solution.py:288
  23.7 2.8 %collective-permute-start.4 = (bf16[2,368,128]{2,1,0:T(8,128)(2,1)S(1)}, bf16[2,368,128]{2,1,0:T(8,128)(2,1)S(1)}, u32[]{:S(2)}, u32[]{:S(2)}) collective-permute-start(bf16[2,368,128]{2,1,0:T(8,128)(2,1)S(1)} %collective-permute-done.3.refs_2_), channel_id=1, source_target_pairs={{0,1},{1,0},{2,3},{3,2},{4,5},{5,4},{6,7},{7,6},{8,9},{9,8},{10,11... | collective-permute-start | bytes 565256 | tf_op jit(solution)/shard_map/ppermute | solution.py:288
  24.2 2.3 %collective-permute-start.6 = (bf16[2,368,128]{2,1,0:T(8,128)(2,1)S(1)}, bf16[2,368,128]{2,1,0:T(8,128)(2,1)S(1)}, u32[]{:S(2)}, u32[]{:S(2)}) collective-permute-start(bf16[2,368,128]{2,1,0:T(8,128)(2,1)S(1)} %collective-permute-done.5.refs_2_), channel_id=1, source_target_pairs={{0,1},{1,0},{2,3},{3,2},{4,5},{5,4},{6,7},{7,6},{8,9},{9,8},{10,11... | collective-permute-start | bytes 565256 | tf_op jit(solution)/shard_map/ppermute | solution.py:288
  28.8 2.2 %collective-permute-start.12 = (bf16[2,368,128]{2,1,0:T(8,128)(2,1)S(1)}, bf16[2,368,128]{2,1,0:T(8,128)(2,1)S(1)}, u32[]{:S(2)}, u32[]{:S(2)}) collective-permute-start(bf16[2,368,128]{2,1,0:T(8,128)(2,1)S(1)} %collective-permute-done.2.refs_0_), channel_id=1, source_target_pairs={{0,1},{1,0},{2,3},{3,2},{4,5},{5,4},{6,7},{7,6},{8,9},{9,8},{10,11... | collective-permute-start | bytes 565256 | tf_op jit(solution)/shard_map/ppermute | solution.py:288
  31.0 2.9 %collective-permute-start.13 = (bf16[4,368,128]{2,1,0:T(8,128)(2,1)S(1)}, bf16[4,368,128]{2,1,0:T(8,128)(2,1)S(1)}, u32[]{:S(2)}, u32[]{:S(2)}) collective-permute-start(bf16[4,368,128]{2,1,0:T(8,128)(2,1)S(1)} %collective-permute-done.10.refs_0_), channel_id=1, source_target_pairs={{0,1},{1,0},{2,3},{3,2},{4,5},{5,4},{6,7},{7,6},{8,9},{9,8},{10,11... | collective-permute-start | bytes 1130504 | tf_op jit(solution)/shard_map/ppermute | solution.py:288
  31.6 2.3 %collective-permute-start.11 = (bf16[4,360,128]{2,1,0:T(8,128)(2,1)S(1)}, bf16[4,360,128]{2,1,0:T(8,128)(2,1)S(1)}, u32[]{:S(2)}, u32[]{:S(2)}) collective-permute-start(bf16[4,360,128]{2,1,0:T(8,128)(2,1)S(1)} %get-tuple-element.70), channel_id=1, source_target_pairs={{0,1},{1,0},{2,3},{3,2},{4,5},{5,4},{6,7},{7,6},{8,9},{9,8},{10,11... | collective-permute-start | bytes 1105928 | tf_op jit(solution)/shard_map/ppermute | solution.py:288
  33.9 2.9 %collective-permute-start.14 = (bf16[4,360,128]{2,1,0:T(8,128)(2,1)S(1)}, bf16[4,360,128]{2,1,0:T(8,128)(2,1)S(1)}, u32[]{:S(2)}, u32[]{:S(2)}) collective-permute-start(bf16[4,360,128]{2,1,0:T(8,128)(2,1)S(1)} %get-tuple-element.87), channel_id=1, source_target_pairs={{0,1},{1,0},{2,3},{3,2},{4,5},{5,4},{6,7},{7,6},{8,9},{9,8},{10,11... | collective-permute-start | bytes 1105928 | tf_op jit(solution)/shard_map/ppermute | solution.py:288
  36.6 3.9 %collective-permute-start.16 = (bf16[4,360,128]{2,1,0:T(8,128)(2,1)S(1)}, bf16[4,360,128]{2,1,0:T(8,128)(2,1)S(1)}, u32[]{:S(2)}, u32[]{:S(2)}) collective-permute-start(bf16[4,360,128]{2,1,0:T(8,128)(2,1)S(1)} %get-tuple-element.90), channel_id=1, source_target_pairs={{0,1},{1,0},{2,3},{3,2},{4,5},{5,4},{6,7},{7,6},{8,9},{9,8},{10,11... | collective-permute-start | bytes 1105928 | tf_op jit(solution)/shard_map/ppermute | solution.py:288
  36.9 7.5 %collective-permute-start.18 = (bf16[2,360,128]{2,1,0:T(8,128)(2,1)S(1)}, bf16[2,360,128]{2,1,0:T(8,128)(2,1)S(1)}, u32[]{:S(2)}, u32[]{:S(2)}) collective-permute-start(bf16[2,360,128]{2,1,0:T(8,128)(2,1)S(1)} %get-tuple-element.95), channel_id=1, source_target_pairs={{0,4},{1,5},{2,6},{3,7},{4,0},{5,1},{6,2},{7,3},{8,12},{9,13},{10,... | collective-permute-start | bytes 552968 | tf_op jit(solution)/shard_map/ppermute | solution.py:288
  37.5 11.5 %collective-permute-start.19 = (bf16[2,360,128]{2,1,0:T(8,128)(2,1)S(1)}, bf16[2,360,128]{2,1,0:T(8,128)(2,1)S(1)}, u32[]{:S(2)}, u32[]{:S(2)}) collective-permute-start(bf16[2,360,128]{2,1,0:T(8,128)(2,1)S(1)} %get-tuple-element.96), channel_id=1, source_target_pairs={{0,6},{1,7},{2,4},{3,5},{4,2},{5,3},{6,0},{7,1},{8,14},{9,15},{10,... | collective-permute-start | bytes 552968 | tf_op jit(solution)/shard_map/ppermute | solution.py:288
  40.0 10.4 %collective-permute-start.20 = (bf16[2,360,128]{2,1,0:T(8,128)(2,1)S(1)}, bf16[2,360,128]{2,1,0:T(8,128)(2,1)S(1)}, u32[]{:S(2)}, u32[]{:S(2)}) collective-permute-start(bf16[2,360,128]{2,1,0:T(8,128)(2,1)S(1)} %add_convert_fusion.1), channel_id=1, source_target_pairs={{0,2},{1,3},{2,0},{3,1},{4,6},{5,7},{6,4},{7,5},{8,10},{9,11},{10,... | collective-permute-start | bytes 552968 | tf_op jit(solution)/shard_map/ppermute | solution.py:288
  40.6 14.1 %collective-permute-start.17 = (bf16[4,360,128]{2,1,0:T(8,128)(2,1)S(1)}, bf16[4,360,128]{2,1,0:T(8,128)(2,1)S(1)}, u32[]{:S(2)}, u32[]{:S(2)}) collective-permute-start(bf16[4,360,128]{2,1,0:T(8,128)(2,1)S(1)} %add_convert_fusion), channel_id=1, source_target_pairs={{0,8},{1,9},{2,10},{3,11},{4,12},{5,13},{6,14},{7,15},{8,0},{9,1},... | collective-permute-start | bytes 1105928 | tf_op jit(solution)/shard_map/ppermute | solution.py:288
  42.4 12.3 %collective-permute-start.15 = (bf16[4,360,128]{2,1,0:T(8,128)(2,1)S(1)}, bf16[4,360,128]{2,1,0:T(8,128)(2,1)S(1)}, u32[]{:S(2)}, u32[]{:S(2)}) collective-permute-start(bf16[4,360,128]{2,1,0:T(8,128)(2,1)S(1)} %get-tuple-element.88), channel_id=1, source_target_pairs={{0,1},{1,0},{2,3},{3,2},{4,5},{5,4},{6,7},{7,6},{8,9},{9,8},{10,11... | collective-permute-start | bytes 1105928 | tf_op jit(solution)/shard_map/ppermute | solution.py:288
  50.5 10.2 %collective-permute-start.24 = (bf16[360,128]{1,0:T(8,128)(2,1)S(1)}, bf16[360,128]{1,0:T(8,128)(2,1)S(1)}, u32[]{:S(2)}, u32[]{:S(2)}) collective-permute-start(bf16[360,128]{1,0:T(8,128)(2,1)S(1)} %get-tuple-element.99), channel_id=1, source_target_pairs={{0,16},{1,17},{2,18},{3,19},{4,20},{5,21},{6,22},{7,23},{8,24},{9,... | collective-permute-start | bytes 276488 | tf_op jit(solution)/shard_map/ppermute | solution.py:288
  54.1 6.5 %collective-permute-start.25 = (bf16[360,128]{1,0:T(8,128)(2,1)S(1)}, bf16[360,128]{1,0:T(8,128)(2,1)S(1)}, u32[]{:S(2)}, u32[]{:S(2)}) collective-permute-start(bf16[360,128]{1,0:T(8,128)(2,1)S(1)} %get-tuple-element.100), channel_id=1, source_target_pairs={{0,24},{1,25},{2,26},{3,27},{4,28},{5,29},{6,30},{7,31},{8,16},{9,... | collective-permute-start | bytes 276488 | tf_op jit(solution)/shard_map/ppermute | solution.py:288
  54.8 5.9 %collective-permute-start.21 = (bf16[360,128]{1,0:T(8,128)(2,1)S(1)}, bf16[360,128]{1,0:T(8,128)(2,1)S(1)}, u32[]{:S(2)}, u32[]{:S(2)}) collective-permute-start(bf16[360,128]{1,0:T(8,128)(2,1)S(1)} %get-tuple-element.101), channel_id=1, source_target_pairs={{0,4},{1,5},{2,6},{3,7},{4,0},{5,1},{6,2},{7,3},{8,12},{9,13},{10,... | collective-permute-start | bytes 276488 | tf_op jit(solution)/shard_map/ppermute | solution.py:288
  55.7 5.5 %collective-permute-start.22 = (bf16[360,128]{1,0:T(8,128)(2,1)S(1)}, bf16[360,128]{1,0:T(8,128)(2,1)S(1)}, u32[]{:S(2)}, u32[]{:S(2)}) collective-permute-start(bf16[360,128]{1,0:T(8,128)(2,1)S(1)} %get-tuple-element.103), channel_id=1, source_target_pairs={{0,6},{1,7},{2,4},{3,5},{4,2},{5,3},{6,0},{7,1},{8,14},{9,15},{10,... | collective-permute-start | bytes 276488 | tf_op jit(solution)/shard_map/ppermute | solution.py:288
  56.9 5.3 %collective-permute-start.23 = (bf16[360,128]{1,0:T(8,128)(2,1)S(1)}, bf16[360,128]{1,0:T(8,128)(2,1)S(1)}, u32[]{:S(2)}, u32[]{:S(2)}) collective-permute-start(bf16[360,128]{1,0:T(8,128)(2,1)S(1)} %get-tuple-element.102), channel_id=1, source_target_pairs={{0,2},{1,3},{2,0},{3,1},{4,6},{5,7},{6,4},{7,5},{8,10},{9,11},{10,... | collective-permute-start | bytes 276488 | tf_op jit(solution)/shard_map/ppermute | solution.py:288

commit v13 on v11

--- a/solution.py
+++ b/solution.py
@@ -329,13 +329,12 @@
         (near, far, x_0, swap(x_0, core)), pairs(0, 2), slots, weights, sizes, 1
     )
     z_near = swap(jnp.concatenate([near, x_0], axis=0), along_z)
-    x_high, y_high, d_high, keep_0, send_0, z_near = tied(
-        (x_high, y_high, d_high, keep_0, send_0, z_near)
-    )
-    got_0 = swap(send_0, core)
-    high = (z_high, swap(z_high, core), y_high, swap(y_high, core))
+    z_core = swap(z_high, core)
+    x_high, y_high, d_high, keep_0, z_core, z_near = tied(
+        (x_high, y_high, d_high, keep_0, z_core, z_near)
+    )
+    high = (z_high, z_core, y_high, swap(y_high, core))
     high = high + (x_high, swap(x_high, core), d_high, swap(d_high, core))
-    got_0, high = tied((got_0, high))
     line = [[[(4 * x + k, n) for k in range(groups)] for x in range(2)] for n in range(2)]
     keep_2, send_2 = run_expert(high, line[0], slots, weights, sizes, 1)
     got_2 = swap(send_2, core)
@@ -347,7 +346,8 @@
     blocks = [[(k % 2, 2 * x + k // 2) for k in range(groups)] for x in range(2)]
     keep_1, send_1 = run_expert(near_1, blocks, slots, weights, sizes, 1)
     got_1 = swap(send_1, core)
-    keep_1, got_3 = tied((keep_1, got_3))
+    keep_1, got_3, send_0 = tied((keep_1, got_3, send_0))
+    got_0 = swap(send_0, core)
     z_back = swap(add_up(keep_1, got_1), along_z)
 
     def spread(*terms):

time: 61.2 us -> 62.2 us (1.016)
  waiting for transfers between devices: 21.4 us -> 22.2 us
    ppermute x26, waiting for transfers between devices: 21.4 us -> 22.2 us  [swap(): lax.ppermute(array, ('seq', 'rep'), [(i, i ^ step) for i in range(devices)])]
  transfers between devices with their start and end apart: 26 -> 26, of which waited for: 12 -> 11; matrix products, arithmetic and copies ran while one was open for 4% -> 4% of each run, Pallas kernels for 13% -> 13%
where the time goes in v13:
time: 62.2 us; the launch traced here: 62 us
  starting transfers between devices  22.9 us (37%)
  waiting for transfers between devices  22.2 us (36%)
  Pallas kernels  12.4 us (20%)
  other arithmetic  3.02 us (5%)
  local copies, waits for them, and re-layouts  1.25 us (2%)
    ppermute x26, starting transfers between devices, swap(): lax.ppermute(array, ('seq', 'rep'), [(i, i ^ step) for i in range(devices)])  22.9 us
    ppermute x26, waiting for transfers between devices, swap(): lax.ppermute(array, ('seq', 'rep'), [(i, i ^ step) for i in range(devices)])  22.2 us
    pallas_call x4, Pallas kernels, run_expert(): pl.pallas_call(functools.partial(expert_kernel, quarter, per, blocks, slo...  8.79 us
    pallas_call x1, Pallas kernels, make_pieces(): pl.pallas_call(functools.partial(pieces_kernel, groups, per, experts), in...  2.35 us
    unnamed x10, local copies, waits for them, and re-layouts  1.25 us
  transfers between devices with their start and end apart: 26, of which 11 were waited for; matrix products, arithmetic and copies ran while one was open for 4% of the time, Pallas kernels for 13%

profile of v13, /device:TPU:0, one launch (start us, length us, event | category | flops | bytes accessed | tf_op | source)
XLA Modules:
  0.0 62.0 jit_solution(6266344008281068823)
XLA Ops:
  0.0 2.4 %shard_map.100 = (bf16[368,128]{1,0:T(8,128)(2,1)}, bf16[2,368,128]{2,1,0:T(8,128)(2,1)}, bf16[2,368,128]{2,1,0:T(8,128)(2,1)}) custom-call(bf16[1440,128]{1,0:T(8,128)(2,1)} %bitcast.37, f32[1440]{0:T(1024)} %refs_1_.1, s32[4,128]{1,0:T(4,128)} %bitcast.40, f32[4,128]{1,0:T(4,128)} %bitcast.41), custom_call_target="tpu_custom_call" | custom-call | tf_op jit(solution)/shard_map/pallas_call | solution.py:188
  2.4 3.0 %collective-permute-start.5 = (bf16[2,368,128]{2,1,0:T(8,128)(2,1)}, bf16[2,368,128]{2,1,0:T(8,128)(2,1)S(1)}, u32[]{:S(2)}, u32[]{:S(2)}) collective-permute-start(bf16[2,368,128]{2,1,0:T(8,128)(2,1)} %get-tuple-element.57.refs_0_), channel_id=1, source_target_pairs={{0,4},{1,5},{2,6},{3,7},{4,0},{5,1},{6,2},{7,3},{8,12},{9,13},{10,... | collective-permute-start | bytes 565256 | tf_op jit(solution)/shard_map/ppermute | solution.py:288
  5.4 3.6 %collective-permute-start.1 = (bf16[368,128]{1,0:T(8,128)(2,1)}, bf16[368,128]{1,0:T(8,128)(2,1)S(1)}, u32[]{:S(2)}, u32[]{:S(2)}) collective-permute-start(bf16[368,128]{1,0:T(8,128)(2,1)} %get-tuple-element.52), channel_id=1, source_target_pairs={{0,24},{1,25},{2,26},{3,27},{4,28},{5,29},{6,30},{7,31},{8,16},{9,... | collective-permute-start | bytes 282632 | tf_op jit(solution)/shard_map/ppermute | solution.py:288
  9.0 0.7 %pad_maximum_fusion.5.biases_ref = f32[3,360]{1,0:T(4,128)S(1)} fusion(f32[1,360]{1,0:T(1,128)} %param.19, f32[1,360]{1,0:T(1,128)} %param.17, f32[1,360]{1,0:T(1,128)} %param.15), kind=kLoop, calls=%fused_computation.29 | loop fusion | flops 2160 | bytes 8640 | tf_op jit(solution)/shard_map/concatenate | solution.py:298
  9.7 1.2 %copy-done.2 = bf16[1,360,1440]{2,1,0:T(8,128)(2,1)S(1)} copy-done((bf16[1,360,1440]{2,1,0:T(8,128)(2,1)S(1)}, bf16[1,360,1440]{2,1,0:T(8,128)(2,1)}, u32[]{:S(2)}) %copy-start.2) | copy-done | bytes 1036824
  11.0 0.4 shard_map.102
  11.4 0.1 collective-permute-start.6
  11.5 1.0 %pad_maximum_fusion = bf16[4,368,128]{2,1,0:T(8,128)(2,1)S(1)} fusion(bf16[2,368,128]{2,1,0:T(8,128)(2,1)S(1)} %collective-permute-done.5.refs_2_, bf16[2,368,128]{2,1,0:T(8,128)(2,1)} %get-tuple-element.57.refs_0_), kind=kLoop, calls=%fused_computation.1 | loop fusion | flops 188416 | bytes 753664 | tf_op jit(solution)/shard_map/concatenate | solution.py:331
  12.4 0.8 %collective-permute-start.8 = (bf16[4,368,128]{2,1,0:T(8,128)(2,1)S(1)}, bf16[4,368,128]{2,1,0:T(8,128)(2,1)S(1)}, u32[]{:S(2)}, u32[]{:S(2)}) collective-permute-start(bf16[4,368,128]{2,1,0:T(8,128)(2,1)S(1)} %pad_maximum_fusion), channel_id=1, source_target_pairs={{0,8},{1,9},{2,10},{3,11},{4,12},{5,13},{6,14},{7,15},{8,0},{9,1},... | collective-permute-start | bytes 1130504 | tf_op jit(solution)/shard_map/ppermute | solution.py:288
  13.3 0.8 %shard_map.101 = (bf16[768,1536]{1,0:T(8,128)(2,1)S(1)}, f32[768,128]{1,0:T(8,128)S(1)}) custom-call(bf16[1440,360]{1,0:T(8,128)(2,1)S(1)} %bitcast.34, bf16[1440,360]{1,0:T(8,128)(2,1)S(1)} %bitcast.35, f32[3,360]{1,0:T(4,128)S(1)} %pad_maximum_fusion.5.biases_ref), custom_call_target="tpu_custom_call" | custom-call | bytes 8294400 | tf_op jit(solution)/shard_map/pallas_call | solution.py:116
  14.1 2.8 %collective-permute-done = bf16[368,128]{1,0:T(8,128)(2,1)S(1)} collective-permute-done((bf16[368,128]{1,0:T(8,128)(2,1)}, bf16[368,128]{1,0:T(8,128)(2,1)S(1)}, u32[]{:S(2)}, u32[]{:S(2)}) %collective-permute-start) | collective-permute-done | bytes 94240 | tf_op jit(solution)/shard_map/ppermute | solution.py:288
  17.0 1.6 %collective-permute-start.4 = (bf16[2,368,128]{2,1,0:T(8,128)(2,1)S(1)}, bf16[2,368,128]{2,1,0:T(8,128)(2,1)S(1)}, u32[]{:S(2)}, u32[]{:S(2)}) collective-permute-start(bf16[2,368,128]{2,1,0:T(8,128)(2,1)S(1)} %pad_maximum_fusion.1.refs_0_), channel_id=1, source_target_pairs={{0,6},{1,7},{2,4},{3,5},{4,2},{5,3},{6,0},{7,1},{8,14},{9,15},{10,... | collective-permute-start | bytes 565256 | tf_op jit(solution)/shard_map/ppermute | solution.py:288
  18.6 0.5 collective-permute-start.3
  19.1 1.5 %collective-permute-start.2 = (bf16[2,368,128]{2,1,0:T(8,128)(2,1)S(1)}, bf16[2,368,128]{2,1,0:T(8,128)(2,1)S(1)}, u32[]{:S(2)}, u32[]{:S(2)}) collective-permute-start(bf16[2,368,128]{2,1,0:T(8,128)(2,1)S(1)} %pad_maximum_fusion.1.refs_0_), channel_id=1, source_target_pairs={{0,4},{1,5},{2,6},{3,7},{4,0},{5,1},{6,2},{7,3},{8,12},{9,13},{10,... | collective-permute-start | bytes 565256 | tf_op jit(solution)/shard_map/ppermute | solution.py:288
  20.6 2.2 %shard_map.103 = (bf16[4,360,128]{2,1,0:T(8,128)(2,1)S(1)}, bf16[4,360,128]{2,1,0:T(8,128)(2,1)S(1)}) custom-call(bf16[2,368,128]{2,1,0:T(8,128)(2,1)S(1)} %copy-done.3, bf16[2,368,128]{2,1,0:T(8,128)(2,1)S(1)} %copy-done.4, bf16[2,368,128]{2,1,0:T(8,128)(2,1)S(1)} %collective-permute-done.5.refs_2_, ...), custom_call_target="tpu_custom_call" | custom-call | flops 1811939328 | bytes 3538944 | tf_op jit(solution)/shard_map/pallas_call | solution.py:253
  22.8 2.8 %collective-permute-done.4.refs_6_ = bf16[2,368,128]{2,1,0:T(8,128)(2,1)S(1)} collective-permute-done((bf16[2,368,128]{2,1,0:T(8,128)(2,1)S(1)}, bf16[2,368,128]{2,1,0:T(8,128)(2,1)S(1)}, u32[]{:S(2)}, u32[]{:S(2)}) %collective-permute-start.4) | collective-permute-done | bytes 188448 | tf_op jit(solution)/shard_map/ppermute | solution.py:288
  25.6 3.5 %collective-permute-done.3.refs_2_ = bf16[2,368,128]{2,1,0:T(8,128)(2,1)S(1)} collective-permute-done((bf16[2,368,128]{2,1,0:T(8,128)(2,1)S(1)}, bf16[2,368,128]{2,1,0:T(8,128)(2,1)S(1)}, u32[]{:S(2)}, u32[]{:S(2)}) %collective-permute-start.3) | collective-permute-done | bytes 188448 | tf_op jit(solution)/shard_map/ppermute | solution.py:288
  29.1 0.1 collective-permute-done.2.refs_4_
  29.2 0.5 collective-permute-start.10
  29.7 0.9 %collective-permute-done.9.refs_3_ = bf16[2,368,128]{2,1,0:T(8,128)(2,1)S(1)} collective-permute-done((bf16[2,368,128]{2,1,0:T(8,128)(2,1)S(1)}, bf16[2,368,128]{2,1,0:T(8,128)(2,1)S(1)}, u32[]{:S(2)}, u32[]{:S(2)}) %collective-permute-start.9) | collective-permute-done | bytes 188448 | tf_op jit(solution)/shard_map/ppermute | solution.py:288
  30.6 0.3 collective-permute-done.10.refs_5_
  30.9 0.3 collective-permute-done.11.refs_7_
  31.2 2.2 %shard_map.104 = (bf16[4,360,128]{2,1,0:T(8,128)(2,1)S(1)}, bf16[4,360,128]{2,1,0:T(8,128)(2,1)S(1)}) custom-call(bf16[2,368,128]{2,1,0:T(8,128)(2,1)S(1)} %pad_maximum_fusion.1.refs_0_, bf16[2,368,128]{2,1,0:T(8,128)(2,1)S(1)} %collective-permute-done.7.refs_1_, bf16[2,368,128]{2,1,0:T(8,128)(2,1)S(1)} %collective-permute-done.3.refs_2_, ...), custom_call_target="tpu_custom_call" | custom-call | flops 1811939328 | bytes 3538944 | tf_op jit(solution)/shard_map/pallas_call | solution.py:253
  33.4 0.3 collective-permute-start.13
  33.7 0.3 collective-permute-start.12
  34.0 2.2 %shard_map.105 = (bf16[4,360,128]{2,1,0:T(8,128)(2,1)S(1)}, bf16[4,360,128]{2,1,0:T(8,128)(2,1)S(1)}) custom-call(bf16[2,368,128]{2,1,0:T(8,128)(2,1)S(1)} %pad_maximum_fusion.1.refs_0_, bf16[2,368,128]{2,1,0:T(8,128)(2,1)S(1)} %collective-permute-done.7.refs_1_, bf16[2,368,128]{2,1,0:T(8,128)(2,1)S(1)} %collective-permute-done.3.refs_2_, ...), custom_call_target="tpu_custom_call" | custom-call | flops 1811939328 | bytes 3538944 | tf_op jit(solution)/shard_map/pallas_call | solution.py:253
  36.2 0.3 collective-permute-start.14
  36.5 2.2 %shard_map.106 = (bf16[4,360,128]{2,1,0:T(8,128)(2,1)S(1)}, bf16[4,360,128]{2,1,0:T(8,128)(2,1)S(1)}) custom-call(bf16[4,368,128]{2,1,0:T(8,128)(2,1)S(1)} %collective-permute-done.8.refs_0_, bf16[4,368,128]{2,1,0:T(8,128)(2,1)S(1)} %collective-permute-done.13.refs_1_, bf16[768,1536]{1,0:T(8,128)(2,1)S(1)} %get-tuple-element.62.refs_4_.refs_8_.refs_2_, ...), custom_call_target="tpu_custom_call" | custom-call | flops 1811939328 | bytes 3538944 | tf_op jit(solution)/shard_map/pallas_call | solution.py:253
  38.7 0.3 collective-permute-start.16
  39.0 0.1 add_convert_fusion.11
  39.1 0.1 add_convert_fusion.10
  39.2 1.5 %collective-permute-start.19 = (bf16[2,360,128]{2,1,0:T(8,128)(2,1)S(1)}, bf16[2,360,128]{2,1,0:T(8,128)(2,1)S(1)}, u32[]{:S(2)}, u32[]{:S(2)}) collective-permute-start(bf16[2,360,128]{2,1,0:T(8,128)(2,1)S(1)} %pad_maximum_fusion.3), channel_id=1, source_target_pairs={{0,6},{1,7},{2,4},{3,5},{4,2},{5,3},{6,0},{7,1},{8,14},{9,15},{10,... | collective-permute-start | bytes 552968 | tf_op jit(solution)/shard_map/ppermute | solution.py:288
  40.7 0.7 %collective-permute-start.20 = (bf16[2,360,128]{2,1,0:T(8,128)(2,1)S(1)}, bf16[2,360,128]{2,1,0:T(8,128)(2,1)S(1)}, u32[]{:S(2)}, u32[]{:S(2)}) collective-permute-start(bf16[2,360,128]{2,1,0:T(8,128)(2,1)S(1)} %pad_maximum_fusion.4), channel_id=1, source_target_pairs={{0,2},{1,3},{2,0},{3,1},{4,6},{5,7},{6,4},{7,5},{8,10},{9,11},{10,... | collective-permute-start | bytes 552968 | tf_op jit(solution)/shard_map/ppermute | solution.py:288
  41.4 1.6 %collective-permute-start.18 = (bf16[2,360,128]{2,1,0:T(8,128)(2,1)S(1)}, bf16[2,360,128]{2,1,0:T(8,128)(2,1)S(1)}, u32[]{:S(2)}, u32[]{:S(2)}) collective-permute-start(bf16[2,360,128]{2,1,0:T(8,128)(2,1)S(1)} %pad_maximum_fusion.2), channel_id=1, source_target_pairs={{0,4},{1,5},{2,6},{3,7},{4,0},{5,1},{6,2},{7,3},{8,12},{9,13},{10,... | collective-permute-start | bytes 552968 | tf_op jit(solution)/shard_map/ppermute | solution.py:288
  43.0 0.1 add_convert_fusion
  43.1 0.1 collective-permute-start.17
  43.2 4.5 %collective-permute-done.19 = bf16[2,360,128]{2,1,0:T(8,128)(2,1)S(1)} collective-permute-done((bf16[2,360,128]{2,1,0:T(8,128)(2,1)S(1)}, bf16[2,360,128]{2,1,0:T(8,128)(2,1)S(1)}, u32[]{:S(2)}, u32[]{:S(2)}) %collective-permute-start.19) | collective-permute-done | bytes 184352 | tf_op jit(solution)/shard_map/ppermute | solution.py:288
  47.7 3.2 %collective-permute-done.20 = bf16[2,360,128]{2,1,0:T(8,128)(2,1)S(1)} collective-permute-done((bf16[2,360,128]{2,1,0:T(8,128)(2,1)S(1)}, bf16[2,360,128]{2,1,0:T(8,128)(2,1)S(1)}, u32[]{:S(2)}, u32[]{:S(2)}) %collective-permute-start.20) | collective-permute-done | bytes 184352 | tf_op jit(solution)/shard_map/ppermute | solution.py:288
  50.9 0.1 fusion.8
  51.1 0.5 collective-permute-start.24
  51.6 2.1 %collective-permute-start.25 = (bf16[360,128]{1,0:T(8,128)(2,1)S(1)}, bf16[360,128]{1,0:T(8,128)(2,1)S(1)}, u32[]{:S(2)}, u32[]{:S(2)}) collective-permute-start(bf16[360,128]{1,0:T(8,128)(2,1)S(1)} %get-tuple-element.109), channel_id=1, source_target_pairs={{0,24},{1,25},{2,26},{3,27},{4,28},{5,29},{6,30},{7,31},{8,16},{9,... | collective-permute-start | bytes 276488 | tf_op jit(solution)/shard_map/ppermute | solution.py:288
  53.7 0.1 fusion.5
  53.8 0.5 collective-permute-start.21
  54.3 1.4 %collective-permute-start.23 = (bf16[360,128]{1,0:T(8,128)(2,1)S(1)}, bf16[360,128]{1,0:T(8,128)(2,1)S(1)}, u32[]{:S(2)}, u32[]{:S(2)}) collective-permute-start(bf16[360,128]{1,0:T(8,128)(2,1)S(1)} %get-tuple-element.100), channel_id=1, source_target_pairs={{0,2},{1,3},{2,0},{3,1},{4,6},{5,7},{6,4},{7,5},{8,10},{9,11},{10,... | collective-permute-start | bytes 276488 | tf_op jit(solution)/shard_map/ppermute | solution.py:288
  55.7 1.6 %collective-permute-start.22 = (bf16[360,128]{1,0:T(8,128)(2,1)S(1)}, bf16[360,128]{1,0:T(8,128)(2,1)S(1)}, u32[]{:S(2)}, u32[]{:S(2)}) collective-permute-start(bf16[360,128]{1,0:T(8,128)(2,1)S(1)} %get-tuple-element.101), channel_id=1, source_target_pairs={{0,6},{1,7},{2,4},{3,5},{4,2},{5,3},{6,0},{7,1},{8,14},{9,15},{10,... | collective-permute-start | bytes 276488 | tf_op jit(solution)/shard_map/ppermute | solution.py:288
  57.4 3.1 %collective-permute-done.24 = bf16[360,128]{1,0:T(8,128)(2,1)S(1)} collective-permute-done((bf16[360,128]{1,0:T(8,128)(2,1)S(1)}, bf16[360,128]{1,0:T(8,128)(2,1)S(1)}, u32[]{:S(2)}, u32[]{:S(2)}) %collective-permute-start.24) | collective-permute-done | bytes 92192 | tf_op jit(solution)/shard_map/ppermute | solution.py:288
  60.5 0.7 %collective-permute-done.22 = bf16[360,128]{1,0:T(8,128)(2,1)S(1)} collective-permute-done((bf16[360,128]{1,0:T(8,128)(2,1)S(1)}, bf16[360,128]{1,0:T(8,128)(2,1)S(1)}, u32[]{:S(2)}, u32[]{:S(2)}) %collective-permute-start.22) | collective-permute-done | bytes 92192 | tf_op jit(solution)/shard_map/ppermute | solution.py:288
  61.2 0.8 %fusion.10 = bf16[128,360]{0,1:T(8,128)(2,1)} fusion(bf16[360,128]{1,0:T(8,128)(2,1)S(1)} %collective-permute-done.25, bf16[360,128]{1,0:T(8,128)(2,1)S(1)} %collective-permute-done.24, bf16[360,128]{1,0:T(8,128)(2,1)S(1)} %collective-permute-done.23, bf16[360,128]{1,0:T(8,128)(2,1)S(1)} %collective-permute-done.22, ...), kind=kLoop, calls=%fused_computation.28 | loop fusion | flops 737280 | bytes 829440 | tf_op jit(solution)/shard_map/transpose | solution.py:367
  (33 shorter events, 0.3 us)
Async XLA Ops:
  0.0 13.3 %copy-start = (bf16[1,1440,360]{2,1,0:T(8,128)(2,1)S(1)}, bf16[1,1440,360]{2,1,0:T(8,128)(2,1)}, u32[]{:S(2)}) copy-start(bf16[1,1440,360]{2,1,0:T(8,128)(2,1)} %param.14) | copy-start | bytes 3110404
  0.0 13.3 %copy-start.1 = (bf16[1,1440,360]{2,1,0:T(8,128)(2,1)S(1)}, bf16[1,1440,360]{2,1,0:T(8,128)(2,1)}, u32[]{:S(2)}) copy-start(bf16[1,1440,360]{2,1,0:T(8,128)(2,1)} %param.16) | copy-start | bytes 3110404
  2.4 9.0 %collective-permute-start.5 = (bf16[2,368,128]{2,1,0:T(8,128)(2,1)}, bf16[2,368,128]{2,1,0:T(8,128)(2,1)S(1)}, u32[]{:S(2)}, u32[]{:S(2)}) collective-permute-start(bf16[2,368,128]{2,1,0:T(8,128)(2,1)} %get-tuple-element.57.refs_0_), channel_id=1, source_target_pairs={{0,4},{1,5},{2,6},{3,7},{4,0},{5,1},{6,2},{7,3},{8,12},{9,13},{10,... | collective-permute-start | bytes 565256 | tf_op jit(solution)/shard_map/ppermute | solution.py:288
  5.4 8.7 %collective-permute-start.1 = (bf16[368,128]{1,0:T(8,128)(2,1)}, bf16[368,128]{1,0:T(8,128)(2,1)S(1)}, u32[]{:S(2)}, u32[]{:S(2)}) collective-permute-start(bf16[368,128]{1,0:T(8,128)(2,1)} %get-tuple-element.52), channel_id=1, source_target_pairs={{0,24},{1,25},{2,26},{3,27},{4,28},{5,29},{6,30},{7,31},{8,16},{9,... | collective-permute-start | bytes 282632 | tf_op jit(solution)/shard_map/ppermute | solution.py:288
  9.0 8.0 %collective-permute-start = (bf16[368,128]{1,0:T(8,128)(2,1)}, bf16[368,128]{1,0:T(8,128)(2,1)S(1)}, u32[]{:S(2)}, u32[]{:S(2)}) collective-permute-start(bf16[368,128]{1,0:T(8,128)(2,1)} %get-tuple-element.52), channel_id=1, source_target_pairs={{0,16},{1,17},{2,18},{3,19},{4,20},{5,21},{6,22},{7,23},{8,24},{9,... | collective-permute-start | bytes 282632 | tf_op jit(solution)/shard_map/ppermute | solution.py:288
  9.7 1.2 %copy-start.2 = (bf16[1,360,1440]{2,1,0:T(8,128)(2,1)S(1)}, bf16[1,360,1440]{2,1,0:T(8,128)(2,1)}, u32[]{:S(2)}) copy-start(bf16[1,360,1440]{2,1,0:T(8,128)(2,1)} %param.18) | copy-start | bytes 3110404
  11.4 7.7 %collective-permute-start.6 = (bf16[2,368,128]{2,1,0:T(8,128)(2,1)S(1)}, bf16[2,368,128]{2,1,0:T(8,128)(2,1)S(1)}, u32[]{:S(2)}, u32[]{:S(2)}) collective-permute-start(bf16[2,368,128]{2,1,0:T(8,128)(2,1)S(1)} %collective-permute-done.5.refs_2_), channel_id=1, source_target_pairs={{0,1},{1,0},{2,3},{3,2},{4,5},{5,4},{6,7},{7,6},{8,9},{9,8},{10,11... | collective-permute-start | bytes 565256 | tf_op jit(solution)/shard_map/ppermute | solution.py:288
  12.4 16.8 %collective-permute-start.8 = (bf16[4,368,128]{2,1,0:T(8,128)(2,1)S(1)}, bf16[4,368,128]{2,1,0:T(8,128)(2,1)S(1)}, u32[]{:S(2)}, u32[]{:S(2)}) collective-permute-start(bf16[4,368,128]{2,1,0:T(8,128)(2,1)S(1)} %pad_maximum_fusion), channel_id=1, source_target_pairs={{0,8},{1,9},{2,10},{3,11},{4,12},{5,13},{6,14},{7,15},{8,0},{9,1},... | collective-permute-start | bytes 1130504 | tf_op jit(solution)/shard_map/ppermute | solution.py:288
  13.3 7.3 %copy-start.3 = (bf16[2,368,128]{2,1,0:T(8,128)(2,1)S(1)}, bf16[2,368,128]{2,1,0:T(8,128)(2,1)}, u32[]{:S(2)}) copy-start(bf16[2,368,128]{2,1,0:T(8,128)(2,1)} %get-tuple-element.57.refs_0_) | copy-start | bytes 565252
  13.3 7.3 %copy-start.4 = (bf16[2,368,128]{2,1,0:T(8,128)(2,1)S(1)}, bf16[2,368,128]{2,1,0:T(8,128)(2,1)}, u32[]{:S(2)}) copy-start(bf16[2,368,128]{2,1,0:T(8,128)(2,1)} %get-tuple-element.58.refs_1_) | copy-start | bytes 565252
  16.9 5.9 %collective-permute-start.7 = (bf16[2,368,128]{2,1,0:T(8,128)(2,1)S(1)}, bf16[2,368,128]{2,1,0:T(8,128)(2,1)S(1)}, u32[]{:S(2)}, u32[]{:S(2)}) collective-permute-start(bf16[2,368,128]{2,1,0:T(8,128)(2,1)S(1)} %pad_maximum_fusion.1.refs_0_), channel_id=1, source_target_pairs={{0,1},{1,0},{2,3},{3,2},{4,5},{5,4},{6,7},{7,6},{8,9},{9,8},{10,11... | collective-permute-start | bytes 565256 | tf_op jit(solution)/shard_map/ppermute | solution.py:288
  17.0 8.5 %collective-permute-start.4 = (bf16[2,368,128]{2,1,0:T(8,128)(2,1)S(1)}, bf16[2,368,128]{2,1,0:T(8,128)(2,1)S(1)}, u32[]{:S(2)}, u32[]{:S(2)}) collective-permute-start(bf16[2,368,128]{2,1,0:T(8,128)(2,1)S(1)} %pad_maximum_fusion.1.refs_0_), channel_id=1, source_target_pairs={{0,6},{1,7},{2,4},{3,5},{4,2},{5,3},{6,0},{7,1},{8,14},{9,15},{10,... | collective-permute-start | bytes 565256 | tf_op jit(solution)/shard_map/ppermute | solution.py:288
  18.6 10.5 %collective-permute-start.3 = (bf16[2,368,128]{2,1,0:T(8,128)(2,1)S(1)}, bf16[2,368,128]{2,1,0:T(8,128)(2,1)S(1)}, u32[]{:S(2)}, u32[]{:S(2)}) collective-permute-start(bf16[2,368,128]{2,1,0:T(8,128)(2,1)S(1)} %pad_maximum_fusion.1.refs_0_), channel_id=1, source_target_pairs={{0,2},{1,3},{2,0},{3,1},{4,6},{5,7},{6,4},{7,5},{8,10},{9,11},{10,... | collective-permute-start | bytes 565256 | tf_op jit(solution)/shard_map/ppermute | solution.py:288
  19.1 10.1 %collective-permute-start.2 = (bf16[2,368,128]{2,1,0:T(8,128)(2,1)S(1)}, bf16[2,368,128]{2,1,0:T(8,128)(2,1)S(1)}, u32[]{:S(2)}, u32[]{:S(2)}) collective-permute-start(bf16[2,368,128]{2,1,0:T(8,128)(2,1)S(1)} %pad_maximum_fusion.1.refs_0_), channel_id=1, source_target_pairs={{0,4},{1,5},{2,6},{3,7},{4,0},{5,1},{6,2},{7,3},{8,12},{9,13},{10,... | collective-permute-start | bytes 565256 | tf_op jit(solution)/shard_map/ppermute | solution.py:288
  29.2 1.4 %collective-permute-start.9 = (bf16[2,368,128]{2,1,0:T(8,128)(2,1)S(1)}, bf16[2,368,128]{2,1,0:T(8,128)(2,1)S(1)}, u32[]{:S(2)}, u32[]{:S(2)}) collective-permute-start(bf16[2,368,128]{2,1,0:T(8,128)(2,1)S(1)} %collective-permute-done.3.refs_2_), channel_id=1, source_target_pairs={{0,1},{1,0},{2,3},{3,2},{4,5},{5,4},{6,7},{7,6},{8,9},{9,8},{10,11... | collective-permute-start | bytes 565256 | tf_op jit(solution)/shard_map/ppermute | solution.py:288
  29.2 1.7 %collective-permute-start.10 = (bf16[2,368,128]{2,1,0:T(8,128)(2,1)S(1)}, bf16[2,368,128]{2,1,0:T(8,128)(2,1)S(1)}, u32[]{:S(2)}, u32[]{:S(2)}) collective-permute-start(bf16[2,368,128]{2,1,0:T(8,128)(2,1)S(1)} %collective-permute-done.2.refs_4_), channel_id=1, source_target_pairs={{0,1},{1,0},{2,3},{3,2},{4,5},{5,4},{6,7},{7,6},{8,9},{9,8},{10,11... | collective-permute-start | bytes 565256 | tf_op jit(solution)/shard_map/ppermute | solution.py:288
  29.7 1.5 %collective-permute-start.11 = (bf16[2,368,128]{2,1,0:T(8,128)(2,1)S(1)}, bf16[2,368,128]{2,1,0:T(8,128)(2,1)S(1)}, u32[]{:S(2)}, u32[]{:S(2)}) collective-permute-start(bf16[2,368,128]{2,1,0:T(8,128)(2,1)S(1)} %collective-permute-done.4.refs_6_), channel_id=1, source_target_pairs={{0,1},{1,0},{2,3},{3,2},{4,5},{5,4},{6,7},{7,6},{8,9},{9,8},{10,11... | collective-permute-start | bytes 565256 | tf_op jit(solution)/shard_map/ppermute | solution.py:288
  33.4 2.8 %collective-permute-start.13 = (bf16[4,368,128]{2,1,0:T(8,128)(2,1)S(1)}, bf16[4,368,128]{2,1,0:T(8,128)(2,1)S(1)}, u32[]{:S(2)}, u32[]{:S(2)}) collective-permute-start(bf16[4,368,128]{2,1,0:T(8,128)(2,1)S(1)} %collective-permute-done.8.refs_0_), channel_id=1, source_target_pairs={{0,1},{1,0},{2,3},{3,2},{4,5},{5,4},{6,7},{7,6},{8,9},{9,8},{10,11... | collective-permute-start | bytes 1130504 | tf_op jit(solution)/shard_map/ppermute | solution.py:288
  33.7 2.5 %collective-permute-start.12 = (bf16[4,360,128]{2,1,0:T(8,128)(2,1)S(1)}, bf16[4,360,128]{2,1,0:T(8,128)(2,1)S(1)}, u32[]{:S(2)}, u32[]{:S(2)}) collective-permute-start(bf16[4,360,128]{2,1,0:T(8,128)(2,1)S(1)} %get-tuple-element.72), channel_id=1, source_target_pairs={{0,1},{1,0},{2,3},{3,2},{4,5},{5,4},{6,7},{7,6},{8,9},{9,8},{10,11... | collective-permute-start | bytes 1105928 | tf_op jit(solution)/shard_map/ppermute | solution.py:288
  36.2 2.9 %collective-permute-start.14 = (bf16[4,360,128]{2,1,0:T(8,128)(2,1)S(1)}, bf16[4,360,128]{2,1,0:T(8,128)(2,1)S(1)}, u32[]{:S(2)}, u32[]{:S(2)}) collective-permute-start(bf16[4,360,128]{2,1,0:T(8,128)(2,1)S(1)} %get-tuple-element.89), channel_id=1, source_target_pairs={{0,1},{1,0},{2,3},{3,2},{4,5},{5,4},{6,7},{7,6},{8,9},{9,8},{10,11... | collective-permute-start | bytes 1105928 | tf_op jit(solution)/shard_map/ppermute | solution.py:288
  38.7 4.3 %collective-permute-start.16 = (bf16[4,360,128]{2,1,0:T(8,128)(2,1)S(1)}, bf16[4,360,128]{2,1,0:T(8,128)(2,1)S(1)}, u32[]{:S(2)}, u32[]{:S(2)}) collective-permute-start(bf16[4,360,128]{2,1,0:T(8,128)(2,1)S(1)} %get-tuple-element.93), channel_id=1, source_target_pairs={{0,1},{1,0},{2,3},{3,2},{4,5},{5,4},{6,7},{7,6},{8,9},{9,8},{10,11... | collective-permute-start | bytes 1105928 | tf_op jit(solution)/shard_map/ppermute | solution.py:288
  39.2 8.5 %collective-permute-start.19 = (bf16[2,360,128]{2,1,0:T(8,128)(2,1)S(1)}, bf16[2,360,128]{2,1,0:T(8,128)(2,1)S(1)}, u32[]{:S(2)}, u32[]{:S(2)}) collective-permute-start(bf16[2,360,128]{2,1,0:T(8,128)(2,1)S(1)} %pad_maximum_fusion.3), channel_id=1, source_target_pairs={{0,6},{1,7},{2,4},{3,5},{4,2},{5,3},{6,0},{7,1},{8,14},{9,15},{10,... | collective-permute-start | bytes 552968 | tf_op jit(solution)/shard_map/ppermute | solution.py:288
  40.7 10.2 %collective-permute-start.20 = (bf16[2,360,128]{2,1,0:T(8,128)(2,1)S(1)}, bf16[2,360,128]{2,1,0:T(8,128)(2,1)S(1)}, u32[]{:S(2)}, u32[]{:S(2)}) collective-permute-start(bf16[2,360,128]{2,1,0:T(8,128)(2,1)S(1)} %pad_maximum_fusion.4), channel_id=1, source_target_pairs={{0,2},{1,3},{2,0},{3,1},{4,6},{5,7},{6,4},{7,5},{8,10},{9,11},{10,... | collective-permute-start | bytes 552968 | tf_op jit(solution)/shard_map/ppermute | solution.py:288
  41.4 9.5 %collective-permute-start.18 = (bf16[2,360,128]{2,1,0:T(8,128)(2,1)S(1)}, bf16[2,360,128]{2,1,0:T(8,128)(2,1)S(1)}, u32[]{:S(2)}, u32[]{:S(2)}) collective-permute-start(bf16[2,360,128]{2,1,0:T(8,128)(2,1)S(1)} %pad_maximum_fusion.2), channel_id=1, source_target_pairs={{0,4},{1,5},{2,6},{3,7},{4,0},{5,1},{6,2},{7,3},{8,12},{9,13},{10,... | collective-permute-start | bytes 552968 | tf_op jit(solution)/shard_map/ppermute | solution.py:288
  43.1 10.6 %collective-permute-start.17 = (bf16[4,360,128]{2,1,0:T(8,128)(2,1)S(1)}, bf16[4,360,128]{2,1,0:T(8,128)(2,1)S(1)}, u32[]{:S(2)}, u32[]{:S(2)}) collective-permute-start(bf16[4,360,128]{2,1,0:T(8,128)(2,1)S(1)} %add_convert_fusion), channel_id=1, source_target_pairs={{0,8},{1,9},{2,10},{3,11},{4,12},{5,13},{6,14},{7,15},{8,0},{9,1},... | collective-permute-start | bytes 1105928 | tf_op jit(solution)/shard_map/ppermute | solution.py:288
  43.2 10.6 %collective-permute-start.15 = (bf16[4,360,128]{2,1,0:T(8,128)(2,1)S(1)}, bf16[4,360,128]{2,1,0:T(8,128)(2,1)S(1)}, u32[]{:S(2)}, u32[]{:S(2)}) collective-permute-start(bf16[4,360,128]{2,1,0:T(8,128)(2,1)S(1)} %get-tuple-element.91), channel_id=1, source_target_pairs={{0,1},{1,0},{2,3},{3,2},{4,5},{5,4},{6,7},{7,6},{8,9},{9,8},{10,11... | collective-permute-start | bytes 1105928 | tf_op jit(solution)/shard_map/ppermute | solution.py:288
  51.1 9.4 %collective-permute-start.24 = (bf16[360,128]{1,0:T(8,128)(2,1)S(1)}, bf16[360,128]{1,0:T(8,128)(2,1)S(1)}, u32[]{:S(2)}, u32[]{:S(2)}) collective-permute-start(bf16[360,128]{1,0:T(8,128)(2,1)S(1)} %get-tuple-element.108), channel_id=1, source_target_pairs={{0,16},{1,17},{2,18},{3,19},{4,20},{5,21},{6,22},{7,23},{8,24},{9,... | collective-permute-start | bytes 276488 | tf_op jit(solution)/shard_map/ppermute | solution.py:288
  51.6 8.9 %collective-permute-start.25 = (bf16[360,128]{1,0:T(8,128)(2,1)S(1)}, bf16[360,128]{1,0:T(8,128)(2,1)S(1)}, u32[]{:S(2)}, u32[]{:S(2)}) collective-permute-start(bf16[360,128]{1,0:T(8,128)(2,1)S(1)} %get-tuple-element.109), channel_id=1, source_target_pairs={{0,24},{1,25},{2,26},{3,27},{4,28},{5,29},{6,30},{7,31},{8,16},{9,... | collective-permute-start | bytes 276488 | tf_op jit(solution)/shard_map/ppermute | solution.py:288
  53.8 6.7 %collective-permute-start.21 = (bf16[360,128]{1,0:T(8,128)(2,1)S(1)}, bf16[360,128]{1,0:T(8,128)(2,1)S(1)}, u32[]{:S(2)}, u32[]{:S(2)}) collective-permute-start(bf16[360,128]{1,0:T(8,128)(2,1)S(1)} %get-tuple-element.99), channel_id=1, source_target_pairs={{0,4},{1,5},{2,6},{3,7},{4,0},{5,1},{6,2},{7,3},{8,12},{9,13},{10,... | collective-permute-start | bytes 276488 | tf_op jit(solution)/shard_map/ppermute | solution.py:288
  54.3 6.2 %collective-permute-start.23 = (bf16[360,128]{1,0:T(8,128)(2,1)S(1)}, bf16[360,128]{1,0:T(8,128)(2,1)S(1)}, u32[]{:S(2)}, u32[]{:S(2)}) collective-permute-start(bf16[360,128]{1,0:T(8,128)(2,1)S(1)} %get-tuple-element.100), channel_id=1, source_target_pairs={{0,2},{1,3},{2,0},{3,1},{4,6},{5,7},{6,4},{7,5},{8,10},{9,11},{10,... | collective-permute-start | bytes 276488 | tf_op jit(solution)/shard_map/ppermute | solution.py:288
  55.7 5.5 %collective-permute-start.22 = (bf16[360,128]{1,0:T(8,128)(2,1)S(1)}, bf16[360,128]{1,0:T(8,128)(2,1)S(1)}, u32[]{:S(2)}, u32[]{:S(2)}) collective-permute-start(bf16[360,128]{1,0:T(8,128)(2,1)S(1)} %get-tuple-element.101), channel_id=1, source_target_pairs={{0,6},{1,7},{2,4},{3,5},{4,2},{5,3},{6,0},{7,1},{8,14},{9,15},{10,... | collective-permute-start | bytes 276488 | tf_op jit(solution)/shard_map/ppermute | solution.py:288

commit v14 on v13

--- a/solution.py
+++ b/solution.py
@@ -333,20 +333,21 @@
     x_high, y_high, d_high, keep_0, z_core, z_near = tied(
         (x_high, y_high, d_high, keep_0, z_core, z_near)
     )
+    near_1 = (z_near, swap(z_near, core))
     high = (z_high, z_core, y_high, swap(y_high, core))
     high = high + (x_high, swap(x_high, core), d_high, swap(d_high, core))
+    blocks = [[(k % 2, 2 * x + k // 2) for k in range(groups)] for x in range(2)]
+    keep_1, send_1 = run_expert(near_1, blocks, slots, weights, sizes, 1)
+    high, keep_1, send_1 = tied((high, keep_1, send_1))
+    got_1 = swap(send_1, core)
     line = [[[(4 * x + k, n) for k in range(groups)] for x in range(2)] for n in range(2)]
     keep_2, send_2 = run_expert(high, line[0], slots, weights, sizes, 1)
     got_2 = swap(send_2, core)
-    keep_2, high, z_near = tied((keep_2, high, z_near))
-    near_1 = (z_near, swap(z_near, core))
+    keep_2, high = tied((keep_2, high))
     keep_3, send_3 = run_expert(high, line[1], slots, weights, sizes, 1)
-    got_2, keep_3, send_3, near_1 = tied((got_2, keep_3, send_3, near_1))
+    got_2, keep_3, send_3 = tied((got_2, keep_3, send_3))
     got_3 = swap(send_3, core)
-    blocks = [[(k % 2, 2 * x + k // 2) for k in range(groups)] for x in range(2)]
-    keep_1, send_1 = run_expert(near_1, blocks, slots, weights, sizes, 1)
-    got_1 = swap(send_1, core)
-    keep_1, got_3, send_0 = tied((keep_1, got_3, send_0))
+    got_1, got_3, send_0 = tied((got_1, got_3, send_0))
     got_0 = swap(send_0, core)
     z_back = swap(add_up(keep_1, got_1), along_z)
 

time: 62.2 us -> 62.9 us (1.011)
  transfers between devices with their start and end apart: 26 -> 26, of which waited for: 11 -> 10; matrix products, arithmetic and copies ran while one was open for 4% -> 3% of each run, Pallas kernels for 13% -> 12%
where the time goes in v14:
time: 62.9 us; the launch traced here: 62.7 us
  starting transfers between devices  23 us (37%)
  waiting for transfers between devices  22.8 us (36%)
  Pallas kernels  12.4 us (20%)
  other arithmetic  3.04 us (5%)
  local copies, waits for them, and re-layouts  1.25 us (2%)
    ppermute x26, starting transfers between devices, swap(): lax.ppermute(array, ('seq', 'rep'), [(i, i ^ step) for i in range(devices)])  23 us
    ppermute x26, waiting for transfers between devices, swap(): lax.ppermute(array, ('seq', 'rep'), [(i, i ^ step) for i in range(devices)])  22.8 us
    pallas_call x4, Pallas kernels, run_expert(): pl.pallas_call(functools.partial(expert_kernel, quarter, per, blocks, slo...  8.79 us
    pallas_call x1, Pallas kernels, make_pieces(): pl.pallas_call(functools.partial(pieces_kernel, groups, per, experts), in...  2.35 us
  transfers between devices with their start and end apart: 26, of which 10 were waited for; matrix products, arithmetic and copies ran while one was open for 3% of the time, Pallas kernels for 12%

profile of v14, /device:TPU:0, one launch (start us, length us, event | category | flops | bytes accessed | tf_op | source)
XLA Modules:
  0.0 62.7 jit_solution(6308835436761630113)
XLA Ops:
  0.0 2.4 %shard_map.100 = (bf16[368,128]{1,0:T(8,128)(2,1)}, bf16[2,368,128]{2,1,0:T(8,128)(2,1)}, bf16[2,368,128]{2,1,0:T(8,128)(2,1)}) custom-call(bf16[1440,128]{1,0:T(8,128)(2,1)} %bitcast.37, f32[1440]{0:T(1024)} %refs_1_.1, s32[4,128]{1,0:T(4,128)} %bitcast.40, f32[4,128]{1,0:T(4,128)} %bitcast.41), custom_call_target="tpu_custom_call" | custom-call | tf_op jit(solution)/shard_map/pallas_call | solution.py:188
  2.4 3.0 %collective-permute-start.5 = (bf16[2,368,128]{2,1,0:T(8,128)(2,1)}, bf16[2,368,128]{2,1,0:T(8,128)(2,1)S(1)}, u32[]{:S(2)}, u32[]{:S(2)}) collective-permute-start(bf16[2,368,128]{2,1,0:T(8,128)(2,1)} %get-tuple-element.64.refs_0_), channel_id=1, source_target_pairs={{0,4},{1,5},{2,6},{3,7},{4,0},{5,1},{6,2},{7,3},{8,12},{9,13},{10,... | collective-permute-start | bytes 565256 | tf_op jit(solution)/shard_map/ppermute | solution.py:288
  5.4 3.6 %collective-permute-start.1 = (bf16[368,128]{1,0:T(8,128)(2,1)}, bf16[368,128]{1,0:T(8,128)(2,1)S(1)}, u32[]{:S(2)}, u32[]{:S(2)}) collective-permute-start(bf16[368,128]{1,0:T(8,128)(2,1)} %get-tuple-element.59), channel_id=1, source_target_pairs={{0,24},{1,25},{2,26},{3,27},{4,28},{5,29},{6,30},{7,31},{8,16},{9,... | collective-permute-start | bytes 282632 | tf_op jit(solution)/shard_map/ppermute | solution.py:288
  9.0 0.7 %pad_maximum_fusion.5.biases_ref = f32[3,360]{1,0:T(4,128)S(1)} fusion(f32[1,360]{1,0:T(1,128)} %param.19, f32[1,360]{1,0:T(1,128)} %param.17, f32[1,360]{1,0:T(1,128)} %param.15), kind=kLoop, calls=%fused_computation.29 | loop fusion | flops 2160 | bytes 8640 | tf_op jit(solution)/shard_map/concatenate | solution.py:298
  9.7 1.2 %copy-done.2 = bf16[1,360,1440]{2,1,0:T(8,128)(2,1)S(1)} copy-done((bf16[1,360,1440]{2,1,0:T(8,128)(2,1)S(1)}, bf16[1,360,1440]{2,1,0:T(8,128)(2,1)}, u32[]{:S(2)}) %copy-start.2) | copy-done | bytes 1036824
  11.0 0.4 shard_map.102
  11.5 1.0 %pad_maximum_fusion = bf16[4,368,128]{2,1,0:T(8,128)(2,1)S(1)} fusion(bf16[2,368,128]{2,1,0:T(8,128)(2,1)S(1)} %collective-permute-done.5.refs_2_, bf16[2,368,128]{2,1,0:T(8,128)(2,1)} %get-tuple-element.64.refs_0_), kind=kLoop, calls=%fused_computation.1 | loop fusion | flops 188416 | bytes 753664 | tf_op jit(solution)/shard_map/concatenate | solution.py:331
  12.4 0.8 %collective-permute-start.8 = (bf16[4,368,128]{2,1,0:T(8,128)(2,1)S(1)}, bf16[4,368,128]{2,1,0:T(8,128)(2,1)S(1)}, u32[]{:S(2)}, u32[]{:S(2)}) collective-permute-start(bf16[4,368,128]{2,1,0:T(8,128)(2,1)S(1)} %pad_maximum_fusion), channel_id=1, source_target_pairs={{0,8},{1,9},{2,10},{3,11},{4,12},{5,13},{6,14},{7,15},{8,0},{9,1},... | collective-permute-start | bytes 1130504 | tf_op jit(solution)/shard_map/ppermute | solution.py:288
  13.3 0.8 %shard_map.101 = (bf16[768,1536]{1,0:T(8,128)(2,1)S(1)}, f32[768,128]{1,0:T(8,128)S(1)}) custom-call(bf16[1440,360]{1,0:T(8,128)(2,1)S(1)} %bitcast.34, bf16[1440,360]{1,0:T(8,128)(2,1)S(1)} %bitcast.35, f32[3,360]{1,0:T(4,128)S(1)} %pad_maximum_fusion.5.biases_ref), custom_call_target="tpu_custom_call" | custom-call | bytes 8294400 | tf_op jit(solution)/shard_map/pallas_call | solution.py:116
  14.1 2.8 %collective-permute-done = bf16[368,128]{1,0:T(8,128)(2,1)S(1)} collective-permute-done((bf16[368,128]{1,0:T(8,128)(2,1)}, bf16[368,128]{1,0:T(8,128)(2,1)S(1)}, u32[]{:S(2)}, u32[]{:S(2)}) %collective-permute-start) | collective-permute-done | bytes 94240 | tf_op jit(solution)/shard_map/ppermute | solution.py:288
  16.9 0.1 collective-permute-start.7
  17.0 1.6 %collective-permute-start.4 = (bf16[2,368,128]{2,1,0:T(8,128)(2,1)S(1)}, bf16[2,368,128]{2,1,0:T(8,128)(2,1)S(1)}, u32[]{:S(2)}, u32[]{:S(2)}) collective-permute-start(bf16[2,368,128]{2,1,0:T(8,128)(2,1)S(1)} %pad_maximum_fusion.1.refs_0_), channel_id=1, source_target_pairs={{0,6},{1,7},{2,4},{3,5},{4,2},{5,3},{6,0},{7,1},{8,14},{9,15},{10,... | collective-permute-start | bytes 565256 | tf_op jit(solution)/shard_map/ppermute | solution.py:288
  18.6 0.5 collective-permute-start.3
  19.1 1.5 %collective-permute-start.2 = (bf16[2,368,128]{2,1,0:T(8,128)(2,1)S(1)}, bf16[2,368,128]{2,1,0:T(8,128)(2,1)S(1)}, u32[]{:S(2)}, u32[]{:S(2)}) collective-permute-start(bf16[2,368,128]{2,1,0:T(8,128)(2,1)S(1)} %pad_maximum_fusion.1.refs_0_), channel_id=1, source_target_pairs={{0,4},{1,5},{2,6},{3,7},{4,0},{5,1},{6,2},{7,3},{8,12},{9,13},{10,... | collective-permute-start | bytes 565256 | tf_op jit(solution)/shard_map/ppermute | solution.py:288
  20.6 2.2 %shard_map.103 = (bf16[4,360,128]{2,1,0:T(8,128)(2,1)S(1)}, bf16[4,360,128]{2,1,0:T(8,128)(2,1)S(1)}) custom-call(bf16[2,368,128]{2,1,0:T(8,128)(2,1)S(1)} %copy-done.3, bf16[2,368,128]{2,1,0:T(8,128)(2,1)S(1)} %copy-done.4, bf16[2,368,128]{2,1,0:T(8,128)(2,1)S(1)} %collective-permute-done.5.refs_2_, ...), custom_call_target="tpu_custom_call" | custom-call | flops 1811939328 | bytes 3538944 | tf_op jit(solution)/shard_map/pallas_call | solution.py:253
  22.8 2.8 %collective-permute-done.4.refs_6_ = bf16[2,368,128]{2,1,0:T(8,128)(2,1)S(1)} collective-permute-done((bf16[2,368,128]{2,1,0:T(8,128)(2,1)S(1)}, bf16[2,368,128]{2,1,0:T(8,128)(2,1)S(1)}, u32[]{:S(2)}, u32[]{:S(2)}) %collective-permute-start.4) | collective-permute-done | bytes 188448 | tf_op jit(solution)/shard_map/ppermute | solution.py:288
  25.6 3.5 %collective-permute-done.3.refs_2_ = bf16[2,368,128]{2,1,0:T(8,128)(2,1)S(1)} collective-permute-done((bf16[2,368,128]{2,1,0:T(8,128)(2,1)S(1)}, bf16[2,368,128]{2,1,0:T(8,128)(2,1)S(1)}, u32[]{:S(2)}, u32[]{:S(2)}) %collective-permute-start.3) | collective-permute-done | bytes 188448 | tf_op jit(solution)/shard_map/ppermute | solution.py:288
  29.1 0.1 collective-permute-done.2.refs_4_
  29.2 0.5 collective-permute-start.9
  29.7 0.5 collective-permute-start.11
  30.2 0.7 %collective-permute-done.12.refs_1_ = bf16[4,368,128]{2,1,0:T(8,128)(2,1)S(1)} collective-permute-done((bf16[4,368,128]{2,1,0:T(8,128)(2,1)S(1)}, bf16[4,368,128]{2,1,0:T(8,128)(2,1)S(1)}, u32[]{:S(2)}, u32[]{:S(2)}) %collective-permute-start.12) | collective-permute-done | bytes 376864 | tf_op jit(solution)/shard_map/ppermute | solution.py:288
  30.9 2.2 %shard_map.104 = (bf16[4,360,128]{2,1,0:T(8,128)(2,1)S(1)}, bf16[4,360,128]{2,1,0:T(8,128)(2,1)S(1)}) custom-call(bf16[4,368,128]{2,1,0:T(8,128)(2,1)S(1)} %collective-permute-done.8.refs_0_, bf16[4,368,128]{2,1,0:T(8,128)(2,1)S(1)} %collective-permute-done.12.refs_1_, bf16[768,1536]{1,0:T(8,128)(2,1)S(1)} %get-tuple-element.69.refs_4_.refs_2_.refs_8_, ...), custom_call_target="tpu_custom_call" | custom-call | flops 1811939328 | bytes 3538944 | tf_op jit(solution)/shard_map/pallas_call | solution.py:253
  33.1 2.2 %shard_map.105 = (bf16[4,360,128]{2,1,0:T(8,128)(2,1)S(1)}, bf16[4,360,128]{2,1,0:T(8,128)(2,1)S(1)}) custom-call(bf16[2,368,128]{2,1,0:T(8,128)(2,1)S(1)} %pad_maximum_fusion.1.refs_0_, bf16[2,368,128]{2,1,0:T(8,128)(2,1)S(1)} %collective-permute-done.7.refs_1_, bf16[2,368,128]{2,1,0:T(8,128)(2,1)S(1)} %collective-permute-done.3.refs_2_, ...), custom_call_target="tpu_custom_call" | custom-call | flops 1811939328 | bytes 3538944 | tf_op jit(solution)/shard_map/pallas_call | solution.py:253
  35.4 0.2 collective-permute-start.14
  35.6 0.4 collective-permute-start.13
  35.9 2.2 %shard_map.106 = (bf16[4,360,128]{2,1,0:T(8,128)(2,1)S(1)}, bf16[4,360,128]{2,1,0:T(8,128)(2,1)S(1)}) custom-call(bf16[2,368,128]{2,1,0:T(8,128)(2,1)S(1)} %pad_maximum_fusion.1.refs_0_, bf16[2,368,128]{2,1,0:T(8,128)(2,1)S(1)} %collective-permute-done.7.refs_1_, bf16[2,368,128]{2,1,0:T(8,128)(2,1)S(1)} %collective-permute-done.3.refs_2_, ...), custom_call_target="tpu_custom_call" | custom-call | flops 1811939328 | bytes 3538944 | tf_op jit(solution)/shard_map/pallas_call | solution.py:253
  38.1 0.2 collective-permute-start.15
  38.4 0.1 add_convert_fusion.11
  38.4 1.5 %collective-permute-done.15 = bf16[4,360,128]{2,1,0:T(8,128)(2,1)S(1)} collective-permute-done((bf16[4,360,128]{2,1,0:T(8,128)(2,1)S(1)}, bf16[4,360,128]{2,1,0:T(8,128)(2,1)S(1)}, u32[]{:S(2)}, u32[]{:S(2)}) %collective-permute-start.15) | collective-permute-done | bytes 368672 | tf_op jit(solution)/shard_map/ppermute | solution.py:288
  39.9 0.1 add_convert_fusion.10
  40.0 1.5 %collective-permute-start.19 = (bf16[2,360,128]{2,1,0:T(8,128)(2,1)S(1)}, bf16[2,360,128]{2,1,0:T(8,128)(2,1)S(1)}, u32[]{:S(2)}, u32[]{:S(2)}) collective-permute-start(bf16[2,360,128]{2,1,0:T(8,128)(2,1)S(1)} %pad_maximum_fusion.3), channel_id=1, source_target_pairs={{0,6},{1,7},{2,4},{3,5},{4,2},{5,3},{6,0},{7,1},{8,14},{9,15},{10,... | collective-permute-start | bytes 552968 | tf_op jit(solution)/shard_map/ppermute | solution.py:288
  41.5 0.7 %collective-permute-start.20 = (bf16[2,360,128]{2,1,0:T(8,128)(2,1)S(1)}, bf16[2,360,128]{2,1,0:T(8,128)(2,1)S(1)}, u32[]{:S(2)}, u32[]{:S(2)}) collective-permute-start(bf16[2,360,128]{2,1,0:T(8,128)(2,1)S(1)} %pad_maximum_fusion.4), channel_id=1, source_target_pairs={{0,2},{1,3},{2,0},{3,1},{4,6},{5,7},{6,4},{7,5},{8,10},{9,11},{10,... | collective-permute-start | bytes 552968 | tf_op jit(solution)/shard_map/ppermute | solution.py:288
  42.2 1.6 %collective-permute-start.18 = (bf16[2,360,128]{2,1,0:T(8,128)(2,1)S(1)}, bf16[2,360,128]{2,1,0:T(8,128)(2,1)S(1)}, u32[]{:S(2)}, u32[]{:S(2)}) collective-permute-start(bf16[2,360,128]{2,1,0:T(8,128)(2,1)S(1)} %pad_maximum_fusion.2), channel_id=1, source_target_pairs={{0,4},{1,5},{2,6},{3,7},{4,0},{5,1},{6,2},{7,3},{8,12},{9,13},{10,... | collective-permute-start | bytes 552968 | tf_op jit(solution)/shard_map/ppermute | solution.py:288
  43.8 0.1 add_convert_fusion
  43.9 0.1 collective-permute-start.17
  43.9 0.1 collective-permute-start.16
  44.0 4.5 %collective-permute-done.19 = bf16[2,360,128]{2,1,0:T(8,128)(2,1)S(1)} collective-permute-done((bf16[2,360,128]{2,1,0:T(8,128)(2,1)S(1)}, bf16[2,360,128]{2,1,0:T(8,128)(2,1)S(1)}, u32[]{:S(2)}, u32[]{:S(2)}) %collective-permute-start.19) | collective-permute-done | bytes 184352 | tf_op jit(solution)/shard_map/ppermute | solution.py:288
  48.5 3.1 %collective-permute-done.20 = bf16[2,360,128]{2,1,0:T(8,128)(2,1)S(1)} collective-permute-done((bf16[2,360,128]{2,1,0:T(8,128)(2,1)S(1)}, bf16[2,360,128]{2,1,0:T(8,128)(2,1)S(1)}, u32[]{:S(2)}, u32[]{:S(2)}) %collective-permute-start.20) | collective-permute-done | bytes 184352 | tf_op jit(solution)/shard_map/ppermute | solution.py:288
  51.6 0.1 fusion.8
  51.8 0.5 collective-permute-start.24
  52.3 2.1 %collective-permute-start.25 = (bf16[360,128]{1,0:T(8,128)(2,1)S(1)}, bf16[360,128]{1,0:T(8,128)(2,1)S(1)}, u32[]{:S(2)}, u32[]{:S(2)}) collective-permute-start(bf16[360,128]{1,0:T(8,128)(2,1)S(1)} %get-tuple-element.123), channel_id=1, source_target_pairs={{0,24},{1,25},{2,26},{3,27},{4,28},{5,29},{6,30},{7,31},{8,16},{9,... | collective-permute-start | bytes 276488 | tf_op jit(solution)/shard_map/ppermute | solution.py:288
  54.4 0.1 fusion.5
  54.5 0.5 collective-permute-start.21
  55.0 1.4 %collective-permute-start.23 = (bf16[360,128]{1,0:T(8,128)(2,1)S(1)}, bf16[360,128]{1,0:T(8,128)(2,1)S(1)}, u32[]{:S(2)}, u32[]{:S(2)}) collective-permute-start(bf16[360,128]{1,0:T(8,128)(2,1)S(1)} %get-tuple-element.114), channel_id=1, source_target_pairs={{0,2},{1,3},{2,0},{3,1},{4,6},{5,7},{6,4},{7,5},{8,10},{9,11},{10,... | collective-permute-start | bytes 276488 | tf_op jit(solution)/shard_map/ppermute | solution.py:288
  56.4 1.6 %collective-permute-start.22 = (bf16[360,128]{1,0:T(8,128)(2,1)S(1)}, bf16[360,128]{1,0:T(8,128)(2,1)S(1)}, u32[]{:S(2)}, u32[]{:S(2)}) collective-permute-start(bf16[360,128]{1,0:T(8,128)(2,1)S(1)} %get-tuple-element.115), channel_id=1, source_target_pairs={{0,6},{1,7},{2,4},{3,5},{4,2},{5,3},{6,0},{7,1},{8,14},{9,15},{10,... | collective-permute-start | bytes 276488 | tf_op jit(solution)/shard_map/ppermute | solution.py:288
  58.1 3.1 %collective-permute-done.24 = bf16[360,128]{1,0:T(8,128)(2,1)S(1)} collective-permute-done((bf16[360,128]{1,0:T(8,128)(2,1)S(1)}, bf16[360,128]{1,0:T(8,128)(2,1)S(1)}, u32[]{:S(2)}, u32[]{:S(2)}) %collective-permute-start.24) | collective-permute-done | bytes 92192 | tf_op jit(solution)/shard_map/ppermute | solution.py:288
  61.2 0.7 %collective-permute-done.22 = bf16[360,128]{1,0:T(8,128)(2,1)S(1)} collective-permute-done((bf16[360,128]{1,0:T(8,128)(2,1)S(1)}, bf16[360,128]{1,0:T(8,128)(2,1)S(1)}, u32[]{:S(2)}, u32[]{:S(2)}) %collective-permute-start.22) | collective-permute-done | bytes 92192 | tf_op jit(solution)/shard_map/ppermute | solution.py:288
  61.9 0.8 %fusion.10 = bf16[128,360]{0,1:T(8,128)(2,1)} fusion(bf16[360,128]{1,0:T(8,128)(2,1)S(1)} %collective-permute-done.25, bf16[360,128]{1,0:T(8,128)(2,1)S(1)} %collective-permute-done.24, bf16[360,128]{1,0:T(8,128)(2,1)S(1)} %collective-permute-done.23, bf16[360,128]{1,0:T(8,128)(2,1)S(1)} %collective-permute-done.22, ...), kind=kLoop, calls=%fused_computation.28 | loop fusion | flops 737280 | bytes 829440 | tf_op jit(solution)/shard_map/transpose | solution.py:368
  (33 shorter events, 0.2 us)
Async XLA Ops:
  0.0 13.3 %copy-start = (bf16[1,1440,360]{2,1,0:T(8,128)(2,1)S(1)}, bf16[1,1440,360]{2,1,0:T(8,128)(2,1)}, u32[]{:S(2)}) copy-start(bf16[1,1440,360]{2,1,0:T(8,128)(2,1)} %param.14) | copy-start | bytes 3110404
  0.0 13.3 %copy-start.1 = (bf16[1,1440,360]{2,1,0:T(8,128)(2,1)S(1)}, bf16[1,1440,360]{2,1,0:T(8,128)(2,1)}, u32[]{:S(2)}) copy-start(bf16[1,1440,360]{2,1,0:T(8,128)(2,1)} %param.16) | copy-start | bytes 3110404
  2.4 9.0 %collective-permute-start.5 = (bf16[2,368,128]{2,1,0:T(8,128)(2,1)}, bf16[2,368,128]{2,1,0:T(8,128)(2,1)S(1)}, u32[]{:S(2)}, u32[]{:S(2)}) collective-permute-start(bf16[2,368,128]{2,1,0:T(8,128)(2,1)} %get-tuple-element.64.refs_0_), channel_id=1, source_target_pairs={{0,4},{1,5},{2,6},{3,7},{4,0},{5,1},{6,2},{7,3},{8,12},{9,13},{10,... | collective-permute-start | bytes 565256 | tf_op jit(solution)/shard_map/ppermute | solution.py:288
  5.4 8.7 %collective-permute-start.1 = (bf16[368,128]{1,0:T(8,128)(2,1)}, bf16[368,128]{1,0:T(8,128)(2,1)S(1)}, u32[]{:S(2)}, u32[]{:S(2)}) collective-permute-start(bf16[368,128]{1,0:T(8,128)(2,1)} %get-tuple-element.59), channel_id=1, source_target_pairs={{0,24},{1,25},{2,26},{3,27},{4,28},{5,29},{6,30},{7,31},{8,16},{9,... | collective-permute-start | bytes 282632 | tf_op jit(solution)/shard_map/ppermute | solution.py:288
  9.0 8.0 %collective-permute-start = (bf16[368,128]{1,0:T(8,128)(2,1)}, bf16[368,128]{1,0:T(8,128)(2,1)S(1)}, u32[]{:S(2)}, u32[]{:S(2)}) collective-permute-start(bf16[368,128]{1,0:T(8,128)(2,1)} %get-tuple-element.59), channel_id=1, source_target_pairs={{0,16},{1,17},{2,18},{3,19},{4,20},{5,21},{6,22},{7,23},{8,24},{9,... | collective-permute-start | bytes 282632 | tf_op jit(solution)/shard_map/ppermute | solution.py:288
  9.7 1.2 %copy-start.2 = (bf16[1,360,1440]{2,1,0:T(8,128)(2,1)S(1)}, bf16[1,360,1440]{2,1,0:T(8,128)(2,1)}, u32[]{:S(2)}) copy-start(bf16[1,360,1440]{2,1,0:T(8,128)(2,1)} %param.18) | copy-start | bytes 3110404
  11.4 7.7 %collective-permute-start.6 = (bf16[2,368,128]{2,1,0:T(8,128)(2,1)S(1)}, bf16[2,368,128]{2,1,0:T(8,128)(2,1)S(1)}, u32[]{:S(2)}, u32[]{:S(2)}) collective-permute-start(bf16[2,368,128]{2,1,0:T(8,128)(2,1)S(1)} %collective-permute-done.5.refs_2_), channel_id=1, source_target_pairs={{0,1},{1,0},{2,3},{3,2},{4,5},{5,4},{6,7},{7,6},{8,9},{9,8},{10,11... | collective-permute-start | bytes 565256 | tf_op jit(solution)/shard_map/ppermute | solution.py:288
  12.4 16.8 %collective-permute-start.8 = (bf16[4,368,128]{2,1,0:T(8,128)(2,1)S(1)}, bf16[4,368,128]{2,1,0:T(8,128)(2,1)S(1)}, u32[]{:S(2)}, u32[]{:S(2)}) collective-permute-start(bf16[4,368,128]{2,1,0:T(8,128)(2,1)S(1)} %pad_maximum_fusion), channel_id=1, source_target_pairs={{0,8},{1,9},{2,10},{3,11},{4,12},{5,13},{6,14},{7,15},{8,0},{9,1},... | collective-permute-start | bytes 1130504 | tf_op jit(solution)/shard_map/ppermute | solution.py:288
  13.3 7.3 %copy-start.3 = (bf16[2,368,128]{2,1,0:T(8,128)(2,1)S(1)}, bf16[2,368,128]{2,1,0:T(8,128)(2,1)}, u32[]{:S(2)}) copy-start(bf16[2,368,128]{2,1,0:T(8,128)(2,1)} %get-tuple-element.64.refs_0_) | copy-start | bytes 565252
  13.3 7.3 %copy-start.4 = (bf16[2,368,128]{2,1,0:T(8,128)(2,1)S(1)}, bf16[2,368,128]{2,1,0:T(8,128)(2,1)}, u32[]{:S(2)}) copy-start(bf16[2,368,128]{2,1,0:T(8,128)(2,1)} %get-tuple-element.65.refs_1_) | copy-start | bytes 565252
  16.9 5.8 %collective-permute-start.7 = (bf16[2,368,128]{2,1,0:T(8,128)(2,1)S(1)}, bf16[2,368,128]{2,1,0:T(8,128)(2,1)S(1)}, u32[]{:S(2)}, u32[]{:S(2)}) collective-permute-start(bf16[2,368,128]{2,1,0:T(8,128)(2,1)S(1)} %pad_maximum_fusion.1.refs_0_), channel_id=1, source_target_pairs={{0,1},{1,0},{2,3},{3,2},{4,5},{5,4},{6,7},{7,6},{8,9},{9,8},{10,11... | collective-permute-start | bytes 565256 | tf_op jit(solution)/shard_map/ppermute | solution.py:288
  17.0 8.5 %collective-permute-start.4 = (bf16[2,368,128]{2,1,0:T(8,128)(2,1)S(1)}, bf16[2,368,128]{2,1,0:T(8,128)(2,1)S(1)}, u32[]{:S(2)}, u32[]{:S(2)}) collective-permute-start(bf16[2,368,128]{2,1,0:T(8,128)(2,1)S(1)} %pad_maximum_fusion.1.refs_0_), channel_id=1, source_target_pairs={{0,6},{1,7},{2,4},{3,5},{4,2},{5,3},{6,0},{7,1},{8,14},{9,15},{10,... | collective-permute-start | bytes 565256 | tf_op jit(solution)/shard_map/ppermute | solution.py:288
  18.6 10.5 %collective-permute-start.3 = (bf16[2,368,128]{2,1,0:T(8,128)(2,1)S(1)}, bf16[2,368,128]{2,1,0:T(8,128)(2,1)S(1)}, u32[]{:S(2)}, u32[]{:S(2)}) collective-permute-start(bf16[2,368,128]{2,1,0:T(8,128)(2,1)S(1)} %pad_maximum_fusion.1.refs_0_), channel_id=1, source_target_pairs={{0,2},{1,3},{2,0},{3,1},{4,6},{5,7},{6,4},{7,5},{8,10},{9,11},{10,... | collective-permute-start | bytes 565256 | tf_op jit(solution)/shard_map/ppermute | solution.py:288
  19.1 10.1 %collective-permute-start.2 = (bf16[2,368,128]{2,1,0:T(8,128)(2,1)S(1)}, bf16[2,368,128]{2,1,0:T(8,128)(2,1)S(1)}, u32[]{:S(2)}, u32[]{:S(2)}) collective-permute-start(bf16[2,368,128]{2,1,0:T(8,128)(2,1)S(1)} %pad_maximum_fusion.1.refs_0_), channel_id=1, source_target_pairs={{0,4},{1,5},{2,6},{3,7},{4,0},{5,1},{6,2},{7,3},{8,12},{9,13},{10,... | collective-permute-start | bytes 565256 | tf_op jit(solution)/shard_map/ppermute | solution.py:288
  29.2 1.7 %collective-permute-start.12 = (bf16[4,368,128]{2,1,0:T(8,128)(2,1)S(1)}, bf16[4,368,128]{2,1,0:T(8,128)(2,1)S(1)}, u32[]{:S(2)}, u32[]{:S(2)}) collective-permute-start(bf16[4,368,128]{2,1,0:T(8,128)(2,1)S(1)} %collective-permute-done.8.refs_0_), channel_id=1, source_target_pairs={{0,1},{1,0},{2,3},{3,2},{4,5},{5,4},{6,7},{7,6},{8,9},{9,8},{10,11... | collective-permute-start | bytes 1130504 | tf_op jit(solution)/shard_map/ppermute | solution.py:288
  29.2 3.9 %collective-permute-start.9 = (bf16[2,368,128]{2,1,0:T(8,128)(2,1)S(1)}, bf16[2,368,128]{2,1,0:T(8,128)(2,1)S(1)}, u32[]{:S(2)}, u32[]{:S(2)}) collective-permute-start(bf16[2,368,128]{2,1,0:T(8,128)(2,1)S(1)} %collective-permute-done.3.refs_2_), channel_id=1, source_target_pairs={{0,1},{1,0},{2,3},{3,2},{4,5},{5,4},{6,7},{7,6},{8,9},{9,8},{10,11... | collective-permute-start | bytes 565256 | tf_op jit(solution)/shard_map/ppermute | solution.py:288
  29.7 3.4 %collective-permute-start.10 = (bf16[2,368,128]{2,1,0:T(8,128)(2,1)S(1)}, bf16[2,368,128]{2,1,0:T(8,128)(2,1)S(1)}, u32[]{:S(2)}, u32[]{:S(2)}) collective-permute-start(bf16[2,368,128]{2,1,0:T(8,128)(2,1)S(1)} %collective-permute-done.2.refs_4_), channel_id=1, source_target_pairs={{0,1},{1,0},{2,3},{3,2},{4,5},{5,4},{6,7},{7,6},{8,9},{9,8},{10,11... | collective-permute-start | bytes 565256 | tf_op jit(solution)/shard_map/ppermute | solution.py:288
  29.7 3.4 %collective-permute-start.11 = (bf16[2,368,128]{2,1,0:T(8,128)(2,1)S(1)}, bf16[2,368,128]{2,1,0:T(8,128)(2,1)S(1)}, u32[]{:S(2)}, u32[]{:S(2)}) collective-permute-start(bf16[2,368,128]{2,1,0:T(8,128)(2,1)S(1)} %collective-permute-done.4.refs_6_), channel_id=1, source_target_pairs={{0,1},{1,0},{2,3},{3,2},{4,5},{5,4},{6,7},{7,6},{8,9},{9,8},{10,11... | collective-permute-start | bytes 565256 | tf_op jit(solution)/shard_map/ppermute | solution.py:288
  35.4 2.8 %collective-permute-start.14 = (bf16[4,360,128]{2,1,0:T(8,128)(2,1)S(1)}, bf16[4,360,128]{2,1,0:T(8,128)(2,1)S(1)}, u32[]{:S(2)}, u32[]{:S(2)}) collective-permute-start(bf16[4,360,128]{2,1,0:T(8,128)(2,1)S(1)} %get-tuple-element.91), channel_id=1, source_target_pairs={{0,1},{1,0},{2,3},{3,2},{4,5},{5,4},{6,7},{7,6},{8,9},{9,8},{10,11... | collective-permute-start | bytes 1105928 | tf_op jit(solution)/shard_map/ppermute | solution.py:288
  35.6 2.9 %collective-permute-start.13 = (bf16[4,360,128]{2,1,0:T(8,128)(2,1)S(1)}, bf16[4,360,128]{2,1,0:T(8,128)(2,1)S(1)}, u32[]{:S(2)}, u32[]{:S(2)}) collective-permute-start(bf16[4,360,128]{2,1,0:T(8,128)(2,1)S(1)} %get-tuple-element.82), channel_id=1, source_target_pairs={{0,1},{1,0},{2,3},{3,2},{4,5},{5,4},{6,7},{7,6},{8,9},{9,8},{10,11... | collective-permute-start | bytes 1105928 | tf_op jit(solution)/shard_map/ppermute | solution.py:288
  38.1 1.8 %collective-permute-start.15 = (bf16[4,360,128]{2,1,0:T(8,128)(2,1)S(1)}, bf16[4,360,128]{2,1,0:T(8,128)(2,1)S(1)}, u32[]{:S(2)}, u32[]{:S(2)}) collective-permute-start(bf16[4,360,128]{2,1,0:T(8,128)(2,1)S(1)} %get-tuple-element.103), channel_id=1, source_target_pairs={{0,1},{1,0},{2,3},{3,2},{4,5},{5,4},{6,7},{7,6},{8,9},{9,8},{10,11... | collective-permute-start | bytes 1105928 | tf_op jit(solution)/shard_map/ppermute | solution.py:288
  40.0 8.5 %collective-permute-start.19 = (bf16[2,360,128]{2,1,0:T(8,128)(2,1)S(1)}, bf16[2,360,128]{2,1,0:T(8,128)(2,1)S(1)}, u32[]{:S(2)}, u32[]{:S(2)}) collective-permute-start(bf16[2,360,128]{2,1,0:T(8,128)(2,1)S(1)} %pad_maximum_fusion.3), channel_id=1, source_target_pairs={{0,6},{1,7},{2,4},{3,5},{4,2},{5,3},{6,0},{7,1},{8,14},{9,15},{10,... | collective-permute-start | bytes 552968 | tf_op jit(solution)/shard_map/ppermute | solution.py:288
  41.5 10.1 %collective-permute-start.20 = (bf16[2,360,128]{2,1,0:T(8,128)(2,1)S(1)}, bf16[2,360,128]{2,1,0:T(8,128)(2,1)S(1)}, u32[]{:S(2)}, u32[]{:S(2)}) collective-permute-start(bf16[2,360,128]{2,1,0:T(8,128)(2,1)S(1)} %pad_maximum_fusion.4), channel_id=1, source_target_pairs={{0,2},{1,3},{2,0},{3,1},{4,6},{5,7},{6,4},{7,5},{8,10},{9,11},{10,... | collective-permute-start | bytes 552968 | tf_op jit(solution)/shard_map/ppermute | solution.py:288
  42.2 9.4 %collective-permute-start.18 = (bf16[2,360,128]{2,1,0:T(8,128)(2,1)S(1)}, bf16[2,360,128]{2,1,0:T(8,128)(2,1)S(1)}, u32[]{:S(2)}, u32[]{:S(2)}) collective-permute-start(bf16[2,360,128]{2,1,0:T(8,128)(2,1)S(1)} %pad_maximum_fusion.2), channel_id=1, source_target_pairs={{0,4},{1,5},{2,6},{3,7},{4,0},{5,1},{6,2},{7,3},{8,12},{9,13},{10,... | collective-permute-start | bytes 552968 | tf_op jit(solution)/shard_map/ppermute | solution.py:288
  43.9 10.5 %collective-permute-start.17 = (bf16[4,360,128]{2,1,0:T(8,128)(2,1)S(1)}, bf16[4,360,128]{2,1,0:T(8,128)(2,1)S(1)}, u32[]{:S(2)}, u32[]{:S(2)}) collective-permute-start(bf16[4,360,128]{2,1,0:T(8,128)(2,1)S(1)} %add_convert_fusion), channel_id=1, source_target_pairs={{0,8},{1,9},{2,10},{3,11},{4,12},{5,13},{6,14},{7,15},{8,0},{9,1},... | collective-permute-start | bytes 1105928 | tf_op jit(solution)/shard_map/ppermute | solution.py:288
  43.9 10.5 %collective-permute-start.16 = (bf16[4,360,128]{2,1,0:T(8,128)(2,1)S(1)}, bf16[4,360,128]{2,1,0:T(8,128)(2,1)S(1)}, u32[]{:S(2)}, u32[]{:S(2)}) collective-permute-start(bf16[4,360,128]{2,1,0:T(8,128)(2,1)S(1)} %get-tuple-element.105), channel_id=1, source_target_pairs={{0,1},{1,0},{2,3},{3,2},{4,5},{5,4},{6,7},{7,6},{8,9},{9,8},{10,11... | collective-permute-start | bytes 1105928 | tf_op jit(solution)/shard_map/ppermute | solution.py:288
  51.8 9.4 %collective-permute-start.24 = (bf16[360,128]{1,0:T(8,128)(2,1)S(1)}, bf16[360,128]{1,0:T(8,128)(2,1)S(1)}, u32[]{:S(2)}, u32[]{:S(2)}) collective-permute-start(bf16[360,128]{1,0:T(8,128)(2,1)S(1)} %get-tuple-element.122), channel_id=1, source_target_pairs={{0,16},{1,17},{2,18},{3,19},{4,20},{5,21},{6,22},{7,23},{8,24},{9,... | collective-permute-start | bytes 276488 | tf_op jit(solution)/shard_map/ppermute | solution.py:288
  52.3 8.9 %collective-permute-start.25 = (bf16[360,128]{1,0:T(8,128)(2,1)S(1)}, bf16[360,128]{1,0:T(8,128)(2,1)S(1)}, u32[]{:S(2)}, u32[]{:S(2)}) collective-permute-start(bf16[360,128]{1,0:T(8,128)(2,1)S(1)} %get-tuple-element.123), channel_id=1, source_target_pairs={{0,24},{1,25},{2,26},{3,27},{4,28},{5,29},{6,30},{7,31},{8,16},{9,... | collective-permute-start | bytes 276488 | tf_op jit(solution)/shard_map/ppermute | solution.py:288
  54.5 6.7 %collective-permute-start.21 = (bf16[360,128]{1,0:T(8,128)(2,1)S(1)}, bf16[360,128]{1,0:T(8,128)(2,1)S(1)}, u32[]{:S(2)}, u32[]{:S(2)}) collective-permute-start(bf16[360,128]{1,0:T(8,128)(2,1)S(1)} %get-tuple-element.113), channel_id=1, source_target_pairs={{0,4},{1,5},{2,6},{3,7},{4,0},{5,1},{6,2},{7,3},{8,12},{9,13},{10,... | collective-permute-start | bytes 276488 | tf_op jit(solution)/shard_map/ppermute | solution.py:288
  55.0 6.2 %collective-permute-start.23 = (bf16[360,128]{1,0:T(8,128)(2,1)S(1)}, bf16[360,128]{1,0:T(8,128)(2,1)S(1)}, u32[]{:S(2)}, u32[]{:S(2)}) collective-permute-start(bf16[360,128]{1,0:T(8,128)(2,1)S(1)} %get-tuple-element.114), channel_id=1, source_target_pairs={{0,2},{1,3},{2,0},{3,1},{4,6},{5,7},{6,4},{7,5},{8,10},{9,11},{10,... | collective-permute-start | bytes 276488 | tf_op jit(solution)/shard_map/ppermute | solution.py:288
  56.4 5.5 %collective-permute-start.22 = (bf16[360,128]{1,0:T(8,128)(2,1)S(1)}, bf16[360,128]{1,0:T(8,128)(2,1)S(1)}, u32[]{:S(2)}, u32[]{:S(2)}) collective-permute-start(bf16[360,128]{1,0:T(8,128)(2,1)S(1)} %get-tuple-element.115), channel_id=1, source_target_pairs={{0,6},{1,7},{2,4},{3,5},{4,2},{5,3},{6,0},{7,1},{8,14},{9,15},{10,... | collective-permute-start | bytes 276488 | tf_op jit(solution)/shard_map/ppermute | solution.py:288

commit v15 on v13

--- a/solution.py
+++ b/solution.py
@@ -92,13 +92,21 @@
     features, hidden = gate_ref.shape
     quarter = features // groups
     hidden_pad, size = round_up(hidden, 128), round_up(quarter, 128)
+    half = hidden_pad // 2
     for n, weight in enumerate((gate_ref, up_ref)):
         values = weight[...].astype(jnp.float32)
-        rows = slice(n * hidden_pad, (n + 1) * hidden_pad)
+        added = column(biases_ref[n : n + 1], hidden_pad, bias_out.shape[1])
+        halves = [
+            (slice(h * half, (h + 1) * half), slice((2 * h + n) * half, (2 * h + n + 1) * half))
+            for h in range(2)
+        ]
         for q in range(groups):
             part = padded(values[q * quarter : (q + 1) * quarter], size, hidden_pad)
-            weight_out[rows, q * size : (q + 1) * size] = part.T.astype(jnp.bfloat16)
-        bias_out[rows] = column(biases_ref[n : n + 1], hidden_pad, bias_out.shape[1])
+            part = part.T.astype(jnp.bfloat16)
+            for own, rows in halves:
+                weight_out[rows, q * size : (q + 1) * size] = part[own]
+        for own, rows in halves:
+            bias_out[rows] = added[own]
 
 
 def outward_kernel(groups, down_ref, biases_ref, weight_out, bias_out):
@@ -228,9 +236,13 @@
                 terms = values.astype(jnp.float32)[quarter:]
                 shares[j] += jnp.sum(jnp.where(mine, terms, 0.0), axis=0, keepdims=True)
         wide = jnp.concatenate(shares, axis=1)
-        both = jnp.dot(gate_up_ref[...], rows_ref[...], preferred_element_type=jnp.float32)
-        both = both + jnp.concatenate([bias_ref[...]] * count, axis=1)
-        activated = gated(both[:hidden], both[hidden:])
+        activated = []
+        for part in range(2):
+            at = slice(part * hidden, (part + 1) * hidden)
+            both = jnp.dot(gate_up_ref[at], rows_ref[...], preferred_element_type=jnp.float32)
+            both = both + jnp.concatenate([bias_ref[at]] * count, axis=1)
+            activated.append(gated(both[: hidden // 2], both[hidden // 2 :]))
+        activated = jnp.concatenate(activated, axis=0)
         for k in range(groups):
             own_rows = down_ref[pl.ds(pl.multiple_of((rep ^ k) * size, size), size), :]
             rows = jnp.dot(own_rows, activated, preferred_element_type=jnp.float32)
@@ -329,11 +341,10 @@
         (near, far, x_0, swap(x_0, core)), pairs(0, 2), slots, weights, sizes, 1
     )
     z_near = swap(jnp.concatenate([near, x_0], axis=0), along_z)
-    z_core = swap(z_high, core)
-    x_high, y_high, d_high, keep_0, z_core, z_near = tied(
-        (x_high, y_high, d_high, keep_0, z_core, z_near)
-    )
-    high = (z_high, z_core, y_high, swap(y_high, core))
+    z_high, x_high, y_high, d_high, keep_0, send_0, z_near = tied(
+        (z_high, x_high, y_high, d_high, keep_0, send_0, z_near)
+    )
+    high = (z_high, swap(z_high, core), y_high, swap(y_high, core))
     high = high + (x_high, swap(x_high, core), d_high, swap(d_high, core))
     line = [[[(4 * x + k, n) for k in range(groups)] for x in range(2)] for n in range(2)]
     keep_2, send_2 = run_expert(high, line[0], slots, weights, sizes, 1)

time: 62.2 us -> 58.8 us (0.945)
  Pallas kernels: 12.4 us -> 9.45 us
    pallas_call x4, Pallas kernels: 8.79 us -> 5.87 us  [run_expert(): pl.pallas_call(functools.partial(expert_kernel, quarter, per, blocks, slo...]
  transfers between devices with their start and end apart: 26 -> 26, of which waited for: 11 -> 13; matrix products, arithmetic and copies ran while one was open for 4% -> 4% of each run, Pallas kernels for 13% -> 10%
where the time goes in v15:
time: 58.8 us; the launch traced here: 58.6 us
  starting transfers between devices  22.7 us (39%)
  waiting for transfers between devices  21.9 us (37%)
  Pallas kernels  9.45 us (16%)
  other arithmetic  3.02 us (5%)
  local copies, waits for them, and re-layouts  1.26 us (2%)
    ppermute x26, starting transfers between devices, swap(): lax.ppermute(array, ('seq', 'rep'), [(i, i ^ step) for i in range(devices)])  22.7 us
    ppermute x26, waiting for transfers between devices, swap(): lax.ppermute(array, ('seq', 'rep'), [(i, i ^ step) for i in range(devices)])  21.9 us
    pallas_call x4, Pallas kernels, run_expert(): pl.pallas_call(functools.partial(expert_kernel, quarter, per, blocks, slo...  5.87 us
    pallas_call x1, Pallas kernels, make_pieces(): pl.pallas_call(functools.partial(pieces_kernel, groups, per, experts), in...  2.35 us
    unnamed x10, local copies, waits for them, and re-layouts  1.26 us
    pallas_call x2, Pallas kernels, arrange(): pl.pallas_call(functools.partial(kernel, groups), out_shape=[jax.ShapeDty...  1.23 us
  transfers between devices with their start and end apart: 26, of which 13 were waited for; matrix products, arithmetic and copies ran while one was open for 4% of the time, Pallas kernels for 10%

profile of v15, /device:TPU:0, one launch (start us, length us, event | category | flops | bytes accessed | tf_op | source)
XLA Modules:
  0.0 58.6 jit_solution(12323489398095648734)
XLA Ops:
  0.0 2.4 %shard_map.100 = (bf16[368,128]{1,0:T(8,128)(2,1)}, bf16[2,368,128]{2,1,0:T(8,128)(2,1)}, bf16[2,368,128]{2,1,0:T(8,128)(2,1)}) custom-call(bf16[1440,128]{1,0:T(8,128)(2,1)} %bitcast.37, f32[1440]{0:T(1024)} %refs_1_.1, s32[4,128]{1,0:T(4,128)} %bitcast.40, f32[4,128]{1,0:T(4,128)} %bitcast.41), custom_call_target="tpu_custom_call" | custom-call | tf_op jit(solution)/shard_map/pallas_call | solution.py:196
  2.4 3.0 %collective-permute-start.5 = (bf16[2,368,128]{2,1,0:T(8,128)(2,1)}, bf16[2,368,128]{2,1,0:T(8,128)(2,1)S(1)}, u32[]{:S(2)}, u32[]{:S(2)}) collective-permute-start(bf16[2,368,128]{2,1,0:T(8,128)(2,1)} %get-tuple-element.58.refs_0_), channel_id=1, source_target_pairs={{0,4},{1,5},{2,6},{3,7},{4,0},{5,1},{6,2},{7,3},{8,12},{9,13},{10,... | collective-permute-start | bytes 565256 | tf_op jit(solution)/shard_map/ppermute | solution.py:300
  5.4 3.6 %collective-permute-start.1 = (bf16[368,128]{1,0:T(8,128)(2,1)}, bf16[368,128]{1,0:T(8,128)(2,1)S(1)}, u32[]{:S(2)}, u32[]{:S(2)}) collective-permute-start(bf16[368,128]{1,0:T(8,128)(2,1)} %get-tuple-element.53), channel_id=1, source_target_pairs={{0,24},{1,25},{2,26},{3,27},{4,28},{5,29},{6,30},{7,31},{8,16},{9,... | collective-permute-start | bytes 282632 | tf_op jit(solution)/shard_map/ppermute | solution.py:300
  9.0 0.7 %pad_maximum_fusion.5.biases_ref = f32[3,360]{1,0:T(4,128)S(1)} fusion(f32[1,360]{1,0:T(1,128)} %param.19, f32[1,360]{1,0:T(1,128)} %param.17, f32[1,360]{1,0:T(1,128)} %param.15), kind=kLoop, calls=%fused_computation.29 | loop fusion | flops 2160 | bytes 8640 | tf_op jit(solution)/shard_map/concatenate | solution.py:310
  9.7 1.2 %copy-done.2 = bf16[1,360,1440]{2,1,0:T(8,128)(2,1)S(1)} copy-done((bf16[1,360,1440]{2,1,0:T(8,128)(2,1)S(1)}, bf16[1,360,1440]{2,1,0:T(8,128)(2,1)}, u32[]{:S(2)}) %copy-start.2) | copy-done | bytes 1036824
  11.0 0.4 shard_map.102
  11.4 1.0 %pad_maximum_fusion = bf16[4,368,128]{2,1,0:T(8,128)(2,1)S(1)} fusion(bf16[2,368,128]{2,1,0:T(8,128)(2,1)S(1)} %collective-permute-done.5.refs_2_, bf16[2,368,128]{2,1,0:T(8,128)(2,1)} %get-tuple-element.58.refs_0_), kind=kLoop, calls=%fused_computation.1 | loop fusion | flops 188416 | bytes 753664 | tf_op jit(solution)/shard_map/concatenate | solution.py:343
  12.4 0.8 %collective-permute-start.7 = (bf16[4,368,128]{2,1,0:T(8,128)(2,1)S(1)}, bf16[4,368,128]{2,1,0:T(8,128)(2,1)S(1)}, u32[]{:S(2)}, u32[]{:S(2)}) collective-permute-start(bf16[4,368,128]{2,1,0:T(8,128)(2,1)S(1)} %pad_maximum_fusion), channel_id=1, source_target_pairs={{0,8},{1,9},{2,10},{3,11},{4,12},{5,13},{6,14},{7,15},{8,0},{9,1},... | collective-permute-start | bytes 1130504 | tf_op jit(solution)/shard_map/ppermute | solution.py:300
  13.3 0.8 %shard_map.101 = (bf16[768,1536]{1,0:T(8,128)(2,1)S(1)}, f32[768,128]{1,0:T(8,128)S(1)}) custom-call(bf16[1440,360]{1,0:T(8,128)(2,1)S(1)} %bitcast.34, bf16[1440,360]{1,0:T(8,128)(2,1)S(1)} %bitcast.35, f32[3,360]{1,0:T(4,128)S(1)} %pad_maximum_fusion.5.biases_ref), custom_call_target="tpu_custom_call" | custom-call | bytes 8294400 | tf_op jit(solution)/shard_map/pallas_call | solution.py:124
  14.1 2.9 %collective-permute-done = bf16[368,128]{1,0:T(8,128)(2,1)S(1)} collective-permute-done((bf16[368,128]{1,0:T(8,128)(2,1)}, bf16[368,128]{1,0:T(8,128)(2,1)S(1)}, u32[]{:S(2)}, u32[]{:S(2)}) %collective-permute-start) | collective-permute-done | bytes 94240 | tf_op jit(solution)/shard_map/ppermute | solution.py:300
  17.0 1.6 %collective-permute-start.4 = (bf16[2,368,128]{2,1,0:T(8,128)(2,1)S(1)}, bf16[2,368,128]{2,1,0:T(8,128)(2,1)S(1)}, u32[]{:S(2)}, u32[]{:S(2)}) collective-permute-start(bf16[2,368,128]{2,1,0:T(8,128)(2,1)S(1)} %pad_maximum_fusion.1.refs_0_), channel_id=1, source_target_pairs={{0,6},{1,7},{2,4},{3,5},{4,2},{5,3},{6,0},{7,1},{8,14},{9,15},{10,... | collective-permute-start | bytes 565256 | tf_op jit(solution)/shard_map/ppermute | solution.py:300
  18.5 0.5 collective-permute-start.3
  19.0 1.5 %collective-permute-start.2 = (bf16[2,368,128]{2,1,0:T(8,128)(2,1)S(1)}, bf16[2,368,128]{2,1,0:T(8,128)(2,1)S(1)}, u32[]{:S(2)}, u32[]{:S(2)}) collective-permute-start(bf16[2,368,128]{2,1,0:T(8,128)(2,1)S(1)} %pad_maximum_fusion.1.refs_0_), channel_id=1, source_target_pairs={{0,4},{1,5},{2,6},{3,7},{4,0},{5,1},{6,2},{7,3},{8,12},{9,13},{10,... | collective-permute-start | bytes 565256 | tf_op jit(solution)/shard_map/ppermute | solution.py:300
  20.5 1.5 %shard_map.103 = (bf16[4,360,128]{2,1,0:T(8,128)(2,1)S(1)}, bf16[4,360,128]{2,1,0:T(8,128)(2,1)S(1)}) custom-call(bf16[2,368,128]{2,1,0:T(8,128)(2,1)S(1)} %copy-done.3, bf16[2,368,128]{2,1,0:T(8,128)(2,1)S(1)} %copy-done.4, bf16[2,368,128]{2,1,0:T(8,128)(2,1)S(1)} %collective-permute-done.5.refs_2_, ...), custom_call_target="tpu_custom_call" | custom-call | flops 1811939328 | bytes 3538944 | tf_op jit(solution)/shard_map/pallas_call | solution.py:265
  22.0 3.6 %collective-permute-done.4.refs_6_ = bf16[2,368,128]{2,1,0:T(8,128)(2,1)S(1)} collective-permute-done((bf16[2,368,128]{2,1,0:T(8,128)(2,1)S(1)}, bf16[2,368,128]{2,1,0:T(8,128)(2,1)S(1)}, u32[]{:S(2)}, u32[]{:S(2)}) %collective-permute-start.4) | collective-permute-done | bytes 188448 | tf_op jit(solution)/shard_map/ppermute | solution.py:300
  25.6 2.2 %collective-permute-done.3.refs_2_ = bf16[2,368,128]{2,1,0:T(8,128)(2,1)S(1)} collective-permute-done((bf16[2,368,128]{2,1,0:T(8,128)(2,1)S(1)}, bf16[2,368,128]{2,1,0:T(8,128)(2,1)S(1)}, u32[]{:S(2)}, u32[]{:S(2)}) %collective-permute-start.3) | collective-permute-done | bytes 188448 | tf_op jit(solution)/shard_map/ppermute | solution.py:300
  27.8 0.1 collective-permute-done.2.refs_4_
  27.9 0.5 collective-permute-start.9
  28.4 0.5 collective-permute-start.11
  28.9 0.4 collective-permute-done.8.refs_1_
  29.3 0.3 collective-permute-done.9.refs_3_
  29.6 0.3 collective-permute-done.10.refs_5_
  29.9 0.3 collective-permute-done.11.refs_7_
  30.2 1.5 %shard_map.104 = (bf16[4,360,128]{2,1,0:T(8,128)(2,1)S(1)}, bf16[4,360,128]{2,1,0:T(8,128)(2,1)S(1)}) custom-call(bf16[2,368,128]{2,1,0:T(8,128)(2,1)S(1)} %pad_maximum_fusion.1.refs_0_, bf16[2,368,128]{2,1,0:T(8,128)(2,1)S(1)} %collective-permute-done.8.refs_1_, bf16[2,368,128]{2,1,0:T(8,128)(2,1)S(1)} %collective-permute-done.3.refs_2_, ...), custom_call_target="tpu_custom_call" | custom-call | flops 1811939328 | bytes 3538944 | tf_op jit(solution)/shard_map/pallas_call | solution.py:265
  31.6 0.3 collective-permute-start.13
  31.9 0.3 collective-permute-start.12
  32.2 1.5 %shard_map.105 = (bf16[4,360,128]{2,1,0:T(8,128)(2,1)S(1)}, bf16[4,360,128]{2,1,0:T(8,128)(2,1)S(1)}) custom-call(bf16[2,368,128]{2,1,0:T(8,128)(2,1)S(1)} %pad_maximum_fusion.1.refs_0_, bf16[2,368,128]{2,1,0:T(8,128)(2,1)S(1)} %collective-permute-done.8.refs_1_, bf16[2,368,128]{2,1,0:T(8,128)(2,1)S(1)} %collective-permute-done.3.refs_2_, ...), custom_call_target="tpu_custom_call" | custom-call | flops 1811939328 | bytes 3538944 | tf_op jit(solution)/shard_map/pallas_call | solution.py:265
  33.7 0.2 collective-permute-done.12
  33.9 0.2 collective-permute-start.14
  34.2 1.5 %shard_map.106 = (bf16[4,360,128]{2,1,0:T(8,128)(2,1)S(1)}, bf16[4,360,128]{2,1,0:T(8,128)(2,1)S(1)}) custom-call(bf16[4,368,128]{2,1,0:T(8,128)(2,1)S(1)} %collective-permute-done.7.refs_0_, bf16[4,368,128]{2,1,0:T(8,128)(2,1)S(1)} %collective-permute-done.13.refs_1_, bf16[768,1536]{1,0:T(8,128)(2,1)S(1)} %get-tuple-element.63.refs_4_.refs_8_.refs_2_, ...), custom_call_target="tpu_custom_call" | custom-call | flops 1811939328 | bytes 3538944 | tf_op jit(solution)/shard_map/pallas_call | solution.py:265
  35.6 0.3 collective-permute-start.16
  36.1 0.1 add_convert_fusion.10
  36.2 1.5 %collective-permute-start.19 = (bf16[2,360,128]{2,1,0:T(8,128)(2,1)S(1)}, bf16[2,360,128]{2,1,0:T(8,128)(2,1)S(1)}, u32[]{:S(2)}, u32[]{:S(2)}) collective-permute-start(bf16[2,360,128]{2,1,0:T(8,128)(2,1)S(1)} %pad_maximum_fusion.3), channel_id=1, source_target_pairs={{0,6},{1,7},{2,4},{3,5},{4,2},{5,3},{6,0},{7,1},{8,14},{9,15},{10,... | collective-permute-start | bytes 552968 | tf_op jit(solution)/shard_map/ppermute | solution.py:300
  37.7 0.7 %collective-permute-start.20 = (bf16[2,360,128]{2,1,0:T(8,128)(2,1)S(1)}, bf16[2,360,128]{2,1,0:T(8,128)(2,1)S(1)}, u32[]{:S(2)}, u32[]{:S(2)}) collective-permute-start(bf16[2,360,128]{2,1,0:T(8,128)(2,1)S(1)} %pad_maximum_fusion.4), channel_id=1, source_target_pairs={{0,2},{1,3},{2,0},{3,1},{4,6},{5,7},{6,4},{7,5},{8,10},{9,11},{10,... | collective-permute-start | bytes 552968 | tf_op jit(solution)/shard_map/ppermute | solution.py:300
  38.3 1.6 %collective-permute-start.18 = (bf16[2,360,128]{2,1,0:T(8,128)(2,1)S(1)}, bf16[2,360,128]{2,1,0:T(8,128)(2,1)S(1)}, u32[]{:S(2)}, u32[]{:S(2)}) collective-permute-start(bf16[2,360,128]{2,1,0:T(8,128)(2,1)S(1)} %pad_maximum_fusion.2), channel_id=1, source_target_pairs={{0,4},{1,5},{2,6},{3,7},{4,0},{5,1},{6,2},{7,3},{8,12},{9,13},{10,... | collective-permute-start | bytes 552968 | tf_op jit(solution)/shard_map/ppermute | solution.py:300
  39.9 0.1 add_convert_fusion
  40.2 4.5 %collective-permute-done.19 = bf16[2,360,128]{2,1,0:T(8,128)(2,1)S(1)} collective-permute-done((bf16[2,360,128]{2,1,0:T(8,128)(2,1)S(1)}, bf16[2,360,128]{2,1,0:T(8,128)(2,1)S(1)}, u32[]{:S(2)}, u32[]{:S(2)}) %collective-permute-start.19) | collective-permute-done | bytes 184352 | tf_op jit(solution)/shard_map/ppermute | solution.py:300
  44.7 3.2 %collective-permute-done.20 = bf16[2,360,128]{2,1,0:T(8,128)(2,1)S(1)} collective-permute-done((bf16[2,360,128]{2,1,0:T(8,128)(2,1)S(1)}, bf16[2,360,128]{2,1,0:T(8,128)(2,1)S(1)}, u32[]{:S(2)}, u32[]{:S(2)}) %collective-permute-start.20) | collective-permute-done | bytes 184352 | tf_op jit(solution)/shard_map/ppermute | solution.py:300
  47.9 0.1 fusion.8
  48.0 1.0 %collective-permute-start.24 = (bf16[360,128]{1,0:T(8,128)(2,1)S(1)}, bf16[360,128]{1,0:T(8,128)(2,1)S(1)}, u32[]{:S(2)}, u32[]{:S(2)}) collective-permute-start(bf16[360,128]{1,0:T(8,128)(2,1)S(1)} %get-tuple-element.110), channel_id=1, source_target_pairs={{0,16},{1,17},{2,18},{3,19},{4,20},{5,21},{6,22},{7,23},{8,24},{9,... | collective-permute-start | bytes 276488 | tf_op jit(solution)/shard_map/ppermute | solution.py:300
  49.0 1.2 %collective-permute-start.25 = (bf16[360,128]{1,0:T(8,128)(2,1)S(1)}, bf16[360,128]{1,0:T(8,128)(2,1)S(1)}, u32[]{:S(2)}, u32[]{:S(2)}) collective-permute-start(bf16[360,128]{1,0:T(8,128)(2,1)S(1)} %get-tuple-element.111), channel_id=1, source_target_pairs={{0,24},{1,25},{2,26},{3,27},{4,28},{5,29},{6,30},{7,31},{8,16},{9,... | collective-permute-start | bytes 276488 | tf_op jit(solution)/shard_map/ppermute | solution.py:300
  50.2 0.1 fusion.5
  50.3 0.6 %collective-permute-start.21 = (bf16[360,128]{1,0:T(8,128)(2,1)S(1)}, bf16[360,128]{1,0:T(8,128)(2,1)S(1)}, u32[]{:S(2)}, u32[]{:S(2)}) collective-permute-start(bf16[360,128]{1,0:T(8,128)(2,1)S(1)} %get-tuple-element.101), channel_id=1, source_target_pairs={{0,4},{1,5},{2,6},{3,7},{4,0},{5,1},{6,2},{7,3},{8,12},{9,13},{10,... | collective-permute-start | bytes 276488 | tf_op jit(solution)/shard_map/ppermute | solution.py:300
  50.9 1.4 %collective-permute-start.23 = (bf16[360,128]{1,0:T(8,128)(2,1)S(1)}, bf16[360,128]{1,0:T(8,128)(2,1)S(1)}, u32[]{:S(2)}, u32[]{:S(2)}) collective-permute-start(bf16[360,128]{1,0:T(8,128)(2,1)S(1)} %get-tuple-element.102), channel_id=1, source_target_pairs={{0,2},{1,3},{2,0},{3,1},{4,6},{5,7},{6,4},{7,5},{8,10},{9,11},{10,... | collective-permute-start | bytes 276488 | tf_op jit(solution)/shard_map/ppermute | solution.py:300
  52.3 1.5 %collective-permute-start.22 = (bf16[360,128]{1,0:T(8,128)(2,1)S(1)}, bf16[360,128]{1,0:T(8,128)(2,1)S(1)}, u32[]{:S(2)}, u32[]{:S(2)}) collective-permute-start(bf16[360,128]{1,0:T(8,128)(2,1)S(1)} %get-tuple-element.103), channel_id=1, source_target_pairs={{0,6},{1,7},{2,4},{3,5},{4,2},{5,3},{6,0},{7,1},{8,14},{9,15},{10,... | collective-permute-start | bytes 276488 | tf_op jit(solution)/shard_map/ppermute | solution.py:300
  53.9 3.1 %collective-permute-done.24 = bf16[360,128]{1,0:T(8,128)(2,1)S(1)} collective-permute-done((bf16[360,128]{1,0:T(8,128)(2,1)S(1)}, bf16[360,128]{1,0:T(8,128)(2,1)S(1)}, u32[]{:S(2)}, u32[]{:S(2)}) %collective-permute-start.24) | collective-permute-done | bytes 92192 | tf_op jit(solution)/shard_map/ppermute | solution.py:300
  57.0 0.8 %collective-permute-done.22 = bf16[360,128]{1,0:T(8,128)(2,1)S(1)} collective-permute-done((bf16[360,128]{1,0:T(8,128)(2,1)S(1)}, bf16[360,128]{1,0:T(8,128)(2,1)S(1)}, u32[]{:S(2)}, u32[]{:S(2)}) %collective-permute-start.22) | collective-permute-done | bytes 92192 | tf_op jit(solution)/shard_map/ppermute | solution.py:300
  57.8 0.8 %fusion.10 = bf16[128,360]{0,1:T(8,128)(2,1)} fusion(bf16[360,128]{1,0:T(8,128)(2,1)S(1)} %collective-permute-done.25, bf16[360,128]{1,0:T(8,128)(2,1)S(1)} %collective-permute-done.24, bf16[360,128]{1,0:T(8,128)(2,1)S(1)} %collective-permute-done.23, bf16[360,128]{1,0:T(8,128)(2,1)S(1)} %collective-permute-done.22, ...), kind=kLoop, calls=%fused_computation.28 | loop fusion | flops 737280 | bytes 829440 | tf_op jit(solution)/shard_map/transpose | solution.py:378
  (33 shorter events, 0.4 us)
Async XLA Ops:
  0.0 13.2 %copy-start = (bf16[1,1440,360]{2,1,0:T(8,128)(2,1)S(1)}, bf16[1,1440,360]{2,1,0:T(8,128)(2,1)}, u32[]{:S(2)}) copy-start(bf16[1,1440,360]{2,1,0:T(8,128)(2,1)} %param.14) | copy-start | bytes 3110404
  0.0 13.2 %copy-start.1 = (bf16[1,1440,360]{2,1,0:T(8,128)(2,1)S(1)}, bf16[1,1440,360]{2,1,0:T(8,128)(2,1)}, u32[]{:S(2)}) copy-start(bf16[1,1440,360]{2,1,0:T(8,128)(2,1)} %param.16) | copy-start | bytes 3110404
  2.4 9.0 %collective-permute-start.5 = (bf16[2,368,128]{2,1,0:T(8,128)(2,1)}, bf16[2,368,128]{2,1,0:T(8,128)(2,1)S(1)}, u32[]{:S(2)}, u32[]{:S(2)}) collective-permute-start(bf16[2,368,128]{2,1,0:T(8,128)(2,1)} %get-tuple-element.58.refs_0_), channel_id=1, source_target_pairs={{0,4},{1,5},{2,6},{3,7},{4,0},{5,1},{6,2},{7,3},{8,12},{9,13},{10,... | collective-permute-start | bytes 565256 | tf_op jit(solution)/shard_map/ppermute | solution.py:300
  5.4 8.7 %collective-permute-start.1 = (bf16[368,128]{1,0:T(8,128)(2,1)}, bf16[368,128]{1,0:T(8,128)(2,1)S(1)}, u32[]{:S(2)}, u32[]{:S(2)}) collective-permute-start(bf16[368,128]{1,0:T(8,128)(2,1)} %get-tuple-element.53), channel_id=1, source_target_pairs={{0,24},{1,25},{2,26},{3,27},{4,28},{5,29},{6,30},{7,31},{8,16},{9,... | collective-permute-start | bytes 282632 | tf_op jit(solution)/shard_map/ppermute | solution.py:300
  9.0 8.0 %collective-permute-start = (bf16[368,128]{1,0:T(8,128)(2,1)}, bf16[368,128]{1,0:T(8,128)(2,1)S(1)}, u32[]{:S(2)}, u32[]{:S(2)}) collective-permute-start(bf16[368,128]{1,0:T(8,128)(2,1)} %get-tuple-element.53), channel_id=1, source_target_pairs={{0,16},{1,17},{2,18},{3,19},{4,20},{5,21},{6,22},{7,23},{8,24},{9,... | collective-permute-start | bytes 282632 | tf_op jit(solution)/shard_map/ppermute | solution.py:300
  9.7 1.2 %copy-start.2 = (bf16[1,360,1440]{2,1,0:T(8,128)(2,1)S(1)}, bf16[1,360,1440]{2,1,0:T(8,128)(2,1)}, u32[]{:S(2)}) copy-start(bf16[1,360,1440]{2,1,0:T(8,128)(2,1)} %param.18) | copy-start | bytes 3110404
  12.4 15.5 %collective-permute-start.7 = (bf16[4,368,128]{2,1,0:T(8,128)(2,1)S(1)}, bf16[4,368,128]{2,1,0:T(8,128)(2,1)S(1)}, u32[]{:S(2)}, u32[]{:S(2)}) collective-permute-start(bf16[4,368,128]{2,1,0:T(8,128)(2,1)S(1)} %pad_maximum_fusion), channel_id=1, source_target_pairs={{0,8},{1,9},{2,10},{3,11},{4,12},{5,13},{6,14},{7,15},{8,0},{9,1},... | collective-permute-start | bytes 1130504 | tf_op jit(solution)/shard_map/ppermute | solution.py:300
  13.2 7.3 %collective-permute-start.6 = (bf16[2,368,128]{2,1,0:T(8,128)(2,1)S(1)}, bf16[2,368,128]{2,1,0:T(8,128)(2,1)S(1)}, u32[]{:S(2)}, u32[]{:S(2)}) collective-permute-start(bf16[2,368,128]{2,1,0:T(8,128)(2,1)S(1)} %collective-permute-done.5.refs_2_), channel_id=1, source_target_pairs={{0,1},{1,0},{2,3},{3,2},{4,5},{5,4},{6,7},{7,6},{8,9},{9,8},{10,11... | collective-permute-start | bytes 565256 | tf_op jit(solution)/shard_map/ppermute | solution.py:300
  13.2 7.3 %copy-start.3 = (bf16[2,368,128]{2,1,0:T(8,128)(2,1)S(1)}, bf16[2,368,128]{2,1,0:T(8,128)(2,1)}, u32[]{:S(2)}) copy-start(bf16[2,368,128]{2,1,0:T(8,128)(2,1)} %get-tuple-element.58.refs_0_) | copy-start | bytes 565252
  13.2 7.3 %copy-start.4 = (bf16[2,368,128]{2,1,0:T(8,128)(2,1)S(1)}, bf16[2,368,128]{2,1,0:T(8,128)(2,1)}, u32[]{:S(2)}) copy-start(bf16[2,368,128]{2,1,0:T(8,128)(2,1)} %get-tuple-element.59.refs_1_) | copy-start | bytes 565252
  17.0 8.7 %collective-permute-start.4 = (bf16[2,368,128]{2,1,0:T(8,128)(2,1)S(1)}, bf16[2,368,128]{2,1,0:T(8,128)(2,1)S(1)}, u32[]{:S(2)}, u32[]{:S(2)}) collective-permute-start(bf16[2,368,128]{2,1,0:T(8,128)(2,1)S(1)} %pad_maximum_fusion.1.refs_0_), channel_id=1, source_target_pairs={{0,6},{1,7},{2,4},{3,5},{4,2},{5,3},{6,0},{7,1},{8,14},{9,15},{10,... | collective-permute-start | bytes 565256 | tf_op jit(solution)/shard_map/ppermute | solution.py:300
  18.5 9.3 %collective-permute-start.3 = (bf16[2,368,128]{2,1,0:T(8,128)(2,1)S(1)}, bf16[2,368,128]{2,1,0:T(8,128)(2,1)S(1)}, u32[]{:S(2)}, u32[]{:S(2)}) collective-permute-start(bf16[2,368,128]{2,1,0:T(8,128)(2,1)S(1)} %pad_maximum_fusion.1.refs_0_), channel_id=1, source_target_pairs={{0,2},{1,3},{2,0},{3,1},{4,6},{5,7},{6,4},{7,5},{8,10},{9,11},{10,... | collective-permute-start | bytes 565256 | tf_op jit(solution)/shard_map/ppermute | solution.py:300
  19.0 8.9 %collective-permute-start.2 = (bf16[2,368,128]{2,1,0:T(8,128)(2,1)S(1)}, bf16[2,368,128]{2,1,0:T(8,128)(2,1)S(1)}, u32[]{:S(2)}, u32[]{:S(2)}) collective-permute-start(bf16[2,368,128]{2,1,0:T(8,128)(2,1)S(1)} %pad_maximum_fusion.1.refs_0_), channel_id=1, source_target_pairs={{0,4},{1,5},{2,6},{3,7},{4,0},{5,1},{6,2},{7,3},{8,12},{9,13},{10,... | collective-permute-start | bytes 565256 | tf_op jit(solution)/shard_map/ppermute | solution.py:300
  27.9 1.4 %collective-permute-start.8 = (bf16[2,368,128]{2,1,0:T(8,128)(2,1)S(1)}, bf16[2,368,128]{2,1,0:T(8,128)(2,1)S(1)}, u32[]{:S(2)}, u32[]{:S(2)}) collective-permute-start(bf16[2,368,128]{2,1,0:T(8,128)(2,1)S(1)} %pad_maximum_fusion.1.refs_0_), channel_id=1, source_target_pairs={{0,1},{1,0},{2,3},{3,2},{4,5},{5,4},{6,7},{7,6},{8,9},{9,8},{10,11... | collective-permute-start | bytes 565256 | tf_op jit(solution)/shard_map/ppermute | solution.py:300
  27.9 1.7 %collective-permute-start.9 = (bf16[2,368,128]{2,1,0:T(8,128)(2,1)S(1)}, bf16[2,368,128]{2,1,0:T(8,128)(2,1)S(1)}, u32[]{:S(2)}, u32[]{:S(2)}) collective-permute-start(bf16[2,368,128]{2,1,0:T(8,128)(2,1)S(1)} %collective-permute-done.3.refs_2_), channel_id=1, source_target_pairs={{0,1},{1,0},{2,3},{3,2},{4,5},{5,4},{6,7},{7,6},{8,9},{9,8},{10,11... | collective-permute-start | bytes 565256 | tf_op jit(solution)/shard_map/ppermute | solution.py:300
  28.4 1.5 %collective-permute-start.10 = (bf16[2,368,128]{2,1,0:T(8,128)(2,1)S(1)}, bf16[2,368,128]{2,1,0:T(8,128)(2,1)S(1)}, u32[]{:S(2)}, u32[]{:S(2)}) collective-permute-start(bf16[2,368,128]{2,1,0:T(8,128)(2,1)S(1)} %collective-permute-done.2.refs_4_), channel_id=1, source_target_pairs={{0,1},{1,0},{2,3},{3,2},{4,5},{5,4},{6,7},{7,6},{8,9},{9,8},{10,11... | collective-permute-start | bytes 565256 | tf_op jit(solution)/shard_map/ppermute | solution.py:300
  28.4 1.7 %collective-permute-start.11 = (bf16[2,368,128]{2,1,0:T(8,128)(2,1)S(1)}, bf16[2,368,128]{2,1,0:T(8,128)(2,1)S(1)}, u32[]{:S(2)}, u32[]{:S(2)}) collective-permute-start(bf16[2,368,128]{2,1,0:T(8,128)(2,1)S(1)} %collective-permute-done.4.refs_6_), channel_id=1, source_target_pairs={{0,1},{1,0},{2,3},{3,2},{4,5},{5,4},{6,7},{7,6},{8,9},{9,8},{10,11... | collective-permute-start | bytes 565256 | tf_op jit(solution)/shard_map/ppermute | solution.py:300
  31.6 2.3 %collective-permute-start.13 = (bf16[4,368,128]{2,1,0:T(8,128)(2,1)S(1)}, bf16[4,368,128]{2,1,0:T(8,128)(2,1)S(1)}, u32[]{:S(2)}, u32[]{:S(2)}) collective-permute-start(bf16[4,368,128]{2,1,0:T(8,128)(2,1)S(1)} %collective-permute-done.7.refs_0_), channel_id=1, source_target_pairs={{0,1},{1,0},{2,3},{3,2},{4,5},{5,4},{6,7},{7,6},{8,9},{9,8},{10,11... | collective-permute-start | bytes 1130504 | tf_op jit(solution)/shard_map/ppermute | solution.py:300
  31.9 2.0 %collective-permute-start.12 = (bf16[4,360,128]{2,1,0:T(8,128)(2,1)S(1)}, bf16[4,360,128]{2,1,0:T(8,128)(2,1)S(1)}, u32[]{:S(2)}, u32[]{:S(2)}) collective-permute-start(bf16[4,360,128]{2,1,0:T(8,128)(2,1)S(1)} %get-tuple-element.74), channel_id=1, source_target_pairs={{0,1},{1,0},{2,3},{3,2},{4,5},{5,4},{6,7},{7,6},{8,9},{9,8},{10,11... | collective-permute-start | bytes 1105928 | tf_op jit(solution)/shard_map/ppermute | solution.py:300
  33.9 2.1 %collective-permute-start.14 = (bf16[4,360,128]{2,1,0:T(8,128)(2,1)S(1)}, bf16[4,360,128]{2,1,0:T(8,128)(2,1)S(1)}, u32[]{:S(2)}, u32[]{:S(2)}) collective-permute-start(bf16[4,360,128]{2,1,0:T(8,128)(2,1)S(1)} %get-tuple-element.91), channel_id=1, source_target_pairs={{0,1},{1,0},{2,3},{3,2},{4,5},{5,4},{6,7},{7,6},{8,9},{9,8},{10,11... | collective-permute-start | bytes 1105928 | tf_op jit(solution)/shard_map/ppermute | solution.py:300
  35.6 4.3 %collective-permute-start.16 = (bf16[4,360,128]{2,1,0:T(8,128)(2,1)S(1)}, bf16[4,360,128]{2,1,0:T(8,128)(2,1)S(1)}, u32[]{:S(2)}, u32[]{:S(2)}) collective-permute-start(bf16[4,360,128]{2,1,0:T(8,128)(2,1)S(1)} %get-tuple-element.95), channel_id=1, source_target_pairs={{0,1},{1,0},{2,3},{3,2},{4,5},{5,4},{6,7},{7,6},{8,9},{9,8},{10,11... | collective-permute-start | bytes 1105928 | tf_op jit(solution)/shard_map/ppermute | solution.py:300
  36.2 8.5 %collective-permute-start.19 = (bf16[2,360,128]{2,1,0:T(8,128)(2,1)S(1)}, bf16[2,360,128]{2,1,0:T(8,128)(2,1)S(1)}, u32[]{:S(2)}, u32[]{:S(2)}) collective-permute-start(bf16[2,360,128]{2,1,0:T(8,128)(2,1)S(1)} %pad_maximum_fusion.3), channel_id=1, source_target_pairs={{0,6},{1,7},{2,4},{3,5},{4,2},{5,3},{6,0},{7,1},{8,14},{9,15},{10,... | collective-permute-start | bytes 552968 | tf_op jit(solution)/shard_map/ppermute | solution.py:300
  37.7 10.2 %collective-permute-start.20 = (bf16[2,360,128]{2,1,0:T(8,128)(2,1)S(1)}, bf16[2,360,128]{2,1,0:T(8,128)(2,1)S(1)}, u32[]{:S(2)}, u32[]{:S(2)}) collective-permute-start(bf16[2,360,128]{2,1,0:T(8,128)(2,1)S(1)} %pad_maximum_fusion.4), channel_id=1, source_target_pairs={{0,2},{1,3},{2,0},{3,1},{4,6},{5,7},{6,4},{7,5},{8,10},{9,11},{10,... | collective-permute-start | bytes 552968 | tf_op jit(solution)/shard_map/ppermute | solution.py:300
  38.3 9.5 %collective-permute-start.18 = (bf16[2,360,128]{2,1,0:T(8,128)(2,1)S(1)}, bf16[2,360,128]{2,1,0:T(8,128)(2,1)S(1)}, u32[]{:S(2)}, u32[]{:S(2)}) collective-permute-start(bf16[2,360,128]{2,1,0:T(8,128)(2,1)S(1)} %pad_maximum_fusion.2), channel_id=1, source_target_pairs={{0,4},{1,5},{2,6},{3,7},{4,0},{5,1},{6,2},{7,3},{8,12},{9,13},{10,... | collective-permute-start | bytes 552968 | tf_op jit(solution)/shard_map/ppermute | solution.py:300
  40.0 10.2 %collective-permute-start.17 = (bf16[4,360,128]{2,1,0:T(8,128)(2,1)S(1)}, bf16[4,360,128]{2,1,0:T(8,128)(2,1)S(1)}, u32[]{:S(2)}, u32[]{:S(2)}) collective-permute-start(bf16[4,360,128]{2,1,0:T(8,128)(2,1)S(1)} %add_convert_fusion), channel_id=1, source_target_pairs={{0,8},{1,9},{2,10},{3,11},{4,12},{5,13},{6,14},{7,15},{8,0},{9,1},... | collective-permute-start | bytes 1105928 | tf_op jit(solution)/shard_map/ppermute | solution.py:300
  40.1 10.1 %collective-permute-start.15 = (bf16[4,360,128]{2,1,0:T(8,128)(2,1)S(1)}, bf16[4,360,128]{2,1,0:T(8,128)(2,1)S(1)}, u32[]{:S(2)}, u32[]{:S(2)}) collective-permute-start(bf16[4,360,128]{2,1,0:T(8,128)(2,1)S(1)} %get-tuple-element.93), channel_id=1, source_target_pairs={{0,1},{1,0},{2,3},{3,2},{4,5},{5,4},{6,7},{7,6},{8,9},{9,8},{10,11... | collective-permute-start | bytes 1105928 | tf_op jit(solution)/shard_map/ppermute | solution.py:300
  48.0 9.0 %collective-permute-start.24 = (bf16[360,128]{1,0:T(8,128)(2,1)S(1)}, bf16[360,128]{1,0:T(8,128)(2,1)S(1)}, u32[]{:S(2)}, u32[]{:S(2)}) collective-permute-start(bf16[360,128]{1,0:T(8,128)(2,1)S(1)} %get-tuple-element.110), channel_id=1, source_target_pairs={{0,16},{1,17},{2,18},{3,19},{4,20},{5,21},{6,22},{7,23},{8,24},{9,... | collective-permute-start | bytes 276488 | tf_op jit(solution)/shard_map/ppermute | solution.py:300
  49.0 8.0 %collective-permute-start.25 = (bf16[360,128]{1,0:T(8,128)(2,1)S(1)}, bf16[360,128]{1,0:T(8,128)(2,1)S(1)}, u32[]{:S(2)}, u32[]{:S(2)}) collective-permute-start(bf16[360,128]{1,0:T(8,128)(2,1)S(1)} %get-tuple-element.111), channel_id=1, source_target_pairs={{0,24},{1,25},{2,26},{3,27},{4,28},{5,29},{6,30},{7,31},{8,16},{9,... | collective-permute-start | bytes 276488 | tf_op jit(solution)/shard_map/ppermute | solution.py:300
  50.3 6.7 %collective-permute-start.21 = (bf16[360,128]{1,0:T(8,128)(2,1)S(1)}, bf16[360,128]{1,0:T(8,128)(2,1)S(1)}, u32[]{:S(2)}, u32[]{:S(2)}) collective-permute-start(bf16[360,128]{1,0:T(8,128)(2,1)S(1)} %get-tuple-element.101), channel_id=1, source_target_pairs={{0,4},{1,5},{2,6},{3,7},{4,0},{5,1},{6,2},{7,3},{8,12},{9,13},{10,... | collective-permute-start | bytes 276488 | tf_op jit(solution)/shard_map/ppermute | solution.py:300
  50.9 6.1 %collective-permute-start.23 = (bf16[360,128]{1,0:T(8,128)(2,1)S(1)}, bf16[360,128]{1,0:T(8,128)(2,1)S(1)}, u32[]{:S(2)}, u32[]{:S(2)}) collective-permute-start(bf16[360,128]{1,0:T(8,128)(2,1)S(1)} %get-tuple-element.102), channel_id=1, source_target_pairs={{0,2},{1,3},{2,0},{3,1},{4,6},{5,7},{6,4},{7,5},{8,10},{9,11},{10,... | collective-permute-start | bytes 276488 | tf_op jit(solution)/shard_map/ppermute | solution.py:300
  52.3 5.5 %collective-permute-start.22 = (bf16[360,128]{1,0:T(8,128)(2,1)S(1)}, bf16[360,128]{1,0:T(8,128)(2,1)S(1)}, u32[]{:S(2)}, u32[]{:S(2)}) collective-permute-start(bf16[360,128]{1,0:T(8,128)(2,1)S(1)} %get-tuple-element.103), channel_id=1, source_target_pairs={{0,6},{1,7},{2,4},{3,5},{4,2},{5,3},{6,0},{7,1},{8,14},{9,15},{10,... | collective-permute-start | bytes 276488 | tf_op jit(solution)/shard_map/ppermute | solution.py:300

commit v16 on v15

--- a/solution.py
+++ b/solution.py
@@ -92,20 +92,20 @@
     features, hidden = gate_ref.shape
     quarter = features // groups
     hidden_pad, size = round_up(hidden, 128), round_up(quarter, 128)
-    half = hidden_pad // 2
+    step = 128
     for n, weight in enumerate((gate_ref, up_ref)):
         values = weight[...].astype(jnp.float32)
         added = column(biases_ref[n : n + 1], hidden_pad, bias_out.shape[1])
-        halves = [
-            (slice(h * half, (h + 1) * half), slice((2 * h + n) * half, (2 * h + n + 1) * half))
-            for h in range(2)
+        blocks = [
+            (slice(b * step, (b + 1) * step), slice((2 * b + n) * step, (2 * b + n + 1) * step))
+            for b in range(hidden_pad // step)
         ]
         for q in range(groups):
             part = padded(values[q * quarter : (q + 1) * quarter], size, hidden_pad)
             part = part.T.astype(jnp.bfloat16)
-            for own, rows in halves:
+            for own, rows in blocks:
                 weight_out[rows, q * size : (q + 1) * size] = part[own]
-        for own, rows in halves:
+        for own, rows in blocks:
             bias_out[rows] = added[own]
 
 
@@ -237,11 +237,11 @@
                 shares[j] += jnp.sum(jnp.where(mine, terms, 0.0), axis=0, keepdims=True)
         wide = jnp.concatenate(shares, axis=1)
         activated = []
-        for part in range(2):
-            at = slice(part * hidden, (part + 1) * hidden)
+        for part in range(hidden // 128):
+            at = slice(part * 256, (part + 1) * 256)
             both = jnp.dot(gate_up_ref[at], rows_ref[...], preferred_element_type=jnp.float32)
             both = both + jnp.concatenate([bias_ref[at]] * count, axis=1)
-            activated.append(gated(both[: hidden // 2], both[hidden // 2 :]))
+            activated.append(gated(both[:128], both[128:]))
         activated = jnp.concatenate(activated, axis=0)
         for k in range(groups):
             own_rows = down_ref[pl.ds(pl.multiple_of((rep ^ k) * size, size), size), :]

time: 58.8 us -> 59.5 us (1.012)
  Pallas kernels: 9.45 us -> 10.6 us
    pallas_call x4, Pallas kernels: 5.87 us -> 7 us  [run_expert(): pl.pallas_call(functools.partial(expert_kernel, quarter, per, blocks, slo...]
  transfers between devices with their start and end apart: 26 -> 26, of which waited for: 13 -> 12; matrix products, arithmetic and copies ran while one was open for 4% -> 4% of each run, Pallas kernels for 10% -> 11%
where the time goes in v16:
time: 59.5 us; the launch traced here: 59.3 us
  starting transfers between devices  22.8 us (38%)
  waiting for transfers between devices  21.4 us (36%)
  Pallas kernels  10.6 us (18%)
  other arithmetic  3.02 us (5%)
  local copies, waits for them, and re-layouts  1.26 us (2%)
    ppermute x26, starting transfers between devices, swap(): lax.ppermute(array, ('seq', 'rep'), [(i, i ^ step) for i in range(devices)])  22.8 us
    ppermute x26, waiting for transfers between devices, swap(): lax.ppermute(array, ('seq', 'rep'), [(i, i ^ step) for i in range(devices)])  21.4 us
    pallas_call x4, Pallas kernels, run_expert(): pl.pallas_call(functools.partial(expert_kernel, quarter, per, blocks, slo...  7 us
    pallas_call x1, Pallas kernels, make_pieces(): pl.pallas_call(functools.partial(pieces_kernel, groups, per, experts), in...  2.35 us
    unnamed x10, local copies, waits for them, and re-layouts  1.26 us
    pallas_call x2, Pallas kernels, arrange(): pl.pallas_call(functools.partial(kernel, groups), out_shape=[jax.ShapeDty...  1.23 us
  transfers between devices with their start and end apart: 26, of which 12 were waited for; matrix products, arithmetic and copies ran while one was open for 4% of the time, Pallas kernels for 11%

profile of v16, /device:TPU:0, one launch (start us, length us, event | category | flops | bytes accessed | tf_op | source)
XLA Modules:
  0.0 59.3 jit_solution(15737476220222577235)
XLA Ops:
  0.0 2.4 %shard_map.100 = (bf16[368,128]{1,0:T(8,128)(2,1)}, bf16[2,368,128]{2,1,0:T(8,128)(2,1)}, bf16[2,368,128]{2,1,0:T(8,128)(2,1)}) custom-call(bf16[1440,128]{1,0:T(8,128)(2,1)} %bitcast.37, f32[1440]{0:T(1024)} %refs_1_.1, s32[4,128]{1,0:T(4,128)} %bitcast.40, f32[4,128]{1,0:T(4,128)} %bitcast.41), custom_call_target="tpu_custom_call" | custom-call | tf_op jit(solution)/shard_map/pallas_call | solution.py:196
  2.4 3.0 %collective-permute-start.5 = (bf16[2,368,128]{2,1,0:T(8,128)(2,1)}, bf16[2,368,128]{2,1,0:T(8,128)(2,1)S(1)}, u32[]{:S(2)}, u32[]{:S(2)}) collective-permute-start(bf16[2,368,128]{2,1,0:T(8,128)(2,1)} %get-tuple-element.58.refs_0_), channel_id=1, source_target_pairs={{0,4},{1,5},{2,6},{3,7},{4,0},{5,1},{6,2},{7,3},{8,12},{9,13},{10,... | collective-permute-start | bytes 565256 | tf_op jit(solution)/shard_map/ppermute | solution.py:300
  5.4 3.6 %collective-permute-start.1 = (bf16[368,128]{1,0:T(8,128)(2,1)}, bf16[368,128]{1,0:T(8,128)(2,1)S(1)}, u32[]{:S(2)}, u32[]{:S(2)}) collective-permute-start(bf16[368,128]{1,0:T(8,128)(2,1)} %get-tuple-element.53), channel_id=1, source_target_pairs={{0,24},{1,25},{2,26},{3,27},{4,28},{5,29},{6,30},{7,31},{8,16},{9,... | collective-permute-start | bytes 282632 | tf_op jit(solution)/shard_map/ppermute | solution.py:300
  9.0 0.7 %pad_maximum_fusion.5.biases_ref = f32[3,360]{1,0:T(4,128)S(1)} fusion(f32[1,360]{1,0:T(1,128)} %param.19, f32[1,360]{1,0:T(1,128)} %param.17, f32[1,360]{1,0:T(1,128)} %param.15), kind=kLoop, calls=%fused_computation.29 | loop fusion | flops 2160 | bytes 8640 | tf_op jit(solution)/shard_map/concatenate | solution.py:310
  9.7 1.2 %copy-done.2 = bf16[1,360,1440]{2,1,0:T(8,128)(2,1)S(1)} copy-done((bf16[1,360,1440]{2,1,0:T(8,128)(2,1)S(1)}, bf16[1,360,1440]{2,1,0:T(8,128)(2,1)}, u32[]{:S(2)}) %copy-start.2) | copy-done | bytes 1036824
  11.0 0.4 shard_map.102
  11.4 1.0 %pad_maximum_fusion = bf16[4,368,128]{2,1,0:T(8,128)(2,1)S(1)} fusion(bf16[2,368,128]{2,1,0:T(8,128)(2,1)S(1)} %collective-permute-done.5.refs_2_, bf16[2,368,128]{2,1,0:T(8,128)(2,1)} %get-tuple-element.58.refs_0_), kind=kLoop, calls=%fused_computation.1 | loop fusion | flops 188416 | bytes 753664 | tf_op jit(solution)/shard_map/concatenate | solution.py:343
  12.4 0.8 %collective-permute-start.7 = (bf16[4,368,128]{2,1,0:T(8,128)(2,1)S(1)}, bf16[4,368,128]{2,1,0:T(8,128)(2,1)S(1)}, u32[]{:S(2)}, u32[]{:S(2)}) collective-permute-start(bf16[4,368,128]{2,1,0:T(8,128)(2,1)S(1)} %pad_maximum_fusion), channel_id=1, source_target_pairs={{0,8},{1,9},{2,10},{3,11},{4,12},{5,13},{6,14},{7,15},{8,0},{9,1},... | collective-permute-start | bytes 1130504 | tf_op jit(solution)/shard_map/ppermute | solution.py:300
  13.3 0.8 %shard_map.101 = (bf16[768,1536]{1,0:T(8,128)(2,1)S(1)}, f32[768,128]{1,0:T(8,128)S(1)}) custom-call(bf16[1440,360]{1,0:T(8,128)(2,1)S(1)} %bitcast.34, bf16[1440,360]{1,0:T(8,128)(2,1)S(1)} %bitcast.35, f32[3,360]{1,0:T(4,128)S(1)} %pad_maximum_fusion.5.biases_ref), custom_call_target="tpu_custom_call" | custom-call | bytes 8294400 | tf_op jit(solution)/shard_map/pallas_call | solution.py:124
  14.1 2.9 %collective-permute-done = bf16[368,128]{1,0:T(8,128)(2,1)S(1)} collective-permute-done((bf16[368,128]{1,0:T(8,128)(2,1)}, bf16[368,128]{1,0:T(8,128)(2,1)S(1)}, u32[]{:S(2)}, u32[]{:S(2)}) %collective-permute-start) | collective-permute-done | bytes 94240 | tf_op jit(solution)/shard_map/ppermute | solution.py:300
  17.0 1.6 %collective-permute-start.4 = (bf16[2,368,128]{2,1,0:T(8,128)(2,1)S(1)}, bf16[2,368,128]{2,1,0:T(8,128)(2,1)S(1)}, u32[]{:S(2)}, u32[]{:S(2)}) collective-permute-start(bf16[2,368,128]{2,1,0:T(8,128)(2,1)S(1)} %pad_maximum_fusion.1.refs_0_), channel_id=1, source_target_pairs={{0,6},{1,7},{2,4},{3,5},{4,2},{5,3},{6,0},{7,1},{8,14},{9,15},{10,... | collective-permute-start | bytes 565256 | tf_op jit(solution)/shard_map/ppermute | solution.py:300
  18.5 0.5 collective-permute-start.3
  19.0 1.5 %collective-permute-start.2 = (bf16[2,368,128]{2,1,0:T(8,128)(2,1)S(1)}, bf16[2,368,128]{2,1,0:T(8,128)(2,1)S(1)}, u32[]{:S(2)}, u32[]{:S(2)}) collective-permute-start(bf16[2,368,128]{2,1,0:T(8,128)(2,1)S(1)} %pad_maximum_fusion.1.refs_0_), channel_id=1, source_target_pairs={{0,4},{1,5},{2,6},{3,7},{4,0},{5,1},{6,2},{7,3},{8,12},{9,13},{10,... | collective-permute-start | bytes 565256 | tf_op jit(solution)/shard_map/ppermute | solution.py:300
  20.5 1.8 %shard_map.103 = (bf16[4,360,128]{2,1,0:T(8,128)(2,1)S(1)}, bf16[4,360,128]{2,1,0:T(8,128)(2,1)S(1)}) custom-call(bf16[2,368,128]{2,1,0:T(8,128)(2,1)S(1)} %copy-done.3, bf16[2,368,128]{2,1,0:T(8,128)(2,1)S(1)} %copy-done.4, bf16[2,368,128]{2,1,0:T(8,128)(2,1)S(1)} %collective-permute-done.5.refs_2_, ...), custom_call_target="tpu_custom_call" | custom-call | flops 1811939328 | bytes 3538944 | tf_op jit(solution)/shard_map/pallas_call | solution.py:265
  22.3 3.3 %collective-permute-done.4.refs_6_ = bf16[2,368,128]{2,1,0:T(8,128)(2,1)S(1)} collective-permute-done((bf16[2,368,128]{2,1,0:T(8,128)(2,1)S(1)}, bf16[2,368,128]{2,1,0:T(8,128)(2,1)S(1)}, u32[]{:S(2)}, u32[]{:S(2)}) %collective-permute-start.4) | collective-permute-done | bytes 188448 | tf_op jit(solution)/shard_map/ppermute | solution.py:300
  25.6 2.2 %collective-permute-done.3.refs_2_ = bf16[2,368,128]{2,1,0:T(8,128)(2,1)S(1)} collective-permute-done((bf16[2,368,128]{2,1,0:T(8,128)(2,1)S(1)}, bf16[2,368,128]{2,1,0:T(8,128)(2,1)S(1)}, u32[]{:S(2)}, u32[]{:S(2)}) %collective-permute-start.3) | collective-permute-done | bytes 188448 | tf_op jit(solution)/shard_map/ppermute | solution.py:300
  27.8 0.1 collective-permute-done.2.refs_4_
  27.9 0.5 collective-permute-start.9
  28.4 0.5 collective-permute-start.11
  28.9 0.4 collective-permute-done.8.refs_1_
  29.3 0.3 collective-permute-done.9.refs_3_
  29.6 0.3 collective-permute-done.10.refs_5_
  29.9 0.3 collective-permute-done.11.refs_7_
  30.2 1.8 %shard_map.104 = (bf16[4,360,128]{2,1,0:T(8,128)(2,1)S(1)}, bf16[4,360,128]{2,1,0:T(8,128)(2,1)S(1)}) custom-call(bf16[2,368,128]{2,1,0:T(8,128)(2,1)S(1)} %pad_maximum_fusion.1.refs_0_, bf16[2,368,128]{2,1,0:T(8,128)(2,1)S(1)} %collective-permute-done.8.refs_1_, bf16[2,368,128]{2,1,0:T(8,128)(2,1)S(1)} %collective-permute-done.3.refs_2_, ...), custom_call_target="tpu_custom_call" | custom-call | flops 1811939328 | bytes 3538944 | tf_op jit(solution)/shard_map/pallas_call | solution.py:265
  31.9 0.3 collective-permute-start.13
  32.2 0.3 collective-permute-start.12
  32.5 1.7 %shard_map.105 = (bf16[4,360,128]{2,1,0:T(8,128)(2,1)S(1)}, bf16[4,360,128]{2,1,0:T(8,128)(2,1)S(1)}) custom-call(bf16[2,368,128]{2,1,0:T(8,128)(2,1)S(1)} %pad_maximum_fusion.1.refs_0_, bf16[2,368,128]{2,1,0:T(8,128)(2,1)S(1)} %collective-permute-done.8.refs_1_, bf16[2,368,128]{2,1,0:T(8,128)(2,1)S(1)} %collective-permute-done.3.refs_2_, ...), custom_call_target="tpu_custom_call" | custom-call | flops 1811939328 | bytes 3538944 | tf_op jit(solution)/shard_map/pallas_call | solution.py:265
  34.3 0.3 collective-permute-start.14
  34.6 1.7 %shard_map.106 = (bf16[4,360,128]{2,1,0:T(8,128)(2,1)S(1)}, bf16[4,360,128]{2,1,0:T(8,128)(2,1)S(1)}) custom-call(bf16[4,368,128]{2,1,0:T(8,128)(2,1)S(1)} %collective-permute-done.7.refs_0_, bf16[4,368,128]{2,1,0:T(8,128)(2,1)S(1)} %collective-permute-done.13.refs_1_, bf16[768,1536]{1,0:T(8,128)(2,1)S(1)} %get-tuple-element.63.refs_4_.refs_8_.refs_2_, ...), custom_call_target="tpu_custom_call" | custom-call | flops 1811939328 | bytes 3538944 | tf_op jit(solution)/shard_map/pallas_call | solution.py:265
  36.3 0.3 collective-permute-start.16
  36.7 0.1 add_convert_fusion.11
  36.8 0.1 add_convert_fusion.10
  36.9 1.5 %collective-permute-start.19 = (bf16[2,360,128]{2,1,0:T(8,128)(2,1)S(1)}, bf16[2,360,128]{2,1,0:T(8,128)(2,1)S(1)}, u32[]{:S(2)}, u32[]{:S(2)}) collective-permute-start(bf16[2,360,128]{2,1,0:T(8,128)(2,1)S(1)} %pad_maximum_fusion.3), channel_id=1, source_target_pairs={{0,6},{1,7},{2,4},{3,5},{4,2},{5,3},{6,0},{7,1},{8,14},{9,15},{10,... | collective-permute-start | bytes 552968 | tf_op jit(solution)/shard_map/ppermute | solution.py:300
  38.4 0.7 %collective-permute-start.20 = (bf16[2,360,128]{2,1,0:T(8,128)(2,1)S(1)}, bf16[2,360,128]{2,1,0:T(8,128)(2,1)S(1)}, u32[]{:S(2)}, u32[]{:S(2)}) collective-permute-start(bf16[2,360,128]{2,1,0:T(8,128)(2,1)S(1)} %pad_maximum_fusion.4), channel_id=1, source_target_pairs={{0,2},{1,3},{2,0},{3,1},{4,6},{5,7},{6,4},{7,5},{8,10},{9,11},{10,... | collective-permute-start | bytes 552968 | tf_op jit(solution)/shard_map/ppermute | solution.py:300
  39.0 1.6 %collective-permute-start.18 = (bf16[2,360,128]{2,1,0:T(8,128)(2,1)S(1)}, bf16[2,360,128]{2,1,0:T(8,128)(2,1)S(1)}, u32[]{:S(2)}, u32[]{:S(2)}) collective-permute-start(bf16[2,360,128]{2,1,0:T(8,128)(2,1)S(1)} %pad_maximum_fusion.2), channel_id=1, source_target_pairs={{0,4},{1,5},{2,6},{3,7},{4,0},{5,1},{6,2},{7,3},{8,12},{9,13},{10,... | collective-permute-start | bytes 552968 | tf_op jit(solution)/shard_map/ppermute | solution.py:300
  40.6 0.1 add_convert_fusion
  40.9 4.5 %collective-permute-done.19 = bf16[2,360,128]{2,1,0:T(8,128)(2,1)S(1)} collective-permute-done((bf16[2,360,128]{2,1,0:T(8,128)(2,1)S(1)}, bf16[2,360,128]{2,1,0:T(8,128)(2,1)S(1)}, u32[]{:S(2)}, u32[]{:S(2)}) %collective-permute-start.19) | collective-permute-done | bytes 184352 | tf_op jit(solution)/shard_map/ppermute | solution.py:300
  45.3 3.2 %collective-permute-done.20 = bf16[2,360,128]{2,1,0:T(8,128)(2,1)S(1)} collective-permute-done((bf16[2,360,128]{2,1,0:T(8,128)(2,1)S(1)}, bf16[2,360,128]{2,1,0:T(8,128)(2,1)S(1)}, u32[]{:S(2)}, u32[]{:S(2)}) %collective-permute-start.20) | collective-permute-done | bytes 184352 | tf_op jit(solution)/shard_map/ppermute | solution.py:300
  48.6 0.1 fusion.8
  48.7 1.0 %collective-permute-start.24 = (bf16[360,128]{1,0:T(8,128)(2,1)S(1)}, bf16[360,128]{1,0:T(8,128)(2,1)S(1)}, u32[]{:S(2)}, u32[]{:S(2)}) collective-permute-start(bf16[360,128]{1,0:T(8,128)(2,1)S(1)} %get-tuple-element.110), channel_id=1, source_target_pairs={{0,16},{1,17},{2,18},{3,19},{4,20},{5,21},{6,22},{7,23},{8,24},{9,... | collective-permute-start | bytes 276488 | tf_op jit(solution)/shard_map/ppermute | solution.py:300
  49.7 1.1 %collective-permute-start.25 = (bf16[360,128]{1,0:T(8,128)(2,1)S(1)}, bf16[360,128]{1,0:T(8,128)(2,1)S(1)}, u32[]{:S(2)}, u32[]{:S(2)}) collective-permute-start(bf16[360,128]{1,0:T(8,128)(2,1)S(1)} %get-tuple-element.111), channel_id=1, source_target_pairs={{0,24},{1,25},{2,26},{3,27},{4,28},{5,29},{6,30},{7,31},{8,16},{9,... | collective-permute-start | bytes 276488 | tf_op jit(solution)/shard_map/ppermute | solution.py:300
  50.9 0.1 fusion.5
  51.0 0.6 %collective-permute-start.21 = (bf16[360,128]{1,0:T(8,128)(2,1)S(1)}, bf16[360,128]{1,0:T(8,128)(2,1)S(1)}, u32[]{:S(2)}, u32[]{:S(2)}) collective-permute-start(bf16[360,128]{1,0:T(8,128)(2,1)S(1)} %get-tuple-element.101), channel_id=1, source_target_pairs={{0,4},{1,5},{2,6},{3,7},{4,0},{5,1},{6,2},{7,3},{8,12},{9,13},{10,... | collective-permute-start | bytes 276488 | tf_op jit(solution)/shard_map/ppermute | solution.py:300
  51.6 1.4 %collective-permute-start.23 = (bf16[360,128]{1,0:T(8,128)(2,1)S(1)}, bf16[360,128]{1,0:T(8,128)(2,1)S(1)}, u32[]{:S(2)}, u32[]{:S(2)}) collective-permute-start(bf16[360,128]{1,0:T(8,128)(2,1)S(1)} %get-tuple-element.102), channel_id=1, source_target_pairs={{0,2},{1,3},{2,0},{3,1},{4,6},{5,7},{6,4},{7,5},{8,10},{9,11},{10,... | collective-permute-start | bytes 276488 | tf_op jit(solution)/shard_map/ppermute | solution.py:300
  53.0 1.5 %collective-permute-start.22 = (bf16[360,128]{1,0:T(8,128)(2,1)S(1)}, bf16[360,128]{1,0:T(8,128)(2,1)S(1)}, u32[]{:S(2)}, u32[]{:S(2)}) collective-permute-start(bf16[360,128]{1,0:T(8,128)(2,1)S(1)} %get-tuple-element.103), channel_id=1, source_target_pairs={{0,6},{1,7},{2,4},{3,5},{4,2},{5,3},{6,0},{7,1},{8,14},{9,15},{10,... | collective-permute-start | bytes 276488 | tf_op jit(solution)/shard_map/ppermute | solution.py:300
  54.5 3.1 %collective-permute-done.24 = bf16[360,128]{1,0:T(8,128)(2,1)S(1)} collective-permute-done((bf16[360,128]{1,0:T(8,128)(2,1)S(1)}, bf16[360,128]{1,0:T(8,128)(2,1)S(1)}, u32[]{:S(2)}, u32[]{:S(2)}) %collective-permute-start.24) | collective-permute-done | bytes 92192 | tf_op jit(solution)/shard_map/ppermute | solution.py:300
  57.7 0.8 %collective-permute-done.22 = bf16[360,128]{1,0:T(8,128)(2,1)S(1)} collective-permute-done((bf16[360,128]{1,0:T(8,128)(2,1)S(1)}, bf16[360,128]{1,0:T(8,128)(2,1)S(1)}, u32[]{:S(2)}, u32[]{:S(2)}) %collective-permute-start.22) | collective-permute-done | bytes 92192 | tf_op jit(solution)/shard_map/ppermute | solution.py:300
  58.5 0.8 %fusion.10 = bf16[128,360]{0,1:T(8,128)(2,1)} fusion(bf16[360,128]{1,0:T(8,128)(2,1)S(1)} %collective-permute-done.25, bf16[360,128]{1,0:T(8,128)(2,1)S(1)} %collective-permute-done.24, bf16[360,128]{1,0:T(8,128)(2,1)S(1)} %collective-permute-done.23, bf16[360,128]{1,0:T(8,128)(2,1)S(1)} %collective-permute-done.22, ...), kind=kLoop, calls=%fused_computation.28 | loop fusion | flops 737280 | bytes 829440 | tf_op jit(solution)/shard_map/transpose | solution.py:378
  (33 shorter events, 0.3 us)
Async XLA Ops:
  0.0 13.2 %copy-start = (bf16[1,1440,360]{2,1,0:T(8,128)(2,1)S(1)}, bf16[1,1440,360]{2,1,0:T(8,128)(2,1)}, u32[]{:S(2)}) copy-start(bf16[1,1440,360]{2,1,0:T(8,128)(2,1)} %param.14) | copy-start | bytes 3110404
  0.0 13.2 %copy-start.1 = (bf16[1,1440,360]{2,1,0:T(8,128)(2,1)S(1)}, bf16[1,1440,360]{2,1,0:T(8,128)(2,1)}, u32[]{:S(2)}) copy-start(bf16[1,1440,360]{2,1,0:T(8,128)(2,1)} %param.16) | copy-start | bytes 3110404
  2.4 9.0 %collective-permute-start.5 = (bf16[2,368,128]{2,1,0:T(8,128)(2,1)}, bf16[2,368,128]{2,1,0:T(8,128)(2,1)S(1)}, u32[]{:S(2)}, u32[]{:S(2)}) collective-permute-start(bf16[2,368,128]{2,1,0:T(8,128)(2,1)} %get-tuple-element.58.refs_0_), channel_id=1, source_target_pairs={{0,4},{1,5},{2,6},{3,7},{4,0},{5,1},{6,2},{7,3},{8,12},{9,13},{10,... | collective-permute-start | bytes 565256 | tf_op jit(solution)/shard_map/ppermute | solution.py:300
  5.4 8.7 %collective-permute-start.1 = (bf16[368,128]{1,0:T(8,128)(2,1)}, bf16[368,128]{1,0:T(8,128)(2,1)S(1)}, u32[]{:S(2)}, u32[]{:S(2)}) collective-permute-start(bf16[368,128]{1,0:T(8,128)(2,1)} %get-tuple-element.53), channel_id=1, source_target_pairs={{0,24},{1,25},{2,26},{3,27},{4,28},{5,29},{6,30},{7,31},{8,16},{9,... | collective-permute-start | bytes 282632 | tf_op jit(solution)/shard_map/ppermute | solution.py:300
  9.0 8.0 %collective-permute-start = (bf16[368,128]{1,0:T(8,128)(2,1)}, bf16[368,128]{1,0:T(8,128)(2,1)S(1)}, u32[]{:S(2)}, u32[]{:S(2)}) collective-permute-start(bf16[368,128]{1,0:T(8,128)(2,1)} %get-tuple-element.53), channel_id=1, source_target_pairs={{0,16},{1,17},{2,18},{3,19},{4,20},{5,21},{6,22},{7,23},{8,24},{9,... | collective-permute-start | bytes 282632 | tf_op jit(solution)/shard_map/ppermute | solution.py:300
  9.7 1.2 %copy-start.2 = (bf16[1,360,1440]{2,1,0:T(8,128)(2,1)S(1)}, bf16[1,360,1440]{2,1,0:T(8,128)(2,1)}, u32[]{:S(2)}) copy-start(bf16[1,360,1440]{2,1,0:T(8,128)(2,1)} %param.18) | copy-start | bytes 3110404
  12.4 15.5 %collective-permute-start.7 = (bf16[4,368,128]{2,1,0:T(8,128)(2,1)S(1)}, bf16[4,368,128]{2,1,0:T(8,128)(2,1)S(1)}, u32[]{:S(2)}, u32[]{:S(2)}) collective-permute-start(bf16[4,368,128]{2,1,0:T(8,128)(2,1)S(1)} %pad_maximum_fusion), channel_id=1, source_target_pairs={{0,8},{1,9},{2,10},{3,11},{4,12},{5,13},{6,14},{7,15},{8,0},{9,1},... | collective-permute-start | bytes 1130504 | tf_op jit(solution)/shard_map/ppermute | solution.py:300
  13.2 7.3 %collective-permute-start.6 = (bf16[2,368,128]{2,1,0:T(8,128)(2,1)S(1)}, bf16[2,368,128]{2,1,0:T(8,128)(2,1)S(1)}, u32[]{:S(2)}, u32[]{:S(2)}) collective-permute-start(bf16[2,368,128]{2,1,0:T(8,128)(2,1)S(1)} %collective-permute-done.5.refs_2_), channel_id=1, source_target_pairs={{0,1},{1,0},{2,3},{3,2},{4,5},{5,4},{6,7},{7,6},{8,9},{9,8},{10,11... | collective-permute-start | bytes 565256 | tf_op jit(solution)/shard_map/ppermute | solution.py:300
  13.2 7.3 %copy-start.3 = (bf16[2,368,128]{2,1,0:T(8,128)(2,1)S(1)}, bf16[2,368,128]{2,1,0:T(8,128)(2,1)}, u32[]{:S(2)}) copy-start(bf16[2,368,128]{2,1,0:T(8,128)(2,1)} %get-tuple-element.58.refs_0_) | copy-start | bytes 565252
  13.2 7.3 %copy-start.4 = (bf16[2,368,128]{2,1,0:T(8,128)(2,1)S(1)}, bf16[2,368,128]{2,1,0:T(8,128)(2,1)}, u32[]{:S(2)}) copy-start(bf16[2,368,128]{2,1,0:T(8,128)(2,1)} %get-tuple-element.59.refs_1_) | copy-start | bytes 565252
  17.0 8.7 %collective-permute-start.4 = (bf16[2,368,128]{2,1,0:T(8,128)(2,1)S(1)}, bf16[2,368,128]{2,1,0:T(8,128)(2,1)S(1)}, u32[]{:S(2)}, u32[]{:S(2)}) collective-permute-start(bf16[2,368,128]{2,1,0:T(8,128)(2,1)S(1)} %pad_maximum_fusion.1.refs_0_), channel_id=1, source_target_pairs={{0,6},{1,7},{2,4},{3,5},{4,2},{5,3},{6,0},{7,1},{8,14},{9,15},{10,... | collective-permute-start | bytes 565256 | tf_op jit(solution)/shard_map/ppermute | solution.py:300
  18.5 9.3 %collective-permute-start.3 = (bf16[2,368,128]{2,1,0:T(8,128)(2,1)S(1)}, bf16[2,368,128]{2,1,0:T(8,128)(2,1)S(1)}, u32[]{:S(2)}, u32[]{:S(2)}) collective-permute-start(bf16[2,368,128]{2,1,0:T(8,128)(2,1)S(1)} %pad_maximum_fusion.1.refs_0_), channel_id=1, source_target_pairs={{0,2},{1,3},{2,0},{3,1},{4,6},{5,7},{6,4},{7,5},{8,10},{9,11},{10,... | collective-permute-start | bytes 565256 | tf_op jit(solution)/shard_map/ppermute | solution.py:300
  19.0 8.9 %collective-permute-start.2 = (bf16[2,368,128]{2,1,0:T(8,128)(2,1)S(1)}, bf16[2,368,128]{2,1,0:T(8,128)(2,1)S(1)}, u32[]{:S(2)}, u32[]{:S(2)}) collective-permute-start(bf16[2,368,128]{2,1,0:T(8,128)(2,1)S(1)} %pad_maximum_fusion.1.refs_0_), channel_id=1, source_target_pairs={{0,4},{1,5},{2,6},{3,7},{4,0},{5,1},{6,2},{7,3},{8,12},{9,13},{10,... | collective-permute-start | bytes 565256 | tf_op jit(solution)/shard_map/ppermute | solution.py:300
  27.9 1.4 %collective-permute-start.8 = (bf16[2,368,128]{2,1,0:T(8,128)(2,1)S(1)}, bf16[2,368,128]{2,1,0:T(8,128)(2,1)S(1)}, u32[]{:S(2)}, u32[]{:S(2)}) collective-permute-start(bf16[2,368,128]{2,1,0:T(8,128)(2,1)S(1)} %pad_maximum_fusion.1.refs_0_), channel_id=1, source_target_pairs={{0,1},{1,0},{2,3},{3,2},{4,5},{5,4},{6,7},{7,6},{8,9},{9,8},{10,11... | collective-permute-start | bytes 565256 | tf_op jit(solution)/shard_map/ppermute | solution.py:300
  27.9 1.7 %collective-permute-start.9 = (bf16[2,368,128]{2,1,0:T(8,128)(2,1)S(1)}, bf16[2,368,128]{2,1,0:T(8,128)(2,1)S(1)}, u32[]{:S(2)}, u32[]{:S(2)}) collective-permute-start(bf16[2,368,128]{2,1,0:T(8,128)(2,1)S(1)} %collective-permute-done.3.refs_2_), channel_id=1, source_target_pairs={{0,1},{1,0},{2,3},{3,2},{4,5},{5,4},{6,7},{7,6},{8,9},{9,8},{10,11... | collective-permute-start | bytes 565256 | tf_op jit(solution)/shard_map/ppermute | solution.py:300
  28.4 1.5 %collective-permute-start.10 = (bf16[2,368,128]{2,1,0:T(8,128)(2,1)S(1)}, bf16[2,368,128]{2,1,0:T(8,128)(2,1)S(1)}, u32[]{:S(2)}, u32[]{:S(2)}) collective-permute-start(bf16[2,368,128]{2,1,0:T(8,128)(2,1)S(1)} %collective-permute-done.2.refs_4_), channel_id=1, source_target_pairs={{0,1},{1,0},{2,3},{3,2},{4,5},{5,4},{6,7},{7,6},{8,9},{9,8},{10,11... | collective-permute-start | bytes 565256 | tf_op jit(solution)/shard_map/ppermute | solution.py:300
  28.4 1.7 %collective-permute-start.11 = (bf16[2,368,128]{2,1,0:T(8,128)(2,1)S(1)}, bf16[2,368,128]{2,1,0:T(8,128)(2,1)S(1)}, u32[]{:S(2)}, u32[]{:S(2)}) collective-permute-start(bf16[2,368,128]{2,1,0:T(8,128)(2,1)S(1)} %collective-permute-done.4.refs_6_), channel_id=1, source_target_pairs={{0,1},{1,0},{2,3},{3,2},{4,5},{5,4},{6,7},{7,6},{8,9},{9,8},{10,11... | collective-permute-start | bytes 565256 | tf_op jit(solution)/shard_map/ppermute | solution.py:300
  31.9 2.3 %collective-permute-start.13 = (bf16[4,368,128]{2,1,0:T(8,128)(2,1)S(1)}, bf16[4,368,128]{2,1,0:T(8,128)(2,1)S(1)}, u32[]{:S(2)}, u32[]{:S(2)}) collective-permute-start(bf16[4,368,128]{2,1,0:T(8,128)(2,1)S(1)} %collective-permute-done.7.refs_0_), channel_id=1, source_target_pairs={{0,1},{1,0},{2,3},{3,2},{4,5},{5,4},{6,7},{7,6},{8,9},{9,8},{10,11... | collective-permute-start | bytes 1130504 | tf_op jit(solution)/shard_map/ppermute | solution.py:300
  32.2 2.0 %collective-permute-start.12 = (bf16[4,360,128]{2,1,0:T(8,128)(2,1)S(1)}, bf16[4,360,128]{2,1,0:T(8,128)(2,1)S(1)}, u32[]{:S(2)}, u32[]{:S(2)}) collective-permute-start(bf16[4,360,128]{2,1,0:T(8,128)(2,1)S(1)} %get-tuple-element.74), channel_id=1, source_target_pairs={{0,1},{1,0},{2,3},{3,2},{4,5},{5,4},{6,7},{7,6},{8,9},{9,8},{10,11... | collective-permute-start | bytes 1105928 | tf_op jit(solution)/shard_map/ppermute | solution.py:300
  34.3 2.5 %collective-permute-start.14 = (bf16[4,360,128]{2,1,0:T(8,128)(2,1)S(1)}, bf16[4,360,128]{2,1,0:T(8,128)(2,1)S(1)}, u32[]{:S(2)}, u32[]{:S(2)}) collective-permute-start(bf16[4,360,128]{2,1,0:T(8,128)(2,1)S(1)} %get-tuple-element.91), channel_id=1, source_target_pairs={{0,1},{1,0},{2,3},{3,2},{4,5},{5,4},{6,7},{7,6},{8,9},{9,8},{10,11... | collective-permute-start | bytes 1105928 | tf_op jit(solution)/shard_map/ppermute | solution.py:300
  36.3 4.3 %collective-permute-start.16 = (bf16[4,360,128]{2,1,0:T(8,128)(2,1)S(1)}, bf16[4,360,128]{2,1,0:T(8,128)(2,1)S(1)}, u32[]{:S(2)}, u32[]{:S(2)}) collective-permute-start(bf16[4,360,128]{2,1,0:T(8,128)(2,1)S(1)} %get-tuple-element.95), channel_id=1, source_target_pairs={{0,1},{1,0},{2,3},{3,2},{4,5},{5,4},{6,7},{7,6},{8,9},{9,8},{10,11... | collective-permute-start | bytes 1105928 | tf_op jit(solution)/shard_map/ppermute | solution.py:300
  36.9 8.5 %collective-permute-start.19 = (bf16[2,360,128]{2,1,0:T(8,128)(2,1)S(1)}, bf16[2,360,128]{2,1,0:T(8,128)(2,1)S(1)}, u32[]{:S(2)}, u32[]{:S(2)}) collective-permute-start(bf16[2,360,128]{2,1,0:T(8,128)(2,1)S(1)} %pad_maximum_fusion.3), channel_id=1, source_target_pairs={{0,6},{1,7},{2,4},{3,5},{4,2},{5,3},{6,0},{7,1},{8,14},{9,15},{10,... | collective-permute-start | bytes 552968 | tf_op jit(solution)/shard_map/ppermute | solution.py:300
  38.4 10.2 %collective-permute-start.20 = (bf16[2,360,128]{2,1,0:T(8,128)(2,1)S(1)}, bf16[2,360,128]{2,1,0:T(8,128)(2,1)S(1)}, u32[]{:S(2)}, u32[]{:S(2)}) collective-permute-start(bf16[2,360,128]{2,1,0:T(8,128)(2,1)S(1)} %pad_maximum_fusion.4), channel_id=1, source_target_pairs={{0,2},{1,3},{2,0},{3,1},{4,6},{5,7},{6,4},{7,5},{8,10},{9,11},{10,... | collective-permute-start | bytes 552968 | tf_op jit(solution)/shard_map/ppermute | solution.py:300
  39.0 9.5 %collective-permute-start.18 = (bf16[2,360,128]{2,1,0:T(8,128)(2,1)S(1)}, bf16[2,360,128]{2,1,0:T(8,128)(2,1)S(1)}, u32[]{:S(2)}, u32[]{:S(2)}) collective-permute-start(bf16[2,360,128]{2,1,0:T(8,128)(2,1)S(1)} %pad_maximum_fusion.2), channel_id=1, source_target_pairs={{0,4},{1,5},{2,6},{3,7},{4,0},{5,1},{6,2},{7,3},{8,12},{9,13},{10,... | collective-permute-start | bytes 552968 | tf_op jit(solution)/shard_map/ppermute | solution.py:300
  40.7 10.2 %collective-permute-start.17 = (bf16[4,360,128]{2,1,0:T(8,128)(2,1)S(1)}, bf16[4,360,128]{2,1,0:T(8,128)(2,1)S(1)}, u32[]{:S(2)}, u32[]{:S(2)}) collective-permute-start(bf16[4,360,128]{2,1,0:T(8,128)(2,1)S(1)} %add_convert_fusion), channel_id=1, source_target_pairs={{0,8},{1,9},{2,10},{3,11},{4,12},{5,13},{6,14},{7,15},{8,0},{9,1},... | collective-permute-start | bytes 1105928 | tf_op jit(solution)/shard_map/ppermute | solution.py:300
  40.8 10.1 %collective-permute-start.15 = (bf16[4,360,128]{2,1,0:T(8,128)(2,1)S(1)}, bf16[4,360,128]{2,1,0:T(8,128)(2,1)S(1)}, u32[]{:S(2)}, u32[]{:S(2)}) collective-permute-start(bf16[4,360,128]{2,1,0:T(8,128)(2,1)S(1)} %get-tuple-element.93), channel_id=1, source_target_pairs={{0,1},{1,0},{2,3},{3,2},{4,5},{5,4},{6,7},{7,6},{8,9},{9,8},{10,11... | collective-permute-start | bytes 1105928 | tf_op jit(solution)/shard_map/ppermute | solution.py:300
  48.7 9.0 %collective-permute-start.24 = (bf16[360,128]{1,0:T(8,128)(2,1)S(1)}, bf16[360,128]{1,0:T(8,128)(2,1)S(1)}, u32[]{:S(2)}, u32[]{:S(2)}) collective-permute-start(bf16[360,128]{1,0:T(8,128)(2,1)S(1)} %get-tuple-element.110), channel_id=1, source_target_pairs={{0,16},{1,17},{2,18},{3,19},{4,20},{5,21},{6,22},{7,23},{8,24},{9,... | collective-permute-start | bytes 276488 | tf_op jit(solution)/shard_map/ppermute | solution.py:300
  49.7 8.0 %collective-permute-start.25 = (bf16[360,128]{1,0:T(8,128)(2,1)S(1)}, bf16[360,128]{1,0:T(8,128)(2,1)S(1)}, u32[]{:S(2)}, u32[]{:S(2)}) collective-permute-start(bf16[360,128]{1,0:T(8,128)(2,1)S(1)} %get-tuple-element.111), channel_id=1, source_target_pairs={{0,24},{1,25},{2,26},{3,27},{4,28},{5,29},{6,30},{7,31},{8,16},{9,... | collective-permute-start | bytes 276488 | tf_op jit(solution)/shard_map/ppermute | solution.py:300
  51.0 6.7 %collective-permute-start.21 = (bf16[360,128]{1,0:T(8,128)(2,1)S(1)}, bf16[360,128]{1,0:T(8,128)(2,1)S(1)}, u32[]{:S(2)}, u32[]{:S(2)}) collective-permute-start(bf16[360,128]{1,0:T(8,128)(2,1)S(1)} %get-tuple-element.101), channel_id=1, source_target_pairs={{0,4},{1,5},{2,6},{3,7},{4,0},{5,1},{6,2},{7,3},{8,12},{9,13},{10,... | collective-permute-start | bytes 276488 | tf_op jit(solution)/shard_map/ppermute | solution.py:300
  51.6 6.1 %collective-permute-start.23 = (bf16[360,128]{1,0:T(8,128)(2,1)S(1)}, bf16[360,128]{1,0:T(8,128)(2,1)S(1)}, u32[]{:S(2)}, u32[]{:S(2)}) collective-permute-start(bf16[360,128]{1,0:T(8,128)(2,1)S(1)} %get-tuple-element.102), channel_id=1, source_target_pairs={{0,2},{1,3},{2,0},{3,1},{4,6},{5,7},{6,4},{7,5},{8,10},{9,11},{10,... | collective-permute-start | bytes 276488 | tf_op jit(solution)/shard_map/ppermute | solution.py:300
  53.0 5.5 %collective-permute-start.22 = (bf16[360,128]{1,0:T(8,128)(2,1)S(1)}, bf16[360,128]{1,0:T(8,128)(2,1)S(1)}, u32[]{:S(2)}, u32[]{:S(2)}) collective-permute-start(bf16[360,128]{1,0:T(8,128)(2,1)S(1)} %get-tuple-element.103), channel_id=1, source_target_pairs={{0,6},{1,7},{2,4},{3,5},{4,2},{5,3},{6,0},{7,1},{8,14},{9,15},{10,... | collective-permute-start | bytes 276488 | tf_op jit(solution)/shard_map/ppermute | solution.py:300

commit v17 on v15

--- a/solution.py
+++ b/solution.py
@@ -134,29 +134,22 @@
     )(*arrays)
 
 
-def fetch(sources, targets, sems):
+def pieces_kernel(groups, per, experts, *refs):
+    sources, (one_ref, near_ref, far_ref), targets = refs[:4], refs[4:7], refs[7:11]
+    tokens_ref, gain_ref, ids_ref, weights_ref = targets
     copies = [
-        pltpu.make_async_copy(source, target, sems.at[n])
+        pltpu.make_async_copy(source, target, refs[11].at[n])
         for n, (source, target) in enumerate(zip(sources, targets))
     ]
     for copy in copies:
         copy.start()
-    for copy in copies:
+    for copy in copies[1:]:
         copy.wait()
-
-
-def pieces_kernel(groups, per, experts, *refs):
-    sources, (one_ref, near_ref, far_ref) = refs[:4], refs[4:7]
-    tokens_ref, gain_ref, ids_ref, weights_ref = refs[7:11]
-    fetch(sources, refs[7:11], refs[11])
     features, lanes = tokens_ref.shape
     quarter = features // groups
     tail = one_ref.shape[0] - quarter
     rep = lax.axis_index("rep")
-    values = tokens_ref[...].astype(jnp.float32)
-    scale = lax.rsqrt(jnp.mean(values * values, axis=0, keepdims=True) + 1e-05)
     gain = jnp.broadcast_to(gain_ref[...].reshape(1, features), (lanes, features)).T
-    normed = values * scale * gain
     row = lax.broadcasted_iota(jnp.int32, (tail, lanes), 0)
     chosen = lax.broadcasted_iota(jnp.int32, (round_up(experts, 8), lanes), 0)
     shares = jnp.zeros(chosen.shape, jnp.float32)
@@ -167,6 +160,7 @@
         term = shares.astype(jnp.bfloat16).astype(jnp.float32)
         terms.append(term)
         shares = shares - term
+    tails = []
     for q in range(groups):
         rows = jnp.zeros((tail, lanes), jnp.float32)
         for n, term in enumerate(terms):
@@ -174,7 +168,13 @@
                 expert = q * per + i
                 if expert < experts:
                     rows = jnp.where(row == n * per + i, term[expert : expert + 1], rows)
-        piece = jnp.concatenate([normed[q * quarter : (q + 1) * quarter], rows], axis=0)
+        tails.append(rows)
+    copies[0].wait()
+    values = tokens_ref[...].astype(jnp.float32)
+    scale = lax.rsqrt(jnp.mean(values * values, axis=0, keepdims=True) + 1e-05)
+    normed = values * scale * gain
+    for q in range(groups):
+        piece = jnp.concatenate([normed[q * quarter : (q + 1) * quarter], tails[q]], axis=0)
         piece = piece.astype(jnp.bfloat16)
         k = rep ^ q
         for side, target in enumerate((near_ref, far_ref)):

time: 58.8 us -> 58.9 us (level)
  no operation moved by 1% of the time
where the time goes in v17:
time: 58.9 us; the launch traced here: 58.7 us
  starting transfers between devices  22.7 us (39%)
  waiting for transfers between devices  21.9 us (37%)
  Pallas kernels  9.56 us (16%)
  other arithmetic  3.02 us (5%)
  local copies, waits for them, and re-layouts  1.26 us (2%)
    ppermute x26, starting transfers between devices, swap(): lax.ppermute(array, ('seq', 'rep'), [(i, i ^ step) for i in range(devices)])  22.7 us
    ppermute x26, waiting for transfers between devices, swap(): lax.ppermute(array, ('seq', 'rep'), [(i, i ^ step) for i in range(devices)])  21.9 us
    pallas_call x4, Pallas kernels, run_expert(): pl.pallas_call(functools.partial(expert_kernel, quarter, per, blocks, slo...  5.87 us
    pallas_call x1, Pallas kernels, make_pieces(): pl.pallas_call(functools.partial(pieces_kernel, groups, per, experts), in...  2.46 us
    unnamed x10, local copies, waits for them, and re-layouts  1.26 us
    pallas_call x2, Pallas kernels, arrange(): pl.pallas_call(functools.partial(kernel, groups), out_shape=[jax.ShapeDty...  1.23 us
  transfers between devices with their start and end apart: 26, of which 13 were waited for; matrix products, arithmetic and copies ran while one was open for 4% of the time, Pallas kernels for 10%

profile of v17, /device:TPU:0, one launch (start us, length us, event | category | flops | bytes accessed | tf_op | source)
XLA Modules:
  0.0 58.7 jit_solution(9206703754094425639)
XLA Ops:
  0.0 2.5 %shard_map.100 = (bf16[368,128]{1,0:T(8,128)(2,1)}, bf16[2,368,128]{2,1,0:T(8,128)(2,1)}, bf16[2,368,128]{2,1,0:T(8,128)(2,1)}) custom-call(bf16[1440,128]{1,0:T(8,128)(2,1)} %bitcast.37, f32[1440]{0:T(1024)} %refs_1_.1, s32[4,128]{1,0:T(4,128)} %bitcast.40, f32[4,128]{1,0:T(4,128)} %bitcast.41), custom_call_target="tpu_custom_call" | custom-call | tf_op jit(solution)/shard_map/pallas_call | solution.py:196
  2.5 3.0 %collective-permute-start.5 = (bf16[2,368,128]{2,1,0:T(8,128)(2,1)}, bf16[2,368,128]{2,1,0:T(8,128)(2,1)S(1)}, u32[]{:S(2)}, u32[]{:S(2)}) collective-permute-start(bf16[2,368,128]{2,1,0:T(8,128)(2,1)} %get-tuple-element.58.refs_0_), channel_id=1, source_target_pairs={{0,4},{1,5},{2,6},{3,7},{4,0},{5,1},{6,2},{7,3},{8,12},{9,13},{10,... | collective-permute-start | bytes 565256 | tf_op jit(solution)/shard_map/ppermute | solution.py:300
  5.5 3.6 %collective-permute-start.1 = (bf16[368,128]{1,0:T(8,128)(2,1)}, bf16[368,128]{1,0:T(8,128)(2,1)S(1)}, u32[]{:S(2)}, u32[]{:S(2)}) collective-permute-start(bf16[368,128]{1,0:T(8,128)(2,1)} %get-tuple-element.53), channel_id=1, source_target_pairs={{0,24},{1,25},{2,26},{3,27},{4,28},{5,29},{6,30},{7,31},{8,16},{9,... | collective-permute-start | bytes 282632 | tf_op jit(solution)/shard_map/ppermute | solution.py:300
  9.1 0.7 %pad_maximum_fusion.5.biases_ref = f32[3,360]{1,0:T(4,128)S(1)} fusion(f32[1,360]{1,0:T(1,128)} %param.19, f32[1,360]{1,0:T(1,128)} %param.17, f32[1,360]{1,0:T(1,128)} %param.15), kind=kLoop, calls=%fused_computation.29 | loop fusion | flops 2160 | bytes 8640 | tf_op jit(solution)/shard_map/concatenate | solution.py:310
  9.8 1.2 %copy-done.2 = bf16[1,360,1440]{2,1,0:T(8,128)(2,1)S(1)} copy-done((bf16[1,360,1440]{2,1,0:T(8,128)(2,1)S(1)}, bf16[1,360,1440]{2,1,0:T(8,128)(2,1)}, u32[]{:S(2)}) %copy-start.2) | copy-done | bytes 1036824
  11.1 0.4 shard_map.102
  11.5 1.0 %pad_maximum_fusion = bf16[4,368,128]{2,1,0:T(8,128)(2,1)S(1)} fusion(bf16[2,368,128]{2,1,0:T(8,128)(2,1)S(1)} %collective-permute-done.5.refs_2_, bf16[2,368,128]{2,1,0:T(8,128)(2,1)} %get-tuple-element.58.refs_0_), kind=kLoop, calls=%fused_computation.1 | loop fusion | flops 188416 | bytes 753664 | tf_op jit(solution)/shard_map/concatenate | solution.py:343
  12.5 0.8 %collective-permute-start.7 = (bf16[4,368,128]{2,1,0:T(8,128)(2,1)S(1)}, bf16[4,368,128]{2,1,0:T(8,128)(2,1)S(1)}, u32[]{:S(2)}, u32[]{:S(2)}) collective-permute-start(bf16[4,368,128]{2,1,0:T(8,128)(2,1)S(1)} %pad_maximum_fusion), channel_id=1, source_target_pairs={{0,8},{1,9},{2,10},{3,11},{4,12},{5,13},{6,14},{7,15},{8,0},{9,1},... | collective-permute-start | bytes 1130504 | tf_op jit(solution)/shard_map/ppermute | solution.py:300
  13.4 0.8 %shard_map.101 = (bf16[768,1536]{1,0:T(8,128)(2,1)S(1)}, f32[768,128]{1,0:T(8,128)S(1)}) custom-call(bf16[1440,360]{1,0:T(8,128)(2,1)S(1)} %bitcast.34, bf16[1440,360]{1,0:T(8,128)(2,1)S(1)} %bitcast.35, f32[3,360]{1,0:T(4,128)S(1)} %pad_maximum_fusion.5.biases_ref), custom_call_target="tpu_custom_call" | custom-call | bytes 8294400 | tf_op jit(solution)/shard_map/pallas_call | solution.py:124
  14.2 2.9 %collective-permute-done = bf16[368,128]{1,0:T(8,128)(2,1)S(1)} collective-permute-done((bf16[368,128]{1,0:T(8,128)(2,1)}, bf16[368,128]{1,0:T(8,128)(2,1)S(1)}, u32[]{:S(2)}, u32[]{:S(2)}) %collective-permute-start) | collective-permute-done | bytes 94240 | tf_op jit(solution)/shard_map/ppermute | solution.py:300
  17.1 1.6 %collective-permute-start.4 = (bf16[2,368,128]{2,1,0:T(8,128)(2,1)S(1)}, bf16[2,368,128]{2,1,0:T(8,128)(2,1)S(1)}, u32[]{:S(2)}, u32[]{:S(2)}) collective-permute-start(bf16[2,368,128]{2,1,0:T(8,128)(2,1)S(1)} %pad_maximum_fusion.1.refs_0_), channel_id=1, source_target_pairs={{0,6},{1,7},{2,4},{3,5},{4,2},{5,3},{6,0},{7,1},{8,14},{9,15},{10,... | collective-permute-start | bytes 565256 | tf_op jit(solution)/shard_map/ppermute | solution.py:300
  18.6 0.5 collective-permute-start.3
  19.1 1.5 %collective-permute-start.2 = (bf16[2,368,128]{2,1,0:T(8,128)(2,1)S(1)}, bf16[2,368,128]{2,1,0:T(8,128)(2,1)S(1)}, u32[]{:S(2)}, u32[]{:S(2)}) collective-permute-start(bf16[2,368,128]{2,1,0:T(8,128)(2,1)S(1)} %pad_maximum_fusion.1.refs_0_), channel_id=1, source_target_pairs={{0,4},{1,5},{2,6},{3,7},{4,0},{5,1},{6,2},{7,3},{8,12},{9,13},{10,... | collective-permute-start | bytes 565256 | tf_op jit(solution)/shard_map/ppermute | solution.py:300
  20.6 1.5 %shard_map.103 = (bf16[4,360,128]{2,1,0:T(8,128)(2,1)S(1)}, bf16[4,360,128]{2,1,0:T(8,128)(2,1)S(1)}) custom-call(bf16[2,368,128]{2,1,0:T(8,128)(2,1)S(1)} %copy-done.3, bf16[2,368,128]{2,1,0:T(8,128)(2,1)S(1)} %copy-done.4, bf16[2,368,128]{2,1,0:T(8,128)(2,1)S(1)} %collective-permute-done.5.refs_2_, ...), custom_call_target="tpu_custom_call" | custom-call | flops 1811939328 | bytes 3538944 | tf_op jit(solution)/shard_map/pallas_call | solution.py:265
  22.1 3.6 %collective-permute-done.4.refs_6_ = bf16[2,368,128]{2,1,0:T(8,128)(2,1)S(1)} collective-permute-done((bf16[2,368,128]{2,1,0:T(8,128)(2,1)S(1)}, bf16[2,368,128]{2,1,0:T(8,128)(2,1)S(1)}, u32[]{:S(2)}, u32[]{:S(2)}) %collective-permute-start.4) | collective-permute-done | bytes 188448 | tf_op jit(solution)/shard_map/ppermute | solution.py:300
  25.7 2.2 %collective-permute-done.3.refs_2_ = bf16[2,368,128]{2,1,0:T(8,128)(2,1)S(1)} collective-permute-done((bf16[2,368,128]{2,1,0:T(8,128)(2,1)S(1)}, bf16[2,368,128]{2,1,0:T(8,128)(2,1)S(1)}, u32[]{:S(2)}, u32[]{:S(2)}) %collective-permute-start.3) | collective-permute-done | bytes 188448 | tf_op jit(solution)/shard_map/ppermute | solution.py:300
  27.9 0.1 collective-permute-done.2.refs_4_
  28.0 0.5 collective-permute-start.9
  28.6 0.5 collective-permute-start.11
  29.0 0.4 collective-permute-done.8.refs_1_
  29.5 0.3 collective-permute-done.9.refs_3_
  29.7 0.3 collective-permute-done.10.refs_5_
  30.0 0.3 collective-permute-done.11.refs_7_
  30.3 1.5 %shard_map.104 = (bf16[4,360,128]{2,1,0:T(8,128)(2,1)S(1)}, bf16[4,360,128]{2,1,0:T(8,128)(2,1)S(1)}) custom-call(bf16[2,368,128]{2,1,0:T(8,128)(2,1)S(1)} %pad_maximum_fusion.1.refs_0_, bf16[2,368,128]{2,1,0:T(8,128)(2,1)S(1)} %collective-permute-done.8.refs_1_, bf16[2,368,128]{2,1,0:T(8,128)(2,1)S(1)} %collective-permute-done.3.refs_2_, ...), custom_call_target="tpu_custom_call" | custom-call | flops 1811939328 | bytes 3538944 | tf_op jit(solution)/shard_map/pallas_call | solution.py:265
  31.7 0.3 collective-permute-start.13
  32.0 0.3 collective-permute-start.12
  32.3 1.5 %shard_map.105 = (bf16[4,360,128]{2,1,0:T(8,128)(2,1)S(1)}, bf16[4,360,128]{2,1,0:T(8,128)(2,1)S(1)}) custom-call(bf16[2,368,128]{2,1,0:T(8,128)(2,1)S(1)} %pad_maximum_fusion.1.refs_0_, bf16[2,368,128]{2,1,0:T(8,128)(2,1)S(1)} %collective-permute-done.8.refs_1_, bf16[2,368,128]{2,1,0:T(8,128)(2,1)S(1)} %collective-permute-done.3.refs_2_, ...), custom_call_target="tpu_custom_call" | custom-call | flops 1811939328 | bytes 3538944 | tf_op jit(solution)/shard_map/pallas_call | solution.py:265
  33.8 0.2 collective-permute-done.12
  34.0 0.2 collective-permute-start.14
  34.3 1.5 %shard_map.106 = (bf16[4,360,128]{2,1,0:T(8,128)(2,1)S(1)}, bf16[4,360,128]{2,1,0:T(8,128)(2,1)S(1)}) custom-call(bf16[4,368,128]{2,1,0:T(8,128)(2,1)S(1)} %collective-permute-done.7.refs_0_, bf16[4,368,128]{2,1,0:T(8,128)(2,1)S(1)} %collective-permute-done.13.refs_1_, bf16[768,1536]{1,0:T(8,128)(2,1)S(1)} %get-tuple-element.63.refs_4_.refs_8_.refs_2_, ...), custom_call_target="tpu_custom_call" | custom-call | flops 1811939328 | bytes 3538944 | tf_op jit(solution)/shard_map/pallas_call | solution.py:265
  35.7 0.3 collective-permute-start.16
  36.2 0.1 add_convert_fusion.10
  36.3 1.5 %collective-permute-start.19 = (bf16[2,360,128]{2,1,0:T(8,128)(2,1)S(1)}, bf16[2,360,128]{2,1,0:T(8,128)(2,1)S(1)}, u32[]{:S(2)}, u32[]{:S(2)}) collective-permute-start(bf16[2,360,128]{2,1,0:T(8,128)(2,1)S(1)} %pad_maximum_fusion.3), channel_id=1, source_target_pairs={{0,6},{1,7},{2,4},{3,5},{4,2},{5,3},{6,0},{7,1},{8,14},{9,15},{10,... | collective-permute-start | bytes 552968 | tf_op jit(solution)/shard_map/ppermute | solution.py:300
  37.8 0.7 %collective-permute-start.20 = (bf16[2,360,128]{2,1,0:T(8,128)(2,1)S(1)}, bf16[2,360,128]{2,1,0:T(8,128)(2,1)S(1)}, u32[]{:S(2)}, u32[]{:S(2)}) collective-permute-start(bf16[2,360,128]{2,1,0:T(8,128)(2,1)S(1)} %pad_maximum_fusion.4), channel_id=1, source_target_pairs={{0,2},{1,3},{2,0},{3,1},{4,6},{5,7},{6,4},{7,5},{8,10},{9,11},{10,... | collective-permute-start | bytes 552968 | tf_op jit(solution)/shard_map/ppermute | solution.py:300
  38.5 1.6 %collective-permute-start.18 = (bf16[2,360,128]{2,1,0:T(8,128)(2,1)S(1)}, bf16[2,360,128]{2,1,0:T(8,128)(2,1)S(1)}, u32[]{:S(2)}, u32[]{:S(2)}) collective-permute-start(bf16[2,360,128]{2,1,0:T(8,128)(2,1)S(1)} %pad_maximum_fusion.2), channel_id=1, source_target_pairs={{0,4},{1,5},{2,6},{3,7},{4,0},{5,1},{6,2},{7,3},{8,12},{9,13},{10,... | collective-permute-start | bytes 552968 | tf_op jit(solution)/shard_map/ppermute | solution.py:300
  40.0 0.1 add_convert_fusion
  40.3 4.5 %collective-permute-done.19 = bf16[2,360,128]{2,1,0:T(8,128)(2,1)S(1)} collective-permute-done((bf16[2,360,128]{2,1,0:T(8,128)(2,1)S(1)}, bf16[2,360,128]{2,1,0:T(8,128)(2,1)S(1)}, u32[]{:S(2)}, u32[]{:S(2)}) %collective-permute-start.19) | collective-permute-done | bytes 184352 | tf_op jit(solution)/shard_map/ppermute | solution.py:300
  44.8 3.2 %collective-permute-done.20 = bf16[2,360,128]{2,1,0:T(8,128)(2,1)S(1)} collective-permute-done((bf16[2,360,128]{2,1,0:T(8,128)(2,1)S(1)}, bf16[2,360,128]{2,1,0:T(8,128)(2,1)S(1)}, u32[]{:S(2)}, u32[]{:S(2)}) %collective-permute-start.20) | collective-permute-done | bytes 184352 | tf_op jit(solution)/shard_map/ppermute | solution.py:300
  48.0 0.1 fusion.8
  48.1 1.0 %collective-permute-start.24 = (bf16[360,128]{1,0:T(8,128)(2,1)S(1)}, bf16[360,128]{1,0:T(8,128)(2,1)S(1)}, u32[]{:S(2)}, u32[]{:S(2)}) collective-permute-start(bf16[360,128]{1,0:T(8,128)(2,1)S(1)} %get-tuple-element.110), channel_id=1, source_target_pairs={{0,16},{1,17},{2,18},{3,19},{4,20},{5,21},{6,22},{7,23},{8,24},{9,... | collective-permute-start | bytes 276488 | tf_op jit(solution)/shard_map/ppermute | solution.py:300
  49.1 1.1 %collective-permute-start.25 = (bf16[360,128]{1,0:T(8,128)(2,1)S(1)}, bf16[360,128]{1,0:T(8,128)(2,1)S(1)}, u32[]{:S(2)}, u32[]{:S(2)}) collective-permute-start(bf16[360,128]{1,0:T(8,128)(2,1)S(1)} %get-tuple-element.111), channel_id=1, source_target_pairs={{0,24},{1,25},{2,26},{3,27},{4,28},{5,29},{6,30},{7,31},{8,16},{9,... | collective-permute-start | bytes 276488 | tf_op jit(solution)/shard_map/ppermute | solution.py:300
  50.3 0.1 fusion.5
  50.4 0.6 %collective-permute-start.21 = (bf16[360,128]{1,0:T(8,128)(2,1)S(1)}, bf16[360,128]{1,0:T(8,128)(2,1)S(1)}, u32[]{:S(2)}, u32[]{:S(2)}) collective-permute-start(bf16[360,128]{1,0:T(8,128)(2,1)S(1)} %get-tuple-element.101), channel_id=1, source_target_pairs={{0,4},{1,5},{2,6},{3,7},{4,0},{5,1},{6,2},{7,3},{8,12},{9,13},{10,... | collective-permute-start | bytes 276488 | tf_op jit(solution)/shard_map/ppermute | solution.py:300
  51.0 1.4 %collective-permute-start.23 = (bf16[360,128]{1,0:T(8,128)(2,1)S(1)}, bf16[360,128]{1,0:T(8,128)(2,1)S(1)}, u32[]{:S(2)}, u32[]{:S(2)}) collective-permute-start(bf16[360,128]{1,0:T(8,128)(2,1)S(1)} %get-tuple-element.102), channel_id=1, source_target_pairs={{0,2},{1,3},{2,0},{3,1},{4,6},{5,7},{6,4},{7,5},{8,10},{9,11},{10,... | collective-permute-start | bytes 276488 | tf_op jit(solution)/shard_map/ppermute | solution.py:300
  52.5 1.5 %collective-permute-start.22 = (bf16[360,128]{1,0:T(8,128)(2,1)S(1)}, bf16[360,128]{1,0:T(8,128)(2,1)S(1)}, u32[]{:S(2)}, u32[]{:S(2)}) collective-permute-start(bf16[360,128]{1,0:T(8,128)(2,1)S(1)} %get-tuple-element.103), channel_id=1, source_target_pairs={{0,6},{1,7},{2,4},{3,5},{4,2},{5,3},{6,0},{7,1},{8,14},{9,15},{10,... | collective-permute-start | bytes 276488 | tf_op jit(solution)/shard_map/ppermute | solution.py:300
  54.0 3.1 %collective-permute-done.24 = bf16[360,128]{1,0:T(8,128)(2,1)S(1)} collective-permute-done((bf16[360,128]{1,0:T(8,128)(2,1)S(1)}, bf16[360,128]{1,0:T(8,128)(2,1)S(1)}, u32[]{:S(2)}, u32[]{:S(2)}) %collective-permute-start.24) | collective-permute-done | bytes 92192 | tf_op jit(solution)/shard_map/ppermute | solution.py:300
  57.1 0.8 %collective-permute-done.22 = bf16[360,128]{1,0:T(8,128)(2,1)S(1)} collective-permute-done((bf16[360,128]{1,0:T(8,128)(2,1)S(1)}, bf16[360,128]{1,0:T(8,128)(2,1)S(1)}, u32[]{:S(2)}, u32[]{:S(2)}) %collective-permute-start.22) | collective-permute-done | bytes 92192 | tf_op jit(solution)/shard_map/ppermute | solution.py:300
  57.9 0.8 %fusion.10 = bf16[128,360]{0,1:T(8,128)(2,1)} fusion(bf16[360,128]{1,0:T(8,128)(2,1)S(1)} %collective-permute-done.25, bf16[360,128]{1,0:T(8,128)(2,1)S(1)} %collective-permute-done.24, bf16[360,128]{1,0:T(8,128)(2,1)S(1)} %collective-permute-done.23, bf16[360,128]{1,0:T(8,128)(2,1)S(1)} %collective-permute-done.22, ...), kind=kLoop, calls=%fused_computation.28 | loop fusion | flops 737280 | bytes 829440 | tf_op jit(solution)/shard_map/transpose | solution.py:378
  (33 shorter events, 0.4 us)
Async XLA Ops:
  0.0 13.3 %copy-start = (bf16[1,1440,360]{2,1,0:T(8,128)(2,1)S(1)}, bf16[1,1440,360]{2,1,0:T(8,128)(2,1)}, u32[]{:S(2)}) copy-start(bf16[1,1440,360]{2,1,0:T(8,128)(2,1)} %param.14) | copy-start | bytes 3110404
  0.0 13.3 %copy-start.1 = (bf16[1,1440,360]{2,1,0:T(8,128)(2,1)S(1)}, bf16[1,1440,360]{2,1,0:T(8,128)(2,1)}, u32[]{:S(2)}) copy-start(bf16[1,1440,360]{2,1,0:T(8,128)(2,1)} %param.16) | copy-start | bytes 3110404
  2.5 9.0 %collective-permute-start.5 = (bf16[2,368,128]{2,1,0:T(8,128)(2,1)}, bf16[2,368,128]{2,1,0:T(8,128)(2,1)S(1)}, u32[]{:S(2)}, u32[]{:S(2)}) collective-permute-start(bf16[2,368,128]{2,1,0:T(8,128)(2,1)} %get-tuple-element.58.refs_0_), channel_id=1, source_target_pairs={{0,4},{1,5},{2,6},{3,7},{4,0},{5,1},{6,2},{7,3},{8,12},{9,13},{10,... | collective-permute-start | bytes 565256 | tf_op jit(solution)/shard_map/ppermute | solution.py:300
  5.5 8.7 %collective-permute-start.1 = (bf16[368,128]{1,0:T(8,128)(2,1)}, bf16[368,128]{1,0:T(8,128)(2,1)S(1)}, u32[]{:S(2)}, u32[]{:S(2)}) collective-permute-start(bf16[368,128]{1,0:T(8,128)(2,1)} %get-tuple-element.53), channel_id=1, source_target_pairs={{0,24},{1,25},{2,26},{3,27},{4,28},{5,29},{6,30},{7,31},{8,16},{9,... | collective-permute-start | bytes 282632 | tf_op jit(solution)/shard_map/ppermute | solution.py:300
  9.1 8.0 %collective-permute-start = (bf16[368,128]{1,0:T(8,128)(2,1)}, bf16[368,128]{1,0:T(8,128)(2,1)S(1)}, u32[]{:S(2)}, u32[]{:S(2)}) collective-permute-start(bf16[368,128]{1,0:T(8,128)(2,1)} %get-tuple-element.53), channel_id=1, source_target_pairs={{0,16},{1,17},{2,18},{3,19},{4,20},{5,21},{6,22},{7,23},{8,24},{9,... | collective-permute-start | bytes 282632 | tf_op jit(solution)/shard_map/ppermute | solution.py:300
  9.8 1.2 %copy-start.2 = (bf16[1,360,1440]{2,1,0:T(8,128)(2,1)S(1)}, bf16[1,360,1440]{2,1,0:T(8,128)(2,1)}, u32[]{:S(2)}) copy-start(bf16[1,360,1440]{2,1,0:T(8,128)(2,1)} %param.18) | copy-start | bytes 3110404
  12.5 15.5 %collective-permute-start.7 = (bf16[4,368,128]{2,1,0:T(8,128)(2,1)S(1)}, bf16[4,368,128]{2,1,0:T(8,128)(2,1)S(1)}, u32[]{:S(2)}, u32[]{:S(2)}) collective-permute-start(bf16[4,368,128]{2,1,0:T(8,128)(2,1)S(1)} %pad_maximum_fusion), channel_id=1, source_target_pairs={{0,8},{1,9},{2,10},{3,11},{4,12},{5,13},{6,14},{7,15},{8,0},{9,1},... | collective-permute-start | bytes 1130504 | tf_op jit(solution)/shard_map/ppermute | solution.py:300
  13.3 7.3 %collective-permute-start.6 = (bf16[2,368,128]{2,1,0:T(8,128)(2,1)S(1)}, bf16[2,368,128]{2,1,0:T(8,128)(2,1)S(1)}, u32[]{:S(2)}, u32[]{:S(2)}) collective-permute-start(bf16[2,368,128]{2,1,0:T(8,128)(2,1)S(1)} %collective-permute-done.5.refs_2_), channel_id=1, source_target_pairs={{0,1},{1,0},{2,3},{3,2},{4,5},{5,4},{6,7},{7,6},{8,9},{9,8},{10,11... | collective-permute-start | bytes 565256 | tf_op jit(solution)/shard_map/ppermute | solution.py:300
  13.3 7.3 %copy-start.3 = (bf16[2,368,128]{2,1,0:T(8,128)(2,1)S(1)}, bf16[2,368,128]{2,1,0:T(8,128)(2,1)}, u32[]{:S(2)}) copy-start(bf16[2,368,128]{2,1,0:T(8,128)(2,1)} %get-tuple-element.58.refs_0_) | copy-start | bytes 565252
  13.3 7.3 %copy-start.4 = (bf16[2,368,128]{2,1,0:T(8,128)(2,1)S(1)}, bf16[2,368,128]{2,1,0:T(8,128)(2,1)}, u32[]{:S(2)}) copy-start(bf16[2,368,128]{2,1,0:T(8,128)(2,1)} %get-tuple-element.59.refs_1_) | copy-start | bytes 565252
  17.1 8.7 %collective-permute-start.4 = (bf16[2,368,128]{2,1,0:T(8,128)(2,1)S(1)}, bf16[2,368,128]{2,1,0:T(8,128)(2,1)S(1)}, u32[]{:S(2)}, u32[]{:S(2)}) collective-permute-start(bf16[2,368,128]{2,1,0:T(8,128)(2,1)S(1)} %pad_maximum_fusion.1.refs_0_), channel_id=1, source_target_pairs={{0,6},{1,7},{2,4},{3,5},{4,2},{5,3},{6,0},{7,1},{8,14},{9,15},{10,... | collective-permute-start | bytes 565256 | tf_op jit(solution)/shard_map/ppermute | solution.py:300
  18.6 9.3 %collective-permute-start.3 = (bf16[2,368,128]{2,1,0:T(8,128)(2,1)S(1)}, bf16[2,368,128]{2,1,0:T(8,128)(2,1)S(1)}, u32[]{:S(2)}, u32[]{:S(2)}) collective-permute-start(bf16[2,368,128]{2,1,0:T(8,128)(2,1)S(1)} %pad_maximum_fusion.1.refs_0_), channel_id=1, source_target_pairs={{0,2},{1,3},{2,0},{3,1},{4,6},{5,7},{6,4},{7,5},{8,10},{9,11},{10,... | collective-permute-start | bytes 565256 | tf_op jit(solution)/shard_map/ppermute | solution.py:300
  19.1 8.9 %collective-permute-start.2 = (bf16[2,368,128]{2,1,0:T(8,128)(2,1)S(1)}, bf16[2,368,128]{2,1,0:T(8,128)(2,1)S(1)}, u32[]{:S(2)}, u32[]{:S(2)}) collective-permute-start(bf16[2,368,128]{2,1,0:T(8,128)(2,1)S(1)} %pad_maximum_fusion.1.refs_0_), channel_id=1, source_target_pairs={{0,4},{1,5},{2,6},{3,7},{4,0},{5,1},{6,2},{7,3},{8,12},{9,13},{10,... | collective-permute-start | bytes 565256 | tf_op jit(solution)/shard_map/ppermute | solution.py:300
  28.0 1.4 %collective-permute-start.8 = (bf16[2,368,128]{2,1,0:T(8,128)(2,1)S(1)}, bf16[2,368,128]{2,1,0:T(8,128)(2,1)S(1)}, u32[]{:S(2)}, u32[]{:S(2)}) collective-permute-start(bf16[2,368,128]{2,1,0:T(8,128)(2,1)S(1)} %pad_maximum_fusion.1.refs_0_), channel_id=1, source_target_pairs={{0,1},{1,0},{2,3},{3,2},{4,5},{5,4},{6,7},{7,6},{8,9},{9,8},{10,11... | collective-permute-start | bytes 565256 | tf_op jit(solution)/shard_map/ppermute | solution.py:300
  28.0 1.7 %collective-permute-start.9 = (bf16[2,368,128]{2,1,0:T(8,128)(2,1)S(1)}, bf16[2,368,128]{2,1,0:T(8,128)(2,1)S(1)}, u32[]{:S(2)}, u32[]{:S(2)}) collective-permute-start(bf16[2,368,128]{2,1,0:T(8,128)(2,1)S(1)} %collective-permute-done.3.refs_2_), channel_id=1, source_target_pairs={{0,1},{1,0},{2,3},{3,2},{4,5},{5,4},{6,7},{7,6},{8,9},{9,8},{10,11... | collective-permute-start | bytes 565256 | tf_op jit(solution)/shard_map/ppermute | solution.py:300
  28.5 1.5 %collective-permute-start.10 = (bf16[2,368,128]{2,1,0:T(8,128)(2,1)S(1)}, bf16[2,368,128]{2,1,0:T(8,128)(2,1)S(1)}, u32[]{:S(2)}, u32[]{:S(2)}) collective-permute-start(bf16[2,368,128]{2,1,0:T(8,128)(2,1)S(1)} %collective-permute-done.2.refs_4_), channel_id=1, source_target_pairs={{0,1},{1,0},{2,3},{3,2},{4,5},{5,4},{6,7},{7,6},{8,9},{9,8},{10,11... | collective-permute-start | bytes 565256 | tf_op jit(solution)/shard_map/ppermute | solution.py:300
  28.6 1.7 %collective-permute-start.11 = (bf16[2,368,128]{2,1,0:T(8,128)(2,1)S(1)}, bf16[2,368,128]{2,1,0:T(8,128)(2,1)S(1)}, u32[]{:S(2)}, u32[]{:S(2)}) collective-permute-start(bf16[2,368,128]{2,1,0:T(8,128)(2,1)S(1)} %collective-permute-done.4.refs_6_), channel_id=1, source_target_pairs={{0,1},{1,0},{2,3},{3,2},{4,5},{5,4},{6,7},{7,6},{8,9},{9,8},{10,11... | collective-permute-start | bytes 565256 | tf_op jit(solution)/shard_map/ppermute | solution.py:300
  31.7 2.3 %collective-permute-start.13 = (bf16[4,368,128]{2,1,0:T(8,128)(2,1)S(1)}, bf16[4,368,128]{2,1,0:T(8,128)(2,1)S(1)}, u32[]{:S(2)}, u32[]{:S(2)}) collective-permute-start(bf16[4,368,128]{2,1,0:T(8,128)(2,1)S(1)} %collective-permute-done.7.refs_0_), channel_id=1, source_target_pairs={{0,1},{1,0},{2,3},{3,2},{4,5},{5,4},{6,7},{7,6},{8,9},{9,8},{10,11... | collective-permute-start | bytes 1130504 | tf_op jit(solution)/shard_map/ppermute | solution.py:300
  32.0 2.0 %collective-permute-start.12 = (bf16[4,360,128]{2,1,0:T(8,128)(2,1)S(1)}, bf16[4,360,128]{2,1,0:T(8,128)(2,1)S(1)}, u32[]{:S(2)}, u32[]{:S(2)}) collective-permute-start(bf16[4,360,128]{2,1,0:T(8,128)(2,1)S(1)} %get-tuple-element.74), channel_id=1, source_target_pairs={{0,1},{1,0},{2,3},{3,2},{4,5},{5,4},{6,7},{7,6},{8,9},{9,8},{10,11... | collective-permute-start | bytes 1105928 | tf_op jit(solution)/shard_map/ppermute | solution.py:300
  34.0 2.1 %collective-permute-start.14 = (bf16[4,360,128]{2,1,0:T(8,128)(2,1)S(1)}, bf16[4,360,128]{2,1,0:T(8,128)(2,1)S(1)}, u32[]{:S(2)}, u32[]{:S(2)}) collective-permute-start(bf16[4,360,128]{2,1,0:T(8,128)(2,1)S(1)} %get-tuple-element.91), channel_id=1, source_target_pairs={{0,1},{1,0},{2,3},{3,2},{4,5},{5,4},{6,7},{7,6},{8,9},{9,8},{10,11... | collective-permute-start | bytes 1105928 | tf_op jit(solution)/shard_map/ppermute | solution.py:300
  35.7 4.3 %collective-permute-start.16 = (bf16[4,360,128]{2,1,0:T(8,128)(2,1)S(1)}, bf16[4,360,128]{2,1,0:T(8,128)(2,1)S(1)}, u32[]{:S(2)}, u32[]{:S(2)}) collective-permute-start(bf16[4,360,128]{2,1,0:T(8,128)(2,1)S(1)} %get-tuple-element.95), channel_id=1, source_target_pairs={{0,1},{1,0},{2,3},{3,2},{4,5},{5,4},{6,7},{7,6},{8,9},{9,8},{10,11... | collective-permute-start | bytes 1105928 | tf_op jit(solution)/shard_map/ppermute | solution.py:300
  36.3 8.5 %collective-permute-start.19 = (bf16[2,360,128]{2,1,0:T(8,128)(2,1)S(1)}, bf16[2,360,128]{2,1,0:T(8,128)(2,1)S(1)}, u32[]{:S(2)}, u32[]{:S(2)}) collective-permute-start(bf16[2,360,128]{2,1,0:T(8,128)(2,1)S(1)} %pad_maximum_fusion.3), channel_id=1, source_target_pairs={{0,6},{1,7},{2,4},{3,5},{4,2},{5,3},{6,0},{7,1},{8,14},{9,15},{10,... | collective-permute-start | bytes 552968 | tf_op jit(solution)/shard_map/ppermute | solution.py:300
  37.8 10.2 %collective-permute-start.20 = (bf16[2,360,128]{2,1,0:T(8,128)(2,1)S(1)}, bf16[2,360,128]{2,1,0:T(8,128)(2,1)S(1)}, u32[]{:S(2)}, u32[]{:S(2)}) collective-permute-start(bf16[2,360,128]{2,1,0:T(8,128)(2,1)S(1)} %pad_maximum_fusion.4), channel_id=1, source_target_pairs={{0,2},{1,3},{2,0},{3,1},{4,6},{5,7},{6,4},{7,5},{8,10},{9,11},{10,... | collective-permute-start | bytes 552968 | tf_op jit(solution)/shard_map/ppermute | solution.py:300
  38.5 9.5 %collective-permute-start.18 = (bf16[2,360,128]{2,1,0:T(8,128)(2,1)S(1)}, bf16[2,360,128]{2,1,0:T(8,128)(2,1)S(1)}, u32[]{:S(2)}, u32[]{:S(2)}) collective-permute-start(bf16[2,360,128]{2,1,0:T(8,128)(2,1)S(1)} %pad_maximum_fusion.2), channel_id=1, source_target_pairs={{0,4},{1,5},{2,6},{3,7},{4,0},{5,1},{6,2},{7,3},{8,12},{9,13},{10,... | collective-permute-start | bytes 552968 | tf_op jit(solution)/shard_map/ppermute | solution.py:300
  40.1 10.2 %collective-permute-start.17 = (bf16[4,360,128]{2,1,0:T(8,128)(2,1)S(1)}, bf16[4,360,128]{2,1,0:T(8,128)(2,1)S(1)}, u32[]{:S(2)}, u32[]{:S(2)}) collective-permute-start(bf16[4,360,128]{2,1,0:T(8,128)(2,1)S(1)} %add_convert_fusion), channel_id=1, source_target_pairs={{0,8},{1,9},{2,10},{3,11},{4,12},{5,13},{6,14},{7,15},{8,0},{9,1},... | collective-permute-start | bytes 1105928 | tf_op jit(solution)/shard_map/ppermute | solution.py:300
  40.2 10.1 %collective-permute-start.15 = (bf16[4,360,128]{2,1,0:T(8,128)(2,1)S(1)}, bf16[4,360,128]{2,1,0:T(8,128)(2,1)S(1)}, u32[]{:S(2)}, u32[]{:S(2)}) collective-permute-start(bf16[4,360,128]{2,1,0:T(8,128)(2,1)S(1)} %get-tuple-element.93), channel_id=1, source_target_pairs={{0,1},{1,0},{2,3},{3,2},{4,5},{5,4},{6,7},{7,6},{8,9},{9,8},{10,11... | collective-permute-start | bytes 1105928 | tf_op jit(solution)/shard_map/ppermute | solution.py:300
  48.1 9.0 %collective-permute-start.24 = (bf16[360,128]{1,0:T(8,128)(2,1)S(1)}, bf16[360,128]{1,0:T(8,128)(2,1)S(1)}, u32[]{:S(2)}, u32[]{:S(2)}) collective-permute-start(bf16[360,128]{1,0:T(8,128)(2,1)S(1)} %get-tuple-element.110), channel_id=1, source_target_pairs={{0,16},{1,17},{2,18},{3,19},{4,20},{5,21},{6,22},{7,23},{8,24},{9,... | collective-permute-start | bytes 276488 | tf_op jit(solution)/shard_map/ppermute | solution.py:300
  49.1 7.9 %collective-permute-start.25 = (bf16[360,128]{1,0:T(8,128)(2,1)S(1)}, bf16[360,128]{1,0:T(8,128)(2,1)S(1)}, u32[]{:S(2)}, u32[]{:S(2)}) collective-permute-start(bf16[360,128]{1,0:T(8,128)(2,1)S(1)} %get-tuple-element.111), channel_id=1, source_target_pairs={{0,24},{1,25},{2,26},{3,27},{4,28},{5,29},{6,30},{7,31},{8,16},{9,... | collective-permute-start | bytes 276488 | tf_op jit(solution)/shard_map/ppermute | solution.py:300
  50.4 6.7 %collective-permute-start.21 = (bf16[360,128]{1,0:T(8,128)(2,1)S(1)}, bf16[360,128]{1,0:T(8,128)(2,1)S(1)}, u32[]{:S(2)}, u32[]{:S(2)}) collective-permute-start(bf16[360,128]{1,0:T(8,128)(2,1)S(1)} %get-tuple-element.101), channel_id=1, source_target_pairs={{0,4},{1,5},{2,6},{3,7},{4,0},{5,1},{6,2},{7,3},{8,12},{9,13},{10,... | collective-permute-start | bytes 276488 | tf_op jit(solution)/shard_map/ppermute | solution.py:300
  51.0 6.1 %collective-permute-start.23 = (bf16[360,128]{1,0:T(8,128)(2,1)S(1)}, bf16[360,128]{1,0:T(8,128)(2,1)S(1)}, u32[]{:S(2)}, u32[]{:S(2)}) collective-permute-start(bf16[360,128]{1,0:T(8,128)(2,1)S(1)} %get-tuple-element.102), channel_id=1, source_target_pairs={{0,2},{1,3},{2,0},{3,1},{4,6},{5,7},{6,4},{7,5},{8,10},{9,11},{10,... | collective-permute-start | bytes 276488 | tf_op jit(solution)/shard_map/ppermute | solution.py:300
  52.5 5.5 %collective-permute-start.22 = (bf16[360,128]{1,0:T(8,128)(2,1)S(1)}, bf16[360,128]{1,0:T(8,128)(2,1)S(1)}, u32[]{:S(2)}, u32[]{:S(2)}) collective-permute-start(bf16[360,128]{1,0:T(8,128)(2,1)S(1)} %get-tuple-element.103), channel_id=1, source_target_pairs={{0,6},{1,7},{2,4},{3,5},{4,2},{5,3},{6,0},{7,1},{8,14},{9,15},{10,... | collective-permute-start | bytes 276488 | tf_op jit(solution)/shard_map/ppermute | solution.py:300

commit v18 on v15

--- a/solution.py
+++ b/solution.py
@@ -215,6 +215,7 @@
     hidden = gate_up_ref.shape[0] // 2
     rep, seq = lax.axis_index("rep"), lax.axis_index("seq")
     halves = len(scratch)
+    used = round_up(quarter, 16)
     count = len(blocks) // halves
     row = lax.broadcasted_iota(jnp.int32, (piece_rows - quarter, lanes), 0)
     for half in range(halves):
@@ -244,10 +245,10 @@
             activated.append(gated(both[: hidden // 2], both[hidden // 2 :]))
         activated = jnp.concatenate(activated, axis=0)
         for k in range(groups):
-            own_rows = down_ref[pl.ds(pl.multiple_of((rep ^ k) * size, size), size), :]
+            own_rows = down_ref[pl.ds(pl.multiple_of((rep ^ k) * size, size), used), :]
             rows = jnp.dot(own_rows, activated, preferred_element_type=jnp.float32)
             if k == 0:
-                rows = rows + jnp.concatenate([down_bias_ref[...]] * count, axis=1)
+                rows = rows + jnp.concatenate([down_bias_ref[:used]] * count, axis=1)
             rows = (rows * wide).astype(jnp.bfloat16)
             target = send_ref if k % 2 else keep_ref
             for j in range(count):

time: 58.8 us -> 58.7 us (level)
  no operation moved by 1% of the time
where the time goes in v18:
time: 58.7 us; the launch traced here: 58.5 us
  starting transfers between devices  22.7 us (39%)
  waiting for transfers between devices  21.9 us (37%)
  Pallas kernels  9.4 us (16%)
  other arithmetic  3.02 us (5%)
  local copies, waits for them, and re-layouts  1.26 us (2%)
    ppermute x26, starting transfers between devices, swap(): lax.ppermute(array, ('seq', 'rep'), [(i, i ^ step) for i in range(devices)])  22.7 us
    ppermute x26, waiting for transfers between devices, swap(): lax.ppermute(array, ('seq', 'rep'), [(i, i ^ step) for i in range(devices)])  21.9 us
    pallas_call x4, Pallas kernels, run_expert(): pl.pallas_call(functools.partial(expert_kernel, quarter, per, blocks, slo...  5.81 us
    pallas_call x1, Pallas kernels, make_pieces(): pl.pallas_call(functools.partial(pieces_kernel, groups, per, experts), in...  2.35 us
    unnamed x10, local copies, waits for them, and re-layouts  1.26 us
    pallas_call x2, Pallas kernels, arrange(): pl.pallas_call(functools.partial(kernel, groups), out_shape=[jax.ShapeDty...  1.23 us
  transfers between devices with their start and end apart: 26, of which 13 were waited for; matrix products, arithmetic and copies ran while one was open for 4% of the time, Pallas kernels for 10%

profile of v18, /device:TPU:0, one launch (start us, length us, event | category | flops | bytes accessed | tf_op | source)
XLA Modules:
  0.0 58.5 jit_solution(15499595509242008434)
XLA Ops:
  0.0 2.4 %shard_map.100 = (bf16[368,128]{1,0:T(8,128)(2,1)}, bf16[2,368,128]{2,1,0:T(8,128)(2,1)}, bf16[2,368,128]{2,1,0:T(8,128)(2,1)}) custom-call(bf16[1440,128]{1,0:T(8,128)(2,1)} %bitcast.37, f32[1440]{0:T(1024)} %refs_1_.1, s32[4,128]{1,0:T(4,128)} %bitcast.40, f32[4,128]{1,0:T(4,128)} %bitcast.41), custom_call_target="tpu_custom_call" | custom-call | tf_op jit(solution)/shard_map/pallas_call | solution.py:196
  2.4 3.0 %collective-permute-start.5 = (bf16[2,368,128]{2,1,0:T(8,128)(2,1)}, bf16[2,368,128]{2,1,0:T(8,128)(2,1)S(1)}, u32[]{:S(2)}, u32[]{:S(2)}) collective-permute-start(bf16[2,368,128]{2,1,0:T(8,128)(2,1)} %get-tuple-element.58.refs_0_), channel_id=1, source_target_pairs={{0,4},{1,5},{2,6},{3,7},{4,0},{5,1},{6,2},{7,3},{8,12},{9,13},{10,... | collective-permute-start | bytes 565256 | tf_op jit(solution)/shard_map/ppermute | solution.py:301
  5.4 3.6 %collective-permute-start.1 = (bf16[368,128]{1,0:T(8,128)(2,1)}, bf16[368,128]{1,0:T(8,128)(2,1)S(1)}, u32[]{:S(2)}, u32[]{:S(2)}) collective-permute-start(bf16[368,128]{1,0:T(8,128)(2,1)} %get-tuple-element.53), channel_id=1, source_target_pairs={{0,24},{1,25},{2,26},{3,27},{4,28},{5,29},{6,30},{7,31},{8,16},{9,... | collective-permute-start | bytes 282632 | tf_op jit(solution)/shard_map/ppermute | solution.py:301
  9.0 0.7 %pad_maximum_fusion.5.biases_ref = f32[3,360]{1,0:T(4,128)S(1)} fusion(f32[1,360]{1,0:T(1,128)} %param.19, f32[1,360]{1,0:T(1,128)} %param.17, f32[1,360]{1,0:T(1,128)} %param.15), kind=kLoop, calls=%fused_computation.29 | loop fusion | flops 2160 | bytes 8640 | tf_op jit(solution)/shard_map/concatenate | solution.py:311
  9.7 1.2 %copy-done.2 = bf16[1,360,1440]{2,1,0:T(8,128)(2,1)S(1)} copy-done((bf16[1,360,1440]{2,1,0:T(8,128)(2,1)S(1)}, bf16[1,360,1440]{2,1,0:T(8,128)(2,1)}, u32[]{:S(2)}) %copy-start.2) | copy-done | bytes 1036824
  11.0 0.4 shard_map.102
  11.4 1.0 %pad_maximum_fusion = bf16[4,368,128]{2,1,0:T(8,128)(2,1)S(1)} fusion(bf16[2,368,128]{2,1,0:T(8,128)(2,1)S(1)} %collective-permute-done.5.refs_2_, bf16[2,368,128]{2,1,0:T(8,128)(2,1)} %get-tuple-element.58.refs_0_), kind=kLoop, calls=%fused_computation.1 | loop fusion | flops 188416 | bytes 753664 | tf_op jit(solution)/shard_map/concatenate | solution.py:344
  12.4 0.8 %collective-permute-start.7 = (bf16[4,368,128]{2,1,0:T(8,128)(2,1)S(1)}, bf16[4,368,128]{2,1,0:T(8,128)(2,1)S(1)}, u32[]{:S(2)}, u32[]{:S(2)}) collective-permute-start(bf16[4,368,128]{2,1,0:T(8,128)(2,1)S(1)} %pad_maximum_fusion), channel_id=1, source_target_pairs={{0,8},{1,9},{2,10},{3,11},{4,12},{5,13},{6,14},{7,15},{8,0},{9,1},... | collective-permute-start | bytes 1130504 | tf_op jit(solution)/shard_map/ppermute | solution.py:301
  13.3 0.8 %shard_map.101 = (bf16[768,1536]{1,0:T(8,128)(2,1)S(1)}, f32[768,128]{1,0:T(8,128)S(1)}) custom-call(bf16[1440,360]{1,0:T(8,128)(2,1)S(1)} %bitcast.34, bf16[1440,360]{1,0:T(8,128)(2,1)S(1)} %bitcast.35, f32[3,360]{1,0:T(4,128)S(1)} %pad_maximum_fusion.5.biases_ref), custom_call_target="tpu_custom_call" | custom-call | bytes 8294400 | tf_op jit(solution)/shard_map/pallas_call | solution.py:124
  14.1 2.9 %collective-permute-done = bf16[368,128]{1,0:T(8,128)(2,1)S(1)} collective-permute-done((bf16[368,128]{1,0:T(8,128)(2,1)}, bf16[368,128]{1,0:T(8,128)(2,1)S(1)}, u32[]{:S(2)}, u32[]{:S(2)}) %collective-permute-start) | collective-permute-done | bytes 94240 | tf_op jit(solution)/shard_map/ppermute | solution.py:301
  17.0 1.6 %collective-permute-start.4 = (bf16[2,368,128]{2,1,0:T(8,128)(2,1)S(1)}, bf16[2,368,128]{2,1,0:T(8,128)(2,1)S(1)}, u32[]{:S(2)}, u32[]{:S(2)}) collective-permute-start(bf16[2,368,128]{2,1,0:T(8,128)(2,1)S(1)} %pad_maximum_fusion.1.refs_0_), channel_id=1, source_target_pairs={{0,6},{1,7},{2,4},{3,5},{4,2},{5,3},{6,0},{7,1},{8,14},{9,15},{10,... | collective-permute-start | bytes 565256 | tf_op jit(solution)/shard_map/ppermute | solution.py:301
  18.5 0.5 collective-permute-start.3
  19.0 1.5 %collective-permute-start.2 = (bf16[2,368,128]{2,1,0:T(8,128)(2,1)S(1)}, bf16[2,368,128]{2,1,0:T(8,128)(2,1)S(1)}, u32[]{:S(2)}, u32[]{:S(2)}) collective-permute-start(bf16[2,368,128]{2,1,0:T(8,128)(2,1)S(1)} %pad_maximum_fusion.1.refs_0_), channel_id=1, source_target_pairs={{0,4},{1,5},{2,6},{3,7},{4,0},{5,1},{6,2},{7,3},{8,12},{9,13},{10,... | collective-permute-start | bytes 565256 | tf_op jit(solution)/shard_map/ppermute | solution.py:301
  20.5 1.5 %shard_map.103 = (bf16[4,360,128]{2,1,0:T(8,128)(2,1)S(1)}, bf16[4,360,128]{2,1,0:T(8,128)(2,1)S(1)}) custom-call(bf16[2,368,128]{2,1,0:T(8,128)(2,1)S(1)} %copy-done.3, bf16[2,368,128]{2,1,0:T(8,128)(2,1)S(1)} %copy-done.4, bf16[2,368,128]{2,1,0:T(8,128)(2,1)S(1)} %collective-permute-done.5.refs_2_, ...), custom_call_target="tpu_custom_call" | custom-call | flops 1811939328 | bytes 3538944 | tf_op jit(solution)/shard_map/pallas_call | solution.py:266
  22.0 3.6 %collective-permute-done.4.refs_6_ = bf16[2,368,128]{2,1,0:T(8,128)(2,1)S(1)} collective-permute-done((bf16[2,368,128]{2,1,0:T(8,128)(2,1)S(1)}, bf16[2,368,128]{2,1,0:T(8,128)(2,1)S(1)}, u32[]{:S(2)}, u32[]{:S(2)}) %collective-permute-start.4) | collective-permute-done | bytes 188448 | tf_op jit(solution)/shard_map/ppermute | solution.py:301
  25.6 2.2 %collective-permute-done.3.refs_2_ = bf16[2,368,128]{2,1,0:T(8,128)(2,1)S(1)} collective-permute-done((bf16[2,368,128]{2,1,0:T(8,128)(2,1)S(1)}, bf16[2,368,128]{2,1,0:T(8,128)(2,1)S(1)}, u32[]{:S(2)}, u32[]{:S(2)}) %collective-permute-start.3) | collective-permute-done | bytes 188448 | tf_op jit(solution)/shard_map/ppermute | solution.py:301
  27.8 0.1 collective-permute-done.2.refs_4_
  27.9 0.5 collective-permute-start.9
  28.4 0.5 collective-permute-start.11
  28.9 0.4 collective-permute-done.8.refs_1_
  29.3 0.3 collective-permute-done.9.refs_3_
  29.6 0.3 collective-permute-done.10.refs_5_
  29.9 0.3 collective-permute-done.11.refs_7_
  30.2 1.5 %shard_map.104 = (bf16[4,360,128]{2,1,0:T(8,128)(2,1)S(1)}, bf16[4,360,128]{2,1,0:T(8,128)(2,1)S(1)}) custom-call(bf16[2,368,128]{2,1,0:T(8,128)(2,1)S(1)} %pad_maximum_fusion.1.refs_0_, bf16[2,368,128]{2,1,0:T(8,128)(2,1)S(1)} %collective-permute-done.8.refs_1_, bf16[2,368,128]{2,1,0:T(8,128)(2,1)S(1)} %collective-permute-done.3.refs_2_, ...), custom_call_target="tpu_custom_call" | custom-call | flops 1811939328 | bytes 3538944 | tf_op jit(solution)/shard_map/pallas_call | solution.py:266
  31.6 0.3 collective-permute-start.13
  31.9 0.3 collective-permute-start.12
  32.2 1.5 %shard_map.105 = (bf16[4,360,128]{2,1,0:T(8,128)(2,1)S(1)}, bf16[4,360,128]{2,1,0:T(8,128)(2,1)S(1)}) custom-call(bf16[2,368,128]{2,1,0:T(8,128)(2,1)S(1)} %pad_maximum_fusion.1.refs_0_, bf16[2,368,128]{2,1,0:T(8,128)(2,1)S(1)} %collective-permute-done.8.refs_1_, bf16[2,368,128]{2,1,0:T(8,128)(2,1)S(1)} %collective-permute-done.3.refs_2_, ...), custom_call_target="tpu_custom_call" | custom-call | flops 1811939328 | bytes 3538944 | tf_op jit(solution)/shard_map/pallas_call | solution.py:266
  33.7 0.3 collective-permute-done.12
  33.9 0.2 collective-permute-start.14
  34.2 1.4 %shard_map.106 = (bf16[4,360,128]{2,1,0:T(8,128)(2,1)S(1)}, bf16[4,360,128]{2,1,0:T(8,128)(2,1)S(1)}) custom-call(bf16[4,368,128]{2,1,0:T(8,128)(2,1)S(1)} %collective-permute-done.7.refs_0_, bf16[4,368,128]{2,1,0:T(8,128)(2,1)S(1)} %collective-permute-done.13.refs_1_, bf16[768,1536]{1,0:T(8,128)(2,1)S(1)} %get-tuple-element.63.refs_4_.refs_8_.refs_2_, ...), custom_call_target="tpu_custom_call" | custom-call | flops 1811939328 | bytes 3538944 | tf_op jit(solution)/shard_map/pallas_call | solution.py:266
  35.6 0.3 collective-permute-start.16
  36.0 0.1 add_convert_fusion.10
  36.1 1.5 %collective-permute-start.19 = (bf16[2,360,128]{2,1,0:T(8,128)(2,1)S(1)}, bf16[2,360,128]{2,1,0:T(8,128)(2,1)S(1)}, u32[]{:S(2)}, u32[]{:S(2)}) collective-permute-start(bf16[2,360,128]{2,1,0:T(8,128)(2,1)S(1)} %pad_maximum_fusion.3), channel_id=1, source_target_pairs={{0,6},{1,7},{2,4},{3,5},{4,2},{5,3},{6,0},{7,1},{8,14},{9,15},{10,... | collective-permute-start | bytes 552968 | tf_op jit(solution)/shard_map/ppermute | solution.py:301
  37.6 0.7 %collective-permute-start.20 = (bf16[2,360,128]{2,1,0:T(8,128)(2,1)S(1)}, bf16[2,360,128]{2,1,0:T(8,128)(2,1)S(1)}, u32[]{:S(2)}, u32[]{:S(2)}) collective-permute-start(bf16[2,360,128]{2,1,0:T(8,128)(2,1)S(1)} %pad_maximum_fusion.4), channel_id=1, source_target_pairs={{0,2},{1,3},{2,0},{3,1},{4,6},{5,7},{6,4},{7,5},{8,10},{9,11},{10,... | collective-permute-start | bytes 552968 | tf_op jit(solution)/shard_map/ppermute | solution.py:301
  38.3 1.6 %collective-permute-start.18 = (bf16[2,360,128]{2,1,0:T(8,128)(2,1)S(1)}, bf16[2,360,128]{2,1,0:T(8,128)(2,1)S(1)}, u32[]{:S(2)}, u32[]{:S(2)}) collective-permute-start(bf16[2,360,128]{2,1,0:T(8,128)(2,1)S(1)} %pad_maximum_fusion.2), channel_id=1, source_target_pairs={{0,4},{1,5},{2,6},{3,7},{4,0},{5,1},{6,2},{7,3},{8,12},{9,13},{10,... | collective-permute-start | bytes 552968 | tf_op jit(solution)/shard_map/ppermute | solution.py:301
  39.9 0.1 add_convert_fusion
  40.1 4.5 %collective-permute-done.19 = bf16[2,360,128]{2,1,0:T(8,128)(2,1)S(1)} collective-permute-done((bf16[2,360,128]{2,1,0:T(8,128)(2,1)S(1)}, bf16[2,360,128]{2,1,0:T(8,128)(2,1)S(1)}, u32[]{:S(2)}, u32[]{:S(2)}) %collective-permute-start.19) | collective-permute-done | bytes 184352 | tf_op jit(solution)/shard_map/ppermute | solution.py:301
  44.6 3.2 %collective-permute-done.20 = bf16[2,360,128]{2,1,0:T(8,128)(2,1)S(1)} collective-permute-done((bf16[2,360,128]{2,1,0:T(8,128)(2,1)S(1)}, bf16[2,360,128]{2,1,0:T(8,128)(2,1)S(1)}, u32[]{:S(2)}, u32[]{:S(2)}) %collective-permute-start.20) | collective-permute-done | bytes 184352 | tf_op jit(solution)/shard_map/ppermute | solution.py:301
  47.8 0.1 fusion.8
  48.0 1.0 %collective-permute-start.24 = (bf16[360,128]{1,0:T(8,128)(2,1)S(1)}, bf16[360,128]{1,0:T(8,128)(2,1)S(1)}, u32[]{:S(2)}, u32[]{:S(2)}) collective-permute-start(bf16[360,128]{1,0:T(8,128)(2,1)S(1)} %get-tuple-element.110), channel_id=1, source_target_pairs={{0,16},{1,17},{2,18},{3,19},{4,20},{5,21},{6,22},{7,23},{8,24},{9,... | collective-permute-start | bytes 276488 | tf_op jit(solution)/shard_map/ppermute | solution.py:301
  49.0 1.2 %collective-permute-start.25 = (bf16[360,128]{1,0:T(8,128)(2,1)S(1)}, bf16[360,128]{1,0:T(8,128)(2,1)S(1)}, u32[]{:S(2)}, u32[]{:S(2)}) collective-permute-start(bf16[360,128]{1,0:T(8,128)(2,1)S(1)} %get-tuple-element.111), channel_id=1, source_target_pairs={{0,24},{1,25},{2,26},{3,27},{4,28},{5,29},{6,30},{7,31},{8,16},{9,... | collective-permute-start | bytes 276488 | tf_op jit(solution)/shard_map/ppermute | solution.py:301
  50.1 0.1 fusion.5
  50.3 0.6 %collective-permute-start.21 = (bf16[360,128]{1,0:T(8,128)(2,1)S(1)}, bf16[360,128]{1,0:T(8,128)(2,1)S(1)}, u32[]{:S(2)}, u32[]{:S(2)}) collective-permute-start(bf16[360,128]{1,0:T(8,128)(2,1)S(1)} %get-tuple-element.101), channel_id=1, source_target_pairs={{0,4},{1,5},{2,6},{3,7},{4,0},{5,1},{6,2},{7,3},{8,12},{9,13},{10,... | collective-permute-start | bytes 276488 | tf_op jit(solution)/shard_map/ppermute | solution.py:301
  50.9 1.4 %collective-permute-start.23 = (bf16[360,128]{1,0:T(8,128)(2,1)S(1)}, bf16[360,128]{1,0:T(8,128)(2,1)S(1)}, u32[]{:S(2)}, u32[]{:S(2)}) collective-permute-start(bf16[360,128]{1,0:T(8,128)(2,1)S(1)} %get-tuple-element.102), channel_id=1, source_target_pairs={{0,2},{1,3},{2,0},{3,1},{4,6},{5,7},{6,4},{7,5},{8,10},{9,11},{10,... | collective-permute-start | bytes 276488 | tf_op jit(solution)/shard_map/ppermute | solution.py:301
  52.3 1.5 %collective-permute-start.22 = (bf16[360,128]{1,0:T(8,128)(2,1)S(1)}, bf16[360,128]{1,0:T(8,128)(2,1)S(1)}, u32[]{:S(2)}, u32[]{:S(2)}) collective-permute-start(bf16[360,128]{1,0:T(8,128)(2,1)S(1)} %get-tuple-element.103), channel_id=1, source_target_pairs={{0,6},{1,7},{2,4},{3,5},{4,2},{5,3},{6,0},{7,1},{8,14},{9,15},{10,... | collective-permute-start | bytes 276488 | tf_op jit(solution)/shard_map/ppermute | solution.py:301
  53.8 3.1 %collective-permute-done.24 = bf16[360,128]{1,0:T(8,128)(2,1)S(1)} collective-permute-done((bf16[360,128]{1,0:T(8,128)(2,1)S(1)}, bf16[360,128]{1,0:T(8,128)(2,1)S(1)}, u32[]{:S(2)}, u32[]{:S(2)}) %collective-permute-start.24) | collective-permute-done | bytes 92192 | tf_op jit(solution)/shard_map/ppermute | solution.py:301
  57.0 0.8 %collective-permute-done.22 = bf16[360,128]{1,0:T(8,128)(2,1)S(1)} collective-permute-done((bf16[360,128]{1,0:T(8,128)(2,1)S(1)}, bf16[360,128]{1,0:T(8,128)(2,1)S(1)}, u32[]{:S(2)}, u32[]{:S(2)}) %collective-permute-start.22) | collective-permute-done | bytes 92192 | tf_op jit(solution)/shard_map/ppermute | solution.py:301
  57.8 0.8 %fusion.10 = bf16[128,360]{0,1:T(8,128)(2,1)} fusion(bf16[360,128]{1,0:T(8,128)(2,1)S(1)} %collective-permute-done.25, bf16[360,128]{1,0:T(8,128)(2,1)S(1)} %collective-permute-done.24, bf16[360,128]{1,0:T(8,128)(2,1)S(1)} %collective-permute-done.23, bf16[360,128]{1,0:T(8,128)(2,1)S(1)} %collective-permute-done.22, ...), kind=kLoop, calls=%fused_computation.28 | loop fusion | flops 737280 | bytes 829440 | tf_op jit(solution)/shard_map/transpose | solution.py:379
  (33 shorter events, 0.4 us)
Async XLA Ops:
  0.0 13.2 %copy-start = (bf16[1,1440,360]{2,1,0:T(8,128)(2,1)S(1)}, bf16[1,1440,360]{2,1,0:T(8,128)(2,1)}, u32[]{:S(2)}) copy-start(bf16[1,1440,360]{2,1,0:T(8,128)(2,1)} %param.14) | copy-start | bytes 3110404
  0.0 13.2 %copy-start.1 = (bf16[1,1440,360]{2,1,0:T(8,128)(2,1)S(1)}, bf16[1,1440,360]{2,1,0:T(8,128)(2,1)}, u32[]{:S(2)}) copy-start(bf16[1,1440,360]{2,1,0:T(8,128)(2,1)} %param.16) | copy-start | bytes 3110404
  2.4 9.0 %collective-permute-start.5 = (bf16[2,368,128]{2,1,0:T(8,128)(2,1)}, bf16[2,368,128]{2,1,0:T(8,128)(2,1)S(1)}, u32[]{:S(2)}, u32[]{:S(2)}) collective-permute-start(bf16[2,368,128]{2,1,0:T(8,128)(2,1)} %get-tuple-element.58.refs_0_), channel_id=1, source_target_pairs={{0,4},{1,5},{2,6},{3,7},{4,0},{5,1},{6,2},{7,3},{8,12},{9,13},{10,... | collective-permute-start | bytes 565256 | tf_op jit(solution)/shard_map/ppermute | solution.py:301
  5.4 8.7 %collective-permute-start.1 = (bf16[368,128]{1,0:T(8,128)(2,1)}, bf16[368,128]{1,0:T(8,128)(2,1)S(1)}, u32[]{:S(2)}, u32[]{:S(2)}) collective-permute-start(bf16[368,128]{1,0:T(8,128)(2,1)} %get-tuple-element.53), channel_id=1, source_target_pairs={{0,24},{1,25},{2,26},{3,27},{4,28},{5,29},{6,30},{7,31},{8,16},{9,... | collective-permute-start | bytes 282632 | tf_op jit(solution)/shard_map/ppermute | solution.py:301
  9.0 8.0 %collective-permute-start = (bf16[368,128]{1,0:T(8,128)(2,1)}, bf16[368,128]{1,0:T(8,128)(2,1)S(1)}, u32[]{:S(2)}, u32[]{:S(2)}) collective-permute-start(bf16[368,128]{1,0:T(8,128)(2,1)} %get-tuple-element.53), channel_id=1, source_target_pairs={{0,16},{1,17},{2,18},{3,19},{4,20},{5,21},{6,22},{7,23},{8,24},{9,... | collective-permute-start | bytes 282632 | tf_op jit(solution)/shard_map/ppermute | solution.py:301
  9.7 1.2 %copy-start.2 = (bf16[1,360,1440]{2,1,0:T(8,128)(2,1)S(1)}, bf16[1,360,1440]{2,1,0:T(8,128)(2,1)}, u32[]{:S(2)}) copy-start(bf16[1,360,1440]{2,1,0:T(8,128)(2,1)} %param.18) | copy-start | bytes 3110404
  12.4 15.5 %collective-permute-start.7 = (bf16[4,368,128]{2,1,0:T(8,128)(2,1)S(1)}, bf16[4,368,128]{2,1,0:T(8,128)(2,1)S(1)}, u32[]{:S(2)}, u32[]{:S(2)}) collective-permute-start(bf16[4,368,128]{2,1,0:T(8,128)(2,1)S(1)} %pad_maximum_fusion), channel_id=1, source_target_pairs={{0,8},{1,9},{2,10},{3,11},{4,12},{5,13},{6,14},{7,15},{8,0},{9,1},... | collective-permute-start | bytes 1130504 | tf_op jit(solution)/shard_map/ppermute | solution.py:301
  13.2 7.3 %collective-permute-start.6 = (bf16[2,368,128]{2,1,0:T(8,128)(2,1)S(1)}, bf16[2,368,128]{2,1,0:T(8,128)(2,1)S(1)}, u32[]{:S(2)}, u32[]{:S(2)}) collective-permute-start(bf16[2,368,128]{2,1,0:T(8,128)(2,1)S(1)} %collective-permute-done.5.refs_2_), channel_id=1, source_target_pairs={{0,1},{1,0},{2,3},{3,2},{4,5},{5,4},{6,7},{7,6},{8,9},{9,8},{10,11... | collective-permute-start | bytes 565256 | tf_op jit(solution)/shard_map/ppermute | solution.py:301
  13.2 7.3 %copy-start.3 = (bf16[2,368,128]{2,1,0:T(8,128)(2,1)S(1)}, bf16[2,368,128]{2,1,0:T(8,128)(2,1)}, u32[]{:S(2)}) copy-start(bf16[2,368,128]{2,1,0:T(8,128)(2,1)} %get-tuple-element.58.refs_0_) | copy-start | bytes 565252
  13.2 7.3 %copy-start.4 = (bf16[2,368,128]{2,1,0:T(8,128)(2,1)S(1)}, bf16[2,368,128]{2,1,0:T(8,128)(2,1)}, u32[]{:S(2)}) copy-start(bf16[2,368,128]{2,1,0:T(8,128)(2,1)} %get-tuple-element.59.refs_1_) | copy-start | bytes 565252
  17.0 8.7 %collective-permute-start.4 = (bf16[2,368,128]{2,1,0:T(8,128)(2,1)S(1)}, bf16[2,368,128]{2,1,0:T(8,128)(2,1)S(1)}, u32[]{:S(2)}, u32[]{:S(2)}) collective-permute-start(bf16[2,368,128]{2,1,0:T(8,128)(2,1)S(1)} %pad_maximum_fusion.1.refs_0_), channel_id=1, source_target_pairs={{0,6},{1,7},{2,4},{3,5},{4,2},{5,3},{6,0},{7,1},{8,14},{9,15},{10,... | collective-permute-start | bytes 565256 | tf_op jit(solution)/shard_map/ppermute | solution.py:301
  18.5 9.3 %collective-permute-start.3 = (bf16[2,368,128]{2,1,0:T(8,128)(2,1)S(1)}, bf16[2,368,128]{2,1,0:T(8,128)(2,1)S(1)}, u32[]{:S(2)}, u32[]{:S(2)}) collective-permute-start(bf16[2,368,128]{2,1,0:T(8,128)(2,1)S(1)} %pad_maximum_fusion.1.refs_0_), channel_id=1, source_target_pairs={{0,2},{1,3},{2,0},{3,1},{4,6},{5,7},{6,4},{7,5},{8,10},{9,11},{10,... | collective-permute-start | bytes 565256 | tf_op jit(solution)/shard_map/ppermute | solution.py:301
  19.0 8.9 %collective-permute-start.2 = (bf16[2,368,128]{2,1,0:T(8,128)(2,1)S(1)}, bf16[2,368,128]{2,1,0:T(8,128)(2,1)S(1)}, u32[]{:S(2)}, u32[]{:S(2)}) collective-permute-start(bf16[2,368,128]{2,1,0:T(8,128)(2,1)S(1)} %pad_maximum_fusion.1.refs_0_), channel_id=1, source_target_pairs={{0,4},{1,5},{2,6},{3,7},{4,0},{5,1},{6,2},{7,3},{8,12},{9,13},{10,... | collective-permute-start | bytes 565256 | tf_op jit(solution)/shard_map/ppermute | solution.py:301
  27.9 1.4 %collective-permute-start.8 = (bf16[2,368,128]{2,1,0:T(8,128)(2,1)S(1)}, bf16[2,368,128]{2,1,0:T(8,128)(2,1)S(1)}, u32[]{:S(2)}, u32[]{:S(2)}) collective-permute-start(bf16[2,368,128]{2,1,0:T(8,128)(2,1)S(1)} %pad_maximum_fusion.1.refs_0_), channel_id=1, source_target_pairs={{0,1},{1,0},{2,3},{3,2},{4,5},{5,4},{6,7},{7,6},{8,9},{9,8},{10,11... | collective-permute-start | bytes 565256 | tf_op jit(solution)/shard_map/ppermute | solution.py:301
  27.9 1.7 %collective-permute-start.9 = (bf16[2,368,128]{2,1,0:T(8,128)(2,1)S(1)}, bf16[2,368,128]{2,1,0:T(8,128)(2,1)S(1)}, u32[]{:S(2)}, u32[]{:S(2)}) collective-permute-start(bf16[2,368,128]{2,1,0:T(8,128)(2,1)S(1)} %collective-permute-done.3.refs_2_), channel_id=1, source_target_pairs={{0,1},{1,0},{2,3},{3,2},{4,5},{5,4},{6,7},{7,6},{8,9},{9,8},{10,11... | collective-permute-start | bytes 565256 | tf_op jit(solution)/shard_map/ppermute | solution.py:301
  28.4 1.5 %collective-permute-start.10 = (bf16[2,368,128]{2,1,0:T(8,128)(2,1)S(1)}, bf16[2,368,128]{2,1,0:T(8,128)(2,1)S(1)}, u32[]{:S(2)}, u32[]{:S(2)}) collective-permute-start(bf16[2,368,128]{2,1,0:T(8,128)(2,1)S(1)} %collective-permute-done.2.refs_4_), channel_id=1, source_target_pairs={{0,1},{1,0},{2,3},{3,2},{4,5},{5,4},{6,7},{7,6},{8,9},{9,8},{10,11... | collective-permute-start | bytes 565256 | tf_op jit(solution)/shard_map/ppermute | solution.py:301
  28.4 1.7 %collective-permute-start.11 = (bf16[2,368,128]{2,1,0:T(8,128)(2,1)S(1)}, bf16[2,368,128]{2,1,0:T(8,128)(2,1)S(1)}, u32[]{:S(2)}, u32[]{:S(2)}) collective-permute-start(bf16[2,368,128]{2,1,0:T(8,128)(2,1)S(1)} %collective-permute-done.4.refs_6_), channel_id=1, source_target_pairs={{0,1},{1,0},{2,3},{3,2},{4,5},{5,4},{6,7},{7,6},{8,9},{9,8},{10,11... | collective-permute-start | bytes 565256 | tf_op jit(solution)/shard_map/ppermute | solution.py:301
  31.6 2.3 %collective-permute-start.13 = (bf16[4,368,128]{2,1,0:T(8,128)(2,1)S(1)}, bf16[4,368,128]{2,1,0:T(8,128)(2,1)S(1)}, u32[]{:S(2)}, u32[]{:S(2)}) collective-permute-start(bf16[4,368,128]{2,1,0:T(8,128)(2,1)S(1)} %collective-permute-done.7.refs_0_), channel_id=1, source_target_pairs={{0,1},{1,0},{2,3},{3,2},{4,5},{5,4},{6,7},{7,6},{8,9},{9,8},{10,11... | collective-permute-start | bytes 1130504 | tf_op jit(solution)/shard_map/ppermute | solution.py:301
  31.9 2.0 %collective-permute-start.12 = (bf16[4,360,128]{2,1,0:T(8,128)(2,1)S(1)}, bf16[4,360,128]{2,1,0:T(8,128)(2,1)S(1)}, u32[]{:S(2)}, u32[]{:S(2)}) collective-permute-start(bf16[4,360,128]{2,1,0:T(8,128)(2,1)S(1)} %get-tuple-element.74), channel_id=1, source_target_pairs={{0,1},{1,0},{2,3},{3,2},{4,5},{5,4},{6,7},{7,6},{8,9},{9,8},{10,11... | collective-permute-start | bytes 1105928 | tf_op jit(solution)/shard_map/ppermute | solution.py:301
  33.9 2.1 %collective-permute-start.14 = (bf16[4,360,128]{2,1,0:T(8,128)(2,1)S(1)}, bf16[4,360,128]{2,1,0:T(8,128)(2,1)S(1)}, u32[]{:S(2)}, u32[]{:S(2)}) collective-permute-start(bf16[4,360,128]{2,1,0:T(8,128)(2,1)S(1)} %get-tuple-element.91), channel_id=1, source_target_pairs={{0,1},{1,0},{2,3},{3,2},{4,5},{5,4},{6,7},{7,6},{8,9},{9,8},{10,11... | collective-permute-start | bytes 1105928 | tf_op jit(solution)/shard_map/ppermute | solution.py:301
  35.6 4.3 %collective-permute-start.16 = (bf16[4,360,128]{2,1,0:T(8,128)(2,1)S(1)}, bf16[4,360,128]{2,1,0:T(8,128)(2,1)S(1)}, u32[]{:S(2)}, u32[]{:S(2)}) collective-permute-start(bf16[4,360,128]{2,1,0:T(8,128)(2,1)S(1)} %get-tuple-element.95), channel_id=1, source_target_pairs={{0,1},{1,0},{2,3},{3,2},{4,5},{5,4},{6,7},{7,6},{8,9},{9,8},{10,11... | collective-permute-start | bytes 1105928 | tf_op jit(solution)/shard_map/ppermute | solution.py:301
  36.1 8.5 %collective-permute-start.19 = (bf16[2,360,128]{2,1,0:T(8,128)(2,1)S(1)}, bf16[2,360,128]{2,1,0:T(8,128)(2,1)S(1)}, u32[]{:S(2)}, u32[]{:S(2)}) collective-permute-start(bf16[2,360,128]{2,1,0:T(8,128)(2,1)S(1)} %pad_maximum_fusion.3), channel_id=1, source_target_pairs={{0,6},{1,7},{2,4},{3,5},{4,2},{5,3},{6,0},{7,1},{8,14},{9,15},{10,... | collective-permute-start | bytes 552968 | tf_op jit(solution)/shard_map/ppermute | solution.py:301
  37.6 10.2 %collective-permute-start.20 = (bf16[2,360,128]{2,1,0:T(8,128)(2,1)S(1)}, bf16[2,360,128]{2,1,0:T(8,128)(2,1)S(1)}, u32[]{:S(2)}, u32[]{:S(2)}) collective-permute-start(bf16[2,360,128]{2,1,0:T(8,128)(2,1)S(1)} %pad_maximum_fusion.4), channel_id=1, source_target_pairs={{0,2},{1,3},{2,0},{3,1},{4,6},{5,7},{6,4},{7,5},{8,10},{9,11},{10,... | collective-permute-start | bytes 552968 | tf_op jit(solution)/shard_map/ppermute | solution.py:301
  38.3 9.5 %collective-permute-start.18 = (bf16[2,360,128]{2,1,0:T(8,128)(2,1)S(1)}, bf16[2,360,128]{2,1,0:T(8,128)(2,1)S(1)}, u32[]{:S(2)}, u32[]{:S(2)}) collective-permute-start(bf16[2,360,128]{2,1,0:T(8,128)(2,1)S(1)} %pad_maximum_fusion.2), channel_id=1, source_target_pairs={{0,4},{1,5},{2,6},{3,7},{4,0},{5,1},{6,2},{7,3},{8,12},{9,13},{10,... | collective-permute-start | bytes 552968 | tf_op jit(solution)/shard_map/ppermute | solution.py:301
  40.0 10.2 %collective-permute-start.17 = (bf16[4,360,128]{2,1,0:T(8,128)(2,1)S(1)}, bf16[4,360,128]{2,1,0:T(8,128)(2,1)S(1)}, u32[]{:S(2)}, u32[]{:S(2)}) collective-permute-start(bf16[4,360,128]{2,1,0:T(8,128)(2,1)S(1)} %add_convert_fusion), channel_id=1, source_target_pairs={{0,8},{1,9},{2,10},{3,11},{4,12},{5,13},{6,14},{7,15},{8,0},{9,1},... | collective-permute-start | bytes 1105928 | tf_op jit(solution)/shard_map/ppermute | solution.py:301
  40.1 10.1 %collective-permute-start.15 = (bf16[4,360,128]{2,1,0:T(8,128)(2,1)S(1)}, bf16[4,360,128]{2,1,0:T(8,128)(2,1)S(1)}, u32[]{:S(2)}, u32[]{:S(2)}) collective-permute-start(bf16[4,360,128]{2,1,0:T(8,128)(2,1)S(1)} %get-tuple-element.93), channel_id=1, source_target_pairs={{0,1},{1,0},{2,3},{3,2},{4,5},{5,4},{6,7},{7,6},{8,9},{9,8},{10,11... | collective-permute-start | bytes 1105928 | tf_op jit(solution)/shard_map/ppermute | solution.py:301
  48.0 9.0 %collective-permute-start.24 = (bf16[360,128]{1,0:T(8,128)(2,1)S(1)}, bf16[360,128]{1,0:T(8,128)(2,1)S(1)}, u32[]{:S(2)}, u32[]{:S(2)}) collective-permute-start(bf16[360,128]{1,0:T(8,128)(2,1)S(1)} %get-tuple-element.110), channel_id=1, source_target_pairs={{0,16},{1,17},{2,18},{3,19},{4,20},{5,21},{6,22},{7,23},{8,24},{9,... | collective-permute-start | bytes 276488 | tf_op jit(solution)/shard_map/ppermute | solution.py:301
  49.0 8.0 %collective-permute-start.25 = (bf16[360,128]{1,0:T(8,128)(2,1)S(1)}, bf16[360,128]{1,0:T(8,128)(2,1)S(1)}, u32[]{:S(2)}, u32[]{:S(2)}) collective-permute-start(bf16[360,128]{1,0:T(8,128)(2,1)S(1)} %get-tuple-element.111), channel_id=1, source_target_pairs={{0,24},{1,25},{2,26},{3,27},{4,28},{5,29},{6,30},{7,31},{8,16},{9,... | collective-permute-start | bytes 276488 | tf_op jit(solution)/shard_map/ppermute | solution.py:301
  50.3 6.7 %collective-permute-start.21 = (bf16[360,128]{1,0:T(8,128)(2,1)S(1)}, bf16[360,128]{1,0:T(8,128)(2,1)S(1)}, u32[]{:S(2)}, u32[]{:S(2)}) collective-permute-start(bf16[360,128]{1,0:T(8,128)(2,1)S(1)} %get-tuple-element.101), channel_id=1, source_target_pairs={{0,4},{1,5},{2,6},{3,7},{4,0},{5,1},{6,2},{7,3},{8,12},{9,13},{10,... | collective-permute-start | bytes 276488 | tf_op jit(solution)/shard_map/ppermute | solution.py:301
  50.9 6.1 %collective-permute-start.23 = (bf16[360,128]{1,0:T(8,128)(2,1)S(1)}, bf16[360,128]{1,0:T(8,128)(2,1)S(1)}, u32[]{:S(2)}, u32[]{:S(2)}) collective-permute-start(bf16[360,128]{1,0:T(8,128)(2,1)S(1)} %get-tuple-element.102), channel_id=1, source_target_pairs={{0,2},{1,3},{2,0},{3,1},{4,6},{5,7},{6,4},{7,5},{8,10},{9,11},{10,... | collective-permute-start | bytes 276488 | tf_op jit(solution)/shard_map/ppermute | solution.py:301
  52.3 5.5 %collective-permute-start.22 = (bf16[360,128]{1,0:T(8,128)(2,1)S(1)}, bf16[360,128]{1,0:T(8,128)(2,1)S(1)}, u32[]{:S(2)}, u32[]{:S(2)}) collective-permute-start(bf16[360,128]{1,0:T(8,128)(2,1)S(1)} %get-tuple-element.103), channel_id=1, source_target_pairs={{0,6},{1,7},{2,4},{3,5},{4,2},{5,3},{6,0},{7,1},{8,14},{9,15},{10,... | collective-permute-start | bytes 276488 | tf_op jit(solution)/shard_map/ppermute | solution.py:301

commit v19 on v18

--- a/solution.py
+++ b/solution.py
@@ -234,7 +234,7 @@
                 at, index = blocks[half * count + j][k]
                 values = arrays[at][index]
                 rows_ref[at_row, j * lanes : (j + 1) * lanes] = values
-                terms = values.astype(jnp.float32)[quarter:]
+                terms = values[quarter // 16 * 16 :].astype(jnp.float32)[quarter % 16 :]
                 shares[j] += jnp.sum(jnp.where(mine, terms, 0.0), axis=0, keepdims=True)
         wide = jnp.concatenate(shares, axis=1)
         activated = []

time: 58.7 us -> 58.7 us (level)
  no operation moved by 1% of the time
where the time goes in v19:
time: 58.7 us; the launch traced here: 58.5 us
  starting transfers between devices  22.7 us (39%)
  waiting for transfers between devices  21.9 us (37%)
  Pallas kernels  9.4 us (16%)
  other arithmetic  3.02 us (5%)
  local copies, waits for them, and re-layouts  1.26 us (2%)
    ppermute x26, starting transfers between devices, swap(): lax.ppermute(array, ('seq', 'rep'), [(i, i ^ step) for i in range(devices)])  22.7 us
    ppermute x26, waiting for transfers between devices, swap(): lax.ppermute(array, ('seq', 'rep'), [(i, i ^ step) for i in range(devices)])  21.9 us
    pallas_call x4, Pallas kernels, run_expert(): pl.pallas_call(functools.partial(expert_kernel, quarter, per, blocks, slo...  5.81 us
    pallas_call x1, Pallas kernels, make_pieces(): pl.pallas_call(functools.partial(pieces_kernel, groups, per, experts), in...  2.35 us
    unnamed x10, local copies, waits for them, and re-layouts  1.26 us
    pallas_call x2, Pallas kernels, arrange(): pl.pallas_call(functools.partial(kernel, groups), out_shape=[jax.ShapeDty...  1.23 us
  transfers between devices with their start and end apart: 26, of which 13 were waited for; matrix products, arithmetic and copies ran while one was open for 4% of the time, Pallas kernels for 10%

profile of v19, /device:TPU:0, one launch (start us, length us, event | category | flops | bytes accessed | tf_op | source)
XLA Modules:
  0.0 58.5 jit_solution(15499595509242008434)
XLA Ops:
  0.0 2.4 %shard_map.100 = (bf16[368,128]{1,0:T(8,128)(2,1)}, bf16[2,368,128]{2,1,0:T(8,128)(2,1)}, bf16[2,368,128]{2,1,0:T(8,128)(2,1)}) custom-call(bf16[1440,128]{1,0:T(8,128)(2,1)} %bitcast.37, f32[1440]{0:T(1024)} %refs_1_.1, s32[4,128]{1,0:T(4,128)} %bitcast.40, f32[4,128]{1,0:T(4,128)} %bitcast.41), custom_call_target="tpu_custom_call" | custom-call | tf_op jit(solution)/shard_map/pallas_call | solution.py:196
  2.4 3.0 %collective-permute-start.5 = (bf16[2,368,128]{2,1,0:T(8,128)(2,1)}, bf16[2,368,128]{2,1,0:T(8,128)(2,1)S(1)}, u32[]{:S(2)}, u32[]{:S(2)}) collective-permute-start(bf16[2,368,128]{2,1,0:T(8,128)(2,1)} %get-tuple-element.58.refs_0_), channel_id=1, source_target_pairs={{0,4},{1,5},{2,6},{3,7},{4,0},{5,1},{6,2},{7,3},{8,12},{9,13},{10,... | collective-permute-start | bytes 565256 | tf_op jit(solution)/shard_map/ppermute | solution.py:301
  5.4 3.6 %collective-permute-start.1 = (bf16[368,128]{1,0:T(8,128)(2,1)}, bf16[368,128]{1,0:T(8,128)(2,1)S(1)}, u32[]{:S(2)}, u32[]{:S(2)}) collective-permute-start(bf16[368,128]{1,0:T(8,128)(2,1)} %get-tuple-element.53), channel_id=1, source_target_pairs={{0,24},{1,25},{2,26},{3,27},{4,28},{5,29},{6,30},{7,31},{8,16},{9,... | collective-permute-start | bytes 282632 | tf_op jit(solution)/shard_map/ppermute | solution.py:301
  9.0 0.7 %pad_maximum_fusion.5.biases_ref = f32[3,360]{1,0:T(4,128)S(1)} fusion(f32[1,360]{1,0:T(1,128)} %param.19, f32[1,360]{1,0:T(1,128)} %param.17, f32[1,360]{1,0:T(1,128)} %param.15), kind=kLoop, calls=%fused_computation.29 | loop fusion | flops 2160 | bytes 8640 | tf_op jit(solution)/shard_map/concatenate | solution.py:311
  9.7 1.2 %copy-done.2 = bf16[1,360,1440]{2,1,0:T(8,128)(2,1)S(1)} copy-done((bf16[1,360,1440]{2,1,0:T(8,128)(2,1)S(1)}, bf16[1,360,1440]{2,1,0:T(8,128)(2,1)}, u32[]{:S(2)}) %copy-start.2) | copy-done | bytes 1036824
  11.0 0.4 shard_map.102
  11.4 1.0 %pad_maximum_fusion = bf16[4,368,128]{2,1,0:T(8,128)(2,1)S(1)} fusion(bf16[2,368,128]{2,1,0:T(8,128)(2,1)S(1)} %collective-permute-done.5.refs_2_, bf16[2,368,128]{2,1,0:T(8,128)(2,1)} %get-tuple-element.58.refs_0_), kind=kLoop, calls=%fused_computation.1 | loop fusion | flops 188416 | bytes 753664 | tf_op jit(solution)/shard_map/concatenate | solution.py:344
  12.4 0.8 %collective-permute-start.7 = (bf16[4,368,128]{2,1,0:T(8,128)(2,1)S(1)}, bf16[4,368,128]{2,1,0:T(8,128)(2,1)S(1)}, u32[]{:S(2)}, u32[]{:S(2)}) collective-permute-start(bf16[4,368,128]{2,1,0:T(8,128)(2,1)S(1)} %pad_maximum_fusion), channel_id=1, source_target_pairs={{0,8},{1,9},{2,10},{3,11},{4,12},{5,13},{6,14},{7,15},{8,0},{9,1},... | collective-permute-start | bytes 1130504 | tf_op jit(solution)/shard_map/ppermute | solution.py:301
  13.3 0.8 %shard_map.101 = (bf16[768,1536]{1,0:T(8,128)(2,1)S(1)}, f32[768,128]{1,0:T(8,128)S(1)}) custom-call(bf16[1440,360]{1,0:T(8,128)(2,1)S(1)} %bitcast.34, bf16[1440,360]{1,0:T(8,128)(2,1)S(1)} %bitcast.35, f32[3,360]{1,0:T(4,128)S(1)} %pad_maximum_fusion.5.biases_ref), custom_call_target="tpu_custom_call" | custom-call | bytes 8294400 | tf_op jit(solution)/shard_map/pallas_call | solution.py:124
  14.1 2.9 %collective-permute-done = bf16[368,128]{1,0:T(8,128)(2,1)S(1)} collective-permute-done((bf16[368,128]{1,0:T(8,128)(2,1)}, bf16[368,128]{1,0:T(8,128)(2,1)S(1)}, u32[]{:S(2)}, u32[]{:S(2)}) %collective-permute-start) | collective-permute-done | bytes 94240 | tf_op jit(solution)/shard_map/ppermute | solution.py:301
  17.0 1.6 %collective-permute-start.4 = (bf16[2,368,128]{2,1,0:T(8,128)(2,1)S(1)}, bf16[2,368,128]{2,1,0:T(8,128)(2,1)S(1)}, u32[]{:S(2)}, u32[]{:S(2)}) collective-permute-start(bf16[2,368,128]{2,1,0:T(8,128)(2,1)S(1)} %pad_maximum_fusion.1.refs_0_), channel_id=1, source_target_pairs={{0,6},{1,7},{2,4},{3,5},{4,2},{5,3},{6,0},{7,1},{8,14},{9,15},{10,... | collective-permute-start | bytes 565256 | tf_op jit(solution)/shard_map/ppermute | solution.py:301
  18.5 0.5 collective-permute-start.3
  19.0 1.5 %collective-permute-start.2 = (bf16[2,368,128]{2,1,0:T(8,128)(2,1)S(1)}, bf16[2,368,128]{2,1,0:T(8,128)(2,1)S(1)}, u32[]{:S(2)}, u32[]{:S(2)}) collective-permute-start(bf16[2,368,128]{2,1,0:T(8,128)(2,1)S(1)} %pad_maximum_fusion.1.refs_0_), channel_id=1, source_target_pairs={{0,4},{1,5},{2,6},{3,7},{4,0},{5,1},{6,2},{7,3},{8,12},{9,13},{10,... | collective-permute-start | bytes 565256 | tf_op jit(solution)/shard_map/ppermute | solution.py:301
  20.5 1.5 %shard_map.103 = (bf16[4,360,128]{2,1,0:T(8,128)(2,1)S(1)}, bf16[4,360,128]{2,1,0:T(8,128)(2,1)S(1)}) custom-call(bf16[2,368,128]{2,1,0:T(8,128)(2,1)S(1)} %copy-done.3, bf16[2,368,128]{2,1,0:T(8,128)(2,1)S(1)} %copy-done.4, bf16[2,368,128]{2,1,0:T(8,128)(2,1)S(1)} %collective-permute-done.5.refs_2_, ...), custom_call_target="tpu_custom_call" | custom-call | flops 1811939328 | bytes 3538944 | tf_op jit(solution)/shard_map/pallas_call | solution.py:266
  22.0 3.6 %collective-permute-done.4.refs_6_ = bf16[2,368,128]{2,1,0:T(8,128)(2,1)S(1)} collective-permute-done((bf16[2,368,128]{2,1,0:T(8,128)(2,1)S(1)}, bf16[2,368,128]{2,1,0:T(8,128)(2,1)S(1)}, u32[]{:S(2)}, u32[]{:S(2)}) %collective-permute-start.4) | collective-permute-done | bytes 188448 | tf_op jit(solution)/shard_map/ppermute | solution.py:301
  25.6 2.2 %collective-permute-done.3.refs_2_ = bf16[2,368,128]{2,1,0:T(8,128)(2,1)S(1)} collective-permute-done((bf16[2,368,128]{2,1,0:T(8,128)(2,1)S(1)}, bf16[2,368,128]{2,1,0:T(8,128)(2,1)S(1)}, u32[]{:S(2)}, u32[]{:S(2)}) %collective-permute-start.3) | collective-permute-done | bytes 188448 | tf_op jit(solution)/shard_map/ppermute | solution.py:301
  27.8 0.1 collective-permute-done.2.refs_4_
  27.9 0.5 collective-permute-start.9
  28.4 0.5 collective-permute-start.11
  28.9 0.4 collective-permute-done.8.refs_1_
  29.3 0.3 collective-permute-done.9.refs_3_
  29.6 0.3 collective-permute-done.10.refs_5_
  29.9 0.3 collective-permute-done.11.refs_7_
  30.2 1.5 %shard_map.104 = (bf16[4,360,128]{2,1,0:T(8,128)(2,1)S(1)}, bf16[4,360,128]{2,1,0:T(8,128)(2,1)S(1)}) custom-call(bf16[2,368,128]{2,1,0:T(8,128)(2,1)S(1)} %pad_maximum_fusion.1.refs_0_, bf16[2,368,128]{2,1,0:T(8,128)(2,1)S(1)} %collective-permute-done.8.refs_1_, bf16[2,368,128]{2,1,0:T(8,128)(2,1)S(1)} %collective-permute-done.3.refs_2_, ...), custom_call_target="tpu_custom_call" | custom-call | flops 1811939328 | bytes 3538944 | tf_op jit(solution)/shard_map/pallas_call | solution.py:266
  31.6 0.3 collective-permute-start.13
  31.9 0.3 collective-permute-start.12
  32.2 1.5 %shard_map.105 = (bf16[4,360,128]{2,1,0:T(8,128)(2,1)S(1)}, bf16[4,360,128]{2,1,0:T(8,128)(2,1)S(1)}) custom-call(bf16[2,368,128]{2,1,0:T(8,128)(2,1)S(1)} %pad_maximum_fusion.1.refs_0_, bf16[2,368,128]{2,1,0:T(8,128)(2,1)S(1)} %collective-permute-done.8.refs_1_, bf16[2,368,128]{2,1,0:T(8,128)(2,1)S(1)} %collective-permute-done.3.refs_2_, ...), custom_call_target="tpu_custom_call" | custom-call | flops 1811939328 | bytes 3538944 | tf_op jit(solution)/shard_map/pallas_call | solution.py:266
  33.7 0.3 collective-permute-done.12
  33.9 0.2 collective-permute-start.14
  34.2 1.4 %shard_map.106 = (bf16[4,360,128]{2,1,0:T(8,128)(2,1)S(1)}, bf16[4,360,128]{2,1,0:T(8,128)(2,1)S(1)}) custom-call(bf16[4,368,128]{2,1,0:T(8,128)(2,1)S(1)} %collective-permute-done.7.refs_0_, bf16[4,368,128]{2,1,0:T(8,128)(2,1)S(1)} %collective-permute-done.13.refs_1_, bf16[768,1536]{1,0:T(8,128)(2,1)S(1)} %get-tuple-element.63.refs_4_.refs_8_.refs_2_, ...), custom_call_target="tpu_custom_call" | custom-call | flops 1811939328 | bytes 3538944 | tf_op jit(solution)/shard_map/pallas_call | solution.py:266
  35.6 0.3 collective-permute-start.16
  36.0 0.1 add_convert_fusion.10
  36.1 1.5 %collective-permute-start.19 = (bf16[2,360,128]{2,1,0:T(8,128)(2,1)S(1)}, bf16[2,360,128]{2,1,0:T(8,128)(2,1)S(1)}, u32[]{:S(2)}, u32[]{:S(2)}) collective-permute-start(bf16[2,360,128]{2,1,0:T(8,128)(2,1)S(1)} %pad_maximum_fusion.3), channel_id=1, source_target_pairs={{0,6},{1,7},{2,4},{3,5},{4,2},{5,3},{6,0},{7,1},{8,14},{9,15},{10,... | collective-permute-start | bytes 552968 | tf_op jit(solution)/shard_map/ppermute | solution.py:301
  37.6 0.7 %collective-permute-start.20 = (bf16[2,360,128]{2,1,0:T(8,128)(2,1)S(1)}, bf16[2,360,128]{2,1,0:T(8,128)(2,1)S(1)}, u32[]{:S(2)}, u32[]{:S(2)}) collective-permute-start(bf16[2,360,128]{2,1,0:T(8,128)(2,1)S(1)} %pad_maximum_fusion.4), channel_id=1, source_target_pairs={{0,2},{1,3},{2,0},{3,1},{4,6},{5,7},{6,4},{7,5},{8,10},{9,11},{10,... | collective-permute-start | bytes 552968 | tf_op jit(solution)/shard_map/ppermute | solution.py:301
  38.3 1.6 %collective-permute-start.18 = (bf16[2,360,128]{2,1,0:T(8,128)(2,1)S(1)}, bf16[2,360,128]{2,1,0:T(8,128)(2,1)S(1)}, u32[]{:S(2)}, u32[]{:S(2)}) collective-permute-start(bf16[2,360,128]{2,1,0:T(8,128)(2,1)S(1)} %pad_maximum_fusion.2), channel_id=1, source_target_pairs={{0,4},{1,5},{2,6},{3,7},{4,0},{5,1},{6,2},{7,3},{8,12},{9,13},{10,... | collective-permute-start | bytes 552968 | tf_op jit(solution)/shard_map/ppermute | solution.py:301
  39.9 0.1 add_convert_fusion
  40.1 4.5 %collective-permute-done.19 = bf16[2,360,128]{2,1,0:T(8,128)(2,1)S(1)} collective-permute-done((bf16[2,360,128]{2,1,0:T(8,128)(2,1)S(1)}, bf16[2,360,128]{2,1,0:T(8,128)(2,1)S(1)}, u32[]{:S(2)}, u32[]{:S(2)}) %collective-permute-start.19) | collective-permute-done | bytes 184352 | tf_op jit(solution)/shard_map/ppermute | solution.py:301
  44.6 3.2 %collective-permute-done.20 = bf16[2,360,128]{2,1,0:T(8,128)(2,1)S(1)} collective-permute-done((bf16[2,360,128]{2,1,0:T(8,128)(2,1)S(1)}, bf16[2,360,128]{2,1,0:T(8,128)(2,1)S(1)}, u32[]{:S(2)}, u32[]{:S(2)}) %collective-permute-start.20) | collective-permute-done | bytes 184352 | tf_op jit(solution)/shard_map/ppermute | solution.py:301
  47.8 0.1 fusion.8
  48.0 1.0 %collective-permute-start.24 = (bf16[360,128]{1,0:T(8,128)(2,1)S(1)}, bf16[360,128]{1,0:T(8,128)(2,1)S(1)}, u32[]{:S(2)}, u32[]{:S(2)}) collective-permute-start(bf16[360,128]{1,0:T(8,128)(2,1)S(1)} %get-tuple-element.110), channel_id=1, source_target_pairs={{0,16},{1,17},{2,18},{3,19},{4,20},{5,21},{6,22},{7,23},{8,24},{9,... | collective-permute-start | bytes 276488 | tf_op jit(solution)/shard_map/ppermute | solution.py:301
  49.0 1.2 %collective-permute-start.25 = (bf16[360,128]{1,0:T(8,128)(2,1)S(1)}, bf16[360,128]{1,0:T(8,128)(2,1)S(1)}, u32[]{:S(2)}, u32[]{:S(2)}) collective-permute-start(bf16[360,128]{1,0:T(8,128)(2,1)S(1)} %get-tuple-element.111), channel_id=1, source_target_pairs={{0,24},{1,25},{2,26},{3,27},{4,28},{5,29},{6,30},{7,31},{8,16},{9,... | collective-permute-start | bytes 276488 | tf_op jit(solution)/shard_map/ppermute | solution.py:301
  50.1 0.1 fusion.5
  50.3 0.6 %collective-permute-start.21 = (bf16[360,128]{1,0:T(8,128)(2,1)S(1)}, bf16[360,128]{1,0:T(8,128)(2,1)S(1)}, u32[]{:S(2)}, u32[]{:S(2)}) collective-permute-start(bf16[360,128]{1,0:T(8,128)(2,1)S(1)} %get-tuple-element.101), channel_id=1, source_target_pairs={{0,4},{1,5},{2,6},{3,7},{4,0},{5,1},{6,2},{7,3},{8,12},{9,13},{10,... | collective-permute-start | bytes 276488 | tf_op jit(solution)/shard_map/ppermute | solution.py:301
  50.9 1.4 %collective-permute-start.23 = (bf16[360,128]{1,0:T(8,128)(2,1)S(1)}, bf16[360,128]{1,0:T(8,128)(2,1)S(1)}, u32[]{:S(2)}, u32[]{:S(2)}) collective-permute-start(bf16[360,128]{1,0:T(8,128)(2,1)S(1)} %get-tuple-element.102), channel_id=1, source_target_pairs={{0,2},{1,3},{2,0},{3,1},{4,6},{5,7},{6,4},{7,5},{8,10},{9,11},{10,... | collective-permute-start | bytes 276488 | tf_op jit(solution)/shard_map/ppermute | solution.py:301
  52.3 1.5 %collective-permute-start.22 = (bf16[360,128]{1,0:T(8,128)(2,1)S(1)}, bf16[360,128]{1,0:T(8,128)(2,1)S(1)}, u32[]{:S(2)}, u32[]{:S(2)}) collective-permute-start(bf16[360,128]{1,0:T(8,128)(2,1)S(1)} %get-tuple-element.103), channel_id=1, source_target_pairs={{0,6},{1,7},{2,4},{3,5},{4,2},{5,3},{6,0},{7,1},{8,14},{9,15},{10,... | collective-permute-start | bytes 276488 | tf_op jit(solution)/shard_map/ppermute | solution.py:301
  53.8 3.1 %collective-permute-done.24 = bf16[360,128]{1,0:T(8,128)(2,1)S(1)} collective-permute-done((bf16[360,128]{1,0:T(8,128)(2,1)S(1)}, bf16[360,128]{1,0:T(8,128)(2,1)S(1)}, u32[]{:S(2)}, u32[]{:S(2)}) %collective-permute-start.24) | collective-permute-done | bytes 92192 | tf_op jit(solution)/shard_map/ppermute | solution.py:301
  57.0 0.8 %collective-permute-done.22 = bf16[360,128]{1,0:T(8,128)(2,1)S(1)} collective-permute-done((bf16[360,128]{1,0:T(8,128)(2,1)S(1)}, bf16[360,128]{1,0:T(8,128)(2,1)S(1)}, u32[]{:S(2)}, u32[]{:S(2)}) %collective-permute-start.22) | collective-permute-done | bytes 92192 | tf_op jit(solution)/shard_map/ppermute | solution.py:301
  57.8 0.8 %fusion.10 = bf16[128,360]{0,1:T(8,128)(2,1)} fusion(bf16[360,128]{1,0:T(8,128)(2,1)S(1)} %collective-permute-done.25, bf16[360,128]{1,0:T(8,128)(2,1)S(1)} %collective-permute-done.24, bf16[360,128]{1,0:T(8,128)(2,1)S(1)} %collective-permute-done.23, bf16[360,128]{1,0:T(8,128)(2,1)S(1)} %collective-permute-done.22, ...), kind=kLoop, calls=%fused_computation.28 | loop fusion | flops 737280 | bytes 829440 | tf_op jit(solution)/shard_map/transpose | solution.py:379
  (33 shorter events, 0.4 us)
Async XLA Ops:
  0.0 13.2 %copy-start = (bf16[1,1440,360]{2,1,0:T(8,128)(2,1)S(1)}, bf16[1,1440,360]{2,1,0:T(8,128)(2,1)}, u32[]{:S(2)}) copy-start(bf16[1,1440,360]{2,1,0:T(8,128)(2,1)} %param.14) | copy-start | bytes 3110404
  0.0 13.2 %copy-start.1 = (bf16[1,1440,360]{2,1,0:T(8,128)(2,1)S(1)}, bf16[1,1440,360]{2,1,0:T(8,128)(2,1)}, u32[]{:S(2)}) copy-start(bf16[1,1440,360]{2,1,0:T(8,128)(2,1)} %param.16) | copy-start | bytes 3110404
  2.4 9.0 %collective-permute-start.5 = (bf16[2,368,128]{2,1,0:T(8,128)(2,1)}, bf16[2,368,128]{2,1,0:T(8,128)(2,1)S(1)}, u32[]{:S(2)}, u32[]{:S(2)}) collective-permute-start(bf16[2,368,128]{2,1,0:T(8,128)(2,1)} %get-tuple-element.58.refs_0_), channel_id=1, source_target_pairs={{0,4},{1,5},{2,6},{3,7},{4,0},{5,1},{6,2},{7,3},{8,12},{9,13},{10,... | collective-permute-start | bytes 565256 | tf_op jit(solution)/shard_map/ppermute | solution.py:301
  5.4 8.7 %collective-permute-start.1 = (bf16[368,128]{1,0:T(8,128)(2,1)}, bf16[368,128]{1,0:T(8,128)(2,1)S(1)}, u32[]{:S(2)}, u32[]{:S(2)}) collective-permute-start(bf16[368,128]{1,0:T(8,128)(2,1)} %get-tuple-element.53), channel_id=1, source_target_pairs={{0,24},{1,25},{2,26},{3,27},{4,28},{5,29},{6,30},{7,31},{8,16},{9,... | collective-permute-start | bytes 282632 | tf_op jit(solution)/shard_map/ppermute | solution.py:301
  9.0 8.0 %collective-permute-start = (bf16[368,128]{1,0:T(8,128)(2,1)}, bf16[368,128]{1,0:T(8,128)(2,1)S(1)}, u32[]{:S(2)}, u32[]{:S(2)}) collective-permute-start(bf16[368,128]{1,0:T(8,128)(2,1)} %get-tuple-element.53), channel_id=1, source_target_pairs={{0,16},{1,17},{2,18},{3,19},{4,20},{5,21},{6,22},{7,23},{8,24},{9,... | collective-permute-start | bytes 282632 | tf_op jit(solution)/shard_map/ppermute | solution.py:301
  9.7 1.2 %copy-start.2 = (bf16[1,360,1440]{2,1,0:T(8,128)(2,1)S(1)}, bf16[1,360,1440]{2,1,0:T(8,128)(2,1)}, u32[]{:S(2)}) copy-start(bf16[1,360,1440]{2,1,0:T(8,128)(2,1)} %param.18) | copy-start | bytes 3110404
  12.4 15.5 %collective-permute-start.7 = (bf16[4,368,128]{2,1,0:T(8,128)(2,1)S(1)}, bf16[4,368,128]{2,1,0:T(8,128)(2,1)S(1)}, u32[]{:S(2)}, u32[]{:S(2)}) collective-permute-start(bf16[4,368,128]{2,1,0:T(8,128)(2,1)S(1)} %pad_maximum_fusion), channel_id=1, source_target_pairs={{0,8},{1,9},{2,10},{3,11},{4,12},{5,13},{6,14},{7,15},{8,0},{9,1},... | collective-permute-start | bytes 1130504 | tf_op jit(solution)/shard_map/ppermute | solution.py:301
  13.2 7.3 %collective-permute-start.6 = (bf16[2,368,128]{2,1,0:T(8,128)(2,1)S(1)}, bf16[2,368,128]{2,1,0:T(8,128)(2,1)S(1)}, u32[]{:S(2)}, u32[]{:S(2)}) collective-permute-start(bf16[2,368,128]{2,1,0:T(8,128)(2,1)S(1)} %collective-permute-done.5.refs_2_), channel_id=1, source_target_pairs={{0,1},{1,0},{2,3},{3,2},{4,5},{5,4},{6,7},{7,6},{8,9},{9,8},{10,11... | collective-permute-start | bytes 565256 | tf_op jit(solution)/shard_map/ppermute | solution.py:301
  13.2 7.3 %copy-start.3 = (bf16[2,368,128]{2,1,0:T(8,128)(2,1)S(1)}, bf16[2,368,128]{2,1,0:T(8,128)(2,1)}, u32[]{:S(2)}) copy-start(bf16[2,368,128]{2,1,0:T(8,128)(2,1)} %get-tuple-element.58.refs_0_) | copy-start | bytes 565252
  13.2 7.3 %copy-start.4 = (bf16[2,368,128]{2,1,0:T(8,128)(2,1)S(1)}, bf16[2,368,128]{2,1,0:T(8,128)(2,1)}, u32[]{:S(2)}) copy-start(bf16[2,368,128]{2,1,0:T(8,128)(2,1)} %get-tuple-element.59.refs_1_) | copy-start | bytes 565252
  17.0 8.7 %collective-permute-start.4 = (bf16[2,368,128]{2,1,0:T(8,128)(2,1)S(1)}, bf16[2,368,128]{2,1,0:T(8,128)(2,1)S(1)}, u32[]{:S(2)}, u32[]{:S(2)}) collective-permute-start(bf16[2,368,128]{2,1,0:T(8,128)(2,1)S(1)} %pad_maximum_fusion.1.refs_0_), channel_id=1, source_target_pairs={{0,6},{1,7},{2,4},{3,5},{4,2},{5,3},{6,0},{7,1},{8,14},{9,15},{10,... | collective-permute-start | bytes 565256 | tf_op jit(solution)/shard_map/ppermute | solution.py:301
  18.5 9.3 %collective-permute-start.3 = (bf16[2,368,128]{2,1,0:T(8,128)(2,1)S(1)}, bf16[2,368,128]{2,1,0:T(8,128)(2,1)S(1)}, u32[]{:S(2)}, u32[]{:S(2)}) collective-permute-start(bf16[2,368,128]{2,1,0:T(8,128)(2,1)S(1)} %pad_maximum_fusion.1.refs_0_), channel_id=1, source_target_pairs={{0,2},{1,3},{2,0},{3,1},{4,6},{5,7},{6,4},{7,5},{8,10},{9,11},{10,... | collective-permute-start | bytes 565256 | tf_op jit(solution)/shard_map/ppermute | solution.py:301
  19.0 8.9 %collective-permute-start.2 = (bf16[2,368,128]{2,1,0:T(8,128)(2,1)S(1)}, bf16[2,368,128]{2,1,0:T(8,128)(2,1)S(1)}, u32[]{:S(2)}, u32[]{:S(2)}) collective-permute-start(bf16[2,368,128]{2,1,0:T(8,128)(2,1)S(1)} %pad_maximum_fusion.1.refs_0_), channel_id=1, source_target_pairs={{0,4},{1,5},{2,6},{3,7},{4,0},{5,1},{6,2},{7,3},{8,12},{9,13},{10,... | collective-permute-start | bytes 565256 | tf_op jit(solution)/shard_map/ppermute | solution.py:301
  27.9 1.4 %collective-permute-start.8 = (bf16[2,368,128]{2,1,0:T(8,128)(2,1)S(1)}, bf16[2,368,128]{2,1,0:T(8,128)(2,1)S(1)}, u32[]{:S(2)}, u32[]{:S(2)}) collective-permute-start(bf16[2,368,128]{2,1,0:T(8,128)(2,1)S(1)} %pad_maximum_fusion.1.refs_0_), channel_id=1, source_target_pairs={{0,1},{1,0},{2,3},{3,2},{4,5},{5,4},{6,7},{7,6},{8,9},{9,8},{10,11... | collective-permute-start | bytes 565256 | tf_op jit(solution)/shard_map/ppermute | solution.py:301
  27.9 1.7 %collective-permute-start.9 = (bf16[2,368,128]{2,1,0:T(8,128)(2,1)S(1)}, bf16[2,368,128]{2,1,0:T(8,128)(2,1)S(1)}, u32[]{:S(2)}, u32[]{:S(2)}) collective-permute-start(bf16[2,368,128]{2,1,0:T(8,128)(2,1)S(1)} %collective-permute-done.3.refs_2_), channel_id=1, source_target_pairs={{0,1},{1,0},{2,3},{3,2},{4,5},{5,4},{6,7},{7,6},{8,9},{9,8},{10,11... | collective-permute-start | bytes 565256 | tf_op jit(solution)/shard_map/ppermute | solution.py:301
  28.4 1.5 %collective-permute-start.10 = (bf16[2,368,128]{2,1,0:T(8,128)(2,1)S(1)}, bf16[2,368,128]{2,1,0:T(8,128)(2,1)S(1)}, u32[]{:S(2)}, u32[]{:S(2)}) collective-permute-start(bf16[2,368,128]{2,1,0:T(8,128)(2,1)S(1)} %collective-permute-done.2.refs_4_), channel_id=1, source_target_pairs={{0,1},{1,0},{2,3},{3,2},{4,5},{5,4},{6,7},{7,6},{8,9},{9,8},{10,11... | collective-permute-start | bytes 565256 | tf_op jit(solution)/shard_map/ppermute | solution.py:301
  28.4 1.7 %collective-permute-start.11 = (bf16[2,368,128]{2,1,0:T(8,128)(2,1)S(1)}, bf16[2,368,128]{2,1,0:T(8,128)(2,1)S(1)}, u32[]{:S(2)}, u32[]{:S(2)}) collective-permute-start(bf16[2,368,128]{2,1,0:T(8,128)(2,1)S(1)} %collective-permute-done.4.refs_6_), channel_id=1, source_target_pairs={{0,1},{1,0},{2,3},{3,2},{4,5},{5,4},{6,7},{7,6},{8,9},{9,8},{10,11... | collective-permute-start | bytes 565256 | tf_op jit(solution)/shard_map/ppermute | solution.py:301
  31.6 2.3 %collective-permute-start.13 = (bf16[4,368,128]{2,1,0:T(8,128)(2,1)S(1)}, bf16[4,368,128]{2,1,0:T(8,128)(2,1)S(1)}, u32[]{:S(2)}, u32[]{:S(2)}) collective-permute-start(bf16[4,368,128]{2,1,0:T(8,128)(2,1)S(1)} %collective-permute-done.7.refs_0_), channel_id=1, source_target_pairs={{0,1},{1,0},{2,3},{3,2},{4,5},{5,4},{6,7},{7,6},{8,9},{9,8},{10,11... | collective-permute-start | bytes 1130504 | tf_op jit(solution)/shard_map/ppermute | solution.py:301
  31.9 2.0 %collective-permute-start.12 = (bf16[4,360,128]{2,1,0:T(8,128)(2,1)S(1)}, bf16[4,360,128]{2,1,0:T(8,128)(2,1)S(1)}, u32[]{:S(2)}, u32[]{:S(2)}) collective-permute-start(bf16[4,360,128]{2,1,0:T(8,128)(2,1)S(1)} %get-tuple-element.74), channel_id=1, source_target_pairs={{0,1},{1,0},{2,3},{3,2},{4,5},{5,4},{6,7},{7,6},{8,9},{9,8},{10,11... | collective-permute-start | bytes 1105928 | tf_op jit(solution)/shard_map/ppermute | solution.py:301
  33.9 2.1 %collective-permute-start.14 = (bf16[4,360,128]{2,1,0:T(8,128)(2,1)S(1)}, bf16[4,360,128]{2,1,0:T(8,128)(2,1)S(1)}, u32[]{:S(2)}, u32[]{:S(2)}) collective-permute-start(bf16[4,360,128]{2,1,0:T(8,128)(2,1)S(1)} %get-tuple-element.91), channel_id=1, source_target_pairs={{0,1},{1,0},{2,3},{3,2},{4,5},{5,4},{6,7},{7,6},{8,9},{9,8},{10,11... | collective-permute-start | bytes 1105928 | tf_op jit(solution)/shard_map/ppermute | solution.py:301
  35.6 4.3 %collective-permute-start.16 = (bf16[4,360,128]{2,1,0:T(8,128)(2,1)S(1)}, bf16[4,360,128]{2,1,0:T(8,128)(2,1)S(1)}, u32[]{:S(2)}, u32[]{:S(2)}) collective-permute-start(bf16[4,360,128]{2,1,0:T(8,128)(2,1)S(1)} %get-tuple-element.95), channel_id=1, source_target_pairs={{0,1},{1,0},{2,3},{3,2},{4,5},{5,4},{6,7},{7,6},{8,9},{9,8},{10,11... | collective-permute-start | bytes 1105928 | tf_op jit(solution)/shard_map/ppermute | solution.py:301
  36.1 8.5 %collective-permute-start.19 = (bf16[2,360,128]{2,1,0:T(8,128)(2,1)S(1)}, bf16[2,360,128]{2,1,0:T(8,128)(2,1)S(1)}, u32[]{:S(2)}, u32[]{:S(2)}) collective-permute-start(bf16[2,360,128]{2,1,0:T(8,128)(2,1)S(1)} %pad_maximum_fusion.3), channel_id=1, source_target_pairs={{0,6},{1,7},{2,4},{3,5},{4,2},{5,3},{6,0},{7,1},{8,14},{9,15},{10,... | collective-permute-start | bytes 552968 | tf_op jit(solution)/shard_map/ppermute | solution.py:301
  37.6 10.2 %collective-permute-start.20 = (bf16[2,360,128]{2,1,0:T(8,128)(2,1)S(1)}, bf16[2,360,128]{2,1,0:T(8,128)(2,1)S(1)}, u32[]{:S(2)}, u32[]{:S(2)}) collective-permute-start(bf16[2,360,128]{2,1,0:T(8,128)(2,1)S(1)} %pad_maximum_fusion.4), channel_id=1, source_target_pairs={{0,2},{1,3},{2,0},{3,1},{4,6},{5,7},{6,4},{7,5},{8,10},{9,11},{10,... | collective-permute-start | bytes 552968 | tf_op jit(solution)/shard_map/ppermute | solution.py:301
  38.3 9.5 %collective-permute-start.18 = (bf16[2,360,128]{2,1,0:T(8,128)(2,1)S(1)}, bf16[2,360,128]{2,1,0:T(8,128)(2,1)S(1)}, u32[]{:S(2)}, u32[]{:S(2)}) collective-permute-start(bf16[2,360,128]{2,1,0:T(8,128)(2,1)S(1)} %pad_maximum_fusion.2), channel_id=1, source_target_pairs={{0,4},{1,5},{2,6},{3,7},{4,0},{5,1},{6,2},{7,3},{8,12},{9,13},{10,... | collective-permute-start | bytes 552968 | tf_op jit(solution)/shard_map/ppermute | solution.py:301
  40.0 10.2 %collective-permute-start.17 = (bf16[4,360,128]{2,1,0:T(8,128)(2,1)S(1)}, bf16[4,360,128]{2,1,0:T(8,128)(2,1)S(1)}, u32[]{:S(2)}, u32[]{:S(2)}) collective-permute-start(bf16[4,360,128]{2,1,0:T(8,128)(2,1)S(1)} %add_convert_fusion), channel_id=1, source_target_pairs={{0,8},{1,9},{2,10},{3,11},{4,12},{5,13},{6,14},{7,15},{8,0},{9,1},... | collective-permute-start | bytes 1105928 | tf_op jit(solution)/shard_map/ppermute | solution.py:301
  40.1 10.1 %collective-permute-start.15 = (bf16[4,360,128]{2,1,0:T(8,128)(2,1)S(1)}, bf16[4,360,128]{2,1,0:T(8,128)(2,1)S(1)}, u32[]{:S(2)}, u32[]{:S(2)}) collective-permute-start(bf16[4,360,128]{2,1,0:T(8,128)(2,1)S(1)} %get-tuple-element.93), channel_id=1, source_target_pairs={{0,1},{1,0},{2,3},{3,2},{4,5},{5,4},{6,7},{7,6},{8,9},{9,8},{10,11... | collective-permute-start | bytes 1105928 | tf_op jit(solution)/shard_map/ppermute | solution.py:301
  48.0 9.0 %collective-permute-start.24 = (bf16[360,128]{1,0:T(8,128)(2,1)S(1)}, bf16[360,128]{1,0:T(8,128)(2,1)S(1)}, u32[]{:S(2)}, u32[]{:S(2)}) collective-permute-start(bf16[360,128]{1,0:T(8,128)(2,1)S(1)} %get-tuple-element.110), channel_id=1, source_target_pairs={{0,16},{1,17},{2,18},{3,19},{4,20},{5,21},{6,22},{7,23},{8,24},{9,... | collective-permute-start | bytes 276488 | tf_op jit(solution)/shard_map/ppermute | solution.py:301
  49.0 8.0 %collective-permute-start.25 = (bf16[360,128]{1,0:T(8,128)(2,1)S(1)}, bf16[360,128]{1,0:T(8,128)(2,1)S(1)}, u32[]{:S(2)}, u32[]{:S(2)}) collective-permute-start(bf16[360,128]{1,0:T(8,128)(2,1)S(1)} %get-tuple-element.111), channel_id=1, source_target_pairs={{0,24},{1,25},{2,26},{3,27},{4,28},{5,29},{6,30},{7,31},{8,16},{9,... | collective-permute-start | bytes 276488 | tf_op jit(solution)/shard_map/ppermute | solution.py:301
  50.3 6.7 %collective-permute-start.21 = (bf16[360,128]{1,0:T(8,128)(2,1)S(1)}, bf16[360,128]{1,0:T(8,128)(2,1)S(1)}, u32[]{:S(2)}, u32[]{:S(2)}) collective-permute-start(bf16[360,128]{1,0:T(8,128)(2,1)S(1)} %get-tuple-element.101), channel_id=1, source_target_pairs={{0,4},{1,5},{2,6},{3,7},{4,0},{5,1},{6,2},{7,3},{8,12},{9,13},{10,... | collective-permute-start | bytes 276488 | tf_op jit(solution)/shard_map/ppermute | solution.py:301
  50.9 6.1 %collective-permute-start.23 = (bf16[360,128]{1,0:T(8,128)(2,1)S(1)}, bf16[360,128]{1,0:T(8,128)(2,1)S(1)}, u32[]{:S(2)}, u32[]{:S(2)}) collective-permute-start(bf16[360,128]{1,0:T(8,128)(2,1)S(1)} %get-tuple-element.102), channel_id=1, source_target_pairs={{0,2},{1,3},{2,0},{3,1},{4,6},{5,7},{6,4},{7,5},{8,10},{9,11},{10,... | collective-permute-start | bytes 276488 | tf_op jit(solution)/shard_map/ppermute | solution.py:301
  52.3 5.5 %collective-permute-start.22 = (bf16[360,128]{1,0:T(8,128)(2,1)S(1)}, bf16[360,128]{1,0:T(8,128)(2,1)S(1)}, u32[]{:S(2)}, u32[]{:S(2)}) collective-permute-start(bf16[360,128]{1,0:T(8,128)(2,1)S(1)} %get-tuple-element.103), channel_id=1, source_target_pairs={{0,6},{1,7},{2,4},{3,5},{4,2},{5,3},{6,0},{7,1},{8,14},{9,15},{10,... | collective-permute-start | bytes 276488 | tf_op jit(solution)/shard_map/ppermute | solution.py:301
